TPU v7x, 32 devices: a whole 2x2x4 slice. The times are simulated.
32 devices in a mesh: seq: 4 (over x, core), head: 8 (over z, y).
Axes of the slice: x: 2, y: 2, z: 4, core: 2. Of those that a mesh axis runs over, the one named last changes fastest.
Arguments:
- tokens: bfloat16 [2048, 2048], P('seq', 'head'), may hold values from -6 to 6
- norm_gain: float32 [2048], replicated, may hold values from 0.25 to 1.75
- w_qkv: bfloat16 [3, 2048, 2048], P(None, None, 'head'), may hold values from -0.125 to 0.125
- head_scale: float32 [16], P('head'), may hold values from 4 to 24
- w_out: bfloat16 [2048, 2048], P('head'), may hold values from -0.25 to 0.25
- scale_ids: int32 [2048], replicated, may hold values from 0 to 9, as said below
Outputs:
- branch_out: bfloat16 [2048, 2048], P('seq', 'head')
Inputs may be any that keep to these rules, and one draw needn't show every extreme that they name: scale_ids never falls from one token to the next, and every scale from 0 to 9 occurs.
All inputs are finite; a program needn't handle non-finite values.
Results may differ from a plain program's by a relative error of at most 0.014.
Values may be sent and summed in bfloat16 or wider, within the bound.
No kernel may reach another device: no remote copies, remote signals or barrier semaphores. Data moves between devices by JAX's collectives and lax.ppermute only.
A program may use at most 128 MiB of HBM per device.

v0:
```python
import math

import jax
import jax.numpy as jnp
from jax import lax
from jax.sharding import PartitionSpec as P


def rms_normed(tokens, norm_gain):
    values = tokens.astype(jnp.float32)
    power = jnp.mean(values * values, axis=-1, keepdims=True)
    return (values * lax.rsqrt(power + 1e-06) * norm_gain).astype(jnp.bfloat16)


def unit_rows(values, factor):
    power = jnp.sum(values * values, axis=-1, keepdims=True)
    return (values * lax.rsqrt(power + 1e-06) * factor).astype(jnp.bfloat16)


def body(tokens, norm_gain, w_qkv, head_scale, w_out, scale_ids):
    rows = tokens.shape[0]
    local_ids = lax.dynamic_slice_in_dim(scale_ids, lax.axis_index("seq") * rows, rows)
    query_top = jnp.max(local_ids)
    wide = lax.all_gather(tokens, "head", axis=1, tiled=True)
    normed = rms_normed(wide, norm_gain)
    projected = jnp.einsum("td,cdf->ctf", normed, w_qkv, preferred_element_type=jnp.float32)
    local_heads = head_scale.shape[0]
    head_size = projected.shape[2] // local_heads
    query_n = unit_rows(
        projected[0].reshape(rows, local_heads, head_size), head_scale[None, :, None]
    )
    key_n = unit_rows(projected[1].reshape(rows, local_heads, head_size), 1.0)
    val_b = projected[2].reshape(rows, local_heads, head_size).astype(jnp.bfloat16)
    start_top = jnp.full((local_heads, rows), -1e30, jnp.float32)
    start_total = jnp.zeros((local_heads, rows), jnp.float32)
    start_acc = jnp.zeros((rows, local_heads, head_size), jnp.float32)
    keys = lax.all_gather(key_n, "seq", axis=0, tiled=True)
    vals = lax.all_gather(val_b, "seq", axis=0, tiled=True)
    count = keys.shape[0]
    ksize = math.gcd(count, 2048)
    kcount = count // ksize
    key_blocks = keys.reshape(kcount, ksize, local_heads, head_size)
    val_blocks = vals.reshape(kcount, ksize, local_heads, head_size)
    block_starts = jnp.arange(kcount, dtype=jnp.int32) * ksize

    def step(state, blk):
        kblk, vblk, offset = blk
        kid = lax.dynamic_slice_in_dim(scale_ids, offset, ksize)

        def update(st):
            tops, totals, accs = st
            score = jnp.einsum("qhd,khd->hqk", query_n, kblk, preferred_element_type=jnp.float32)
            allowed = (kid[None, :] <= local_ids[:, None])[None]
            score = jnp.where(allowed, score, -1e30)
            new_top = jnp.maximum(tops, jnp.max(score, axis=-1))
            expo = jnp.where(allowed, jnp.exp(score - new_top[:, :, None]), 0.0)
            shrink = jnp.exp(tops - new_top)
            new_total = totals * shrink + jnp.sum(expo, axis=-1)
            summed = jnp.einsum(
                "hqk,khd->qhd", expo.astype(jnp.bfloat16), vblk, preferred_element_type=jnp.float32
            )
            new_acc = accs * jnp.transpose(shrink)[:, :, None] + summed
            return (new_top, new_total, new_acc)

        def keep(st):
            return st

        return (lax.cond(jnp.min(kid) <= query_top, update, keep, state), None)

    result, unused = lax.scan(
        step, (start_top, start_total, start_acc), (key_blocks, val_blocks, block_starts)
    )
    tops, totals, accs = result
    attended = accs / jnp.transpose(totals)[:, :, None]
    attended = attended.reshape(rows, local_heads * head_size).astype(jnp.bfloat16)
    w_cols = lax.all_to_all(w_out, "head", split_axis=1, concat_axis=0, tiled=True)
    return jnp.dot(
        lax.all_gather(attended, "head", axis=1, tiled=True),
        w_cols,
        preferred_element_type=jnp.float32,
    ).astype(jnp.bfloat16)


def solution(mesh):
    placed = (P("seq", "head"), P(), P(None, None, "head"), P("head"), P("head", None), P())
    return jax.shard_map(
        body, mesh=mesh, in_specs=placed, out_specs=P("seq", "head"), check_vma=False
    )
```

profile of v0, /device:TPU:10, one launch (start us, length us, event | category | flops | bytes accessed | tf_op | source)
XLA Modules:
  0.0 186.0 jit_solution(13459597560922630607)
XLA Ops:
  6.5 0.0 copy-start
  6.5 0.0 all-gather.5.cloned.1.call-start
  6.5 0.7 all-gather.5.cloned.1.call-update
  7.3 0.0 all-gather.9.cloned.1.call-start
  7.3 52.5 %all-gather.5.cloned.1.call-done = bf16[512,2048]{1,0:T(8,128)(2,1)} async-done(((bf16[512,256]{1,0:T(8,128)(2,1)}), bf16[512,2048]{1,0:T(8,128)(2,1)}) %all-gather.5.cloned.1.call-update) | async-done | bytes 2097168 | tf_op jit(solution)/shard_map/all_gather | solution.py:24
  59.8 2.1 %fusion.14 = f32[512]{0:T(512)S(1)} fusion(bf16[512,2048]{1,0:T(8,128)(2,1)} %all-gather.5.cloned.1.call-done), kind=kLoop, calls=%fused_computation.17 | loop fusion | flops 3145216 | bytes 2099200 | tf_op jit(solution)/shard_map/reduce_sum | solution.py:11
  61.9 0.0 copy-done
  61.9 3.5 %fusion.22 = f32[3,512,256]{1,2,0:T(8,128)S(1)} fusion(bf16[3,2048,256]{2,1,0:T(8,128)(2,1)S(1)} %copy-done, bf16[512,2048]{1,0:T(8,128)(2,1)} %all-gather.5.cloned.1.call-done, f32[2048]{0:T(1024)} %param.9, f32[512]{0:T(512)S(1)} %add_rsqrt_fusion.2), kind=kOutput, calls=%fused_computation.24 | convolution fusion | flops 1614807040 | bytes 6825984 | tf_op jit(solution)/shard_map/td,cdf->ctf/dot_general | solution.py:26
  65.4 0.0 copy-start.2
  65.4 1.2 copy-done.2
  66.6 0.0 copy-start.3
  66.6 0.0 copy-start.4
  66.6 0.8 copy.19
  67.5 0.0 all-gather.9.cloned.1.call-update
  67.5 0.0 all-gather.7.cloned.1.call-start
  67.5 2.3 %fusion.26 = (f32[1,512,256]{1,2,0:T(8,128)}, f32[1,512,256]{1,2,0:T(8,128)}) fusion(f32[3,512,256]{1,2,0:T(8,128)} %copy-done.2), kind=kLoop, calls=%fused_computation.36 | loop fusion | bytes 2097152 | tf_op jit(solution)/shard_map/slice | solution.py:32
  69.8 2.0 %copy.18 = f32[512,2,128]{2,0,1:T(8,128)} copy(f32[512,2,128]{0,2,1:T(8,128)} %bitcast.29) | data formatting | bytes 1048576 | tf_op jit(solution)/shard_map/reshape;squeeze | solution.py:32
  71.8 1.1 multiply_reduce_fusion
  73.0 2.0 %multiply_convert_fusion = bf16[512,2,128]{2,0,1:T(8,128)(2,1)} fusion(f32[512,2,128]{2,0,1:T(8,128)} %copy.18, f32[512,2]{0,1:T(2,128)S(1)} %add_rsqrt_fusion), kind=kLoop, calls=%fused_computation.28 | loop fusion | flops 262144 | bytes 790528 | tf_op jit(solution)/shard_map/convert_element_type | solution.py:17
  74.9 0.0 all-gather.7.cloned.1.call-update
  75.0 0.0 all-gather.11.cloned.1.call-start
  75.0 0.0 copy-done.3
  75.0 0.7 reduce_min.10
  75.7 0.8 fusion.25
  77.8 0.8 broadcast_in_dim.49
  78.6 2.0 %copy.17 = f32[512,2,128]{2,0,1:T(8,128)} copy(f32[512,2,128]{0,2,1:T(8,128)} %bitcast.27) | data formatting | bytes 1048576 | tf_op jit(solution)/shard_map/reshape;squeeze | solution.py:30
  80.7 1.1 multiply_reduce_fusion.1
  81.8 0.0 copy-done.4
  81.8 1.3 multiply_convert_fusion.1
  83.1 0.4 all-gather.9.cloned.1.call-done
  83.5 18.3 %all-gather.7.cloned.1.call-done = bf16[2048,2,128]{2,0,1:T(8,128)(2,1)} async-done(((bf16[512,2,128]{2,0,1:T(8,128)(2,1)}), bf16[2048,2,128]{2,0,1:T(8,128)(2,1)}) %all-gather.7.cloned.1.call-update) | async-done | bytes 1048592 | tf_op jit(solution)/shard_map/all_gather | solution.py:37
  101.8 11.5 %conditional.1 = (f32[2,512]{1,0:T(2,128)S(1)}, f32[512,2,128]{0,2,1:T(8,128)}) conditional(s32[]{:T(128)} %convert_element_type.34, (f32[2,512]{1,0:T(2,128)S(1)}, f32[512,2,128]{2,0,1:T(8,128)}) %tuple.22, (s32[2048]{0:T(1024)S(1)}, s32[512]{0:T(512)S(1)}, bf16[512,2,128]{2,0,1:T(8,128)(2,1)S(1)}, bf16[2048,2,128]{2,0,1:T(8,128)(2,1)}, ...), branch_computations={%region_5.6_spmd, %region_6.9_spmd} | conditional | flops 1096027136 | bytes 40167496 | solution.py:68
  101.8 0.7 broadcast_compare_fusion
  102.5 2.8 %select_reduce_fusion = (f32[2,512]{1,0:T(2,128)S(1)}, f32[2,512,2048]{2,1,0:T(8,128)S(1)}) fusion(pred[512,2048]{1,0:T(8,128)(4,1)S(1)} %broadcast_compare_fusion, bf16[512,2,128]{2,0,1:T(8,128)(2,1)S(1)} %get-tuple-element.89, bf16[2048,2,128]{2,0,1:T(8,128)(2,1)} %get-tuple-element.90), kind=kOutput, calls=%fused_computation.1 | convolution fusion | flops 541064192 | bytes 10752000 | tf_op jit(solution)/shard_map/while/body/eval_jaxpr/cond/branch_1_fun/qhd,khd->hqk/dot_general | solution.py:52
  105.3 0.0 copy-start.1
  105.3 0.0 copy-start.5
  105.3 2.6 %fusion.1 = f32[2,512]{1,0:T(2,128)S(1)} fusion(f32[2,512,2048]{2,1,0:T(8,128)S(1)} %get-tuple-element.105, f32[2,512]{1,0:T(2,128)S(1)} %broadcast_maximum_fusion, pred[512,2048]{1,0:T(8,128)(4,1)S(1)} %broadcast_compare_fusion), kind=kLoop, calls=%fused_computation.3 | loop fusion | flops 8387584 | bytes 9445376 | tf_op jit(solution)/shard_map/while/body/eval_jaxpr/cond/branch_1_fun/reduce_sum | solution.py:58
  107.9 0.0 copy-done.1
  107.9 0.0 copy-done.5
  107.9 3.4 %fusion.8 = f32[512,2,128]{2,0,1:T(8,128)} fusion(bf16[2048,2,128]{2,0,1:T(8,128)(2,1)S(1)} %copy-done.5, f32[2,512,2048]{2,1,0:T(8,128)S(1)} %get-tuple-element.105, f32[2,512]{1,0:T(2,128)S(1)} %broadcast_maximum_fusion, pred[512,2048]{1,0:T(8,128)(4,1)S(1)} %broadcast_compare_fusion, f32[512,2,128]{2,0,1:T(8,128)S(1)} %copy-done.1, ...), kind=kOutput, calls=%fused_computation.8 | convolution fusion | flops 545521664 | bytes 11542528 | tf_op jit(solution)/shard_map/while/body/eval_jaxpr/cond/branch_1_fun/hqk,khd->qhd/dot_general | solution.py:59
  111.3 2.0 %copy.25 = f32[512,2,128]{0,2,1:T(8,128)} copy(f32[512,2,128]{2,0,1:T(8,128)} %fusion.8) | data formatting | bytes 1048576 | tf_op jit(solution)/shard_map/while/body/eval_jaxpr/cond | solution.py:68
  113.3 1.8 divide_convert_fusion
  115.1 0.0 all-gather.11.cloned.1.call-update
  115.1 2.3 %copy.21 = bf16[256,2048]{0,1:T(8,128)(2,1)} copy(bf16[256,2048]{1,0:T(8,128)(2,1)} %param.12) | data formatting | bytes 2097152 | tf_op args[4]
  117.4 42.1 %all_to_all.19 = bf16[256,8,256]{0,2,1:T(8,128)(2,1)} all-to-all(bf16[256,8,256]{0,2,1:T(8,128)(2,1)} %bitcast.33), channel_id=1, replica_groups=mesh['seq'=4,'head'=8] {'head'}, dimensions={1} | all-to-all | bytes 2097152 | tf_op jit(solution)/shard_map/all_to_all | solution.py:76
  159.5 2.3 %copy.22 = bf16[8,256,256]{2,1,0:T(8,128)(2,1)} copy(bf16[8,256,256]{1,2,0:T(8,128)(2,1)} %bitcast.32) | data formatting | bytes 2097152 | tf_op jit(solution)/shard_map/all_to_all | solution.py:76
  161.7 14.4 %all-gather.11.cloned.1.call-done = bf16[512,2048]{0,1:T(8,128)(2,1)} async-done(((bf16[512,256]{0,1:T(8,128)(2,1)}), bf16[512,2048]{0,1:T(8,128)(2,1)}) %all-gather.11.cloned.1.call-update) | async-done | bytes 2097168 | tf_op jit(solution)/shard_map/all_gather | solution.py:78
  176.1 3.3 %convolution_convert_fusion = bf16[512,256]{1,0:T(8,128)(2,1)} fusion(bf16[512,2048]{0,1:T(8,128)(2,1)} %all-gather.11.cloned.1.call-done, bf16[2048,256]{1,0:T(8,128)(2,1)} %bitcast.31), kind=kOutput, calls=%fused_computation.25 | convolution fusion | flops 537001984 | bytes 3407872 | tf_op jit(solution)/shard_map/dot_general | solution.py:77
  (7 shorter events, 0.1 us)
Async XLA Ops:
  6.5 55.4 %copy-start = (bf16[3,2048,256]{2,1,0:T(8,128)(2,1)S(1)}, bf16[3,2048,256]{2,1,0:T(8,128)(2,1)}, u32[]{:S(2)}) copy-start(bf16[3,2048,256]{2,1,0:T(8,128)(2,1)} %param.10) | copy-start | bytes 9437188
  6.5 53.3 %all-gather.5.cloned.1.call-start = ((), (), s32[]{:S(2)}) async-start(), calls=%async_computation.1 | async-start | bytes 2359296 | tf_op jit(solution)/shard_map/all_gather | solution.py:24
  7.3 76.2 %all-gather.9.cloned.1.call-start = ((), (), s32[]{:S(2)}) async-start(), calls=%async_computation.3 | async-start | bytes 1310720 | tf_op jit(solution)/shard_map/all_gather | solution.py:38
  65.4 1.2 copy-start.2
  66.6 8.4 %copy-start.3 = (s32[2048]{0:T(1024)S(1)}, s32[2048]{0:T(1024)}, u32[]{:S(2)}) copy-start(s32[2048]{0:T(1024)} %param.13) | copy-start | bytes 24580
  66.6 15.2 %copy-start.4 = (f32[2]{0:T(128)S(1)}, f32[2]{0:T(128)}, u32[]{:S(2)}) copy-start(f32[2]{0:T(128)} %param.11) | copy-start | bytes 28
  67.5 34.3 %all-gather.7.cloned.1.call-start = ((), (), s32[]{:S(2)}) async-start(), calls=%async_computation.2 | async-start | bytes 1310720 | tf_op jit(solution)/shard_map/all_gather | solution.py:37
  75.0 101.2 %all-gather.11.cloned.1.call-start = ((), (), s32[]{:S(2)}) async-start(), calls=%async_computation.4 | async-start | bytes 2359296 | tf_op jit(solution)/shard_map/all_gather | solution.py:78
  105.3 2.6 %copy-start.1 = (f32[512,2,128]{2,0,1:T(8,128)S(1)}, f32[512,2,128]{2,0,1:T(8,128)}, u32[]{:S(2)}) copy-start(f32[512,2,128]{2,0,1:T(8,128)} %get-tuple-element.91) | copy-start | bytes 1572868 | tf_op jit(solution)/shard_map/while/body/eval_jaxpr/cond
  105.3 2.6 %copy-start.5 = (bf16[2048,2,128]{2,0,1:T(8,128)(2,1)S(1)}, bf16[2048,2,128]{2,0,1:T(8,128)(2,1)}, u32[]{:S(2)}) copy-start(bf16[2048,2,128]{2,0,1:T(8,128)(2,1)} %get-tuple-element.92) | copy-start | bytes 3145732 | tf_op jit(solution)/shard_map/while/body/eval_jaxpr/cond
Sparse Core Ops, SparseCore 0:
  9.4 50.3 all-gather.4
  67.6 15.8 all-gather.8
  85.0 16.7 all-gather.6
  115.2 60.8 all-gather.10
where the time goes:
time: 189 us; the launch traced here: 186 us
  waiting for transfers between devices  86.4 us (46%)
  blocking collectives  42.1 us (22%)
  local copies, waits for them, and re-layouts  15.8 us (8%)
  between operations  14.5 us (8%)
  other arithmetic  14 us (7%)
  matrix products  13 us (7%)
    all_gather x1, waiting for transfers between devices, body(): wide = lax.all_gather(tokens, 'head', axis=1, tiled=True)  52.5 us
    all_to_all x1, blocking collectives, body(): lax.all_to_all(w_out, 'head', split_axis=1, concat_axis=0, tiled=True)  42.1 us
    all_gather x1, waiting for transfers between devices, body(): keys = lax.all_gather(key_n, 'seq', axis=0, tiled=True)  18.3 us
    all_gather x1, waiting for transfers between devices, body(): lax.all_gather(attended, 'head', axis=1, tiled=True)  14.4 us
  transfers between devices with their start and end apart: 4, of which 4 were waited for; matrix products, arithmetic and copies ran while one was open for 10% of the time, Pallas kernels for 0%

commit v1 on v0

v1 whole, which is shorter than its diff:
```python
import functools
import math

import jax
import jax.numpy as jnp
from jax import lax
from jax.experimental import pallas as pl
from jax.experimental.pallas import tpu as pltpu
from jax.sharding import PartitionSpec as P

CHUNKS = 1
LOG2E = math.log2(math.e)
VMEM = pl.BlockSpec(memory_space=pltpu.VMEM)
SMEM = pl.BlockSpec(memory_space=pltpu.SMEM)
F32 = jnp.float32
BF16 = jnp.bfloat16


def along(value, senders, step):
    return lax.ppermute(
        value, "head", [(2 * z + y, 2 * (z + step) + y) for z in senders for y in (0, 1)]
    )


def across(value, members):
    return lax.ppermute(value, "head", [(2 * z + y, 2 * z + 1 - y) for z in members for y in (0, 1)])


def gather_line(block, length):
    found = [((0, 1, 0), block)]
    ups, downs = [block], [block]
    swaps = [((0, 1, 1), across(block, range(length)))]
    for step in range(1, length):
        ups.append(along(ups[-1], range(step - 1, length - 1), 1))
        downs.append(along(downs[-1], range(1, length - step + 1), -1))
        found.append(((step, -1, 0), ups[-1]))
        found.append(((step, 1, 0), downs[-1]))
        swaps.append(((step, -1, 1), across(ups[-1], range(step, length))))
        swaps.append(((step, 1, 1), across(downs[-1], range(0, length - step))))
    return found + swaps


def project_kernel(rules, length, head_size, info, factor, *refs):
    blocks, (w_ref, q_ref, kv_ref, wide) = refs[: len(rules)], refs[len(rules) :]
    place, row = info[0], info[1]
    width = blocks[0].shape[1]
    for (step, side, other), block in zip(rules, blocks):
        source = place + side * step
        lane = (2 * source + (row if other == 0 else 1 - row)) * width

        @pl.when((source >= 0) & (source < length))
        def _():
            wide[:, pl.ds(pl.multiple_of(lane, width), width)] = block[...]

    rows, depth = wide.shape
    tile = math.gcd(rows, 128)
    out_width = q_ref.shape[1]

    @pl.loop(0, rows // tile)
    def _(index):
        here = pl.ds(pl.multiple_of(index * tile, tile), tile)
        x = wide[here, :]
        values = x.astype(F32)
        power = jnp.sum(values * values, axis=-1, keepdims=True) * (1.0 / depth)
        scale = lax.rsqrt(power + 1e-06)
        q = jnp.dot(x, w_ref[0], preferred_element_type=F32) * scale
        k = jnp.dot(x, w_ref[1], preferred_element_type=F32) * scale
        v = jnp.dot(x, w_ref[2], preferred_element_type=F32) * scale
        for head in range(out_width // head_size):
            lanes = slice(head * head_size, (head + 1) * head_size)
            qh, kh = q[:, lanes], k[:, lanes]
            q_size = lax.rsqrt(jnp.sum(qh * qh, axis=-1, keepdims=True) + 1e-06)
            k_size = lax.rsqrt(jnp.sum(kh * kh, axis=-1, keepdims=True) + 1e-06)
            q_ref[here, lanes] = (qh * (q_size * (factor[head] * LOG2E))).astype(BF16)
            kv_ref[here, lanes] = (kh * k_size).astype(BF16)
        kv_ref[here, out_width:] = v.astype(BF16)


def project(rules, blocks, weights, factor, info, length, head_size):
    rows, width = blocks[0].shape
    depth, out_width = weights.shape[1:]
    return pl.pallas_call(
        functools.partial(project_kernel, rules, length, head_size),
        out_shape=(
            jax.ShapeDtypeStruct((rows, out_width), BF16),
            jax.ShapeDtypeStruct((rows, 2 * out_width), BF16),
        ),
        in_specs=[SMEM, SMEM] + [VMEM] * (len(rules) + 1),
        out_specs=(VMEM, VMEM),
        scratch_shapes=[pltpu.VMEM((rows, depth), BF16)],
        compiler_params=pltpu.CompilerParams(vmem_limit_bytes=32 << 20),
        cost_estimate=pl.CostEstimate(
            flops=6 * rows * depth * out_width,
            bytes_accessed=2 * (rows * depth + 3 * depth * out_width),
            transcendentals=0,
        ),
        name="project",
    )(info, factor, *blocks, weights)


def attend_blocks(sources, ids, q_first, q_refs, id_col, id_row, kv_refs, v_ones, acc, head_size):
    heads = q_refs[0].shape[1] // head_size
    keys = kv_refs[0].shape[0]
    rows = q_refs[0].shape[0]
    for number, kv_ref in enumerate(kv_refs):
        for head in range(heads):
            start = (heads + head) * head_size
            v_ones[head, :, :head_size] = kv_ref[:, start : start + head_size]
            v_ones[head, :, head_size:] = jnp.ones((keys, head_size), BF16)
        first = sources[number]
        key_low, key_high = ids[first], ids[first + keys - 1]
        tile = math.gcd(rows, 256)
        for chunk, q_ref in enumerate(q_refs):

            @pl.loop(0, rows // tile)
            def _(index):
                here = pl.ds(pl.multiple_of(index * tile, tile), tile)
                base = chunk * rows + index * tile
                there = pl.ds(pl.multiple_of(base, tile), tile)
                q_low = ids[q_first + base]
                q_high = ids[q_first + base + tile - 1]

                def add(masked):
                    if masked:
                        allowed = id_row[first // keys] <= id_col[there, :]
                    for head in range(heads):
                        lanes = slice(head * head_size, (head + 1) * head_size)
                        score = lax.dot_general(
                            q_ref[here, lanes],
                            kv_ref[:, lanes],
                            (((1,), (1,)), ((), ())),
                            preferred_element_type=F32,
                        )
                        weight = jnp.exp2(score)
                        if masked:
                            weight = jnp.where(allowed, weight, 0.0)
                        wide = slice(2 * head * head_size, 2 * (head + 1) * head_size)
                        acc[there, wide] += jnp.dot(
                            weight.astype(BF16), v_ones[head], preferred_element_type=F32
                        )

                @pl.when(key_high <= q_low)
                def _():
                    add(False)

                @pl.when((key_high > q_low) & (key_low <= q_high))
                def _():
                    add(True)


def first_kernel(count_q, count_kv, head_size, info, ids, *refs):
    q_refs = refs[:count_q]
    id_col, id_row = refs[count_q : count_q + 2]
    kv_refs = refs[count_q + 2 : count_q + 2 + count_kv]
    acc, v_ones = refs[count_q + 2 + count_kv :]
    acc[...] = jnp.zeros_like(acc)
    sources = [info[3 + number] for number in range(count_kv)]
    attend_blocks(sources, ids, info[2], q_refs, id_col, id_row, kv_refs, v_ones, acc, head_size)


def last_kernel(count_q, count_kv, head_size, roles, length, info, ids, *refs):
    q_refs = refs[:count_q]
    id_col, id_row = refs[count_q : count_q + 2]
    kv_refs = refs[count_q + 2 : count_q + 2 + count_kv]
    rest = refs[count_q + 2 + count_kv :]
    acc_in, w_ref = rest[:2]
    outs, (v_ones, acc, attended) = rest[2:-3], rest[-3:]
    acc[...] = acc_in[...]
    sources = [info[3 + number] for number in range(count_kv)]
    attend_blocks(sources, ids, info[2], q_refs, id_col, id_row, kv_refs, v_ones, acc, head_size)
    heads = q_refs[0].shape[1] // head_size
    for head in range(heads):
        start = 2 * head * head_size
        attended[:, head * head_size : (head + 1) * head_size] = (
            acc[:, start : start + head_size]
            / acc[:, start + head_size : start + 2 * head_size]
        ).astype(BF16)
    place, row = info[0], info[1]
    width = outs[0].shape[1]
    for number, role in enumerate(roles):
        goal, valid = role(place)

        @pl.when(valid)
        def _():
            for other in (1, 0):
                lane = (2 * goal + (row if other == 0 else 1 - row)) * width
                outs[2 * number + 1 - other][...] = jnp.dot(
                    attended[...],
                    w_ref[:, pl.ds(pl.multiple_of(lane, width), width)],
                    preferred_element_type=F32,
                ).astype(BF16)


def attend_first(info, ids, queries, id_col, id_row, kvs, head_size):
    rows, width = queries[0].shape
    total = rows * len(queries)
    keys = kvs[0].shape[0]
    heads = width // head_size
    return pl.pallas_call(
        functools.partial(first_kernel, len(queries), len(kvs), head_size),
        out_shape=jax.ShapeDtypeStruct((total, 2 * width), F32),
        in_specs=[SMEM, SMEM] + [VMEM] * (len(queries) + 2 + len(kvs)),
        out_specs=VMEM,
        scratch_shapes=[pltpu.VMEM((heads, keys, 2 * head_size), BF16)],
        compiler_params=pltpu.CompilerParams(vmem_limit_bytes=48 << 20),
        cost_estimate=pl.CostEstimate(
            flops=6 * total * keys * len(kvs) * width,
            bytes_accessed=4 * keys * len(kvs) * width + 4 * total * width,
            transcendentals=total * keys * len(kvs) * heads,
        ),
        name="attend_first",
    )(info, ids, *queries, id_col, id_row, *kvs)


def attend_last(info, ids, queries, id_col, id_row, kvs, acc, w_out, roles, length, head_size):
    rows, width = queries[0].shape
    total = rows * len(queries)
    keys = kvs[0].shape[0]
    heads = width // head_size
    out_width = w_out.shape[1] // (2 * length)
    outs = 2 * len(roles)
    return pl.pallas_call(
        functools.partial(last_kernel, len(queries), len(kvs), head_size, roles, length),
        out_shape=(jax.ShapeDtypeStruct((total, out_width), BF16),) * outs,
        in_specs=[SMEM, SMEM] + [VMEM] * (len(queries) + 4 + len(kvs)),
        out_specs=(VMEM,) * outs,
        scratch_shapes=[
            pltpu.VMEM((heads, keys, 2 * head_size), BF16),
            pltpu.VMEM((total, 2 * width), F32),
            pltpu.VMEM((total, width), BF16),
        ],
        compiler_params=pltpu.CompilerParams(vmem_limit_bytes=48 << 20),
        cost_estimate=pl.CostEstimate(
            flops=6 * total * keys * len(kvs) * width + 2 * total * width * w_out.shape[1],
            bytes_accessed=4 * keys * len(kvs) * width + 4 * total * width * 4,
            transcendentals=total * keys * len(kvs) * heads,
        ),
        name="attend_last",
    )(info, ids, *queries, id_col, id_row, *kvs, acc, w_out)


def total_of(*parts):
    return sum(part.astype(F32) for part in parts).astype(BF16)


def line_roles(length):
    roles = []
    for step in range(length - 1, 0, -1):
        roles.append(lambda place, step=step: (place + step, place + step < length))
        roles.append(lambda place, step=step: (place - step, place - step >= 0))
    roles.append(lambda place: (place, place >= 0))
    return roles


def body(mesh_shape, tokens, norm_gain, w_qkv, head_scale, w_out, scale_ids):
    length = mesh_shape["head"] // 2
    outer = mesh_shape["seq"] // 2
    rows, width = tokens.shape
    head_size = w_qkv.shape[2] // head_scale.shape[0]
    chunk_rows = rows // CHUNKS
    head_at, seq_at = lax.axis_index("head"), lax.axis_index("seq")
    place, row = head_at // 2, head_at % 2
    chip, core = seq_at // 2, seq_at % 2

    weights = (w_qkv.astype(F32) * norm_gain[None, :, None]).astype(BF16)
    id_row = scale_ids.reshape(-1, 1, chunk_rows)
    id_col = lax.dynamic_slice_in_dim(scale_ids, seq_at * rows, rows)[:, None]

    info = jnp.stack([place, row]).astype(jnp.int32)
    queries, near, near_at, far, far_at = [], [], [], [], []
    for number in range(CHUNKS):
        part = tokens[number * chunk_rows : (number + 1) * chunk_rows]
        gathered = gather_line(part, length)
        query, kv = project(
            [rule for rule, data in gathered],
            [data for rule, data in gathered],
            weights, head_scale, info, length, head_size,
        )
        queries.append(query)
        swap = [(2 * a + b, 2 * a + 1 - b) for a in range(outer) for b in (0, 1)]
        start = number * chunk_rows
        for step in range(outer):
            if step:
                shift = [
                    (2 * a + b, 2 * ((a + step) % outer) + b) for a in range(outer) for b in (0, 1)
                ]
                held = lax.ppermute(kv, "seq", shift)
            else:
                held = kv
            source = 2 * ((chip + outer - step) % outer)
            group, group_at = (far, far_at) if step else (near, near_at)
            group.append(held)
            group_at.append((source + core) * rows + start)
            group.append(lax.ppermute(held, "seq", swap))
            group_at.append((source + 1 - core) * rows + start)

    near_info = jnp.stack([place, row, seq_at * rows] + near_at).astype(jnp.int32)
    far_info = jnp.stack([place, row, seq_at * rows] + far_at).astype(jnp.int32)
    acc = attend_first(near_info, scale_ids, queries, id_col, id_row, near, head_size)
    roles = line_roles(length)
    parts = attend_last(
        far_info, scale_ids, queries, id_col, id_row, far, acc, w_out, roles, length, head_size
    )
    up = down = None
    number = 0
    for step in range(length - 1, 0, -1):
        up_senders, down_senders = range(0, length - step), range(step, length)
        up_parts = [parts[number + 1], across(parts[number], up_senders)]
        down_parts = [parts[number + 3], across(parts[number + 2], down_senders)]
        if up is not None:
            up_parts.append(up)
            down_parts.append(down)
        up = along(total_of(*up_parts), up_senders, 1)
        down = along(total_of(*down_parts), down_senders, -1)
        number += 4
    return total_of(parts[number + 1], across(parts[number], range(length)), up, down)


def solution(mesh):
    placed = (P("seq", "head"), P(), P(None, None, "head"), P("head"), P("head", None), P())
    return jax.shard_map(
        functools.partial(body, dict(mesh.shape)),
        mesh=mesh,
        in_specs=placed,
        out_specs=P("seq", "head"),
        check_vma=False,
    )
```

time: 189 us -> 121 us (0.64)
  starting transfers between devices: 0.12 us -> 52.9 us
  waiting for transfers between devices: 86.4 us -> 39.5 us
  blocking collectives: 42.1 us -> 0 us
  Pallas kernels: 0 us -> 14.3 us
  between operations: 14.5 us -> 0.35 us
  matrix products: 13 us -> 0 us
  other arithmetic: 14 us -> 3.98 us
  local copies, waits for them, and re-layouts: 15.8 us -> 7.96 us
    all_gather x4 -> x0, waiting for transfers between devices: 85.6 us -> none  [the longest x1 52.5 us: body(): wide = lax.all_gather(tokens, 'head', axis=1, tiled=True)]
    ppermute x0 -> x29, starting transfers between devices: none -> 52.9 us  [the longest x12 26.6 us: along(): lax.ppermute(value, 'head', [(2 * z + y, 2 * (z + step) + y) for z in sen...]
    all_to_all x1 -> x0, blocking collectives: 42.1 us -> none  [body(): lax.all_to_all(w_out, 'head', split_axis=1, concat_axis=0, tiled=True)]
    ppermute x0 -> x29, waiting for transfers between devices: none -> 39.5 us  [the longest x12 24.3 us: along(): lax.ppermute(value, 'head', [(2 * z + y, 2 * (z + step) + y) for z in sen...]
    pallas_call x0 -> x3, Pallas kernels: none -> 14.3 us  [the longest x1 5.49 us: project(): pl.pallas_call(functools.partial(project_kernel, rules, length, head_size...]
    dot_general x4 -> x0, matrix products: 13 us -> none  [the longest x1 3.51 us: body(): jnp.einsum('td,cdf->ctf', normed, w_qkv, preferred_element_type=jnp.float32)]
    reduce_sum x4 -> x0, other arithmetic: 6.85 us -> none  [the longest x1 2.57 us: update(): new_total = totals * shrink + jnp.sum(expo, axis=-1)]
    unnamed x9 -> x24, local copies, waits for them, and re-layouts: 3.43 us -> 7.57 us
  transfers between devices with their start and end apart: 4 -> 29, of which waited for: 4 -> 12; matrix products, arithmetic and copies ran while one was open for 10% -> 3% of each run, Pallas kernels for 0% -> 3%
where the time goes in v1:
time: 121 us; the launch traced here: 119 us
  starting transfers between devices  52.9 us (44%)
  waiting for transfers between devices  39.5 us (33%)
  Pallas kernels  14.3 us (12%)
  local copies, waits for them, and re-layouts  7.96 us (7%)
  other arithmetic  3.98 us (3%)
    ppermute x12, starting transfers between devices, along(): lax.ppermute(value, 'head', [(2 * z + y, 2 * (z + step) + y) for z in sen...  26.6 us
    ppermute x14, starting transfers between devices, across(): lax.ppermute(value, 'head', [(2 * z + y, 2 * z + 1 - y) for z in members...  25.8 us
    ppermute x12, waiting for transfers between devices, along(): lax.ppermute(value, 'head', [(2 * z + y, 2 * (z + step) + y) for z in sen...  24.3 us
    ppermute x1, waiting for transfers between devices, body(): held = lax.ppermute(kv, 'seq', shift)  11.4 us
    unnamed x24, local copies, waits for them, and re-layouts  7.57 us
    pallas_call x1, Pallas kernels, project(): pl.pallas_call(functools.partial(project_kernel, rules, length, head_size...  5.49 us
    pallas_call x1, Pallas kernels, attend_last(): pl.pallas_call(functools.partial(last_kernel, len(queries), len(kvs), hea...  5.3 us
    ppermute x14, waiting for transfers between devices, across(): lax.ppermute(value, 'head', [(2 * z + y, 2 * z + 1 - y) for z in members...  3.86 us
  transfers between devices with their start and end apart: 29, of which 12 were waited for; matrix products, arithmetic and copies ran while one was open for 3% of the time, Pallas kernels for 3%

profile of v1, /device:TPU:10, one launch (start us, length us, event | category | flops | bytes accessed | tf_op | source)
XLA Modules:
  0.0 119.0 jit_solution(10061519832232915140)
XLA Ops:
  0.0 3.6 %collective-permute-start = (bf16[512,256]{1,0:T(8,128)(2,1)}, bf16[512,256]{1,0:T(8,128)(2,1)S(1)}, u32[]{:S(2)}, u32[]{:S(2)}) collective-permute-start(bf16[512,256]{1,0:T(8,128)(2,1)} %refs_0_.1), channel_id=1, source_target_pairs={{0,2},{1,3},{2,4},{3,5},{4,6},{5,7},{8,10},{9,11},{10,12},{11,13},... | collective-permute-start | bytes 786440 | tf_op jit(solution)/shard_map/ppermute | solution.py:20
  3.6 2.4 %collective-permute-start.1 = (bf16[512,256]{1,0:T(8,128)(2,1)}, bf16[512,256]{1,0:T(8,128)(2,1)}, u32[]{:S(2)}, u32[]{:S(2)}) collective-permute-start(bf16[512,256]{1,0:T(8,128)(2,1)} %refs_0_.1), channel_id=1, source_target_pairs={{2,0},{3,1},{4,2},{5,3},{6,4},{7,5},{10,8},{11,9},{12,10},{13,11},... | collective-permute-start | bytes 786440 | tf_op jit(solution)/shard_map/ppermute | solution.py:20
  6.0 4.3 %collective-permute-done.refs_1_ = bf16[512,256]{1,0:T(8,128)(2,1)S(1)} collective-permute-done((bf16[512,256]{1,0:T(8,128)(2,1)}, bf16[512,256]{1,0:T(8,128)(2,1)S(1)}, u32[]{:S(2)}, u32[]{:S(2)}) %collective-permute-start) | collective-permute-done | bytes 262176 | tf_op jit(solution)/shard_map/ppermute | solution.py:20
  10.3 4.2 %collective-permute-start.2 = (bf16[512,256]{1,0:T(8,128)(2,1)S(1)}, bf16[512,256]{1,0:T(8,128)(2,1)}, u32[]{:S(2)}, u32[]{:S(2)}) collective-permute-start(bf16[512,256]{1,0:T(8,128)(2,1)S(1)} %collective-permute-done.refs_1_), channel_id=1, source_target_pairs={{2,4},{3,5},{4,6},{5,7},{10,12},{11,13},{12,14},{13,15},{18,20},{1... | collective-permute-start | bytes 786440 | tf_op jit(solution)/shard_map/ppermute | solution.py:20
  14.5 1.9 %collective-permute-start.3 = (bf16[512,256]{1,0:T(8,128)(2,1)}, bf16[512,256]{1,0:T(8,128)(2,1)}, u32[]{:S(2)}, u32[]{:S(2)}) collective-permute-start(bf16[512,256]{1,0:T(8,128)(2,1)} %collective-permute-done.1.refs_2_), channel_id=1, source_target_pairs={{2,0},{3,1},{4,2},{5,3},{10,8},{11,9},{12,10},{13,11},{18,16},{19,... | collective-permute-start | bytes 786440 | tf_op jit(solution)/shard_map/ppermute | solution.py:20
  16.4 1.6 %collective-permute-start.6 = (bf16[512,256]{1,0:T(8,128)(2,1)}, bf16[512,256]{1,0:T(8,128)(2,1)S(1)}, u32[]{:S(2)}, u32[]{:S(2)}) collective-permute-start(bf16[512,256]{1,0:T(8,128)(2,1)} %refs_0_.1), channel_id=1, source_target_pairs={{0,1},{1,0},{2,3},{3,2},{4,5},{5,4},{6,7},{7,6},{8,9},{9,8},{10,11... | collective-permute-start | bytes 786440 | tf_op jit(solution)/shard_map/ppermute | solution.py:26
  18.0 2.4 %collective-permute-start.7 = (bf16[512,256]{1,0:T(8,128)(2,1)S(1)}, bf16[512,256]{1,0:T(8,128)(2,1)S(1)}, u32[]{:S(2)}, u32[]{:S(2)}) collective-permute-start(bf16[512,256]{1,0:T(8,128)(2,1)S(1)} %collective-permute-done.refs_1_), channel_id=1, source_target_pairs={{2,3},{3,2},{4,5},{5,4},{6,7},{7,6},{10,11},{11,10},{12,13},{13,12... | collective-permute-start | bytes 786440 | tf_op jit(solution)/shard_map/ppermute | solution.py:26
  20.4 0.7 copy-done.1
  21.1 1.4 %collective-permute-start.4 = (bf16[512,256]{1,0:T(8,128)(2,1)}, bf16[512,256]{1,0:T(8,128)(2,1)}, u32[]{:S(2)}, u32[]{:S(2)}) collective-permute-start(bf16[512,256]{1,0:T(8,128)(2,1)} %collective-permute-done.2.refs_3_), channel_id=1, source_target_pairs={{4,6},{5,7},{12,14},{13,15},{20,22},{21,23},{28,30},{29,31}} | collective-permute-start | bytes 786440 | tf_op jit(solution)/shard_map/ppermute | solution.py:20
  22.5 1.1 collective-permute-done.3.refs_4_
  23.6 2.9 %collective-permute-start.5 = (bf16[512,256]{1,0:T(8,128)(2,1)}, bf16[512,256]{1,0:T(8,128)(2,1)}, u32[]{:S(2)}, u32[]{:S(2)}) collective-permute-start(bf16[512,256]{1,0:T(8,128)(2,1)} %collective-permute-done.3.refs_4_), channel_id=1, source_target_pairs={{2,0},{3,1},{10,8},{11,9},{18,16},{19,17},{26,24},{27,25}} | collective-permute-start | bytes 786440 | tf_op jit(solution)/shard_map/ppermute | solution.py:20
  26.5 3.4 %collective-permute-start.8 = (bf16[512,256]{1,0:T(8,128)(2,1)}, bf16[512,256]{1,0:T(8,128)(2,1)}, u32[]{:S(2)}, u32[]{:S(2)}) collective-permute-start(bf16[512,256]{1,0:T(8,128)(2,1)} %collective-permute-done.1.refs_2_), channel_id=1, source_target_pairs={{0,1},{1,0},{2,3},{3,2},{4,5},{5,4},{8,9},{9,8},{10,11},{11,10},{1... | collective-permute-start | bytes 786440 | tf_op jit(solution)/shard_map/ppermute | solution.py:26
  29.9 0.7 copy-done.3
  30.6 2.4 %collective-permute-start.10 = (bf16[512,256]{1,0:T(8,128)(2,1)}, bf16[512,256]{1,0:T(8,128)(2,1)}, u32[]{:S(2)}, u32[]{:S(2)}) collective-permute-start(bf16[512,256]{1,0:T(8,128)(2,1)} %collective-permute-done.3.refs_4_), channel_id=1, source_target_pairs={{0,1},{1,0},{2,3},{3,2},{8,9},{9,8},{10,11},{11,10},{16,17},{17,16... | collective-permute-start | bytes 786440 | tf_op jit(solution)/shard_map/ppermute | solution.py:26
  33.0 0.7 copy-done.5
  33.7 1.4 %collective-permute-start.9 = (bf16[512,256]{1,0:T(8,128)(2,1)}, bf16[512,256]{1,0:T(8,128)(2,1)}, u32[]{:S(2)}, u32[]{:S(2)}) collective-permute-start(bf16[512,256]{1,0:T(8,128)(2,1)} %collective-permute-done.2.refs_3_), channel_id=1, source_target_pairs={{4,5},{5,4},{6,7},{7,6},{12,13},{13,12},{14,15},{15,14},{20,21},{2... | collective-permute-start | bytes 786440 | tf_op jit(solution)/shard_map/ppermute | solution.py:26
  35.1 1.4 %collective-permute-start.11 = (bf16[512,256]{1,0:T(8,128)(2,1)}, bf16[512,256]{1,0:T(8,128)(2,1)}, u32[]{:S(2)}, u32[]{:S(2)}) collective-permute-start(bf16[512,256]{1,0:T(8,128)(2,1)} %collective-permute-done.4.refs_5_), channel_id=1, source_target_pairs={{6,7},{7,6},{14,15},{15,14},{22,23},{23,22},{30,31},{31,30}} | collective-permute-start | bytes 786440 | tf_op jit(solution)/shard_map/ppermute | solution.py:26
  36.4 1.4 %collective-permute-start.12 = (bf16[512,256]{1,0:T(8,128)(2,1)}, bf16[512,256]{1,0:T(8,128)(2,1)}, u32[]{:S(2)}, u32[]{:S(2)}) collective-permute-start(bf16[512,256]{1,0:T(8,128)(2,1)} %collective-permute-done.5.refs_6_), channel_id=1, source_target_pairs={{0,1},{1,0},{8,9},{9,8},{16,17},{17,16},{24,25},{25,24}} | collective-permute-start | bytes 786440 | tf_op jit(solution)/shard_map/ppermute | solution.py:26
  37.8 2.5 %multiply_convert_fusion.refs_14_ = bf16[3,2048,256]{2,1,0:T(8,128)(2,1)S(1)} fusion(bf16[3,2048,256]{2,1,0:T(8,128)(2,1)} %param.8, f32[2048]{0:T(1024)} %param.7), kind=kLoop, calls=%fused_computation | loop fusion | flops 4718592 | bytes 6299648 | tf_op jit(solution)/shard_map/convert_element_type | solution.py:265
  40.7 0.9 copy-done.2
  41.6 0.9 copy-done.4
  42.6 0.9 copy-done.6
  43.5 5.5 %project.1 = (bf16[512,256]{1,0:T(8,128)(2,1)S(1)}, bf16[512,512]{1,0:T(8,128)(2,1)}) custom-call(s32[2]{0:T(128)S(1)} %pad_add_fusion.info, f32[2]{0:T(128)S(1)} %copy-done.7, bf16[512,256]{1,0:T(8,128)(2,1)S(1)} %copy-done, bf16[512,256]{1,0:T(8,128)(2,1)S(1)} %copy-done.2, bf16[512,256]{1,0:T(8,128)(2,1)} %collective-permute-done.1.refs_2_, ...), custom_call_target="tpu_custom_call" | custom-call | flops 1610612736 | bytes 5242880 | tf_op jit(solution)/shard_map/project/pallas_call | solution.py:82
  49.0 0.7 copy-done.9
  50.3 11.4 %collective-permute-done.13.refs_3_ = bf16[512,512]{1,0:T(8,128)(2,1)S(1)} collective-permute-done((bf16[512,512]{1,0:T(8,128)(2,1)}, bf16[512,512]{1,0:T(8,128)(2,1)S(1)}, u32[]{:S(2)}, u32[]{:S(2)}) %collective-permute-start.13) | collective-permute-done | bytes 524320 | tf_op jit(solution)/shard_map/ppermute | solution.py:287
  62.1 1.0 copy-done.10
  63.0 3.5 %attend_first.1.refs_5_ = f32[512,512]{1,0:T(8,128)S(1)} custom-call(s32[5]{0:T(128)S(1)} %stack.44.info, s32[2048]{0:T(1024)S(1)} %copy-done.8, bf16[512,256]{1,0:T(8,128)(2,1)S(1)} %copy-done.10, s32[512,1]{1,0:T(8,128)S(1)} %copy.8.refs_1_, s32[4,1,512]{2,1,0:T(1,128)S(1)} %bitcast.9, bf16[512,512]{1,0:T(8,128)(2,1)} %get-tuple-element.22.refs_3_, ...), custom_call_target="tpu_custom_call" | custom-call | flops 805306368 | bytes 1572864 | tf_op jit(solution)/shard_map/attend_first/pallas_call | solution.py:199
  66.5 1.0 copy-done.11
  67.5 5.3 %attend_last.1 = (bf16[512,256]{1,0:T(8,128)(2,1)S(1)}, bf16[512,256]{1,0:T(8,128)(2,1)S(1)}, bf16[512,256]{1,0:T(8,128)(2,1)S(1)}, bf16[512,256]{1,0:T(8,128)(2...) custom-call(s32[5]{0:T(128)S(1)} %stack.40.info, ...), custom_call_target="tpu_custom_call" | custom-call | flops 1342177280 | bytes 3145728 | tf_op jit(solution)/shard_map/attend_last/pallas_call | solution.py:222
  72.8 0.7 collective-permute-start.19
  74.2 2.5 %collective-permute-start.18 = (bf16[512,256]{1,0:T(8,128)(2,1)S(1)}, bf16[512,256]{1,0:T(8,128)(2,1)S(1)}, u32[]{:S(2)}, u32[]{:S(2)}) collective-permute-start(bf16[512,256]{1,0:T(8,128)(2,1)S(1)} %get-tuple-element.28), channel_id=1, source_target_pairs={{0,1},{1,0},{2,3},{3,2},{8,9},{9,8},{10,11},{11,10},{16,17},{17,16... | collective-permute-start | bytes 786440 | tf_op jit(solution)/shard_map/ppermute | solution.py:26
  76.8 1.3 %collective-permute-start.20 = (bf16[512,256]{1,0:T(8,128)(2,1)S(1)}, bf16[512,256]{1,0:T(8,128)(2,1)S(1)}, u32[]{:S(2)}, u32[]{:S(2)}) collective-permute-start(bf16[512,256]{1,0:T(8,128)(2,1)S(1)} %add_convert_fusion.6), channel_id=1, source_target_pairs={{0,2},{1,3},{8,10},{9,11},{16,18},{17,19},{24,26},{25,27}} | collective-permute-start | bytes 786440 | tf_op jit(solution)/shard_map/ppermute | solution.py:20
  78.1 0.7 collective-permute-start.24
  78.9 0.7 collective-permute-start.26
  79.6 3.3 %collective-permute-start.17 = (bf16[512,256]{1,0:T(8,128)(2,1)S(1)}, bf16[512,256]{1,0:T(8,128)(2,1)S(1)}, u32[]{:S(2)}, u32[]{:S(2)}) collective-permute-start(bf16[512,256]{1,0:T(8,128)(2,1)S(1)} %get-tuple-element.26), channel_id=1, source_target_pairs={{0,1},{1,0},{2,3},{3,2},{4,5},{5,4},{8,9},{9,8},{10,11},{11,10},{1... | collective-permute-start | bytes 786440 | tf_op jit(solution)/shard_map/ppermute | solution.py:26
  82.9 2.3 %collective-permute-done.18 = bf16[512,256]{1,0:T(8,128)(2,1)S(1)} collective-permute-done((bf16[512,256]{1,0:T(8,128)(2,1)S(1)}, bf16[512,256]{1,0:T(8,128)(2,1)S(1)}, u32[]{:S(2)}, u32[]{:S(2)}) %collective-permute-start.18) | collective-permute-done | bytes 262176 | tf_op jit(solution)/shard_map/ppermute | solution.py:26
  85.2 10.4 %collective-permute-done.20 = bf16[512,256]{1,0:T(8,128)(2,1)S(1)} collective-permute-done((bf16[512,256]{1,0:T(8,128)(2,1)S(1)}, bf16[512,256]{1,0:T(8,128)(2,1)S(1)}, u32[]{:S(2)}, u32[]{:S(2)}) %collective-permute-start.20) | collective-permute-done | bytes 262176 | tf_op jit(solution)/shard_map/ppermute | solution.py:20
  95.7 1.9 %collective-permute-start.21 = (bf16[512,256]{1,0:T(8,128)(2,1)S(1)}, bf16[512,256]{1,0:T(8,128)(2,1)S(1)}, u32[]{:S(2)}, u32[]{:S(2)}) collective-permute-start(bf16[512,256]{1,0:T(8,128)(2,1)S(1)} %add_convert_fusion.5), channel_id=1, source_target_pairs={{0,2},{1,3},{2,4},{3,5},{8,10},{9,11},{10,12},{11,13},{16,18},{17,... | collective-permute-start | bytes 786440 | tf_op jit(solution)/shard_map/ppermute | solution.py:20
  97.6 3.5 %collective-permute-start.23 = (bf16[512,256]{1,0:T(8,128)(2,1)S(1)}, bf16[512,256]{1,0:T(8,128)(2,1)S(1)}, u32[]{:S(2)}, u32[]{:S(2)}) collective-permute-start(bf16[512,256]{1,0:T(8,128)(2,1)S(1)} %get-tuple-element.32), channel_id=1, source_target_pairs={{2,3},{3,2},{4,5},{5,4},{6,7},{7,6},{10,11},{11,10},{12,13},{13,12... | collective-permute-start | bytes 786440 | tf_op jit(solution)/shard_map/ppermute | solution.py:26
  101.2 1.3 %collective-permute-start.27 = (bf16[512,256]{1,0:T(8,128)(2,1)S(1)}, bf16[512,256]{1,0:T(8,128)(2,1)S(1)}, u32[]{:S(2)}, u32[]{:S(2)}) collective-permute-start(bf16[512,256]{1,0:T(8,128)(2,1)S(1)} %add_convert_fusion.2), channel_id=1, source_target_pairs={{4,2},{5,3},{6,4},{7,5},{12,10},{13,11},{14,12},{15,13},{20,18},{2... | collective-permute-start | bytes 786440 | tf_op jit(solution)/shard_map/ppermute | solution.py:20
  103.0 1.4 %collective-permute-done.21 = bf16[512,256]{1,0:T(8,128)(2,1)S(1)} collective-permute-done((bf16[512,256]{1,0:T(8,128)(2,1)S(1)}, bf16[512,256]{1,0:T(8,128)(2,1)S(1)}, u32[]{:S(2)}, u32[]{:S(2)}) %collective-permute-start.21) | collective-permute-done | bytes 262176 | tf_op jit(solution)/shard_map/ppermute | solution.py:20
  104.6 3.1 %collective-permute-start.22 = (bf16[512,256]{1,0:T(8,128)(2,1)S(1)}, bf16[512,256]{1,0:T(8,128)(2,1)S(1)}, u32[]{:S(2)}, u32[]{:S(2)}) collective-permute-start(bf16[512,256]{1,0:T(8,128)(2,1)S(1)} %add_convert_fusion.4), channel_id=1, source_target_pairs={{0,2},{1,3},{2,4},{3,5},{4,6},{5,7},{8,10},{9,11},{10,12},{11,13},... | collective-permute-start | bytes 786440 | tf_op jit(solution)/shard_map/ppermute | solution.py:20
  107.7 1.0 collective-permute-done.23
  108.7 1.0 collective-permute-done.27
  109.8 1.9 %collective-permute-start.28 = (bf16[512,256]{1,0:T(8,128)(2,1)S(1)}, bf16[512,256]{1,0:T(8,128)(2,1)S(1)}, u32[]{:S(2)}, u32[]{:S(2)}) collective-permute-start(bf16[512,256]{1,0:T(8,128)(2,1)S(1)} %add_convert_fusion.1), channel_id=1, source_target_pairs={{2,0},{3,1},{4,2},{5,3},{6,4},{7,5},{10,8},{11,9},{12,10},{13,11},... | collective-permute-start | bytes 786440 | tf_op jit(solution)/shard_map/ppermute | solution.py:20
  112.0 0.8 collective-permute-done.22
  112.8 5.3 %collective-permute-done.28 = bf16[512,256]{1,0:T(8,128)(2,1)S(1)} collective-permute-done((bf16[512,256]{1,0:T(8,128)(2,1)S(1)}, bf16[512,256]{1,0:T(8,128)(2,1)S(1)}, u32[]{:S(2)}, u32[]{:S(2)}) %collective-permute-start.28) | collective-permute-done | bytes 262176 | tf_op jit(solution)/shard_map/ppermute | solution.py:20
  118.1 0.9 add_convert_fusion
  (50 shorter events, 3.4 us)
Async XLA Ops:
  0.0 40.7 %copy-start = (bf16[512,256]{1,0:T(8,128)(2,1)S(1)}, bf16[512,256]{1,0:T(8,128)(2,1)}, u32[]{:S(2)}) copy-start(bf16[512,256]{1,0:T(8,128)(2,1)} %refs_0_.1) | copy-start | bytes 786436
  0.0 40.7 %copy-start.7 = (f32[2]{0:T(128)S(1)}, f32[2]{0:T(128)}, u32[]{:S(2)}) copy-start(f32[2]{0:T(128)} %factor.1) | copy-start | bytes 28
  0.0 10.3 %collective-permute-start = (bf16[512,256]{1,0:T(8,128)(2,1)}, bf16[512,256]{1,0:T(8,128)(2,1)S(1)}, u32[]{:S(2)}, u32[]{:S(2)}) collective-permute-start(bf16[512,256]{1,0:T(8,128)(2,1)} %refs_0_.1), channel_id=1, source_target_pairs={{0,2},{1,3},{2,4},{3,5},{4,6},{5,7},{8,10},{9,11},{10,12},{11,13},... | collective-permute-start | bytes 786440 | tf_op jit(solution)/shard_map/ppermute | solution.py:20
  3.6 10.8 %collective-permute-start.1 = (bf16[512,256]{1,0:T(8,128)(2,1)}, bf16[512,256]{1,0:T(8,128)(2,1)}, u32[]{:S(2)}, u32[]{:S(2)}) collective-permute-start(bf16[512,256]{1,0:T(8,128)(2,1)} %refs_0_.1), channel_id=1, source_target_pairs={{2,0},{3,1},{4,2},{5,3},{6,4},{7,5},{10,8},{11,9},{12,10},{13,11},... | collective-permute-start | bytes 786440 | tf_op jit(solution)/shard_map/ppermute | solution.py:20
  10.3 10.8 %collective-permute-start.2 = (bf16[512,256]{1,0:T(8,128)(2,1)S(1)}, bf16[512,256]{1,0:T(8,128)(2,1)}, u32[]{:S(2)}, u32[]{:S(2)}) collective-permute-start(bf16[512,256]{1,0:T(8,128)(2,1)S(1)} %collective-permute-done.refs_1_), channel_id=1, source_target_pairs={{2,4},{3,5},{4,6},{5,7},{10,12},{11,13},{12,14},{13,15},{18,20},{1... | collective-permute-start | bytes 786440 | tf_op jit(solution)/shard_map/ppermute | solution.py:20
  14.5 9.1 %collective-permute-start.3 = (bf16[512,256]{1,0:T(8,128)(2,1)}, bf16[512,256]{1,0:T(8,128)(2,1)}, u32[]{:S(2)}, u32[]{:S(2)}) collective-permute-start(bf16[512,256]{1,0:T(8,128)(2,1)} %collective-permute-done.1.refs_2_), channel_id=1, source_target_pairs={{2,0},{3,1},{4,2},{5,3},{10,8},{11,9},{12,10},{13,11},{18,16},{19,... | collective-permute-start | bytes 786440 | tf_op jit(solution)/shard_map/ppermute | solution.py:20
  16.4 13.5 %collective-permute-start.6 = (bf16[512,256]{1,0:T(8,128)(2,1)}, bf16[512,256]{1,0:T(8,128)(2,1)S(1)}, u32[]{:S(2)}, u32[]{:S(2)}) collective-permute-start(bf16[512,256]{1,0:T(8,128)(2,1)} %refs_0_.1), channel_id=1, source_target_pairs={{0,1},{1,0},{2,3},{3,2},{4,5},{5,4},{6,7},{7,6},{8,9},{9,8},{10,11... | collective-permute-start | bytes 786440 | tf_op jit(solution)/shard_map/ppermute | solution.py:26
  18.0 15.0 %collective-permute-start.7 = (bf16[512,256]{1,0:T(8,128)(2,1)S(1)}, bf16[512,256]{1,0:T(8,128)(2,1)S(1)}, u32[]{:S(2)}, u32[]{:S(2)}) collective-permute-start(bf16[512,256]{1,0:T(8,128)(2,1)S(1)} %collective-permute-done.refs_1_), channel_id=1, source_target_pairs={{2,3},{3,2},{4,5},{5,4},{6,7},{7,6},{10,11},{11,10},{12,13},{13,12... | collective-permute-start | bytes 786440 | tf_op jit(solution)/shard_map/ppermute | solution.py:26
  20.4 0.7 copy-start.1
  21.1 14.0 %collective-permute-start.4 = (bf16[512,256]{1,0:T(8,128)(2,1)}, bf16[512,256]{1,0:T(8,128)(2,1)}, u32[]{:S(2)}, u32[]{:S(2)}) collective-permute-start(bf16[512,256]{1,0:T(8,128)(2,1)} %collective-permute-done.2.refs_3_), channel_id=1, source_target_pairs={{4,6},{5,7},{12,14},{13,15},{20,22},{21,23},{28,30},{29,31}} | collective-permute-start | bytes 786440 | tf_op jit(solution)/shard_map/ppermute | solution.py:20
  23.6 12.9 %collective-permute-start.5 = (bf16[512,256]{1,0:T(8,128)(2,1)}, bf16[512,256]{1,0:T(8,128)(2,1)}, u32[]{:S(2)}, u32[]{:S(2)}) collective-permute-start(bf16[512,256]{1,0:T(8,128)(2,1)} %collective-permute-done.3.refs_4_), channel_id=1, source_target_pairs={{2,0},{3,1},{10,8},{11,9},{18,16},{19,17},{26,24},{27,25}} | collective-permute-start | bytes 786440 | tf_op jit(solution)/shard_map/ppermute | solution.py:20
  26.5 13.9 %collective-permute-start.8 = (bf16[512,256]{1,0:T(8,128)(2,1)}, bf16[512,256]{1,0:T(8,128)(2,1)}, u32[]{:S(2)}, u32[]{:S(2)}) collective-permute-start(bf16[512,256]{1,0:T(8,128)(2,1)} %collective-permute-done.1.refs_2_), channel_id=1, source_target_pairs={{0,1},{1,0},{2,3},{3,2},{4,5},{5,4},{8,9},{9,8},{10,11},{11,10},{1... | collective-permute-start | bytes 786440 | tf_op jit(solution)/shard_map/ppermute | solution.py:26
  29.9 0.7 copy-start.3
  30.6 10.1 %collective-permute-start.10 = (bf16[512,256]{1,0:T(8,128)(2,1)}, bf16[512,256]{1,0:T(8,128)(2,1)}, u32[]{:S(2)}, u32[]{:S(2)}) collective-permute-start(bf16[512,256]{1,0:T(8,128)(2,1)} %collective-permute-done.3.refs_4_), channel_id=1, source_target_pairs={{0,1},{1,0},{2,3},{3,2},{8,9},{9,8},{10,11},{11,10},{16,17},{17,16... | collective-permute-start | bytes 786440 | tf_op jit(solution)/shard_map/ppermute | solution.py:26
  33.0 0.7 copy-start.5
  33.7 6.9 %collective-permute-start.9 = (bf16[512,256]{1,0:T(8,128)(2,1)}, bf16[512,256]{1,0:T(8,128)(2,1)}, u32[]{:S(2)}, u32[]{:S(2)}) collective-permute-start(bf16[512,256]{1,0:T(8,128)(2,1)} %collective-permute-done.2.refs_3_), channel_id=1, source_target_pairs={{4,5},{5,4},{6,7},{7,6},{12,13},{13,12},{14,15},{15,14},{20,21},{2... | collective-permute-start | bytes 786440 | tf_op jit(solution)/shard_map/ppermute | solution.py:26
  35.1 5.6 %collective-permute-start.11 = (bf16[512,256]{1,0:T(8,128)(2,1)}, bf16[512,256]{1,0:T(8,128)(2,1)}, u32[]{:S(2)}, u32[]{:S(2)}) collective-permute-start(bf16[512,256]{1,0:T(8,128)(2,1)} %collective-permute-done.4.refs_5_), channel_id=1, source_target_pairs={{6,7},{7,6},{14,15},{15,14},{22,23},{23,22},{30,31},{31,30}} | collective-permute-start | bytes 786440 | tf_op jit(solution)/shard_map/ppermute | solution.py:26
  36.4 4.2 %collective-permute-start.12 = (bf16[512,256]{1,0:T(8,128)(2,1)}, bf16[512,256]{1,0:T(8,128)(2,1)}, u32[]{:S(2)}, u32[]{:S(2)}) collective-permute-start(bf16[512,256]{1,0:T(8,128)(2,1)} %collective-permute-done.5.refs_6_), channel_id=1, source_target_pairs={{0,1},{1,0},{8,9},{9,8},{16,17},{17,16},{24,25},{25,24}} | collective-permute-start | bytes 786440 | tf_op jit(solution)/shard_map/ppermute | solution.py:26
  40.7 1.0 copy-start.2
  41.6 0.9 copy-start.4
  42.6 0.9 copy-start.6
  43.5 18.1 %copy-start.8 = (s32[2048]{0:T(1024)S(1)}, s32[2048]{0:T(1024)}, u32[]{:S(2)}) copy-start(s32[2048]{0:T(1024)} %ids.3) | copy-start | bytes 24580
  49.0 0.7 copy-start.9
  49.7 11.9 %collective-permute-start.13 = (bf16[512,512]{1,0:T(8,128)(2,1)}, bf16[512,512]{1,0:T(8,128)(2,1)S(1)}, u32[]{:S(2)}, u32[]{:S(2)}) collective-permute-start(bf16[512,512]{1,0:T(8,128)(2,1)} %get-tuple-element.22.refs_3_), channel_id=1, source_target_pairs={{0,16},{8,24},{16,0},{24,8},{1,17},{9,25},{17,1},{25,9},{2,18},{10... | collective-permute-start | bytes 1572872 | tf_op jit(solution)/shard_map/ppermute | solution.py:287
  50.3 11.8 %collective-permute-start.15 = (bf16[512,512]{1,0:T(8,128)(2,1)}, bf16[512,512]{1,0:T(8,128)(2,1)S(1)}, u32[]{:S(2)}, u32[]{:S(2)}) collective-permute-start(bf16[512,512]{1,0:T(8,128)(2,1)} %get-tuple-element.22.refs_3_), channel_id=1, source_target_pairs={{0,8},{8,0},{16,24},{24,16},{1,9},{9,1},{17,25},{25,17},{2,10},{10... | collective-permute-start | bytes 1572872 | tf_op jit(solution)/shard_map/ppermute | solution.py:294
  61.6 5.9 %collective-permute-start.14 = (bf16[512,512]{1,0:T(8,128)(2,1)S(1)}, bf16[512,512]{1,0:T(8,128)(2,1)S(1)}, u32[]{:S(2)}, u32[]{:S(2)}) collective-permute-start(bf16[512,512]{1,0:T(8,128)(2,1)S(1)} %collective-permute-done.13.refs_3_), channel_id=1, source_target_pairs={{0,8},{8,0},{16,24},{24,16},{1,9},{9,1},{17,25},{25,17},{2,10},{10... | collective-permute-start | bytes 1572872 | tf_op jit(solution)/shard_map/ppermute | solution.py:294
  62.1 1.0 copy-start.10
  66.5 1.0 copy-start.11
  72.8 3.9 %collective-permute-start.19 = (bf16[512,256]{1,0:T(8,128)(2,1)S(1)}, bf16[512,256]{1,0:T(8,128)(2,1)S(1)}, u32[]{:S(2)}, u32[]{:S(2)}) collective-permute-start(bf16[512,256]{1,0:T(8,128)(2,1)S(1)} %get-tuple-element.30), channel_id=1, source_target_pairs={{0,1},{1,0},{8,9},{9,8},{16,17},{17,16},{24,25},{25,24}} | collective-permute-start | bytes 786440 | tf_op jit(solution)/shard_map/ppermute | solution.py:26
  73.5 5.3 %collective-permute-start.25 = (bf16[512,256]{1,0:T(8,128)(2,1)S(1)}, bf16[512,256]{1,0:T(8,128)(2,1)S(1)}, u32[]{:S(2)}, u32[]{:S(2)}) collective-permute-start(bf16[512,256]{1,0:T(8,128)(2,1)S(1)} %get-tuple-element.36), channel_id=1, source_target_pairs={{6,7},{7,6},{14,15},{15,14},{22,23},{23,22},{30,31},{31,30}} | collective-permute-start | bytes 786440 | tf_op jit(solution)/shard_map/ppermute | solution.py:26
  74.2 11.0 %collective-permute-start.18 = (bf16[512,256]{1,0:T(8,128)(2,1)S(1)}, bf16[512,256]{1,0:T(8,128)(2,1)S(1)}, u32[]{:S(2)}, u32[]{:S(2)}) collective-permute-start(bf16[512,256]{1,0:T(8,128)(2,1)S(1)} %get-tuple-element.28), channel_id=1, source_target_pairs={{0,1},{1,0},{2,3},{3,2},{8,9},{9,8},{10,11},{11,10},{16,17},{17,16... | collective-permute-start | bytes 786440 | tf_op jit(solution)/shard_map/ppermute | solution.py:26
  76.8 18.7 %collective-permute-start.20 = (bf16[512,256]{1,0:T(8,128)(2,1)S(1)}, bf16[512,256]{1,0:T(8,128)(2,1)S(1)}, u32[]{:S(2)}, u32[]{:S(2)}) collective-permute-start(bf16[512,256]{1,0:T(8,128)(2,1)S(1)} %add_convert_fusion.6), channel_id=1, source_target_pairs={{0,2},{1,3},{8,10},{9,11},{16,18},{17,19},{24,26},{25,27}} | collective-permute-start | bytes 786440 | tf_op jit(solution)/shard_map/ppermute | solution.py:20
  78.1 23.0 %collective-permute-start.24 = (bf16[512,256]{1,0:T(8,128)(2,1)S(1)}, bf16[512,256]{1,0:T(8,128)(2,1)S(1)}, u32[]{:S(2)}, u32[]{:S(2)}) collective-permute-start(bf16[512,256]{1,0:T(8,128)(2,1)S(1)} %get-tuple-element.34), channel_id=1, source_target_pairs={{4,5},{5,4},{6,7},{7,6},{12,13},{13,12},{14,15},{15,14},{20,21},{2... | collective-permute-start | bytes 786440 | tf_op jit(solution)/shard_map/ppermute | solution.py:26
  78.9 22.2 %collective-permute-start.26 = (bf16[512,256]{1,0:T(8,128)(2,1)S(1)}, bf16[512,256]{1,0:T(8,128)(2,1)S(1)}, u32[]{:S(2)}, u32[]{:S(2)}) collective-permute-start(bf16[512,256]{1,0:T(8,128)(2,1)S(1)} %add_convert_fusion.3), channel_id=1, source_target_pairs={{6,4},{7,5},{14,12},{15,13},{22,20},{23,21},{30,28},{31,29}} | collective-permute-start | bytes 786440 | tf_op jit(solution)/shard_map/ppermute | solution.py:20
  79.6 23.5 %collective-permute-start.17 = (bf16[512,256]{1,0:T(8,128)(2,1)S(1)}, bf16[512,256]{1,0:T(8,128)(2,1)S(1)}, u32[]{:S(2)}, u32[]{:S(2)}) collective-permute-start(bf16[512,256]{1,0:T(8,128)(2,1)S(1)} %get-tuple-element.26), channel_id=1, source_target_pairs={{0,1},{1,0},{2,3},{3,2},{4,5},{5,4},{8,9},{9,8},{10,11},{11,10},{1... | collective-permute-start | bytes 786440 | tf_op jit(solution)/shard_map/ppermute | solution.py:26
  95.7 8.8 %collective-permute-start.21 = (bf16[512,256]{1,0:T(8,128)(2,1)S(1)}, bf16[512,256]{1,0:T(8,128)(2,1)S(1)}, u32[]{:S(2)}, u32[]{:S(2)}) collective-permute-start(bf16[512,256]{1,0:T(8,128)(2,1)S(1)} %add_convert_fusion.5), channel_id=1, source_target_pairs={{0,2},{1,3},{2,4},{3,5},{8,10},{9,11},{10,12},{11,13},{16,18},{17,... | collective-permute-start | bytes 786440 | tf_op jit(solution)/shard_map/ppermute | solution.py:20
  97.6 11.1 %collective-permute-start.23 = (bf16[512,256]{1,0:T(8,128)(2,1)S(1)}, bf16[512,256]{1,0:T(8,128)(2,1)S(1)}, u32[]{:S(2)}, u32[]{:S(2)}) collective-permute-start(bf16[512,256]{1,0:T(8,128)(2,1)S(1)} %get-tuple-element.32), channel_id=1, source_target_pairs={{2,3},{3,2},{4,5},{5,4},{6,7},{7,6},{10,11},{11,10},{12,13},{13,12... | collective-permute-start | bytes 786440 | tf_op jit(solution)/shard_map/ppermute | solution.py:26
  101.2 8.5 %collective-permute-start.27 = (bf16[512,256]{1,0:T(8,128)(2,1)S(1)}, bf16[512,256]{1,0:T(8,128)(2,1)S(1)}, u32[]{:S(2)}, u32[]{:S(2)}) collective-permute-start(bf16[512,256]{1,0:T(8,128)(2,1)S(1)} %add_convert_fusion.2), channel_id=1, source_target_pairs={{4,2},{5,3},{6,4},{7,5},{12,10},{13,11},{14,12},{15,13},{20,18},{2... | collective-permute-start | bytes 786440 | tf_op jit(solution)/shard_map/ppermute | solution.py:20
  102.5 9.5 %collective-permute-start.16 = (bf16[512,256]{1,0:T(8,128)(2,1)S(1)}, bf16[512,256]{1,0:T(8,128)(2,1)S(1)}, u32[]{:S(2)}, u32[]{:S(2)}) collective-permute-start(bf16[512,256]{1,0:T(8,128)(2,1)S(1)} %get-tuple-element.24), channel_id=1, source_target_pairs={{0,1},{1,0},{2,3},{3,2},{4,5},{5,4},{6,7},{7,6},{8,9},{9,8},{10,11... | collective-permute-start | bytes 786440 | tf_op jit(solution)/shard_map/ppermute | solution.py:26
  104.6 8.3 %collective-permute-start.22 = (bf16[512,256]{1,0:T(8,128)(2,1)S(1)}, bf16[512,256]{1,0:T(8,128)(2,1)S(1)}, u32[]{:S(2)}, u32[]{:S(2)}) collective-permute-start(bf16[512,256]{1,0:T(8,128)(2,1)S(1)} %add_convert_fusion.4), channel_id=1, source_target_pairs={{0,2},{1,3},{2,4},{3,5},{4,6},{5,7},{8,10},{9,11},{10,12},{11,13},... | collective-permute-start | bytes 786440 | tf_op jit(solution)/shard_map/ppermute | solution.py:20
  109.8 8.3 %collective-permute-start.28 = (bf16[512,256]{1,0:T(8,128)(2,1)S(1)}, bf16[512,256]{1,0:T(8,128)(2,1)S(1)}, u32[]{:S(2)}, u32[]{:S(2)}) collective-permute-start(bf16[512,256]{1,0:T(8,128)(2,1)S(1)} %add_convert_fusion.1), channel_id=1, source_target_pairs={{2,0},{3,1},{4,2},{5,3},{6,4},{7,5},{10,8},{11,9},{12,10},{13,11},... | collective-permute-start | bytes 786440 | tf_op jit(solution)/shard_map/ppermute | solution.py:20

commit v2 on v1

v2 whole, which is shorter than its diff:
```python
import functools
import math

import jax
import jax.numpy as jnp
from jax import lax
from jax.experimental import pallas as pl
from jax.experimental.pallas import tpu as pltpu
from jax.sharding import PartitionSpec as P

LOG2E = math.log2(math.e)
VMEM = pl.BlockSpec(memory_space=pltpu.VMEM)
SMEM = pl.BlockSpec(memory_space=pltpu.SMEM)
F32 = jnp.float32
BF16 = jnp.bfloat16


def ring_order(count):
    line = count // 2
    return [2 * z for z in range(line)] + [2 * z + 1 for z in reversed(range(line))]


def ring_place(index, count):
    return jnp.where(index % 2 == 0, index // 2, count - 1 - index // 2)


def ring_index(place, count):
    return jnp.where(place < count // 2, 2 * place, 2 * (count - 1 - place) + 1)


def along(value, step, count):
    order = ring_order(count)
    return lax.ppermute(
        value, "head", [(order[p], order[(p + step) % count]) for p in range(count)]
    )


def gather_kernel(count, has_acc, head_size, at, factor, *refs):
    blocks, gains, weights = refs[:count], refs[count : 2 * count], refs[2 * count : 3 * count]
    rest = refs[3 * count :]
    if has_acc:
        acc_in, power_in = rest[:2]
        rest = rest[2:]
    rows, width = blocks[0].shape
    groups, _, out_width = weights[0].shape
    tile = math.gcd(rows, 128)

    @pl.loop(0, rows // tile)
    def _(index):
        here = pl.ds(pl.multiple_of(index * tile, tile), tile)
        power = power_in[here, :] if has_acc else None
        scaled = []
        for block, gain in zip(blocks, gains):
            values = block[here, :].astype(F32)
            scaled.append((values * gain[0]).astype(BF16))
            square = values * values
            for lane in range(0, width, 128):
                piece = square[:, lane : lane + 128]
                power = piece if power is None else power + piece
        sums = []
        for group in range(groups):
            total = acc_in[here, group * out_width : (group + 1) * out_width] if has_acc else None
            for x, w_ref in zip(scaled, weights):
                product = jnp.dot(x, w_ref[group], preferred_element_type=F32)
                total = product if total is None else total + product
            sums.append(total)
        if head_size is None:
            acc, power_out = rest
            for group, total in enumerate(sums):
                acc[here, group * out_width : (group + 1) * out_width] = total
            power_out[here, :] = power
        else:
            q_ref, kv_ref = rest
            mean = jnp.sum(power, axis=-1, keepdims=True) * factor[out_width // head_size]
            scale = lax.rsqrt(mean + 1e-06)
            q, k, v = (total * scale for total in sums)
            for head in range(out_width // head_size):
                lanes = slice(head * head_size, (head + 1) * head_size)
                qh, kh = q[:, lanes], k[:, lanes]
                q_size = lax.rsqrt(jnp.sum(qh * qh, axis=-1, keepdims=True) + 1e-06)
                k_size = lax.rsqrt(jnp.sum(kh * kh, axis=-1, keepdims=True) + 1e-06)
                q_ref[here, lanes] = (qh * (q_size * (factor[head] * LOG2E))).astype(BF16)
                kv_ref[here, lanes] = (kh * k_size).astype(BF16)
            kv_ref[here, out_width:] = v.astype(BF16)


def gather_step(at, factor, blocks, gain, weights, state, head_size=None):
    rows, width = blocks[0].shape
    groups, depth, out_width = weights.shape
    count = len(blocks)
    whole = lambda shape: pl.BlockSpec(shape, lambda i, at, factor: (0, 0))
    in_specs = [whole((rows, width))] * count
    in_specs += [
        pl.BlockSpec((1, 1, width), lambda i, at, factor, n=n: (at[n], 0, 0)) for n in range(count)
    ]
    in_specs += [
        pl.BlockSpec((groups, width, out_width), lambda i, at, factor, n=n: (0, at[n], 0))
        for n in range(count)
    ]
    shapes = [(rows, groups * out_width), (rows, 128)]
    if state is not None:
        in_specs += [whole(shape) for shape in shapes]
    kinds = [F32, F32]
    if head_size is not None:
        shapes, kinds = [(rows, out_width), (rows, 2 * out_width)], [BF16, BF16]
    return pl.pallas_call(
        functools.partial(gather_kernel, count, state is not None, head_size),
        out_shape=tuple(jax.ShapeDtypeStruct(s, kind) for s, kind in zip(shapes, kinds)),
        grid_spec=pltpu.PrefetchScalarGridSpec(
            num_scalar_prefetch=2,
            grid=(1,),
            in_specs=in_specs,
            out_specs=tuple(whole(shape) for shape in shapes),
        ),
        compiler_params=pltpu.CompilerParams(vmem_limit_bytes=32 << 20),
        cost_estimate=pl.CostEstimate(
            flops=2 * rows * width * count * groups * out_width,
            bytes_accessed=2 * width * count * (rows + groups * out_width)
            + 8 * rows * groups * out_width,
            transcendentals=0,
        ),
        name="gather_step" if head_size is None else "gather_last",
    )(at, factor, *blocks, *[gain] * count, *[weights] * count, *(state or ()))


def attend_blocks(sources, ids, q_first, q_refs, id_col, id_row, kv_refs, v_ones, acc, head_size):
    heads = q_refs[0].shape[1] // head_size
    keys = kv_refs[0].shape[0]
    rows = q_refs[0].shape[0]
    for number, kv_ref in enumerate(kv_refs):
        for head in range(heads):
            start = (heads + head) * head_size
            v_ones[head, :, :head_size] = kv_ref[:, start : start + head_size]
            v_ones[head, :, head_size:] = jnp.ones((keys, head_size), BF16)
        first = sources[number]
        key_low, key_high = ids[first], ids[first + keys - 1]
        tile = math.gcd(rows, 256)
        for chunk, q_ref in enumerate(q_refs):

            @pl.loop(0, rows // tile)
            def _(index):
                here = pl.ds(pl.multiple_of(index * tile, tile), tile)
                base = chunk * rows + index * tile
                there = pl.ds(pl.multiple_of(base, tile), tile)
                q_low = ids[q_first + base]
                q_high = ids[q_first + base + tile - 1]

                def add(masked):
                    if masked:
                        allowed = id_row[first // keys] <= id_col[there, :]
                    for head in range(heads):
                        lanes = slice(head * head_size, (head + 1) * head_size)
                        score = lax.dot_general(
                            q_ref[here, lanes],
                            kv_ref[:, lanes],
                            (((1,), (1,)), ((), ())),
                            preferred_element_type=F32,
                        )
                        weight = jnp.exp2(score)
                        if masked:
                            weight = jnp.where(allowed, weight, 0.0)
                        wide = slice(2 * head * head_size, 2 * (head + 1) * head_size)
                        acc[there, wide] += jnp.dot(
                            weight.astype(BF16), v_ones[head], preferred_element_type=F32
                        )

                @pl.when(key_high <= q_low)
                def _():
                    add(False)

                @pl.when((key_high > q_low) & (key_low <= q_high))
                def _():
                    add(True)


def first_kernel(count_q, count_kv, head_size, info, ids, *refs):
    q_refs = refs[:count_q]
    id_col, id_row = refs[count_q : count_q + 2]
    kv_refs = refs[count_q + 2 : count_q + 2 + count_kv]
    acc, v_ones = refs[count_q + 2 + count_kv :]
    acc[...] = jnp.zeros_like(acc)
    sources = [info[1 + number] for number in range(count_kv)]
    attend_blocks(sources, ids, info[0], q_refs, id_col, id_row, kv_refs, v_ones, acc, head_size)


def last_kernel(count_q, count_kv, head_size, count_out, info, ids, *refs):
    q_refs = refs[:count_q]
    id_col, id_row = refs[count_q : count_q + 2]
    kv_refs = refs[count_q + 2 : count_q + 2 + count_kv]
    rest = refs[count_q + 2 + count_kv :]
    acc_in, w_ref = rest[:2]
    outs, (v_ones, acc, attended) = rest[2:-3], rest[-3:]
    acc[...] = acc_in[...]
    sources = [info[count_out + 1 + number] for number in range(count_kv)]
    attend_blocks(sources, ids, info[count_out], q_refs, id_col, id_row, kv_refs, v_ones, acc, head_size)
    heads = q_refs[0].shape[1] // head_size
    for head in range(heads):
        start = 2 * head * head_size
        attended[:, head * head_size : (head + 1) * head_size] = (
            acc[:, start : start + head_size]
            / acc[:, start + head_size : start + 2 * head_size]
        ).astype(BF16)
    width = outs[0].shape[1]
    for number, out in enumerate(outs):
        lane = info[number] * width
        out[...] = jnp.dot(
            attended[...],
            w_ref[:, pl.ds(pl.multiple_of(lane, width), width)],
            preferred_element_type=F32,
        ).astype(BF16)


def attend_first(info, ids, queries, id_col, id_row, kvs, head_size):
    rows, width = queries[0].shape
    total = rows * len(queries)
    keys = kvs[0].shape[0]
    heads = width // head_size
    return pl.pallas_call(
        functools.partial(first_kernel, len(queries), len(kvs), head_size),
        out_shape=jax.ShapeDtypeStruct((total, 2 * width), F32),
        in_specs=[SMEM, SMEM] + [VMEM] * (len(queries) + 2 + len(kvs)),
        out_specs=VMEM,
        scratch_shapes=[pltpu.VMEM((heads, keys, 2 * head_size), BF16)],
        compiler_params=pltpu.CompilerParams(vmem_limit_bytes=48 << 20),
        cost_estimate=pl.CostEstimate(
            flops=6 * total * keys * len(kvs) * width,
            bytes_accessed=4 * keys * len(kvs) * width + 4 * total * width,
            transcendentals=total * keys * len(kvs) * heads,
        ),
        name="attend_first",
    )(info, ids, *queries, id_col, id_row, *kvs)


def attend_last(info, ids, queries, id_col, id_row, kvs, acc, w_out, count_out, head_size):
    rows, width = queries[0].shape
    total = rows * len(queries)
    keys = kvs[0].shape[0]
    heads = width // head_size
    out_width = w_out.shape[1] // count_out
    return pl.pallas_call(
        functools.partial(last_kernel, len(queries), len(kvs), head_size, count_out),
        out_shape=(jax.ShapeDtypeStruct((total, out_width), BF16),) * count_out,
        in_specs=[SMEM, SMEM] + [VMEM] * (len(queries) + 4 + len(kvs)),
        out_specs=(VMEM,) * count_out,
        scratch_shapes=[
            pltpu.VMEM((heads, keys, 2 * head_size), BF16),
            pltpu.VMEM((total, 2 * width), F32),
            pltpu.VMEM((total, width), BF16),
        ],
        compiler_params=pltpu.CompilerParams(vmem_limit_bytes=48 << 20),
        cost_estimate=pl.CostEstimate(
            flops=6 * total * keys * len(kvs) * width + 2 * total * width * w_out.shape[1],
            bytes_accessed=4 * keys * len(kvs) * width + 4 * total * width * 4,
            transcendentals=total * keys * len(kvs) * heads,
        ),
        name="attend_last",
    )(info, ids, *queries, id_col, id_row, *kvs, acc, w_out)


def total_of(*parts):
    return sum(part.astype(F32) for part in parts).astype(BF16)


def body(mesh_shape, tokens, norm_gain, w_qkv, head_scale, w_out, scale_ids):
    ring = mesh_shape["head"]
    outer = mesh_shape["seq"] // 2
    rows, width = tokens.shape
    head_size = w_qkv.shape[2] // head_scale.shape[0]
    head_at, seq_at = lax.axis_index("head"), lax.axis_index("seq")
    place = ring_place(head_at, ring)
    chip, core = seq_at // 2, seq_at % 2
    index_at = lambda offset: ring_index((place + offset + ring) % ring, ring)

    id_row = scale_ids.reshape(-1, 1, rows)
    id_col = lax.dynamic_slice_in_dim(scale_ids, seq_at * rows, rows)[:, None]

    ahead, behind = ring // 2, ring - 1 - ring // 2
    gain = norm_gain.reshape(ring, 1, width)
    factor = jnp.concatenate([head_scale, jnp.full((1,), 1.0 / (ring * width), F32)])
    state, held_up, held_down = None, tokens, tokens
    blocks, offsets = [tokens], [0]
    for step in range(1, ahead + 1):
        held_up = along(held_up, 1, ring)
        blocks.append(held_up)
        offsets.append(-step)
        if step <= behind:
            held_down = along(held_down, -1, ring)
            blocks.append(held_down)
            offsets.append(step)
        if step in (1, ahead - 1, ahead):
            at = jnp.stack([index_at(offset) for offset in offsets]).astype(jnp.int32)
            state = gather_step(
                at, factor, blocks, gain, w_qkv, state, head_size if step == ahead else None
            )
            blocks, offsets = [], []
    query, kv = state

    swap = [(2 * a + b, 2 * a + 1 - b) for a in range(outer) for b in (0, 1)]
    near, near_at, far, far_at = [], [], [], []
    for step in range(outer):
        held = kv
        if step:
            shift = [(2 * a + b, 2 * ((a + step) % outer) + b) for a in range(outer) for b in (0, 1)]
            held = lax.ppermute(kv, "seq", shift)
        source = 2 * ((chip + outer - step) % outer)
        group, group_at = (far, far_at) if step else (near, near_at)
        group.append(held)
        group_at.append((source + core) * rows)
        group_at.append((source + 1 - core) * rows)
        if not step:
            group.append(lax.ppermute(held, "seq", swap))
    near_info = jnp.stack([seq_at * rows] + near_at).astype(jnp.int32)
    acc = attend_first(near_info, scale_ids, [query], id_col, id_row, near, head_size)
    acc, *far = lax.optimization_barrier((acc, *far))
    far = [data for held in far for data in (held, lax.ppermute(held, "seq", swap))]

    goals = list(range(ahead, 0, -1)) + list(range(-behind, 0)) + [0]
    far_info = jnp.stack([index_at(goal) for goal in goals] + [seq_at * rows] + far_at)
    parts = attend_last(
        far_info.astype(jnp.int32),
        scale_ids, [query], id_col, id_row, far, acc, w_out, ring, head_size,
    )
    up = along(parts[0], 1, ring)
    down = along(parts[ahead], -1, ring)
    for step in range(1, ahead):
        up = along(total_of(parts[step], up), 1, ring)
        if step < behind:
            down = along(total_of(parts[ahead + step], down), -1, ring)
    return total_of(parts[-1], up, down)


def solution(mesh):
    placed = (P("seq", "head"), P(), P(None, None, "head"), P("head"), P("head", None), P())
    return jax.shard_map(
        functools.partial(body, dict(mesh.shape)),
        mesh=mesh,
        in_specs=placed,
        out_specs=P("seq", "head"),
        check_vma=False,
    )
```

time: 121 us -> 87.9 us (0.73)
  the two profiles are of different devices: /device:TPU:10 before, /device:TPU:0 now
where the time goes in v2:
time: 87.9 us; the launch traced here: 87.7 us
  waiting for transfers between devices  50.6 us (58%)
  starting transfers between devices  18.4 us (21%)
  Pallas kernels  10.2 us (12%)
  local copies, waits for them, and re-layouts  6.09 us (7%)
  other arithmetic  2.12 us (2%)
    ppermute x14, waiting for transfers between devices, along(): lax.ppermute(value, 'head', [(order[p], order[(p + step) % count]) for p...  39.9 us
    ppermute x14, starting transfers between devices, along(): lax.ppermute(value, 'head', [(order[p], order[(p + step) % count]) for p...  16.8 us
    ppermute x1, waiting for transfers between devices, body(): held = lax.ppermute(kv, 'seq', shift)  8.84 us
    pallas_call x3, Pallas kernels, gather_step(): pl.pallas_call(functools.partial(gather_kernel, count, state is not None,...  5.97 us
    unnamed x16, local copies, waits for them, and re-layouts  5.78 us
    pallas_call x1, Pallas kernels, attend_first(): pl.pallas_call(functools.partial(first_kernel, len(queries), len(kvs), he...  2.58 us
    ppermute x1, waiting for transfers between devices, body(): lax.ppermute(held, 'seq', swap)  1.82 us
  transfers between devices with their start and end apart: 17, of which 10 were waited for; matrix products, arithmetic and copies ran while one was open for 2% of the time, Pallas kernels for 8%

profile of v2, /device:TPU:0, one launch (start us, length us, event | category | flops | bytes accessed | tf_op | source)
XLA Modules:
  0.0 87.7 jit_solution(13190911797535358657)
XLA Ops:
  0.0 3.0 %collective-permute-start = (bf16[512,256]{1,0:T(8,128)(2,1)}, bf16[512,256]{1,0:T(8,128)(2,1)S(1)}, u32[]{:S(2)}, u32[]{:S(2)}) collective-permute-start(bf16[512,256]{1,0:T(8,128)(2,1)} %refs_0_.1), channel_id=1, source_target_pairs={{0,2},{2,4},{4,6},{6,7},{7,5},{5,3},{3,1},{1,0},{8,10},{10,12},{12... | collective-permute-start | bytes 786440 | tf_op jit(solution)/shard_map/ppermute | solution.py:33
  3.0 6.5 %collective-permute-done.refs_1_ = bf16[512,256]{1,0:T(8,128)(2,1)S(1)} collective-permute-done((bf16[512,256]{1,0:T(8,128)(2,1)}, bf16[512,256]{1,0:T(8,128)(2,1)S(1)}, u32[]{:S(2)}, u32[]{:S(2)}) %collective-permute-start) | collective-permute-done | bytes 262176 | tf_op jit(solution)/shard_map/ppermute | solution.py:33
  9.5 1.8 %collective-permute-start.1 = (bf16[512,256]{1,0:T(8,128)(2,1)S(1)}, bf16[512,256]{1,0:T(8,128)(2,1)S(1)}, u32[]{:S(2)}, u32[]{:S(2)}) collective-permute-start(bf16[512,256]{1,0:T(8,128)(2,1)S(1)} %collective-permute-done.refs_1_), channel_id=1, source_target_pairs={{0,2},{2,4},{4,6},{6,7},{7,5},{5,3},{3,1},{1,0},{8,10},{10,12},{12... | collective-permute-start | bytes 786440 | tf_op jit(solution)/shard_map/ppermute | solution.py:33
  11.3 0.2 collective-permute-start.5
  11.5 5.5 %collective-permute-done.1.refs_0_ = bf16[512,256]{1,0:T(8,128)(2,1)S(1)} collective-permute-done((bf16[512,256]{1,0:T(8,128)(2,1)S(1)}, bf16[512,256]{1,0:T(8,128)(2,1)S(1)}, u32[]{:S(2)}, u32[]{:S(2)}) %collective-permute-start.1) | collective-permute-done | bytes 262176 | tf_op jit(solution)/shard_map/ppermute | solution.py:33
  17.0 1.5 %collective-permute-start.2 = (bf16[512,256]{1,0:T(8,128)(2,1)S(1)}, bf16[512,256]{1,0:T(8,128)(2,1)S(1)}, u32[]{:S(2)}, u32[]{:S(2)}) collective-permute-start(bf16[512,256]{1,0:T(8,128)(2,1)S(1)} %collective-permute-done.1.refs_0_), channel_id=1, source_target_pairs={{0,2},{2,4},{4,6},{6,7},{7,5},{5,3},{3,1},{1,0},{8,10},{10,12},{12... | collective-permute-start | bytes 786440 | tf_op jit(solution)/shard_map/ppermute | solution.py:33
  18.5 0.7 pad_maximum_fusion.factor
  19.2 0.5 collective-permute-start.6
  19.7 3.8 %collective-permute-done.2.refs_2_ = bf16[512,256]{1,0:T(8,128)(2,1)S(1)} collective-permute-done((bf16[512,256]{1,0:T(8,128)(2,1)S(1)}, bf16[512,256]{1,0:T(8,128)(2,1)S(1)}, u32[]{:S(2)}, u32[]{:S(2)}) %collective-permute-start.2) | collective-permute-done | bytes 262176 | tf_op jit(solution)/shard_map/ppermute | solution.py:33
  23.5 1.7 %collective-permute-start.3 = (bf16[512,256]{1,0:T(8,128)(2,1)S(1)}, bf16[512,256]{1,0:T(8,128)(2,1)S(1)}, u32[]{:S(2)}, u32[]{:S(2)}) collective-permute-start(bf16[512,256]{1,0:T(8,128)(2,1)S(1)} %collective-permute-done.2.refs_2_), channel_id=1, source_target_pairs={{0,2},{2,4},{4,6},{6,7},{7,5},{5,3},{3,1},{1,0},{8,10},{10,12},{12... | collective-permute-start | bytes 786440 | tf_op jit(solution)/shard_map/ppermute | solution.py:33
  25.3 0.1 pad_add_fusion.1.at
  25.4 0.1 pad_add_fusion.at
  25.5 1.9 %copy-done = bf16[3,2048,256]{2,1,0:T(8,128)(2,1)S(1)} copy-done((bf16[3,2048,256]{2,1,0:T(8,128)(2,1)S(1)}, bf16[3,2048,256]{2,1,0:T(8,128)(2,1)}, u32[]{:S(2)}) %copy-start) | copy-done | bytes 3145752
  27.4 0.7 copy-done.2
  28.1 0.9 %copy-done.3 = bf16[512,256]{1,0:T(8,128)(2,1)S(1)} copy-done((bf16[512,256]{1,0:T(8,128)(2,1)S(1)}, bf16[512,256]{1,0:T(8,128)(2,1)}, u32[]{:S(2)}) %copy-start.3) | copy-done | bytes 262168
  29.0 1.9 %gather_step.2 = (f32[512,768]{1,0:T(8,128)S(1)}, f32[512,128]{1,0:T(8,128)S(1)}) custom-call(s32[3]{0:T(128)S(1)} %pad_add_fusion.1.at, f32[3]{0:T(128)S(1)} %pad_maximum_fusion.factor, bf16[512,256]{1,0:T(8,128)(2,1)S(1)} %copy-done.3, bf16[512,256]{1,0:T(8,128)(2,1)S(1)} %collective-permute-done.refs_1_, ...), custom_call_target="tpu_custom_call" | custom-call | flops 603979776 | bytes 5111808 | tf_op jit(solution)/shard_map/gather_step/pallas_call | solution.py:106
  31.0 2.2 %gather_step.3 = (f32[512,768]{1,0:T(8,128)S(1)}, f32[512,128]{1,0:T(8,128)S(1)}) custom-call(s32[4]{0:T(128)S(1)} %pad_add_fusion.at, f32[3]{0:T(128)S(1)} %pad_maximum_fusion.factor, bf16[512,256]{1,0:T(8,128)(2,1)S(1)} %collective-permute-done.1.refs_0_, bf16[512,256]{1,0:T(8,128)(2,1)S(1)} %collective-permute-done.5.refs_1_, ...), custom_call_target="tpu_custom_call" | custom-call | flops 805306368 | bytes 5767168 | tf_op jit(solution)/shard_map/gather_step/pallas_call | solution.py:106
  33.2 1.8 %gather_last.1 = (bf16[512,256]{1,0:T(8,128)(2,1)S(1)}, bf16[512,512]{1,0:T(8,128)(2,1)S(1)}) custom-call(s32[1]{0:T(128)} %bitcast.11.at, f32[3]{0:T(128)S(1)} %pad_maximum_fusion.factor, bf16[512,256]{1,0:T(8,128)(2,1)S(1)} %collective-permute-done.3.refs_0_, f32[8,1,256]{2,1,0:T(1,128)S(1)} %bitcast.24, bf16[3,2048,256]{2,1,0:T(8,128)(2,1)S(1)} %copy-done.1, ...), custom_call_target="tpu_custom_call" | custom-call | flops 201326592 | bytes 3801088 | tf_op jit(solution)/shard_map/gather_last/pallas_call | solution.py:106
  35.1 0.1 collective-permute-start.7
  35.1 1.6 %collective-permute-start.8 = (bf16[512,512]{1,0:T(8,128)(2,1)S(1)}, bf16[512,512]{1,0:T(8,128)(2,1)S(1)}, u32[]{:S(2)}, u32[]{:S(2)}) collective-permute-start(bf16[512,512]{1,0:T(8,128)(2,1)S(1)} %get-tuple-element.26.refs_3_), channel_id=1, source_target_pairs={{0,16},{8,24},{16,0},{24,8},{1,17},{9,25},{17,1},{25,9},{2,18},{10... | collective-permute-start | bytes 1572872 | tf_op jit(solution)/shard_map/ppermute | solution.py:304
  36.7 0.1 dynamic_slice.3
  36.8 0.1 copy.8.refs_1_
  36.9 0.1 pad_add_fusion.2.info
  37.0 2.6 %attend_first.1.refs_5_ = f32[512,512]{1,0:T(8,128)S(1)} custom-call(s32[3]{0:T(128)S(1)} %pad_add_fusion.2.info, s32[2048]{0:T(1024)S(1)} %copy-done.4, bf16[512,256]{1,0:T(8,128)(2,1)S(1)} %get-tuple-element.25.refs_0_, s32[512,1]{1,0:T(8,128)S(1)} %copy.8.refs_1_, s32[4,1,512]{2,1,0:T(1,128)S(1)} %bitcast.25, ...), custom_call_target="tpu_custom_call" | custom-call | flops 805306368 | bytes 1572864 | tf_op jit(solution)/shard_map/attend_first/pallas_call | solution.py:218
  39.6 1.0 %copy-done.6 = f32[512,512]{1,0:T(8,128)} copy-done((f32[512,512]{1,0:T(8,128)}, f32[512,512]{1,0:T(8,128)S(1)}, u32[]{:S(2)}) %copy-start.6) | copy-done | bytes 1048600
  40.6 8.8 %collective-permute-done.8.refs_3_ = bf16[512,512]{1,0:T(8,128)(2,1)S(1)} collective-permute-done((bf16[512,512]{1,0:T(8,128)(2,1)S(1)}, bf16[512,512]{1,0:T(8,128)(2,1)S(1)}, u32[]{:S(2)}, u32[]{:S(2)}) %collective-permute-start.8) | collective-permute-done | bytes 524320 | tf_op jit(solution)/shard_map/ppermute | solution.py:304
  49.5 0.1 stack.73.info
  49.6 1.8 %collective-permute-done.9.refs_4_ = bf16[512,512]{1,0:T(8,128)(2,1)S(1)} collective-permute-done((bf16[512,512]{1,0:T(8,128)(2,1)S(1)}, bf16[512,512]{1,0:T(8,128)(2,1)S(1)}, u32[]{:S(2)}, u32[]{:S(2)}) %collective-permute-start.9) | collective-permute-done | bytes 524320 | tf_op jit(solution)/shard_map/ppermute | solution.py:315
  51.4 1.2 %copy-done.7 = f32[512,512]{1,0:T(8,128)S(1)} copy-done((f32[512,512]{1,0:T(8,128)S(1)}, f32[512,512]{1,0:T(8,128)}, u32[]{:S(2)}) %copy-start.7) | copy-done | bytes 1048600
  52.6 1.7 %attend_last.1 = (bf16[512,256]{1,0:T(8,128)(2,1)S(1)}, bf16[512,256]{1,0:T(8,128)(2,1)S(1)}, bf16[512,256]{1,0:T(8,128)(2,1)S(1)}, bf16[512,256]{1,0:T(8,128)(2...) custom-call(s32[11]{0:T(128)S(1)} %stack.73.info, ...), custom_call_target="tpu_custom_call" | custom-call | flops 1342177280 | bytes 3145728 | tf_op jit(solution)/shard_map/attend_last/pallas_call | solution.py:240
  54.3 1.6 %collective-permute-start.10 = (bf16[512,256]{1,0:T(8,128)(2,1)S(1)}, bf16[512,256]{1,0:T(8,128)(2,1)S(1)}, u32[]{:S(2)}, u32[]{:S(2)}) collective-permute-start(bf16[512,256]{1,0:T(8,128)(2,1)S(1)} %get-tuple-element.33), channel_id=1, source_target_pairs={{0,2},{2,4},{4,6},{6,7},{7,5},{5,3},{3,1},{1,0},{8,10},{10,12},{12... | collective-permute-start | bytes 786440 | tf_op jit(solution)/shard_map/ppermute | solution.py:33
  55.9 0.5 collective-permute-start.14
  56.4 6.9 %collective-permute-done.10 = bf16[512,256]{1,0:T(8,128)(2,1)S(1)} collective-permute-done((bf16[512,256]{1,0:T(8,128)(2,1)S(1)}, bf16[512,256]{1,0:T(8,128)(2,1)S(1)}, u32[]{:S(2)}, u32[]{:S(2)}) %collective-permute-start.10) | collective-permute-done | bytes 262176 | tf_op jit(solution)/shard_map/ppermute | solution.py:33
  63.3 0.1 add_convert_fusion.5
  63.4 1.6 %collective-permute-start.11 = (bf16[512,256]{1,0:T(8,128)(2,1)S(1)}, bf16[512,256]{1,0:T(8,128)(2,1)S(1)}, u32[]{:S(2)}, u32[]{:S(2)}) collective-permute-start(bf16[512,256]{1,0:T(8,128)(2,1)S(1)} %add_convert_fusion.5), channel_id=1, source_target_pairs={{0,2},{2,4},{4,6},{6,7},{7,5},{5,3},{3,1},{1,0},{8,10},{10,12},{12... | collective-permute-start | bytes 786440 | tf_op jit(solution)/shard_map/ppermute | solution.py:33
  65.0 0.1 collective-permute-done.14
  65.1 0.1 add_convert_fusion.2
  65.2 0.5 collective-permute-start.15
  65.7 6.3 %collective-permute-done.11 = bf16[512,256]{1,0:T(8,128)(2,1)S(1)} collective-permute-done((bf16[512,256]{1,0:T(8,128)(2,1)S(1)}, bf16[512,256]{1,0:T(8,128)(2,1)S(1)}, u32[]{:S(2)}, u32[]{:S(2)}) %collective-permute-start.11) | collective-permute-done | bytes 262176 | tf_op jit(solution)/shard_map/ppermute | solution.py:33
  72.0 0.1 add_convert_fusion.4
  72.1 1.6 %collective-permute-start.12 = (bf16[512,256]{1,0:T(8,128)(2,1)S(1)}, bf16[512,256]{1,0:T(8,128)(2,1)S(1)}, u32[]{:S(2)}, u32[]{:S(2)}) collective-permute-start(bf16[512,256]{1,0:T(8,128)(2,1)S(1)} %add_convert_fusion.4), channel_id=1, source_target_pairs={{0,2},{2,4},{4,6},{6,7},{7,5},{5,3},{3,1},{1,0},{8,10},{10,12},{12... | collective-permute-start | bytes 786440 | tf_op jit(solution)/shard_map/ppermute | solution.py:33
  73.7 0.1 add_convert_fusion.1
  73.8 0.5 collective-permute-start.16
  74.3 5.6 %collective-permute-done.12 = bf16[512,256]{1,0:T(8,128)(2,1)S(1)} collective-permute-done((bf16[512,256]{1,0:T(8,128)(2,1)S(1)}, bf16[512,256]{1,0:T(8,128)(2,1)S(1)}, u32[]{:S(2)}, u32[]{:S(2)}) %collective-permute-start.12) | collective-permute-done | bytes 262176 | tf_op jit(solution)/shard_map/ppermute | solution.py:33
  79.9 0.1 add_convert_fusion.3
  80.0 1.6 %collective-permute-start.13 = (bf16[512,256]{1,0:T(8,128)(2,1)S(1)}, bf16[512,256]{1,0:T(8,128)(2,1)S(1)}, u32[]{:S(2)}, u32[]{:S(2)}) collective-permute-start(bf16[512,256]{1,0:T(8,128)(2,1)S(1)} %add_convert_fusion.3), channel_id=1, source_target_pairs={{0,2},{2,4},{4,6},{6,7},{7,5},{5,3},{3,1},{1,0},{8,10},{10,12},{12... | collective-permute-start | bytes 786440 | tf_op jit(solution)/shard_map/ppermute | solution.py:33
  81.6 5.3 %collective-permute-done.13 = bf16[512,256]{1,0:T(8,128)(2,1)S(1)} collective-permute-done((bf16[512,256]{1,0:T(8,128)(2,1)S(1)}, bf16[512,256]{1,0:T(8,128)(2,1)S(1)}, u32[]{:S(2)}, u32[]{:S(2)}) %collective-permute-start.13) | collective-permute-done | bytes 262176 | tf_op jit(solution)/shard_map/ppermute | solution.py:33
  86.9 0.8 add_convert_fusion
  (20 shorter events, 0.1 us)
Async XLA Ops:
  0.0 9.5 %collective-permute-start = (bf16[512,256]{1,0:T(8,128)(2,1)}, bf16[512,256]{1,0:T(8,128)(2,1)S(1)}, u32[]{:S(2)}, u32[]{:S(2)}) collective-permute-start(bf16[512,256]{1,0:T(8,128)(2,1)} %refs_0_.1), channel_id=1, source_target_pairs={{0,2},{2,4},{4,6},{6,7},{7,5},{5,3},{3,1},{1,0},{8,10},{10,12},{12... | collective-permute-start | bytes 786440 | tf_op jit(solution)/shard_map/ppermute | solution.py:33
  3.0 8.3 %collective-permute-start.4 = (bf16[512,256]{1,0:T(8,128)(2,1)}, bf16[512,256]{1,0:T(8,128)(2,1)S(1)}, u32[]{:S(2)}, u32[]{:S(2)}) collective-permute-start(bf16[512,256]{1,0:T(8,128)(2,1)} %refs_0_.1), channel_id=1, source_target_pairs={{0,1},{2,0},{4,2},{6,4},{7,6},{5,7},{3,5},{1,3},{8,9},{10,8},{12,1... | collective-permute-start | bytes 786440 | tf_op jit(solution)/shard_map/ppermute | solution.py:33
  9.5 7.5 %collective-permute-start.1 = (bf16[512,256]{1,0:T(8,128)(2,1)S(1)}, bf16[512,256]{1,0:T(8,128)(2,1)S(1)}, u32[]{:S(2)}, u32[]{:S(2)}) collective-permute-start(bf16[512,256]{1,0:T(8,128)(2,1)S(1)} %collective-permute-done.refs_1_), channel_id=1, source_target_pairs={{0,2},{2,4},{4,6},{6,7},{7,5},{5,3},{3,1},{1,0},{8,10},{10,12},{12... | collective-permute-start | bytes 786440 | tf_op jit(solution)/shard_map/ppermute | solution.py:33
  11.3 7.9 %collective-permute-start.5 = (bf16[512,256]{1,0:T(8,128)(2,1)S(1)}, bf16[512,256]{1,0:T(8,128)(2,1)S(1)}, u32[]{:S(2)}, u32[]{:S(2)}) collective-permute-start(bf16[512,256]{1,0:T(8,128)(2,1)S(1)} %collective-permute-done.4.refs_2_), channel_id=1, source_target_pairs={{0,1},{2,0},{4,2},{6,4},{7,6},{5,7},{3,5},{1,3},{8,9},{10,8},{12,1... | collective-permute-start | bytes 786440 | tf_op jit(solution)/shard_map/ppermute | solution.py:33
  17.0 6.6 %collective-permute-start.2 = (bf16[512,256]{1,0:T(8,128)(2,1)S(1)}, bf16[512,256]{1,0:T(8,128)(2,1)S(1)}, u32[]{:S(2)}, u32[]{:S(2)}) collective-permute-start(bf16[512,256]{1,0:T(8,128)(2,1)S(1)} %collective-permute-done.1.refs_0_), channel_id=1, source_target_pairs={{0,2},{2,4},{4,6},{6,7},{7,5},{5,3},{3,1},{1,0},{8,10},{10,12},{12... | collective-permute-start | bytes 786440 | tf_op jit(solution)/shard_map/ppermute | solution.py:33
  19.2 11.8 %collective-permute-start.6 = (bf16[512,256]{1,0:T(8,128)(2,1)S(1)}, bf16[512,256]{1,0:T(8,128)(2,1)S(1)}, u32[]{:S(2)}, u32[]{:S(2)}) collective-permute-start(bf16[512,256]{1,0:T(8,128)(2,1)S(1)} %collective-permute-done.5.refs_1_), channel_id=1, source_target_pairs={{0,1},{2,0},{4,2},{6,4},{7,6},{5,7},{3,5},{1,3},{8,9},{10,8},{12,1... | collective-permute-start | bytes 786440 | tf_op jit(solution)/shard_map/ppermute | solution.py:33
  23.5 9.6 %collective-permute-start.3 = (bf16[512,256]{1,0:T(8,128)(2,1)S(1)}, bf16[512,256]{1,0:T(8,128)(2,1)S(1)}, u32[]{:S(2)}, u32[]{:S(2)}) collective-permute-start(bf16[512,256]{1,0:T(8,128)(2,1)S(1)} %collective-permute-done.2.refs_2_), channel_id=1, source_target_pairs={{0,2},{2,4},{4,6},{6,7},{7,5},{5,3},{3,1},{1,0},{8,10},{10,12},{12... | collective-permute-start | bytes 786440 | tf_op jit(solution)/shard_map/ppermute | solution.py:33
  25.5 1.9 %copy-start = (bf16[3,2048,256]{2,1,0:T(8,128)(2,1)S(1)}, bf16[3,2048,256]{2,1,0:T(8,128)(2,1)}, u32[]{:S(2)}) copy-start(bf16[3,2048,256]{2,1,0:T(8,128)(2,1)} %refs_2_.1) | copy-start | bytes 9437188
  27.4 0.7 copy-start.2
  28.1 0.9 %copy-start.3 = (bf16[512,256]{1,0:T(8,128)(2,1)S(1)}, bf16[512,256]{1,0:T(8,128)(2,1)}, u32[]{:S(2)}) copy-start(bf16[512,256]{1,0:T(8,128)(2,1)} %refs_0_.1) | copy-start | bytes 786436
  29.0 2.0 %copy-start.1 = (bf16[3,2048,256]{2,1,0:T(8,128)(2,1)S(1)}, bf16[3,2048,256]{2,1,0:T(8,128)(2,1)}, u32[]{:S(2)}) copy-start(bf16[3,2048,256]{2,1,0:T(8,128)(2,1)} %refs_2_.1) | copy-start | bytes 9437188
  33.2 3.5 %copy-start.4 = (s32[2048]{0:T(1024)S(1)}, s32[2048]{0:T(1024)}, u32[]{:S(2)}) copy-start(s32[2048]{0:T(1024)} %ids.3) | copy-start | bytes 24580
  35.1 2.0 %collective-permute-start.7 = (bf16[512,512]{1,0:T(8,128)(2,1)S(1)}, bf16[512,512]{1,0:T(8,128)(2,1)S(1)}, u32[]{:S(2)}, u32[]{:S(2)}) collective-permute-start(bf16[512,512]{1,0:T(8,128)(2,1)S(1)} %get-tuple-element.26.refs_3_), channel_id=1, source_target_pairs={{0,8},{8,0},{16,24},{24,16},{1,9},{9,1},{17,25},{25,17},{2,10},{10... | collective-permute-start | bytes 1572872 | tf_op jit(solution)/shard_map/ppermute | solution.py:311
  35.1 14.3 %collective-permute-start.8 = (bf16[512,512]{1,0:T(8,128)(2,1)S(1)}, bf16[512,512]{1,0:T(8,128)(2,1)S(1)}, u32[]{:S(2)}, u32[]{:S(2)}) collective-permute-start(bf16[512,512]{1,0:T(8,128)(2,1)S(1)} %get-tuple-element.26.refs_3_), channel_id=1, source_target_pairs={{0,16},{8,24},{16,0},{24,8},{1,17},{9,25},{17,1},{25,9},{2,18},{10... | collective-permute-start | bytes 1572872 | tf_op jit(solution)/shard_map/ppermute | solution.py:304
  36.9 14.5 %copy-start.5 = (bf16[256,2048]{1,0:T(8,128)(2,1)S(1)}, bf16[256,2048]{1,0:T(8,128)(2,1)}, u32[]{:S(2)}) copy-start(bf16[256,2048]{1,0:T(8,128)(2,1)} %refs_6_.3) | copy-start | bytes 3145732
  39.6 1.0 %copy-start.6 = (f32[512,512]{1,0:T(8,128)}, f32[512,512]{1,0:T(8,128)S(1)}, u32[]{:S(2)}) copy-start(f32[512,512]{1,0:T(8,128)S(1)} %attend_first.1.refs_5_) | copy-start | bytes 3145732
  49.5 1.9 %collective-permute-start.9 = (bf16[512,512]{1,0:T(8,128)(2,1)S(1)}, bf16[512,512]{1,0:T(8,128)(2,1)S(1)}, u32[]{:S(2)}, u32[]{:S(2)}) collective-permute-start(bf16[512,512]{1,0:T(8,128)(2,1)S(1)} %collective-permute-done.8.refs_3_), channel_id=1, source_target_pairs={{0,8},{8,0},{16,24},{24,16},{1,9},{9,1},{17,25},{25,17},{2,10},{10... | collective-permute-start | bytes 1572872 | tf_op jit(solution)/shard_map/ppermute | solution.py:315
  51.4 1.2 %copy-start.7 = (f32[512,512]{1,0:T(8,128)S(1)}, f32[512,512]{1,0:T(8,128)}, u32[]{:S(2)}) copy-start(f32[512,512]{1,0:T(8,128)} %copy-done.6) | copy-start | bytes 3145732
  54.3 9.0 %collective-permute-start.10 = (bf16[512,256]{1,0:T(8,128)(2,1)S(1)}, bf16[512,256]{1,0:T(8,128)(2,1)S(1)}, u32[]{:S(2)}, u32[]{:S(2)}) collective-permute-start(bf16[512,256]{1,0:T(8,128)(2,1)S(1)} %get-tuple-element.33), channel_id=1, source_target_pairs={{0,2},{2,4},{4,6},{6,7},{7,5},{5,3},{3,1},{1,0},{8,10},{10,12},{12... | collective-permute-start | bytes 786440 | tf_op jit(solution)/shard_map/ppermute | solution.py:33
  55.9 9.2 %collective-permute-start.14 = (bf16[512,256]{1,0:T(8,128)(2,1)S(1)}, bf16[512,256]{1,0:T(8,128)(2,1)S(1)}, u32[]{:S(2)}, u32[]{:S(2)}) collective-permute-start(bf16[512,256]{1,0:T(8,128)(2,1)S(1)} %get-tuple-element.36), channel_id=1, source_target_pairs={{0,1},{2,0},{4,2},{6,4},{7,6},{5,7},{3,5},{1,3},{8,9},{10,8},{12,1... | collective-permute-start | bytes 786440 | tf_op jit(solution)/shard_map/ppermute | solution.py:33
  63.4 8.6 %collective-permute-start.11 = (bf16[512,256]{1,0:T(8,128)(2,1)S(1)}, bf16[512,256]{1,0:T(8,128)(2,1)S(1)}, u32[]{:S(2)}, u32[]{:S(2)}) collective-permute-start(bf16[512,256]{1,0:T(8,128)(2,1)S(1)} %add_convert_fusion.5), channel_id=1, source_target_pairs={{0,2},{2,4},{4,6},{6,7},{7,5},{5,3},{3,1},{1,0},{8,10},{10,12},{12... | collective-permute-start | bytes 786440 | tf_op jit(solution)/shard_map/ppermute | solution.py:33
  65.2 8.5 %collective-permute-start.15 = (bf16[512,256]{1,0:T(8,128)(2,1)S(1)}, bf16[512,256]{1,0:T(8,128)(2,1)S(1)}, u32[]{:S(2)}, u32[]{:S(2)}) collective-permute-start(bf16[512,256]{1,0:T(8,128)(2,1)S(1)} %add_convert_fusion.2), channel_id=1, source_target_pairs={{0,1},{2,0},{4,2},{6,4},{7,6},{5,7},{3,5},{1,3},{8,9},{10,8},{12,1... | collective-permute-start | bytes 786440 | tf_op jit(solution)/shard_map/ppermute | solution.py:33
  72.1 7.8 %collective-permute-start.12 = (bf16[512,256]{1,0:T(8,128)(2,1)S(1)}, bf16[512,256]{1,0:T(8,128)(2,1)S(1)}, u32[]{:S(2)}, u32[]{:S(2)}) collective-permute-start(bf16[512,256]{1,0:T(8,128)(2,1)S(1)} %add_convert_fusion.4), channel_id=1, source_target_pairs={{0,2},{2,4},{4,6},{6,7},{7,5},{5,3},{3,1},{1,0},{8,10},{10,12},{12... | collective-permute-start | bytes 786440 | tf_op jit(solution)/shard_map/ppermute | solution.py:33
  73.8 7.8 %collective-permute-start.16 = (bf16[512,256]{1,0:T(8,128)(2,1)S(1)}, bf16[512,256]{1,0:T(8,128)(2,1)S(1)}, u32[]{:S(2)}, u32[]{:S(2)}) collective-permute-start(bf16[512,256]{1,0:T(8,128)(2,1)S(1)} %add_convert_fusion.1), channel_id=1, source_target_pairs={{0,1},{2,0},{4,2},{6,4},{7,6},{5,7},{3,5},{1,3},{8,9},{10,8},{12,1... | collective-permute-start | bytes 786440 | tf_op jit(solution)/shard_map/ppermute | solution.py:33
  80.0 6.9 %collective-permute-start.13 = (bf16[512,256]{1,0:T(8,128)(2,1)S(1)}, bf16[512,256]{1,0:T(8,128)(2,1)S(1)}, u32[]{:S(2)}, u32[]{:S(2)}) collective-permute-start(bf16[512,256]{1,0:T(8,128)(2,1)S(1)} %add_convert_fusion.3), channel_id=1, source_target_pairs={{0,2},{2,4},{4,6},{6,7},{7,5},{5,3},{3,1},{1,0},{8,10},{10,12},{12... | collective-permute-start | bytes 786440 | tf_op jit(solution)/shard_map/ppermute | solution.py:33

commit v3 on v0

v3 whole, which is shorter than its diff:
```python
import functools
import math

import jax
import jax.numpy as jnp
from jax import lax
from jax.experimental import pallas as pl
from jax.experimental.pallas import tpu as pltpu
from jax.sharding import PartitionSpec as P

LOG2E = math.log2(math.e)
VMEM = pl.BlockSpec(memory_space=pltpu.VMEM)
SMEM = pl.BlockSpec(memory_space=pltpu.SMEM)
F32 = jnp.float32
BF16 = jnp.bfloat16


def ring_order(count):
    line = count // 2
    return [2 * z for z in range(line)] + [2 * z + 1 for z in reversed(range(line))]


def ring_place(index, count):
    return jnp.where(index % 2 == 0, index // 2, count - 1 - index // 2)


def ring_index(place, count):
    return jnp.where(place < count // 2, 2 * place, 2 * (count - 1 - place) + 1)


def along(value, step, count):
    order = ring_order(count)
    return lax.ppermute(
        value, "head", [(order[p], order[(p + step) % count]) for p in range(count)]
    )


def gather_kernel(streams, count, has_state, head_size, at, factor, *refs):
    gain_ref, w_hbm = refs[:2]
    per_in = count + (2 if has_state else 0)
    ins = [refs[2 + s * per_in : 2 + (s + 1) * per_in] for s in range(streams)]
    outs = refs[2 + streams * per_in : -2]
    w_ref, sems = refs[-2:]
    width = ins[0][0].shape[1]
    rows = ins[0][0].shape[0]
    groups, out_width = w_hbm.shape[0], w_hbm.shape[2]

    def fetch(n):
        start = pl.multiple_of(at[n] * width, width)
        return pltpu.make_async_copy(w_hbm.at[:, pl.ds(start, width), :], w_ref.at[n], sems.at[n])

    for n in range(count):
        fetch(n).start()
    for n in range(count):
        fetch(n).wait()
    tile = math.gcd(rows, 128)
    for stream in range(streams):
        blocks = ins[stream][:count]
        state = ins[stream][count:]
        out = outs[2 * stream : 2 * stream + 2]

        @pl.loop(0, rows // tile)
        def _(index):
            here = pl.ds(pl.multiple_of(index * tile, tile), tile)
            power = state[1][here, :] if has_state else None
            scaled = []
            for n, block in enumerate(blocks):
                values = block[here, :].astype(F32)
                scaled.append((values * gain_ref[pl.ds(at[n], 1), :]).astype(BF16))
                square = values * values
                for lane in range(0, width, 128):
                    piece = square[:, lane : lane + 128]
                    power = piece if power is None else power + piece
            sums = []
            for group in range(groups):
                total = state[0][here, group * out_width : (group + 1) * out_width] if has_state else None
                for n, x in enumerate(scaled):
                    product = jnp.dot(x, w_ref[n, group], preferred_element_type=F32)
                    total = product if total is None else total + product
                sums.append(total)
            if head_size is None:
                for group, total in enumerate(sums):
                    out[0][here, group * out_width : (group + 1) * out_width] = total
                out[1][here, :] = power
            else:
                mean = jnp.sum(power, axis=-1, keepdims=True) * (1.0 / w_hbm.shape[1])
                scale = lax.rsqrt(mean + 1e-06)
                q, k, v = (total * scale for total in sums)
                for head in range(out_width // head_size):
                    lanes = slice(head * head_size, (head + 1) * head_size)
                    qh, kh = q[:, lanes], k[:, lanes]
                    q_size = lax.rsqrt(jnp.sum(qh * qh, axis=-1, keepdims=True) + 1e-06)
                    k_size = lax.rsqrt(jnp.sum(kh * kh, axis=-1, keepdims=True) + 1e-06)
                    out[0][here, lanes] = (qh * (q_size * (factor[head] * LOG2E))).astype(BF16)
                    out[1][here, lanes] = (kh * k_size).astype(BF16)
                out[1][here, out_width:] = v.astype(BF16)


def gather_step(at, factor, blocks, gain, weights, state, head_size=None):
    streams, count = len(blocks), len(blocks[0])
    rows, width = blocks[0][0].shape
    groups, depth, out_width = weights.shape
    if head_size is None:
        shapes, kinds = [(rows, groups * out_width), (rows, 128)], [F32, F32]
    else:
        shapes, kinds = [(rows, out_width), (rows, 2 * out_width)], [BF16, BF16]
    operands = []
    for stream in range(streams):
        operands += blocks[stream]
        operands += state[stream] if state else ()
    result = pl.pallas_call(
        functools.partial(gather_kernel, streams, count, bool(state), head_size),
        out_shape=tuple(jax.ShapeDtypeStruct(s, k) for s, k in zip(shapes, kinds)) * streams,
        in_specs=[SMEM, SMEM, VMEM, pl.BlockSpec(memory_space=pltpu.HBM)] + [VMEM] * len(operands),
        out_specs=(VMEM,) * (2 * streams),
        scratch_shapes=[
            pltpu.VMEM((count, groups, width, out_width), BF16),
            pltpu.SemaphoreType.DMA((count,)),
        ],
        compiler_params=pltpu.CompilerParams(vmem_limit_bytes=16 << 20),
        cost_estimate=pl.CostEstimate(
            flops=2 * streams * rows * width * count * groups * out_width,
            bytes_accessed=2 * width * count * (streams * rows + groups * out_width)
            + 8 * streams * rows * groups * out_width,
            transcendentals=0,
        ),
        name="gather_step" if head_size is None else "gather_last",
    )(at, factor, gain, weights, *operands)
    return [result[2 * s : 2 * s + 2] for s in range(streams)]


def attend_blocks(sources, ids, q_first, q_refs, id_col, id_row, kv_refs, v_ones, acc, head_size):
    heads = q_refs[0].shape[1] // head_size
    keys = kv_refs[0].shape[0]
    rows = q_refs[0].shape[0]
    for number, kv_ref in enumerate(kv_refs):
        for head in range(heads):
            start = (heads + head) * head_size
            v_ones[head, :, :head_size] = kv_ref[:, start : start + head_size]
            v_ones[head, :, head_size:] = jnp.ones((keys, head_size), BF16)
        first = sources[number]
        key_low, key_high = ids[first], ids[first + keys - 1]
        tile = math.gcd(rows, 256)
        for chunk, q_ref in enumerate(q_refs):

            @pl.loop(0, rows // tile)
            def _(index):
                here = pl.ds(pl.multiple_of(index * tile, tile), tile)
                base = chunk * rows + index * tile
                there = pl.ds(pl.multiple_of(base, tile), tile)
                q_low = ids[q_first + base]
                q_high = ids[q_first + base + tile - 1]

                def add(masked):
                    if masked:
                        allowed = id_row[first // keys] <= id_col[there, :]
                    for head in range(heads):
                        lanes = slice(head * head_size, (head + 1) * head_size)
                        score = lax.dot_general(
                            q_ref[here, lanes],
                            kv_ref[:, lanes],
                            (((1,), (1,)), ((), ())),
                            preferred_element_type=F32,
                        )
                        weight = jnp.exp2(score)
                        if masked:
                            weight = jnp.where(allowed, weight, 0.0)
                        wide = slice(2 * head * head_size, 2 * (head + 1) * head_size)
                        acc[there, wide] += jnp.dot(
                            weight.astype(BF16), v_ones[head], preferred_element_type=F32
                        )

                @pl.when(key_high <= q_low)
                def _():
                    add(False)

                @pl.when((key_high > q_low) & (key_low <= q_high))
                def _():
                    add(True)


def attend_kernel(count_q, count_kv, head_size, has_acc, count_out, info, ids, *refs):
    q_refs, rest = refs[:count_q], refs[count_q:]
    (id_col, id_row), rest = rest[:2], rest[2:]
    kv_refs, rest = rest[:count_kv], rest[count_kv:]
    rows, width = q_refs[0].shape
    if has_acc:
        acc_in, rest = rest[0], rest[1:]
    if count_out:
        w_ref, outs, (v_ones, acc, attended) = rest[0], rest[1:-3], rest[-3:]
    else:
        accs, (v_ones, acc) = rest[:-2], rest[-2:]
    acc[...] = acc_in[...] if has_acc else jnp.zeros_like(acc)
    sources = [info[number] for number in range(count_kv)]
    attend_blocks(
        sources, ids, info[count_kv], q_refs, id_col, id_row, kv_refs, v_ones, acc, head_size
    )
    if not count_out:
        for number, out in enumerate(accs):
            out[...] = acc[number * rows : (number + 1) * rows, :]
        return
    for head in range(width // head_size):
        start = 2 * head * head_size
        attended[:, head * head_size : (head + 1) * head_size] = (
            acc[:, start : start + head_size]
            / acc[:, start + head_size : start + 2 * head_size]
        ).astype(BF16)
    out_width = outs[0].shape[1]
    for number, out in enumerate(outs):
        lane = info[count_kv + 1 + number] * out_width
        out[...] = jnp.dot(
            attended[...],
            w_ref[:, pl.ds(pl.multiple_of(lane, out_width), out_width)],
            preferred_element_type=F32,
        ).astype(BF16)


def attend(info, ids, queries, id_col, id_row, kvs, head_size, acc=None, w_out=None, count_out=0):
    rows, width = queries[0].shape
    total = rows * len(queries)
    keys = kvs[0].shape[0]
    heads = width // head_size
    scratch = [
        pltpu.VMEM((heads, keys, 2 * head_size), BF16),
        pltpu.VMEM((total, 2 * width), F32),
    ]
    operands = [*queries, id_col, id_row, *kvs]
    if acc is not None:
        operands.append(acc)
    if count_out:
        operands.append(w_out)
        scratch.append(pltpu.VMEM((total, width), BF16))
        shape = jax.ShapeDtypeStruct((total, w_out.shape[1] // count_out), BF16)
    else:
        shape = jax.ShapeDtypeStruct((rows, 2 * width), F32)
    outs = count_out or len(queries)
    return pl.pallas_call(
        functools.partial(
            attend_kernel, len(queries), len(kvs), head_size, acc is not None, count_out
        ),
        out_shape=(shape,) * outs,
        in_specs=[SMEM, SMEM] + [VMEM] * len(operands),
        out_specs=(VMEM,) * outs,
        scratch_shapes=scratch,
        compiler_params=pltpu.CompilerParams(
            vmem_limit_bytes=(16 << 20) + 2 * kvs[0].size * 2 * len(kvs)
        ),
        cost_estimate=pl.CostEstimate(
            flops=6 * total * keys * len(kvs) * width + 2 * total * width * width * count_out,
            bytes_accessed=4 * keys * len(kvs) * width + 8 * total * width,
            transcendentals=total * keys * len(kvs) * heads,
        ),
        name="attend_last" if count_out else "attend",
    )(info, ids, *operands)


def total_of(*parts):
    return sum(part.astype(F32) for part in parts).astype(BF16)


def body(mesh_shape, tokens, norm_gain, w_qkv, head_scale, w_out, scale_ids):
    ring = mesh_shape["head"]
    outer = mesh_shape["seq"] // 2
    rows, width = tokens.shape
    half = rows // 2
    head_size = w_qkv.shape[2] // head_scale.shape[0]
    head_at, seq_at = lax.axis_index("head"), lax.axis_index("seq")
    place = ring_place(head_at, ring)
    chip, core = seq_at // 2, seq_at % 2
    index_at = lambda offset: ring_index((place + offset + ring) % ring, ring)
    numbers = lambda values: jnp.stack(values).astype(jnp.int32)

    streams = (0, 1)
    farthest = ring // 2
    reach = [(farthest, farthest - 1), (farthest - 1, farthest)]
    id_row = scale_ids.reshape(-1, 1, half)
    id_col = lax.dynamic_slice_in_dim(scale_ids, seq_at * rows, rows)[:, None]

    gain = norm_gain.reshape(ring, width)
    held = [[tokens[s * half : (s + 1) * half]] * 2 for s in streams]
    waiting, offsets, state = [[held[s][0]] for s in streams], [0], None
    for step in range(1, farthest + 1):
        for s in streams:
            for way, sign in enumerate((1, -1)):
                if step <= reach[s][way]:
                    held[s][way] = along(held[s][way], sign, ring)
        if 2 < step and state is not None:
            held, state = lax.optimization_barrier((held, state))
        for s in streams:
            waiting[s] += [held[s][way] for way in (0, 1) if step <= reach[s][way]]
        offsets += [-step, step] if step < farthest else [-step]
        if step < farthest - 1:
            at = numbers([index_at(offset) for offset in offsets])
            state = gather_step(at, head_scale, waiting, gain, w_qkv, state)
            waiting, offsets = [[] for s in streams], []
    at = numbers([index_at(offset) for offset in offsets])
    query, kv = [], []
    for s in streams:
        ((q, k_v),) = gather_step(
            at, head_scale, waiting[s : s + 1], gain, w_qkv, state[s : s + 1], head_size
        )
        query.append(q)
        kv.append(k_v)

    swap = [(2 * a + b, 2 * a + 1 - b) for a in range(outer) for b in (0, 1)]
    near, near_at, far, far_at = [], [], [], []
    for s in streams:
        for step in range(outer):
            source = 2 * ((chip + outer - step) % outer)
            places = [(source + core) * rows + s * half, (source + 1 - core) * rows + s * half]
            if step:
                shift = [
                    (2 * a + b, 2 * ((a + step) % outer) + b) for a in range(outer) for b in (0, 1)
                ]
                far.append(lax.ppermute(kv[s], "seq", shift))
                far_at += places
            else:
                near += [kv[s], lax.ppermute(kv[s], "seq", swap)]
                near_at += places
    near_info = numbers(near_at + [seq_at * rows])
    accs = attend(near_info, scale_ids, query, id_col, id_row, near, head_size)
    accs, far = lax.optimization_barrier((accs, far))
    far = [data for block in far for data in (block, lax.ppermute(block, "seq", swap))]

    parts, goals = [], []
    for s in streams:
        up, down = reach[s]
        goals = list(range(up, 0, -1)) + list(range(-down, 0)) + [0]
        info = numbers(far_at + [seq_at * rows + s * half] + [index_at(goal) for goal in goals])
        parts.append(
            attend(
                info, scale_ids, [query[s]], id_col[s * half : (s + 1) * half], id_row, far,
                head_size, accs[s], w_out, ring,
            )
        )
    sums = [[None, None] for s in streams]
    for step in range(farthest, 0, -1):
        for s in streams:
            for way, sign in enumerate((1, -1)):
                if step <= reach[s][way]:
                    first = 0 if way == 0 else reach[s][0]
                    part = parts[s][first + reach[s][way] - step]
                    if sums[s][way] is not None:
                        part = total_of(part, sums[s][way])
                    sums[s][way] = along(part, sign, ring)
    return jnp.concatenate([total_of(parts[s][-1], *sums[s]) for s in streams])


def solution(mesh):
    placed = (P("seq", "head"), P(), P(None, None, "head"), P("head"), P("head", None), P())
    return jax.shard_map(
        functools.partial(body, dict(mesh.shape)),
        mesh=mesh,
        in_specs=placed,
        out_specs=P("seq", "head"),
        check_vma=False,
    )
```

time: 189 us -> 105 us (0.56)
  waiting for transfers between devices: 86.4 us -> 27.5 us
  blocking collectives: 42.1 us -> 0 us
  starting transfers between devices: 0.12 us -> 32.3 us
  Pallas kernels: 0 us -> 21.2 us
  between operations: 14.5 us -> 0.31 us
  matrix products: 13 us -> 0 us
  other arithmetic: 14 us -> 2.36 us
  local copies, waits for them, and re-layouts: 15.8 us -> 20.2 us
    all_gather x4 -> x0, waiting for transfers between devices: 85.6 us -> none  [the longest x1 52.5 us: body(): wide = lax.all_gather(tokens, 'head', axis=1, tiled=True)]
    all_to_all x1 -> x0, blocking collectives: 42.1 us -> none  [body(): lax.all_to_all(w_out, 'head', split_axis=1, concat_axis=0, tiled=True)]
    ppermute x0 -> x34, starting transfers between devices: none -> 32.3 us  [the longest x28 29.1 us: along(): lax.ppermute(value, 'head', [(order[p], order[(p + step) % count]) for p...]
    ppermute x0 -> x34, waiting for transfers between devices: none -> 27.5 us  [the longest x28 19.3 us: along(): lax.ppermute(value, 'head', [(order[p], order[(p + step) % count]) for p...]
    pallas_call x0 -> x7, Pallas kernels: none -> 21.2 us  [the longest x3 11.3 us: attend(): pl.pallas_call(functools.partial(attend_kernel, len(queries), len(kvs), h...]
    unnamed x9 -> x66, local copies, waits for them, and re-layouts: 3.43 us -> 17.8 us
    dot_general x4 -> x0, matrix products: 13 us -> none  [the longest x1 3.51 us: body(): jnp.einsum('td,cdf->ctf', normed, w_qkv, preferred_element_type=jnp.float32)]
    reduce_sum x4 -> x0, other arithmetic: 6.85 us -> none  [the longest x1 2.57 us: update(): new_total = totals * shrink + jnp.sum(expo, axis=-1)]
  transfers between devices with their start and end apart: 4 -> 34, of which waited for: 4 -> 17; matrix products, arithmetic and copies ran while one was open for 10% -> 3% of each run, Pallas kernels for 0% -> 14%
where the time goes in v3:
time: 105 us; the launch traced here: 104 us
  starting transfers between devices  32.3 us (31%)
  waiting for transfers between devices  27.5 us (26%)
  Pallas kernels  21.2 us (20%)
  local copies, waits for them, and re-layouts  20.2 us (19%)
  other arithmetic  2.36 us (2%)
    ppermute x28, starting transfers between devices, along(): lax.ppermute(value, 'head', [(order[p], order[(p + step) % count]) for p...  29.1 us
    ppermute x28, waiting for transfers between devices, along(): lax.ppermute(value, 'head', [(order[p], order[(p + step) % count]) for p...  19.3 us
    unnamed x66, local copies, waits for them, and re-layouts  17.8 us
    pallas_call x3, Pallas kernels, attend(): pl.pallas_call(functools.partial(attend_kernel, len(queries), len(kvs), h...  11.3 us
    pallas_call x4, Pallas kernels, gather_step(): pl.pallas_call(functools.partial(gather_kernel, streams, count, bool(stat...  9.91 us
    ppermute x2, waiting for transfers between devices, body(): far.append(lax.ppermute(kv[s], 'seq', shift))  6.99 us
  transfers between devices with their start and end apart: 34, of which 17 were waited for; matrix products, arithmetic and copies ran while one was open for 3% of the time, Pallas kernels for 14%

profile of v3, /device:TPU:10, one launch (start us, length us, event | category | flops | bytes accessed | tf_op | source)
XLA Modules:
  0.0 103.8 jit_solution(4773469148870779417)
XLA Ops:
  0.0 1.0 fusion
  1.5 1.6 %collective-permute-start = (bf16[256,256]{1,0:T(8,128)(2,1)S(1)}, bf16[256,256]{1,0:T(8,128)(2,1)S(1)}, u32[]{:S(2)}, u32[]{:S(2)}) collective-permute-start(bf16[256,256]{1,0:T(8,128)(2,1)S(1)} %get-tuple-element.102.refs_2_), channel_id=1, source_target_pairs={{0,2},{2,4},{4,6},{6,7},{7,5},{5,3},{3,1},{1,0},{8,10},{10,12},{12... | collective-permute-start | bytes 393224 | tf_op jit(solution)/shard_map/ppermute | solution.py:33
  3.5 1.6 %collective-permute-start.6 = (bf16[256,256]{1,0:T(8,128)(2,1)S(1)}, bf16[256,256]{1,0:T(8,128)(2,1)S(1)}, u32[]{:S(2)}, u32[]{:S(2)}) collective-permute-start(bf16[256,256]{1,0:T(8,128)(2,1)S(1)} %get-tuple-element.101.refs_5_), channel_id=1, source_target_pairs={{0,2},{2,4},{4,6},{6,7},{7,5},{5,3},{3,1},{1,0},{8,10},{10,12},{12... | collective-permute-start | bytes 393224 | tf_op jit(solution)/shard_map/ppermute | solution.py:33
  5.1 2.3 %collective-permute-done.9.refs_7_ = bf16[256,256]{1,0:T(8,128)(2,1)S(1)} collective-permute-done((bf16[256,256]{1,0:T(8,128)(2,1)S(1)}, bf16[256,256]{1,0:T(8,128)(2,1)S(1)}, u32[]{:S(2)}, u32[]{:S(2)}) %collective-permute-start.9) | collective-permute-done | bytes 131104 | tf_op jit(solution)/shard_map/ppermute | solution.py:33
  7.9 1.6 %collective-permute-start.1 = (bf16[256,256]{1,0:T(8,128)(2,1)S(1)}, bf16[256,256]{1,0:T(8,128)(2,1)}, u32[]{:S(2)}, u32[]{:S(2)}) collective-permute-start(bf16[256,256]{1,0:T(8,128)(2,1)S(1)} %collective-permute-done.refs_3_), channel_id=1, source_target_pairs={{0,2},{2,4},{4,6},{6,7},{7,5},{5,3},{3,1},{1,0},{8,10},{10,12},{12... | collective-permute-start | bytes 393224 | tf_op jit(solution)/shard_map/ppermute | solution.py:33
  9.5 0.8 collective-permute-done.3.refs_4_
  11.3 1.6 %collective-permute-start.7 = (bf16[256,256]{1,0:T(8,128)(2,1)S(1)}, bf16[256,256]{1,0:T(8,128)(2,1)}, u32[]{:S(2)}, u32[]{:S(2)}) collective-permute-start(bf16[256,256]{1,0:T(8,128)(2,1)S(1)} %collective-permute-done.6.refs_6_), channel_id=1, source_target_pairs={{0,2},{2,4},{4,6},{6,7},{7,5},{5,3},{3,1},{1,0},{8,10},{10,12},{12... | collective-permute-start | bytes 393224 | tf_op jit(solution)/shard_map/ppermute | solution.py:33
  14.3 1.6 %collective-permute-start.2 = (bf16[256,256]{1,0:T(8,128)(2,1)}, bf16[256,256]{1,0:T(8,128)(2,1)}, u32[]{:S(2)}, u32[]{:S(2)}) collective-permute-start(bf16[256,256]{1,0:T(8,128)(2,1)} %collective-permute-done.1.refs_2_), channel_id=1, source_target_pairs={{0,2},{2,4},{4,6},{6,7},{7,5},{5,3},{3,1},{1,0},{8,10},{10,12},{12... | collective-permute-start | bytes 393224 | tf_op jit(solution)/shard_map/ppermute | solution.py:33
  15.9 0.8 collective-permute-done.4.refs_3_
  17.2 1.6 %collective-permute-start.8 = (bf16[256,256]{1,0:T(8,128)(2,1)}, bf16[256,256]{1,0:T(8,128)(2,1)}, u32[]{:S(2)}, u32[]{:S(2)}) collective-permute-start(bf16[256,256]{1,0:T(8,128)(2,1)} %collective-permute-done.7.refs_6_), channel_id=1, source_target_pairs={{0,2},{2,4},{4,6},{6,7},{7,5},{5,3},{3,1},{1,0},{8,10},{10,12},{12... | collective-permute-start | bytes 393224 | tf_op jit(solution)/shard_map/ppermute | solution.py:33
  18.8 0.7 reshape.8.refs_0_
  19.5 1.9 %copy-done = bf16[3,2048,256]{2,1,0:T(8,128)(2,1)S(1)} copy-done((bf16[3,2048,256]{2,1,0:T(8,128)(2,1)S(1)}, bf16[3,2048,256]{2,1,0:T(8,128)(2,1)}, u32[]{:S(2)}) %copy-start) | copy-done | bytes 3145752
  21.4 0.9 copy-done.10
  22.3 0.9 copy-done.12
  23.2 0.9 copy-done.14
  24.8 2.1 %gather_step.2 = (f32[256,768]{1,0:T(8,128)S(1)}, f32[256,128]{1,0:T(8,128)S(1)}, f32[256,768]{1,0:T(8,128)S(1)}, f32[256,128]{1,0:T(8,128)S(1)}) custom-call(s32[3]{0:T(128)S(1)} %pad_add_fusion.2.at, f32[2]{0:T(128)S(1)} %copy-done.30, f32[8,256]{1,0:T(8,128)S(1)} %reshape.8.refs_0_, bf16[3,2048,256]{2,1,0:T(8,128)(2,1)S(1)} %copy-done, ...), custom_call_target="tpu_custom_call" | custom-call | flops 603979776 | bytes 5111808 | tf_op jit(solution)/shard_map/gather_step/pallas_call | solution.py:111
  26.9 2.4 %gather_step.3 = (f32[256,768]{1,0:T(8,128)S(1)}, f32[256,128]{1,0:T(8,128)S(1)}, f32[256,768]{1,0:T(8,128)S(1)}, f32[256,128]{1,0:T(8,128)S(1)}) custom-call(s32[2]{0:T(128)S(1)} %pad_add_fusion.1.at, f32[2]{0:T(128)S(1)} %copy-done.30, f32[8,256]{1,0:T(8,128)S(1)} %reshape.8.refs_0_, bf16[3,2048,256]{2,1,0:T(8,128)(2,1)S(1)} %copy-done.1, ...), custom_call_target="tpu_custom_call" | custom-call | flops 402653184 | bytes 4456448 | tf_op jit(solution)/shard_map/gather_step/pallas_call | solution.py:111
  29.3 0.9 copy-done.4
  30.2 0.9 copy-done.6
  31.8 1.6 %collective-permute-start.12 = (bf16[256,256]{1,0:T(8,128)(2,1)}, bf16[256,256]{1,0:T(8,128)(2,1)S(1)}, u32[]{:S(2)}, u32[]{:S(2)}) collective-permute-start(bf16[256,256]{1,0:T(8,128)(2,1)} %collective-permute-done.2.refs_2_), channel_id=1, source_target_pairs={{0,2},{2,4},{4,6},{6,7},{7,5},{5,3},{3,1},{1,0},{8,10},{10,12},{12... | collective-permute-start | bytes 393224 | tf_op jit(solution)/shard_map/ppermute | solution.py:33
  33.9 3.1 %collective-permute-done.12.refs_4_ = bf16[256,256]{1,0:T(8,128)(2,1)S(1)} collective-permute-done((bf16[256,256]{1,0:T(8,128)(2,1)}, bf16[256,256]{1,0:T(8,128)(2,1)S(1)}, u32[]{:S(2)}, u32[]{:S(2)}) %collective-permute-start.12) | collective-permute-done | bytes 131104 | tf_op jit(solution)/shard_map/ppermute | solution.py:33
  37.0 1.6 %collective-permute-done.13.refs_4_ = bf16[256,256]{1,0:T(8,128)(2,1)S(1)} collective-permute-done((bf16[256,256]{1,0:T(8,128)(2,1)}, bf16[256,256]{1,0:T(8,128)(2,1)S(1)}, u32[]{:S(2)}, u32[]{:S(2)}) %collective-permute-start.13) | collective-permute-done | bytes 131104 | tf_op jit(solution)/shard_map/ppermute | solution.py:33
  39.2 1.1 %copy-done.7 = f32[256,768]{1,0:T(8,128)S(1)} copy-done((f32[256,768]{1,0:T(8,128)S(1)}, f32[256,768]{1,0:T(8,128)}, u32[]{:S(2)}) %copy-start.7) | copy-done | bytes 786456
  40.4 2.8 %gather_last.2 = (bf16[256,256]{1,0:T(8,128)(2,1)S(1)}, bf16[256,512]{1,0:T(8,128)(2,1)}) custom-call(s32[3]{0:T(128)S(1)} %pad_add_fusion.at, f32[2]{0:T(128)S(1)} %copy-done.31, f32[8,256]{1,0:T(8,128)S(1)} %reshape.8.refs_0_, bf16[3,2048,256]{2,1,0:T(8,128)(2,1)S(1)} %copy-done.1, bf16[256,256]{1,0:T(8,128)(2,1)} %collective-permute-done.2.refs_2_, ...), custom_call_target="tpu_custom_call" | custom-call | flops 301989888 | bytes 3145728 | tf_op jit(solution)/shard_map/gather_last/pallas_call | solution.py:111
  43.3 0.9 copy-done.20
  44.2 2.7 %gather_last.3 = (bf16[256,256]{1,0:T(8,128)(2,1)S(1)}, bf16[256,512]{1,0:T(8,128)(2,1)}) custom-call(s32[3]{0:T(128)S(1)} %pad_add_fusion.at, f32[2]{0:T(128)S(1)} %copy-done.31, f32[8,256]{1,0:T(8,128)S(1)} %reshape.8.refs_0_, bf16[3,2048,256]{2,1,0:T(8,128)(2,1)S(1)} %copy-done.1, bf16[256,256]{1,0:T(8,128)(2,1)} %collective-permute-done.8.refs_2_, ...), custom_call_target="tpu_custom_call" | custom-call | flops 301989888 | bytes 3145728 | tf_op jit(solution)/shard_map/gather_last/pallas_call | solution.py:111
  48.0 1.5 %collective-permute-start.17 = (bf16[256,512]{1,0:T(8,128)(2,1)}, bf16[256,512]{1,0:T(8,128)(2,1)S(1)}, u32[]{:S(2)}, u32[]{:S(2)}) collective-permute-start(bf16[256,512]{1,0:T(8,128)(2,1)} %get-tuple-element.78.refs_6_), channel_id=1, source_target_pairs={{0,16},{8,24},{16,0},{24,8},{1,17},{9,25},{17,1},{25,9},{2,18},{10... | collective-permute-start | bytes 786440 | tf_op jit(solution)/shard_map/ppermute | solution.py:315
  49.8 4.7 %attend.1 = (f32[256,512]{1,0:T(8,128)S(1)}, f32[256,512]{1,0:T(8,128)S(1)}) custom-call(s32[5]{0:T(128)S(1)} %stack.117.info, s32[2048]{0:T(1024)S(1)} %copy-done.8, bf16[256,256]{1,0:T(8,128)(2,1)S(1)} %get-tuple-element.72.refs_0_, bf16[256,256]{1,0:T(8,128)(2,1)S(1)} %get-tuple-element.76.refs_1_.refs_0_, s32[512,1]{1,0:T(8,128)S(1)} %copy.7.refs_2_, ...), custom_call_target="tpu_custom_call" | custom-call | flops 805306368 | bytes 2097152 | tf_op jit(solution)/shard_map/attend/pallas_call | solution.py:237
  54.6 2.2 %collective-permute-done.16.refs_3_ = bf16[256,512]{1,0:T(8,128)(2,1)S(1)} collective-permute-done((bf16[256,512]{1,0:T(8,128)(2,1)}, bf16[256,512]{1,0:T(8,128)(2,1)S(1)}, u32[]{:S(2)}, u32[]{:S(2)}) %collective-permute-start.16) | collective-permute-done | bytes 262176 | tf_op jit(solution)/shard_map/ppermute | solution.py:315
  56.8 4.7 %collective-permute-done.17.refs_5_ = bf16[256,512]{1,0:T(8,128)(2,1)S(1)} collective-permute-done((bf16[256,512]{1,0:T(8,128)(2,1)}, bf16[256,512]{1,0:T(8,128)(2,1)S(1)}, u32[]{:S(2)}, u32[]{:S(2)}) %collective-permute-start.17) | collective-permute-done | bytes 262176 | tf_op jit(solution)/shard_map/ppermute | solution.py:315
  62.3 0.8 collective-permute-done.18.refs_4_
  63.5 1.2 %copy-done.2 = bf16[256,2048]{1,0:T(8,128)(2,1)S(1)} copy-done((bf16[256,2048]{1,0:T(8,128)(2,1)S(1)}, bf16[256,2048]{1,0:T(8,128)(2,1)}, u32[]{:S(2)}) %copy-start.2) | copy-done | bytes 1048600
  64.7 0.9 copy-done.16
  65.6 3.6 %attend_last.2 = (bf16[256,256]{1,0:T(8,128)(2,1)}, bf16[256,256]{1,0:T(8,128)(2,1)S(1)}, bf16[256,256]{1,0:T(8,128)(2,1)S(1)}, bf16[256,256]{1,0:T(8,128)(2,1)S...) custom-call(s32[13]{0:T(128)S(1)} %stack.108.info, ...), custom_call_target="tpu_custom_call" | custom-call | flops 671088640 | bytes 1572864 | tf_op jit(solution)/shard_map/attend_last/pallas_call | solution.py:237
  73.1 1.6 %collective-permute-start.20 = (bf16[256,256]{1,0:T(8,128)(2,1)}, bf16[256,256]{1,0:T(8,128)(2,1)}, u32[]{:S(2)}, u32[]{:S(2)}) collective-permute-start(bf16[256,256]{1,0:T(8,128)(2,1)} %get-tuple-element.88), channel_id=1, source_target_pairs={{0,2},{2,4},{4,6},{6,7},{7,5},{5,3},{3,1},{1,0},{8,10},{10,12},{12... | collective-permute-start | bytes 393224 | tf_op jit(solution)/shard_map/ppermute | solution.py:33
  75.4 2.9 %attend_last.3 = (bf16[256,256]{1,0:T(8,128)(2,1)S(1)}, bf16[256,256]{1,0:T(8,128)(2,1)S(1)}, bf16[256,256]{1,0:T(8,128)(2,1)S(1)}, bf16[256,256]{1,0:T(8,128)(2...) custom-call(s32[13]{0:T(128)S(1)} %stack.119.info, ...), custom_call_target="tpu_custom_call" | custom-call | flops 671088640 | bytes 1572864 | tf_op jit(solution)/shard_map/attend_last/pallas_call | solution.py:237
  78.3 1.6 %collective-permute-start.27 = (bf16[256,256]{1,0:T(8,128)(2,1)S(1)}, bf16[256,256]{1,0:T(8,128)(2,1)S(1)}, u32[]{:S(2)}, u32[]{:S(2)}) collective-permute-start(bf16[256,256]{1,0:T(8,128)(2,1)S(1)} %get-tuple-element.96), channel_id=1, source_target_pairs={{0,2},{2,4},{4,6},{6,7},{7,5},{5,3},{3,1},{1,0},{8,10},{10,12},{12... | collective-permute-start | bytes 393224 | tf_op jit(solution)/shard_map/ppermute | solution.py:33
  80.4 1.0 add_convert_fusion.11
  81.4 1.6 %collective-permute-start.21 = (bf16[256,256]{1,0:T(8,128)(2,1)S(1)}, bf16[256,256]{1,0:T(8,128)(2,1)S(1)}, u32[]{:S(2)}, u32[]{:S(2)}) collective-permute-start(bf16[256,256]{1,0:T(8,128)(2,1)S(1)} %add_convert_fusion.11), channel_id=1, source_target_pairs={{0,2},{2,4},{4,6},{6,7},{7,5},{5,3},{3,1},{1,0},{8,10},{10,12},{12... | collective-permute-start | bytes 393224 | tf_op jit(solution)/shard_map/ppermute | solution.py:33
  83.7 1.6 %collective-permute-start.28 = (bf16[256,256]{1,0:T(8,128)(2,1)S(1)}, bf16[256,256]{1,0:T(8,128)(2,1)S(1)}, u32[]{:S(2)}, u32[]{:S(2)}) collective-permute-start(bf16[256,256]{1,0:T(8,128)(2,1)S(1)} %add_convert_fusion.5), channel_id=1, source_target_pairs={{0,2},{2,4},{4,6},{6,7},{7,5},{5,3},{3,1},{1,0},{8,10},{10,12},{12... | collective-permute-start | bytes 393224 | tf_op jit(solution)/shard_map/ppermute | solution.py:33
  86.0 1.6 %collective-permute-done.21 = bf16[256,256]{1,0:T(8,128)(2,1)S(1)} collective-permute-done((bf16[256,256]{1,0:T(8,128)(2,1)S(1)}, bf16[256,256]{1,0:T(8,128)(2,1)S(1)}, u32[]{:S(2)}, u32[]{:S(2)}) %collective-permute-start.21) | collective-permute-done | bytes 131104 | tf_op jit(solution)/shard_map/ppermute | solution.py:33
  87.6 1.6 %collective-permute-start.22 = (bf16[256,256]{1,0:T(8,128)(2,1)S(1)}, bf16[256,256]{1,0:T(8,128)(2,1)S(1)}, u32[]{:S(2)}, u32[]{:S(2)}) collective-permute-start(bf16[256,256]{1,0:T(8,128)(2,1)S(1)} %add_convert_fusion.10), channel_id=1, source_target_pairs={{0,2},{2,4},{4,6},{6,7},{7,5},{5,3},{3,1},{1,0},{8,10},{10,12},{12... | collective-permute-start | bytes 393224 | tf_op jit(solution)/shard_map/ppermute | solution.py:33
  90.4 1.6 %collective-permute-start.29 = (bf16[256,256]{1,0:T(8,128)(2,1)S(1)}, bf16[256,256]{1,0:T(8,128)(2,1)S(1)}, u32[]{:S(2)}, u32[]{:S(2)}) collective-permute-start(bf16[256,256]{1,0:T(8,128)(2,1)S(1)} %add_convert_fusion.4), channel_id=1, source_target_pairs={{0,2},{2,4},{4,6},{6,7},{7,5},{5,3},{3,1},{1,0},{8,10},{10,12},{12... | collective-permute-start | bytes 393224 | tf_op jit(solution)/shard_map/ppermute | solution.py:33
  92.6 0.7 collective-permute-done.22
  93.2 1.6 %collective-permute-start.23 = (bf16[256,256]{1,0:T(8,128)(2,1)S(1)}, bf16[256,256]{1,0:T(8,128)(2,1)S(1)}, u32[]{:S(2)}, u32[]{:S(2)}) collective-permute-start(bf16[256,256]{1,0:T(8,128)(2,1)S(1)} %add_convert_fusion.9), channel_id=1, source_target_pairs={{0,2},{2,4},{4,6},{6,7},{7,5},{5,3},{3,1},{1,0},{8,10},{10,12},{12... | collective-permute-start | bytes 393224 | tf_op jit(solution)/shard_map/ppermute | solution.py:33
  94.9 2.7 %collective-permute-done.32 = bf16[256,256]{1,0:T(8,128)(2,1)S(1)} collective-permute-done((bf16[256,256]{1,0:T(8,128)(2,1)S(1)}, bf16[256,256]{1,0:T(8,128)(2,1)S(1)}, u32[]{:S(2)}, u32[]{:S(2)}) %collective-permute-start.32) | collective-permute-done | bytes 131104 | tf_op jit(solution)/shard_map/ppermute | solution.py:33
  98.3 4.7 %collective-permute-done.33 = bf16[256,256]{1,0:T(8,128)(2,1)S(1)} collective-permute-done((bf16[256,256]{1,0:T(8,128)(2,1)S(1)}, bf16[256,256]{1,0:T(8,128)(2,1)S(1)}, u32[]{:S(2)}, u32[]{:S(2)}) %collective-permute-start.33) | collective-permute-done | bytes 131104 | tf_op jit(solution)/shard_map/ppermute | solution.py:33
  103.1 0.7 pad_maximum_fusion
  (119 shorter events, 18.5 us)
Async XLA Ops:
  1.0 6.4 %collective-permute-start.9 = (bf16[256,256]{1,0:T(8,128)(2,1)S(1)}, bf16[256,256]{1,0:T(8,128)(2,1)S(1)}, u32[]{:S(2)}, u32[]{:S(2)}) collective-permute-start(bf16[256,256]{1,0:T(8,128)(2,1)S(1)} %get-tuple-element.101.refs_5_), channel_id=1, source_target_pairs={{0,1},{2,0},{4,2},{6,4},{7,6},{5,7},{3,5},{1,3},{8,9},{10,8},{12,1... | collective-permute-start | bytes 393224 | tf_op jit(solution)/shard_map/ppermute | solution.py:33
  1.5 6.4 %collective-permute-start = (bf16[256,256]{1,0:T(8,128)(2,1)S(1)}, bf16[256,256]{1,0:T(8,128)(2,1)S(1)}, u32[]{:S(2)}, u32[]{:S(2)}) collective-permute-start(bf16[256,256]{1,0:T(8,128)(2,1)S(1)} %get-tuple-element.102.refs_2_), channel_id=1, source_target_pairs={{0,2},{2,4},{4,6},{6,7},{7,5},{5,3},{3,1},{1,0},{8,10},{10,12},{12... | collective-permute-start | bytes 393224 | tf_op jit(solution)/shard_map/ppermute | solution.py:33
  3.1 7.2 %collective-permute-start.3 = (bf16[256,256]{1,0:T(8,128)(2,1)S(1)}, bf16[256,256]{1,0:T(8,128)(2,1)S(1)}, u32[]{:S(2)}, u32[]{:S(2)}) collective-permute-start(bf16[256,256]{1,0:T(8,128)(2,1)S(1)} %get-tuple-element.102.refs_2_), channel_id=1, source_target_pairs={{0,1},{2,0},{4,2},{6,4},{7,6},{5,7},{3,5},{1,3},{8,9},{10,8},{12,1... | collective-permute-start | bytes 393224 | tf_op jit(solution)/shard_map/ppermute | solution.py:33
  3.5 7.8 %collective-permute-start.6 = (bf16[256,256]{1,0:T(8,128)(2,1)S(1)}, bf16[256,256]{1,0:T(8,128)(2,1)S(1)}, u32[]{:S(2)}, u32[]{:S(2)}) collective-permute-start(bf16[256,256]{1,0:T(8,128)(2,1)S(1)} %get-tuple-element.101.refs_5_), channel_id=1, source_target_pairs={{0,2},{2,4},{4,6},{6,7},{7,5},{5,3},{3,1},{1,0},{8,10},{10,12},{12... | collective-permute-start | bytes 393224 | tf_op jit(solution)/shard_map/ppermute | solution.py:33
  7.4 6.2 %collective-permute-start.10 = (bf16[256,256]{1,0:T(8,128)(2,1)S(1)}, bf16[256,256]{1,0:T(8,128)(2,1)}, u32[]{:S(2)}, u32[]{:S(2)}) collective-permute-start(bf16[256,256]{1,0:T(8,128)(2,1)S(1)} %collective-permute-done.9.refs_7_), channel_id=1, source_target_pairs={{0,1},{2,0},{4,2},{6,4},{7,6},{5,7},{3,5},{1,3},{8,9},{10,8},{12,1... | collective-permute-start | bytes 393224 | tf_op jit(solution)/shard_map/ppermute | solution.py:33
  7.9 10.9 %copy-start.9 = (bf16[256,256]{1,0:T(8,128)(2,1)}, bf16[256,256]{1,0:T(8,128)(2,1)S(1)}, u32[]{:S(2)}) copy-start(bf16[256,256]{1,0:T(8,128)(2,1)S(1)} %collective-permute-done.refs_3_) | copy-start | bytes 393220
  7.9 6.5 %collective-permute-start.1 = (bf16[256,256]{1,0:T(8,128)(2,1)S(1)}, bf16[256,256]{1,0:T(8,128)(2,1)}, u32[]{:S(2)}, u32[]{:S(2)}) collective-permute-start(bf16[256,256]{1,0:T(8,128)(2,1)S(1)} %collective-permute-done.refs_3_), channel_id=1, source_target_pairs={{0,2},{2,4},{4,6},{6,7},{7,5},{5,3},{3,1},{1,0},{8,10},{10,12},{12... | collective-permute-start | bytes 393224 | tf_op jit(solution)/shard_map/ppermute | solution.py:33
  10.2 6.5 %collective-permute-start.4 = (bf16[256,256]{1,0:T(8,128)(2,1)S(1)}, bf16[256,256]{1,0:T(8,128)(2,1)}, u32[]{:S(2)}, u32[]{:S(2)}) collective-permute-start(bf16[256,256]{1,0:T(8,128)(2,1)S(1)} %collective-permute-done.3.refs_4_), channel_id=1, source_target_pairs={{0,1},{2,0},{4,2},{6,4},{7,6},{5,7},{3,5},{1,3},{8,9},{10,8},{12,1... | collective-permute-start | bytes 393224 | tf_op jit(solution)/shard_map/ppermute | solution.py:33
  11.3 5.8 %collective-permute-start.7 = (bf16[256,256]{1,0:T(8,128)(2,1)S(1)}, bf16[256,256]{1,0:T(8,128)(2,1)}, u32[]{:S(2)}, u32[]{:S(2)}) collective-permute-start(bf16[256,256]{1,0:T(8,128)(2,1)S(1)} %collective-permute-done.6.refs_6_), channel_id=1, source_target_pairs={{0,2},{2,4},{4,6},{6,7},{7,5},{5,3},{3,1},{1,0},{8,10},{10,12},{12... | collective-permute-start | bytes 393224 | tf_op jit(solution)/shard_map/ppermute | solution.py:33
  13.6 18.1 %collective-permute-start.11 = (bf16[256,256]{1,0:T(8,128)(2,1)}, bf16[256,256]{1,0:T(8,128)(2,1)}, u32[]{:S(2)}, u32[]{:S(2)}) collective-permute-start(bf16[256,256]{1,0:T(8,128)(2,1)} %collective-permute-done.10.refs_7_), channel_id=1, source_target_pairs={{0,1},{2,0},{4,2},{6,4},{7,6},{5,7},{3,5},{1,3},{8,9},{10,8},{12,1... | collective-permute-start | bytes 393224 | tf_op jit(solution)/shard_map/ppermute | solution.py:33
  14.3 17.4 %collective-permute-start.2 = (bf16[256,256]{1,0:T(8,128)(2,1)}, bf16[256,256]{1,0:T(8,128)(2,1)}, u32[]{:S(2)}, u32[]{:S(2)}) collective-permute-start(bf16[256,256]{1,0:T(8,128)(2,1)} %collective-permute-done.1.refs_2_), channel_id=1, source_target_pairs={{0,2},{2,4},{4,6},{6,7},{7,5},{5,3},{3,1},{1,0},{8,10},{10,12},{12... | collective-permute-start | bytes 393224 | tf_op jit(solution)/shard_map/ppermute | solution.py:33
  16.7 15.0 %collective-permute-start.5 = (bf16[256,256]{1,0:T(8,128)(2,1)}, bf16[256,256]{1,0:T(8,128)(2,1)}, u32[]{:S(2)}, u32[]{:S(2)}) collective-permute-start(bf16[256,256]{1,0:T(8,128)(2,1)} %collective-permute-done.4.refs_3_), channel_id=1, source_target_pairs={{0,1},{2,0},{4,2},{6,4},{7,6},{5,7},{3,5},{1,3},{8,9},{10,8},{12,1... | collective-permute-start | bytes 393224 | tf_op jit(solution)/shard_map/ppermute | solution.py:33
  17.2 14.6 %collective-permute-start.8 = (bf16[256,256]{1,0:T(8,128)(2,1)}, bf16[256,256]{1,0:T(8,128)(2,1)}, u32[]{:S(2)}, u32[]{:S(2)}) collective-permute-start(bf16[256,256]{1,0:T(8,128)(2,1)} %collective-permute-done.7.refs_6_), channel_id=1, source_target_pairs={{0,2},{2,4},{4,6},{6,7},{7,5},{5,3},{3,1},{1,0},{8,10},{10,12},{12... | collective-permute-start | bytes 393224 | tf_op jit(solution)/shard_map/ppermute | solution.py:33
  19.5 1.9 %copy-start = (bf16[3,2048,256]{2,1,0:T(8,128)(2,1)S(1)}, bf16[3,2048,256]{2,1,0:T(8,128)(2,1)}, u32[]{:S(2)}) copy-start(bf16[3,2048,256]{2,1,0:T(8,128)(2,1)} %refs_1_.7) | copy-start | bytes 9437188
  24.8 2.1 %copy-start.1 = (bf16[3,2048,256]{2,1,0:T(8,128)(2,1)S(1)}, bf16[3,2048,256]{2,1,0:T(8,128)(2,1)}, u32[]{:S(2)}) copy-start(bf16[3,2048,256]{2,1,0:T(8,128)(2,1)} %refs_1_.7) | copy-start | bytes 9437188
  26.9 12.4 %copy-start.31 = (f32[2]{0:T(128)S(1)}, f32[2]{0:T(128)}, u32[]{:S(2)}) copy-start(f32[2]{0:T(128)} %factor.7) | copy-start | bytes 28
  31.8 5.2 %collective-permute-start.12 = (bf16[256,256]{1,0:T(8,128)(2,1)}, bf16[256,256]{1,0:T(8,128)(2,1)S(1)}, u32[]{:S(2)}, u32[]{:S(2)}) collective-permute-start(bf16[256,256]{1,0:T(8,128)(2,1)} %collective-permute-done.2.refs_2_), channel_id=1, source_target_pairs={{0,2},{2,4},{4,6},{6,7},{7,5},{5,3},{3,1},{1,0},{8,10},{10,12},{12... | collective-permute-start | bytes 393224 | tf_op jit(solution)/shard_map/ppermute | solution.py:33
  33.4 5.2 %collective-permute-start.13 = (bf16[256,256]{1,0:T(8,128)(2,1)}, bf16[256,256]{1,0:T(8,128)(2,1)S(1)}, u32[]{:S(2)}, u32[]{:S(2)}) collective-permute-start(bf16[256,256]{1,0:T(8,128)(2,1)} %collective-permute-done.11.refs_3_), channel_id=1, source_target_pairs={{0,1},{2,0},{4,2},{6,4},{7,6},{5,7},{3,5},{1,3},{8,9},{10,8},{12,1... | collective-permute-start | bytes 393224 | tf_op jit(solution)/shard_map/ppermute | solution.py:33
  33.8 9.4 %copy-start.5 = (f32[256,768]{1,0:T(8,128)S(1)}, f32[256,768]{1,0:T(8,128)}, u32[]{:S(2)}) copy-start(f32[256,768]{1,0:T(8,128)} %copy-done.4) | copy-start | bytes 2359300
  40.4 2.9 %copy-start.18 = (f32[256,128]{1,0:T(8,128)S(1)}, f32[256,128]{1,0:T(8,128)}, u32[]{:S(2)}) copy-start(f32[256,128]{1,0:T(8,128)} %copy-done.17) | copy-start | bytes 393220
  43.1 11.4 %copy-start.15 = (bf16[256,256]{1,0:T(8,128)(2,1)}, bf16[256,256]{1,0:T(8,128)(2,1)S(1)}, u32[]{:S(2)}) copy-start(bf16[256,256]{1,0:T(8,128)(2,1)S(1)} %get-tuple-element.72.refs_0_) | copy-start | bytes 393220
  43.2 6.3 %copy-start.8 = (s32[2048]{0:T(1024)S(1)}, s32[2048]{0:T(1024)}, u32[]{:S(2)}) copy-start(s32[2048]{0:T(1024)} %ids.5) | copy-start | bytes 24580
  43.2 6.6 %collective-permute-start.14 = (bf16[256,512]{1,0:T(8,128)(2,1)}, bf16[256,512]{1,0:T(8,128)(2,1)}, u32[]{:S(2)}, u32[]{:S(2)}) collective-permute-start(bf16[256,512]{1,0:T(8,128)(2,1)} %get-tuple-element.77.refs_4_), channel_id=1, source_target_pairs={{0,8},{8,0},{16,24},{24,16},{1,9},{9,1},{17,25},{25,17},{2,10},{10... | collective-permute-start | bytes 786440 | tf_op jit(solution)/shard_map/ppermute | solution.py:318
  46.9 2.9 %collective-permute-start.15 = (bf16[256,512]{1,0:T(8,128)(2,1)}, bf16[256,512]{1,0:T(8,128)(2,1)S(1)}, u32[]{:S(2)}, u32[]{:S(2)}) collective-permute-start(bf16[256,512]{1,0:T(8,128)(2,1)} %get-tuple-element.78.refs_6_), channel_id=1, source_target_pairs={{0,8},{8,0},{16,24},{24,16},{1,9},{9,1},{17,25},{25,17},{2,10},{10... | collective-permute-start | bytes 786440 | tf_op jit(solution)/shard_map/ppermute | solution.py:318
  47.4 9.4 %collective-permute-start.16 = (bf16[256,512]{1,0:T(8,128)(2,1)}, bf16[256,512]{1,0:T(8,128)(2,1)S(1)}, u32[]{:S(2)}, u32[]{:S(2)}) collective-permute-start(bf16[256,512]{1,0:T(8,128)(2,1)} %get-tuple-element.77.refs_4_), channel_id=1, source_target_pairs={{0,16},{8,24},{16,0},{24,8},{1,17},{9,25},{17,1},{25,9},{2,18},{10... | collective-permute-start | bytes 786440 | tf_op jit(solution)/shard_map/ppermute | solution.py:315
  48.0 13.6 %collective-permute-start.17 = (bf16[256,512]{1,0:T(8,128)(2,1)}, bf16[256,512]{1,0:T(8,128)(2,1)S(1)}, u32[]{:S(2)}, u32[]{:S(2)}) collective-permute-start(bf16[256,512]{1,0:T(8,128)(2,1)} %get-tuple-element.78.refs_6_), channel_id=1, source_target_pairs={{0,16},{8,24},{16,0},{24,8},{1,17},{9,25},{17,1},{25,9},{2,18},{10... | collective-permute-start | bytes 786440 | tf_op jit(solution)/shard_map/ppermute | solution.py:315
  49.7 25.7 %copy-start.3 = (bf16[256,2048]{1,0:T(8,128)(2,1)S(1)}, bf16[256,2048]{1,0:T(8,128)(2,1)}, u32[]{:S(2)}) copy-start(bf16[256,2048]{1,0:T(8,128)(2,1)} %refs_8_.3) | copy-start | bytes 3145732
  61.6 1.5 %collective-permute-start.18 = (bf16[256,512]{1,0:T(8,128)(2,1)S(1)}, bf16[256,512]{1,0:T(8,128)(2,1)S(1)}, u32[]{:S(2)}, u32[]{:S(2)}) collective-permute-start(bf16[256,512]{1,0:T(8,128)(2,1)S(1)} %collective-permute-done.16.refs_3_), channel_id=1, source_target_pairs={{0,8},{8,0},{16,24},{24,16},{1,9},{9,1},{17,25},{25,17},{2,10},{10... | collective-permute-start | bytes 786440 | tf_op jit(solution)/shard_map/ppermute | solution.py:323
  61.6 1.9 %collective-permute-start.19 = (bf16[256,512]{1,0:T(8,128)(2,1)S(1)}, bf16[256,512]{1,0:T(8,128)(2,1)S(1)}, u32[]{:S(2)}, u32[]{:S(2)}) collective-permute-start(bf16[256,512]{1,0:T(8,128)(2,1)S(1)} %collective-permute-done.17.refs_5_), channel_id=1, source_target_pairs={{0,8},{8,0},{16,24},{24,16},{1,9},{9,1},{17,25},{25,17},{2,10},{10... | collective-permute-start | bytes 786440 | tf_op jit(solution)/shard_map/ppermute | solution.py:323
  63.5 1.2 %copy-start.2 = (bf16[256,2048]{1,0:T(8,128)(2,1)S(1)}, bf16[256,2048]{1,0:T(8,128)(2,1)}, u32[]{:S(2)}) copy-start(bf16[256,2048]{1,0:T(8,128)(2,1)} %refs_8_.3) | copy-start | bytes 3145732
  73.1 10.0 %copy-start.26 = (bf16[256,256]{1,0:T(8,128)(2,1)S(1)}, bf16[256,256]{1,0:T(8,128)(2,1)}, u32[]{:S(2)}) copy-start(bf16[256,256]{1,0:T(8,128)(2,1)} %copy-done.25) | copy-start | bytes 393220
  73.1 14.5 %copy-start.24 = (bf16[256,256]{1,0:T(8,128)(2,1)S(1)}, bf16[256,256]{1,0:T(8,128)(2,1)}, u32[]{:S(2)}) copy-start(bf16[256,256]{1,0:T(8,128)(2,1)} %copy-done.23) | copy-start | bytes 393220
  73.1 16.2 %copy-start.22 = (bf16[256,256]{1,0:T(8,128)(2,1)S(1)}, bf16[256,256]{1,0:T(8,128)(2,1)}, u32[]{:S(2)}) copy-start(bf16[256,256]{1,0:T(8,128)(2,1)} %copy-done.21) | copy-start | bytes 393220
  73.1 7.4 %collective-permute-start.20 = (bf16[256,256]{1,0:T(8,128)(2,1)}, bf16[256,256]{1,0:T(8,128)(2,1)}, u32[]{:S(2)}, u32[]{:S(2)}) collective-permute-start(bf16[256,256]{1,0:T(8,128)(2,1)} %get-tuple-element.88), channel_id=1, source_target_pairs={{0,2},{2,4},{4,6},{6,7},{7,5},{5,3},{3,1},{1,0},{8,10},{10,12},{12... | collective-permute-start | bytes 393224 | tf_op jit(solution)/shard_map/ppermute | solution.py:33
  74.9 23.4 %copy-start.29 = (bf16[256,256]{1,0:T(8,128)(2,1)S(1)}, bf16[256,256]{1,0:T(8,128)(2,1)}, u32[]{:S(2)}) copy-start(bf16[256,256]{1,0:T(8,128)(2,1)} %copy-done.28) | copy-start | bytes 393220
  74.9 8.2 %collective-permute-start.24 = (bf16[256,256]{1,0:T(8,128)(2,1)}, bf16[256,256]{1,0:T(8,128)(2,1)S(1)}, u32[]{:S(2)}, u32[]{:S(2)}) collective-permute-start(bf16[256,256]{1,0:T(8,128)(2,1)} %copy-done.32), channel_id=1, source_target_pairs={{0,1},{2,0},{4,2},{6,4},{7,6},{5,7},{3,5},{1,3},{8,9},{10,8},{12,1... | collective-permute-start | bytes 393224 | tf_op jit(solution)/shard_map/ppermute | solution.py:33
  78.3 5.3 %collective-permute-start.27 = (bf16[256,256]{1,0:T(8,128)(2,1)S(1)}, bf16[256,256]{1,0:T(8,128)(2,1)S(1)}, u32[]{:S(2)}, u32[]{:S(2)}) collective-permute-start(bf16[256,256]{1,0:T(8,128)(2,1)S(1)} %get-tuple-element.96), channel_id=1, source_target_pairs={{0,2},{2,4},{4,6},{6,7},{7,5},{5,3},{3,1},{1,0},{8,10},{10,12},{12... | collective-permute-start | bytes 393224 | tf_op jit(solution)/shard_map/ppermute | solution.py:33
  80.0 5.4 %collective-permute-start.30 = (bf16[256,256]{1,0:T(8,128)(2,1)S(1)}, bf16[256,256]{1,0:T(8,128)(2,1)S(1)}, u32[]{:S(2)}, u32[]{:S(2)}) collective-permute-start(bf16[256,256]{1,0:T(8,128)(2,1)S(1)} %get-tuple-element.100), channel_id=1, source_target_pairs={{0,1},{2,0},{4,2},{6,4},{7,6},{5,7},{3,5},{1,3},{8,9},{10,8},{12,1... | collective-permute-start | bytes 393224 | tf_op jit(solution)/shard_map/ppermute | solution.py:33
  81.4 6.2 %collective-permute-start.21 = (bf16[256,256]{1,0:T(8,128)(2,1)S(1)}, bf16[256,256]{1,0:T(8,128)(2,1)S(1)}, u32[]{:S(2)}, u32[]{:S(2)}) collective-permute-start(bf16[256,256]{1,0:T(8,128)(2,1)S(1)} %add_convert_fusion.11), channel_id=1, source_target_pairs={{0,2},{2,4},{4,6},{6,7},{7,5},{5,3},{3,1},{1,0},{8,10},{10,12},{12... | collective-permute-start | bytes 393224 | tf_op jit(solution)/shard_map/ppermute | solution.py:33
  83.1 6.2 %collective-permute-start.25 = (bf16[256,256]{1,0:T(8,128)(2,1)S(1)}, bf16[256,256]{1,0:T(8,128)(2,1)S(1)}, u32[]{:S(2)}, u32[]{:S(2)}) collective-permute-start(bf16[256,256]{1,0:T(8,128)(2,1)S(1)} %add_convert_fusion.8), channel_id=1, source_target_pairs={{0,1},{2,0},{4,2},{6,4},{7,6},{5,7},{3,5},{1,3},{8,9},{10,8},{12,1... | collective-permute-start | bytes 393224 | tf_op jit(solution)/shard_map/ppermute | solution.py:33
  83.7 6.7 %collective-permute-start.28 = (bf16[256,256]{1,0:T(8,128)(2,1)S(1)}, bf16[256,256]{1,0:T(8,128)(2,1)S(1)}, u32[]{:S(2)}, u32[]{:S(2)}) collective-permute-start(bf16[256,256]{1,0:T(8,128)(2,1)S(1)} %add_convert_fusion.5), channel_id=1, source_target_pairs={{0,2},{2,4},{4,6},{6,7},{7,5},{5,3},{3,1},{1,0},{8,10},{10,12},{12... | collective-permute-start | bytes 393224 | tf_op jit(solution)/shard_map/ppermute | solution.py:33
  85.4 6.6 %collective-permute-start.31 = (bf16[256,256]{1,0:T(8,128)(2,1)S(1)}, bf16[256,256]{1,0:T(8,128)(2,1)S(1)}, u32[]{:S(2)}, u32[]{:S(2)}) collective-permute-start(bf16[256,256]{1,0:T(8,128)(2,1)S(1)} %add_convert_fusion.3), channel_id=1, source_target_pairs={{0,1},{2,0},{4,2},{6,4},{7,6},{5,7},{3,5},{1,3},{8,9},{10,8},{12,1... | collective-permute-start | bytes 393224 | tf_op jit(solution)/shard_map/ppermute | solution.py:33
  87.6 5.6 %collective-permute-start.22 = (bf16[256,256]{1,0:T(8,128)(2,1)S(1)}, bf16[256,256]{1,0:T(8,128)(2,1)S(1)}, u32[]{:S(2)}, u32[]{:S(2)}) collective-permute-start(bf16[256,256]{1,0:T(8,128)(2,1)S(1)} %add_convert_fusion.10), channel_id=1, source_target_pairs={{0,2},{2,4},{4,6},{6,7},{7,5},{5,3},{3,1},{1,0},{8,10},{10,12},{12... | collective-permute-start | bytes 393224 | tf_op jit(solution)/shard_map/ppermute | solution.py:33
  89.3 8.8 %collective-permute-start.26 = (bf16[256,256]{1,0:T(8,128)(2,1)S(1)}, bf16[256,256]{1,0:T(8,128)(2,1)S(1)}, u32[]{:S(2)}, u32[]{:S(2)}) collective-permute-start(bf16[256,256]{1,0:T(8,128)(2,1)S(1)} %add_convert_fusion.7), channel_id=1, source_target_pairs={{0,1},{2,0},{4,2},{6,4},{7,6},{5,7},{3,5},{1,3},{8,9},{10,8},{12,1... | collective-permute-start | bytes 393224 | tf_op jit(solution)/shard_map/ppermute | solution.py:33
  90.4 8.0 %collective-permute-start.29 = (bf16[256,256]{1,0:T(8,128)(2,1)S(1)}, bf16[256,256]{1,0:T(8,128)(2,1)S(1)}, u32[]{:S(2)}, u32[]{:S(2)}) collective-permute-start(bf16[256,256]{1,0:T(8,128)(2,1)S(1)} %add_convert_fusion.4), channel_id=1, source_target_pairs={{0,2},{2,4},{4,6},{6,7},{7,5},{5,3},{3,1},{1,0},{8,10},{10,12},{12... | collective-permute-start | bytes 393224 | tf_op jit(solution)/shard_map/ppermute | solution.py:33
  92.0 5.5 %collective-permute-start.32 = (bf16[256,256]{1,0:T(8,128)(2,1)S(1)}, bf16[256,256]{1,0:T(8,128)(2,1)S(1)}, u32[]{:S(2)}, u32[]{:S(2)}) collective-permute-start(bf16[256,256]{1,0:T(8,128)(2,1)S(1)} %add_convert_fusion.2), channel_id=1, source_target_pairs={{0,1},{2,0},{4,2},{6,4},{7,6},{5,7},{3,5},{1,3},{8,9},{10,8},{12,1... | collective-permute-start | bytes 393224 | tf_op jit(solution)/shard_map/ppermute | solution.py:33
  93.2 5.0 %collective-permute-start.23 = (bf16[256,256]{1,0:T(8,128)(2,1)S(1)}, bf16[256,256]{1,0:T(8,128)(2,1)S(1)}, u32[]{:S(2)}, u32[]{:S(2)}) collective-permute-start(bf16[256,256]{1,0:T(8,128)(2,1)S(1)} %add_convert_fusion.9), channel_id=1, source_target_pairs={{0,2},{2,4},{4,6},{6,7},{7,5},{5,3},{3,1},{1,0},{8,10},{10,12},{12... | collective-permute-start | bytes 393224 | tf_op jit(solution)/shard_map/ppermute | solution.py:33
  97.6 5.4 %collective-permute-start.33 = (bf16[256,256]{1,0:T(8,128)(2,1)S(1)}, bf16[256,256]{1,0:T(8,128)(2,1)S(1)}, u32[]{:S(2)}, u32[]{:S(2)}) collective-permute-start(bf16[256,256]{1,0:T(8,128)(2,1)S(1)} %add_convert_fusion.1), channel_id=1, source_target_pairs={{0,1},{2,0},{4,2},{6,4},{7,6},{5,7},{3,5},{1,3},{8,9},{10,8},{12,1... | collective-permute-start | bytes 393224 | tf_op jit(solution)/shard_map/ppermute | solution.py:33
  (19 other events, 14.6 us)

commit v4 on v3

v4 whole, which is shorter than its diff:
```python
import functools
import math

import jax
import jax.numpy as jnp
from jax import lax
from jax.experimental import pallas as pl
from jax.experimental.pallas import tpu as pltpu
from jax.sharding import PartitionSpec as P

LOG2E = math.log2(math.e)
VMEM = pl.BlockSpec(memory_space=pltpu.VMEM)
SMEM = pl.BlockSpec(memory_space=pltpu.SMEM)
F32 = jnp.float32
BF16 = jnp.bfloat16


def ring_order(count):
    line = count // 2
    return [2 * z for z in range(line)] + [2 * z + 1 for z in reversed(range(line))]


def ring_place(index, count):
    return jnp.where(index % 2 == 0, index // 2, count - 1 - index // 2)


def ring_index(place, count):
    return jnp.where(place < count // 2, 2 * place, 2 * (count - 1 - place) + 1)


def along(value, seq_count, count, start_lane=0, end_lane=0):
    order = ring_order(count)
    pairs = []
    for seq in range(seq_count):
        core = seq % 2
        lane = core if start_lane == 0 else 1 - core
        goal = seq - core + (lane if end_lane == 0 else 1 - lane)
        step = 1 - 2 * lane
        for p in range(count):
            pairs.append((seq * count + order[p], goal * count + order[(p + step) % count]))
    return lax.ppermute(value, ("seq", "head"), pairs)


def swapped(value, seq_count):
    return lax.ppermute(value, "seq", [(seq, seq + 1 - 2 * (seq % 2)) for seq in range(seq_count)])


def gather_kernel(count, has_state, head_size, at, factor, gain_ref, w_hbm, *refs):
    blocks, refs = refs[:count], refs[count:]
    if has_state:
        (acc_in, power_in), refs = refs[:2], refs[2:]
    outs, (w_ref, sems) = refs[:-2], refs[-2:]
    rows, width = blocks[0].shape
    groups, out_width = w_hbm.shape[0], w_hbm.shape[2]

    def fetch(n):
        start = pl.multiple_of(at[n] * width, width)
        return pltpu.make_async_copy(w_hbm.at[:, pl.ds(start, width), :], w_ref.at[n], sems.at[n])

    for n in range(count):
        fetch(n).start()
    for n in range(count):
        fetch(n).wait()
    tile = math.gcd(rows, 128)

    def step(index, out_at, store):
        here = pl.ds(pl.multiple_of(index * tile, tile), tile)
        power = power_in[here, :] if has_state else None
        scaled = []
        for n, block in enumerate(blocks):
            values = block[here, :].astype(F32)
            scaled.append((values * gain_ref[pl.ds(at[n], 1), :]).astype(BF16))
            square = values * values
            for lane in range(0, width, 128):
                piece = square[:, lane : lane + 128]
                power = piece if power is None else power + piece
        sums = []
        for group in range(groups):
            lanes = slice(group * out_width, (group + 1) * out_width)
            total = acc_in[here, lanes] if has_state else None
            for n, x in enumerate(scaled):
                product = jnp.dot(x, w_ref[n, group], preferred_element_type=F32)
                total = product if total is None else total + product
            sums.append(total)
        store(here, out_at, sums, power)

    if head_size is None:
        acc, power_out = outs

        def keep(here, out_at, sums, power):
            for group, total in enumerate(sums):
                acc[here, group * out_width : (group + 1) * out_width] = total
            power_out[here, :] = power

        pl.loop(0, rows // tile)(lambda index: step(index, None, keep))
        return

    q_ref, kv_refs = outs[0], outs[1:]
    per = kv_refs[0].shape[0] // tile
    for number, kv_ref in enumerate(kv_refs):

        def finish(here, there, sums, power):
            mean = jnp.sum(power, axis=-1, keepdims=True) * (1.0 / w_hbm.shape[1])
            scale = lax.rsqrt(mean + 1e-06)
            q, k, v = (total * scale for total in sums)
            for head in range(out_width // head_size):
                lanes = slice(head * head_size, (head + 1) * head_size)
                qh, kh = q[:, lanes], k[:, lanes]
                q_size = lax.rsqrt(jnp.sum(qh * qh, axis=-1, keepdims=True) + 1e-06)
                k_size = lax.rsqrt(jnp.sum(kh * kh, axis=-1, keepdims=True) + 1e-06)
                q_ref[here, lanes] = (qh * (q_size * (factor[head] * LOG2E))).astype(BF16)
                kv_ref[there, lanes] = (kh * k_size).astype(BF16)
            kv_ref[there, out_width:] = v.astype(BF16)

        @pl.loop(0, per)
        def _(index):
            there = pl.ds(pl.multiple_of(index * tile, tile), tile)
            step(number * per + index, there, finish)


def gather_step(at, factor, blocks, gain, weights, state, head_size=None):
    count = len(blocks)
    rows, width = blocks[0].shape
    groups, depth, out_width = weights.shape
    if head_size is None:
        shapes, kinds = [(rows, groups * out_width), (rows, 128)], [F32, F32]
    else:
        shapes = [(rows, out_width), (rows // 2, 2 * out_width), (rows // 2, 2 * out_width)]
        kinds = [BF16, BF16, BF16]
    operands = [*blocks, *(state or ())]
    return pl.pallas_call(
        functools.partial(gather_kernel, count, bool(state), head_size),
        out_shape=tuple(jax.ShapeDtypeStruct(s, k) for s, k in zip(shapes, kinds)),
        in_specs=[SMEM, SMEM, VMEM, pl.BlockSpec(memory_space=pltpu.HBM)] + [VMEM] * len(operands),
        out_specs=(VMEM,) * len(shapes),
        scratch_shapes=[
            pltpu.VMEM((count, groups, width, out_width), BF16),
            pltpu.SemaphoreType.DMA((count,)),
        ],
        compiler_params=pltpu.CompilerParams(vmem_limit_bytes=16 << 20),
        cost_estimate=pl.CostEstimate(
            flops=2 * rows * width * count * groups * out_width,
            bytes_accessed=2 * width * count * (rows + groups * out_width)
            + 8 * rows * groups * out_width,
            transcendentals=0,
        ),
        name="gather_step" if head_size is None else "gather_last",
    )(at, factor, gain, weights, *operands)


def attend_blocks(sources, ids, q_first, q_refs, id_col, id_row, kv_refs, v_ones, acc, head_size):
    heads = q_refs[0].shape[1] // head_size
    keys = kv_refs[0].shape[0]
    rows = q_refs[0].shape[0]
    for number, kv_ref in enumerate(kv_refs):
        for head in range(heads):
            start = (heads + head) * head_size
            v_ones[head, :, :head_size] = kv_ref[:, start : start + head_size]
            v_ones[head, :, head_size:] = jnp.ones((keys, head_size), BF16)
        first = sources[number]
        key_low, key_high = ids[first], ids[first + keys - 1]
        tile = math.gcd(rows, 256)
        for chunk, q_ref in enumerate(q_refs):

            @pl.loop(0, rows // tile)
            def _(index):
                here = pl.ds(pl.multiple_of(index * tile, tile), tile)
                base = chunk * rows + index * tile
                there = pl.ds(pl.multiple_of(base, tile), tile)
                q_low = ids[q_first + base]
                q_high = ids[q_first + base + tile - 1]

                def add(masked):
                    if masked:
                        allowed = id_row[first // keys] <= id_col[there, :]
                    for head in range(heads):
                        lanes = slice(head * head_size, (head + 1) * head_size)
                        score = lax.dot_general(
                            q_ref[here, lanes],
                            kv_ref[:, lanes],
                            (((1,), (1,)), ((), ())),
                            preferred_element_type=F32,
                        )
                        weight = jnp.exp2(score)
                        if masked:
                            weight = jnp.where(allowed, weight, 0.0)
                        wide = slice(2 * head * head_size, 2 * (head + 1) * head_size)
                        acc[there, wide] += jnp.dot(
                            weight.astype(BF16), v_ones[head], preferred_element_type=F32
                        )

                @pl.when(key_high <= q_low)
                def _():
                    add(False)

                @pl.when((key_high > q_low) & (key_low <= q_high))
                def _():
                    add(True)


def attend_kernel(count_q, count_kv, head_size, has_acc, count_out, info, ids, *refs):
    q_refs, rest = refs[:count_q], refs[count_q:]
    (id_col, id_row), rest = rest[:2], rest[2:]
    kv_refs, rest = rest[:count_kv], rest[count_kv:]
    rows, width = q_refs[0].shape
    if has_acc:
        acc_in, rest = rest[0], rest[1:]
    if count_out:
        w_ref, outs, (v_ones, acc, attended) = rest[0], rest[1:-3], rest[-3:]
    else:
        accs, (v_ones, acc) = rest[:-2], rest[-2:]
    acc[...] = acc_in[...] if has_acc else jnp.zeros_like(acc)
    sources = [info[number] for number in range(count_kv)]
    attend_blocks(
        sources, ids, info[count_kv], q_refs, id_col, id_row, kv_refs, v_ones, acc, head_size
    )
    if not count_out:
        for number, out in enumerate(accs):
            out[...] = acc[number * rows : (number + 1) * rows, :]
        return
    for head in range(width // head_size):
        start = 2 * head * head_size
        attended[:, head * head_size : (head + 1) * head_size] = (
            acc[:, start : start + head_size]
            / acc[:, start + head_size : start + 2 * head_size]
        ).astype(BF16)
    out_width = outs[0].shape[1]
    for number, out in enumerate(outs):
        lane = info[count_kv + 1 + number] * out_width
        out[...] = jnp.dot(
            attended[...],
            w_ref[:, pl.ds(pl.multiple_of(lane, out_width), out_width)],
            preferred_element_type=F32,
        ).astype(BF16)


def attend(info, ids, queries, id_col, id_row, kvs, head_size, acc=None, w_out=None, count_out=0):
    rows, width = queries[0].shape
    total = rows * len(queries)
    keys = kvs[0].shape[0]
    heads = width // head_size
    scratch = [
        pltpu.VMEM((heads, keys, 2 * head_size), BF16),
        pltpu.VMEM((total, 2 * width), F32),
    ]
    operands = [*queries, id_col, id_row, *kvs]
    if acc is not None:
        operands.append(acc)
    if count_out:
        operands.append(w_out)
        scratch.append(pltpu.VMEM((total, width), BF16))
        shape = jax.ShapeDtypeStruct((total, w_out.shape[1] // count_out), BF16)
    else:
        shape = jax.ShapeDtypeStruct((rows, 2 * width), F32)
    outs = count_out or len(queries)
    return pl.pallas_call(
        functools.partial(
            attend_kernel, len(queries), len(kvs), head_size, acc is not None, count_out
        ),
        out_shape=(shape,) * outs,
        in_specs=[SMEM, SMEM] + [VMEM] * len(operands),
        out_specs=(VMEM,) * outs,
        scratch_shapes=scratch,
        compiler_params=pltpu.CompilerParams(
            vmem_limit_bytes=(16 << 20) + 2 * kvs[0].size * 2 * len(kvs)
        ),
        cost_estimate=pl.CostEstimate(
            flops=6 * total * keys * len(kvs) * width + 2 * total * width * width * count_out,
            bytes_accessed=4 * keys * len(kvs) * width + 8 * total * width,
            transcendentals=total * keys * len(kvs) * heads,
        ),
        name="attend_last" if count_out else "attend",
    )(info, ids, *operands)


def total_of(*parts):
    return sum(part.astype(F32) for part in parts).astype(BF16)


def body(mesh_shape, tokens, norm_gain, w_qkv, head_scale, w_out, scale_ids):
    ring, seqs = mesh_shape["head"], mesh_shape["seq"]
    outer = seqs // 2
    rows, width = tokens.shape
    half = rows // 2
    head_size = w_qkv.shape[2] // head_scale.shape[0]
    head_at, seq_at = lax.axis_index("head"), lax.axis_index("seq")
    place = ring_place(head_at, ring)
    chip, core = seq_at // 2, seq_at % 2
    toward = 1 - 2 * core
    index_at = lambda offset: ring_index((place + toward * offset + ring) % ring, ring)
    numbers = lambda values: jnp.stack(values).astype(jnp.int32)
    id_row = scale_ids.reshape(-1, 1, half)
    id_col = lax.dynamic_slice_in_dim(scale_ids, seq_at * rows, rows)[:, None]

    farthest = ring // 2
    gain = norm_gain.reshape(ring, width)
    own = other = tokens
    waiting, offsets, state = [tokens], [0], None
    for step in range(1, farthest):
        own = along(own, seqs, ring)
        other = along(other, seqs, ring, start_lane=int(step == 1))
        if state is not None:
            own, other, state = lax.optimization_barrier((own, other, state))
        waiting += [own, swapped(other, seqs)]
        offsets += [-step, step]
        if step < farthest - 1:
            at = numbers([index_at(offset) for offset in offsets])
            state = gather_step(at, head_scale, waiting, gain, w_qkv, state)
            waiting, offsets = [], []
    waiting.append(along(own, seqs, ring))
    offsets.append(-farthest)
    at = numbers([index_at(offset) for offset in offsets])
    query, *kvs = gather_step(at, head_scale, waiting, gain, w_qkv, state, head_size)

    near, near_at = [], []
    far, far_at = [[] for kv in kvs], [[] for kv in kvs]
    for s, kv in enumerate(kvs):
        for step in range(outer):
            source = 2 * ((chip + outer - step) % outer)
            places = [(source + core) * rows + s * half, (source + 1 - core) * rows + s * half]
            if step:
                shift = [
                    (2 * a + b, 2 * ((a + step) % outer) + b) for a in range(outer) for b in (0, 1)
                ]
                far[s].append(lax.ppermute(kv, "seq", shift))
                far_at[s] += places
            else:
                near += [kv, swapped(kv, seqs)]
                near_at += places
    first = [seq_at * rows]
    (acc,) = attend(numbers(near_at + first), scale_ids, [query], id_col, id_row, near, head_size)
    goals = list(range(farthest, -farthest, -1))
    for s in range(len(kvs)):
        acc, far[s] = lax.optimization_barrier((acc, far[s]))
        blocks = [data for block in far[s] for data in (block, swapped(block, seqs))]
        if s + 1 < len(kvs):
            (acc,) = attend(
                numbers(far_at[s] + first), scale_ids, [query], id_col, id_row, blocks, head_size,
                acc,
            )
    info = numbers(far_at[-1] + first + [index_at(goal) for goal in goals])
    parts = attend(
        info, scale_ids, [query], id_col, id_row, blocks, head_size, acc, w_out, ring
    )
    parts = dict(zip(goals, parts))
    own = along(parts[farthest], seqs, ring)
    other = along(parts[1 - farthest], seqs, ring, start_lane=1)
    for step in range(farthest - 1, 0, -1):
        own = along(total_of(parts[step], own), seqs, ring)
        if step > 1:
            part = swapped(parts[1 - step], seqs)
            other = along(total_of(part, other), seqs, ring, end_lane=int(step == 2))
    return total_of(parts[0], own, other)


def solution(mesh):
    placed = (P("seq", "head"), P(), P(None, None, "head"), P("head"), P("head", None), P())
    return jax.shard_map(
        functools.partial(body, dict(mesh.shape)),
        mesh=mesh,
        in_specs=placed,
        out_specs=P("seq", "head"),
        check_vma=False,
    )
```

time: 105 us -> 99.1 us (0.944)
  starting transfers between devices: 32.3 us -> 19.5 us
  waiting for transfers between devices: 27.5 us -> 40.2 us
  local copies, waits for them, and re-layouts: 20.2 us -> 17.6 us
  Pallas kernels: 21.2 us -> 18.9 us
    ppermute x34 -> x25, starting transfers between devices: 32.3 us -> 19.5 us  [the longest x14 17.9 us: along(): return lax.ppermute(value, ('seq', 'head'), pairs)]
    ppermute x34 -> x25, waiting for transfers between devices: 27.5 us -> 40.2 us  [the longest x14 30.9 us: along(): return lax.ppermute(value, ('seq', 'head'), pairs)]
    pallas_call x4 -> x3, Pallas kernels: 9.91 us -> 8.47 us  [gather_step(): pl.pallas_call(functools.partial(gather_kernel, count, bool(state), head_...]
    unnamed x66 -> x40, local copies, waits for them, and re-layouts: 17.8 us -> 16.5 us
    slice x4 -> x0, local copies, waits for them, and re-layouts: 1.26 us -> none  [the longest x1 0.98 us: body(): held = [[tokens[s * half:(s + 1) * half]] * 2 for s in streams]]
  transfers between devices with their start and end apart: 34 -> 25, of which waited for: 17 -> 17; matrix products, arithmetic and copies ran while one was open for 3% -> 2% of each run, Pallas kernels for 14% -> 12%
where the time goes in v4:
time: 99.1 us; the launch traced here: 97.7 us
  waiting for transfers between devices  40.2 us (41%)
  starting transfers between devices  19.5 us (20%)
  Pallas kernels  18.9 us (19%)
  local copies, waits for them, and re-layouts  17.6 us (18%)
  other arithmetic  1.46 us (1%)
    ppermute x14, waiting for transfers between devices, along(): return lax.ppermute(value, ('seq', 'head'), pairs)  30.9 us
    ppermute x14, starting transfers between devices, along(): return lax.ppermute(value, ('seq', 'head'), pairs)  17.9 us
    unnamed x40, local copies, waits for them, and re-layouts  16.5 us
    pallas_call x3, Pallas kernels, attend(): pl.pallas_call(functools.partial(attend_kernel, len(queries), len(kvs), h...  10.4 us
    pallas_call x3, Pallas kernels, gather_step(): pl.pallas_call(functools.partial(gather_kernel, count, bool(state), head_...  8.47 us
    ppermute x2, waiting for transfers between devices, body(): far[s].append(lax.ppermute(kv, 'seq', shift))  6.07 us
    ppermute x9, waiting for transfers between devices, swapped(): lax.ppermute(value, 'seq', [(seq, seq + 1 - 2 * (seq % 2)) for seq in ran...  3.27 us
  transfers between devices with their start and end apart: 25, of which 17 were waited for; matrix products, arithmetic and copies ran while one was open for 2% of the time, Pallas kernels for 12%

profile of v4, /device:TPU:10, one launch (start us, length us, event | category | flops | bytes accessed | tf_op | source)
XLA Modules:
  0.0 97.7 jit_solution(8721746560896885826)
XLA Ops:
  0.0 1.6 %collective-permute-start = (bf16[512,256]{1,0:T(8,128)(2,1)}, bf16[512,256]{1,0:T(8,128)(2,1)}, u32[]{:S(2)}, u32[]{:S(2)}) collective-permute-start(bf16[512,256]{1,0:T(8,128)(2,1)} %refs_0_.1), channel_id=1, source_target_pairs={{0,2},{2,4},{4,6},{6,7},{7,5},{5,3},{3,1},{1,0},{8,9},{10,8},{12,1... | collective-permute-start | bytes 786440 | tf_op jit(solution)/shard_map/ppermute | solution.py:41
  1.6 6.8 %collective-permute-done.2 = bf16[512,256]{1,0:T(8,128)(2,1)} collective-permute-done((bf16[512,256]{1,0:T(8,128)(2,1)}, bf16[512,256]{1,0:T(8,128)(2,1)}, u32[]{:S(2)}, u32[]{:S(2)}) %collective-permute-start.2) | collective-permute-done | bytes 262176 | tf_op jit(solution)/shard_map/ppermute | solution.py:41
  8.4 0.6 collective-permute-done.refs_1_
  8.9 1.6 %collective-permute-start.1 = (bf16[512,256]{1,0:T(8,128)(2,1)}, bf16[512,256]{1,0:T(8,128)(2,1)S(1)}, u32[]{:S(2)}, u32[]{:S(2)}) collective-permute-start(bf16[512,256]{1,0:T(8,128)(2,1)} %collective-permute-done.refs_1_), channel_id=1, source_target_pairs={{0,2},{2,4},{4,6},{6,7},{7,5},{5,3},{3,1},{1,0},{8,9},{10,8},{12,1... | collective-permute-start | bytes 786440 | tf_op jit(solution)/shard_map/ppermute | solution.py:41
  10.5 1.6 %collective-permute-start.3 = (bf16[512,256]{1,0:T(8,128)(2,1)}, bf16[512,256]{1,0:T(8,128)(2,1)}, u32[]{:S(2)}, u32[]{:S(2)}) collective-permute-start(bf16[512,256]{1,0:T(8,128)(2,1)} %collective-permute-done.2), channel_id=1, source_target_pairs={{0,2},{2,4},{4,6},{6,7},{7,5},{5,3},{3,1},{1,0},{8,9},{10,8},{12,1... | collective-permute-start | bytes 786440 | tf_op jit(solution)/shard_map/ppermute | solution.py:41
  12.1 0.7 reshape.6.gain_ref
  12.9 0.7 copy-done.7
  13.6 1.9 %copy-done = bf16[3,2048,256]{2,1,0:T(8,128)(2,1)S(1)} copy-done((bf16[3,2048,256]{2,1,0:T(8,128)(2,1)S(1)}, bf16[3,2048,256]{2,1,0:T(8,128)(2,1)}, u32[]{:S(2)}) %copy-start) | copy-done | bytes 3145752
  15.5 0.9 copy-done.6
  16.4 0.9 copy-done.8
  17.4 0.7 copy-done.17
  18.0 2.7 %gather_step.2 = (f32[512,768]{1,0:T(8,128)S(1)}, f32[512,128]{1,0:T(8,128)S(1)}) custom-call(s32[3]{0:T(128)S(1)} %pad_add_fusion.1.at, f32[2]{0:T(128)S(1)} %copy-done.17, f32[8,256]{1,0:T(8,128)S(1)} %reshape.6.gain_ref, bf16[3,2048,256]{2,1,0:T(8,128)(2,1)S(1)} %copy-done, bf16[512,256]{1,0:T(8,128)(2,1)S(1)} %copy-done.6, ...), custom_call_target="tpu_custom_call" | custom-call | flops 603979776 | bytes 5111808 | tf_op jit(solution)/shard_map/gather_step/pallas_call | solution.py:131
  20.7 1.2 %copy-done.4 = f32[512,768]{1,0:T(8,128)} copy-done((f32[512,768]{1,0:T(8,128)}, f32[512,768]{1,0:T(8,128)S(1)}, u32[]{:S(2)}) %copy-start.4) | copy-done | bytes 1572888
  21.8 0.7 copy-done.11
  22.6 1.6 %collective-permute-start.5 = (bf16[512,256]{1,0:T(8,128)(2,1)S(1)}, bf16[512,256]{1,0:T(8,128)(2,1)}, u32[]{:S(2)}, u32[]{:S(2)}) collective-permute-start(bf16[512,256]{1,0:T(8,128)(2,1)S(1)} %collective-permute-done.1.refs_0_), channel_id=1, source_target_pairs={{0,2},{2,4},{4,6},{6,7},{7,5},{5,3},{3,1},{1,0},{8,9},{10,8},{12,1... | collective-permute-start | bytes 786440 | tf_op jit(solution)/shard_map/ppermute | solution.py:41
  24.7 1.4 %copy-done.5 = f32[512,768]{1,0:T(8,128)S(1)} copy-done((f32[512,768]{1,0:T(8,128)S(1)}, f32[512,768]{1,0:T(8,128)}, u32[]{:S(2)}) %copy-start.5) | copy-done | bytes 1572888
  26.1 0.9 copy-done.12
  27.0 2.2 %gather_step.3 = (f32[512,768]{1,0:T(8,128)S(1)}, f32[512,128]{1,0:T(8,128)S(1)}) custom-call(s32[2]{0:T(128)S(1)} %pad_add_fusion.2.at, f32[2]{0:T(128)S(1)} %copy-done.18, f32[8,256]{1,0:T(8,128)S(1)} %reshape.6.gain_ref, bf16[3,2048,256]{2,1,0:T(8,128)(2,1)S(1)} %copy-done.1, bf16[512,256]{1,0:T(8,128)(2,1)S(1)} %collective-permute-done.1.refs_0_, ...), custom_call_target="tpu_custom_call" | custom-call | flops 402653184 | bytes 4456448 | tf_op jit(solution)/shard_map/gather_step/pallas_call | solution.py:131
  29.3 1.2 %copy-done.2 = f32[512,768]{1,0:T(8,128)} copy-done((f32[512,768]{1,0:T(8,128)}, f32[512,768]{1,0:T(8,128)S(1)}, u32[]{:S(2)}) %copy-start.2) | copy-done | bytes 1572888
  30.4 0.7 copy-done.9
  31.1 0.8 collective-permute-done.6
  31.9 1.5 %collective-permute-start.9 = (bf16[512,256]{1,0:T(8,128)(2,1)}, bf16[512,256]{1,0:T(8,128)(2,1)}, u32[]{:S(2)}, u32[]{:S(2)}) collective-permute-start(bf16[512,256]{1,0:T(8,128)(2,1)} %collective-permute-done.5.refs_0_), channel_id=1, source_target_pairs={{0,2},{2,4},{4,6},{6,7},{7,5},{5,3},{3,1},{1,0},{8,9},{10,8},{12,1... | collective-permute-start | bytes 786440 | tf_op jit(solution)/shard_map/ppermute | solution.py:41
  33.6 4.9 %collective-permute-done.9.refs_2_ = bf16[512,256]{1,0:T(8,128)(2,1)} collective-permute-done((bf16[512,256]{1,0:T(8,128)(2,1)}, bf16[512,256]{1,0:T(8,128)(2,1)}, u32[]{:S(2)}, u32[]{:S(2)}) %collective-permute-start.9) | collective-permute-done | bytes 262176 | tf_op jit(solution)/shard_map/ppermute | solution.py:41
  38.6 1.4 %copy-done.3 = f32[512,768]{1,0:T(8,128)S(1)} copy-done((f32[512,768]{1,0:T(8,128)S(1)}, f32[512,768]{1,0:T(8,128)}, u32[]{:S(2)}) %copy-start.3) | copy-done | bytes 1572888
  40.0 0.9 copy-done.10
  41.0 3.6 %gather_last.1 = (bf16[512,256]{1,0:T(8,128)(2,1)S(1)}, bf16[256,512]{1,0:T(8,128)(2,1)}, bf16[256,512]{1,0:T(8,128)(2,1)}) custom-call(s32[3]{0:T(128)S(1)} %pad_add_fusion.at, f32[2]{0:T(128)S(1)} %copy-done.18, f32[8,256]{1,0:T(8,128)S(1)} %reshape.6.gain_ref, bf16[3,2048,256]{2,1,0:T(8,128)(2,1)S(1)} %copy-done.1, ...), custom_call_target="tpu_custom_call" | custom-call | flops 603979776 | bytes 5111808 | tf_op jit(solution)/shard_map/gather_last/pallas_call | solution.py:131
  44.6 0.7 copy-done.13
  45.8 0.5 collective-permute-start.12
  47.4 0.9 copy-done.14
  48.3 4.6 %attend.2.refs_5_ = f32[512,512]{1,0:T(8,128)S(1)} custom-call(s32[5]{0:T(128)S(1)} %stack.104.info, s32[2048]{0:T(1024)S(1)} %copy-done.16, bf16[512,256]{1,0:T(8,128)(2,1)S(1)} %copy-done.14, s32[512,1]{1,0:T(8,128)S(1)} %copy.9.refs_1_, s32[8,1,256]{2,1,0:T(1,128)S(1)} %bitcast.20, bf16[256,512]{1,0:T(8,128)(2,1)} %get-tuple-element.45.refs_3_, ...), custom_call_target="tpu_custom_call" | custom-call | flops 805306368 | bytes 2097152 | tf_op jit(solution)/shard_map/attend/pallas_call | solution.py:256
  53.0 1.2 %collective-permute-done.12.refs_3_ = bf16[256,512]{1,0:T(8,128)(2,1)S(1)} collective-permute-done((bf16[256,512]{1,0:T(8,128)(2,1)}, bf16[256,512]{1,0:T(8,128)(2,1)S(1)}, u32[]{:S(2)}, u32[]{:S(2)}) %collective-permute-start.12) | collective-permute-done | bytes 262176 | tf_op jit(solution)/shard_map/ppermute | solution.py:325
  54.2 0.5 collective-permute-start.14
  54.8 0.9 collective-permute-done.13.refs_4_
  55.7 2.5 %attend.3.refs_5_ = f32[512,512]{1,0:T(8,128)S(1)} custom-call(s32[3]{0:T(128)S(1)} %pad_add_fusion.3.info, s32[2048]{0:T(1024)S(1)} %copy-done.16, bf16[512,256]{1,0:T(8,128)(2,1)S(1)} %copy-done.15, s32[512,1]{1,0:T(8,128)S(1)} %copy.9.refs_1_, s32[8,1,256]{2,1,0:T(1,128)S(1)} %bitcast.21, bf16[256,512]{1,0:T(8,128)(2,1)S(1)} %collective-permute-done.12.refs_3_, ...), custom_call_target="tpu_custom_call" | custom-call | flops 402653184 | bytes 1572864 | tf_op jit(solution)/shard_map/attend/pallas_call | solution.py:256
  58.3 4.9 %collective-permute-done.14.refs_3_ = bf16[256,512]{1,0:T(8,128)(2,1)S(1)} collective-permute-done((bf16[256,512]{1,0:T(8,128)(2,1)}, bf16[256,512]{1,0:T(8,128)(2,1)S(1)}, u32[]{:S(2)}, u32[]{:S(2)}) %collective-permute-start.14) | collective-permute-done | bytes 262176 | tf_op jit(solution)/shard_map/ppermute | solution.py:325
  63.2 1.4 %collective-permute-done.15.refs_4_ = bf16[256,512]{1,0:T(8,128)(2,1)S(1)} collective-permute-done((bf16[256,512]{1,0:T(8,128)(2,1)S(1)}, bf16[256,512]{1,0:T(8,128)(2,1)S(1)}, u32[]{:S(2)}, u32[]{:S(2)}) %collective-permute-start.15) | collective-permute-done | bytes 262176 | tf_op jit(solution)/shard_map/ppermute | solution.py:45
  64.7 1.2 %copy-done.19 = bf16[256,2048]{1,0:T(8,128)(2,1)S(1)} copy-done((bf16[256,2048]{1,0:T(8,128)(2,1)S(1)}, bf16[256,2048]{1,0:T(8,128)(2,1)}, u32[]{:S(2)}) %copy-start.19) | copy-done | bytes 1048600
  65.9 3.2 %attend_last.1 = (bf16[512,256]{1,0:T(8,128)(2,1)S(1)}, bf16[512,256]{1,0:T(8,128)(2,1)S(1)}, bf16[512,256]{1,0:T(8,128)(2,1)S(1)}, bf16[512,256]{1,0:T(8,128)(2...) custom-call(s32[11]{0:T(128)S(1)} %stack.92.info, ...), custom_call_target="tpu_custom_call" | custom-call | flops 939524096 | bytes 1572864 | tf_op jit(solution)/shard_map/attend_last/pallas_call | solution.py:256
  69.1 1.6 %collective-permute-start.16 = (bf16[512,256]{1,0:T(8,128)(2,1)S(1)}, bf16[512,256]{1,0:T(8,128)(2,1)S(1)}, u32[]{:S(2)}, u32[]{:S(2)}) collective-permute-start(bf16[512,256]{1,0:T(8,128)(2,1)S(1)} %get-tuple-element.55), channel_id=1, source_target_pairs={{0,2},{2,4},{4,6},{6,7},{7,5},{5,3},{3,1},{1,0},{8,9},{10,8},{12,1... | collective-permute-start | bytes 786440 | tf_op jit(solution)/shard_map/ppermute | solution.py:41
  70.7 0.6 collective-permute-start.22
  71.3 6.1 %collective-permute-done.16 = bf16[512,256]{1,0:T(8,128)(2,1)S(1)} collective-permute-done((bf16[512,256]{1,0:T(8,128)(2,1)S(1)}, bf16[512,256]{1,0:T(8,128)(2,1)S(1)}, u32[]{:S(2)}, u32[]{:S(2)}) %collective-permute-start.16) | collective-permute-done | bytes 262176 | tf_op jit(solution)/shard_map/ppermute | solution.py:41
  77.5 2.4 %collective-permute-start.17 = (bf16[512,256]{1,0:T(8,128)(2,1)S(1)}, bf16[512,256]{1,0:T(8,128)(2,1)S(1)}, u32[]{:S(2)}, u32[]{:S(2)}) collective-permute-start(bf16[512,256]{1,0:T(8,128)(2,1)S(1)} %add_convert_fusion.5), channel_id=1, source_target_pairs={{0,2},{2,4},{4,6},{6,7},{7,5},{5,3},{3,1},{1,0},{8,9},{10,8},{12,1... | collective-permute-start | bytes 786440 | tf_op jit(solution)/shard_map/ppermute | solution.py:41
  80.1 3.8 %collective-permute-done.17 = bf16[512,256]{1,0:T(8,128)(2,1)S(1)} collective-permute-done((bf16[512,256]{1,0:T(8,128)(2,1)S(1)}, bf16[512,256]{1,0:T(8,128)(2,1)S(1)}, u32[]{:S(2)}, u32[]{:S(2)}) %collective-permute-start.17) | collective-permute-done | bytes 262176 | tf_op jit(solution)/shard_map/ppermute | solution.py:41
  84.0 2.4 %collective-permute-start.18 = (bf16[512,256]{1,0:T(8,128)(2,1)S(1)}, bf16[512,256]{1,0:T(8,128)(2,1)S(1)}, u32[]{:S(2)}, u32[]{:S(2)}) collective-permute-start(bf16[512,256]{1,0:T(8,128)(2,1)S(1)} %add_convert_fusion.4), channel_id=1, source_target_pairs={{0,2},{2,4},{4,6},{6,7},{7,5},{5,3},{3,1},{1,0},{8,9},{10,8},{12,1... | collective-permute-start | bytes 786440 | tf_op jit(solution)/shard_map/ppermute | solution.py:41
  86.9 3.5 %collective-permute-done.18 = bf16[512,256]{1,0:T(8,128)(2,1)S(1)} collective-permute-done((bf16[512,256]{1,0:T(8,128)(2,1)S(1)}, bf16[512,256]{1,0:T(8,128)(2,1)S(1)}, u32[]{:S(2)}, u32[]{:S(2)}) %collective-permute-start.18) | collective-permute-done | bytes 262176 | tf_op jit(solution)/shard_map/ppermute | solution.py:41
  90.5 2.4 %collective-permute-start.19 = (bf16[512,256]{1,0:T(8,128)(2,1)S(1)}, bf16[512,256]{1,0:T(8,128)(2,1)S(1)}, u32[]{:S(2)}, u32[]{:S(2)}) collective-permute-start(bf16[512,256]{1,0:T(8,128)(2,1)S(1)} %add_convert_fusion.3), channel_id=1, source_target_pairs={{0,2},{2,4},{4,6},{6,7},{7,5},{5,3},{3,1},{1,0},{8,9},{10,8},{12,1... | collective-permute-start | bytes 786440 | tf_op jit(solution)/shard_map/ppermute | solution.py:41
  93.1 3.8 %collective-permute-done.19 = bf16[512,256]{1,0:T(8,128)(2,1)S(1)} collective-permute-done((bf16[512,256]{1,0:T(8,128)(2,1)S(1)}, bf16[512,256]{1,0:T(8,128)(2,1)S(1)}, u32[]{:S(2)}, u32[]{:S(2)}) %collective-permute-start.19) | collective-permute-done | bytes 262176 | tf_op jit(solution)/shard_map/ppermute | solution.py:41
  96.9 0.8 add_convert_fusion
  (63 shorter events, 3.7 us)
Async XLA Ops:
  0.0 8.4 %collective-permute-start.2 = (bf16[512,256]{1,0:T(8,128)(2,1)}, bf16[512,256]{1,0:T(8,128)(2,1)}, u32[]{:S(2)}, u32[]{:S(2)}) collective-permute-start(bf16[512,256]{1,0:T(8,128)(2,1)} %refs_0_.1), channel_id=1, source_target_pairs={{0,9},{2,8},{4,10},{6,12},{7,14},{5,15},{3,13},{1,11},{8,2},{10,4}... | collective-permute-start | bytes 786440 | tf_op jit(solution)/shard_map/ppermute | solution.py:41
  0.0 8.9 %collective-permute-start = (bf16[512,256]{1,0:T(8,128)(2,1)}, bf16[512,256]{1,0:T(8,128)(2,1)}, u32[]{:S(2)}, u32[]{:S(2)}) collective-permute-start(bf16[512,256]{1,0:T(8,128)(2,1)} %refs_0_.1), channel_id=1, source_target_pairs={{0,2},{2,4},{4,6},{6,7},{7,5},{5,3},{3,1},{1,0},{8,9},{10,8},{12,1... | collective-permute-start | bytes 786440 | tf_op jit(solution)/shard_map/ppermute | solution.py:41
  8.4 4.5 %collective-permute-start.4 = (bf16[512,256]{1,0:T(8,128)(2,1)}, bf16[512,256]{1,0:T(8,128)(2,1)S(1)}, u32[]{:S(2)}, u32[]{:S(2)}) collective-permute-start(bf16[512,256]{1,0:T(8,128)(2,1)} %collective-permute-done.2), channel_id=1, source_target_pairs={{0,8},{8,0},{16,24},{24,16},{1,9},{9,1},{17,25},{25,17},{2,10},{10... | collective-permute-start | bytes 786440 | tf_op jit(solution)/shard_map/ppermute | solution.py:45
  8.9 13.6 %collective-permute-start.1 = (bf16[512,256]{1,0:T(8,128)(2,1)}, bf16[512,256]{1,0:T(8,128)(2,1)S(1)}, u32[]{:S(2)}, u32[]{:S(2)}) collective-permute-start(bf16[512,256]{1,0:T(8,128)(2,1)} %collective-permute-done.refs_1_), channel_id=1, source_target_pairs={{0,2},{2,4},{4,6},{6,7},{7,5},{5,3},{3,1},{1,0},{8,9},{10,8},{12,1... | collective-permute-start | bytes 786440 | tf_op jit(solution)/shard_map/ppermute | solution.py:41
  10.5 12.1 %collective-permute-start.3 = (bf16[512,256]{1,0:T(8,128)(2,1)}, bf16[512,256]{1,0:T(8,128)(2,1)}, u32[]{:S(2)}, u32[]{:S(2)}) collective-permute-start(bf16[512,256]{1,0:T(8,128)(2,1)} %collective-permute-done.2), channel_id=1, source_target_pairs={{0,2},{2,4},{4,6},{6,7},{7,5},{5,3},{3,1},{1,0},{8,9},{10,8},{12,1... | collective-permute-start | bytes 786440 | tf_op jit(solution)/shard_map/ppermute | solution.py:41
  12.9 0.7 copy-start.7
  13.6 1.9 %copy-start = (bf16[3,2048,256]{2,1,0:T(8,128)(2,1)S(1)}, bf16[3,2048,256]{2,1,0:T(8,128)(2,1)}, u32[]{:S(2)}) copy-start(bf16[3,2048,256]{2,1,0:T(8,128)(2,1)} %w_hbm.5) | copy-start | bytes 9437188
  15.5 0.9 copy-start.6
  16.4 0.9 copy-start.8
  17.4 0.7 copy-start.17
  18.0 6.7 %copy-start.1 = (bf16[3,2048,256]{2,1,0:T(8,128)(2,1)S(1)}, bf16[3,2048,256]{2,1,0:T(8,128)(2,1)}, u32[]{:S(2)}) copy-start(bf16[3,2048,256]{2,1,0:T(8,128)(2,1)} %w_hbm.5) | copy-start | bytes 9437188
  18.0 6.7 %copy-start.18 = (f32[2]{0:T(128)S(1)}, f32[2]{0:T(128)}, u32[]{:S(2)}) copy-start(f32[2]{0:T(128)} %factor.5) | copy-start | bytes 28
  20.7 1.2 %copy-start.4 = (f32[512,768]{1,0:T(8,128)}, f32[512,768]{1,0:T(8,128)S(1)}, u32[]{:S(2)}) copy-start(f32[512,768]{1,0:T(8,128)S(1)} %get-tuple-element.36.refs_2_) | copy-start | bytes 4718596
  21.8 0.7 copy-start.11
  22.6 2.1 %collective-permute-start.7 = (bf16[512,256]{1,0:T(8,128)(2,1)}, bf16[512,256]{1,0:T(8,128)(2,1)}, u32[]{:S(2)}, u32[]{:S(2)}) collective-permute-start(bf16[512,256]{1,0:T(8,128)(2,1)} %collective-permute-done.3), channel_id=1, source_target_pairs={{0,8},{8,0},{16,24},{24,16},{1,9},{9,1},{17,25},{25,17},{2,10},{10... | collective-permute-start | bytes 786440 | tf_op jit(solution)/shard_map/ppermute | solution.py:45
  22.6 8.6 %collective-permute-start.5 = (bf16[512,256]{1,0:T(8,128)(2,1)S(1)}, bf16[512,256]{1,0:T(8,128)(2,1)}, u32[]{:S(2)}, u32[]{:S(2)}) collective-permute-start(bf16[512,256]{1,0:T(8,128)(2,1)S(1)} %collective-permute-done.1.refs_0_), channel_id=1, source_target_pairs={{0,2},{2,4},{4,6},{6,7},{7,5},{5,3},{3,1},{1,0},{8,9},{10,8},{12,1... | collective-permute-start | bytes 786440 | tf_op jit(solution)/shard_map/ppermute | solution.py:41
  24.1 7.8 %collective-permute-start.6 = (bf16[512,256]{1,0:T(8,128)(2,1)}, bf16[512,256]{1,0:T(8,128)(2,1)}, u32[]{:S(2)}, u32[]{:S(2)}) collective-permute-start(bf16[512,256]{1,0:T(8,128)(2,1)} %collective-permute-done.3), channel_id=1, source_target_pairs={{0,2},{2,4},{4,6},{6,7},{7,5},{5,3},{3,1},{1,0},{8,9},{10,8},{12,1... | collective-permute-start | bytes 786440 | tf_op jit(solution)/shard_map/ppermute | solution.py:41
  24.7 1.4 %copy-start.5 = (f32[512,768]{1,0:T(8,128)S(1)}, f32[512,768]{1,0:T(8,128)}, u32[]{:S(2)}) copy-start(f32[512,768]{1,0:T(8,128)} %copy-done.4) | copy-start | bytes 4718596
  26.1 0.9 copy-start.12
  29.3 1.2 %copy-start.2 = (f32[512,768]{1,0:T(8,128)}, f32[512,768]{1,0:T(8,128)S(1)}, u32[]{:S(2)}) copy-start(f32[512,768]{1,0:T(8,128)S(1)} %get-tuple-element.42.refs_3_) | copy-start | bytes 4718596
  30.4 0.7 copy-start.9
  31.9 1.7 %collective-permute-start.8 = (bf16[512,256]{1,0:T(8,128)(2,1)}, bf16[512,256]{1,0:T(8,128)(2,1)S(1)}, u32[]{:S(2)}, u32[]{:S(2)}) collective-permute-start(bf16[512,256]{1,0:T(8,128)(2,1)} %collective-permute-done.6), channel_id=1, source_target_pairs={{0,8},{8,0},{16,24},{24,16},{1,9},{9,1},{17,25},{25,17},{2,10},{10... | collective-permute-start | bytes 786440 | tf_op jit(solution)/shard_map/ppermute | solution.py:45
  31.9 6.7 %collective-permute-start.9 = (bf16[512,256]{1,0:T(8,128)(2,1)}, bf16[512,256]{1,0:T(8,128)(2,1)}, u32[]{:S(2)}, u32[]{:S(2)}) collective-permute-start(bf16[512,256]{1,0:T(8,128)(2,1)} %collective-permute-done.5.refs_0_), channel_id=1, source_target_pairs={{0,2},{2,4},{4,6},{6,7},{7,5},{5,3},{3,1},{1,0},{8,9},{10,8},{12,1... | collective-permute-start | bytes 786440 | tf_op jit(solution)/shard_map/ppermute | solution.py:41
  38.6 1.4 %copy-start.3 = (f32[512,768]{1,0:T(8,128)S(1)}, f32[512,768]{1,0:T(8,128)}, u32[]{:S(2)}) copy-start(f32[512,768]{1,0:T(8,128)} %copy-done.2) | copy-start | bytes 4718596
  40.0 0.9 copy-start.10
  41.0 5.4 %copy-start.16 = (s32[2048]{0:T(1024)S(1)}, s32[2048]{0:T(1024)}, u32[]{:S(2)}) copy-start(s32[2048]{0:T(1024)} %ids.5) | copy-start | bytes 24580
  44.6 0.7 copy-start.13
  45.3 1.7 %collective-permute-start.10 = (bf16[256,512]{1,0:T(8,128)(2,1)}, bf16[256,512]{1,0:T(8,128)(2,1)S(1)}, u32[]{:S(2)}, u32[]{:S(2)}) collective-permute-start(bf16[256,512]{1,0:T(8,128)(2,1)} %get-tuple-element.45.refs_3_), channel_id=1, source_target_pairs={{0,8},{8,0},{16,24},{24,16},{1,9},{9,1},{17,25},{25,17},{2,10},{10... | collective-permute-start | bytes 786440 | tf_op jit(solution)/shard_map/ppermute | solution.py:45
  45.3 2.1 %collective-permute-start.11 = (bf16[256,512]{1,0:T(8,128)(2,1)}, bf16[256,512]{1,0:T(8,128)(2,1)S(1)}, u32[]{:S(2)}, u32[]{:S(2)}) collective-permute-start(bf16[256,512]{1,0:T(8,128)(2,1)} %get-tuple-element.46.refs_5_), channel_id=1, source_target_pairs={{0,8},{8,0},{16,24},{24,16},{1,9},{9,1},{17,25},{25,17},{2,10},{10... | collective-permute-start | bytes 786440 | tf_op jit(solution)/shard_map/ppermute | solution.py:45
  45.8 8.4 %collective-permute-start.12 = (bf16[256,512]{1,0:T(8,128)(2,1)}, bf16[256,512]{1,0:T(8,128)(2,1)S(1)}, u32[]{:S(2)}, u32[]{:S(2)}) collective-permute-start(bf16[256,512]{1,0:T(8,128)(2,1)} %get-tuple-element.45.refs_3_), channel_id=1, source_target_pairs={{0,16},{8,24},{16,0},{24,8},{1,17},{9,25},{17,1},{25,9},{2,18},{10... | collective-permute-start | bytes 786440 | tf_op jit(solution)/shard_map/ppermute | solution.py:325
  46.4 9.3 %copy-start.15 = (bf16[512,256]{1,0:T(8,128)(2,1)S(1)}, bf16[512,256]{1,0:T(8,128)(2,1)}, u32[]{:S(2)}) copy-start(bf16[512,256]{1,0:T(8,128)(2,1)} %copy-done.13) | copy-start | bytes 786436
  47.4 1.0 copy-start.14
  54.2 1.5 %collective-permute-start.13 = (bf16[256,512]{1,0:T(8,128)(2,1)S(1)}, bf16[256,512]{1,0:T(8,128)(2,1)S(1)}, u32[]{:S(2)}, u32[]{:S(2)}) collective-permute-start(bf16[256,512]{1,0:T(8,128)(2,1)S(1)} %collective-permute-done.12.refs_3_), channel_id=1, source_target_pairs={{0,8},{8,0},{16,24},{24,16},{1,9},{9,1},{17,25},{25,17},{2,10},{10... | collective-permute-start | bytes 786440 | tf_op jit(solution)/shard_map/ppermute | solution.py:45
  54.2 8.9 %collective-permute-start.14 = (bf16[256,512]{1,0:T(8,128)(2,1)}, bf16[256,512]{1,0:T(8,128)(2,1)S(1)}, u32[]{:S(2)}, u32[]{:S(2)}) collective-permute-start(bf16[256,512]{1,0:T(8,128)(2,1)} %get-tuple-element.46.refs_5_), channel_id=1, source_target_pairs={{0,16},{8,24},{16,0},{24,8},{1,17},{9,25},{17,1},{25,9},{2,18},{10... | collective-permute-start | bytes 786440 | tf_op jit(solution)/shard_map/ppermute | solution.py:325
  63.1 1.5 %collective-permute-start.15 = (bf16[256,512]{1,0:T(8,128)(2,1)S(1)}, bf16[256,512]{1,0:T(8,128)(2,1)S(1)}, u32[]{:S(2)}, u32[]{:S(2)}) collective-permute-start(bf16[256,512]{1,0:T(8,128)(2,1)S(1)} %collective-permute-done.14.refs_3_), channel_id=1, source_target_pairs={{0,8},{8,0},{16,24},{24,16},{1,9},{9,1},{17,25},{25,17},{2,10},{10... | collective-permute-start | bytes 786440 | tf_op jit(solution)/shard_map/ppermute | solution.py:45
  64.7 1.2 %copy-start.19 = (bf16[256,2048]{1,0:T(8,128)(2,1)S(1)}, bf16[256,2048]{1,0:T(8,128)(2,1)}, u32[]{:S(2)}) copy-start(bf16[256,2048]{1,0:T(8,128)(2,1)} %refs_6_.1) | copy-start | bytes 3145732
  69.1 8.3 %collective-permute-start.16 = (bf16[512,256]{1,0:T(8,128)(2,1)S(1)}, bf16[512,256]{1,0:T(8,128)(2,1)S(1)}, u32[]{:S(2)}, u32[]{:S(2)}) collective-permute-start(bf16[512,256]{1,0:T(8,128)(2,1)S(1)} %get-tuple-element.55), channel_id=1, source_target_pairs={{0,2},{2,4},{4,6},{6,7},{7,5},{5,3},{3,1},{1,0},{8,9},{10,8},{12,1... | collective-permute-start | bytes 786440 | tf_op jit(solution)/shard_map/ppermute | solution.py:41
  70.7 9.2 %collective-permute-start.21 = (bf16[512,256]{1,0:T(8,128)(2,1)S(1)}, bf16[512,256]{1,0:T(8,128)(2,1)S(1)}, u32[]{:S(2)}, u32[]{:S(2)}) collective-permute-start(bf16[512,256]{1,0:T(8,128)(2,1)S(1)} %get-tuple-element.57), channel_id=1, source_target_pairs={{0,8},{8,0},{16,24},{24,16},{1,9},{9,1},{17,25},{25,17},{2,10},{10... | collective-permute-start | bytes 786440 | tf_op jit(solution)/shard_map/ppermute | solution.py:45
  70.7 9.2 %collective-permute-start.22 = (bf16[512,256]{1,0:T(8,128)(2,1)S(1)}, bf16[512,256]{1,0:T(8,128)(2,1)S(1)}, u32[]{:S(2)}, u32[]{:S(2)}) collective-permute-start(bf16[512,256]{1,0:T(8,128)(2,1)S(1)} %get-tuple-element.58), channel_id=1, source_target_pairs={{0,9},{2,8},{4,10},{6,12},{7,14},{5,15},{3,13},{1,11},{8,2},{10,4}... | collective-permute-start | bytes 786440 | tf_op jit(solution)/shard_map/ppermute | solution.py:41
  77.5 6.4 %collective-permute-start.17 = (bf16[512,256]{1,0:T(8,128)(2,1)S(1)}, bf16[512,256]{1,0:T(8,128)(2,1)S(1)}, u32[]{:S(2)}, u32[]{:S(2)}) collective-permute-start(bf16[512,256]{1,0:T(8,128)(2,1)S(1)} %add_convert_fusion.5), channel_id=1, source_target_pairs={{0,2},{2,4},{4,6},{6,7},{7,5},{5,3},{3,1},{1,0},{8,9},{10,8},{12,1... | collective-permute-start | bytes 786440 | tf_op jit(solution)/shard_map/ppermute | solution.py:41
  79.9 6.5 %collective-permute-start.20 = (bf16[512,256]{1,0:T(8,128)(2,1)S(1)}, bf16[512,256]{1,0:T(8,128)(2,1)S(1)}, u32[]{:S(2)}, u32[]{:S(2)}) collective-permute-start(bf16[512,256]{1,0:T(8,128)(2,1)S(1)} %get-tuple-element.56), channel_id=1, source_target_pairs={{0,8},{8,0},{16,24},{24,16},{1,9},{9,1},{17,25},{25,17},{2,10},{10... | collective-permute-start | bytes 786440 | tf_op jit(solution)/shard_map/ppermute | solution.py:45
  80.0 6.8 %collective-permute-start.23 = (bf16[512,256]{1,0:T(8,128)(2,1)S(1)}, bf16[512,256]{1,0:T(8,128)(2,1)S(1)}, u32[]{:S(2)}, u32[]{:S(2)}) collective-permute-start(bf16[512,256]{1,0:T(8,128)(2,1)S(1)} %add_convert_fusion.2), channel_id=1, source_target_pairs={{0,2},{2,4},{4,6},{6,7},{7,5},{5,3},{3,1},{1,0},{8,9},{10,8},{12,1... | collective-permute-start | bytes 786440 | tf_op jit(solution)/shard_map/ppermute | solution.py:41
  84.0 6.4 %collective-permute-start.18 = (bf16[512,256]{1,0:T(8,128)(2,1)S(1)}, bf16[512,256]{1,0:T(8,128)(2,1)S(1)}, u32[]{:S(2)}, u32[]{:S(2)}) collective-permute-start(bf16[512,256]{1,0:T(8,128)(2,1)S(1)} %add_convert_fusion.4), channel_id=1, source_target_pairs={{0,2},{2,4},{4,6},{6,7},{7,5},{5,3},{3,1},{1,0},{8,9},{10,8},{12,1... | collective-permute-start | bytes 786440 | tf_op jit(solution)/shard_map/ppermute | solution.py:41
  86.8 6.3 %collective-permute-start.24 = (bf16[512,256]{1,0:T(8,128)(2,1)S(1)}, bf16[512,256]{1,0:T(8,128)(2,1)S(1)}, u32[]{:S(2)}, u32[]{:S(2)}) collective-permute-start(bf16[512,256]{1,0:T(8,128)(2,1)S(1)} %add_convert_fusion.1), channel_id=1, source_target_pairs={{0,10},{2,12},{4,14},{6,15},{7,13},{5,11},{3,9},{1,8},{8,1},{10,0}... | collective-permute-start | bytes 786440 | tf_op jit(solution)/shard_map/ppermute | solution.py:41
  90.5 6.4 %collective-permute-start.19 = (bf16[512,256]{1,0:T(8,128)(2,1)S(1)}, bf16[512,256]{1,0:T(8,128)(2,1)S(1)}, u32[]{:S(2)}, u32[]{:S(2)}) collective-permute-start(bf16[512,256]{1,0:T(8,128)(2,1)S(1)} %add_convert_fusion.3), channel_id=1, source_target_pairs={{0,2},{2,4},{4,6},{6,7},{7,5},{5,3},{3,1},{1,0},{8,9},{10,8},{12,1... | collective-permute-start | bytes 786440 | tf_op jit(solution)/shard_map/ppermute | solution.py:41

commit v5 on v4

--- a/solution.py
+++ b/solution.py
@@ -63,7 +63,7 @@
         fetch(n).wait()
     tile = math.gcd(rows, 128)
 
-    def step(index, out_at, store):
+    def step(index, store):
         here = pl.ds(pl.multiple_of(index * tile, tile), tile)
         power = power_in[here, :] if has_state else None
         scaled = []
@@ -82,40 +82,43 @@
                 product = jnp.dot(x, w_ref[n, group], preferred_element_type=F32)
                 total = product if total is None else total + product
             sums.append(total)
-        store(here, out_at, sums, power)
+        store(here, sums, power)
 
     if head_size is None:
         acc, power_out = outs
 
-        def keep(here, out_at, sums, power):
+        def keep(here, sums, power):
             for group, total in enumerate(sums):
                 acc[here, group * out_width : (group + 1) * out_width] = total
             power_out[here, :] = power
 
-        pl.loop(0, rows // tile)(lambda index: step(index, None, keep))
+        pl.loop(0, rows // tile)(lambda index: step(index, keep))
         return
 
-    q_ref, kv_refs = outs[0], outs[1:]
-    per = kv_refs[0].shape[0] // tile
-    for number, kv_ref in enumerate(kv_refs):
-
-        def finish(here, there, sums, power):
-            mean = jnp.sum(power, axis=-1, keepdims=True) * (1.0 / w_hbm.shape[1])
-            scale = lax.rsqrt(mean + 1e-06)
-            q, k, v = (total * scale for total in sums)
-            for head in range(out_width // head_size):
-                lanes = slice(head * head_size, (head + 1) * head_size)
-                qh, kh = q[:, lanes], k[:, lanes]
-                q_size = lax.rsqrt(jnp.sum(qh * qh, axis=-1, keepdims=True) + 1e-06)
-                k_size = lax.rsqrt(jnp.sum(kh * kh, axis=-1, keepdims=True) + 1e-06)
-                q_ref[here, lanes] = (qh * (q_size * (factor[head] * LOG2E))).astype(BF16)
-                kv_ref[there, lanes] = (kh * k_size).astype(BF16)
-            kv_ref[there, out_width:] = v.astype(BF16)
-
-        @pl.loop(0, per)
-        def _(index):
-            there = pl.ds(pl.multiple_of(index * tile, tile), tile)
-            step(number * per + index, there, finish)
+    q_ref, kv_ref = outs
+
+    def finish(here, sums, power):
+        mean = jnp.sum(power, axis=-1, keepdims=True) * (1.0 / w_hbm.shape[1])
+        scale = lax.rsqrt(mean + 1e-06)
+        q, k, v = (total * scale for total in sums)
+        for head in range(out_width // head_size):
+            lanes = slice(head * head_size, (head + 1) * head_size)
+            qh, kh = q[:, lanes], k[:, lanes]
+            q_size = lax.rsqrt(jnp.sum(qh * qh, axis=-1, keepdims=True) + 1e-06)
+            k_size = lax.rsqrt(jnp.sum(kh * kh, axis=-1, keepdims=True) + 1e-06)
+            q_ref[here, lanes] = (qh * (q_size * (factor[head] * LOG2E))).astype(BF16)
+            kv_ref[here, lanes] = (kh * k_size).astype(BF16)
+        kv_ref[here, out_width:] = v.astype(BF16)
+
+    pl.loop(0, rows // tile)(lambda index: step(index, finish))
+
+
+def in_hbm(value):
+    return pltpu.with_memory_space_constraint(value, pltpu.HBM)
+
+
+def in_vmem(value):
+    return pltpu.with_memory_space_constraint(value, pltpu.VMEM)
 
 
 def gather_step(at, factor, blocks, gain, weights, state, head_size=None):
@@ -125,12 +128,11 @@
     if head_size is None:
         shapes, kinds = [(rows, groups * out_width), (rows, 128)], [F32, F32]
     else:
-        shapes = [(rows, out_width), (rows // 2, 2 * out_width), (rows // 2, 2 * out_width)]
-        kinds = [BF16, BF16, BF16]
-    operands = [*blocks, *(state or ())]
+        shapes, kinds = [(rows, out_width), (rows, 2 * out_width)], [BF16, BF16]
+    operands = [*blocks, *map(in_vmem, state or ())]
     return pl.pallas_call(
         functools.partial(gather_kernel, count, bool(state), head_size),
-        out_shape=tuple(jax.ShapeDtypeStruct(s, k) for s, k in zip(shapes, kinds)),
+        out_shape=tuple(pltpu.VMEM(s, k) for s, k in zip(shapes, kinds)),
         in_specs=[SMEM, SMEM, VMEM, pl.BlockSpec(memory_space=pltpu.HBM)] + [VMEM] * len(operands),
         out_specs=(VMEM,) * len(shapes),
         scratch_shapes=[
@@ -145,7 +147,7 @@
             transcendentals=0,
         ),
         name="gather_step" if head_size is None else "gather_last",
-    )(at, factor, gain, weights, *operands)
+    )(at, in_hbm(factor), in_hbm(gain), in_hbm(weights), *operands)
 
 
 def attend_blocks(sources, ids, q_first, q_refs, id_col, id_row, kv_refs, v_ones, acc, head_size):
@@ -243,15 +245,15 @@
         pltpu.VMEM((heads, keys, 2 * head_size), BF16),
         pltpu.VMEM((total, 2 * width), F32),
     ]
-    operands = [*queries, id_col, id_row, *kvs]
+    operands = [*map(in_vmem, queries), id_col, in_hbm(id_row), *map(in_vmem, kvs)]
     if acc is not None:
-        operands.append(acc)
+        operands.append(in_vmem(acc))
     if count_out:
-        operands.append(w_out)
+        operands.append(in_hbm(w_out))
         scratch.append(pltpu.VMEM((total, width), BF16))
-        shape = jax.ShapeDtypeStruct((total, w_out.shape[1] // count_out), BF16)
+        shape = pltpu.VMEM((total, w_out.shape[1] // count_out), BF16)
     else:
-        shape = jax.ShapeDtypeStruct((rows, 2 * width), F32)
+        shape = pltpu.VMEM((rows, 2 * width), F32)
     outs = count_out or len(queries)
     return pl.pallas_call(
         functools.partial(
@@ -270,7 +272,7 @@
             transcendentals=total * keys * len(kvs) * heads,
         ),
         name="attend_last" if count_out else "attend",
-    )(info, ids, *operands)
+    )(info, in_hbm(ids), *operands)
 
 
 def total_of(*parts):
@@ -281,7 +283,6 @@
     ring, seqs = mesh_shape["head"], mesh_shape["seq"]
     outer = seqs // 2
     rows, width = tokens.shape
-    half = rows // 2
     head_size = w_qkv.shape[2] // head_scale.shape[0]
     head_at, seq_at = lax.axis_index("head"), lax.axis_index("seq")
     place = ring_place(head_at, ring)
@@ -289,58 +290,51 @@
     toward = 1 - 2 * core
     index_at = lambda offset: ring_index((place + toward * offset + ring) % ring, ring)
     numbers = lambda values: jnp.stack(values).astype(jnp.int32)
-    id_row = scale_ids.reshape(-1, 1, half)
+    id_row = scale_ids.reshape(-1, 1, rows)
     id_col = lax.dynamic_slice_in_dim(scale_ids, seq_at * rows, rows)[:, None]
 
     farthest = ring // 2
     gain = norm_gain.reshape(ring, width)
     own = other = tokens
-    waiting, offsets, state = [tokens], [0], None
+    waiting, offsets, state = [in_hbm(tokens)], [0], None
     for step in range(1, farthest):
         own = along(own, seqs, ring)
         other = along(other, seqs, ring, start_lane=int(step == 1))
         if state is not None:
             own, other, state = lax.optimization_barrier((own, other, state))
-        waiting += [own, swapped(other, seqs)]
+        waiting += [in_vmem(own), in_vmem(swapped(other, seqs))]
         offsets += [-step, step]
         if step < farthest - 1:
             at = numbers([index_at(offset) for offset in offsets])
             state = gather_step(at, head_scale, waiting, gain, w_qkv, state)
             waiting, offsets = [], []
-    waiting.append(along(own, seqs, ring))
+    waiting.append(in_vmem(along(own, seqs, ring)))
     offsets.append(-farthest)
     at = numbers([index_at(offset) for offset in offsets])
-    query, *kvs = gather_step(at, head_scale, waiting, gain, w_qkv, state, head_size)
-
-    near, near_at = [], []
-    far, far_at = [[] for kv in kvs], [[] for kv in kvs]
-    for s, kv in enumerate(kvs):
-        for step in range(outer):
-            source = 2 * ((chip + outer - step) % outer)
-            places = [(source + core) * rows + s * half, (source + 1 - core) * rows + s * half]
-            if step:
-                shift = [
-                    (2 * a + b, 2 * ((a + step) % outer) + b) for a in range(outer) for b in (0, 1)
-                ]
-                far[s].append(lax.ppermute(kv, "seq", shift))
-                far_at[s] += places
-            else:
-                near += [kv, swapped(kv, seqs)]
-                near_at += places
+    query, kv = gather_step(at, head_scale, waiting, gain, w_qkv, state, head_size)
+
+    far, straight, crossed = [], [], []
+    for step in range(outer):
+        source = 2 * ((chip + outer - step) % outer)
+        straight.append((source + core) * rows)
+        crossed.append((source + 1 - core) * rows)
+        if step:
+            far.append(lax.ppermute(kv, "seq", [
+                (2 * a + b, 2 * ((a + step) % outer) + b) for a in range(outer) for b in (0, 1)
+            ]))
     first = [seq_at * rows]
-    (acc,) = attend(numbers(near_at + first), scale_ids, [query], id_col, id_row, near, head_size)
+    info = numbers(straight[:1] + crossed[:1] + first)
+    keys = [kv, swapped(kv, seqs)]
+    (acc,) = attend(info, scale_ids, [query], id_col, id_row, keys, head_size)
+    acc, far = lax.optimization_barrier((acc, far))
+    far_crossed = [swapped(block, seqs) for block in far]
+    info = numbers(straight[1:] + first)
+    (acc,) = attend(info, scale_ids, [query], id_col, id_row, far, head_size, acc)
+
     goals = list(range(farthest, -farthest, -1))
-    for s in range(len(kvs)):
-        acc, far[s] = lax.optimization_barrier((acc, far[s]))
-        blocks = [data for block in far[s] for data in (block, swapped(block, seqs))]
-        if s + 1 < len(kvs):
-            (acc,) = attend(
-                numbers(far_at[s] + first), scale_ids, [query], id_col, id_row, blocks, head_size,
-                acc,
-            )
-    info = numbers(far_at[-1] + first + [index_at(goal) for goal in goals])
+    info = numbers(crossed[1:] + first + [index_at(goal) for goal in goals])
     parts = attend(
-        info, scale_ids, [query], id_col, id_row, blocks, head_size, acc, w_out, ring
+        info, scale_ids, [query], id_col, id_row, far_crossed, head_size, acc, w_out, ring
     )
     parts = dict(zip(goals, parts))
     own = along(parts[farthest], seqs, ring)

time: 99.1 us -> 88.7 us (0.90)
  local copies, waits for them, and re-layouts: 17.6 us -> 7.24 us
    unnamed x40 -> x12, local copies, waits for them, and re-layouts: 16.5 us -> 4.96 us
    ppermute x2 -> x1, waiting for transfers between devices: 6.07 us -> 9.13 us  [body(): lax.ppermute(kv, 'seq', [(2 * a + b, 2 * ((a + step) % outer) + b) for a...]
    ppermute x9 -> x7, waiting for transfers between devices: 3.27 us -> 0.42 us  [swapped(): lax.ppermute(value, 'seq', [(seq, seq + 1 - 2 * (seq % 2)) for seq in ran...]
    pallas_call x3, Pallas kernels: 8.47 us -> 10.4 us  [gather_step(): pl.pallas_call(functools.partial(gather_kernel, count, bool(state), head_...]
    pallas_call x3, Pallas kernels: 10.4 us -> 8.69 us  [attend(): pl.pallas_call(functools.partial(attend_kernel, len(queries), len(kvs), h...]
  transfers between devices with their start and end apart: 25 -> 22, of which waited for: 17 -> 13; matrix products, arithmetic and copies ran while one was open for 2% -> 3% of each run, Pallas kernels for 12% -> 14%
where the time goes in v5:
time: 88.7 us; the launch traced here: 87.7 us
  waiting for transfers between devices  40.7 us (46%)
  Pallas kernels  19.1 us (22%)
  starting transfers between devices  19 us (21%)
  local copies, waits for them, and re-layouts  7.24 us (8%)
  other arithmetic  1.52 us (2%)
    ppermute x14, waiting for transfers between devices, along(): return lax.ppermute(value, ('seq', 'head'), pairs)  31.2 us
    ppermute x14, starting transfers between devices, along(): return lax.ppermute(value, ('seq', 'head'), pairs)  18.3 us
    pallas_call x3, Pallas kernels, gather_step(): pl.pallas_call(functools.partial(gather_kernel, count, bool(state), head_...  10.4 us
    ppermute x1, waiting for transfers between devices, body(): lax.ppermute(kv, 'seq', [(2 * a + b, 2 * ((a + step) % outer) + b) for a...  9.13 us
    pallas_call x3, Pallas kernels, attend(): pl.pallas_call(functools.partial(attend_kernel, len(queries), len(kvs), h...  8.69 us
    unnamed x12, local copies, waits for them, and re-layouts  4.96 us
  transfers between devices with their start and end apart: 22, of which 13 were waited for; matrix products, arithmetic and copies ran while one was open for 3% of the time, Pallas kernels for 14%

profile of v5, /device:TPU:10, one launch (start us, length us, event | category | flops | bytes accessed | tf_op | source)
XLA Modules:
  0.0 87.7 jit_solution(14446485853305709609)
XLA Ops:
  0.0 1.6 %collective-permute-start = (bf16[512,256]{1,0:T(8,128)(2,1)}, bf16[512,256]{1,0:T(8,128)(2,1)S(1)}, u32[]{:S(2)}, u32[]{:S(2)}) collective-permute-start(bf16[512,256]{1,0:T(8,128)(2,1)} %refs_0_.1), channel_id=1, source_target_pairs={{0,2},{2,4},{4,6},{6,7},{7,5},{5,3},{3,1},{1,0},{8,9},{10,8},{12,1... | collective-permute-start | bytes 786440 | tf_op jit(solution)/shard_map/ppermute | solution.py:41
  1.6 6.7 %collective-permute-done.2 = bf16[512,256]{1,0:T(8,128)(2,1)S(1)} collective-permute-done((bf16[512,256]{1,0:T(8,128)(2,1)}, bf16[512,256]{1,0:T(8,128)(2,1)S(1)}, u32[]{:S(2)}, u32[]{:S(2)}) %collective-permute-start.2) | collective-permute-done | bytes 262176 | tf_op jit(solution)/shard_map/ppermute | solution.py:41
  8.3 0.6 collective-permute-done.refs_1_
  8.8 1.6 %collective-permute-start.1 = (bf16[512,256]{1,0:T(8,128)(2,1)S(1)}, bf16[512,256]{1,0:T(8,128)(2,1)S(1)}, u32[]{:S(2)}, u32[]{:S(2)}) collective-permute-start(bf16[512,256]{1,0:T(8,128)(2,1)S(1)} %collective-permute-done.refs_1_), channel_id=1, source_target_pairs={{0,2},{2,4},{4,6},{6,7},{7,5},{5,3},{3,1},{1,0},{8,9},{10,8},{12,1... | collective-permute-start | bytes 786440 | tf_op jit(solution)/shard_map/ppermute | solution.py:41
  10.4 1.6 %collective-permute-start.3 = (bf16[512,256]{1,0:T(8,128)(2,1)S(1)}, bf16[512,256]{1,0:T(8,128)(2,1)}, u32[]{:S(2)}, u32[]{:S(2)}) collective-permute-start(bf16[512,256]{1,0:T(8,128)(2,1)S(1)} %collective-permute-done.2), channel_id=1, source_target_pairs={{0,2},{2,4},{4,6},{6,7},{7,5},{5,3},{3,1},{1,0},{8,9},{10,8},{12,1... | collective-permute-start | bytes 786440 | tf_op jit(solution)/shard_map/ppermute | solution.py:41
  12.0 1.3 %reshape.6.gain_ref = f32[8,256]{1,0:T(8,128)} reshape(f32[2048]{0:T(1024)} %param.7) | data formatting | bytes 16384 | tf_op jit(solution)/shard_map/reshape | solution.py:297
  13.3 0.1 pad_add_fusion.1.at
  13.3 3.6 %gather_step.2 = (f32[512,768]{1,0:T(8,128)S(1)}, f32[512,128]{1,0:T(8,128)S(1)}) custom-call(s32[3]{0:T(128)S(1)} %pad_add_fusion.1.at, f32[2]{0:T(128)} %factor.5, f32[8,256]{1,0:T(8,128)} %reshape.6.gain_ref, bf16[3,2048,256]{2,1,0:T(8,128)(2,1)} %w_hbm.5, bf16[512,256]{1,0:T(8,128)(2,1)} %refs_0_.1, bf16[512,256]{1,0:T(8,128)(2,1)S(1)} %collective-permute-done.refs_1_, ...), custom_call_target="tpu_custom_call" | custom-call | flops 603979776 | bytes 5111808 | tf_op jit(solution)/shard_map/gather_step/pallas_call | solution.py:133
  16.9 0.7 copy-done.2
  17.7 0.4 collective-permute-done.3
  18.1 1.6 %collective-permute-start.5 = (bf16[512,256]{1,0:T(8,128)(2,1)S(1)}, bf16[512,256]{1,0:T(8,128)(2,1)}, u32[]{:S(2)}, u32[]{:S(2)}) collective-permute-start(bf16[512,256]{1,0:T(8,128)(2,1)S(1)} %collective-permute-done.1.refs_0_), channel_id=1, source_target_pairs={{0,2},{2,4},{4,6},{6,7},{7,5},{5,3},{3,1},{1,0},{8,9},{10,8},{12,1... | collective-permute-start | bytes 786440 | tf_op jit(solution)/shard_map/ppermute | solution.py:41
  19.7 1.6 %collective-permute-start.6 = (bf16[512,256]{1,0:T(8,128)(2,1)}, bf16[512,256]{1,0:T(8,128)(2,1)}, u32[]{:S(2)}, u32[]{:S(2)}) collective-permute-start(bf16[512,256]{1,0:T(8,128)(2,1)} %collective-permute-done.3), channel_id=1, source_target_pairs={{0,2},{2,4},{4,6},{6,7},{7,5},{5,3},{3,1},{1,0},{8,9},{10,8},{12,1... | collective-permute-start | bytes 786440 | tf_op jit(solution)/shard_map/ppermute | solution.py:41
  21.3 0.1 pad_add_fusion.2.at
  21.3 0.7 copy-done.4
  22.0 0.9 %copy-done.3 = f32[512,128]{1,0:T(8,128)S(1)} copy-done((f32[512,128]{1,0:T(8,128)S(1)}, f32[512,128]{1,0:T(8,128)}, u32[]{:S(2)}) %copy-start.3) | copy-done | bytes 262168
  23.0 0.9 %copy-done.5 = bf16[512,256]{1,0:T(8,128)(2,1)S(1)} copy-done((bf16[512,256]{1,0:T(8,128)(2,1)S(1)}, bf16[512,256]{1,0:T(8,128)(2,1)}, u32[]{:S(2)}) %copy-start.5) | copy-done | bytes 262168
  23.9 2.9 %gather_step.3 = (f32[512,768]{1,0:T(8,128)S(1)}, f32[512,128]{1,0:T(8,128)S(1)}) custom-call(s32[2]{0:T(128)S(1)} %pad_add_fusion.2.at, f32[2]{0:T(128)} %factor.5, f32[8,256]{1,0:T(8,128)} %reshape.6.gain_ref, bf16[3,2048,256]{2,1,0:T(8,128)(2,1)} %w_hbm.5, bf16[512,256]{1,0:T(8,128)(2,1)S(1)} %collective-permute-done.1.refs_0_, ...), custom_call_target="tpu_custom_call" | custom-call | flops 402653184 | bytes 4456448 | tf_op jit(solution)/shard_map/gather_step/pallas_call | solution.py:133
  26.9 0.7 copy-done
  27.6 1.6 %collective-permute-start.9 = (bf16[512,256]{1,0:T(8,128)(2,1)}, bf16[512,256]{1,0:T(8,128)(2,1)S(1)}, u32[]{:S(2)}, u32[]{:S(2)}) collective-permute-start(bf16[512,256]{1,0:T(8,128)(2,1)} %collective-permute-done.5.refs_0_), channel_id=1, source_target_pairs={{0,2},{2,4},{4,6},{6,7},{7,5},{5,3},{3,1},{1,0},{8,9},{10,8},{12,1... | collective-permute-start | bytes 786440 | tf_op jit(solution)/shard_map/ppermute | solution.py:41
  29.2 0.1 pad_add_fusion.at
  29.3 0.1 collective-permute-done.8.refs_1_
  29.4 4.9 %collective-permute-done.9.refs_2_ = bf16[512,256]{1,0:T(8,128)(2,1)S(1)} collective-permute-done((bf16[512,256]{1,0:T(8,128)(2,1)}, bf16[512,256]{1,0:T(8,128)(2,1)S(1)}, u32[]{:S(2)}, u32[]{:S(2)}) %collective-permute-start.9) | collective-permute-done | bytes 262176 | tf_op jit(solution)/shard_map/ppermute | solution.py:41
  34.3 0.9 %copy-done.1 = f32[512,128]{1,0:T(8,128)S(1)} copy-done((f32[512,128]{1,0:T(8,128)S(1)}, f32[512,128]{1,0:T(8,128)}, u32[]{:S(2)}) %copy-start.1) | copy-done | bytes 262168
  35.2 3.9 %gather_last.1 = (bf16[512,256]{1,0:T(8,128)(2,1)S(1)}, bf16[512,512]{1,0:T(8,128)(2,1)S(1)}) custom-call(s32[3]{0:T(128)S(1)} %pad_add_fusion.at, f32[2]{0:T(128)} %factor.5, f32[8,256]{1,0:T(8,128)} %reshape.6.gain_ref, bf16[3,2048,256]{2,1,0:T(8,128)(2,1)} %w_hbm.5, bf16[512,256]{1,0:T(8,128)(2,1)} %collective-permute-done.5.refs_0_, ...), custom_call_target="tpu_custom_call" | custom-call | flops 603979776 | bytes 5111808 | tf_op jit(solution)/shard_map/gather_last/pallas_call | solution.py:133
  39.2 0.6 collective-permute-start.11
  39.7 0.8 dynamic_slice.3
  40.5 0.1 copy.9.refs_1_
  40.7 0.1 pad_add_fusion.3.info
  40.7 0.3 collective-permute-done.10.refs_4_
  41.0 3.3 %attend.2.refs_4_ = f32[512,512]{1,0:T(8,128)S(1)} custom-call(s32[3]{0:T(128)S(1)} %pad_add_fusion.3.info, s32[2048]{0:T(1024)} %ids.5, bf16[512,256]{1,0:T(8,128)(2,1)S(1)} %get-tuple-element.41.refs_0_, s32[512,1]{1,0:T(8,128)S(1)} %copy.9.refs_1_, s32[4,1,512]{2,1,0:T(1,128)} %bitcast.16, bf16[512,512]{1,0:T(8,128)(2,1)S(1)} %get-tuple-element.42.refs_3_, ...), custom_call_target="tpu_custom_call" | custom-call | flops 805306368 | bytes 2097152 | tf_op jit(solution)/shard_map/attend/pallas_call | solution.py:258
  44.4 9.1 %collective-permute-done.11.refs_3_ = bf16[512,512]{1,0:T(8,128)(2,1)S(1)} collective-permute-done((bf16[512,512]{1,0:T(8,128)(2,1)S(1)}, bf16[512,512]{1,0:T(8,128)(2,1)S(1)}, u32[]{:S(2)}, u32[]{:S(2)}) %collective-permute-start.11) | collective-permute-done | bytes 524320 | tf_op jit(solution)/shard_map/ppermute | solution.py:322
  53.5 0.1 stack.79.info
  53.7 2.1 %attend.3.refs_4_ = f32[512,512]{1,0:T(8,128)S(1)} custom-call(s32[2]{0:T(128)S(1)} %pad_add_fusion.4.info, s32[2048]{0:T(1024)} %ids.5, bf16[512,256]{1,0:T(8,128)(2,1)S(1)} %get-tuple-element.41.refs_0_, s32[512,1]{1,0:T(8,128)S(1)} %copy.9.refs_1_, s32[4,1,512]{2,1,0:T(1,128)} %bitcast.17, bf16[512,512]{1,0:T(8,128)(2,1)S(1)} %collective-permute-done.11.refs_3_, ...), custom_call_target="tpu_custom_call" | custom-call | flops 402653184 | bytes 1572864 | tf_op jit(solution)/shard_map/attend/pallas_call | solution.py:258
  55.8 3.3 %attend_last.1 = (bf16[512,256]{1,0:T(8,128)(2,1)S(1)}, bf16[512,256]{1,0:T(8,128)(2,1)S(1)}, bf16[512,256]{1,0:T(8,128)(2,1)S(1)}, bf16[512,256]{1,0:T(8,128)(2...) custom-call(s32[10]{0:T(128)S(1)} %stack.79.info, ...), custom_call_target="tpu_custom_call" | custom-call | flops 939524096 | bytes 1572864 | tf_op jit(solution)/shard_map/attend_last/pallas_call | solution.py:258
  59.1 1.6 %collective-permute-start.13 = (bf16[512,256]{1,0:T(8,128)(2,1)S(1)}, bf16[512,256]{1,0:T(8,128)(2,1)S(1)}, u32[]{:S(2)}, u32[]{:S(2)}) collective-permute-start(bf16[512,256]{1,0:T(8,128)(2,1)S(1)} %get-tuple-element.49), channel_id=1, source_target_pairs={{0,2},{2,4},{4,6},{6,7},{7,5},{5,3},{3,1},{1,0},{8,9},{10,8},{12,1... | collective-permute-start | bytes 786440 | tf_op jit(solution)/shard_map/ppermute | solution.py:41
  60.6 0.6 collective-permute-start.19
  61.3 6.1 %collective-permute-done.13 = bf16[512,256]{1,0:T(8,128)(2,1)S(1)} collective-permute-done((bf16[512,256]{1,0:T(8,128)(2,1)S(1)}, bf16[512,256]{1,0:T(8,128)(2,1)S(1)}, u32[]{:S(2)}, u32[]{:S(2)}) %collective-permute-start.13) | collective-permute-done | bytes 262176 | tf_op jit(solution)/shard_map/ppermute | solution.py:41
  67.4 1.8 %collective-permute-start.14 = (bf16[512,256]{1,0:T(8,128)(2,1)S(1)}, bf16[512,256]{1,0:T(8,128)(2,1)S(1)}, u32[]{:S(2)}, u32[]{:S(2)}) collective-permute-start(bf16[512,256]{1,0:T(8,128)(2,1)S(1)} %add_convert_fusion.5), channel_id=1, source_target_pairs={{0,2},{2,4},{4,6},{6,7},{7,5},{5,3},{3,1},{1,0},{8,9},{10,8},{12,1... | collective-permute-start | bytes 786440 | tf_op jit(solution)/shard_map/ppermute | solution.py:41
  69.3 1.2 %collective-permute-start.20 = (bf16[512,256]{1,0:T(8,128)(2,1)S(1)}, bf16[512,256]{1,0:T(8,128)(2,1)S(1)}, u32[]{:S(2)}, u32[]{:S(2)}) collective-permute-start(bf16[512,256]{1,0:T(8,128)(2,1)S(1)} %add_convert_fusion.2), channel_id=1, source_target_pairs={{0,2},{2,4},{4,6},{6,7},{7,5},{5,3},{3,1},{1,0},{8,9},{10,8},{12,1... | collective-permute-start | bytes 786440 | tf_op jit(solution)/shard_map/ppermute | solution.py:41
  70.5 3.3 %collective-permute-done.14 = bf16[512,256]{1,0:T(8,128)(2,1)S(1)} collective-permute-done((bf16[512,256]{1,0:T(8,128)(2,1)S(1)}, bf16[512,256]{1,0:T(8,128)(2,1)S(1)}, u32[]{:S(2)}, u32[]{:S(2)}) %collective-permute-start.14) | collective-permute-done | bytes 262176 | tf_op jit(solution)/shard_map/ppermute | solution.py:41
  73.9 1.8 %collective-permute-start.15 = (bf16[512,256]{1,0:T(8,128)(2,1)S(1)}, bf16[512,256]{1,0:T(8,128)(2,1)S(1)}, u32[]{:S(2)}, u32[]{:S(2)}) collective-permute-start(bf16[512,256]{1,0:T(8,128)(2,1)S(1)} %add_convert_fusion.4), channel_id=1, source_target_pairs={{0,2},{2,4},{4,6},{6,7},{7,5},{5,3},{3,1},{1,0},{8,9},{10,8},{12,1... | collective-permute-start | bytes 786440 | tf_op jit(solution)/shard_map/ppermute | solution.py:41
  75.7 1.0 %collective-permute-done.20 = bf16[512,256]{1,0:T(8,128)(2,1)S(1)} collective-permute-done((bf16[512,256]{1,0:T(8,128)(2,1)S(1)}, bf16[512,256]{1,0:T(8,128)(2,1)S(1)}, u32[]{:S(2)}, u32[]{:S(2)}) %collective-permute-start.20) | collective-permute-done | bytes 262176 | tf_op jit(solution)/shard_map/ppermute | solution.py:41
  76.7 0.1 collective-permute-start.21
  76.8 3.5 %collective-permute-done.15 = bf16[512,256]{1,0:T(8,128)(2,1)S(1)} collective-permute-done((bf16[512,256]{1,0:T(8,128)(2,1)S(1)}, bf16[512,256]{1,0:T(8,128)(2,1)S(1)}, u32[]{:S(2)}, u32[]{:S(2)}) %collective-permute-start.15) | collective-permute-done | bytes 262176 | tf_op jit(solution)/shard_map/ppermute | solution.py:41
  80.4 1.8 %collective-permute-start.16 = (bf16[512,256]{1,0:T(8,128)(2,1)S(1)}, bf16[512,256]{1,0:T(8,128)(2,1)S(1)}, u32[]{:S(2)}, u32[]{:S(2)}) collective-permute-start(bf16[512,256]{1,0:T(8,128)(2,1)S(1)} %add_convert_fusion.3), channel_id=1, source_target_pairs={{0,2},{2,4},{4,6},{6,7},{7,5},{5,3},{3,1},{1,0},{8,9},{10,8},{12,1... | collective-permute-start | bytes 786440 | tf_op jit(solution)/shard_map/ppermute | solution.py:41
  82.2 0.4 collective-permute-done.21
  82.6 4.3 %collective-permute-done.16 = bf16[512,256]{1,0:T(8,128)(2,1)S(1)} collective-permute-done((bf16[512,256]{1,0:T(8,128)(2,1)S(1)}, bf16[512,256]{1,0:T(8,128)(2,1)S(1)}, u32[]{:S(2)}, u32[]{:S(2)}) %collective-permute-start.16) | collective-permute-done | bytes 262176 | tf_op jit(solution)/shard_map/ppermute | solution.py:41
  86.9 0.8 add_convert_fusion
  (29 shorter events, 0.5 us)
Async XLA Ops:
  0.0 8.3 %collective-permute-start.2 = (bf16[512,256]{1,0:T(8,128)(2,1)}, bf16[512,256]{1,0:T(8,128)(2,1)S(1)}, u32[]{:S(2)}, u32[]{:S(2)}) collective-permute-start(bf16[512,256]{1,0:T(8,128)(2,1)} %refs_0_.1), channel_id=1, source_target_pairs={{0,9},{2,8},{4,10},{6,12},{7,14},{5,15},{3,13},{1,11},{8,2},{10,4}... | collective-permute-start | bytes 786440 | tf_op jit(solution)/shard_map/ppermute | solution.py:41
  0.0 8.8 %collective-permute-start = (bf16[512,256]{1,0:T(8,128)(2,1)}, bf16[512,256]{1,0:T(8,128)(2,1)S(1)}, u32[]{:S(2)}, u32[]{:S(2)}) collective-permute-start(bf16[512,256]{1,0:T(8,128)(2,1)} %refs_0_.1), channel_id=1, source_target_pairs={{0,2},{2,4},{4,6},{6,7},{7,5},{5,3},{3,1},{1,0},{8,9},{10,8},{12,1... | collective-permute-start | bytes 786440 | tf_op jit(solution)/shard_map/ppermute | solution.py:41
  8.3 5.1 %collective-permute-start.4 = (bf16[512,256]{1,0:T(8,128)(2,1)S(1)}, bf16[512,256]{1,0:T(8,128)(2,1)S(1)}, u32[]{:S(2)}, u32[]{:S(2)}) collective-permute-start(bf16[512,256]{1,0:T(8,128)(2,1)S(1)} %collective-permute-done.2), channel_id=1, source_target_pairs={{0,8},{8,0},{16,24},{24,16},{1,9},{9,1},{17,25},{25,17},{2,10},{10... | collective-permute-start | bytes 786440 | tf_op jit(solution)/shard_map/ppermute | solution.py:45
  8.8 8.8 %collective-permute-start.1 = (bf16[512,256]{1,0:T(8,128)(2,1)S(1)}, bf16[512,256]{1,0:T(8,128)(2,1)S(1)}, u32[]{:S(2)}, u32[]{:S(2)}) collective-permute-start(bf16[512,256]{1,0:T(8,128)(2,1)S(1)} %collective-permute-done.refs_1_), channel_id=1, source_target_pairs={{0,2},{2,4},{4,6},{6,7},{7,5},{5,3},{3,1},{1,0},{8,9},{10,8},{12,1... | collective-permute-start | bytes 786440 | tf_op jit(solution)/shard_map/ppermute | solution.py:41
  10.4 7.7 %collective-permute-start.3 = (bf16[512,256]{1,0:T(8,128)(2,1)S(1)}, bf16[512,256]{1,0:T(8,128)(2,1)}, u32[]{:S(2)}, u32[]{:S(2)}) collective-permute-start(bf16[512,256]{1,0:T(8,128)(2,1)S(1)} %collective-permute-done.2), channel_id=1, source_target_pairs={{0,2},{2,4},{4,6},{6,7},{7,5},{5,3},{3,1},{1,0},{8,9},{10,8},{12,1... | collective-permute-start | bytes 786440 | tf_op jit(solution)/shard_map/ppermute | solution.py:41
  16.9 0.7 copy-start.2
  18.1 3.2 %collective-permute-start.7 = (bf16[512,256]{1,0:T(8,128)(2,1)}, bf16[512,256]{1,0:T(8,128)(2,1)S(1)}, u32[]{:S(2)}, u32[]{:S(2)}) collective-permute-start(bf16[512,256]{1,0:T(8,128)(2,1)} %collective-permute-done.3), channel_id=1, source_target_pairs={{0,8},{8,0},{16,24},{24,16},{1,9},{9,1},{17,25},{25,17},{2,10},{10... | collective-permute-start | bytes 786440 | tf_op jit(solution)/shard_map/ppermute | solution.py:45
  18.1 9.5 %collective-permute-start.5 = (bf16[512,256]{1,0:T(8,128)(2,1)S(1)}, bf16[512,256]{1,0:T(8,128)(2,1)}, u32[]{:S(2)}, u32[]{:S(2)}) collective-permute-start(bf16[512,256]{1,0:T(8,128)(2,1)S(1)} %collective-permute-done.1.refs_0_), channel_id=1, source_target_pairs={{0,2},{2,4},{4,6},{6,7},{7,5},{5,3},{3,1},{1,0},{8,9},{10,8},{12,1... | collective-permute-start | bytes 786440 | tf_op jit(solution)/shard_map/ppermute | solution.py:41
  19.7 7.9 %collective-permute-start.6 = (bf16[512,256]{1,0:T(8,128)(2,1)}, bf16[512,256]{1,0:T(8,128)(2,1)}, u32[]{:S(2)}, u32[]{:S(2)}) collective-permute-start(bf16[512,256]{1,0:T(8,128)(2,1)} %collective-permute-done.3), channel_id=1, source_target_pairs={{0,2},{2,4},{4,6},{6,7},{7,5},{5,3},{3,1},{1,0},{8,9},{10,8},{12,1... | collective-permute-start | bytes 786440 | tf_op jit(solution)/shard_map/ppermute | solution.py:41
  21.3 0.7 copy-start.4
  22.0 0.9 %copy-start.3 = (f32[512,128]{1,0:T(8,128)S(1)}, f32[512,128]{1,0:T(8,128)}, u32[]{:S(2)}) copy-start(f32[512,128]{1,0:T(8,128)} %copy-done.2) | copy-start | bytes 786436
  23.0 0.9 %copy-start.5 = (bf16[512,256]{1,0:T(8,128)(2,1)S(1)}, bf16[512,256]{1,0:T(8,128)(2,1)}, u32[]{:S(2)}) copy-start(bf16[512,256]{1,0:T(8,128)(2,1)} %copy-done.4) | copy-start | bytes 786436
  26.9 0.7 copy-start
  27.6 1.7 %collective-permute-start.8 = (bf16[512,256]{1,0:T(8,128)(2,1)}, bf16[512,256]{1,0:T(8,128)(2,1)S(1)}, u32[]{:S(2)}, u32[]{:S(2)}) collective-permute-start(bf16[512,256]{1,0:T(8,128)(2,1)} %collective-permute-done.6), channel_id=1, source_target_pairs={{0,8},{8,0},{16,24},{24,16},{1,9},{9,1},{17,25},{25,17},{2,10},{10... | collective-permute-start | bytes 786440 | tf_op jit(solution)/shard_map/ppermute | solution.py:45
  27.6 6.6 %collective-permute-start.9 = (bf16[512,256]{1,0:T(8,128)(2,1)}, bf16[512,256]{1,0:T(8,128)(2,1)S(1)}, u32[]{:S(2)}, u32[]{:S(2)}) collective-permute-start(bf16[512,256]{1,0:T(8,128)(2,1)} %collective-permute-done.5.refs_0_), channel_id=1, source_target_pairs={{0,2},{2,4},{4,6},{6,7},{7,5},{5,3},{3,1},{1,0},{8,9},{10,8},{12,1... | collective-permute-start | bytes 786440 | tf_op jit(solution)/shard_map/ppermute | solution.py:41
  34.3 1.0 %copy-start.1 = (f32[512,128]{1,0:T(8,128)S(1)}, f32[512,128]{1,0:T(8,128)}, u32[]{:S(2)}) copy-start(f32[512,128]{1,0:T(8,128)} %copy-done) | copy-start | bytes 786436
  39.1 2.0 %collective-permute-start.10 = (bf16[512,512]{1,0:T(8,128)(2,1)S(1)}, bf16[512,512]{1,0:T(8,128)(2,1)S(1)}, u32[]{:S(2)}, u32[]{:S(2)}) collective-permute-start(bf16[512,512]{1,0:T(8,128)(2,1)S(1)} %get-tuple-element.42.refs_3_), channel_id=1, source_target_pairs={{0,8},{8,0},{16,24},{24,16},{1,9},{9,1},{17,25},{25,17},{2,10},{10... | collective-permute-start | bytes 1572872 | tf_op jit(solution)/shard_map/ppermute | solution.py:45
  39.2 14.3 %collective-permute-start.11 = (bf16[512,512]{1,0:T(8,128)(2,1)S(1)}, bf16[512,512]{1,0:T(8,128)(2,1)S(1)}, u32[]{:S(2)}, u32[]{:S(2)}) collective-permute-start(bf16[512,512]{1,0:T(8,128)(2,1)S(1)} %get-tuple-element.42.refs_3_), channel_id=1, source_target_pairs={{0,16},{8,24},{16,0},{24,8},{1,17},{9,25},{17,1},{25,9},{2,18},{10... | collective-permute-start | bytes 1572872 | tf_op jit(solution)/shard_map/ppermute | solution.py:322
  53.5 2.3 %collective-permute-start.12 = (bf16[512,512]{1,0:T(8,128)(2,1)S(1)}, bf16[512,512]{1,0:T(8,128)(2,1)S(1)}, u32[]{:S(2)}, u32[]{:S(2)}) collective-permute-start(bf16[512,512]{1,0:T(8,128)(2,1)S(1)} %collective-permute-done.11.refs_3_), channel_id=1, source_target_pairs={{0,8},{8,0},{16,24},{24,16},{1,9},{9,1},{17,25},{25,17},{2,10},{10... | collective-permute-start | bytes 1572872 | tf_op jit(solution)/shard_map/ppermute | solution.py:45
  59.1 8.3 %collective-permute-start.13 = (bf16[512,256]{1,0:T(8,128)(2,1)S(1)}, bf16[512,256]{1,0:T(8,128)(2,1)S(1)}, u32[]{:S(2)}, u32[]{:S(2)}) collective-permute-start(bf16[512,256]{1,0:T(8,128)(2,1)S(1)} %get-tuple-element.49), channel_id=1, source_target_pairs={{0,2},{2,4},{4,6},{6,7},{7,5},{5,3},{3,1},{1,0},{8,9},{10,8},{12,1... | collective-permute-start | bytes 786440 | tf_op jit(solution)/shard_map/ppermute | solution.py:41
  60.6 8.6 %collective-permute-start.18 = (bf16[512,256]{1,0:T(8,128)(2,1)S(1)}, bf16[512,256]{1,0:T(8,128)(2,1)S(1)}, u32[]{:S(2)}, u32[]{:S(2)}) collective-permute-start(bf16[512,256]{1,0:T(8,128)(2,1)S(1)} %get-tuple-element.51), channel_id=1, source_target_pairs={{0,8},{8,0},{16,24},{24,16},{1,9},{9,1},{17,25},{25,17},{2,10},{10... | collective-permute-start | bytes 786440 | tf_op jit(solution)/shard_map/ppermute | solution.py:45
  60.6 8.6 %collective-permute-start.19 = (bf16[512,256]{1,0:T(8,128)(2,1)S(1)}, bf16[512,256]{1,0:T(8,128)(2,1)S(1)}, u32[]{:S(2)}, u32[]{:S(2)}) collective-permute-start(bf16[512,256]{1,0:T(8,128)(2,1)S(1)} %get-tuple-element.52), channel_id=1, source_target_pairs={{0,9},{2,8},{4,10},{6,12},{7,14},{5,15},{3,13},{1,11},{8,2},{10,4}... | collective-permute-start | bytes 786440 | tf_op jit(solution)/shard_map/ppermute | solution.py:41
  67.4 6.4 %collective-permute-start.14 = (bf16[512,256]{1,0:T(8,128)(2,1)S(1)}, bf16[512,256]{1,0:T(8,128)(2,1)S(1)}, u32[]{:S(2)}, u32[]{:S(2)}) collective-permute-start(bf16[512,256]{1,0:T(8,128)(2,1)S(1)} %add_convert_fusion.5), channel_id=1, source_target_pairs={{0,2},{2,4},{4,6},{6,7},{7,5},{5,3},{3,1},{1,0},{8,9},{10,8},{12,1... | collective-permute-start | bytes 786440 | tf_op jit(solution)/shard_map/ppermute | solution.py:41
  69.2 6.5 %collective-permute-start.17 = (bf16[512,256]{1,0:T(8,128)(2,1)S(1)}, bf16[512,256]{1,0:T(8,128)(2,1)S(1)}, u32[]{:S(2)}, u32[]{:S(2)}) collective-permute-start(bf16[512,256]{1,0:T(8,128)(2,1)S(1)} %get-tuple-element.50), channel_id=1, source_target_pairs={{0,8},{8,0},{16,24},{24,16},{1,9},{9,1},{17,25},{25,17},{2,10},{10... | collective-permute-start | bytes 786440 | tf_op jit(solution)/shard_map/ppermute | solution.py:45
  69.3 7.4 %collective-permute-start.20 = (bf16[512,256]{1,0:T(8,128)(2,1)S(1)}, bf16[512,256]{1,0:T(8,128)(2,1)S(1)}, u32[]{:S(2)}, u32[]{:S(2)}) collective-permute-start(bf16[512,256]{1,0:T(8,128)(2,1)S(1)} %add_convert_fusion.2), channel_id=1, source_target_pairs={{0,2},{2,4},{4,6},{6,7},{7,5},{5,3},{3,1},{1,0},{8,9},{10,8},{12,1... | collective-permute-start | bytes 786440 | tf_op jit(solution)/shard_map/ppermute | solution.py:41
  73.9 6.4 %collective-permute-start.15 = (bf16[512,256]{1,0:T(8,128)(2,1)S(1)}, bf16[512,256]{1,0:T(8,128)(2,1)S(1)}, u32[]{:S(2)}, u32[]{:S(2)}) collective-permute-start(bf16[512,256]{1,0:T(8,128)(2,1)S(1)} %add_convert_fusion.4), channel_id=1, source_target_pairs={{0,2},{2,4},{4,6},{6,7},{7,5},{5,3},{3,1},{1,0},{8,9},{10,8},{12,1... | collective-permute-start | bytes 786440 | tf_op jit(solution)/shard_map/ppermute | solution.py:41
  76.7 5.9 %collective-permute-start.21 = (bf16[512,256]{1,0:T(8,128)(2,1)S(1)}, bf16[512,256]{1,0:T(8,128)(2,1)S(1)}, u32[]{:S(2)}, u32[]{:S(2)}) collective-permute-start(bf16[512,256]{1,0:T(8,128)(2,1)S(1)} %add_convert_fusion.1), channel_id=1, source_target_pairs={{0,10},{2,12},{4,14},{6,15},{7,13},{5,11},{3,9},{1,8},{8,1},{10,0}... | collective-permute-start | bytes 786440 | tf_op jit(solution)/shard_map/ppermute | solution.py:41
  80.4 6.4 %collective-permute-start.16 = (bf16[512,256]{1,0:T(8,128)(2,1)S(1)}, bf16[512,256]{1,0:T(8,128)(2,1)S(1)}, u32[]{:S(2)}, u32[]{:S(2)}) collective-permute-start(bf16[512,256]{1,0:T(8,128)(2,1)S(1)} %add_convert_fusion.3), channel_id=1, source_target_pairs={{0,2},{2,4},{4,6},{6,7},{7,5},{5,3},{3,1},{1,0},{8,9},{10,8},{12,1... | collective-permute-start | bytes 786440 | tf_op jit(solution)/shard_map/ppermute | solution.py:41

commit v6 on v5

v6 whole, which is shorter than its diff:
```python
import functools
import math

import jax
import jax.numpy as jnp
from jax import lax
from jax.experimental import pallas as pl
from jax.experimental.pallas import tpu as pltpu
from jax.sharding import PartitionSpec as P

LOG2E = math.log2(math.e)
VMEM = pl.BlockSpec(memory_space=pltpu.VMEM)
SMEM = pl.BlockSpec(memory_space=pltpu.SMEM)
F32 = jnp.float32
BF16 = jnp.bfloat16


def ring_order(count):
    line = count // 2
    return [2 * z for z in range(line)] + [2 * z + 1 for z in reversed(range(line))]


def ring_place(index, count):
    return jnp.where(index % 2 == 0, index // 2, count - 1 - index // 2)


def ring_index(place, count):
    return jnp.where(place < count // 2, 2 * place, 2 * (count - 1 - place) + 1)


def along(value, step, count):
    order = ring_order(count)
    return lax.ppermute(
        value, "head", [(order[p], order[(p + step) % count]) for p in range(count)]
    )


def swapped(value, seq_count):
    return lax.ppermute(value, "seq", [(seq, seq + 1 - 2 * (seq % 2)) for seq in range(seq_count)])


def in_hbm(value):
    return pltpu.with_memory_space_constraint(value, pltpu.HBM)


def in_vmem(value):
    return pltpu.with_memory_space_constraint(value, pltpu.VMEM)


def fold_kernel(gain_ref, w_hbm, out_ref, sems):
    lanes = gain_ref.shape[1]
    chunks = sems.shape[0]
    size = w_hbm.shape[1] // chunks

    def fetch(n):
        here = (slice(None), pl.ds(n * size, size), slice(None))
        return pltpu.make_async_copy(w_hbm.at[here], out_ref.at[here], sems.at[n])

    for n in range(chunks):
        fetch(n).start()
    columns = jnp.transpose(gain_ref[...])
    for n in range(chunks):
        fetch(n).wait()
        for first in range(n * size, (n + 1) * size, lanes):
            column = columns[:, first // lanes : first // lanes + 1]
            for group in range(w_hbm.shape[0]):
                here = (group, slice(first, first + lanes), slice(None))
                out_ref[here] = (out_ref[here].astype(F32) * column).astype(BF16)


def fold_gain(gain, weights):
    groups, depth, width = weights.shape
    lanes = math.gcd(depth, 128)
    return pl.pallas_call(
        fold_kernel,
        out_shape=pltpu.VMEM(weights.shape, BF16),
        in_specs=[VMEM, pl.BlockSpec(memory_space=pltpu.HBM)],
        out_specs=VMEM,
        scratch_shapes=[pltpu.SemaphoreType.DMA((math.gcd(depth // lanes, 8),))],
        compiler_params=pltpu.CompilerParams(vmem_limit_bytes=16 << 20),
        cost_estimate=pl.CostEstimate(
            flops=weights.size, bytes_accessed=4 * weights.size, transcendentals=0
        ),
        name="fold_gain",
    )(in_hbm(gain.reshape(depth // lanes, lanes)), in_hbm(weights))


def project_kernel(head_size, base, at, factor, tokens_hbm, w_ref, *refs):
    blocks, (q_ref, kv_ref, wide, sem) = refs[:-4], refs[-4:]
    rows, width = blocks[0].shape
    out_width = w_ref.shape[2]

    def lanes_of(n):
        return pl.ds(pl.multiple_of(at[n] * width, width), width)

    own = pltpu.make_async_copy(
        tokens_hbm.at[pl.ds(base, rows), :], wide.at[:, lanes_of(0)], sem
    )
    own.start()
    for n, block in enumerate(blocks):
        wide[:, lanes_of(n + 1)] = block[...]
    own.wait()
    depth = wide.shape[1]
    q = jnp.dot(wide[...], w_ref[0], preferred_element_type=F32)
    k = jnp.dot(wide[...], w_ref[1], preferred_element_type=F32)
    v = jnp.dot(wide[...], w_ref[2], preferred_element_type=F32)
    power = None
    for lane in range(0, depth, 128):
        values = wide[:, lane : lane + 128].astype(F32)
        power = values * values if power is None else power + values * values
    scale = lax.rsqrt(jnp.sum(power, axis=-1, keepdims=True) * (1.0 / depth) + 1e-06)
    q, k, v = q * scale, k * scale, v * scale
    for head in range(out_width // head_size):
        lanes = slice(head * head_size, (head + 1) * head_size)
        qh, kh = q[:, lanes], k[:, lanes]
        q_size = lax.rsqrt(jnp.sum(qh * qh, axis=-1, keepdims=True) + 1e-06)
        k_size = lax.rsqrt(jnp.sum(kh * kh, axis=-1, keepdims=True) + 1e-06)
        q_ref[:, lanes] = (qh * (q_size * (factor[head] * LOG2E))).astype(BF16)
        kv_ref[:, lanes] = (kh * k_size).astype(BF16)
    kv_ref[:, out_width:] = v.astype(BF16)


def project(at, factor, tokens, weights, blocks, base, head_size):
    rows, width = blocks[0].shape
    groups, depth, out_width = weights.shape
    return pl.pallas_call(
        functools.partial(project_kernel, head_size, base),
        out_shape=(pltpu.VMEM((rows, out_width), BF16), pltpu.VMEM((rows, 2 * out_width), BF16)),
        in_specs=[SMEM, SMEM, pl.BlockSpec(memory_space=pltpu.HBM)] + [VMEM] * (1 + len(blocks)),
        out_specs=(VMEM, VMEM),
        scratch_shapes=[pltpu.VMEM((rows, depth), BF16), pltpu.SemaphoreType.DMA(())],
        compiler_params=pltpu.CompilerParams(vmem_limit_bytes=16 << 20),
        cost_estimate=pl.CostEstimate(
            flops=2 * rows * depth * groups * out_width,
            bytes_accessed=2 * depth * (rows + groups * out_width),
            transcendentals=0,
        ),
        name="project",
    )(at, in_hbm(factor), in_hbm(tokens), in_vmem(weights), *map(in_vmem, blocks))


def attend_blocks(sources, ids, q_first, q_refs, id_col, id_row, kv_refs, v_ones, acc, head_size):
    heads = q_refs[0].shape[1] // head_size
    keys = kv_refs[0].shape[0]
    rows = q_refs[0].shape[0]
    for number, kv_ref in enumerate(kv_refs):
        for head in range(heads):
            start = (heads + head) * head_size
            v_ones[head, :, :head_size] = kv_ref[:, start : start + head_size]
            v_ones[head, :, head_size:] = jnp.ones((keys, head_size), BF16)
        first = sources[number]
        key_low, key_high = ids[first], ids[first + keys - 1]
        tile = math.gcd(rows, 256)
        for chunk, q_ref in enumerate(q_refs):

            @pl.loop(0, rows // tile)
            def _(index):
                here = pl.ds(pl.multiple_of(index * tile, tile), tile)
                base = chunk * rows + index * tile
                there = pl.ds(pl.multiple_of(base, tile), tile)
                q_low = ids[q_first + base]
                q_high = ids[q_first + base + tile - 1]

                def add(masked):
                    if masked:
                        allowed = id_row[first // keys] <= id_col[there, :]
                    for head in range(heads):
                        lanes = slice(head * head_size, (head + 1) * head_size)
                        score = lax.dot_general(
                            q_ref[here, lanes],
                            kv_ref[:, lanes],
                            (((1,), (1,)), ((), ())),
                            preferred_element_type=F32,
                        )
                        weight = jnp.exp2(score)
                        if masked:
                            weight = jnp.where(allowed, weight, 0.0)
                        wide = slice(2 * head * head_size, 2 * (head + 1) * head_size)
                        acc[there, wide] += jnp.dot(
                            weight.astype(BF16), v_ones[head], preferred_element_type=F32
                        )

                @pl.when(key_high <= q_low)
                def _():
                    add(False)

                @pl.when((key_high > q_low) & (key_low <= q_high))
                def _():
                    add(True)


def attend_kernel(count_q, count_kv, head_size, has_acc, count_out, info, ids, *refs):
    q_refs, rest = refs[:count_q], refs[count_q:]
    (id_col, id_row), rest = rest[:2], rest[2:]
    kv_refs, rest = rest[:count_kv], rest[count_kv:]
    rows, width = q_refs[0].shape
    if has_acc:
        acc_in, rest = rest[0], rest[1:]
    if count_out:
        w_ref, outs, (v_ones, acc, attended) = rest[0], rest[1:-3], rest[-3:]
    else:
        acc_out, v_ones, acc = rest
    acc[...] = acc_in[...] if has_acc else jnp.zeros_like(acc)
    sources = [info[number] for number in range(count_kv)]
    attend_blocks(
        sources, ids, info[count_kv], q_refs, id_col, id_row, kv_refs, v_ones, acc, head_size
    )
    if not count_out:
        acc_out[...] = acc[...]
        return
    for head in range(width // head_size):
        start = 2 * head * head_size
        attended[:, head * head_size : (head + 1) * head_size] = (
            acc[:, start : start + head_size]
            / acc[:, start + head_size : start + 2 * head_size]
        ).astype(BF16)
    out_width = outs[0].shape[1]
    for number, out in enumerate(outs):
        lane = info[count_kv + 1 + number] * out_width
        stream = number * count_q // count_out
        out[...] = jnp.dot(
            attended[stream * rows : (stream + 1) * rows, :],
            w_ref[:, pl.ds(pl.multiple_of(lane, out_width), out_width)],
            preferred_element_type=F32,
        ).astype(BF16)


def attend(info, ids, queries, id_col, id_row, kvs, head_size, acc=None, w_out=None, count_out=0):
    rows, width = queries[0].shape
    total = rows * len(queries)
    keys = kvs[0].shape[0]
    heads = width // head_size
    scratch = [
        pltpu.VMEM((heads, keys, 2 * head_size), BF16),
        pltpu.VMEM((total, 2 * width), F32),
    ]
    operands = [*map(in_vmem, queries), id_col, in_hbm(id_row), *map(in_vmem, kvs)]
    if acc is not None:
        operands.append(in_vmem(acc))
    if count_out:
        operands.append(in_hbm(w_out))
        scratch.append(pltpu.VMEM((total, width), BF16))
        shape = pltpu.VMEM((rows, w_out.shape[1] * len(queries) // count_out), BF16)
    else:
        shape = pltpu.VMEM((total, 2 * width), F32)
    outs = count_out or 1
    return pl.pallas_call(
        functools.partial(
            attend_kernel, len(queries), len(kvs), head_size, acc is not None, count_out
        ),
        out_shape=(shape,) * outs,
        in_specs=[SMEM, SMEM] + [VMEM] * len(operands),
        out_specs=(VMEM,) * outs,
        scratch_shapes=scratch,
        compiler_params=pltpu.CompilerParams(
            vmem_limit_bytes=(16 << 20) + 2 * kvs[0].size * 2 * len(kvs)
        ),
        cost_estimate=pl.CostEstimate(
            flops=6 * total * keys * len(kvs) * width + 2 * rows * width * width * count_out,
            bytes_accessed=4 * keys * len(kvs) * width + 8 * total * width,
            transcendentals=total * keys * len(kvs) * heads,
        ),
        name="attend_last" if count_out else "attend",
    )(info, in_hbm(ids), *operands)


def total_of(*parts):
    return sum(part.astype(F32) for part in parts).astype(BF16)


def body(mesh_shape, tokens, norm_gain, w_qkv, head_scale, w_out, scale_ids):
    ring, seqs = mesh_shape["head"], mesh_shape["seq"]
    outer = seqs // 2
    rows, width = tokens.shape
    half = rows // 2
    head_size = w_qkv.shape[2] // head_scale.shape[0]
    head_at, seq_at = lax.axis_index("head"), lax.axis_index("seq")
    place = ring_place(head_at, ring)
    chip, core = seq_at // 2, seq_at % 2
    index_at = lambda offset: ring_index((place + offset + ring) % ring, ring)
    numbers = lambda values: jnp.stack(values).astype(jnp.int32)
    id_row = scale_ids.reshape(-1, 1, half)
    id_col = lax.dynamic_slice_in_dim(scale_ids, seq_at * rows, rows)[:, None]

    streams, ways = (0, 1), ((0, 1), (1, -1))
    farthest = ring // 2
    reach = [(farthest, farthest - 1), (farthest - 1, farthest)]

    held = [[tokens[s * half : (s + 1) * half]] * 2 for s in streams]
    blocks, offsets = [[] for s in streams], [[0] for s in streams]
    for step in range(1, farthest + 1):
        for s in streams:
            for way, sign in ways:
                if step <= reach[s][way]:
                    held[s][way] = along(held[s][way], sign, ring)
        if step == 1:
            held[1][1], weights = lax.optimization_barrier(
                (held[1][1], fold_gain(norm_gain, w_qkv))
            )
        for s in streams:
            for way, sign in ways:
                if step <= reach[s][way]:
                    blocks[s].append(held[s][way])
                    offsets[s].append(-sign * step)
    queries, kvs = [], []
    for s in streams:
        at = numbers([index_at(offset) for offset in offsets[s]])
        query, kv = project(at, head_scale, tokens, weights, blocks[s], s * half, head_size)
        queries.append(query)
        kvs.append(kv)

    far, straight, crossed = [], [], []
    for step in range(outer):
        source = 2 * ((chip + outer - step) % outer)
        for s in streams:
            straight.append((source + core) * rows + s * half)
            crossed.append((source + 1 - core) * rows + s * half)
            if step:
                far.append(lax.ppermute(kvs[s], "seq", [
                    (2 * a + b, 2 * ((a + step) % outer) + b) for a in range(outer) for b in (0, 1)
                ]))
    first = [seq_at * rows]
    info = numbers(straight[:2] + crossed[:2] + first)
    keys = kvs + [swapped(kv, seqs) for kv in kvs]
    (acc,) = attend(info, scale_ids, queries, id_col, id_row, keys, head_size)
    acc, far = lax.optimization_barrier((acc, far))
    far_crossed = [swapped(block, seqs) for block in far]
    info = numbers(straight[2:] + first)
    (acc,) = attend(info, scale_ids, queries, id_col, id_row, far, head_size, acc)

    goals = [[*range(up, 0, -1), *range(-down, 0), 0] for up, down in reach]
    info = numbers(crossed[2:] + first + [index_at(goal) for goal in goals[0] + goals[1]])
    parts = attend(
        info, scale_ids, queries, id_col, id_row, far_crossed, head_size, acc, w_out, 2 * ring
    )
    parts = [dict(zip(goals[s], parts[s * ring : (s + 1) * ring])) for s in streams]
    sums = [[None, None] for s in streams]
    for step in range(farthest, 0, -1):
        for s in streams:
            for way, sign in ways:
                if step <= reach[s][way]:
                    part = parts[s][sign * step]
                    if sums[s][way] is not None:
                        part = total_of(part, sums[s][way])
                    sums[s][way] = along(part, sign, ring)
    return jnp.concatenate([total_of(parts[s][0], *sums[s]) for s in streams])


def solution(mesh):
    placed = (P("seq", "head"), P(), P(None, None, "head"), P("head"), P("head", None), P())
    return jax.shard_map(
        functools.partial(body, dict(mesh.shape)),
        mesh=mesh,
        in_specs=placed,
        out_specs=P("seq", "head"),
        check_vma=False,
    )
```

time: 88.7 us -> 87.4 us (0.985)
  waiting for transfers between devices: 40.7 us -> 23.4 us
  starting transfers between devices: 19 us -> 32 us
  Pallas kernels: 19.1 us -> 21.8 us
  local copies, waits for them, and re-layouts: 7.24 us -> 8.2 us
    ppermute x15 -> x30, waiting for transfers between devices: 40.3 us -> 23.4 us  [the longest x28 18 us: along(): lax.ppermute(value, 'head', [(order[p], order[(p + step) % count]) for p...]
    ppermute x15 -> x30, starting transfers between devices: 18.9 us -> 31.1 us  [the longest x28 29 us: along(): lax.ppermute(value, 'head', [(order[p], order[(p + step) % count]) for p...]
    pallas_call x3, Pallas kernels: 8.69 us -> 11.3 us  [attend(): pl.pallas_call(functools.partial(attend_kernel, len(queries), len(kvs), h...]
    reshape x1 -> x0, local copies, waits for them, and re-layouts: 1.29 us -> none  [body(): gain = norm_gain.reshape(ring, width)]
    unnamed x12 -> x22, local copies, waits for them, and re-layouts: 4.96 us -> 5.97 us
    slice x0 -> x1, local copies, waits for them, and re-layouts: none -> 0.98 us  [body(): held = [[tokens[s * half:(s + 1) * half]] * 2 for s in streams]]
    ppermute x7 -> x4, starting transfers between devices: 0.09 us -> 0.98 us  [swapped(): lax.ppermute(value, 'seq', [(seq, seq + 1 - 2 * (seq % 2)) for seq in ran...]
  transfers between devices with their start and end apart: 22 -> 34, of which waited for: 13 -> 13; matrix products, arithmetic and copies ran while one was open for 3% -> 2% of each run, Pallas kernels for 14% -> 21%
where the time goes in v6:
time: 87.4 us; the launch traced here: 87 us
  starting transfers between devices  32 us (37%)
  waiting for transfers between devices  23.4 us (27%)
  Pallas kernels  21.8 us (25%)
  local copies, waits for them, and re-layouts  8.2 us (9%)
  other arithmetic  1.25 us (1%)
    ppermute x28, starting transfers between devices, along(): lax.ppermute(value, 'head', [(order[p], order[(p + step) % count]) for p...  29 us
    ppermute x28, waiting for transfers between devices, along(): lax.ppermute(value, 'head', [(order[p], order[(p + step) % count]) for p...  18 us
    pallas_call x3, Pallas kernels, attend(): pl.pallas_call(functools.partial(attend_kernel, len(queries), len(kvs), h...  11.3 us
    pallas_call x2, Pallas kernels, project(): pl.pallas_call(functools.partial(project_kernel, head_size, base), out_sh...  7.64 us
    unnamed x22, local copies, waits for them, and re-layouts  5.97 us
    ppermute x2, waiting for transfers between devices, body(): lax.ppermute(kvs[s], 'seq', [(2 * a + b, 2 * ((a + step) % outer) + b) fo...  5.42 us
    pallas_call x1, Pallas kernels, fold_gain(): pl.pallas_call(fold_kernel, out_shape=pltpu.VMEM(weights.shape, BF16), in...  2.83 us
    ppermute x2, starting transfers between devices, body(): lax.ppermute(kvs[s], 'seq', [(2 * a + b, 2 * ((a + step) % outer) + b) fo...  2.03 us
  transfers between devices with their start and end apart: 34, of which 13 were waited for; matrix products, arithmetic and copies ran while one was open for 2% of the time, Pallas kernels for 21%

profile of v6, /device:TPU:10, one launch (start us, length us, event | category | flops | bytes accessed | tf_op | source)
XLA Modules:
  0.0 87.0 jit_solution(6880885860021088274)
XLA Ops:
  0.0 1.0 %fusion = (bf16[256,256]{1,0:T(8,128)(2,1)S(1)}, bf16[256,256]{1,0:T(8,128)(2,1)S(1)}) fusion(bf16[512,256]{1,0:T(8,128)(2,1)} %tokens_hbm.3), kind=kLoop, calls=%fused_computation.14 | loop fusion | bytes 524288 | tf_op jit(solution)/shard_map/slice | solution.py:289
  1.0 1.6 %collective-permute-start.1 = (bf16[256,256]{1,0:T(8,128)(2,1)S(1)}, bf16[256,256]{1,0:T(8,128)(2,1)S(1)}, u32[]{:S(2)}, u32[]{:S(2)}) collective-permute-start(bf16[256,256]{1,0:T(8,128)(2,1)S(1)} %get-tuple-element.55), channel_id=1, source_target_pairs={{0,2},{2,4},{4,6},{6,7},{7,5},{5,3},{3,1},{1,0},{8,10},{10,12},{12... | collective-permute-start | bytes 393224 | tf_op jit(solution)/shard_map/ppermute | solution.py:33
  3.5 2.8 %collective-permute-done.1.refs_0_ = bf16[256,256]{1,0:T(8,128)(2,1)S(1)} collective-permute-done((bf16[256,256]{1,0:T(8,128)(2,1)S(1)}, bf16[256,256]{1,0:T(8,128)(2,1)S(1)}, u32[]{:S(2)}, u32[]{:S(2)}) %collective-permute-start.1) | collective-permute-done | bytes 131104 | tf_op jit(solution)/shard_map/ppermute | solution.py:33
  6.3 1.6 %collective-permute-start.3 = (bf16[256,256]{1,0:T(8,128)(2,1)S(1)}, bf16[256,256]{1,0:T(8,128)(2,1)S(1)}, u32[]{:S(2)}, u32[]{:S(2)}) collective-permute-start(bf16[256,256]{1,0:T(8,128)(2,1)S(1)} %collective-permute-done.1.refs_0_), channel_id=1, source_target_pairs={{0,2},{2,4},{4,6},{6,7},{7,5},{5,3},{3,1},{1,0},{8,10},{10,12},{12... | collective-permute-start | bytes 393224 | tf_op jit(solution)/shard_map/ppermute | solution.py:33
  7.9 1.6 %collective-permute-start.8 = (bf16[256,256]{1,0:T(8,128)(2,1)S(1)}, bf16[256,256]{1,0:T(8,128)(2,1)S(1)}, u32[]{:S(2)}, u32[]{:S(2)}) collective-permute-start(bf16[256,256]{1,0:T(8,128)(2,1)S(1)} %get-tuple-element.56), channel_id=1, source_target_pairs={{0,2},{2,4},{4,6},{6,7},{7,5},{5,3},{3,1},{1,0},{8,10},{10,12},{12... | collective-permute-start | bytes 393224 | tf_op jit(solution)/shard_map/ppermute | solution.py:33
  9.4 2.8 %fold_gain.1.w_ref = bf16[3,2048,256]{2,1,0:T(8,128)(2,1)S(1)} custom-call(f32[16,128]{1,0:T(8,128)} %bitcast.24, bf16[3,2048,256]{2,1,0:T(8,128)(2,1)} %w_hbm.1), custom_call_target="tpu_custom_call" | custom-call | flops 1572864 | bytes 6291456 | tf_op jit(solution)/shard_map/fold_gain/pallas_call | solution.py:74
  12.3 0.5 collective-permute-start.10
  13.2 0.7 copy-done.2
  13.9 1.6 %collective-permute-start.5 = (bf16[256,256]{1,0:T(8,128)(2,1)S(1)}, bf16[256,256]{1,0:T(8,128)(2,1)}, u32[]{:S(2)}, u32[]{:S(2)}) collective-permute-start(bf16[256,256]{1,0:T(8,128)(2,1)S(1)} %collective-permute-done.3.refs_2_), channel_id=1, source_target_pairs={{0,2},{2,4},{4,6},{6,7},{7,5},{5,3},{3,1},{1,0},{8,10},{10,12},{12... | collective-permute-start | bytes 393224 | tf_op jit(solution)/shard_map/ppermute | solution.py:33
  15.5 0.7 copy-done.4
  16.1 1.6 %collective-permute-start.9 = (bf16[256,256]{1,0:T(8,128)(2,1)S(1)}, bf16[256,256]{1,0:T(8,128)(2,1)}, u32[]{:S(2)}, u32[]{:S(2)}) collective-permute-start(bf16[256,256]{1,0:T(8,128)(2,1)S(1)} %collective-permute-done.8.refs_0_), channel_id=1, source_target_pairs={{0,2},{2,4},{4,6},{6,7},{7,5},{5,3},{3,1},{1,0},{8,10},{10,12},{12... | collective-permute-start | bytes 393224 | tf_op jit(solution)/shard_map/ppermute | solution.py:33
  18.2 0.6 copy-done
  18.8 1.5 %collective-permute-done.4.refs_3_ = bf16[256,256]{1,0:T(8,128)(2,1)} collective-permute-done((bf16[256,256]{1,0:T(8,128)(2,1)S(1)}, bf16[256,256]{1,0:T(8,128)(2,1)}, u32[]{:S(2)}, u32[]{:S(2)}) %collective-permute-start.4) | collective-permute-done | bytes 131104 | tf_op jit(solution)/shard_map/ppermute | solution.py:33
  20.8 1.6 %collective-permute-start.7 = (bf16[256,256]{1,0:T(8,128)(2,1)}, bf16[256,256]{1,0:T(8,128)(2,1)}, u32[]{:S(2)}, u32[]{:S(2)}) collective-permute-start(bf16[256,256]{1,0:T(8,128)(2,1)} %collective-permute-done.5.refs_4_), channel_id=1, source_target_pairs={{0,2},{2,4},{4,6},{6,7},{7,5},{5,3},{3,1},{1,0},{8,10},{10,12},{12... | collective-permute-start | bytes 393224 | tf_op jit(solution)/shard_map/ppermute | solution.py:33
  22.6 1.6 %collective-permute-start.11 = (bf16[256,256]{1,0:T(8,128)(2,1)}, bf16[256,256]{1,0:T(8,128)(2,1)}, u32[]{:S(2)}, u32[]{:S(2)}) collective-permute-start(bf16[256,256]{1,0:T(8,128)(2,1)} %collective-permute-done.9.refs_2_), channel_id=1, source_target_pairs={{0,2},{2,4},{4,6},{6,7},{7,5},{5,3},{3,1},{1,0},{8,10},{10,12},{12... | collective-permute-start | bytes 393224 | tf_op jit(solution)/shard_map/ppermute | solution.py:33
  24.8 1.5 %collective-permute-done.6.refs_5_ = bf16[256,256]{1,0:T(8,128)(2,1)} collective-permute-done((bf16[256,256]{1,0:T(8,128)(2,1)}, bf16[256,256]{1,0:T(8,128)(2,1)}, u32[]{:S(2)}, u32[]{:S(2)}) %collective-permute-start.6) | collective-permute-done | bytes 131104 | tf_op jit(solution)/shard_map/ppermute | solution.py:33
  26.3 0.9 %copy-done.3 = bf16[256,256]{1,0:T(8,128)(2,1)S(1)} copy-done((bf16[256,256]{1,0:T(8,128)(2,1)S(1)}, bf16[256,256]{1,0:T(8,128)(2,1)}, u32[]{:S(2)}) %copy-start.3) | copy-done | bytes 131096
  27.2 0.9 %copy-done.5 = bf16[256,256]{1,0:T(8,128)(2,1)S(1)} copy-done((bf16[256,256]{1,0:T(8,128)(2,1)S(1)}, bf16[256,256]{1,0:T(8,128)(2,1)}, u32[]{:S(2)}) %copy-start.5) | copy-done | bytes 131096
  28.1 3.8 %project.2 = (bf16[256,256]{1,0:T(8,128)(2,1)S(1)}, bf16[256,512]{1,0:T(8,128)(2,1)}) custom-call(s32[8]{0:T(128)S(1)} %stack.107.at, f32[2]{0:T(128)} %factor.3, bf16[512,256]{1,0:T(8,128)(2,1)} %tokens_hbm.3, bf16[3,2048,256]{2,1,0:T(8,128)(2,1)S(1)} %fold_gain.1.w_ref, bf16[256,256]{1,0:T(8,128)(2,1)S(1)} %collective-permute-done.1.refs_0_, ...), custom_call_target="tpu_custom_call" | custom-call | flops 805306368 | bytes 4194304 | tf_op jit(solution)/shard_map/project/pallas_call | solution.py:126
  31.9 0.6 copy-done.6
  32.6 3.8 %project.3 = (bf16[256,256]{1,0:T(8,128)(2,1)S(1)}, bf16[256,512]{1,0:T(8,128)(2,1)}) custom-call(s32[8]{0:T(128)S(1)} %stack.108.at, f32[2]{0:T(128)} %factor.3, bf16[512,256]{1,0:T(8,128)(2,1)} %tokens_hbm.3, bf16[3,2048,256]{2,1,0:T(8,128)(2,1)S(1)} %fold_gain.1.w_ref, bf16[256,256]{1,0:T(8,128)(2,1)S(1)} %collective-permute-done.8.refs_0_, ...), custom_call_target="tpu_custom_call" | custom-call | flops 805306368 | bytes 4194304 | tf_op jit(solution)/shard_map/project/pallas_call | solution.py:126
  36.5 0.6 copy-done.8
  37.6 0.5 collective-permute-start.16
  38.1 1.5 %collective-permute-start.17 = (bf16[256,512]{1,0:T(8,128)(2,1)}, bf16[256,512]{1,0:T(8,128)(2,1)S(1)}, u32[]{:S(2)}, u32[]{:S(2)}) collective-permute-start(bf16[256,512]{1,0:T(8,128)(2,1)} %get-tuple-element.35.refs_5_), channel_id=1, source_target_pairs={{0,16},{8,24},{16,0},{24,8},{1,17},{9,25},{17,1},{25,9},{2,18},{10... | collective-permute-start | bytes 786440 | tf_op jit(solution)/shard_map/ppermute | solution.py:319
  39.6 0.8 dynamic_slice.3
  40.6 0.9 %copy-done.9 = bf16[256,256]{1,0:T(8,128)(2,1)S(1)} copy-done((bf16[256,256]{1,0:T(8,128)(2,1)S(1)}, bf16[256,256]{1,0:T(8,128)(2,1)}, u32[]{:S(2)}) %copy-start.9) | copy-done | bytes 131096
  41.5 4.7 %attend.2.refs_6_ = f32[512,512]{1,0:T(8,128)S(1)} custom-call(s32[5]{0:T(128)S(1)} %stack.113.info, s32[2048]{0:T(1024)} %ids.5, bf16[256,256]{1,0:T(8,128)(2,1)S(1)} %copy-done.7, bf16[256,256]{1,0:T(8,128)(2,1)S(1)} %copy-done.9, s32[512,1]{1,0:T(8,128)S(1)} %copy.9.refs_2_, s32[8,1,256]{2,1,0:T(1,128)} %bitcast.21, ...), custom_call_target="tpu_custom_call" | custom-call | flops 805306368 | bytes 2097152 | tf_op jit(solution)/shard_map/attend/pallas_call | solution.py:247
  46.2 0.7 collective-permute-done.16.refs_4_
  46.9 4.7 %collective-permute-done.17.refs_5_ = bf16[256,512]{1,0:T(8,128)(2,1)S(1)} collective-permute-done((bf16[256,512]{1,0:T(8,128)(2,1)}, bf16[256,512]{1,0:T(8,128)(2,1)S(1)}, u32[]{:S(2)}, u32[]{:S(2)}) %collective-permute-start.17) | collective-permute-done | bytes 262176 | tf_op jit(solution)/shard_map/ppermute | solution.py:319
  51.7 0.5 collective-permute-start.19
  52.3 2.8 %attend.3.refs_6_ = f32[512,512]{1,0:T(8,128)S(1)} custom-call(s32[3]{0:T(128)S(1)} %pad_add_fusion.info, s32[2048]{0:T(1024)} %ids.5, bf16[256,256]{1,0:T(8,128)(2,1)S(1)} %copy-done.7, bf16[256,256]{1,0:T(8,128)(2,1)S(1)} %copy-done.10, s32[512,1]{1,0:T(8,128)S(1)} %copy.9.refs_2_, s32[8,1,256]{2,1,0:T(1,128)} %bitcast.22, ...), custom_call_target="tpu_custom_call" | custom-call | flops 402653184 | bytes 1572864 | tf_op jit(solution)/shard_map/attend/pallas_call | solution.py:247
  55.2 3.8 %attend_last.1 = (bf16[256,256]{1,0:T(8,128)(2,1)S(1)}, bf16[256,256]{1,0:T(8,128)(2,1)S(1)}, bf16[256,256]{1,0:T(8,128)(2,1)S(1)}, bf16[256,256]{1,0:T(8,128)(2...) custom-call(s32[19]{0:T(128)S(1)} %stack.106.info, ...), custom_call_target="tpu_custom_call" | custom-call | flops 939524096 | bytes 1572864 | tf_op jit(solution)/shard_map/attend_last/pallas_call | solution.py:247
  59.5 1.6 %collective-permute-start.27 = (bf16[256,256]{1,0:T(8,128)(2,1)S(1)}, bf16[256,256]{1,0:T(8,128)(2,1)S(1)}, u32[]{:S(2)}, u32[]{:S(2)}) collective-permute-start(bf16[256,256]{1,0:T(8,128)(2,1)S(1)} %get-tuple-element.50), channel_id=1, source_target_pairs={{0,2},{2,4},{4,6},{6,7},{7,5},{5,3},{3,1},{1,0},{8,10},{10,12},{12... | collective-permute-start | bytes 393224 | tf_op jit(solution)/shard_map/ppermute | solution.py:33
  61.5 1.6 %collective-permute-start.20 = (bf16[256,256]{1,0:T(8,128)(2,1)S(1)}, bf16[256,256]{1,0:T(8,128)(2,1)S(1)}, u32[]{:S(2)}, u32[]{:S(2)}) collective-permute-start(bf16[256,256]{1,0:T(8,128)(2,1)S(1)} %get-tuple-element.43), channel_id=1, source_target_pairs={{0,2},{2,4},{4,6},{6,7},{7,5},{5,3},{3,1},{1,0},{8,10},{10,12},{12... | collective-permute-start | bytes 393224 | tf_op jit(solution)/shard_map/ppermute | solution.py:33
  63.1 2.3 %collective-permute-done.30 = bf16[256,256]{1,0:T(8,128)(2,1)S(1)} collective-permute-done((bf16[256,256]{1,0:T(8,128)(2,1)S(1)}, bf16[256,256]{1,0:T(8,128)(2,1)S(1)}, u32[]{:S(2)}, u32[]{:S(2)}) %collective-permute-start.30) | collective-permute-done | bytes 131104 | tf_op jit(solution)/shard_map/ppermute | solution.py:33
  66.0 1.6 %collective-permute-start.28 = (bf16[256,256]{1,0:T(8,128)(2,1)S(1)}, bf16[256,256]{1,0:T(8,128)(2,1)S(1)}, u32[]{:S(2)}, u32[]{:S(2)}) collective-permute-start(bf16[256,256]{1,0:T(8,128)(2,1)S(1)} %add_convert_fusion.5), channel_id=1, source_target_pairs={{0,2},{2,4},{4,6},{6,7},{7,5},{5,3},{3,1},{1,0},{8,10},{10,12},{12... | collective-permute-start | bytes 393224 | tf_op jit(solution)/shard_map/ppermute | solution.py:33
  67.6 0.6 collective-permute-done.24
  68.3 0.5 collective-permute-start.25
  68.8 1.6 %collective-permute-start.21 = (bf16[256,256]{1,0:T(8,128)(2,1)S(1)}, bf16[256,256]{1,0:T(8,128)(2,1)S(1)}, u32[]{:S(2)}, u32[]{:S(2)}) collective-permute-start(bf16[256,256]{1,0:T(8,128)(2,1)S(1)} %add_convert_fusion.11), channel_id=1, source_target_pairs={{0,2},{2,4},{4,6},{6,7},{7,5},{5,3},{3,1},{1,0},{8,10},{10,12},{12... | collective-permute-start | bytes 393224 | tf_op jit(solution)/shard_map/ppermute | solution.py:33
  70.4 1.4 %collective-permute-done.31 = bf16[256,256]{1,0:T(8,128)(2,1)S(1)} collective-permute-done((bf16[256,256]{1,0:T(8,128)(2,1)S(1)}, bf16[256,256]{1,0:T(8,128)(2,1)S(1)}, u32[]{:S(2)}, u32[]{:S(2)}) %collective-permute-start.31) | collective-permute-done | bytes 131104 | tf_op jit(solution)/shard_map/ppermute | solution.py:33
  72.4 1.6 %collective-permute-start.29 = (bf16[256,256]{1,0:T(8,128)(2,1)S(1)}, bf16[256,256]{1,0:T(8,128)(2,1)S(1)}, u32[]{:S(2)}, u32[]{:S(2)}) collective-permute-start(bf16[256,256]{1,0:T(8,128)(2,1)S(1)} %add_convert_fusion.4), channel_id=1, source_target_pairs={{0,2},{2,4},{4,6},{6,7},{7,5},{5,3},{3,1},{1,0},{8,10},{10,12},{12... | collective-permute-start | bytes 393224 | tf_op jit(solution)/shard_map/ppermute | solution.py:33
  74.1 0.6 collective-permute-done.25
  75.3 1.6 %collective-permute-start.22 = (bf16[256,256]{1,0:T(8,128)(2,1)S(1)}, bf16[256,256]{1,0:T(8,128)(2,1)S(1)}, u32[]{:S(2)}, u32[]{:S(2)}) collective-permute-start(bf16[256,256]{1,0:T(8,128)(2,1)S(1)} %add_convert_fusion.10), channel_id=1, source_target_pairs={{0,2},{2,4},{4,6},{6,7},{7,5},{5,3},{3,1},{1,0},{8,10},{10,12},{12... | collective-permute-start | bytes 393224 | tf_op jit(solution)/shard_map/ppermute | solution.py:33
  76.9 0.6 collective-permute-done.32
  78.0 3.1 %collective-permute-done.22 = bf16[256,256]{1,0:T(8,128)(2,1)S(1)} collective-permute-done((bf16[256,256]{1,0:T(8,128)(2,1)S(1)}, bf16[256,256]{1,0:T(8,128)(2,1)S(1)}, u32[]{:S(2)}, u32[]{:S(2)}) %collective-permute-start.22) | collective-permute-done | bytes 131104 | tf_op jit(solution)/shard_map/ppermute | solution.py:33
  81.2 1.6 %collective-permute-start.23 = (bf16[256,256]{1,0:T(8,128)(2,1)S(1)}, bf16[256,256]{1,0:T(8,128)(2,1)S(1)}, u32[]{:S(2)}, u32[]{:S(2)}) collective-permute-start(bf16[256,256]{1,0:T(8,128)(2,1)S(1)} %add_convert_fusion.9), channel_id=1, source_target_pairs={{0,2},{2,4},{4,6},{6,7},{7,5},{5,3},{3,1},{1,0},{8,10},{10,12},{12... | collective-permute-start | bytes 393224 | tf_op jit(solution)/shard_map/ppermute | solution.py:33
  82.9 3.3 %collective-permute-done.23 = bf16[256,256]{1,0:T(8,128)(2,1)S(1)} collective-permute-done((bf16[256,256]{1,0:T(8,128)(2,1)S(1)}, bf16[256,256]{1,0:T(8,128)(2,1)S(1)}, u32[]{:S(2)}, u32[]{:S(2)}) %collective-permute-start.23) | collective-permute-done | bytes 131104 | tf_op jit(solution)/shard_map/ppermute | solution.py:33
  86.2 0.7 pad_maximum_fusion
  (69 shorter events, 7.4 us)
Async XLA Ops:
  1.0 5.3 %collective-permute-start.1 = (bf16[256,256]{1,0:T(8,128)(2,1)S(1)}, bf16[256,256]{1,0:T(8,128)(2,1)S(1)}, u32[]{:S(2)}, u32[]{:S(2)}) collective-permute-start(bf16[256,256]{1,0:T(8,128)(2,1)S(1)} %get-tuple-element.55), channel_id=1, source_target_pairs={{0,2},{2,4},{4,6},{6,7},{7,5},{5,3},{3,1},{1,0},{8,10},{10,12},{12... | collective-permute-start | bytes 393224 | tf_op jit(solution)/shard_map/ppermute | solution.py:33
  2.6 9.7 %collective-permute-start = (bf16[256,256]{1,0:T(8,128)(2,1)S(1)}, bf16[256,256]{1,0:T(8,128)(2,1)S(1)}, u32[]{:S(2)}, u32[]{:S(2)}) collective-permute-start(bf16[256,256]{1,0:T(8,128)(2,1)S(1)} %get-tuple-element.56), channel_id=1, source_target_pairs={{0,1},{2,0},{4,2},{6,4},{7,6},{5,7},{3,5},{1,3},{8,9},{10,8},{12,1... | collective-permute-start | bytes 393224 | tf_op jit(solution)/shard_map/ppermute | solution.py:33
  3.1 9.7 %collective-permute-start.2 = (bf16[256,256]{1,0:T(8,128)(2,1)S(1)}, bf16[256,256]{1,0:T(8,128)(2,1)S(1)}, u32[]{:S(2)}, u32[]{:S(2)}) collective-permute-start(bf16[256,256]{1,0:T(8,128)(2,1)S(1)} %get-tuple-element.55), channel_id=1, source_target_pairs={{0,1},{2,0},{4,2},{6,4},{7,6},{5,7},{3,5},{1,3},{8,9},{10,8},{12,1... | collective-permute-start | bytes 393224 | tf_op jit(solution)/shard_map/ppermute | solution.py:33
  6.3 7.6 %collective-permute-start.3 = (bf16[256,256]{1,0:T(8,128)(2,1)S(1)}, bf16[256,256]{1,0:T(8,128)(2,1)S(1)}, u32[]{:S(2)}, u32[]{:S(2)}) collective-permute-start(bf16[256,256]{1,0:T(8,128)(2,1)S(1)} %collective-permute-done.1.refs_0_), channel_id=1, source_target_pairs={{0,2},{2,4},{4,6},{6,7},{7,5},{5,3},{3,1},{1,0},{8,10},{10,12},{12... | collective-permute-start | bytes 393224 | tf_op jit(solution)/shard_map/ppermute | solution.py:33
  7.9 8.3 %collective-permute-start.8 = (bf16[256,256]{1,0:T(8,128)(2,1)S(1)}, bf16[256,256]{1,0:T(8,128)(2,1)S(1)}, u32[]{:S(2)}, u32[]{:S(2)}) collective-permute-start(bf16[256,256]{1,0:T(8,128)(2,1)S(1)} %get-tuple-element.56), channel_id=1, source_target_pairs={{0,2},{2,4},{4,6},{6,7},{7,5},{5,3},{3,1},{1,0},{8,10},{10,12},{12... | collective-permute-start | bytes 393224 | tf_op jit(solution)/shard_map/ppermute | solution.py:33
  12.3 5.4 %collective-permute-start.10 = (bf16[256,256]{1,0:T(8,128)(2,1)S(1)}, bf16[256,256]{1,0:T(8,128)(2,1)S(1)}, u32[]{:S(2)}, u32[]{:S(2)}) collective-permute-start(bf16[256,256]{1,0:T(8,128)(2,1)S(1)} %collective-permute-done.refs_1_), channel_id=1, source_target_pairs={{0,1},{2,0},{4,2},{6,4},{7,6},{5,7},{3,5},{1,3},{8,9},{10,8},{12,1... | collective-permute-start | bytes 393224 | tf_op jit(solution)/shard_map/ppermute | solution.py:33
  12.8 7.6 %collective-permute-start.4 = (bf16[256,256]{1,0:T(8,128)(2,1)S(1)}, bf16[256,256]{1,0:T(8,128)(2,1)}, u32[]{:S(2)}, u32[]{:S(2)}) collective-permute-start(bf16[256,256]{1,0:T(8,128)(2,1)S(1)} %collective-permute-done.2.refs_1_), channel_id=1, source_target_pairs={{0,1},{2,0},{4,2},{6,4},{7,6},{5,7},{3,5},{1,3},{8,9},{10,8},{12,1... | collective-permute-start | bytes 393224 | tf_op jit(solution)/shard_map/ppermute | solution.py:33
  13.2 0.7 copy-start.2
  13.9 6.9 %collective-permute-start.5 = (bf16[256,256]{1,0:T(8,128)(2,1)S(1)}, bf16[256,256]{1,0:T(8,128)(2,1)}, u32[]{:S(2)}, u32[]{:S(2)}) collective-permute-start(bf16[256,256]{1,0:T(8,128)(2,1)S(1)} %collective-permute-done.3.refs_2_), channel_id=1, source_target_pairs={{0,2},{2,4},{4,6},{6,7},{7,5},{5,3},{3,1},{1,0},{8,10},{10,12},{12... | collective-permute-start | bytes 393224 | tf_op jit(solution)/shard_map/ppermute | solution.py:33
  15.5 0.7 copy-start.4
  16.1 6.5 %collective-permute-start.9 = (bf16[256,256]{1,0:T(8,128)(2,1)S(1)}, bf16[256,256]{1,0:T(8,128)(2,1)}, u32[]{:S(2)}, u32[]{:S(2)}) collective-permute-start(bf16[256,256]{1,0:T(8,128)(2,1)S(1)} %collective-permute-done.8.refs_0_), channel_id=1, source_target_pairs={{0,2},{2,4},{4,6},{6,7},{7,5},{5,3},{3,1},{1,0},{8,10},{10,12},{12... | collective-permute-start | bytes 393224 | tf_op jit(solution)/shard_map/ppermute | solution.py:33
  17.7 6.5 %collective-permute-start.12 = (bf16[256,256]{1,0:T(8,128)(2,1)S(1)}, bf16[256,256]{1,0:T(8,128)(2,1)}, u32[]{:S(2)}, u32[]{:S(2)}) collective-permute-start(bf16[256,256]{1,0:T(8,128)(2,1)S(1)} %collective-permute-done.10.refs_3_), channel_id=1, source_target_pairs={{0,1},{2,0},{4,2},{6,4},{7,6},{5,7},{3,5},{1,3},{8,9},{10,8},{12,1... | collective-permute-start | bytes 393224 | tf_op jit(solution)/shard_map/ppermute | solution.py:33
  18.2 0.7 copy-start
  20.3 5.9 %collective-permute-start.6 = (bf16[256,256]{1,0:T(8,128)(2,1)}, bf16[256,256]{1,0:T(8,128)(2,1)}, u32[]{:S(2)}, u32[]{:S(2)}) collective-permute-start(bf16[256,256]{1,0:T(8,128)(2,1)} %collective-permute-done.4.refs_3_), channel_id=1, source_target_pairs={{0,1},{2,0},{4,2},{6,4},{7,6},{5,7},{3,5},{1,3},{8,9},{10,8},{12,1... | collective-permute-start | bytes 393224 | tf_op jit(solution)/shard_map/ppermute | solution.py:33
  20.8 5.5 %collective-permute-start.7 = (bf16[256,256]{1,0:T(8,128)(2,1)}, bf16[256,256]{1,0:T(8,128)(2,1)}, u32[]{:S(2)}, u32[]{:S(2)}) collective-permute-start(bf16[256,256]{1,0:T(8,128)(2,1)} %collective-permute-done.5.refs_4_), channel_id=1, source_target_pairs={{0,2},{2,4},{4,6},{6,7},{7,5},{5,3},{3,1},{1,0},{8,10},{10,12},{12... | collective-permute-start | bytes 393224 | tf_op jit(solution)/shard_map/ppermute | solution.py:33
  22.6 10.0 %collective-permute-start.11 = (bf16[256,256]{1,0:T(8,128)(2,1)}, bf16[256,256]{1,0:T(8,128)(2,1)}, u32[]{:S(2)}, u32[]{:S(2)}) collective-permute-start(bf16[256,256]{1,0:T(8,128)(2,1)} %collective-permute-done.9.refs_2_), channel_id=1, source_target_pairs={{0,2},{2,4},{4,6},{6,7},{7,5},{5,3},{3,1},{1,0},{8,10},{10,12},{12... | collective-permute-start | bytes 393224 | tf_op jit(solution)/shard_map/ppermute | solution.py:33
  24.2 8.4 %collective-permute-start.13 = (bf16[256,256]{1,0:T(8,128)(2,1)}, bf16[256,256]{1,0:T(8,128)(2,1)}, u32[]{:S(2)}, u32[]{:S(2)}) collective-permute-start(bf16[256,256]{1,0:T(8,128)(2,1)} %collective-permute-done.12.refs_5_), channel_id=1, source_target_pairs={{0,1},{2,0},{4,2},{6,4},{7,6},{5,7},{3,5},{1,3},{8,9},{10,8},{12,1... | collective-permute-start | bytes 393224 | tf_op jit(solution)/shard_map/ppermute | solution.py:33
  24.8 7.8 %copy-start.1 = (bf16[256,256]{1,0:T(8,128)(2,1)S(1)}, bf16[256,256]{1,0:T(8,128)(2,1)}, u32[]{:S(2)}) copy-start(bf16[256,256]{1,0:T(8,128)(2,1)} %copy-done) | copy-start | bytes 393220
  26.3 0.9 %copy-start.3 = (bf16[256,256]{1,0:T(8,128)(2,1)S(1)}, bf16[256,256]{1,0:T(8,128)(2,1)}, u32[]{:S(2)}) copy-start(bf16[256,256]{1,0:T(8,128)(2,1)} %copy-done.2) | copy-start | bytes 393220
  27.2 0.9 %copy-start.5 = (bf16[256,256]{1,0:T(8,128)(2,1)S(1)}, bf16[256,256]{1,0:T(8,128)(2,1)}, u32[]{:S(2)}) copy-start(bf16[256,256]{1,0:T(8,128)(2,1)} %copy-done.4) | copy-start | bytes 393220
  31.9 0.6 copy-start.6
  32.6 8.1 %copy-start.7 = (bf16[256,256]{1,0:T(8,128)(2,1)S(1)}, bf16[256,256]{1,0:T(8,128)(2,1)}, u32[]{:S(2)}) copy-start(bf16[256,256]{1,0:T(8,128)(2,1)} %copy-done.6) | copy-start | bytes 393220
  32.6 8.1 %collective-permute-start.14 = (bf16[256,512]{1,0:T(8,128)(2,1)}, bf16[256,512]{1,0:T(8,128)(2,1)}, u32[]{:S(2)}, u32[]{:S(2)}) collective-permute-start(bf16[256,512]{1,0:T(8,128)(2,1)} %get-tuple-element.34.refs_4_), channel_id=1, source_target_pairs={{0,8},{8,0},{16,24},{24,16},{1,9},{9,1},{17,25},{25,17},{2,10},{10... | collective-permute-start | bytes 786440 | tf_op jit(solution)/shard_map/ppermute | solution.py:39
  36.4 0.7 copy-start.8
  37.1 15.2 %copy-start.10 = (bf16[256,256]{1,0:T(8,128)(2,1)S(1)}, bf16[256,256]{1,0:T(8,128)(2,1)}, u32[]{:S(2)}) copy-start(bf16[256,256]{1,0:T(8,128)(2,1)} %copy-done.8) | copy-start | bytes 393220
  37.1 3.5 %collective-permute-start.15 = (bf16[256,512]{1,0:T(8,128)(2,1)}, bf16[256,512]{1,0:T(8,128)(2,1)S(1)}, u32[]{:S(2)}, u32[]{:S(2)}) collective-permute-start(bf16[256,512]{1,0:T(8,128)(2,1)} %get-tuple-element.35.refs_5_), channel_id=1, source_target_pairs={{0,8},{8,0},{16,24},{24,16},{1,9},{9,1},{17,25},{25,17},{2,10},{10... | collective-permute-start | bytes 786440 | tf_op jit(solution)/shard_map/ppermute | solution.py:39
  37.6 9.4 %collective-permute-start.16 = (bf16[256,512]{1,0:T(8,128)(2,1)}, bf16[256,512]{1,0:T(8,128)(2,1)S(1)}, u32[]{:S(2)}, u32[]{:S(2)}) collective-permute-start(bf16[256,512]{1,0:T(8,128)(2,1)} %get-tuple-element.34.refs_4_), channel_id=1, source_target_pairs={{0,16},{8,24},{16,0},{24,8},{1,17},{9,25},{17,1},{25,9},{2,18},{10... | collective-permute-start | bytes 786440 | tf_op jit(solution)/shard_map/ppermute | solution.py:319
  38.1 13.6 %collective-permute-start.17 = (bf16[256,512]{1,0:T(8,128)(2,1)}, bf16[256,512]{1,0:T(8,128)(2,1)S(1)}, u32[]{:S(2)}, u32[]{:S(2)}) collective-permute-start(bf16[256,512]{1,0:T(8,128)(2,1)} %get-tuple-element.35.refs_5_), channel_id=1, source_target_pairs={{0,16},{8,24},{16,0},{24,8},{1,17},{9,25},{17,1},{25,9},{2,18},{10... | collective-permute-start | bytes 786440 | tf_op jit(solution)/shard_map/ppermute | solution.py:319
  40.6 0.9 %copy-start.9 = (bf16[256,256]{1,0:T(8,128)(2,1)S(1)}, bf16[256,256]{1,0:T(8,128)(2,1)}, u32[]{:S(2)}) copy-start(bf16[256,256]{1,0:T(8,128)(2,1)} %copy-done.8) | copy-start | bytes 393220
  51.7 3.5 %collective-permute-start.18 = (bf16[256,512]{1,0:T(8,128)(2,1)S(1)}, bf16[256,512]{1,0:T(8,128)(2,1)S(1)}, u32[]{:S(2)}, u32[]{:S(2)}) collective-permute-start(bf16[256,512]{1,0:T(8,128)(2,1)S(1)} %collective-permute-done.16.refs_4_), channel_id=1, source_target_pairs={{0,8},{8,0},{16,24},{24,16},{1,9},{9,1},{17,25},{25,17},{2,10},{10... | collective-permute-start | bytes 786440 | tf_op jit(solution)/shard_map/ppermute | solution.py:39
  51.7 3.5 %collective-permute-start.19 = (bf16[256,512]{1,0:T(8,128)(2,1)S(1)}, bf16[256,512]{1,0:T(8,128)(2,1)S(1)}, u32[]{:S(2)}, u32[]{:S(2)}) collective-permute-start(bf16[256,512]{1,0:T(8,128)(2,1)S(1)} %collective-permute-done.17.refs_5_), channel_id=1, source_target_pairs={{0,8},{8,0},{16,24},{24,16},{1,9},{9,1},{17,25},{25,17},{2,10},{10... | collective-permute-start | bytes 786440 | tf_op jit(solution)/shard_map/ppermute | solution.py:39
  59.0 6.4 %collective-permute-start.30 = (bf16[256,256]{1,0:T(8,128)(2,1)S(1)}, bf16[256,256]{1,0:T(8,128)(2,1)S(1)}, u32[]{:S(2)}, u32[]{:S(2)}) collective-permute-start(bf16[256,256]{1,0:T(8,128)(2,1)S(1)} %get-tuple-element.54), channel_id=1, source_target_pairs={{0,1},{2,0},{4,2},{6,4},{7,6},{5,7},{3,5},{1,3},{8,9},{10,8},{12,1... | collective-permute-start | bytes 393224 | tf_op jit(solution)/shard_map/ppermute | solution.py:33
  59.5 6.5 %collective-permute-start.27 = (bf16[256,256]{1,0:T(8,128)(2,1)S(1)}, bf16[256,256]{1,0:T(8,128)(2,1)S(1)}, u32[]{:S(2)}, u32[]{:S(2)}) collective-permute-start(bf16[256,256]{1,0:T(8,128)(2,1)S(1)} %get-tuple-element.50), channel_id=1, source_target_pairs={{0,2},{2,4},{4,6},{6,7},{7,5},{5,3},{3,1},{1,0},{8,10},{10,12},{12... | collective-permute-start | bytes 393224 | tf_op jit(solution)/shard_map/ppermute | solution.py:33
  61.1 7.1 %collective-permute-start.24 = (bf16[256,256]{1,0:T(8,128)(2,1)S(1)}, bf16[256,256]{1,0:T(8,128)(2,1)S(1)}, u32[]{:S(2)}, u32[]{:S(2)}) collective-permute-start(bf16[256,256]{1,0:T(8,128)(2,1)S(1)} %get-tuple-element.46), channel_id=1, source_target_pairs={{0,1},{2,0},{4,2},{6,4},{7,6},{5,7},{3,5},{1,3},{8,9},{10,8},{12,1... | collective-permute-start | bytes 393224 | tf_op jit(solution)/shard_map/ppermute | solution.py:33
  61.5 7.2 %collective-permute-start.20 = (bf16[256,256]{1,0:T(8,128)(2,1)S(1)}, bf16[256,256]{1,0:T(8,128)(2,1)S(1)}, u32[]{:S(2)}, u32[]{:S(2)}) collective-permute-start(bf16[256,256]{1,0:T(8,128)(2,1)S(1)} %get-tuple-element.43), channel_id=1, source_target_pairs={{0,2},{2,4},{4,6},{6,7},{7,5},{5,3},{3,1},{1,0},{8,10},{10,12},{12... | collective-permute-start | bytes 393224 | tf_op jit(solution)/shard_map/ppermute | solution.py:33
  65.5 6.4 %collective-permute-start.31 = (bf16[256,256]{1,0:T(8,128)(2,1)S(1)}, bf16[256,256]{1,0:T(8,128)(2,1)S(1)}, u32[]{:S(2)}, u32[]{:S(2)}) collective-permute-start(bf16[256,256]{1,0:T(8,128)(2,1)S(1)} %add_convert_fusion.3), channel_id=1, source_target_pairs={{0,1},{2,0},{4,2},{6,4},{7,6},{5,7},{3,5},{1,3},{8,9},{10,8},{12,1... | collective-permute-start | bytes 393224 | tf_op jit(solution)/shard_map/ppermute | solution.py:33
  66.0 6.4 %collective-permute-start.28 = (bf16[256,256]{1,0:T(8,128)(2,1)S(1)}, bf16[256,256]{1,0:T(8,128)(2,1)S(1)}, u32[]{:S(2)}, u32[]{:S(2)}) collective-permute-start(bf16[256,256]{1,0:T(8,128)(2,1)S(1)} %add_convert_fusion.5), channel_id=1, source_target_pairs={{0,2},{2,4},{4,6},{6,7},{7,5},{5,3},{3,1},{1,0},{8,10},{10,12},{12... | collective-permute-start | bytes 393224 | tf_op jit(solution)/shard_map/ppermute | solution.py:33
  68.3 6.4 %collective-permute-start.25 = (bf16[256,256]{1,0:T(8,128)(2,1)S(1)}, bf16[256,256]{1,0:T(8,128)(2,1)S(1)}, u32[]{:S(2)}, u32[]{:S(2)}) collective-permute-start(bf16[256,256]{1,0:T(8,128)(2,1)S(1)} %add_convert_fusion.8), channel_id=1, source_target_pairs={{0,1},{2,0},{4,2},{6,4},{7,6},{5,7},{3,5},{1,3},{8,9},{10,8},{12,1... | collective-permute-start | bytes 393224 | tf_op jit(solution)/shard_map/ppermute | solution.py:33
  68.8 6.4 %collective-permute-start.21 = (bf16[256,256]{1,0:T(8,128)(2,1)S(1)}, bf16[256,256]{1,0:T(8,128)(2,1)S(1)}, u32[]{:S(2)}, u32[]{:S(2)}) collective-permute-start(bf16[256,256]{1,0:T(8,128)(2,1)S(1)} %add_convert_fusion.11), channel_id=1, source_target_pairs={{0,2},{2,4},{4,6},{6,7},{7,5},{5,3},{3,1},{1,0},{8,10},{10,12},{12... | collective-permute-start | bytes 393224 | tf_op jit(solution)/shard_map/ppermute | solution.py:33
  71.9 5.6 %collective-permute-start.32 = (bf16[256,256]{1,0:T(8,128)(2,1)S(1)}, bf16[256,256]{1,0:T(8,128)(2,1)S(1)}, u32[]{:S(2)}, u32[]{:S(2)}) collective-permute-start(bf16[256,256]{1,0:T(8,128)(2,1)S(1)} %add_convert_fusion.2), channel_id=1, source_target_pairs={{0,1},{2,0},{4,2},{6,4},{7,6},{5,7},{3,5},{1,3},{8,9},{10,8},{12,1... | collective-permute-start | bytes 393224 | tf_op jit(solution)/shard_map/ppermute | solution.py:33
  72.4 10.4 %collective-permute-start.29 = (bf16[256,256]{1,0:T(8,128)(2,1)S(1)}, bf16[256,256]{1,0:T(8,128)(2,1)S(1)}, u32[]{:S(2)}, u32[]{:S(2)}) collective-permute-start(bf16[256,256]{1,0:T(8,128)(2,1)S(1)} %add_convert_fusion.4), channel_id=1, source_target_pairs={{0,2},{2,4},{4,6},{6,7},{7,5},{5,3},{3,1},{1,0},{8,10},{10,12},{12... | collective-permute-start | bytes 393224 | tf_op jit(solution)/shard_map/ppermute | solution.py:33
  74.7 8.1 %collective-permute-start.26 = (bf16[256,256]{1,0:T(8,128)(2,1)S(1)}, bf16[256,256]{1,0:T(8,128)(2,1)S(1)}, u32[]{:S(2)}, u32[]{:S(2)}) collective-permute-start(bf16[256,256]{1,0:T(8,128)(2,1)S(1)} %add_convert_fusion.7), channel_id=1, source_target_pairs={{0,1},{2,0},{4,2},{6,4},{7,6},{5,7},{3,5},{1,3},{8,9},{10,8},{12,1... | collective-permute-start | bytes 393224 | tf_op jit(solution)/shard_map/ppermute | solution.py:33
  75.3 5.9 %collective-permute-start.22 = (bf16[256,256]{1,0:T(8,128)(2,1)S(1)}, bf16[256,256]{1,0:T(8,128)(2,1)S(1)}, u32[]{:S(2)}, u32[]{:S(2)}) collective-permute-start(bf16[256,256]{1,0:T(8,128)(2,1)S(1)} %add_convert_fusion.10), channel_id=1, source_target_pairs={{0,2},{2,4},{4,6},{6,7},{7,5},{5,3},{3,1},{1,0},{8,10},{10,12},{12... | collective-permute-start | bytes 393224 | tf_op jit(solution)/shard_map/ppermute | solution.py:33
  77.5 5.3 %collective-permute-start.33 = (bf16[256,256]{1,0:T(8,128)(2,1)S(1)}, bf16[256,256]{1,0:T(8,128)(2,1)S(1)}, u32[]{:S(2)}, u32[]{:S(2)}) collective-permute-start(bf16[256,256]{1,0:T(8,128)(2,1)S(1)} %add_convert_fusion.1), channel_id=1, source_target_pairs={{0,1},{2,0},{4,2},{6,4},{7,6},{5,7},{3,5},{1,3},{8,9},{10,8},{12,1... | collective-permute-start | bytes 393224 | tf_op jit(solution)/shard_map/ppermute | solution.py:33
  81.2 5.0 %collective-permute-start.23 = (bf16[256,256]{1,0:T(8,128)(2,1)S(1)}, bf16[256,256]{1,0:T(8,128)(2,1)S(1)}, u32[]{:S(2)}, u32[]{:S(2)}) collective-permute-start(bf16[256,256]{1,0:T(8,128)(2,1)S(1)} %add_convert_fusion.9), channel_id=1, source_target_pairs={{0,2},{2,4},{4,6},{6,7},{7,5},{5,3},{3,1},{1,0},{8,10},{10,12},{12... | collective-permute-start | bytes 393224 | tf_op jit(solution)/shard_map/ppermute | solution.py:33

commit v7 on v6

--- a/solution.py
+++ b/solution.py
@@ -47,88 +47,113 @@
     return pltpu.with_memory_space_constraint(value, pltpu.VMEM)
 
 
-def fold_kernel(gain_ref, w_hbm, out_ref, sems):
+def fold_kernel(order, at, gain_ref, w_hbm, out_ref, sems):
     lanes = gain_ref.shape[1]
-    chunks = sems.shape[0]
-    size = w_hbm.shape[1] // chunks
+    size = w_hbm.shape[1] // len(order)
+    per = size // lanes
 
     def fetch(n):
-        here = (slice(None), pl.ds(n * size, size), slice(None))
-        return pltpu.make_async_copy(w_hbm.at[here], out_ref.at[here], sems.at[n])
-
-    for n in range(chunks):
+        start = pl.multiple_of(at[order[n]] * size, size)
+        return pltpu.make_async_copy(
+            w_hbm.at[:, pl.ds(start, size), :], out_ref.at[:, n * size : (n + 1) * size, :], sems.at[n]
+        )
+
+    for n in range(len(order)):
         fetch(n).start()
-    columns = jnp.transpose(gain_ref[...])
-    for n in range(chunks):
+    for n in range(len(order)):
+        columns = jnp.transpose(gain_ref[pl.ds(at[order[n]] * per, per), :])
         fetch(n).wait()
-        for first in range(n * size, (n + 1) * size, lanes):
-            column = columns[:, first // lanes : first // lanes + 1]
+        for piece in range(per):
+            first = n * size + piece * lanes
             for group in range(w_hbm.shape[0]):
                 here = (group, slice(first, first + lanes), slice(None))
-                out_ref[here] = (out_ref[here].astype(F32) * column).astype(BF16)
-
-
-def fold_gain(gain, weights):
-    groups, depth, width = weights.shape
-    lanes = math.gcd(depth, 128)
+                scaled = out_ref[here].astype(F32) * columns[:, piece : piece + 1]
+                out_ref[here] = scaled.astype(BF16)
+
+
+def fold_gain(order, at, gain, weights):
+    depth = weights.shape[1]
+    lanes = math.gcd(depth // len(order), 128)
     return pl.pallas_call(
-        fold_kernel,
+        functools.partial(fold_kernel, order),
         out_shape=pltpu.VMEM(weights.shape, BF16),
-        in_specs=[VMEM, pl.BlockSpec(memory_space=pltpu.HBM)],
+        in_specs=[SMEM, VMEM, pl.BlockSpec(memory_space=pltpu.HBM)],
         out_specs=VMEM,
-        scratch_shapes=[pltpu.SemaphoreType.DMA((math.gcd(depth // lanes, 8),))],
+        scratch_shapes=[pltpu.SemaphoreType.DMA((len(order),))],
         compiler_params=pltpu.CompilerParams(vmem_limit_bytes=16 << 20),
         cost_estimate=pl.CostEstimate(
             flops=weights.size, bytes_accessed=4 * weights.size, transcendentals=0
         ),
         name="fold_gain",
-    )(in_hbm(gain.reshape(depth // lanes, lanes)), in_hbm(weights))
-
-
-def project_kernel(head_size, base, at, factor, tokens_hbm, w_ref, *refs):
-    blocks, (q_ref, kv_ref, wide, sem) = refs[:-4], refs[-4:]
-    rows, width = blocks[0].shape
-    out_width = w_ref.shape[2]
-
-    def lanes_of(n):
-        return pl.ds(pl.multiple_of(at[n] * width, width), width)
-
-    own = pltpu.make_async_copy(
-        tokens_hbm.at[pl.ds(base, rows), :], wide.at[:, lanes_of(0)], sem
-    )
-    own.start()
-    for n, block in enumerate(blocks):
-        wide[:, lanes_of(n + 1)] = block[...]
-    own.wait()
-    depth = wide.shape[1]
-    q = jnp.dot(wide[...], w_ref[0], preferred_element_type=F32)
-    k = jnp.dot(wide[...], w_ref[1], preferred_element_type=F32)
-    v = jnp.dot(wide[...], w_ref[2], preferred_element_type=F32)
-    power = None
-    for lane in range(0, depth, 128):
-        values = wide[:, lane : lane + 128].astype(F32)
-        power = values * values if power is None else power + values * values
-    scale = lax.rsqrt(jnp.sum(power, axis=-1, keepdims=True) * (1.0 / depth) + 1e-06)
-    q, k, v = q * scale, k * scale, v * scale
-    for head in range(out_width // head_size):
-        lanes = slice(head * head_size, (head + 1) * head_size)
-        qh, kh = q[:, lanes], k[:, lanes]
-        q_size = lax.rsqrt(jnp.sum(qh * qh, axis=-1, keepdims=True) + 1e-06)
-        k_size = lax.rsqrt(jnp.sum(kh * kh, axis=-1, keepdims=True) + 1e-06)
-        q_ref[:, lanes] = (qh * (q_size * (factor[head] * LOG2E))).astype(BF16)
-        kv_ref[:, lanes] = (kh * k_size).astype(BF16)
-    kv_ref[:, out_width:] = v.astype(BF16)
-
-
-def project(at, factor, tokens, weights, blocks, base, head_size):
-    rows, width = blocks[0].shape
+    )(at, in_hbm(gain.reshape(depth // lanes, lanes)), in_hbm(weights))
+
+
+def place_kernel(targets, *refs):
+    blocks, wide, sems = refs[: len(targets)], refs[-2], refs[-1]
+    copies = []
+    for n, (block, (row, lane)) in enumerate(zip(blocks, targets)):
+        rows, width = block.shape
+        here = wide.at[row : row + rows, lane : lane + width]
+        copies.append(pltpu.make_async_copy(block, here, sems.at[n]))
+    for copy in copies:
+        copy.start()
+    for copy in copies:
+        copy.wait()
+
+
+def placed(targets, blocks, wide, shape):
+    operands = [*blocks] + ([] if wide is None else [in_vmem(wide)])
+    return pl.pallas_call(
+        functools.partial(place_kernel, targets),
+        out_shape=pltpu.VMEM(shape, BF16),
+        in_specs=[pl.BlockSpec(memory_space=pl.ANY)] * len(operands),
+        out_specs=pl.BlockSpec(memory_space=pl.ANY),
+        scratch_shapes=[pltpu.SemaphoreType.DMA((len(targets),))],
+        input_output_aliases={} if wide is None else {len(blocks): 0},
+        cost_estimate=pl.CostEstimate(flops=0, bytes_accessed=1 << 20, transcendentals=0),
+        name="place",
+    )(*operands)
+
+
+def project_kernel(head_size, factor, wide, w_ref, *refs):
+    lasts, (q_ref, kv_ref) = refs[:-2], refs[-2:]
+    rows, width = lasts[0].shape
+    depth, out_width = w_ref.shape[1:]
+    done = depth - width
+    for stream, last in enumerate(lasts):
+        here = slice(stream * rows, (stream + 1) * rows)
+        q, k, v = (
+            jnp.dot(wide[here, :done], w_ref[group, :done, :], preferred_element_type=F32)
+            + jnp.dot(last[...], w_ref[group, done:, :], preferred_element_type=F32)
+            for group in range(3)
+        )
+        power = None
+        for lane in range(0, depth, 128):
+            if lane < done:
+                values = wide[here, lane : lane + 128].astype(F32)
+            else:
+                values = last[:, lane - done : lane - done + 128].astype(F32)
+            power = values * values if power is None else power + values * values
+        scale = lax.rsqrt(jnp.sum(power, axis=-1, keepdims=True) * (1.0 / depth) + 1e-06)
+        q, k, v = q * scale, k * scale, v * scale
+        for head in range(out_width // head_size):
+            lanes = slice(head * head_size, (head + 1) * head_size)
+            qh, kh = q[:, lanes], k[:, lanes]
+            q_size = lax.rsqrt(jnp.sum(qh * qh, axis=-1, keepdims=True) + 1e-06)
+            k_size = lax.rsqrt(jnp.sum(kh * kh, axis=-1, keepdims=True) + 1e-06)
+            q_ref[here, lanes] = (qh * (q_size * (factor[head] * LOG2E))).astype(BF16)
+            kv_ref[here, lanes] = (kh * k_size).astype(BF16)
+        kv_ref[here, out_width:] = v.astype(BF16)
+
+
+def project(factor, wide, weights, lasts, head_size):
+    rows = wide.shape[0]
     groups, depth, out_width = weights.shape
     return pl.pallas_call(
-        functools.partial(project_kernel, head_size, base),
+        functools.partial(project_kernel, head_size),
         out_shape=(pltpu.VMEM((rows, out_width), BF16), pltpu.VMEM((rows, 2 * out_width), BF16)),
-        in_specs=[SMEM, SMEM, pl.BlockSpec(memory_space=pltpu.HBM)] + [VMEM] * (1 + len(blocks)),
+        in_specs=[SMEM] + [VMEM] * (2 + len(lasts)),
         out_specs=(VMEM, VMEM),
-        scratch_shapes=[pltpu.VMEM((rows, depth), BF16), pltpu.SemaphoreType.DMA(())],
         compiler_params=pltpu.CompilerParams(vmem_limit_bytes=16 << 20),
         cost_estimate=pl.CostEstimate(
             flops=2 * rows * depth * groups * out_width,
@@ -136,7 +161,7 @@
             transcendentals=0,
         ),
         name="project",
-    )(at, in_hbm(factor), in_hbm(tokens), in_vmem(weights), *map(in_vmem, blocks))
+    )(in_hbm(factor), in_vmem(wide), in_vmem(weights), *map(in_vmem, lasts))
 
 
 def attend_blocks(sources, ids, q_first, q_refs, id_col, id_row, kv_refs, v_ones, acc, head_size):
@@ -189,7 +214,9 @@
                     add(True)
 
 
-def attend_kernel(count_q, count_kv, head_size, has_acc, count_out, info, ids, *refs):
+def attend_kernel(
+    count_q, count_kv, head_size, has_acc, count_out, count_streams, info, ids, *refs
+):
     q_refs, rest = refs[:count_q], refs[count_q:]
     (id_col, id_row), rest = rest[:2], rest[2:]
     kv_refs, rest = rest[:count_kv], rest[count_kv:]
@@ -217,19 +244,20 @@
     out_width = outs[0].shape[1]
     for number, out in enumerate(outs):
         lane = info[count_kv + 1 + number] * out_width
-        stream = number * count_q // count_out
+        first = number * count_streams // count_out * out.shape[0]
         out[...] = jnp.dot(
-            attended[stream * rows : (stream + 1) * rows, :],
+            attended[first : first + out.shape[0], :],
             w_ref[:, pl.ds(pl.multiple_of(lane, out_width), out_width)],
             preferred_element_type=F32,
         ).astype(BF16)
 
 
-def attend(info, ids, queries, id_col, id_row, kvs, head_size, acc=None, w_out=None, count_out=0):
+def attend(info, ids, queries, id_col, id_row, kvs, head_size, acc=None, w_out=None, streams=0):
     rows, width = queries[0].shape
     total = rows * len(queries)
     keys = kvs[0].shape[0]
     heads = width // head_size
+    count_out = streams * w_out.shape[1] // width if streams else 0
     scratch = [
         pltpu.VMEM((heads, keys, 2 * head_size), BF16),
         pltpu.VMEM((total, 2 * width), F32),
@@ -240,13 +268,13 @@
     if count_out:
         operands.append(in_hbm(w_out))
         scratch.append(pltpu.VMEM((total, width), BF16))
-        shape = pltpu.VMEM((rows, w_out.shape[1] * len(queries) // count_out), BF16)
+        shape = pltpu.VMEM((total // streams, w_out.shape[1] * streams // count_out), BF16)
     else:
         shape = pltpu.VMEM((total, 2 * width), F32)
     outs = count_out or 1
     return pl.pallas_call(
         functools.partial(
-            attend_kernel, len(queries), len(kvs), head_size, acc is not None, count_out
+            attend_kernel, len(queries), len(kvs), head_size, acc is not None, count_out, streams
         ),
         out_shape=(shape,) * outs,
         in_specs=[SMEM, SMEM] + [VMEM] * len(operands),
@@ -256,7 +284,7 @@
             vmem_limit_bytes=(16 << 20) + 2 * kvs[0].size * 2 * len(kvs)
         ),
         cost_estimate=pl.CostEstimate(
-            flops=6 * total * keys * len(kvs) * width + 2 * rows * width * width * count_out,
+            flops=6 * total * keys * len(kvs) * width + 2 * total * width * width * count_out,
             bytes_accessed=4 * keys * len(kvs) * width + 8 * total * width,
             transcendentals=total * keys * len(kvs) * heads,
         ),
@@ -279,15 +307,17 @@
     chip, core = seq_at // 2, seq_at % 2
     index_at = lambda offset: ring_index((place + offset + ring) % ring, ring)
     numbers = lambda values: jnp.stack(values).astype(jnp.int32)
-    id_row = scale_ids.reshape(-1, 1, half)
+    id_row = scale_ids.reshape(-1, 1, rows)
     id_col = lax.dynamic_slice_in_dim(scale_ids, seq_at * rows, rows)[:, None]
+    at = [index_at(offset) for offset in range(ring)]
 
     streams, ways = (0, 1), ((0, 1), (1, -1))
     farthest = ring // 2
     reach = [(farthest, farthest - 1), (farthest - 1, farthest)]
 
+    order = [0] + [sign * step % ring for step in range(1, farthest) for sign in (-1, 1)] + [farthest]
     held = [[tokens[s * half : (s + 1) * half]] * 2 for s in streams]
-    blocks, offsets = [[] for s in streams], [[0] for s in streams]
+    wide, blocks, targets = None, [in_hbm(tokens)], [(0, 0)]
     for step in range(1, farthest + 1):
         for s in streams:
             for way, sign in ways:
@@ -295,43 +325,47 @@
                     held[s][way] = along(held[s][way], sign, ring)
         if step == 1:
             held[1][1], weights = lax.optimization_barrier(
-                (held[1][1], fold_gain(norm_gain, w_qkv))
+                (held[1][1], fold_gain(order, numbers(at), norm_gain, w_qkv))
             )
-        for s in streams:
-            for way, sign in ways:
-                if step <= reach[s][way]:
-                    blocks[s].append(held[s][way])
-                    offsets[s].append(-sign * step)
-    queries, kvs = [], []
-    for s in streams:
-        at = numbers([index_at(offset) for offset in offsets[s]])
-        query, kv = project(at, head_scale, tokens, weights, blocks[s], s * half, head_size)
-        queries.append(query)
-        kvs.append(kv)
+        elif step == 2:
+            wide = placed(targets, blocks, wide, (rows, ring * width))
+            blocks, targets = [], []
+        elif step == 3:
+            held[1][1], wide = lax.optimization_barrier(
+                (held[1][1], placed(targets, blocks, wide, (rows, ring * width)))
+            )
+            blocks, targets = [], []
+        if step < farthest:
+            for s in streams:
+                for way, sign in ways:
+                    blocks.append(in_vmem(held[s][way]))
+                    targets.append((s * half, (2 * step - 1 + way) * width))
+    wide = placed(targets, blocks, wide, (rows, ring * width))
+    lasts = [held[0][0], held[1][1]]
+    query, kv = project(head_scale, wide, weights, lasts, head_size)
 
     far, straight, crossed = [], [], []
     for step in range(outer):
         source = 2 * ((chip + outer - step) % outer)
-        for s in streams:
-            straight.append((source + core) * rows + s * half)
-            crossed.append((source + 1 - core) * rows + s * half)
-            if step:
-                far.append(lax.ppermute(kvs[s], "seq", [
-                    (2 * a + b, 2 * ((a + step) % outer) + b) for a in range(outer) for b in (0, 1)
-                ]))
+        straight.append((source + core) * rows)
+        crossed.append((source + 1 - core) * rows)
+        if step:
+            far.append(lax.ppermute(kv, "seq", [
+                (2 * a + b, 2 * ((a + step) % outer) + b) for a in range(outer) for b in (0, 1)
+            ]))
     first = [seq_at * rows]
-    info = numbers(straight[:2] + crossed[:2] + first)
-    keys = kvs + [swapped(kv, seqs) for kv in kvs]
-    (acc,) = attend(info, scale_ids, queries, id_col, id_row, keys, head_size)
+    info = numbers(straight[:1] + crossed[:1] + first)
+    keys = [kv, swapped(kv, seqs)]
+    (acc,) = attend(info, scale_ids, [query], id_col, id_row, keys, head_size)
     acc, far = lax.optimization_barrier((acc, far))
     far_crossed = [swapped(block, seqs) for block in far]
-    info = numbers(straight[2:] + first)
-    (acc,) = attend(info, scale_ids, queries, id_col, id_row, far, head_size, acc)
+    info = numbers(straight[1:] + first)
+    (acc,) = attend(info, scale_ids, [query], id_col, id_row, far, head_size, acc)
 
     goals = [[*range(up, 0, -1), *range(-down, 0), 0] for up, down in reach]
-    info = numbers(crossed[2:] + first + [index_at(goal) for goal in goals[0] + goals[1]])
+    info = numbers(crossed[1:] + first + [at[goal % ring] for goal in goals[0] + goals[1]])
     parts = attend(
-        info, scale_ids, queries, id_col, id_row, far_crossed, head_size, acc, w_out, 2 * ring
+        info, scale_ids, [query], id_col, id_row, far_crossed, head_size, acc, w_out, len(streams)
     )
     parts = [dict(zip(goals[s], parts[s * ring : (s + 1) * ring])) for s in streams]
     sums = [[None, None] for s in streams]

time: 87.4 us -> 84.4 us (0.966)
  Pallas kernels: 21.8 us -> 15.7 us
  waiting for transfers between devices: 23.4 us -> 27 us
  starting transfers between devices: 32 us -> 29.7 us
  local copies, waits for them, and re-layouts: 8.2 us -> 10 us
    ppermute x2 -> x1, waiting for transfers between devices: 5.42 us -> 9.13 us  [body(): lax.ppermute(kv, 'seq', [(2 * a + b, 2 * ((a + step) % outer) + b) for a...]
    pallas_call x3 -> x5, Pallas kernels: 10.5 us -> 6.95 us  [the longest x1 3.01 us: fold_gain(): pl.pallas_call(functools.partial(fold_kernel, order), out_shape=pltpu.VME...]
    pallas_call x3, Pallas kernels: 11.3 us -> 8.71 us  [attend(): pl.pallas_call(functools.partial(attend_kernel, len(queries), len(kvs), h...]
    unnamed x22 -> x12, local copies, waits for them, and re-layouts: 5.97 us -> 7.98 us
    ppermute x2 -> x1, starting transfers between devices: 2.03 us -> 0.53 us  [body(): lax.ppermute(kv, 'seq', [(2 * a + b, 2 * ((a + step) % outer) + b) for a...]
    ppermute x4 -> x2, starting transfers between devices: 0.98 us -> 0.07 us  [swapped(): lax.ppermute(value, 'seq', [(seq, seq + 1 - 2 * (seq % 2)) for seq in ran...]
  transfers between devices with their start and end apart: 34 -> 31, of which waited for: 13 -> 13; matrix products, arithmetic and copies ran while one was open for 2% -> 2% of each run, Pallas kernels for 21% -> 12%
where the time goes in v7:
time: 84.4 us; the launch traced here: 83.9 us
  starting transfers between devices  29.7 us (35%)
  waiting for transfers between devices  27 us (32%)
  Pallas kernels  15.7 us (19%)
  local copies, waits for them, and re-layouts  10 us (12%)
  other arithmetic  1.32 us (2%)
    ppermute x28, starting transfers between devices, along(): lax.ppermute(value, 'head', [(order[p], order[(p + step) % count]) for p...  29.1 us
    ppermute x28, waiting for transfers between devices, along(): lax.ppermute(value, 'head', [(order[p], order[(p + step) % count]) for p...  17.5 us
    ppermute x1, waiting for transfers between devices, body(): lax.ppermute(kv, 'seq', [(2 * a + b, 2 * ((a + step) % outer) + b) for a...  9.13 us
    pallas_call x3, Pallas kernels, attend(): pl.pallas_call(functools.partial(attend_kernel, len(queries), len(kvs), h...  8.71 us
    unnamed x12, local copies, waits for them, and re-layouts  7.98 us
    pallas_call x1, Pallas kernels, fold_gain(): pl.pallas_call(functools.partial(fold_kernel, order), out_shape=pltpu.VME...  3.01 us
    pallas_call x1, Pallas kernels, project(): pl.pallas_call(functools.partial(project_kernel, head_size), out_shape=(p...  2.72 us
  transfers between devices with their start and end apart: 31, of which 13 were waited for; matrix products, arithmetic and copies ran while one was open for 2% of the time, Pallas kernels for 12%

profile of v7, /device:TPU:10, one launch (start us, length us, event | category | flops | bytes accessed | tf_op | source)
XLA Modules:
  0.0 83.9 jit_solution(11158300580496649940)
XLA Ops:
  0.0 1.0 %fusion = (bf16[256,256]{1,0:T(8,128)(2,1)S(1)}, bf16[256,256]{1,0:T(8,128)(2,1)S(1)}) fusion(bf16[512,256]{1,0:T(8,128)(2,1)} %refs_0_.1), kind=kLoop, calls=%fused_computation.15 | loop fusion | bytes 524288 | tf_op jit(solution)/shard_map/slice | solution.py:319
  1.0 0.5 collective-permute-start.9
  1.5 1.6 %collective-permute-start = (bf16[256,256]{1,0:T(8,128)(2,1)S(1)}, bf16[256,256]{1,0:T(8,128)(2,1)S(1)}, u32[]{:S(2)}, u32[]{:S(2)}) collective-permute-start(bf16[256,256]{1,0:T(8,128)(2,1)S(1)} %get-tuple-element.54), channel_id=1, source_target_pairs={{0,2},{2,4},{4,6},{6,7},{7,5},{5,3},{3,1},{1,0},{8,10},{10,12},{12... | collective-permute-start | bytes 393224 | tf_op jit(solution)/shard_map/ppermute | solution.py:33
  3.5 1.6 %collective-permute-start.6 = (bf16[256,256]{1,0:T(8,128)(2,1)S(1)}, bf16[256,256]{1,0:T(8,128)(2,1)S(1)}, u32[]{:S(2)}, u32[]{:S(2)}) collective-permute-start(bf16[256,256]{1,0:T(8,128)(2,1)S(1)} %get-tuple-element.53), channel_id=1, source_target_pairs={{0,2},{2,4},{4,6},{6,7},{7,5},{5,3},{3,1},{1,0},{8,10},{10,12},{12... | collective-permute-start | bytes 393224 | tf_op jit(solution)/shard_map/ppermute | solution.py:33
  5.2 3.0 %fold_gain.1.w_ref = bf16[3,2048,256]{2,1,0:T(8,128)(2,1)S(1)} custom-call(s32[8]{0:T(128)S(1)} %stack.80.at, f32[16,128]{1,0:T(8,128)} %bitcast.19, bf16[3,2048,256]{2,1,0:T(8,128)(2,1)} %w_hbm.1), custom_call_target="tpu_custom_call" | custom-call | flops 1572864 | bytes 6291456 | tf_op jit(solution)/shard_map/fold_gain/pallas_call | solution.py:77
  8.2 1.6 %copy-done.2 = bf16[3,2048,256]{2,1,0:T(8,128)(2,1)} copy-done((bf16[3,2048,256]{2,1,0:T(8,128)(2,1)}, bf16[3,2048,256]{2,1,0:T(8,128)(2,1)S(1)}, u32[]{:S(2)}) %copy-start.2) | copy-done | bytes 3145752
  10.3 1.6 %collective-permute-start.1 = (bf16[256,256]{1,0:T(8,128)(2,1)S(1)}, bf16[256,256]{1,0:T(8,128)(2,1)S(1)}, u32[]{:S(2)}, u32[]{:S(2)}) collective-permute-start(bf16[256,256]{1,0:T(8,128)(2,1)S(1)} %collective-permute-done.refs_1_), channel_id=1, source_target_pairs={{0,2},{2,4},{4,6},{6,7},{7,5},{5,3},{3,1},{1,0},{8,10},{10,12},{12... | collective-permute-start | bytes 393224 | tf_op jit(solution)/shard_map/ppermute | solution.py:33
  12.3 1.6 %collective-permute-start.7 = (bf16[256,256]{1,0:T(8,128)(2,1)S(1)}, bf16[256,256]{1,0:T(8,128)(2,1)S(1)}, u32[]{:S(2)}, u32[]{:S(2)}) collective-permute-start(bf16[256,256]{1,0:T(8,128)(2,1)S(1)} %collective-permute-done.6.refs_3_), channel_id=1, source_target_pairs={{0,2},{2,4},{4,6},{6,7},{7,5},{5,3},{3,1},{1,0},{8,10},{10,12},{12... | collective-permute-start | bytes 393224 | tf_op jit(solution)/shard_map/ppermute | solution.py:33
  13.9 1.9 %collective-permute-done.10.refs_3_ = bf16[256,256]{1,0:T(8,128)(2,1)S(1)} collective-permute-done((bf16[256,256]{1,0:T(8,128)(2,1)S(1)}, bf16[256,256]{1,0:T(8,128)(2,1)S(1)}, u32[]{:S(2)}, u32[]{:S(2)}) %collective-permute-start.10) | collective-permute-done | bytes 131104 | tf_op jit(solution)/shard_map/ppermute | solution.py:33
  16.3 1.6 %collective-permute-start.2 = (bf16[256,256]{1,0:T(8,128)(2,1)S(1)}, bf16[256,256]{1,0:T(8,128)(2,1)S(1)}, u32[]{:S(2)}, u32[]{:S(2)}) collective-permute-start(bf16[256,256]{1,0:T(8,128)(2,1)S(1)} %collective-permute-done.1.refs_0_), channel_id=1, source_target_pairs={{0,2},{2,4},{4,6},{6,7},{7,5},{5,3},{3,1},{1,0},{8,10},{10,12},{12... | collective-permute-start | bytes 393224 | tf_op jit(solution)/shard_map/ppermute | solution.py:33
  17.9 1.0 %place.3.refs_4_ = bf16[512,2048]{1,0:T(8,128)(2,1)S(1)} custom-call(bf16[512,256]{1,0:T(8,128)(2,1)} %refs_0_.1, bf16[256,256]{1,0:T(8,128)(2,1)S(1)} %collective-permute-done.refs_1_, bf16[256,256]{1,0:T(8,128)(2,1)S(1)} %collective-permute-done.3.refs_2_, bf16[256,256]{1,0:T(8,128)(2,1)S(1)} %collective-permute-done.6.refs_3_, ...), custom_call_target="tpu_custom_call" | custom-call | bytes 1048576 | tf_op jit(solution)/shard_map/place/pallas_call | solution.py:106
  18.9 1.3 %copy-done = bf16[512,2048]{1,0:T(8,128)(2,1)} copy-done((bf16[512,2048]{1,0:T(8,128)(2,1)}, bf16[512,2048]{1,0:T(8,128)(2,1)S(1)}, u32[]{:S(2)}) %copy-start) | copy-done | bytes 2097176
  20.6 1.6 %collective-permute-start.8 = (bf16[256,256]{1,0:T(8,128)(2,1)S(1)}, bf16[256,256]{1,0:T(8,128)(2,1)S(1)}, u32[]{:S(2)}, u32[]{:S(2)}) collective-permute-start(bf16[256,256]{1,0:T(8,128)(2,1)S(1)} %collective-permute-done.7.refs_2_), channel_id=1, source_target_pairs={{0,2},{2,4},{4,6},{6,7},{7,5},{5,3},{3,1},{1,0},{8,10},{10,12},{12... | collective-permute-start | bytes 393224 | tf_op jit(solution)/shard_map/ppermute | solution.py:33
  22.2 1.6 %copy-done.1 = bf16[512,2048]{1,0:T(8,128)(2,1)S(1)} copy-done((bf16[512,2048]{1,0:T(8,128)(2,1)S(1)}, bf16[512,2048]{1,0:T(8,128)(2,1)}, u32[]{:S(2)}) %copy-start.1) | copy-done | bytes 2097176
  23.9 0.5 collective-permute-start.13
  24.4 1.6 %collective-permute-start.12 = (bf16[256,256]{1,0:T(8,128)(2,1)S(1)}, bf16[256,256]{1,0:T(8,128)(2,1)S(1)}, u32[]{:S(2)}, u32[]{:S(2)}) collective-permute-start(bf16[256,256]{1,0:T(8,128)(2,1)S(1)} %collective-permute-done.2.refs_0_), channel_id=1, source_target_pairs={{0,2},{2,4},{4,6},{6,7},{7,5},{5,3},{3,1},{1,0},{8,10},{10,12},{12... | collective-permute-start | bytes 393224 | tf_op jit(solution)/shard_map/ppermute | solution.py:33
  26.2 2.8 %collective-permute-done.13.refs_1_ = bf16[256,256]{1,0:T(8,128)(2,1)S(1)} collective-permute-done((bf16[256,256]{1,0:T(8,128)(2,1)S(1)}, bf16[256,256]{1,0:T(8,128)(2,1)S(1)}, u32[]{:S(2)}, u32[]{:S(2)}) %collective-permute-start.13) | collective-permute-done | bytes 131104 | tf_op jit(solution)/shard_map/ppermute | solution.py:33
  29.4 0.7 copy-done.4
  30.1 1.9 %copy-done.3 = bf16[3,2048,256]{2,1,0:T(8,128)(2,1)S(1)} copy-done((bf16[3,2048,256]{2,1,0:T(8,128)(2,1)S(1)}, bf16[3,2048,256]{2,1,0:T(8,128)(2,1)}, u32[]{:S(2)}) %copy-start.3) | copy-done | bytes 3145752
  32.0 0.9 %copy-done.5 = bf16[256,256]{1,0:T(8,128)(2,1)S(1)} copy-done((bf16[256,256]{1,0:T(8,128)(2,1)S(1)}, bf16[256,256]{1,0:T(8,128)(2,1)}, u32[]{:S(2)}) %copy-start.5) | copy-done | bytes 131096
  32.9 2.7 %project.1 = (bf16[512,256]{1,0:T(8,128)(2,1)S(1)}, bf16[512,512]{1,0:T(8,128)(2,1)S(1)}) custom-call(f32[2]{0:T(128)} %factor.1, bf16[512,2048]{1,0:T(8,128)(2,1)S(1)} %place.5.wide, bf16[3,2048,256]{2,1,0:T(8,128)(2,1)S(1)} %copy-done.3, bf16[256,256]{1,0:T(8,128)(2,1)S(1)} %copy-done.5, bf16[256,256]{1,0:T(8,128)(2,1)S(1)} %collective-permute-done.13.refs_1_), custom_call_target="tpu_custom_call" | custom-call | flops 1610612736 | bytes 5242880 | tf_op jit(solution)/shard_map/project/pallas_call | solution.py:152
  35.7 0.5 collective-permute-start.15
  36.2 0.8 dynamic_slice.3
  37.6 3.3 %attend.2.refs_4_ = f32[512,512]{1,0:T(8,128)S(1)} custom-call(s32[3]{0:T(128)S(1)} %pad_add_fusion.info, s32[2048]{0:T(1024)} %ids.5, bf16[512,256]{1,0:T(8,128)(2,1)S(1)} %get-tuple-element.33.refs_0_, s32[512,1]{1,0:T(8,128)S(1)} %copy.11.refs_1_, s32[4,1,512]{2,1,0:T(1,128)} %bitcast.16, bf16[512,512]{1,0:T(8,128)(2,1)S(1)} %get-tuple-element.34.refs_3_, ...), custom_call_target="tpu_custom_call" | custom-call | flops 805306368 | bytes 2097152 | tf_op jit(solution)/shard_map/attend/pallas_call | solution.py:275
  40.9 9.1 %collective-permute-done.15.refs_3_ = bf16[512,512]{1,0:T(8,128)(2,1)S(1)} collective-permute-done((bf16[512,512]{1,0:T(8,128)(2,1)S(1)}, bf16[512,512]{1,0:T(8,128)(2,1)S(1)}, u32[]{:S(2)}, u32[]{:S(2)}) %collective-permute-start.15) | collective-permute-done | bytes 524320 | tf_op jit(solution)/shard_map/ppermute | solution.py:353
  50.2 2.1 %attend.3.refs_4_ = f32[512,512]{1,0:T(8,128)S(1)} custom-call(s32[2]{0:T(128)S(1)} %pad_add_fusion.1.info, s32[2048]{0:T(1024)} %ids.5, bf16[512,256]{1,0:T(8,128)(2,1)S(1)} %get-tuple-element.33.refs_0_, s32[512,1]{1,0:T(8,128)S(1)} %copy.11.refs_1_, s32[4,1,512]{2,1,0:T(1,128)} %bitcast.17, bf16[512,512]{1,0:T(8,128)(2,1)S(1)} %collective-permute-done.15.refs_3_, ...), custom_call_target="tpu_custom_call" | custom-call | flops 402653184 | bytes 1572864 | tf_op jit(solution)/shard_map/attend/pallas_call | solution.py:275
  52.3 3.3 %attend_last.1 = (bf16[256,256]{1,0:T(8,128)(2,1)S(1)}, bf16[256,256]{1,0:T(8,128)(2,1)S(1)}, bf16[256,256]{1,0:T(8,128)(2,1)S(1)}, bf16[256,256]{1,0:T(8,128)(2...) custom-call(s32[18]{0:T(128)S(1)} %stack.79.info, ...), custom_call_target="tpu_custom_call" | custom-call | flops 1476395008 | bytes 1572864 | tf_op jit(solution)/shard_map/attend_last/pallas_call | solution.py:275
  55.6 1.6 %collective-permute-start.17 = (bf16[256,256]{1,0:T(8,128)(2,1)S(1)}, bf16[256,256]{1,0:T(8,128)(2,1)S(1)}, u32[]{:S(2)}, u32[]{:S(2)}) collective-permute-start(bf16[256,256]{1,0:T(8,128)(2,1)S(1)} %get-tuple-element.41), channel_id=1, source_target_pairs={{0,2},{2,4},{4,6},{6,7},{7,5},{5,3},{3,1},{1,0},{8,10},{10,12},{12... | collective-permute-start | bytes 393224 | tf_op jit(solution)/shard_map/ppermute | solution.py:33
  57.7 1.6 %collective-permute-start.24 = (bf16[256,256]{1,0:T(8,128)(2,1)S(1)}, bf16[256,256]{1,0:T(8,128)(2,1)S(1)}, u32[]{:S(2)}, u32[]{:S(2)}) collective-permute-start(bf16[256,256]{1,0:T(8,128)(2,1)S(1)} %get-tuple-element.48), channel_id=1, source_target_pairs={{0,2},{2,4},{4,6},{6,7},{7,5},{5,3},{3,1},{1,0},{8,10},{10,12},{12... | collective-permute-start | bytes 393224 | tf_op jit(solution)/shard_map/ppermute | solution.py:33
  59.7 2.2 %collective-permute-done.17 = bf16[256,256]{1,0:T(8,128)(2,1)S(1)} collective-permute-done((bf16[256,256]{1,0:T(8,128)(2,1)S(1)}, bf16[256,256]{1,0:T(8,128)(2,1)S(1)}, u32[]{:S(2)}, u32[]{:S(2)}) %collective-permute-start.17) | collective-permute-done | bytes 131104 | tf_op jit(solution)/shard_map/ppermute | solution.py:33
  62.0 1.7 %collective-permute-start.18 = (bf16[256,256]{1,0:T(8,128)(2,1)S(1)}, bf16[256,256]{1,0:T(8,128)(2,1)S(1)}, u32[]{:S(2)}, u32[]{:S(2)}) collective-permute-start(bf16[256,256]{1,0:T(8,128)(2,1)S(1)} %add_convert_fusion.11), channel_id=1, source_target_pairs={{0,2},{2,4},{4,6},{6,7},{7,5},{5,3},{3,1},{1,0},{8,10},{10,12},{12... | collective-permute-start | bytes 393224 | tf_op jit(solution)/shard_map/ppermute | solution.py:33
  63.7 0.5 collective-permute-start.22
  64.2 0.6 collective-permute-done.24
  64.8 1.7 %collective-permute-start.25 = (bf16[256,256]{1,0:T(8,128)(2,1)S(1)}, bf16[256,256]{1,0:T(8,128)(2,1)S(1)}, u32[]{:S(2)}, u32[]{:S(2)}) collective-permute-start(bf16[256,256]{1,0:T(8,128)(2,1)S(1)} %add_convert_fusion.5), channel_id=1, source_target_pairs={{0,2},{2,4},{4,6},{6,7},{7,5},{5,3},{3,1},{1,0},{8,10},{10,12},{12... | collective-permute-start | bytes 393224 | tf_op jit(solution)/shard_map/ppermute | solution.py:33
  66.5 0.5 collective-permute-start.28
  67.0 0.6 collective-permute-done.18
  67.6 1.7 %collective-permute-start.19 = (bf16[256,256]{1,0:T(8,128)(2,1)S(1)}, bf16[256,256]{1,0:T(8,128)(2,1)S(1)}, u32[]{:S(2)}, u32[]{:S(2)}) collective-permute-start(bf16[256,256]{1,0:T(8,128)(2,1)S(1)} %add_convert_fusion.10), channel_id=1, source_target_pairs={{0,2},{2,4},{4,6},{6,7},{7,5},{5,3},{3,1},{1,0},{8,10},{10,12},{12... | collective-permute-start | bytes 393224 | tf_op jit(solution)/shard_map/ppermute | solution.py:33
  69.3 0.5 collective-permute-start.23
  69.8 1.5 %collective-permute-done.25 = bf16[256,256]{1,0:T(8,128)(2,1)S(1)} collective-permute-done((bf16[256,256]{1,0:T(8,128)(2,1)S(1)}, bf16[256,256]{1,0:T(8,128)(2,1)S(1)}, u32[]{:S(2)}, u32[]{:S(2)}) %collective-permute-start.25) | collective-permute-done | bytes 131104 | tf_op jit(solution)/shard_map/ppermute | solution.py:33
  71.3 1.7 %collective-permute-start.26 = (bf16[256,256]{1,0:T(8,128)(2,1)S(1)}, bf16[256,256]{1,0:T(8,128)(2,1)S(1)}, u32[]{:S(2)}, u32[]{:S(2)}) collective-permute-start(bf16[256,256]{1,0:T(8,128)(2,1)S(1)} %add_convert_fusion.4), channel_id=1, source_target_pairs={{0,2},{2,4},{4,6},{6,7},{7,5},{5,3},{3,1},{1,0},{8,10},{10,12},{12... | collective-permute-start | bytes 393224 | tf_op jit(solution)/shard_map/ppermute | solution.py:33
  73.0 0.5 collective-permute-start.29
  73.5 0.6 collective-permute-done.19
  74.1 1.7 %collective-permute-start.20 = (bf16[256,256]{1,0:T(8,128)(2,1)S(1)}, bf16[256,256]{1,0:T(8,128)(2,1)S(1)}, u32[]{:S(2)}, u32[]{:S(2)}) collective-permute-start(bf16[256,256]{1,0:T(8,128)(2,1)S(1)} %add_convert_fusion.9), channel_id=1, source_target_pairs={{0,2},{2,4},{4,6},{6,7},{7,5},{5,3},{3,1},{1,0},{8,10},{10,12},{12... | collective-permute-start | bytes 393224 | tf_op jit(solution)/shard_map/ppermute | solution.py:33
  75.8 2.3 %collective-permute-done.29 = bf16[256,256]{1,0:T(8,128)(2,1)S(1)} collective-permute-done((bf16[256,256]{1,0:T(8,128)(2,1)S(1)}, bf16[256,256]{1,0:T(8,128)(2,1)S(1)}, u32[]{:S(2)}, u32[]{:S(2)}) %collective-permute-start.29) | collective-permute-done | bytes 131104 | tf_op jit(solution)/shard_map/ppermute | solution.py:33
  78.1 0.5 collective-permute-start.30
  78.6 0.6 collective-permute-done.20
  79.2 3.9 %collective-permute-done.30 = bf16[256,256]{1,0:T(8,128)(2,1)S(1)} collective-permute-done((bf16[256,256]{1,0:T(8,128)(2,1)S(1)}, bf16[256,256]{1,0:T(8,128)(2,1)S(1)}, u32[]{:S(2)}, u32[]{:S(2)}) %collective-permute-start.30) | collective-permute-done | bytes 131104 | tf_op jit(solution)/shard_map/ppermute | solution.py:33
  83.2 0.7 pad_maximum_fusion
  (54 shorter events, 5.2 us)
Async XLA Ops:
  1.0 8.8 %collective-permute-start.9 = (bf16[256,256]{1,0:T(8,128)(2,1)S(1)}, bf16[256,256]{1,0:T(8,128)(2,1)S(1)}, u32[]{:S(2)}, u32[]{:S(2)}) collective-permute-start(bf16[256,256]{1,0:T(8,128)(2,1)S(1)} %get-tuple-element.53), channel_id=1, source_target_pairs={{0,1},{2,0},{4,2},{6,4},{7,6},{5,7},{3,5},{1,3},{8,9},{10,8},{12,1... | collective-permute-start | bytes 393224 | tf_op jit(solution)/shard_map/ppermute | solution.py:33
  1.5 8.8 %collective-permute-start = (bf16[256,256]{1,0:T(8,128)(2,1)S(1)}, bf16[256,256]{1,0:T(8,128)(2,1)S(1)}, u32[]{:S(2)}, u32[]{:S(2)}) collective-permute-start(bf16[256,256]{1,0:T(8,128)(2,1)S(1)} %get-tuple-element.54), channel_id=1, source_target_pairs={{0,2},{2,4},{4,6},{6,7},{7,5},{5,3},{3,1},{1,0},{8,10},{10,12},{12... | collective-permute-start | bytes 393224 | tf_op jit(solution)/shard_map/ppermute | solution.py:33
  3.1 8.8 %collective-permute-start.3 = (bf16[256,256]{1,0:T(8,128)(2,1)S(1)}, bf16[256,256]{1,0:T(8,128)(2,1)S(1)}, u32[]{:S(2)}, u32[]{:S(2)}) collective-permute-start(bf16[256,256]{1,0:T(8,128)(2,1)S(1)} %get-tuple-element.54), channel_id=1, source_target_pairs={{0,1},{2,0},{4,2},{6,4},{7,6},{5,7},{3,5},{1,3},{8,9},{10,8},{12,1... | collective-permute-start | bytes 393224 | tf_op jit(solution)/shard_map/ppermute | solution.py:33
  3.5 8.8 %collective-permute-start.6 = (bf16[256,256]{1,0:T(8,128)(2,1)S(1)}, bf16[256,256]{1,0:T(8,128)(2,1)S(1)}, u32[]{:S(2)}, u32[]{:S(2)}) collective-permute-start(bf16[256,256]{1,0:T(8,128)(2,1)S(1)} %get-tuple-element.53), channel_id=1, source_target_pairs={{0,2},{2,4},{4,6},{6,7},{7,5},{5,3},{3,1},{1,0},{8,10},{10,12},{12... | collective-permute-start | bytes 393224 | tf_op jit(solution)/shard_map/ppermute | solution.py:33
  8.2 1.6 %copy-start.2 = (bf16[3,2048,256]{2,1,0:T(8,128)(2,1)}, bf16[3,2048,256]{2,1,0:T(8,128)(2,1)S(1)}, u32[]{:S(2)}) copy-start(bf16[3,2048,256]{2,1,0:T(8,128)(2,1)S(1)} %fold_gain.1.w_ref) | copy-start | bytes 9437188
  9.8 6.0 %collective-permute-start.10 = (bf16[256,256]{1,0:T(8,128)(2,1)S(1)}, bf16[256,256]{1,0:T(8,128)(2,1)S(1)}, u32[]{:S(2)}, u32[]{:S(2)}) collective-permute-start(bf16[256,256]{1,0:T(8,128)(2,1)S(1)} %collective-permute-done.9.refs_4_), channel_id=1, source_target_pairs={{0,1},{2,0},{4,2},{6,4},{7,6},{5,7},{3,5},{1,3},{8,9},{10,8},{12,1... | collective-permute-start | bytes 393224 | tf_op jit(solution)/shard_map/ppermute | solution.py:33
  10.3 6.0 %collective-permute-start.1 = (bf16[256,256]{1,0:T(8,128)(2,1)S(1)}, bf16[256,256]{1,0:T(8,128)(2,1)S(1)}, u32[]{:S(2)}, u32[]{:S(2)}) collective-permute-start(bf16[256,256]{1,0:T(8,128)(2,1)S(1)} %collective-permute-done.refs_1_), channel_id=1, source_target_pairs={{0,2},{2,4},{4,6},{6,7},{7,5},{5,3},{3,1},{1,0},{8,10},{10,12},{12... | collective-permute-start | bytes 393224 | tf_op jit(solution)/shard_map/ppermute | solution.py:33
  11.9 8.3 %collective-permute-start.4 = (bf16[256,256]{1,0:T(8,128)(2,1)S(1)}, bf16[256,256]{1,0:T(8,128)(2,1)S(1)}, u32[]{:S(2)}, u32[]{:S(2)}) collective-permute-start(bf16[256,256]{1,0:T(8,128)(2,1)S(1)} %collective-permute-done.3.refs_2_), channel_id=1, source_target_pairs={{0,1},{2,0},{4,2},{6,4},{7,6},{5,7},{3,5},{1,3},{8,9},{10,8},{12,1... | collective-permute-start | bytes 393224 | tf_op jit(solution)/shard_map/ppermute | solution.py:33
  12.3 8.3 %collective-permute-start.7 = (bf16[256,256]{1,0:T(8,128)(2,1)S(1)}, bf16[256,256]{1,0:T(8,128)(2,1)S(1)}, u32[]{:S(2)}, u32[]{:S(2)}) collective-permute-start(bf16[256,256]{1,0:T(8,128)(2,1)S(1)} %collective-permute-done.6.refs_3_), channel_id=1, source_target_pairs={{0,2},{2,4},{4,6},{6,7},{7,5},{5,3},{3,1},{1,0},{8,10},{10,12},{12... | collective-permute-start | bytes 393224 | tf_op jit(solution)/shard_map/ppermute | solution.py:33
  15.8 8.1 %collective-permute-start.11 = (bf16[256,256]{1,0:T(8,128)(2,1)S(1)}, bf16[256,256]{1,0:T(8,128)(2,1)S(1)}, u32[]{:S(2)}, u32[]{:S(2)}) collective-permute-start(bf16[256,256]{1,0:T(8,128)(2,1)S(1)} %collective-permute-done.10.refs_3_), channel_id=1, source_target_pairs={{0,1},{2,0},{4,2},{6,4},{7,6},{5,7},{3,5},{1,3},{8,9},{10,8},{12,1... | collective-permute-start | bytes 393224 | tf_op jit(solution)/shard_map/ppermute | solution.py:33
  16.3 8.2 %collective-permute-start.2 = (bf16[256,256]{1,0:T(8,128)(2,1)S(1)}, bf16[256,256]{1,0:T(8,128)(2,1)S(1)}, u32[]{:S(2)}, u32[]{:S(2)}) collective-permute-start(bf16[256,256]{1,0:T(8,128)(2,1)S(1)} %collective-permute-done.1.refs_0_), channel_id=1, source_target_pairs={{0,2},{2,4},{4,6},{6,7},{7,5},{5,3},{3,1},{1,0},{8,10},{10,12},{12... | collective-permute-start | bytes 393224 | tf_op jit(solution)/shard_map/ppermute | solution.py:33
  18.9 1.3 %copy-start = (bf16[512,2048]{1,0:T(8,128)(2,1)}, bf16[512,2048]{1,0:T(8,128)(2,1)S(1)}, u32[]{:S(2)}) copy-start(bf16[512,2048]{1,0:T(8,128)(2,1)S(1)} %place.3.refs_4_) | copy-start | bytes 6291460
  20.2 5.8 %collective-permute-start.5 = (bf16[256,256]{1,0:T(8,128)(2,1)S(1)}, bf16[256,256]{1,0:T(8,128)(2,1)S(1)}, u32[]{:S(2)}, u32[]{:S(2)}) collective-permute-start(bf16[256,256]{1,0:T(8,128)(2,1)S(1)} %collective-permute-done.4.refs_1_), channel_id=1, source_target_pairs={{0,1},{2,0},{4,2},{6,4},{7,6},{5,7},{3,5},{1,3},{8,9},{10,8},{12,1... | collective-permute-start | bytes 393224 | tf_op jit(solution)/shard_map/ppermute | solution.py:33
  20.6 5.4 %collective-permute-start.8 = (bf16[256,256]{1,0:T(8,128)(2,1)S(1)}, bf16[256,256]{1,0:T(8,128)(2,1)S(1)}, u32[]{:S(2)}, u32[]{:S(2)}) collective-permute-start(bf16[256,256]{1,0:T(8,128)(2,1)S(1)} %collective-permute-done.7.refs_2_), channel_id=1, source_target_pairs={{0,2},{2,4},{4,6},{6,7},{7,5},{5,3},{3,1},{1,0},{8,10},{10,12},{12... | collective-permute-start | bytes 393224 | tf_op jit(solution)/shard_map/ppermute | solution.py:33
  22.2 1.6 %copy-start.1 = (bf16[512,2048]{1,0:T(8,128)(2,1)S(1)}, bf16[512,2048]{1,0:T(8,128)(2,1)}, u32[]{:S(2)}) copy-start(bf16[512,2048]{1,0:T(8,128)(2,1)} %copy-done) | copy-start | bytes 6291460
  23.9 5.0 %collective-permute-start.13 = (bf16[256,256]{1,0:T(8,128)(2,1)S(1)}, bf16[256,256]{1,0:T(8,128)(2,1)S(1)}, u32[]{:S(2)}, u32[]{:S(2)}) collective-permute-start(bf16[256,256]{1,0:T(8,128)(2,1)S(1)} %collective-permute-done.11.refs_3_), channel_id=1, source_target_pairs={{0,1},{2,0},{4,2},{6,4},{7,6},{5,7},{3,5},{1,3},{8,9},{10,8},{12,1... | collective-permute-start | bytes 393224 | tf_op jit(solution)/shard_map/ppermute | solution.py:33
  24.4 5.0 %collective-permute-start.12 = (bf16[256,256]{1,0:T(8,128)(2,1)S(1)}, bf16[256,256]{1,0:T(8,128)(2,1)S(1)}, u32[]{:S(2)}, u32[]{:S(2)}) collective-permute-start(bf16[256,256]{1,0:T(8,128)(2,1)S(1)} %collective-permute-done.2.refs_0_), channel_id=1, source_target_pairs={{0,2},{2,4},{4,6},{6,7},{7,5},{5,3},{3,1},{1,0},{8,10},{10,12},{12... | collective-permute-start | bytes 393224 | tf_op jit(solution)/shard_map/ppermute | solution.py:33
  29.4 0.7 copy-start.4
  30.1 1.9 %copy-start.3 = (bf16[3,2048,256]{2,1,0:T(8,128)(2,1)S(1)}, bf16[3,2048,256]{2,1,0:T(8,128)(2,1)}, u32[]{:S(2)}) copy-start(bf16[3,2048,256]{2,1,0:T(8,128)(2,1)} %copy-done.2) | copy-start | bytes 9437188
  32.0 0.9 %copy-start.5 = (bf16[256,256]{1,0:T(8,128)(2,1)S(1)}, bf16[256,256]{1,0:T(8,128)(2,1)}, u32[]{:S(2)}) copy-start(bf16[256,256]{1,0:T(8,128)(2,1)} %copy-done.4) | copy-start | bytes 393220
  35.6 2.0 %collective-permute-start.14 = (bf16[512,512]{1,0:T(8,128)(2,1)S(1)}, bf16[512,512]{1,0:T(8,128)(2,1)S(1)}, u32[]{:S(2)}, u32[]{:S(2)}) collective-permute-start(bf16[512,512]{1,0:T(8,128)(2,1)S(1)} %get-tuple-element.34.refs_3_), channel_id=1, source_target_pairs={{0,8},{8,0},{16,24},{24,16},{1,9},{9,1},{17,25},{25,17},{2,10},{10... | collective-permute-start | bytes 1572872 | tf_op jit(solution)/shard_map/ppermute | solution.py:39
  35.7 14.3 %collective-permute-start.15 = (bf16[512,512]{1,0:T(8,128)(2,1)S(1)}, bf16[512,512]{1,0:T(8,128)(2,1)S(1)}, u32[]{:S(2)}, u32[]{:S(2)}) collective-permute-start(bf16[512,512]{1,0:T(8,128)(2,1)S(1)} %get-tuple-element.34.refs_3_), channel_id=1, source_target_pairs={{0,16},{8,24},{16,0},{24,8},{1,17},{9,25},{17,1},{25,9},{2,18},{10... | collective-permute-start | bytes 1572872 | tf_op jit(solution)/shard_map/ppermute | solution.py:353
  50.0 2.3 %collective-permute-start.16 = (bf16[512,512]{1,0:T(8,128)(2,1)S(1)}, bf16[512,512]{1,0:T(8,128)(2,1)S(1)}, u32[]{:S(2)}, u32[]{:S(2)}) collective-permute-start(bf16[512,512]{1,0:T(8,128)(2,1)S(1)} %collective-permute-done.15.refs_3_), channel_id=1, source_target_pairs={{0,8},{8,0},{16,24},{24,16},{1,9},{9,1},{17,25},{25,17},{2,10},{10... | collective-permute-start | bytes 1572872 | tf_op jit(solution)/shard_map/ppermute | solution.py:39
  55.6 6.3 %collective-permute-start.17 = (bf16[256,256]{1,0:T(8,128)(2,1)S(1)}, bf16[256,256]{1,0:T(8,128)(2,1)S(1)}, u32[]{:S(2)}, u32[]{:S(2)}) collective-permute-start(bf16[256,256]{1,0:T(8,128)(2,1)S(1)} %get-tuple-element.41), channel_id=1, source_target_pairs={{0,2},{2,4},{4,6},{6,7},{7,5},{5,3},{3,1},{1,0},{8,10},{10,12},{12... | collective-permute-start | bytes 393224 | tf_op jit(solution)/shard_map/ppermute | solution.py:33
  57.3 6.4 %collective-permute-start.21 = (bf16[256,256]{1,0:T(8,128)(2,1)S(1)}, bf16[256,256]{1,0:T(8,128)(2,1)S(1)}, u32[]{:S(2)}, u32[]{:S(2)}) collective-permute-start(bf16[256,256]{1,0:T(8,128)(2,1)S(1)} %get-tuple-element.44), channel_id=1, source_target_pairs={{0,1},{2,0},{4,2},{6,4},{7,6},{5,7},{3,5},{1,3},{8,9},{10,8},{12,1... | collective-permute-start | bytes 393224 | tf_op jit(solution)/shard_map/ppermute | solution.py:33
  57.7 7.1 %collective-permute-start.24 = (bf16[256,256]{1,0:T(8,128)(2,1)S(1)}, bf16[256,256]{1,0:T(8,128)(2,1)S(1)}, u32[]{:S(2)}, u32[]{:S(2)}) collective-permute-start(bf16[256,256]{1,0:T(8,128)(2,1)S(1)} %get-tuple-element.48), channel_id=1, source_target_pairs={{0,2},{2,4},{4,6},{6,7},{7,5},{5,3},{3,1},{1,0},{8,10},{10,12},{12... | collective-permute-start | bytes 393224 | tf_op jit(solution)/shard_map/ppermute | solution.py:33
  59.3 7.2 %collective-permute-start.27 = (bf16[256,256]{1,0:T(8,128)(2,1)S(1)}, bf16[256,256]{1,0:T(8,128)(2,1)S(1)}, u32[]{:S(2)}, u32[]{:S(2)}) collective-permute-start(bf16[256,256]{1,0:T(8,128)(2,1)S(1)} %get-tuple-element.52), channel_id=1, source_target_pairs={{0,1},{2,0},{4,2},{6,4},{7,6},{5,7},{3,5},{1,3},{8,9},{10,8},{12,1... | collective-permute-start | bytes 393224 | tf_op jit(solution)/shard_map/ppermute | solution.py:33
  62.0 5.6 %collective-permute-start.18 = (bf16[256,256]{1,0:T(8,128)(2,1)S(1)}, bf16[256,256]{1,0:T(8,128)(2,1)S(1)}, u32[]{:S(2)}, u32[]{:S(2)}) collective-permute-start(bf16[256,256]{1,0:T(8,128)(2,1)S(1)} %add_convert_fusion.11), channel_id=1, source_target_pairs={{0,2},{2,4},{4,6},{6,7},{7,5},{5,3},{3,1},{1,0},{8,10},{10,12},{12... | collective-permute-start | bytes 393224 | tf_op jit(solution)/shard_map/ppermute | solution.py:33
  63.7 5.6 %collective-permute-start.22 = (bf16[256,256]{1,0:T(8,128)(2,1)S(1)}, bf16[256,256]{1,0:T(8,128)(2,1)S(1)}, u32[]{:S(2)}, u32[]{:S(2)}) collective-permute-start(bf16[256,256]{1,0:T(8,128)(2,1)S(1)} %add_convert_fusion.8), channel_id=1, source_target_pairs={{0,1},{2,0},{4,2},{6,4},{7,6},{5,7},{3,5},{1,3},{8,9},{10,8},{12,1... | collective-permute-start | bytes 393224 | tf_op jit(solution)/shard_map/ppermute | solution.py:33
  64.8 6.5 %collective-permute-start.25 = (bf16[256,256]{1,0:T(8,128)(2,1)S(1)}, bf16[256,256]{1,0:T(8,128)(2,1)S(1)}, u32[]{:S(2)}, u32[]{:S(2)}) collective-permute-start(bf16[256,256]{1,0:T(8,128)(2,1)S(1)} %add_convert_fusion.5), channel_id=1, source_target_pairs={{0,2},{2,4},{4,6},{6,7},{7,5},{5,3},{3,1},{1,0},{8,10},{10,12},{12... | collective-permute-start | bytes 393224 | tf_op jit(solution)/shard_map/ppermute | solution.py:33
  66.5 6.5 %collective-permute-start.28 = (bf16[256,256]{1,0:T(8,128)(2,1)S(1)}, bf16[256,256]{1,0:T(8,128)(2,1)S(1)}, u32[]{:S(2)}, u32[]{:S(2)}) collective-permute-start(bf16[256,256]{1,0:T(8,128)(2,1)S(1)} %add_convert_fusion.3), channel_id=1, source_target_pairs={{0,1},{2,0},{4,2},{6,4},{7,6},{5,7},{3,5},{1,3},{8,9},{10,8},{12,1... | collective-permute-start | bytes 393224 | tf_op jit(solution)/shard_map/ppermute | solution.py:33
  67.6 6.5 %collective-permute-start.19 = (bf16[256,256]{1,0:T(8,128)(2,1)S(1)}, bf16[256,256]{1,0:T(8,128)(2,1)S(1)}, u32[]{:S(2)}, u32[]{:S(2)}) collective-permute-start(bf16[256,256]{1,0:T(8,128)(2,1)S(1)} %add_convert_fusion.10), channel_id=1, source_target_pairs={{0,2},{2,4},{4,6},{6,7},{7,5},{5,3},{3,1},{1,0},{8,10},{10,12},{12... | collective-permute-start | bytes 393224 | tf_op jit(solution)/shard_map/ppermute | solution.py:33
  69.3 9.3 %collective-permute-start.23 = (bf16[256,256]{1,0:T(8,128)(2,1)S(1)}, bf16[256,256]{1,0:T(8,128)(2,1)S(1)}, u32[]{:S(2)}, u32[]{:S(2)}) collective-permute-start(bf16[256,256]{1,0:T(8,128)(2,1)S(1)} %add_convert_fusion.7), channel_id=1, source_target_pairs={{0,1},{2,0},{4,2},{6,4},{7,6},{5,7},{3,5},{1,3},{8,9},{10,8},{12,1... | collective-permute-start | bytes 393224 | tf_op jit(solution)/shard_map/ppermute | solution.py:33
  71.3 7.9 %collective-permute-start.26 = (bf16[256,256]{1,0:T(8,128)(2,1)S(1)}, bf16[256,256]{1,0:T(8,128)(2,1)S(1)}, u32[]{:S(2)}, u32[]{:S(2)}) collective-permute-start(bf16[256,256]{1,0:T(8,128)(2,1)S(1)} %add_convert_fusion.4), channel_id=1, source_target_pairs={{0,2},{2,4},{4,6},{6,7},{7,5},{5,3},{3,1},{1,0},{8,10},{10,12},{12... | collective-permute-start | bytes 393224 | tf_op jit(solution)/shard_map/ppermute | solution.py:33
  73.0 5.0 %collective-permute-start.29 = (bf16[256,256]{1,0:T(8,128)(2,1)S(1)}, bf16[256,256]{1,0:T(8,128)(2,1)S(1)}, u32[]{:S(2)}, u32[]{:S(2)}) collective-permute-start(bf16[256,256]{1,0:T(8,128)(2,1)S(1)} %add_convert_fusion.2), channel_id=1, source_target_pairs={{0,1},{2,0},{4,2},{6,4},{7,6},{5,7},{3,5},{1,3},{8,9},{10,8},{12,1... | collective-permute-start | bytes 393224 | tf_op jit(solution)/shard_map/ppermute | solution.py:33
  74.1 5.0 %collective-permute-start.20 = (bf16[256,256]{1,0:T(8,128)(2,1)S(1)}, bf16[256,256]{1,0:T(8,128)(2,1)S(1)}, u32[]{:S(2)}, u32[]{:S(2)}) collective-permute-start(bf16[256,256]{1,0:T(8,128)(2,1)S(1)} %add_convert_fusion.9), channel_id=1, source_target_pairs={{0,2},{2,4},{4,6},{6,7},{7,5},{5,3},{3,1},{1,0},{8,10},{10,12},{12... | collective-permute-start | bytes 393224 | tf_op jit(solution)/shard_map/ppermute | solution.py:33
  78.1 5.0 %collective-permute-start.30 = (bf16[256,256]{1,0:T(8,128)(2,1)S(1)}, bf16[256,256]{1,0:T(8,128)(2,1)S(1)}, u32[]{:S(2)}, u32[]{:S(2)}) collective-permute-start(bf16[256,256]{1,0:T(8,128)(2,1)S(1)} %add_convert_fusion.1), channel_id=1, source_target_pairs={{0,1},{2,0},{4,2},{6,4},{7,6},{5,7},{3,5},{1,3},{8,9},{10,8},{12,1... | collective-permute-start | bytes 393224 | tf_op jit(solution)/shard_map/ppermute | solution.py:33

commit v8 on v7

--- a/solution.py
+++ b/solution.py
@@ -110,6 +110,7 @@
         out_specs=pl.BlockSpec(memory_space=pl.ANY),
         scratch_shapes=[pltpu.SemaphoreType.DMA((len(targets),))],
         input_output_aliases={} if wide is None else {len(blocks): 0},
+        compiler_params=pltpu.CompilerParams(vmem_limit_bytes=1 << 20),
         cost_estimate=pl.CostEstimate(flops=0, bytes_accessed=1 << 20, transcendentals=0),
         name="place",
     )(*operands)

time: 84.4 us -> 76.9 us (0.911)
  local copies, waits for them, and re-layouts: 10 us -> 2.07 us
    unnamed x12 -> x0, local copies, waits for them, and re-layouts: 7.98 us -> none
  transfers between devices with their start and end apart: 31 -> 31, of which waited for: 13 -> 16; matrix products, arithmetic and copies ran while one was open for 2% -> 2% of each run, Pallas kernels for 12% -> 13%
where the time goes in v8:
time: 76.9 us; the launch traced here: 76.5 us
  starting transfers between devices  29.7 us (39%)
  waiting for transfers between devices  27.4 us (36%)
  Pallas kernels  15.7 us (20%)
  local copies, waits for them, and re-layouts  2.07 us (3%)
  other arithmetic  1.33 us (2%)
    ppermute x28, starting transfers between devices, along(): lax.ppermute(value, 'head', [(order[p], order[(p + step) % count]) for p...  29.1 us
    ppermute x28, waiting for transfers between devices, along(): lax.ppermute(value, 'head', [(order[p], order[(p + step) % count]) for p...  17.9 us
    ppermute x1, waiting for transfers between devices, body(): lax.ppermute(kv, 'seq', [(2 * a + b, 2 * ((a + step) % outer) + b) for a...  9.13 us
    pallas_call x3, Pallas kernels, attend(): pl.pallas_call(functools.partial(attend_kernel, len(queries), len(kvs), h...  8.71 us
    pallas_call x1, Pallas kernels, fold_gain(): pl.pallas_call(functools.partial(fold_kernel, order), out_shape=pltpu.VME...  3.01 us
    pallas_call x1, Pallas kernels, project(): pl.pallas_call(functools.partial(project_kernel, head_size), out_shape=(p...  2.8 us
  transfers between devices with their start and end apart: 31, of which 16 were waited for; matrix products, arithmetic and copies ran while one was open for 2% of the time, Pallas kernels for 13%

profile of v8, /device:TPU:10, one launch (start us, length us, event | category | flops | bytes accessed | tf_op | source)
XLA Modules:
  0.0 76.5 jit_solution(18344374671041906701)
XLA Ops:
  0.0 1.0 %fusion = (bf16[256,256]{1,0:T(8,128)(2,1)S(1)}, bf16[256,256]{1,0:T(8,128)(2,1)S(1)}) fusion(bf16[512,256]{1,0:T(8,128)(2,1)} %refs_0_.1), kind=kLoop, calls=%fused_computation.15 | loop fusion | bytes 524288 | tf_op jit(solution)/shard_map/slice | solution.py:320
  1.0 0.5 collective-permute-start.9
  1.5 1.6 %collective-permute-start = (bf16[256,256]{1,0:T(8,128)(2,1)S(1)}, bf16[256,256]{1,0:T(8,128)(2,1)S(1)}, u32[]{:S(2)}, u32[]{:S(2)}) collective-permute-start(bf16[256,256]{1,0:T(8,128)(2,1)S(1)} %get-tuple-element.54), channel_id=1, source_target_pairs={{0,2},{2,4},{4,6},{6,7},{7,5},{5,3},{3,1},{1,0},{8,10},{10,12},{12... | collective-permute-start | bytes 393224 | tf_op jit(solution)/shard_map/ppermute | solution.py:33
  3.1 0.4 collective-permute-start.3
  3.5 1.6 %collective-permute-start.6 = (bf16[256,256]{1,0:T(8,128)(2,1)S(1)}, bf16[256,256]{1,0:T(8,128)(2,1)S(1)}, u32[]{:S(2)}, u32[]{:S(2)}) collective-permute-start(bf16[256,256]{1,0:T(8,128)(2,1)S(1)} %get-tuple-element.53), channel_id=1, source_target_pairs={{0,2},{2,4},{4,6},{6,7},{7,5},{5,3},{3,1},{1,0},{8,10},{10,12},{12... | collective-permute-start | bytes 393224 | tf_op jit(solution)/shard_map/ppermute | solution.py:33
  5.2 3.0 %fold_gain.1.w_ref = bf16[3,2048,256]{2,1,0:T(8,128)(2,1)S(1)} custom-call(s32[8]{0:T(128)S(1)} %stack.80.at, f32[16,128]{1,0:T(8,128)} %bitcast.19, bf16[3,2048,256]{2,1,0:T(8,128)(2,1)} %w_hbm.1), custom_call_target="tpu_custom_call" | custom-call | flops 1572864 | bytes 6291456 | tf_op jit(solution)/shard_map/fold_gain/pallas_call | solution.py:77
  8.2 0.5 collective-permute-start.10
  8.7 1.6 %collective-permute-start.1 = (bf16[256,256]{1,0:T(8,128)(2,1)S(1)}, bf16[256,256]{1,0:T(8,128)(2,1)S(1)}, u32[]{:S(2)}, u32[]{:S(2)}) collective-permute-start(bf16[256,256]{1,0:T(8,128)(2,1)S(1)} %collective-permute-done.refs_1_), channel_id=1, source_target_pairs={{0,2},{2,4},{4,6},{6,7},{7,5},{5,3},{3,1},{1,0},{8,10},{10,12},{12... | collective-permute-start | bytes 393224 | tf_op jit(solution)/shard_map/ppermute | solution.py:33
  10.3 0.5 collective-permute-start.4
  10.7 1.6 %collective-permute-start.7 = (bf16[256,256]{1,0:T(8,128)(2,1)S(1)}, bf16[256,256]{1,0:T(8,128)(2,1)S(1)}, u32[]{:S(2)}, u32[]{:S(2)}) collective-permute-start(bf16[256,256]{1,0:T(8,128)(2,1)S(1)} %collective-permute-done.6.refs_3_), channel_id=1, source_target_pairs={{0,2},{2,4},{4,6},{6,7},{7,5},{5,3},{3,1},{1,0},{8,10},{10,12},{12... | collective-permute-start | bytes 393224 | tf_op jit(solution)/shard_map/ppermute | solution.py:33
  12.3 1.9 %collective-permute-done.10.refs_3_ = bf16[256,256]{1,0:T(8,128)(2,1)S(1)} collective-permute-done((bf16[256,256]{1,0:T(8,128)(2,1)S(1)}, bf16[256,256]{1,0:T(8,128)(2,1)S(1)}, u32[]{:S(2)}, u32[]{:S(2)}) %collective-permute-start.10) | collective-permute-done | bytes 131104 | tf_op jit(solution)/shard_map/ppermute | solution.py:33
  14.7 1.6 %collective-permute-start.2 = (bf16[256,256]{1,0:T(8,128)(2,1)S(1)}, bf16[256,256]{1,0:T(8,128)(2,1)S(1)}, u32[]{:S(2)}, u32[]{:S(2)}) collective-permute-start(bf16[256,256]{1,0:T(8,128)(2,1)S(1)} %collective-permute-done.1.refs_0_), channel_id=1, source_target_pairs={{0,2},{2,4},{4,6},{6,7},{7,5},{5,3},{3,1},{1,0},{8,10},{10,12},{12... | collective-permute-start | bytes 393224 | tf_op jit(solution)/shard_map/ppermute | solution.py:33
  16.3 1.0 %place.3.refs_4_ = bf16[512,2048]{1,0:T(8,128)(2,1)S(1)} custom-call(bf16[512,256]{1,0:T(8,128)(2,1)} %refs_0_.1, bf16[256,256]{1,0:T(8,128)(2,1)S(1)} %collective-permute-done.refs_1_, bf16[256,256]{1,0:T(8,128)(2,1)S(1)} %collective-permute-done.3.refs_2_, bf16[256,256]{1,0:T(8,128)(2,1)S(1)} %collective-permute-done.6.refs_3_, ...), custom_call_target="tpu_custom_call" | custom-call | bytes 1048576 | tf_op jit(solution)/shard_map/place/pallas_call | solution.py:106
  17.3 0.5 collective-permute-start.5
  17.8 1.6 %collective-permute-start.8 = (bf16[256,256]{1,0:T(8,128)(2,1)S(1)}, bf16[256,256]{1,0:T(8,128)(2,1)S(1)}, u32[]{:S(2)}, u32[]{:S(2)}) collective-permute-start(bf16[256,256]{1,0:T(8,128)(2,1)S(1)} %collective-permute-done.7.refs_2_), channel_id=1, source_target_pairs={{0,2},{2,4},{4,6},{6,7},{7,5},{5,3},{3,1},{1,0},{8,10},{10,12},{12... | collective-permute-start | bytes 393224 | tf_op jit(solution)/shard_map/ppermute | solution.py:33
  19.5 0.5 collective-permute-done.11.refs_3_
  20.4 1.6 %collective-permute-start.12 = (bf16[256,256]{1,0:T(8,128)(2,1)S(1)}, bf16[256,256]{1,0:T(8,128)(2,1)S(1)}, u32[]{:S(2)}, u32[]{:S(2)}) collective-permute-start(bf16[256,256]{1,0:T(8,128)(2,1)S(1)} %collective-permute-done.2.refs_0_), channel_id=1, source_target_pairs={{0,2},{2,4},{4,6},{6,7},{7,5},{5,3},{3,1},{1,0},{8,10},{10,12},{12... | collective-permute-start | bytes 393224 | tf_op jit(solution)/shard_map/ppermute | solution.py:33
  22.3 0.5 collective-permute-done.8.refs_2_
  22.9 2.0 %collective-permute-done.13.refs_1_ = bf16[256,256]{1,0:T(8,128)(2,1)S(1)} collective-permute-done((bf16[256,256]{1,0:T(8,128)(2,1)S(1)}, bf16[256,256]{1,0:T(8,128)(2,1)S(1)}, u32[]{:S(2)}, u32[]{:S(2)}) %collective-permute-start.13) | collective-permute-done | bytes 131104 | tf_op jit(solution)/shard_map/ppermute | solution.py:33
  24.9 0.5 collective-permute-done.12.refs_0_
  25.4 2.8 %project.1 = (bf16[512,256]{1,0:T(8,128)(2,1)S(1)}, bf16[512,512]{1,0:T(8,128)(2,1)S(1)}) custom-call(f32[2]{0:T(128)} %factor.1, bf16[512,2048]{1,0:T(8,128)(2,1)S(1)} %place.5.wide, bf16[3,2048,256]{2,1,0:T(8,128)(2,1)S(1)} %fold_gain.1.w_ref, bf16[256,256]{1,0:T(8,128)(2,1)S(1)} %collective-permute-done.12.refs_0_, ...), custom_call_target="tpu_custom_call" | custom-call | flops 1610612736 | bytes 5242880 | tf_op jit(solution)/shard_map/project/pallas_call | solution.py:153
  28.2 0.5 collective-permute-start.15
  28.8 0.8 dynamic_slice.3
  30.1 3.3 %attend.2.refs_4_ = f32[512,512]{1,0:T(8,128)S(1)} custom-call(s32[3]{0:T(128)S(1)} %pad_add_fusion.info, s32[2048]{0:T(1024)} %ids.5, bf16[512,256]{1,0:T(8,128)(2,1)S(1)} %get-tuple-element.33.refs_0_, s32[512,1]{1,0:T(8,128)S(1)} %copy.11.refs_1_, s32[4,1,512]{2,1,0:T(1,128)} %bitcast.16, bf16[512,512]{1,0:T(8,128)(2,1)S(1)} %get-tuple-element.34.refs_3_, ...), custom_call_target="tpu_custom_call" | custom-call | flops 805306368 | bytes 2097152 | tf_op jit(solution)/shard_map/attend/pallas_call | solution.py:276
  33.5 9.1 %collective-permute-done.15.refs_3_ = bf16[512,512]{1,0:T(8,128)(2,1)S(1)} collective-permute-done((bf16[512,512]{1,0:T(8,128)(2,1)S(1)}, bf16[512,512]{1,0:T(8,128)(2,1)S(1)}, u32[]{:S(2)}, u32[]{:S(2)}) %collective-permute-start.15) | collective-permute-done | bytes 524320 | tf_op jit(solution)/shard_map/ppermute | solution.py:354
  42.8 2.1 %attend.3.refs_4_ = f32[512,512]{1,0:T(8,128)S(1)} custom-call(s32[2]{0:T(128)S(1)} %pad_add_fusion.1.info, s32[2048]{0:T(1024)} %ids.5, bf16[512,256]{1,0:T(8,128)(2,1)S(1)} %get-tuple-element.33.refs_0_, s32[512,1]{1,0:T(8,128)S(1)} %copy.11.refs_1_, s32[4,1,512]{2,1,0:T(1,128)} %bitcast.17, bf16[512,512]{1,0:T(8,128)(2,1)S(1)} %collective-permute-done.15.refs_3_, ...), custom_call_target="tpu_custom_call" | custom-call | flops 402653184 | bytes 1572864 | tf_op jit(solution)/shard_map/attend/pallas_call | solution.py:276
  44.9 3.3 %attend_last.1 = (bf16[256,256]{1,0:T(8,128)(2,1)S(1)}, bf16[256,256]{1,0:T(8,128)(2,1)S(1)}, bf16[256,256]{1,0:T(8,128)(2,1)S(1)}, bf16[256,256]{1,0:T(8,128)(2...) custom-call(s32[18]{0:T(128)S(1)} %stack.79.info, ...), custom_call_target="tpu_custom_call" | custom-call | flops 1476395008 | bytes 1572864 | tf_op jit(solution)/shard_map/attend_last/pallas_call | solution.py:276
  48.2 1.6 %collective-permute-start.17 = (bf16[256,256]{1,0:T(8,128)(2,1)S(1)}, bf16[256,256]{1,0:T(8,128)(2,1)S(1)}, u32[]{:S(2)}, u32[]{:S(2)}) collective-permute-start(bf16[256,256]{1,0:T(8,128)(2,1)S(1)} %get-tuple-element.41), channel_id=1, source_target_pairs={{0,2},{2,4},{4,6},{6,7},{7,5},{5,3},{3,1},{1,0},{8,10},{10,12},{12... | collective-permute-start | bytes 393224 | tf_op jit(solution)/shard_map/ppermute | solution.py:33
  50.3 1.6 %collective-permute-start.24 = (bf16[256,256]{1,0:T(8,128)(2,1)S(1)}, bf16[256,256]{1,0:T(8,128)(2,1)S(1)}, u32[]{:S(2)}, u32[]{:S(2)}) collective-permute-start(bf16[256,256]{1,0:T(8,128)(2,1)S(1)} %get-tuple-element.48), channel_id=1, source_target_pairs={{0,2},{2,4},{4,6},{6,7},{7,5},{5,3},{3,1},{1,0},{8,10},{10,12},{12... | collective-permute-start | bytes 393224 | tf_op jit(solution)/shard_map/ppermute | solution.py:33
  52.3 2.2 %collective-permute-done.17 = bf16[256,256]{1,0:T(8,128)(2,1)S(1)} collective-permute-done((bf16[256,256]{1,0:T(8,128)(2,1)S(1)}, bf16[256,256]{1,0:T(8,128)(2,1)S(1)}, u32[]{:S(2)}, u32[]{:S(2)}) %collective-permute-start.17) | collective-permute-done | bytes 131104 | tf_op jit(solution)/shard_map/ppermute | solution.py:33
  54.6 1.6 %collective-permute-start.18 = (bf16[256,256]{1,0:T(8,128)(2,1)S(1)}, bf16[256,256]{1,0:T(8,128)(2,1)S(1)}, u32[]{:S(2)}, u32[]{:S(2)}) collective-permute-start(bf16[256,256]{1,0:T(8,128)(2,1)S(1)} %add_convert_fusion.11), channel_id=1, source_target_pairs={{0,2},{2,4},{4,6},{6,7},{7,5},{5,3},{3,1},{1,0},{8,10},{10,12},{12... | collective-permute-start | bytes 393224 | tf_op jit(solution)/shard_map/ppermute | solution.py:33
  56.3 0.5 collective-permute-start.22
  56.8 0.6 collective-permute-done.24
  57.4 1.6 %collective-permute-start.25 = (bf16[256,256]{1,0:T(8,128)(2,1)S(1)}, bf16[256,256]{1,0:T(8,128)(2,1)S(1)}, u32[]{:S(2)}, u32[]{:S(2)}) collective-permute-start(bf16[256,256]{1,0:T(8,128)(2,1)S(1)} %add_convert_fusion.5), channel_id=1, source_target_pairs={{0,2},{2,4},{4,6},{6,7},{7,5},{5,3},{3,1},{1,0},{8,10},{10,12},{12... | collective-permute-start | bytes 393224 | tf_op jit(solution)/shard_map/ppermute | solution.py:33
  59.1 0.5 collective-permute-start.28
  59.6 0.6 collective-permute-done.18
  60.2 1.6 %collective-permute-start.19 = (bf16[256,256]{1,0:T(8,128)(2,1)S(1)}, bf16[256,256]{1,0:T(8,128)(2,1)S(1)}, u32[]{:S(2)}, u32[]{:S(2)}) collective-permute-start(bf16[256,256]{1,0:T(8,128)(2,1)S(1)} %add_convert_fusion.10), channel_id=1, source_target_pairs={{0,2},{2,4},{4,6},{6,7},{7,5},{5,3},{3,1},{1,0},{8,10},{10,12},{12... | collective-permute-start | bytes 393224 | tf_op jit(solution)/shard_map/ppermute | solution.py:33
  61.9 0.5 collective-permute-start.23
  62.4 1.5 %collective-permute-done.25 = bf16[256,256]{1,0:T(8,128)(2,1)S(1)} collective-permute-done((bf16[256,256]{1,0:T(8,128)(2,1)S(1)}, bf16[256,256]{1,0:T(8,128)(2,1)S(1)}, u32[]{:S(2)}, u32[]{:S(2)}) %collective-permute-start.25) | collective-permute-done | bytes 131104 | tf_op jit(solution)/shard_map/ppermute | solution.py:33
  63.9 1.6 %collective-permute-start.26 = (bf16[256,256]{1,0:T(8,128)(2,1)S(1)}, bf16[256,256]{1,0:T(8,128)(2,1)S(1)}, u32[]{:S(2)}, u32[]{:S(2)}) collective-permute-start(bf16[256,256]{1,0:T(8,128)(2,1)S(1)} %add_convert_fusion.4), channel_id=1, source_target_pairs={{0,2},{2,4},{4,6},{6,7},{7,5},{5,3},{3,1},{1,0},{8,10},{10,12},{12... | collective-permute-start | bytes 393224 | tf_op jit(solution)/shard_map/ppermute | solution.py:33
  65.6 0.5 collective-permute-start.29
  66.1 0.6 collective-permute-done.19
  66.7 1.6 %collective-permute-start.20 = (bf16[256,256]{1,0:T(8,128)(2,1)S(1)}, bf16[256,256]{1,0:T(8,128)(2,1)S(1)}, u32[]{:S(2)}, u32[]{:S(2)}) collective-permute-start(bf16[256,256]{1,0:T(8,128)(2,1)S(1)} %add_convert_fusion.9), channel_id=1, source_target_pairs={{0,2},{2,4},{4,6},{6,7},{7,5},{5,3},{3,1},{1,0},{8,10},{10,12},{12... | collective-permute-start | bytes 393224 | tf_op jit(solution)/shard_map/ppermute | solution.py:33
  68.4 2.3 %collective-permute-done.29 = bf16[256,256]{1,0:T(8,128)(2,1)S(1)} collective-permute-done((bf16[256,256]{1,0:T(8,128)(2,1)S(1)}, bf16[256,256]{1,0:T(8,128)(2,1)S(1)}, u32[]{:S(2)}, u32[]{:S(2)}) %collective-permute-start.29) | collective-permute-done | bytes 131104 | tf_op jit(solution)/shard_map/ppermute | solution.py:33
  70.7 0.5 collective-permute-start.30
  71.2 0.6 collective-permute-done.20
  71.8 3.9 %collective-permute-done.30 = bf16[256,256]{1,0:T(8,128)(2,1)S(1)} collective-permute-done((bf16[256,256]{1,0:T(8,128)(2,1)S(1)}, bf16[256,256]{1,0:T(8,128)(2,1)S(1)}, u32[]{:S(2)}, u32[]{:S(2)}) %collective-permute-start.30) | collective-permute-done | bytes 131104 | tf_op jit(solution)/shard_map/ppermute | solution.py:33
  75.7 0.7 pad_maximum_fusion
  (42 shorter events, 3.8 us)
Async XLA Ops:
  1.0 7.2 %collective-permute-start.9 = (bf16[256,256]{1,0:T(8,128)(2,1)S(1)}, bf16[256,256]{1,0:T(8,128)(2,1)S(1)}, u32[]{:S(2)}, u32[]{:S(2)}) collective-permute-start(bf16[256,256]{1,0:T(8,128)(2,1)S(1)} %get-tuple-element.53), channel_id=1, source_target_pairs={{0,1},{2,0},{4,2},{6,4},{7,6},{5,7},{3,5},{1,3},{8,9},{10,8},{12,1... | collective-permute-start | bytes 393224 | tf_op jit(solution)/shard_map/ppermute | solution.py:33
  1.5 7.2 %collective-permute-start = (bf16[256,256]{1,0:T(8,128)(2,1)S(1)}, bf16[256,256]{1,0:T(8,128)(2,1)S(1)}, u32[]{:S(2)}, u32[]{:S(2)}) collective-permute-start(bf16[256,256]{1,0:T(8,128)(2,1)S(1)} %get-tuple-element.54), channel_id=1, source_target_pairs={{0,2},{2,4},{4,6},{6,7},{7,5},{5,3},{3,1},{1,0},{8,10},{10,12},{12... | collective-permute-start | bytes 393224 | tf_op jit(solution)/shard_map/ppermute | solution.py:33
  3.1 7.2 %collective-permute-start.3 = (bf16[256,256]{1,0:T(8,128)(2,1)S(1)}, bf16[256,256]{1,0:T(8,128)(2,1)S(1)}, u32[]{:S(2)}, u32[]{:S(2)}) collective-permute-start(bf16[256,256]{1,0:T(8,128)(2,1)S(1)} %get-tuple-element.54), channel_id=1, source_target_pairs={{0,1},{2,0},{4,2},{6,4},{7,6},{5,7},{3,5},{1,3},{8,9},{10,8},{12,1... | collective-permute-start | bytes 393224 | tf_op jit(solution)/shard_map/ppermute | solution.py:33
  3.5 7.2 %collective-permute-start.6 = (bf16[256,256]{1,0:T(8,128)(2,1)S(1)}, bf16[256,256]{1,0:T(8,128)(2,1)S(1)}, u32[]{:S(2)}, u32[]{:S(2)}) collective-permute-start(bf16[256,256]{1,0:T(8,128)(2,1)S(1)} %get-tuple-element.53), channel_id=1, source_target_pairs={{0,2},{2,4},{4,6},{6,7},{7,5},{5,3},{3,1},{1,0},{8,10},{10,12},{12... | collective-permute-start | bytes 393224 | tf_op jit(solution)/shard_map/ppermute | solution.py:33
  8.2 6.0 %collective-permute-start.10 = (bf16[256,256]{1,0:T(8,128)(2,1)S(1)}, bf16[256,256]{1,0:T(8,128)(2,1)S(1)}, u32[]{:S(2)}, u32[]{:S(2)}) collective-permute-start(bf16[256,256]{1,0:T(8,128)(2,1)S(1)} %collective-permute-done.9.refs_4_), channel_id=1, source_target_pairs={{0,1},{2,0},{4,2},{6,4},{7,6},{5,7},{3,5},{1,3},{8,9},{10,8},{12,1... | collective-permute-start | bytes 393224 | tf_op jit(solution)/shard_map/ppermute | solution.py:33
  8.7 6.0 %collective-permute-start.1 = (bf16[256,256]{1,0:T(8,128)(2,1)S(1)}, bf16[256,256]{1,0:T(8,128)(2,1)S(1)}, u32[]{:S(2)}, u32[]{:S(2)}) collective-permute-start(bf16[256,256]{1,0:T(8,128)(2,1)S(1)} %collective-permute-done.refs_1_), channel_id=1, source_target_pairs={{0,2},{2,4},{4,6},{6,7},{7,5},{5,3},{3,1},{1,0},{8,10},{10,12},{12... | collective-permute-start | bytes 393224 | tf_op jit(solution)/shard_map/ppermute | solution.py:33
  10.3 7.0 %collective-permute-start.4 = (bf16[256,256]{1,0:T(8,128)(2,1)S(1)}, bf16[256,256]{1,0:T(8,128)(2,1)S(1)}, u32[]{:S(2)}, u32[]{:S(2)}) collective-permute-start(bf16[256,256]{1,0:T(8,128)(2,1)S(1)} %collective-permute-done.3.refs_2_), channel_id=1, source_target_pairs={{0,1},{2,0},{4,2},{6,4},{7,6},{5,7},{3,5},{1,3},{8,9},{10,8},{12,1... | collective-permute-start | bytes 393224 | tf_op jit(solution)/shard_map/ppermute | solution.py:33
  10.7 7.1 %collective-permute-start.7 = (bf16[256,256]{1,0:T(8,128)(2,1)S(1)}, bf16[256,256]{1,0:T(8,128)(2,1)S(1)}, u32[]{:S(2)}, u32[]{:S(2)}) collective-permute-start(bf16[256,256]{1,0:T(8,128)(2,1)S(1)} %collective-permute-done.6.refs_3_), channel_id=1, source_target_pairs={{0,2},{2,4},{4,6},{6,7},{7,5},{5,3},{3,1},{1,0},{8,10},{10,12},{12... | collective-permute-start | bytes 393224 | tf_op jit(solution)/shard_map/ppermute | solution.py:33
  14.2 5.7 %collective-permute-start.11 = (bf16[256,256]{1,0:T(8,128)(2,1)S(1)}, bf16[256,256]{1,0:T(8,128)(2,1)S(1)}, u32[]{:S(2)}, u32[]{:S(2)}) collective-permute-start(bf16[256,256]{1,0:T(8,128)(2,1)S(1)} %collective-permute-done.10.refs_3_), channel_id=1, source_target_pairs={{0,1},{2,0},{4,2},{6,4},{7,6},{5,7},{3,5},{1,3},{8,9},{10,8},{12,1... | collective-permute-start | bytes 393224 | tf_op jit(solution)/shard_map/ppermute | solution.py:33
  14.7 5.7 %collective-permute-start.2 = (bf16[256,256]{1,0:T(8,128)(2,1)S(1)}, bf16[256,256]{1,0:T(8,128)(2,1)S(1)}, u32[]{:S(2)}, u32[]{:S(2)}) collective-permute-start(bf16[256,256]{1,0:T(8,128)(2,1)S(1)} %collective-permute-done.1.refs_0_), channel_id=1, source_target_pairs={{0,2},{2,4},{4,6},{6,7},{7,5},{5,3},{3,1},{1,0},{8,10},{10,12},{12... | collective-permute-start | bytes 393224 | tf_op jit(solution)/shard_map/ppermute | solution.py:33
  17.3 5.0 %collective-permute-start.5 = (bf16[256,256]{1,0:T(8,128)(2,1)S(1)}, bf16[256,256]{1,0:T(8,128)(2,1)S(1)}, u32[]{:S(2)}, u32[]{:S(2)}) collective-permute-start(bf16[256,256]{1,0:T(8,128)(2,1)S(1)} %collective-permute-done.4.refs_1_), channel_id=1, source_target_pairs={{0,1},{2,0},{4,2},{6,4},{7,6},{5,7},{3,5},{1,3},{8,9},{10,8},{12,1... | collective-permute-start | bytes 393224 | tf_op jit(solution)/shard_map/ppermute | solution.py:33
  17.8 5.0 %collective-permute-start.8 = (bf16[256,256]{1,0:T(8,128)(2,1)S(1)}, bf16[256,256]{1,0:T(8,128)(2,1)S(1)}, u32[]{:S(2)}, u32[]{:S(2)}) collective-permute-start(bf16[256,256]{1,0:T(8,128)(2,1)S(1)} %collective-permute-done.7.refs_2_), channel_id=1, source_target_pairs={{0,2},{2,4},{4,6},{6,7},{7,5},{5,3},{3,1},{1,0},{8,10},{10,12},{12... | collective-permute-start | bytes 393224 | tf_op jit(solution)/shard_map/ppermute | solution.py:33
  19.9 5.0 %collective-permute-start.13 = (bf16[256,256]{1,0:T(8,128)(2,1)S(1)}, bf16[256,256]{1,0:T(8,128)(2,1)S(1)}, u32[]{:S(2)}, u32[]{:S(2)}) collective-permute-start(bf16[256,256]{1,0:T(8,128)(2,1)S(1)} %collective-permute-done.11.refs_3_), channel_id=1, source_target_pairs={{0,1},{2,0},{4,2},{6,4},{7,6},{5,7},{3,5},{1,3},{8,9},{10,8},{12,1... | collective-permute-start | bytes 393224 | tf_op jit(solution)/shard_map/ppermute | solution.py:33
  20.4 5.0 %collective-permute-start.12 = (bf16[256,256]{1,0:T(8,128)(2,1)S(1)}, bf16[256,256]{1,0:T(8,128)(2,1)S(1)}, u32[]{:S(2)}, u32[]{:S(2)}) collective-permute-start(bf16[256,256]{1,0:T(8,128)(2,1)S(1)} %collective-permute-done.2.refs_0_), channel_id=1, source_target_pairs={{0,2},{2,4},{4,6},{6,7},{7,5},{5,3},{3,1},{1,0},{8,10},{10,12},{12... | collective-permute-start | bytes 393224 | tf_op jit(solution)/shard_map/ppermute | solution.py:33
  28.2 2.0 %collective-permute-start.14 = (bf16[512,512]{1,0:T(8,128)(2,1)S(1)}, bf16[512,512]{1,0:T(8,128)(2,1)S(1)}, u32[]{:S(2)}, u32[]{:S(2)}) collective-permute-start(bf16[512,512]{1,0:T(8,128)(2,1)S(1)} %get-tuple-element.34.refs_3_), channel_id=1, source_target_pairs={{0,8},{8,0},{16,24},{24,16},{1,9},{9,1},{17,25},{25,17},{2,10},{10... | collective-permute-start | bytes 1572872 | tf_op jit(solution)/shard_map/ppermute | solution.py:39
  28.2 14.3 %collective-permute-start.15 = (bf16[512,512]{1,0:T(8,128)(2,1)S(1)}, bf16[512,512]{1,0:T(8,128)(2,1)S(1)}, u32[]{:S(2)}, u32[]{:S(2)}) collective-permute-start(bf16[512,512]{1,0:T(8,128)(2,1)S(1)} %get-tuple-element.34.refs_3_), channel_id=1, source_target_pairs={{0,16},{8,24},{16,0},{24,8},{1,17},{9,25},{17,1},{25,9},{2,18},{10... | collective-permute-start | bytes 1572872 | tf_op jit(solution)/shard_map/ppermute | solution.py:354
  42.6 2.3 %collective-permute-start.16 = (bf16[512,512]{1,0:T(8,128)(2,1)S(1)}, bf16[512,512]{1,0:T(8,128)(2,1)S(1)}, u32[]{:S(2)}, u32[]{:S(2)}) collective-permute-start(bf16[512,512]{1,0:T(8,128)(2,1)S(1)} %collective-permute-done.15.refs_3_), channel_id=1, source_target_pairs={{0,8},{8,0},{16,24},{24,16},{1,9},{9,1},{17,25},{25,17},{2,10},{10... | collective-permute-start | bytes 1572872 | tf_op jit(solution)/shard_map/ppermute | solution.py:39
  48.2 6.3 %collective-permute-start.17 = (bf16[256,256]{1,0:T(8,128)(2,1)S(1)}, bf16[256,256]{1,0:T(8,128)(2,1)S(1)}, u32[]{:S(2)}, u32[]{:S(2)}) collective-permute-start(bf16[256,256]{1,0:T(8,128)(2,1)S(1)} %get-tuple-element.41), channel_id=1, source_target_pairs={{0,2},{2,4},{4,6},{6,7},{7,5},{5,3},{3,1},{1,0},{8,10},{10,12},{12... | collective-permute-start | bytes 393224 | tf_op jit(solution)/shard_map/ppermute | solution.py:33
  49.8 6.4 %collective-permute-start.21 = (bf16[256,256]{1,0:T(8,128)(2,1)S(1)}, bf16[256,256]{1,0:T(8,128)(2,1)S(1)}, u32[]{:S(2)}, u32[]{:S(2)}) collective-permute-start(bf16[256,256]{1,0:T(8,128)(2,1)S(1)} %get-tuple-element.44), channel_id=1, source_target_pairs={{0,1},{2,0},{4,2},{6,4},{7,6},{5,7},{3,5},{1,3},{8,9},{10,8},{12,1... | collective-permute-start | bytes 393224 | tf_op jit(solution)/shard_map/ppermute | solution.py:33
  50.3 7.1 %collective-permute-start.24 = (bf16[256,256]{1,0:T(8,128)(2,1)S(1)}, bf16[256,256]{1,0:T(8,128)(2,1)S(1)}, u32[]{:S(2)}, u32[]{:S(2)}) collective-permute-start(bf16[256,256]{1,0:T(8,128)(2,1)S(1)} %get-tuple-element.48), channel_id=1, source_target_pairs={{0,2},{2,4},{4,6},{6,7},{7,5},{5,3},{3,1},{1,0},{8,10},{10,12},{12... | collective-permute-start | bytes 393224 | tf_op jit(solution)/shard_map/ppermute | solution.py:33
  51.9 7.2 %collective-permute-start.27 = (bf16[256,256]{1,0:T(8,128)(2,1)S(1)}, bf16[256,256]{1,0:T(8,128)(2,1)S(1)}, u32[]{:S(2)}, u32[]{:S(2)}) collective-permute-start(bf16[256,256]{1,0:T(8,128)(2,1)S(1)} %get-tuple-element.52), channel_id=1, source_target_pairs={{0,1},{2,0},{4,2},{6,4},{7,6},{5,7},{3,5},{1,3},{8,9},{10,8},{12,1... | collective-permute-start | bytes 393224 | tf_op jit(solution)/shard_map/ppermute | solution.py:33
  54.6 5.6 %collective-permute-start.18 = (bf16[256,256]{1,0:T(8,128)(2,1)S(1)}, bf16[256,256]{1,0:T(8,128)(2,1)S(1)}, u32[]{:S(2)}, u32[]{:S(2)}) collective-permute-start(bf16[256,256]{1,0:T(8,128)(2,1)S(1)} %add_convert_fusion.11), channel_id=1, source_target_pairs={{0,2},{2,4},{4,6},{6,7},{7,5},{5,3},{3,1},{1,0},{8,10},{10,12},{12... | collective-permute-start | bytes 393224 | tf_op jit(solution)/shard_map/ppermute | solution.py:33
  56.3 5.6 %collective-permute-start.22 = (bf16[256,256]{1,0:T(8,128)(2,1)S(1)}, bf16[256,256]{1,0:T(8,128)(2,1)S(1)}, u32[]{:S(2)}, u32[]{:S(2)}) collective-permute-start(bf16[256,256]{1,0:T(8,128)(2,1)S(1)} %add_convert_fusion.8), channel_id=1, source_target_pairs={{0,1},{2,0},{4,2},{6,4},{7,6},{5,7},{3,5},{1,3},{8,9},{10,8},{12,1... | collective-permute-start | bytes 393224 | tf_op jit(solution)/shard_map/ppermute | solution.py:33
  57.4 6.5 %collective-permute-start.25 = (bf16[256,256]{1,0:T(8,128)(2,1)S(1)}, bf16[256,256]{1,0:T(8,128)(2,1)S(1)}, u32[]{:S(2)}, u32[]{:S(2)}) collective-permute-start(bf16[256,256]{1,0:T(8,128)(2,1)S(1)} %add_convert_fusion.5), channel_id=1, source_target_pairs={{0,2},{2,4},{4,6},{6,7},{7,5},{5,3},{3,1},{1,0},{8,10},{10,12},{12... | collective-permute-start | bytes 393224 | tf_op jit(solution)/shard_map/ppermute | solution.py:33
  59.1 6.5 %collective-permute-start.28 = (bf16[256,256]{1,0:T(8,128)(2,1)S(1)}, bf16[256,256]{1,0:T(8,128)(2,1)S(1)}, u32[]{:S(2)}, u32[]{:S(2)}) collective-permute-start(bf16[256,256]{1,0:T(8,128)(2,1)S(1)} %add_convert_fusion.3), channel_id=1, source_target_pairs={{0,1},{2,0},{4,2},{6,4},{7,6},{5,7},{3,5},{1,3},{8,9},{10,8},{12,1... | collective-permute-start | bytes 393224 | tf_op jit(solution)/shard_map/ppermute | solution.py:33
  60.2 6.5 %collective-permute-start.19 = (bf16[256,256]{1,0:T(8,128)(2,1)S(1)}, bf16[256,256]{1,0:T(8,128)(2,1)S(1)}, u32[]{:S(2)}, u32[]{:S(2)}) collective-permute-start(bf16[256,256]{1,0:T(8,128)(2,1)S(1)} %add_convert_fusion.10), channel_id=1, source_target_pairs={{0,2},{2,4},{4,6},{6,7},{7,5},{5,3},{3,1},{1,0},{8,10},{10,12},{12... | collective-permute-start | bytes 393224 | tf_op jit(solution)/shard_map/ppermute | solution.py:33
  61.9 9.3 %collective-permute-start.23 = (bf16[256,256]{1,0:T(8,128)(2,1)S(1)}, bf16[256,256]{1,0:T(8,128)(2,1)S(1)}, u32[]{:S(2)}, u32[]{:S(2)}) collective-permute-start(bf16[256,256]{1,0:T(8,128)(2,1)S(1)} %add_convert_fusion.7), channel_id=1, source_target_pairs={{0,1},{2,0},{4,2},{6,4},{7,6},{5,7},{3,5},{1,3},{8,9},{10,8},{12,1... | collective-permute-start | bytes 393224 | tf_op jit(solution)/shard_map/ppermute | solution.py:33
  63.9 7.9 %collective-permute-start.26 = (bf16[256,256]{1,0:T(8,128)(2,1)S(1)}, bf16[256,256]{1,0:T(8,128)(2,1)S(1)}, u32[]{:S(2)}, u32[]{:S(2)}) collective-permute-start(bf16[256,256]{1,0:T(8,128)(2,1)S(1)} %add_convert_fusion.4), channel_id=1, source_target_pairs={{0,2},{2,4},{4,6},{6,7},{7,5},{5,3},{3,1},{1,0},{8,10},{10,12},{12... | collective-permute-start | bytes 393224 | tf_op jit(solution)/shard_map/ppermute | solution.py:33
  65.6 5.0 %collective-permute-start.29 = (bf16[256,256]{1,0:T(8,128)(2,1)S(1)}, bf16[256,256]{1,0:T(8,128)(2,1)S(1)}, u32[]{:S(2)}, u32[]{:S(2)}) collective-permute-start(bf16[256,256]{1,0:T(8,128)(2,1)S(1)} %add_convert_fusion.2), channel_id=1, source_target_pairs={{0,1},{2,0},{4,2},{6,4},{7,6},{5,7},{3,5},{1,3},{8,9},{10,8},{12,1... | collective-permute-start | bytes 393224 | tf_op jit(solution)/shard_map/ppermute | solution.py:33
  66.7 5.0 %collective-permute-start.20 = (bf16[256,256]{1,0:T(8,128)(2,1)S(1)}, bf16[256,256]{1,0:T(8,128)(2,1)S(1)}, u32[]{:S(2)}, u32[]{:S(2)}) collective-permute-start(bf16[256,256]{1,0:T(8,128)(2,1)S(1)} %add_convert_fusion.9), channel_id=1, source_target_pairs={{0,2},{2,4},{4,6},{6,7},{7,5},{5,3},{3,1},{1,0},{8,10},{10,12},{12... | collective-permute-start | bytes 393224 | tf_op jit(solution)/shard_map/ppermute | solution.py:33
  70.7 5.0 %collective-permute-start.30 = (bf16[256,256]{1,0:T(8,128)(2,1)S(1)}, bf16[256,256]{1,0:T(8,128)(2,1)S(1)}, u32[]{:S(2)}, u32[]{:S(2)}) collective-permute-start(bf16[256,256]{1,0:T(8,128)(2,1)S(1)} %add_convert_fusion.1), channel_id=1, source_target_pairs={{0,1},{2,0},{4,2},{6,4},{7,6},{5,7},{3,5},{1,3},{8,9},{10,8},{12,1... | collective-permute-start | bytes 393224 | tf_op jit(solution)/shard_map/ppermute | solution.py:33

commit v9 on v8

--- a/solution.py
+++ b/solution.py
@@ -116,53 +116,52 @@
     )(*operands)
 
 
-def project_kernel(head_size, factor, wide, w_ref, *refs):
-    lasts, (q_ref, kv_ref) = refs[:-2], refs[-2:]
-    rows, width = lasts[0].shape
+def unit_rows(values, factor):
+    power = jnp.sum(values * values, axis=-1, keepdims=True)
+    return (values * (lax.rsqrt(power + 1e-06) * factor)).astype(BF16)
+
+
+def project_kernel(head_size, base, groups, factor, wide, w_ref, out_ref):
+    rows = out_ref.shape[0]
     depth, out_width = w_ref.shape[1:]
-    done = depth - width
-    for stream, last in enumerate(lasts):
-        here = slice(stream * rows, (stream + 1) * rows)
-        q, k, v = (
-            jnp.dot(wide[here, :done], w_ref[group, :done, :], preferred_element_type=F32)
-            + jnp.dot(last[...], w_ref[group, done:, :], preferred_element_type=F32)
-            for group in range(3)
-        )
+    tile = math.gcd(rows, 256)
+    for first in range(0, rows, tile):
+        here = slice(first, first + tile)
+        there = slice(base + first, base + first + tile)
         power = None
         for lane in range(0, depth, 128):
-            if lane < done:
-                values = wide[here, lane : lane + 128].astype(F32)
-            else:
-                values = last[:, lane - done : lane - done + 128].astype(F32)
+            values = wide[there, lane : lane + 128].astype(F32)
             power = values * values if power is None else power + values * values
         scale = lax.rsqrt(jnp.sum(power, axis=-1, keepdims=True) * (1.0 / depth) + 1e-06)
-        q, k, v = q * scale, k * scale, v * scale
-        for head in range(out_width // head_size):
-            lanes = slice(head * head_size, (head + 1) * head_size)
-            qh, kh = q[:, lanes], k[:, lanes]
-            q_size = lax.rsqrt(jnp.sum(qh * qh, axis=-1, keepdims=True) + 1e-06)
-            k_size = lax.rsqrt(jnp.sum(kh * kh, axis=-1, keepdims=True) + 1e-06)
-            q_ref[here, lanes] = (qh * (q_size * (factor[head] * LOG2E))).astype(BF16)
-            kv_ref[here, lanes] = (kh * k_size).astype(BF16)
-        kv_ref[here, out_width:] = v.astype(BF16)
-
-
-def project(factor, wide, weights, lasts, head_size):
-    rows = wide.shape[0]
-    groups, depth, out_width = weights.shape
+        for number, group in enumerate(groups):
+            start = number * out_width
+            product = jnp.dot(wide[there, :], w_ref[group], preferred_element_type=F32) * scale
+            if group == 2:
+                out_ref[here, start : start + out_width] = product.astype(BF16)
+                continue
+            for head in range(out_width // head_size):
+                lanes = slice(head * head_size, (head + 1) * head_size)
+                amount = factor[head] * LOG2E if group == 0 else 1.0
+                out_ref[here, start + head * head_size : start + (head + 1) * head_size] = unit_rows(
+                    product[:, lanes], amount
+                )
+
+
+def project(factor, wide, weights, base, rows, groups, head_size):
+    depth, out_width = weights.shape[1:]
     return pl.pallas_call(
-        functools.partial(project_kernel, head_size),
-        out_shape=(pltpu.VMEM((rows, out_width), BF16), pltpu.VMEM((rows, 2 * out_width), BF16)),
-        in_specs=[SMEM] + [VMEM] * (2 + len(lasts)),
-        out_specs=(VMEM, VMEM),
+        functools.partial(project_kernel, head_size, base, groups),
+        out_shape=pltpu.VMEM((rows, len(groups) * out_width), BF16),
+        in_specs=[SMEM] + [VMEM] * 2,
+        out_specs=VMEM,
         compiler_params=pltpu.CompilerParams(vmem_limit_bytes=16 << 20),
         cost_estimate=pl.CostEstimate(
-            flops=2 * rows * depth * groups * out_width,
-            bytes_accessed=2 * depth * (rows + groups * out_width),
+            flops=2 * rows * depth * len(groups) * out_width,
+            bytes_accessed=2 * depth * (rows + len(groups) * out_width),
             transcendentals=0,
         ),
-        name="project",
-    )(in_hbm(factor), in_vmem(wide), in_vmem(weights), *map(in_vmem, lasts))
+        name="project_q" if groups == (0,) else "project_kv",
+    )(in_hbm(factor), in_vmem(wide), in_vmem(weights))
 
 
 def attend_blocks(sources, ids, q_first, q_refs, id_col, id_row, kv_refs, v_ones, acc, head_size):
@@ -284,11 +283,7 @@
         compiler_params=pltpu.CompilerParams(
             vmem_limit_bytes=(16 << 20) + 2 * kvs[0].size * 2 * len(kvs)
         ),
-        cost_estimate=pl.CostEstimate(
-            flops=6 * total * keys * len(kvs) * width + 2 * total * width * width * count_out,
-            bytes_accessed=4 * keys * len(kvs) * width + 8 * total * width,
-            transcendentals=total * keys * len(kvs) * heads,
-        ),
+        cost_estimate=pl.CostEstimate(flops=1 << 20, bytes_accessed=1 << 10, transcendentals=0),
         name="attend_last" if count_out else "attend",
     )(info, in_hbm(ids), *operands)
 
@@ -308,7 +303,7 @@
     chip, core = seq_at // 2, seq_at % 2
     index_at = lambda offset: ring_index((place + offset + ring) % ring, ring)
     numbers = lambda values: jnp.stack(values).astype(jnp.int32)
-    id_row = scale_ids.reshape(-1, 1, rows)
+    id_row = scale_ids.reshape(-1, 1, half)
     id_col = lax.dynamic_slice_in_dim(scale_ids, seq_at * rows, rows)[:, None]
     at = [index_at(offset) for offset in range(ring)]
 
@@ -342,29 +337,41 @@
                     blocks.append(in_vmem(held[s][way]))
                     targets.append((s * half, (2 * step - 1 + way) * width))
     wide = placed(targets, blocks, wide, (rows, ring * width))
-    lasts = [held[0][0], held[1][1]]
-    query, kv = project(head_scale, wide, weights, lasts, head_size)
-
-    far, straight, crossed = [], [], []
+    kvs = []
+    for s, last in enumerate((held[0][0], held[1][1])):
+        wide = placed([(s * half, (ring - 1) * width)], [in_vmem(last)], wide, (rows, ring * width))
+        kv = project(head_scale, wide, weights, s * half, half, (1, 2), head_size)
+        wide, kv = lax.optimization_barrier((wide, kv))
+        kvs.append(kv)
+    query = project(head_scale, wide, weights, 0, rows, (0,), head_size)
+
+    far, straight, crossed = [[], []], [[], []], [[], []]
     for step in range(outer):
         source = 2 * ((chip + outer - step) % outer)
-        straight.append((source + core) * rows)
-        crossed.append((source + 1 - core) * rows)
-        if step:
-            far.append(lax.ppermute(kv, "seq", [
-                (2 * a + b, 2 * ((a + step) % outer) + b) for a in range(outer) for b in (0, 1)
-            ]))
+        for s in streams:
+            straight[s].append((source + core) * rows + s * half)
+            crossed[s].append((source + 1 - core) * rows + s * half)
+            if step:
+                far[s].append(lax.ppermute(kvs[s], "seq", [
+                    (2 * a + b, 2 * ((a + step) % outer) + b) for a in range(outer) for b in (0, 1)
+                ]))
     first = [seq_at * rows]
-    info = numbers(straight[:1] + crossed[:1] + first)
-    keys = [kv, swapped(kv, seqs)]
-    (acc,) = attend(info, scale_ids, [query], id_col, id_row, keys, head_size)
-    acc, far = lax.optimization_barrier((acc, far))
-    far_crossed = [swapped(block, seqs) for block in far]
-    info = numbers(straight[1:] + first)
-    (acc,) = attend(info, scale_ids, [query], id_col, id_row, far, head_size, acc)
+    groups = [[(kvs[0], straight[0][0]), (swapped(kvs[0], seqs), crossed[0][0]), (kvs[1], straight[1][0])]]
+    groups.append(list(zip(far[0], straight[0][1:])))
+    groups.append([*zip(far[1], straight[1][1:]), (swapped(kvs[1], seqs), crossed[1][0])])
+    acc = None
+    for number, group in enumerate(groups):
+        keys, places = [key for key, place in group], [place for key, place in group]
+        if number:
+            acc, keys = lax.optimization_barrier((acc, keys))
+        if number == 2:
+            far[1] = keys[:-1]
+            far_crossed = [swapped(block, seqs) for s in streams for block in far[s]]
+        info = numbers(places + first)
+        (acc,) = attend(info, scale_ids, [query], id_col, id_row, keys, head_size, acc)
 
     goals = [[*range(up, 0, -1), *range(-down, 0), 0] for up, down in reach]
-    info = numbers(crossed[1:] + first + [at[goal % ring] for goal in goals[0] + goals[1]])
+    info = numbers(crossed[0][1:] + crossed[1][1:] + first + [at[goal % ring] for goal in goals[0] + goals[1]])
     parts = attend(
         info, scale_ids, [query], id_col, id_row, far_crossed, head_size, acc, w_out, len(streams)
     )

time: 76.9 us -> 82.5 us (1.073)
  Pallas kernels: 15.7 us -> 22.3 us
  waiting for transfers between devices: 27.4 us -> 23.8 us
  starting transfers between devices: 29.7 us -> 32 us
    ppermute x1 -> x2, waiting for transfers between devices: 9.13 us -> 3.32 us  [body(): lax.ppermute(kvs[s], 'seq', [(2 * a + b, 2 * ((a + step) % outer) + b) fo...]
    pallas_call x3 -> x4, Pallas kernels: 8.71 us -> 12 us  [attend(): pl.pallas_call(functools.partial(attend_kernel, len(queries), len(kvs), h...]
    ppermute x28, waiting for transfers between devices: 17.9 us -> 20.5 us  [along(): lax.ppermute(value, 'head', [(order[p], order[(p + step) % count]) for p...]
    pallas_call x1 -> x3, Pallas kernels: 2.8 us -> 4.77 us  [project(): pl.pallas_call(functools.partial(project_kernel, head_size, base, groups)...]
    ppermute x1 -> x2, starting transfers between devices: 0.54 us -> 2.16 us  [body(): lax.ppermute(kvs[s], 'seq', [(2 * a + b, 2 * ((a + step) % outer) + b) fo...]
    pallas_call x3 -> x5, Pallas kernels: 1.22 us -> 2.46 us  [placed(): pl.pallas_call(functools.partial(place_kernel, targets), out_shape=pltpu....]
  transfers between devices with their start and end apart: 31 -> 34, of which waited for: 16 -> 12; matrix products, arithmetic and copies ran while one was open for 2% -> 2% of each run, Pallas kernels for 13% -> 22%
where the time goes in v9:
time: 82.5 us; the launch traced here: 82 us
  starting transfers between devices  32 us (39%)
  waiting for transfers between devices  23.8 us (29%)
  Pallas kernels  22.3 us (27%)
  local copies, waits for them, and re-layouts  2.22 us (3%)
  other arithmetic  1.4 us (2%)
    ppermute x28, starting transfers between devices, along(): lax.ppermute(value, 'head', [(order[p], order[(p + step) % count]) for p...  29.3 us
    ppermute x28, waiting for transfers between devices, along(): lax.ppermute(value, 'head', [(order[p], order[(p + step) % count]) for p...  20.5 us
    pallas_call x4, Pallas kernels, attend(): pl.pallas_call(functools.partial(attend_kernel, len(queries), len(kvs), h...  12 us
    pallas_call x3, Pallas kernels, project(): pl.pallas_call(functools.partial(project_kernel, head_size, base, groups)...  4.77 us
    ppermute x2, waiting for transfers between devices, body(): lax.ppermute(kvs[s], 'seq', [(2 * a + b, 2 * ((a + step) % outer) + b) fo...  3.32 us
    pallas_call x1, Pallas kernels, fold_gain(): pl.pallas_call(functools.partial(fold_kernel, order), out_shape=pltpu.VME...  3.01 us
    pallas_call x5, Pallas kernels, placed(): pl.pallas_call(functools.partial(place_kernel, targets), out_shape=pltpu....  2.46 us
    ppermute x2, starting transfers between devices, body(): lax.ppermute(kvs[s], 'seq', [(2 * a + b, 2 * ((a + step) % outer) + b) fo...  2.16 us
  transfers between devices with their start and end apart: 34, of which 12 were waited for; matrix products, arithmetic and copies ran while one was open for 2% of the time, Pallas kernels for 22%

profile of v9, /device:TPU:10, one launch (start us, length us, event | category | flops | bytes accessed | tf_op | source)
XLA Modules:
  0.0 82.0 jit_solution(17078450212717533243)
XLA Ops:
  0.0 1.0 %fusion = (bf16[256,256]{1,0:T(8,128)(2,1)S(1)}, bf16[256,256]{1,0:T(8,128)(2,1)S(1)}) fusion(bf16[512,256]{1,0:T(8,128)(2,1)} %refs_0_.1), kind=kLoop, calls=%fused_computation.16 | loop fusion | bytes 524288 | tf_op jit(solution)/shard_map/slice | solution.py:315
  1.0 1.6 %collective-permute-start.3 = (bf16[256,256]{1,0:T(8,128)(2,1)S(1)}, bf16[256,256]{1,0:T(8,128)(2,1)S(1)}, u32[]{:S(2)}, u32[]{:S(2)}) collective-permute-start(bf16[256,256]{1,0:T(8,128)(2,1)S(1)} %get-tuple-element.63), channel_id=1, source_target_pairs={{0,2},{2,4},{4,6},{6,7},{7,5},{5,3},{3,1},{1,0},{8,10},{10,12},{12... | collective-permute-start | bytes 393224 | tf_op jit(solution)/shard_map/ppermute | solution.py:33
  3.5 1.6 %collective-permute-start.7 = (bf16[256,256]{1,0:T(8,128)(2,1)S(1)}, bf16[256,256]{1,0:T(8,128)(2,1)S(1)}, u32[]{:S(2)}, u32[]{:S(2)}) collective-permute-start(bf16[256,256]{1,0:T(8,128)(2,1)S(1)} %get-tuple-element.64), channel_id=1, source_target_pairs={{0,2},{2,4},{4,6},{6,7},{7,5},{5,3},{3,1},{1,0},{8,10},{10,12},{12... | collective-permute-start | bytes 393224 | tf_op jit(solution)/shard_map/ppermute | solution.py:33
  5.1 2.3 %collective-permute-done.3.refs_1_ = bf16[256,256]{1,0:T(8,128)(2,1)S(1)} collective-permute-done((bf16[256,256]{1,0:T(8,128)(2,1)S(1)}, bf16[256,256]{1,0:T(8,128)(2,1)S(1)}, u32[]{:S(2)}, u32[]{:S(2)}) %collective-permute-start.3) | collective-permute-done | bytes 131104 | tf_op jit(solution)/shard_map/ppermute | solution.py:33
  7.4 1.6 %collective-permute-start.4 = (bf16[256,256]{1,0:T(8,128)(2,1)S(1)}, bf16[256,256]{1,0:T(8,128)(2,1)S(1)}, u32[]{:S(2)}, u32[]{:S(2)}) collective-permute-start(bf16[256,256]{1,0:T(8,128)(2,1)S(1)} %collective-permute-done.3.refs_1_), channel_id=1, source_target_pairs={{0,2},{2,4},{4,6},{6,7},{7,5},{5,3},{3,1},{1,0},{8,10},{10,12},{12... | collective-permute-start | bytes 393224 | tf_op jit(solution)/shard_map/ppermute | solution.py:33
  9.1 3.0 %fold_gain.1.w_ref = bf16[3,2048,256]{2,1,0:T(8,128)(2,1)S(1)} custom-call(s32[8]{0:T(128)S(1)} %stack.97.at, f32[16,128]{1,0:T(8,128)} %bitcast.24, bf16[3,2048,256]{2,1,0:T(8,128)(2,1)} %w_hbm.1), custom_call_target="tpu_custom_call" | custom-call | flops 1572864 | bytes 6291456 | tf_op jit(solution)/shard_map/fold_gain/pallas_call | solution.py:77
  12.1 0.5 collective-permute-start.1
  12.7 2.0 %collective-permute-start.8 = (bf16[256,256]{1,0:T(8,128)(2,1)S(1)}, bf16[256,256]{1,0:T(8,128)(2,1)S(1)}, u32[]{:S(2)}, u32[]{:S(2)}) collective-permute-start(bf16[256,256]{1,0:T(8,128)(2,1)S(1)} %collective-permute-done.7.refs_3_), channel_id=1, source_target_pairs={{0,2},{2,4},{4,6},{6,7},{7,5},{5,3},{3,1},{1,0},{8,10},{10,12},{12... | collective-permute-start | bytes 393224 | tf_op jit(solution)/shard_map/ppermute | solution.py:33
  14.7 1.6 %collective-permute-start.10 = (bf16[256,256]{1,0:T(8,128)(2,1)S(1)}, bf16[256,256]{1,0:T(8,128)(2,1)S(1)}, u32[]{:S(2)}, u32[]{:S(2)}) collective-permute-start(bf16[256,256]{1,0:T(8,128)(2,1)S(1)} %collective-permute-done.4.refs_0_), channel_id=1, source_target_pairs={{0,2},{2,4},{4,6},{6,7},{7,5},{5,3},{3,1},{1,0},{8,10},{10,12},{12... | collective-permute-start | bytes 393224 | tf_op jit(solution)/shard_map/ppermute | solution.py:33
  16.2 2.0 %collective-permute-done.1.refs_3_ = bf16[256,256]{1,0:T(8,128)(2,1)S(1)} collective-permute-done((bf16[256,256]{1,0:T(8,128)(2,1)S(1)}, bf16[256,256]{1,0:T(8,128)(2,1)S(1)}, u32[]{:S(2)}, u32[]{:S(2)}) %collective-permute-start.1) | collective-permute-done | bytes 131104 | tf_op jit(solution)/shard_map/ppermute | solution.py:33
  18.7 2.4 %collective-permute-done.6.refs_1_ = bf16[256,256]{1,0:T(8,128)(2,1)S(1)} collective-permute-done((bf16[256,256]{1,0:T(8,128)(2,1)S(1)}, bf16[256,256]{1,0:T(8,128)(2,1)S(1)}, u32[]{:S(2)}, u32[]{:S(2)}) %collective-permute-start.6) | collective-permute-done | bytes 131104 | tf_op jit(solution)/shard_map/ppermute | solution.py:33
  21.5 1.6 %collective-permute-start.13 = (bf16[256,256]{1,0:T(8,128)(2,1)S(1)}, bf16[256,256]{1,0:T(8,128)(2,1)S(1)}, u32[]{:S(2)}, u32[]{:S(2)}) collective-permute-start(bf16[256,256]{1,0:T(8,128)(2,1)S(1)} %collective-permute-done.8.refs_2_), channel_id=1, source_target_pairs={{0,2},{2,4},{4,6},{6,7},{7,5},{5,3},{3,1},{1,0},{8,10},{10,12},{12... | collective-permute-start | bytes 393224 | tf_op jit(solution)/shard_map/ppermute | solution.py:33
  23.1 1.6 %collective-permute-start.11 = (bf16[256,256]{1,0:T(8,128)(2,1)S(1)}, bf16[256,256]{1,0:T(8,128)(2,1)}, u32[]{:S(2)}, u32[]{:S(2)}) collective-permute-start(bf16[256,256]{1,0:T(8,128)(2,1)S(1)} %collective-permute-done.10.refs_0_), channel_id=1, source_target_pairs={{0,2},{2,4},{4,6},{6,7},{7,5},{5,3},{3,1},{1,0},{8,10},{10,12},{12... | collective-permute-start | bytes 393224 | tf_op jit(solution)/shard_map/ppermute | solution.py:33
  24.7 1.0 %place.5.refs_4_ = bf16[512,2048]{1,0:T(8,128)(2,1)S(1)} custom-call(bf16[512,256]{1,0:T(8,128)(2,1)} %refs_0_.1, bf16[256,256]{1,0:T(8,128)(2,1)S(1)} %collective-permute-done.3.refs_1_, bf16[256,256]{1,0:T(8,128)(2,1)S(1)} %collective-permute-done.5.refs_2_, bf16[256,256]{1,0:T(8,128)(2,1)S(1)} %collective-permute-done.7.refs_3_, ...), custom_call_target="tpu_custom_call" | custom-call | bytes 1048576 | tf_op jit(solution)/shard_map/place/pallas_call | solution.py:106
  25.8 0.7 collective-permute-start.9
  26.5 0.8 dynamic_slice.3
  27.6 0.6 collective-permute-done.11.refs_0_
  28.2 1.2 %place.8.wide.refs_1_ = bf16[512,2048]{1,0:T(8,128)(2,1)S(1)} custom-call(bf16[256,256]{1,0:T(8,128)(2,1)} %collective-permute-done.11.refs_0_, bf16[512,2048]{1,0:T(8,128)(2,1)S(1)} %place.7.refs_1_), custom_call_target="tpu_custom_call", output_to_operand_aliasing={{}: (1, {})} | custom-call | bytes 1048576 | tf_op jit(solution)/shard_map/place/pallas_call | solution.py:106
  29.5 1.5 %project_kv.2.refs_3_ = bf16[256,512]{1,0:T(8,128)(2,1)S(1)} custom-call(f32[2]{0:T(128)} %factor.5, bf16[512,2048]{1,0:T(8,128)(2,1)S(1)} %place.8.wide.refs_1_, bf16[3,2048,256]{2,1,0:T(8,128)(2,1)S(1)} %copy-done.1), custom_call_target="tpu_custom_call" | custom-call | flops 536870912 | bytes 3145728 | tf_op jit(solution)/shard_map/project_kv/pallas_call | solution.py:152
  31.1 0.6 collective-permute-start.14
  31.8 1.5 %project_kv.3.refs_5_ = bf16[256,512]{1,0:T(8,128)(2,1)S(1)} custom-call(f32[2]{0:T(128)} %factor.5, bf16[512,2048]{1,0:T(8,128)(2,1)S(1)} %place.9.wide, bf16[3,2048,256]{2,1,0:T(8,128)(2,1)S(1)} %copy-done.1), custom_call_target="tpu_custom_call" | custom-call | flops 536870912 | bytes 3145728 | tf_op jit(solution)/shard_map/project_kv/pallas_call | solution.py:152
  33.3 1.6 %collective-permute-start.17 = (bf16[256,512]{1,0:T(8,128)(2,1)S(1)}, bf16[256,512]{1,0:T(8,128)(2,1)S(1)}, u32[]{:S(2)}, u32[]{:S(2)}) collective-permute-start(bf16[256,512]{1,0:T(8,128)(2,1)S(1)} %project_kv.3.refs_5_), channel_id=1, source_target_pairs={{0,16},{8,24},{16,0},{24,8},{1,17},{9,25},{17,1},{25,9},{2,18},{10... | collective-permute-start | bytes 786440 | tf_op jit(solution)/shard_map/ppermute | solution.py:355
  35.0 1.7 %project_q.1.refs_0_ = bf16[512,256]{1,0:T(8,128)(2,1)S(1)} custom-call(f32[2]{0:T(128)} %factor.5, bf16[512,2048]{1,0:T(8,128)(2,1)S(1)} %place.9.wide, bf16[3,2048,256]{2,1,0:T(8,128)(2,1)S(1)} %copy-done.1), custom_call_target="tpu_custom_call" | custom-call | flops 536870912 | bytes 3145728 | tf_op jit(solution)/shard_map/project_q/pallas_call | solution.py:152
  36.8 3.5 %attend.3.refs_4_ = f32[512,512]{1,0:T(8,128)S(1)} custom-call(s32[4]{0:T(128)S(1)} %pad_add_fusion.1.info, s32[2048]{0:T(1024)} %ids.7, bf16[512,256]{1,0:T(8,128)(2,1)S(1)} %project_q.1.refs_0_, s32[512,1]{1,0:T(8,128)S(1)} %copy.14.refs_1_, s32[8,1,256]{2,1,0:T(1,128)} %bitcast.20, bf16[256,512]{1,0:T(8,128)(2,1)S(1)} %project_kv.2.refs_3_, ...), custom_call_target="tpu_custom_call" | custom-call | flops 1048576 | bytes 1024 | tf_op jit(solution)/shard_map/attend/pallas_call | solution.py:275
  40.3 1.8 %attend.4.refs_5_ = f32[512,512]{1,0:T(8,128)S(1)} custom-call(s32[2]{0:T(128)S(1)} %pad_add_fusion.info, s32[2048]{0:T(1024)} %ids.7, bf16[512,256]{1,0:T(8,128)(2,1)S(1)} %project_q.1.refs_0_, s32[512,1]{1,0:T(8,128)S(1)} %copy.14.refs_1_, s32[8,1,256]{2,1,0:T(1,128)} %bitcast.21, bf16[256,512]{1,0:T(8,128)(2,1)S(1)} %collective-permute-done.14.refs_3_, ...), custom_call_target="tpu_custom_call" | custom-call | flops 1048576 | bytes 1024 | tf_op jit(solution)/shard_map/attend/pallas_call | solution.py:275
  42.1 3.3 %collective-permute-done.17.refs_3_ = bf16[256,512]{1,0:T(8,128)(2,1)S(1)} collective-permute-done((bf16[256,512]{1,0:T(8,128)(2,1)S(1)}, bf16[256,512]{1,0:T(8,128)(2,1)S(1)}, u32[]{:S(2)}, u32[]{:S(2)}) %collective-permute-start.17) | collective-permute-done | bytes 262176 | tf_op jit(solution)/shard_map/ppermute | solution.py:355
  45.5 0.5 collective-permute-start.15
  46.2 2.7 %attend.5.refs_5_ = f32[512,512]{1,0:T(8,128)S(1)} custom-call(s32[3]{0:T(128)S(1)} %pad_add_fusion.2.info, s32[2048]{0:T(1024)} %ids.7, bf16[512,256]{1,0:T(8,128)(2,1)S(1)} %project_q.1.refs_0_, s32[512,1]{1,0:T(8,128)S(1)} %copy.14.refs_1_, s32[8,1,256]{2,1,0:T(1,128)} %bitcast.22, bf16[256,512]{1,0:T(8,128)(2,1)S(1)} %collective-permute-done.17.refs_3_, ...), custom_call_target="tpu_custom_call" | custom-call | flops 1048576 | bytes 1024 | tf_op jit(solution)/shard_map/attend/pallas_call | solution.py:275
  48.9 4.0 %attend_last.1 = (bf16[256,256]{1,0:T(8,128)(2,1)S(1)}, bf16[256,256]{1,0:T(8,128)(2,1)S(1)}, bf16[256,256]{1,0:T(8,128)(2,1)S(1)}, bf16[256,256]{1,0:T(8,128)(2...) custom-call(s32[19]{0:T(128)S(1)} %stack.96.info, ...), custom_call_target="tpu_custom_call" | custom-call | flops 1048576 | bytes 1024 | tf_op jit(solution)/shard_map/attend_last/pallas_call | solution.py:275
  52.9 1.6 %collective-permute-start.20 = (bf16[256,256]{1,0:T(8,128)(2,1)S(1)}, bf16[256,256]{1,0:T(8,128)(2,1)S(1)}, u32[]{:S(2)}, u32[]{:S(2)}) collective-permute-start(bf16[256,256]{1,0:T(8,128)(2,1)S(1)} %get-tuple-element.51), channel_id=1, source_target_pairs={{0,2},{2,4},{4,6},{6,7},{7,5},{5,3},{3,1},{1,0},{8,10},{10,12},{12... | collective-permute-start | bytes 393224 | tf_op jit(solution)/shard_map/ppermute | solution.py:33
  54.9 1.6 %collective-permute-start.27 = (bf16[256,256]{1,0:T(8,128)(2,1)S(1)}, bf16[256,256]{1,0:T(8,128)(2,1)S(1)}, u32[]{:S(2)}, u32[]{:S(2)}) collective-permute-start(bf16[256,256]{1,0:T(8,128)(2,1)S(1)} %get-tuple-element.58), channel_id=1, source_target_pairs={{0,2},{2,4},{4,6},{6,7},{7,5},{5,3},{3,1},{1,0},{8,10},{10,12},{12... | collective-permute-start | bytes 393224 | tf_op jit(solution)/shard_map/ppermute | solution.py:33
  57.0 2.3 %collective-permute-done.20 = bf16[256,256]{1,0:T(8,128)(2,1)S(1)} collective-permute-done((bf16[256,256]{1,0:T(8,128)(2,1)S(1)}, bf16[256,256]{1,0:T(8,128)(2,1)S(1)}, u32[]{:S(2)}, u32[]{:S(2)}) %collective-permute-start.20) | collective-permute-done | bytes 131104 | tf_op jit(solution)/shard_map/ppermute | solution.py:33
  59.3 1.6 %collective-permute-start.21 = (bf16[256,256]{1,0:T(8,128)(2,1)S(1)}, bf16[256,256]{1,0:T(8,128)(2,1)S(1)}, u32[]{:S(2)}, u32[]{:S(2)}) collective-permute-start(bf16[256,256]{1,0:T(8,128)(2,1)S(1)} %add_convert_fusion.11), channel_id=1, source_target_pairs={{0,2},{2,4},{4,6},{6,7},{7,5},{5,3},{3,1},{1,0},{8,10},{10,12},{12... | collective-permute-start | bytes 393224 | tf_op jit(solution)/shard_map/ppermute | solution.py:33
  61.0 0.5 collective-permute-start.25
  61.5 0.6 collective-permute-done.27
  62.1 1.6 %collective-permute-start.28 = (bf16[256,256]{1,0:T(8,128)(2,1)S(1)}, bf16[256,256]{1,0:T(8,128)(2,1)S(1)}, u32[]{:S(2)}, u32[]{:S(2)}) collective-permute-start(bf16[256,256]{1,0:T(8,128)(2,1)S(1)} %add_convert_fusion.5), channel_id=1, source_target_pairs={{0,2},{2,4},{4,6},{6,7},{7,5},{5,3},{3,1},{1,0},{8,10},{10,12},{12... | collective-permute-start | bytes 393224 | tf_op jit(solution)/shard_map/ppermute | solution.py:33
  63.8 0.5 collective-permute-start.31
  64.3 1.4 %collective-permute-done.21 = bf16[256,256]{1,0:T(8,128)(2,1)S(1)} collective-permute-done((bf16[256,256]{1,0:T(8,128)(2,1)S(1)}, bf16[256,256]{1,0:T(8,128)(2,1)S(1)}, u32[]{:S(2)}, u32[]{:S(2)}) %collective-permute-start.21) | collective-permute-done | bytes 131104 | tf_op jit(solution)/shard_map/ppermute | solution.py:33
  65.7 1.6 %collective-permute-start.22 = (bf16[256,256]{1,0:T(8,128)(2,1)S(1)}, bf16[256,256]{1,0:T(8,128)(2,1)S(1)}, u32[]{:S(2)}, u32[]{:S(2)}) collective-permute-start(bf16[256,256]{1,0:T(8,128)(2,1)S(1)} %add_convert_fusion.10), channel_id=1, source_target_pairs={{0,2},{2,4},{4,6},{6,7},{7,5},{5,3},{3,1},{1,0},{8,10},{10,12},{12... | collective-permute-start | bytes 393224 | tf_op jit(solution)/shard_map/ppermute | solution.py:33
  67.4 0.5 collective-permute-start.26
  67.9 0.6 collective-permute-done.28
  68.6 1.6 %collective-permute-start.29 = (bf16[256,256]{1,0:T(8,128)(2,1)S(1)}, bf16[256,256]{1,0:T(8,128)(2,1)S(1)}, u32[]{:S(2)}, u32[]{:S(2)}) collective-permute-start(bf16[256,256]{1,0:T(8,128)(2,1)S(1)} %add_convert_fusion.4), channel_id=1, source_target_pairs={{0,2},{2,4},{4,6},{6,7},{7,5},{5,3},{3,1},{1,0},{8,10},{10,12},{12... | collective-permute-start | bytes 393224 | tf_op jit(solution)/shard_map/ppermute | solution.py:33
  70.3 0.5 collective-permute-start.32
  70.8 0.6 collective-permute-done.22
  71.4 1.6 %collective-permute-start.23 = (bf16[256,256]{1,0:T(8,128)(2,1)S(1)}, bf16[256,256]{1,0:T(8,128)(2,1)S(1)}, u32[]{:S(2)}, u32[]{:S(2)}) collective-permute-start(bf16[256,256]{1,0:T(8,128)(2,1)S(1)} %add_convert_fusion.9), channel_id=1, source_target_pairs={{0,2},{2,4},{4,6},{6,7},{7,5},{5,3},{3,1},{1,0},{8,10},{10,12},{12... | collective-permute-start | bytes 393224 | tf_op jit(solution)/shard_map/ppermute | solution.py:33
  73.0 3.1 %collective-permute-done.32 = bf16[256,256]{1,0:T(8,128)(2,1)S(1)} collective-permute-done((bf16[256,256]{1,0:T(8,128)(2,1)S(1)}, bf16[256,256]{1,0:T(8,128)(2,1)S(1)}, u32[]{:S(2)}, u32[]{:S(2)}) %collective-permute-start.32) | collective-permute-done | bytes 131104 | tf_op jit(solution)/shard_map/ppermute | solution.py:33
  76.7 4.5 %collective-permute-done.33 = bf16[256,256]{1,0:T(8,128)(2,1)S(1)} collective-permute-done((bf16[256,256]{1,0:T(8,128)(2,1)S(1)}, bf16[256,256]{1,0:T(8,128)(2,1)S(1)}, u32[]{:S(2)}, u32[]{:S(2)}) %collective-permute-start.33) | collective-permute-done | bytes 131104 | tf_op jit(solution)/shard_map/ppermute | solution.py:33
  81.3 0.7 pad_maximum_fusion
  (58 shorter events, 4.8 us)
Async XLA Ops:
  1.0 6.4 %collective-permute-start.3 = (bf16[256,256]{1,0:T(8,128)(2,1)S(1)}, bf16[256,256]{1,0:T(8,128)(2,1)S(1)}, u32[]{:S(2)}, u32[]{:S(2)}) collective-permute-start(bf16[256,256]{1,0:T(8,128)(2,1)S(1)} %get-tuple-element.63), channel_id=1, source_target_pairs={{0,2},{2,4},{4,6},{6,7},{7,5},{5,3},{3,1},{1,0},{8,10},{10,12},{12... | collective-permute-start | bytes 393224 | tf_op jit(solution)/shard_map/ppermute | solution.py:33
  2.6 9.5 %collective-permute-start = (bf16[256,256]{1,0:T(8,128)(2,1)S(1)}, bf16[256,256]{1,0:T(8,128)(2,1)S(1)}, u32[]{:S(2)}, u32[]{:S(2)}) collective-permute-start(bf16[256,256]{1,0:T(8,128)(2,1)S(1)} %get-tuple-element.64), channel_id=1, source_target_pairs={{0,1},{2,0},{4,2},{6,4},{7,6},{5,7},{3,5},{1,3},{8,9},{10,8},{12,1... | collective-permute-start | bytes 393224 | tf_op jit(solution)/shard_map/ppermute | solution.py:33
  3.1 9.6 %collective-permute-start.5 = (bf16[256,256]{1,0:T(8,128)(2,1)S(1)}, bf16[256,256]{1,0:T(8,128)(2,1)S(1)}, u32[]{:S(2)}, u32[]{:S(2)}) collective-permute-start(bf16[256,256]{1,0:T(8,128)(2,1)S(1)} %get-tuple-element.63), channel_id=1, source_target_pairs={{0,1},{2,0},{4,2},{6,4},{7,6},{5,7},{3,5},{1,3},{8,9},{10,8},{12,1... | collective-permute-start | bytes 393224 | tf_op jit(solution)/shard_map/ppermute | solution.py:33
  3.5 9.2 %collective-permute-start.7 = (bf16[256,256]{1,0:T(8,128)(2,1)S(1)}, bf16[256,256]{1,0:T(8,128)(2,1)S(1)}, u32[]{:S(2)}, u32[]{:S(2)}) collective-permute-start(bf16[256,256]{1,0:T(8,128)(2,1)S(1)} %get-tuple-element.64), channel_id=1, source_target_pairs={{0,2},{2,4},{4,6},{6,7},{7,5},{5,3},{3,1},{1,0},{8,10},{10,12},{12... | collective-permute-start | bytes 393224 | tf_op jit(solution)/shard_map/ppermute | solution.py:33
  7.4 7.2 %collective-permute-start.4 = (bf16[256,256]{1,0:T(8,128)(2,1)S(1)}, bf16[256,256]{1,0:T(8,128)(2,1)S(1)}, u32[]{:S(2)}, u32[]{:S(2)}) collective-permute-start(bf16[256,256]{1,0:T(8,128)(2,1)S(1)} %collective-permute-done.3.refs_1_), channel_id=1, source_target_pairs={{0,2},{2,4},{4,6},{6,7},{7,5},{5,3},{3,1},{1,0},{8,10},{10,12},{12... | collective-permute-start | bytes 393224 | tf_op jit(solution)/shard_map/ppermute | solution.py:33
  12.1 13.7 %copy-start = (bf16[3,2048,256]{2,1,0:T(8,128)(2,1)}, bf16[3,2048,256]{2,1,0:T(8,128)(2,1)S(1)}, u32[]{:S(2)}) copy-start(bf16[3,2048,256]{2,1,0:T(8,128)(2,1)S(1)} %fold_gain.1.w_ref) | copy-start | bytes 9437188
  12.1 6.1 %collective-permute-start.1 = (bf16[256,256]{1,0:T(8,128)(2,1)S(1)}, bf16[256,256]{1,0:T(8,128)(2,1)S(1)}, u32[]{:S(2)}, u32[]{:S(2)}) collective-permute-start(bf16[256,256]{1,0:T(8,128)(2,1)S(1)} %collective-permute-done.refs_4_), channel_id=1, source_target_pairs={{0,1},{2,0},{4,2},{6,4},{7,6},{5,7},{3,5},{1,3},{8,9},{10,8},{12,1... | collective-permute-start | bytes 393224 | tf_op jit(solution)/shard_map/ppermute | solution.py:33
  12.6 8.4 %collective-permute-start.6 = (bf16[256,256]{1,0:T(8,128)(2,1)S(1)}, bf16[256,256]{1,0:T(8,128)(2,1)S(1)}, u32[]{:S(2)}, u32[]{:S(2)}) collective-permute-start(bf16[256,256]{1,0:T(8,128)(2,1)S(1)} %collective-permute-done.5.refs_2_), channel_id=1, source_target_pairs={{0,1},{2,0},{4,2},{6,4},{7,6},{5,7},{3,5},{1,3},{8,9},{10,8},{12,1... | collective-permute-start | bytes 393224 | tf_op jit(solution)/shard_map/ppermute | solution.py:33
  12.7 8.8 %collective-permute-start.8 = (bf16[256,256]{1,0:T(8,128)(2,1)S(1)}, bf16[256,256]{1,0:T(8,128)(2,1)S(1)}, u32[]{:S(2)}, u32[]{:S(2)}) collective-permute-start(bf16[256,256]{1,0:T(8,128)(2,1)S(1)} %collective-permute-done.7.refs_3_), channel_id=1, source_target_pairs={{0,2},{2,4},{4,6},{6,7},{7,5},{5,3},{3,1},{1,0},{8,10},{10,12},{12... | collective-permute-start | bytes 393224 | tf_op jit(solution)/shard_map/ppermute | solution.py:33
  14.7 8.4 %collective-permute-start.10 = (bf16[256,256]{1,0:T(8,128)(2,1)S(1)}, bf16[256,256]{1,0:T(8,128)(2,1)S(1)}, u32[]{:S(2)}, u32[]{:S(2)}) collective-permute-start(bf16[256,256]{1,0:T(8,128)(2,1)S(1)} %collective-permute-done.4.refs_0_), channel_id=1, source_target_pairs={{0,2},{2,4},{4,6},{6,7},{7,5},{5,3},{3,1},{1,0},{8,10},{10,12},{12... | collective-permute-start | bytes 393224 | tf_op jit(solution)/shard_map/ppermute | solution.py:33
  18.2 7.6 %collective-permute-start.2 = (bf16[256,256]{1,0:T(8,128)(2,1)S(1)}, bf16[256,256]{1,0:T(8,128)(2,1)S(1)}, u32[]{:S(2)}, u32[]{:S(2)}) collective-permute-start(bf16[256,256]{1,0:T(8,128)(2,1)S(1)} %collective-permute-done.1.refs_3_), channel_id=1, source_target_pairs={{0,1},{2,0},{4,2},{6,4},{7,6},{5,7},{3,5},{1,3},{8,9},{10,8},{12,1... | collective-permute-start | bytes 393224 | tf_op jit(solution)/shard_map/ppermute | solution.py:33
  21.1 6.4 %collective-permute-start.12 = (bf16[256,256]{1,0:T(8,128)(2,1)S(1)}, bf16[256,256]{1,0:T(8,128)(2,1)S(1)}, u32[]{:S(2)}, u32[]{:S(2)}) collective-permute-start(bf16[256,256]{1,0:T(8,128)(2,1)S(1)} %collective-permute-done.6.refs_1_), channel_id=1, source_target_pairs={{0,1},{2,0},{4,2},{6,4},{7,6},{5,7},{3,5},{1,3},{8,9},{10,8},{12,1... | collective-permute-start | bytes 393224 | tf_op jit(solution)/shard_map/ppermute | solution.py:33
  21.5 5.9 %collective-permute-start.13 = (bf16[256,256]{1,0:T(8,128)(2,1)S(1)}, bf16[256,256]{1,0:T(8,128)(2,1)S(1)}, u32[]{:S(2)}, u32[]{:S(2)}) collective-permute-start(bf16[256,256]{1,0:T(8,128)(2,1)S(1)} %collective-permute-done.8.refs_2_), channel_id=1, source_target_pairs={{0,2},{2,4},{4,6},{6,7},{7,5},{5,3},{3,1},{1,0},{8,10},{10,12},{12... | collective-permute-start | bytes 393224 | tf_op jit(solution)/shard_map/ppermute | solution.py:33
  23.1 5.1 %collective-permute-start.11 = (bf16[256,256]{1,0:T(8,128)(2,1)S(1)}, bf16[256,256]{1,0:T(8,128)(2,1)}, u32[]{:S(2)}, u32[]{:S(2)}) collective-permute-start(bf16[256,256]{1,0:T(8,128)(2,1)S(1)} %collective-permute-done.10.refs_0_), channel_id=1, source_target_pairs={{0,2},{2,4},{4,6},{6,7},{7,5},{5,3},{3,1},{1,0},{8,10},{10,12},{12... | collective-permute-start | bytes 393224 | tf_op jit(solution)/shard_map/ppermute | solution.py:33
  25.8 5.9 %collective-permute-start.9 = (bf16[256,256]{1,0:T(8,128)(2,1)S(1)}, bf16[256,256]{1,0:T(8,128)(2,1)S(1)}, u32[]{:S(2)}, u32[]{:S(2)}) collective-permute-start(bf16[256,256]{1,0:T(8,128)(2,1)S(1)} %collective-permute-done.2.refs_3_), channel_id=1, source_target_pairs={{0,1},{2,0},{4,2},{6,4},{7,6},{5,7},{3,5},{1,3},{8,9},{10,8},{12,1... | collective-permute-start | bytes 393224 | tf_op jit(solution)/shard_map/ppermute | solution.py:33
  27.6 2.0 %copy-start.1 = (bf16[3,2048,256]{2,1,0:T(8,128)(2,1)S(1)}, bf16[3,2048,256]{2,1,0:T(8,128)(2,1)}, u32[]{:S(2)}) copy-start(bf16[3,2048,256]{2,1,0:T(8,128)(2,1)} %copy-done) | copy-start | bytes 9437188
  31.0 5.7 %collective-permute-start.16 = (bf16[256,512]{1,0:T(8,128)(2,1)S(1)}, bf16[256,512]{1,0:T(8,128)(2,1)S(1)}, u32[]{:S(2)}, u32[]{:S(2)}) collective-permute-start(bf16[256,512]{1,0:T(8,128)(2,1)S(1)} %project_kv.2.refs_3_), channel_id=1, source_target_pairs={{0,8},{8,0},{16,24},{24,16},{1,9},{9,1},{17,25},{25,17},{2,10},{10... | collective-permute-start | bytes 786440 | tf_op jit(solution)/shard_map/ppermute | solution.py:39
  31.1 9.2 %collective-permute-start.14 = (bf16[256,512]{1,0:T(8,128)(2,1)S(1)}, bf16[256,512]{1,0:T(8,128)(2,1)S(1)}, u32[]{:S(2)}, u32[]{:S(2)}) collective-permute-start(bf16[256,512]{1,0:T(8,128)(2,1)S(1)} %project_kv.2.refs_3_), channel_id=1, source_target_pairs={{0,16},{8,24},{16,0},{24,8},{1,17},{9,25},{17,1},{25,9},{2,18},{10... | collective-permute-start | bytes 786440 | tf_op jit(solution)/shard_map/ppermute | solution.py:355
  33.3 12.2 %collective-permute-start.17 = (bf16[256,512]{1,0:T(8,128)(2,1)S(1)}, bf16[256,512]{1,0:T(8,128)(2,1)S(1)}, u32[]{:S(2)}, u32[]{:S(2)}) collective-permute-start(bf16[256,512]{1,0:T(8,128)(2,1)S(1)} %project_kv.3.refs_5_), channel_id=1, source_target_pairs={{0,16},{8,24},{16,0},{24,8},{1,17},{9,25},{17,1},{25,9},{2,18},{10... | collective-permute-start | bytes 786440 | tf_op jit(solution)/shard_map/ppermute | solution.py:355
  34.8 10.6 %collective-permute-start.18 = (bf16[256,512]{1,0:T(8,128)(2,1)S(1)}, bf16[256,512]{1,0:T(8,128)(2,1)S(1)}, u32[]{:S(2)}, u32[]{:S(2)}) collective-permute-start(bf16[256,512]{1,0:T(8,128)(2,1)S(1)} %project_kv.3.refs_5_), channel_id=1, source_target_pairs={{0,8},{8,0},{16,24},{24,16},{1,9},{9,1},{17,25},{25,17},{2,10},{10... | collective-permute-start | bytes 786440 | tf_op jit(solution)/shard_map/ppermute | solution.py:39
  45.5 3.4 %collective-permute-start.19 = (bf16[256,512]{1,0:T(8,128)(2,1)S(1)}, bf16[256,512]{1,0:T(8,128)(2,1)}, u32[]{:S(2)}, u32[]{:S(2)}) collective-permute-start(bf16[256,512]{1,0:T(8,128)(2,1)S(1)} %collective-permute-done.17.refs_3_), channel_id=1, source_target_pairs={{0,8},{8,0},{16,24},{24,16},{1,9},{9,1},{17,25},{25,17},{2,10},{10... | collective-permute-start | bytes 786440 | tf_op jit(solution)/shard_map/ppermute | solution.py:39
  45.5 3.4 %collective-permute-start.15 = (bf16[256,512]{1,0:T(8,128)(2,1)S(1)}, bf16[256,512]{1,0:T(8,128)(2,1)}, u32[]{:S(2)}, u32[]{:S(2)}) collective-permute-start(bf16[256,512]{1,0:T(8,128)(2,1)S(1)} %collective-permute-done.14.refs_3_), channel_id=1, source_target_pairs={{0,8},{8,0},{16,24},{24,16},{1,9},{9,1},{17,25},{25,17},{2,10},{10... | collective-permute-start | bytes 786440 | tf_op jit(solution)/shard_map/ppermute | solution.py:39
  52.9 6.4 %collective-permute-start.20 = (bf16[256,256]{1,0:T(8,128)(2,1)S(1)}, bf16[256,256]{1,0:T(8,128)(2,1)S(1)}, u32[]{:S(2)}, u32[]{:S(2)}) collective-permute-start(bf16[256,256]{1,0:T(8,128)(2,1)S(1)} %get-tuple-element.51), channel_id=1, source_target_pairs={{0,2},{2,4},{4,6},{6,7},{7,5},{5,3},{3,1},{1,0},{8,10},{10,12},{12... | collective-permute-start | bytes 393224 | tf_op jit(solution)/shard_map/ppermute | solution.py:33
  54.5 6.5 %collective-permute-start.24 = (bf16[256,256]{1,0:T(8,128)(2,1)S(1)}, bf16[256,256]{1,0:T(8,128)(2,1)S(1)}, u32[]{:S(2)}, u32[]{:S(2)}) collective-permute-start(bf16[256,256]{1,0:T(8,128)(2,1)S(1)} %get-tuple-element.54), channel_id=1, source_target_pairs={{0,1},{2,0},{4,2},{6,4},{7,6},{5,7},{3,5},{1,3},{8,9},{10,8},{12,1... | collective-permute-start | bytes 393224 | tf_op jit(solution)/shard_map/ppermute | solution.py:33
  54.9 7.1 %collective-permute-start.27 = (bf16[256,256]{1,0:T(8,128)(2,1)S(1)}, bf16[256,256]{1,0:T(8,128)(2,1)S(1)}, u32[]{:S(2)}, u32[]{:S(2)}) collective-permute-start(bf16[256,256]{1,0:T(8,128)(2,1)S(1)} %get-tuple-element.58), channel_id=1, source_target_pairs={{0,2},{2,4},{4,6},{6,7},{7,5},{5,3},{3,1},{1,0},{8,10},{10,12},{12... | collective-permute-start | bytes 393224 | tf_op jit(solution)/shard_map/ppermute | solution.py:33
  56.5 7.2 %collective-permute-start.30 = (bf16[256,256]{1,0:T(8,128)(2,1)S(1)}, bf16[256,256]{1,0:T(8,128)(2,1)S(1)}, u32[]{:S(2)}, u32[]{:S(2)}) collective-permute-start(bf16[256,256]{1,0:T(8,128)(2,1)S(1)} %get-tuple-element.62), channel_id=1, source_target_pairs={{0,1},{2,0},{4,2},{6,4},{7,6},{5,7},{3,5},{1,3},{8,9},{10,8},{12,1... | collective-permute-start | bytes 393224 | tf_op jit(solution)/shard_map/ppermute | solution.py:33
  59.3 6.4 %collective-permute-start.21 = (bf16[256,256]{1,0:T(8,128)(2,1)S(1)}, bf16[256,256]{1,0:T(8,128)(2,1)S(1)}, u32[]{:S(2)}, u32[]{:S(2)}) collective-permute-start(bf16[256,256]{1,0:T(8,128)(2,1)S(1)} %add_convert_fusion.11), channel_id=1, source_target_pairs={{0,2},{2,4},{4,6},{6,7},{7,5},{5,3},{3,1},{1,0},{8,10},{10,12},{12... | collective-permute-start | bytes 393224 | tf_op jit(solution)/shard_map/ppermute | solution.py:33
  61.0 6.4 %collective-permute-start.25 = (bf16[256,256]{1,0:T(8,128)(2,1)S(1)}, bf16[256,256]{1,0:T(8,128)(2,1)S(1)}, u32[]{:S(2)}, u32[]{:S(2)}) collective-permute-start(bf16[256,256]{1,0:T(8,128)(2,1)S(1)} %add_convert_fusion.8), channel_id=1, source_target_pairs={{0,1},{2,0},{4,2},{6,4},{7,6},{5,7},{3,5},{1,3},{8,9},{10,8},{12,1... | collective-permute-start | bytes 393224 | tf_op jit(solution)/shard_map/ppermute | solution.py:33
  62.1 6.4 %collective-permute-start.28 = (bf16[256,256]{1,0:T(8,128)(2,1)S(1)}, bf16[256,256]{1,0:T(8,128)(2,1)S(1)}, u32[]{:S(2)}, u32[]{:S(2)}) collective-permute-start(bf16[256,256]{1,0:T(8,128)(2,1)S(1)} %add_convert_fusion.5), channel_id=1, source_target_pairs={{0,2},{2,4},{4,6},{6,7},{7,5},{5,3},{3,1},{1,0},{8,10},{10,12},{12... | collective-permute-start | bytes 393224 | tf_op jit(solution)/shard_map/ppermute | solution.py:33
  63.8 6.4 %collective-permute-start.31 = (bf16[256,256]{1,0:T(8,128)(2,1)S(1)}, bf16[256,256]{1,0:T(8,128)(2,1)S(1)}, u32[]{:S(2)}, u32[]{:S(2)}) collective-permute-start(bf16[256,256]{1,0:T(8,128)(2,1)S(1)} %add_convert_fusion.3), channel_id=1, source_target_pairs={{0,1},{2,0},{4,2},{6,4},{7,6},{5,7},{3,5},{1,3},{8,9},{10,8},{12,1... | collective-permute-start | bytes 393224 | tf_op jit(solution)/shard_map/ppermute | solution.py:33
  65.7 5.6 %collective-permute-start.22 = (bf16[256,256]{1,0:T(8,128)(2,1)S(1)}, bf16[256,256]{1,0:T(8,128)(2,1)S(1)}, u32[]{:S(2)}, u32[]{:S(2)}) collective-permute-start(bf16[256,256]{1,0:T(8,128)(2,1)S(1)} %add_convert_fusion.10), channel_id=1, source_target_pairs={{0,2},{2,4},{4,6},{6,7},{7,5},{5,3},{3,1},{1,0},{8,10},{10,12},{12... | collective-permute-start | bytes 393224 | tf_op jit(solution)/shard_map/ppermute | solution.py:33
  67.4 9.2 %collective-permute-start.26 = (bf16[256,256]{1,0:T(8,128)(2,1)S(1)}, bf16[256,256]{1,0:T(8,128)(2,1)S(1)}, u32[]{:S(2)}, u32[]{:S(2)}) collective-permute-start(bf16[256,256]{1,0:T(8,128)(2,1)S(1)} %add_convert_fusion.7), channel_id=1, source_target_pairs={{0,1},{2,0},{4,2},{6,4},{7,6},{5,7},{3,5},{1,3},{8,9},{10,8},{12,1... | collective-permute-start | bytes 393224 | tf_op jit(solution)/shard_map/ppermute | solution.py:33
  68.6 8.1 %collective-permute-start.29 = (bf16[256,256]{1,0:T(8,128)(2,1)S(1)}, bf16[256,256]{1,0:T(8,128)(2,1)S(1)}, u32[]{:S(2)}, u32[]{:S(2)}) collective-permute-start(bf16[256,256]{1,0:T(8,128)(2,1)S(1)} %add_convert_fusion.4), channel_id=1, source_target_pairs={{0,2},{2,4},{4,6},{6,7},{7,5},{5,3},{3,1},{1,0},{8,10},{10,12},{12... | collective-permute-start | bytes 393224 | tf_op jit(solution)/shard_map/ppermute | solution.py:33
  70.3 5.9 %collective-permute-start.32 = (bf16[256,256]{1,0:T(8,128)(2,1)S(1)}, bf16[256,256]{1,0:T(8,128)(2,1)S(1)}, u32[]{:S(2)}, u32[]{:S(2)}) collective-permute-start(bf16[256,256]{1,0:T(8,128)(2,1)S(1)} %add_convert_fusion.2), channel_id=1, source_target_pairs={{0,1},{2,0},{4,2},{6,4},{7,6},{5,7},{3,5},{1,3},{8,9},{10,8},{12,1... | collective-permute-start | bytes 393224 | tf_op jit(solution)/shard_map/ppermute | solution.py:33
  71.4 5.3 %collective-permute-start.23 = (bf16[256,256]{1,0:T(8,128)(2,1)S(1)}, bf16[256,256]{1,0:T(8,128)(2,1)S(1)}, u32[]{:S(2)}, u32[]{:S(2)}) collective-permute-start(bf16[256,256]{1,0:T(8,128)(2,1)S(1)} %add_convert_fusion.9), channel_id=1, source_target_pairs={{0,2},{2,4},{4,6},{6,7},{7,5},{5,3},{3,1},{1,0},{8,10},{10,12},{12... | collective-permute-start | bytes 393224 | tf_op jit(solution)/shard_map/ppermute | solution.py:33
  76.2 5.0 %collective-permute-start.33 = (bf16[256,256]{1,0:T(8,128)(2,1)S(1)}, bf16[256,256]{1,0:T(8,128)(2,1)S(1)}, u32[]{:S(2)}, u32[]{:S(2)}) collective-permute-start(bf16[256,256]{1,0:T(8,128)(2,1)S(1)} %add_convert_fusion.1), channel_id=1, source_target_pairs={{0,1},{2,0},{4,2},{6,4},{7,6},{5,7},{3,5},{1,3},{8,9},{10,8},{12,1... | collective-permute-start | bytes 393224 | tf_op jit(solution)/shard_map/ppermute | solution.py:33

commit v10 on v9

v10 whole, which is shorter than its diff:
```python
import functools
import math

import jax
import jax.numpy as jnp
from jax import lax
from jax.experimental import pallas as pl
from jax.experimental.pallas import tpu as pltpu
from jax.sharding import PartitionSpec as P

LOG2E = math.log2(math.e)
VMEM = pl.BlockSpec(memory_space=pltpu.VMEM)
SMEM = pl.BlockSpec(memory_space=pltpu.SMEM)
F32 = jnp.float32
BF16 = jnp.bfloat16


def ring_order(count):
    line = count // 2
    return [2 * z for z in range(line)] + [2 * z + 1 for z in reversed(range(line))]


def ring_place(index, count):
    return jnp.where(index % 2 == 0, index // 2, count - 1 - index // 2)


def ring_index(place, count):
    return jnp.where(place < count // 2, 2 * place, 2 * (count - 1 - place) + 1)


def along(value, step, count):
    order = ring_order(count)
    return lax.ppermute(
        value, "head", [(order[p], order[(p + step) % count]) for p in range(count)]
    )


def swapped(value, seq_count):
    return lax.ppermute(value, "seq", [(seq, seq + 1 - 2 * (seq % 2)) for seq in range(seq_count)])


def in_hbm(value):
    return pltpu.with_memory_space_constraint(value, pltpu.HBM)


def in_vmem(value):
    return pltpu.with_memory_space_constraint(value, pltpu.VMEM)


def fold_kernel(order, groups, has_tokens, at, gain_ref, w_hbm, *refs):
    sems = refs[-1]
    out_ref = refs[1] if has_tokens else refs[0]
    lanes = gain_ref.shape[1]
    size = w_hbm.shape[1] // len(order)
    per = size // lanes

    def fetch(n):
        start = pl.multiple_of(at[order[n]] * size, size)
        return pltpu.make_async_copy(
            w_hbm.at[groups[0] : groups[0] + len(groups), pl.ds(start, size), :],
            out_ref.at[:, n * size : (n + 1) * size, :],
            sems.at[n],
        )

    for n in range(len(order)):
        fetch(n).start()
    if has_tokens:
        tokens, wide = refs[0], refs[2]
        own = pltpu.make_async_copy(tokens, wide.at[:, : tokens.shape[1]], sems.at[len(order)])
        own.start()
    for n in range(len(order)):
        columns = jnp.transpose(gain_ref[pl.ds(at[order[n]] * per, per), :])
        fetch(n).wait()
        for piece in range(per):
            first = n * size + piece * lanes
            for group in range(len(groups)):
                here = (group, slice(first, first + lanes), slice(None))
                scaled = out_ref[here].astype(F32) * columns[:, piece : piece + 1]
                out_ref[here] = scaled.astype(BF16)
    if has_tokens:
        own.wait()


def fold_gain(order, groups, at, gain, weights, tokens=None):
    depth, width = weights.shape[1:]
    lanes = math.gcd(depth // len(order), 128)
    hbm = pl.BlockSpec(memory_space=pltpu.HBM)
    operands = [at, in_hbm(gain.reshape(depth // lanes, lanes)), in_hbm(weights)]
    shapes, specs = [pltpu.VMEM((len(groups), depth, width), BF16)], [VMEM]
    if tokens is not None:
        operands.append(in_hbm(tokens))
        shapes.append(pltpu.VMEM((tokens.shape[0], depth), BF16))
        specs.append(pl.BlockSpec(memory_space=pl.ANY))
    size = len(groups) * depth * width
    return pl.pallas_call(
        functools.partial(fold_kernel, order, groups, tokens is not None),
        out_shape=tuple(shapes),
        in_specs=[SMEM, VMEM, hbm] + [hbm] * (len(operands) - 3),
        out_specs=tuple(specs),
        scratch_shapes=[pltpu.SemaphoreType.DMA((len(order) + 1,))],
        compiler_params=pltpu.CompilerParams(vmem_limit_bytes=16 << 20),
        cost_estimate=pl.CostEstimate(flops=size, bytes_accessed=4 * size, transcendentals=0),
        name="fold_gain",
    )(*operands)


def place_kernel(targets, *refs):
    blocks, wide, sems = refs[: len(targets)], refs[-2], refs[-1]
    copies = []
    for n, (block, (row, lane)) in enumerate(zip(blocks, targets)):
        rows, width = block.shape
        here = wide.at[row : row + rows, lane : lane + width]
        copies.append(pltpu.make_async_copy(block, here, sems.at[n]))
    for copy in copies:
        copy.start()
    for copy in copies:
        copy.wait()


def placed(targets, blocks, wide):
    operands = [*map(in_vmem, blocks), in_vmem(wide)]
    return pl.pallas_call(
        functools.partial(place_kernel, targets),
        out_shape=pltpu.VMEM(wide.shape, BF16),
        in_specs=[pl.BlockSpec(memory_space=pl.ANY)] * len(operands),
        out_specs=pl.BlockSpec(memory_space=pl.ANY),
        scratch_shapes=[pltpu.SemaphoreType.DMA((len(targets),))],
        input_output_aliases={len(blocks): 0},
        compiler_params=pltpu.CompilerParams(vmem_limit_bytes=1 << 20),
        cost_estimate=pl.CostEstimate(flops=0, bytes_accessed=1 << 20, transcendentals=0),
        name="place",
    )(*operands)


def unit_rows(values, factor):
    power = jnp.sum(values * values, axis=-1, keepdims=True)
    return (values * (lax.rsqrt(power + 1e-06) * factor)).astype(BF16)


def project_kernel(head_size, base, groups, factor, wide, w_ref, out_ref):
    rows = out_ref.shape[0]
    depth, out_width = w_ref.shape[1:]
    tile = math.gcd(rows, 256)
    for first in range(0, rows, tile):
        here = slice(first, first + tile)
        there = slice(base + first, base + first + tile)
        power = None
        for lane in range(0, depth, 128):
            values = wide[there, lane : lane + 128].astype(F32)
            power = values * values if power is None else power + values * values
        scale = lax.rsqrt(jnp.sum(power, axis=-1, keepdims=True) * (1.0 / depth) + 1e-06)
        for number, group in enumerate(groups):
            start = number * out_width
            product = jnp.dot(wide[there, :], w_ref[number], preferred_element_type=F32) * scale
            if group == 2:
                out_ref[here, start : start + out_width] = product.astype(BF16)
                continue
            for head in range(out_width // head_size):
                lanes = slice(head * head_size, (head + 1) * head_size)
                amount = factor[head] * LOG2E if group == 0 else 1.0
                out_ref[here, start + head * head_size : start + (head + 1) * head_size] = unit_rows(
                    product[:, lanes], amount
                )


def project(factor, wide, weights, base, rows, groups, head_size):
    depth, out_width = weights.shape[1:]
    return pl.pallas_call(
        functools.partial(project_kernel, head_size, base, groups),
        out_shape=pltpu.VMEM((rows, len(groups) * out_width), BF16),
        in_specs=[SMEM] + [VMEM] * 2,
        out_specs=VMEM,
        compiler_params=pltpu.CompilerParams(vmem_limit_bytes=16 << 20),
        cost_estimate=pl.CostEstimate(
            flops=2 * rows * depth * len(groups) * out_width,
            bytes_accessed=2 * depth * (rows + len(groups) * out_width),
            transcendentals=0,
        ),
        name="project_q" if groups == (0,) else "project_kv",
    )(in_hbm(factor), in_vmem(wide), in_vmem(weights))


def attend_blocks(sources, ids, q_first, q_ref, id_col, id_row, kv_refs, v_ones, acc, head_size):
    rows, width = q_ref.shape
    heads = width // head_size
    keys = kv_refs[0].shape[0]
    piece = id_row.shape[2]
    tile = math.gcd(rows, 256)
    for number, kv_ref in enumerate(kv_refs):
        for head in range(heads):
            start = (heads + head) * head_size
            v_ones[head, :, :head_size] = kv_ref[:, start : start + head_size]
            v_ones[head, :, head_size:] = jnp.ones((keys, head_size), BF16)
        first = sources[number]
        key_low, key_high = ids[first], ids[first + keys - 1]

        @pl.loop(0, rows // tile)
        def _(index):
            base = pl.multiple_of(index * tile, tile)
            here = pl.ds(base, tile)
            q_low, q_high = ids[q_first + base], ids[q_first + base + tile - 1]

            def add(low, high, masked):
                if masked:
                    allowed = id_row[first // piece + low // piece] <= id_col[here, :]
                for head in range(heads):
                    lanes = slice(head * head_size, (head + 1) * head_size)
                    score = lax.dot_general(
                        q_ref[here, lanes],
                        kv_ref[low:high, lanes],
                        (((1,), (1,)), ((), ())),
                        preferred_element_type=F32,
                    )
                    weight = jnp.exp2(score)
                    if masked:
                        weight = jnp.where(allowed, weight, 0.0)
                    spread = slice(2 * head * head_size, 2 * (head + 1) * head_size)
                    acc[here, spread] += jnp.dot(
                        weight.astype(BF16), v_ones[head, low:high, :], preferred_element_type=F32
                    )

            @pl.when(key_high <= q_low)
            def _():
                add(0, keys, False)

            @pl.when((key_high > q_low) & (key_low <= q_high))
            def _():
                for low in range(0, keys, piece):
                    piece_low, piece_high = ids[first + low], ids[first + low + piece - 1]

                    @pl.when(piece_high <= q_low)
                    def _():
                        add(low, low + piece, False)

                    @pl.when((piece_high > q_low) & (piece_low <= q_high))
                    def _():
                        add(low, low + piece, True)


def attend_kernel(
    count_kv, head_size, has_acc, count_out, count_streams, info, ids, q_ref, id_col, id_row, *refs
):
    kv_refs, rest = refs[:count_kv], refs[count_kv:]
    width = q_ref.shape[1]
    if has_acc:
        acc_in, rest = rest[0], rest[1:]
    if count_out:
        w_ref, outs, (v_ones, acc, attended) = rest[0], rest[1:-3], rest[-3:]
    else:
        acc_out, v_ones, acc = rest
    acc[...] = acc_in[...] if has_acc else jnp.zeros_like(acc)
    sources = [info[number] for number in range(count_kv)]
    attend_blocks(
        sources, ids, info[count_kv], q_ref, id_col, id_row, kv_refs, v_ones, acc, head_size
    )
    if not count_out:
        acc_out[...] = acc[...]
        return
    for head in range(width // head_size):
        start = 2 * head * head_size
        attended[:, head * head_size : (head + 1) * head_size] = (
            acc[:, start : start + head_size]
            / acc[:, start + head_size : start + 2 * head_size]
        ).astype(BF16)
    out_width = outs[0].shape[1]
    for number, out in enumerate(outs):
        lane = info[count_kv + 1 + number] * out_width
        first = number * count_streams // count_out * out.shape[0]
        out[...] = jnp.dot(
            attended[first : first + out.shape[0], :],
            w_ref[:, pl.ds(pl.multiple_of(lane, out_width), out_width)],
            preferred_element_type=F32,
        ).astype(BF16)


def attend(info, ids, query, id_col, id_row, kvs, head_size, acc=None, w_out=None, streams=0):
    total, width = query.shape
    keys = kvs[0].shape[0]
    heads = width // head_size
    count_out = streams * w_out.shape[1] // width if streams else 0
    scratch = [
        pltpu.VMEM((heads, keys, 2 * head_size), BF16),
        pltpu.VMEM((total, 2 * width), F32),
    ]
    operands = [in_vmem(query), id_col, in_hbm(id_row), *map(in_vmem, kvs)]
    if acc is not None:
        operands.append(in_vmem(acc))
    if count_out:
        operands.append(in_hbm(w_out))
        scratch.append(pltpu.VMEM((total, width), BF16))
        shape = pltpu.VMEM((total // streams, w_out.shape[1] * streams // count_out), BF16)
    else:
        shape = pltpu.VMEM((total, 2 * width), F32)
    outs = count_out or 1
    return pl.pallas_call(
        functools.partial(
            attend_kernel, len(kvs), head_size, acc is not None, count_out, streams
        ),
        out_shape=(shape,) * outs,
        in_specs=[SMEM, SMEM] + [VMEM] * len(operands),
        out_specs=(VMEM,) * outs,
        scratch_shapes=scratch,
        compiler_params=pltpu.CompilerParams(
            vmem_limit_bytes=(16 << 20) + 2 * kvs[0].size * 2 * len(kvs)
        ),
        cost_estimate=pl.CostEstimate(flops=1 << 20, bytes_accessed=1 << 10, transcendentals=0),
        name="attend_last" if count_out else "attend",
    )(info, in_hbm(ids), *operands)


def total_of(*parts):
    return sum(part.astype(F32) for part in parts).astype(BF16)


def body(mesh_shape, tokens, norm_gain, w_qkv, head_scale, w_out, scale_ids):
    ring, seqs = mesh_shape["head"], mesh_shape["seq"]
    outer = seqs // 2
    rows, width = tokens.shape
    half = rows // 2
    head_size = w_qkv.shape[2] // head_scale.shape[0]
    head_at, seq_at = lax.axis_index("head"), lax.axis_index("seq")
    place = ring_place(head_at, ring)
    chip, core = seq_at // 2, seq_at % 2
    index_at = lambda offset: ring_index((place + offset + ring) % ring, ring)
    numbers = lambda values: jnp.stack(values).astype(jnp.int32)
    id_row = scale_ids.reshape(-1, 1, half)
    id_col = lax.dynamic_slice_in_dim(scale_ids, seq_at * rows, rows)[:, None]
    at = [index_at(offset) for offset in range(ring)]

    streams = (0, 1)
    farthest = ring // 2
    reach = [(farthest, farthest - 1), (farthest - 1, farthest)]
    lanes = ((0, 0, 1), (1, 1, -1), (0, 1, -1), (1, 0, 1))

    order = [0] + [sign * step % ring for step in range(1, farthest) for sign in (-1, 1)] + [farthest]
    held = [[tokens[s * half : (s + 1) * half]] * 2 for s in streams]
    wide, blocks, targets = None, [], []
    for step in range(1, farthest + 1):
        for s, way, sign in lanes:
            if step <= reach[s][way]:
                held[s][way] = along(held[s][way], sign, ring)
        if step == 1:
            held[0][0], (w_kv, wide) = lax.optimization_barrier(
                (held[0][0], fold_gain(order, (1, 2), numbers(at), norm_gain, w_qkv, tokens))
            )
        elif step == 2:
            held[0][0], (w_q,) = lax.optimization_barrier(
                (held[0][0], fold_gain(order, (0,), numbers(at), norm_gain, w_qkv))
            )
        if blocks:
            wide = placed(targets, blocks, wide)
        columns = [(2 * step - 1 + way) * width for way in (0, 1)]
        if step == farthest:
            columns = [(ring - 1) * width] * 2
        blocks = [held[s][way] for s, way, sign in lanes if step <= reach[s][way]]
        targets = [(s * half, columns[way]) for s, way, sign in lanes if step <= reach[s][way]]
    wide = placed(targets, blocks, wide)
    kv = project(head_scale, wide, w_kv, 0, rows, (1, 2), head_size)
    query = project(head_scale, wide, w_q, 0, rows, (0,), head_size)

    far, straight, crossed = [], [], []
    for step in range(outer):
        source = 2 * ((chip + outer - step) % outer)
        straight.append((source + core) * rows)
        crossed.append((source + 1 - core) * rows)
        if step:
            far.append(lax.ppermute(kv, "seq", [
                (2 * a + b, 2 * ((a + step) % outer) + b) for a in range(outer) for b in (0, 1)
            ]))
    first = [seq_at * rows]
    info = numbers(straight[:1] + crossed[:1] + first)
    keys = [kv, swapped(kv, seqs)]
    (acc,) = attend(info, scale_ids, query, id_col, id_row, keys, head_size)
    acc, far = lax.optimization_barrier((acc, far))
    far_crossed = [swapped(block, seqs) for block in far]
    info = numbers(straight[1:] + first)
    (acc,) = attend(info, scale_ids, query, id_col, id_row, far, head_size, acc)

    goals = [[*range(up, 0, -1), *range(-down, 0), 0] for up, down in reach]
    info = numbers(crossed[1:] + first + [at[goal % ring] for goal in goals[0] + goals[1]])
    parts = attend(
        info, scale_ids, query, id_col, id_row, far_crossed, head_size, acc, w_out, len(streams)
    )
    parts = [dict(zip(goals[s], parts[s * ring : (s + 1) * ring])) for s in streams]
    sums = [[None, None] for s in streams]
    for step in range(farthest, 0, -1):
        for s, way, sign in lanes:
            if step <= reach[s][way]:
                part = parts[s][sign * step]
                if sums[s][way] is not None:
                    part = total_of(part, sums[s][way])
                sums[s][way] = along(part, sign, ring)
    ends = lax.optimization_barrier([sums[s][way] for s, way, sign in lanes[::-1]])
    for (s, way, sign), end in zip(lanes[::-1], ends):
        sums[s][way] = end
    return jnp.concatenate([total_of(parts[s][0], *sums[s]) for s in streams])


def solution(mesh):
    placed = (P("seq", "head"), P(), P(None, None, "head"), P("head"), P("head", None), P())
    return jax.shard_map(
        functools.partial(body, dict(mesh.shape)),
        mesh=mesh,
        in_specs=placed,
        out_specs=P("seq", "head"),
        check_vma=False,
    )
```

time: 82.5 us -> 80.9 us (0.981)
  starting transfers between devices: 32 us -> 28.3 us
  local copies, waits for them, and re-layouts: 2.22 us -> 3.48 us
    ppermute x2 -> x1, waiting for transfers between devices: 3.32 us -> 6.3 us  [body(): lax.ppermute(kv, 'seq', [(2 * a + b, 2 * ((a + step) % outer) + b) for a...]
    ppermute x28, waiting for transfers between devices: 20.5 us -> 18.3 us  [along(): lax.ppermute(value, 'head', [(order[p], order[(p + step) % count]) for p...]
    ppermute x2 -> x1, starting transfers between devices: 2.16 us -> 0.53 us  [body(): lax.ppermute(kv, 'seq', [(2 * a + b, 2 * ((a + step) % outer) + b) for a...]
    ppermute x28, starting transfers between devices: 29.3 us -> 27.8 us  [along(): lax.ppermute(value, 'head', [(order[p], order[(p + step) % count]) for p...]
    pallas_call x5 -> x4, Pallas kernels: 2.46 us -> 1.26 us  [placed(): pl.pallas_call(functools.partial(place_kernel, targets), out_shape=pltpu....]
    pallas_call x5, Pallas kernels: 15 us -> 16 us  [the longest x3 10 us: attend(): pl.pallas_call(functools.partial(attend_kernel, len(kvs), head_size, acc...]
    pallas_call x3 -> x2, Pallas kernels: 4.77 us -> 4.87 us  [project(): pl.pallas_call(functools.partial(project_kernel, head_size, base, groups)...]
  transfers between devices with their start and end apart: 34 -> 31, of which waited for: 12 -> 14; matrix products, arithmetic and copies ran while one was open for 2% -> 3% of each run, Pallas kernels for 22% -> 20%
where the time goes in v10:
time: 80.9 us; the launch traced here: 80.1 us
  starting transfers between devices  28.3 us (35%)
  waiting for transfers between devices  24.6 us (30%)
  Pallas kernels  22.2 us (27%)
  local copies, waits for them, and re-layouts  3.48 us (4%)
  other arithmetic  1.32 us (2%)
    ppermute x28, starting transfers between devices, along(): lax.ppermute(value, 'head', [(order[p], order[(p + step) % count]) for p...  27.8 us
    ppermute x28, waiting for transfers between devices, along(): lax.ppermute(value, 'head', [(order[p], order[(p + step) % count]) for p...  18.3 us
    pallas_call x3, Pallas kernels, attend(): pl.pallas_call(functools.partial(attend_kernel, len(kvs), head_size, acc...  10 us
    ppermute x1, waiting for transfers between devices, body(): lax.ppermute(kv, 'seq', [(2 * a + b, 2 * ((a + step) % outer) + b) for a...  6.3 us
    pallas_call x2, Pallas kernels, fold_gain(): pl.pallas_call(functools.partial(fold_kernel, order, groups, tokens is no...  6.02 us
    pallas_call x2, Pallas kernels, project(): pl.pallas_call(functools.partial(project_kernel, head_size, base, groups)...  4.87 us
    slice x1, local copies, waits for them, and re-layouts, body(): held = [[tokens[s * half:(s + 1) * half]] * 2 for s in streams]  1.68 us
  transfers between devices with their start and end apart: 31, of which 14 were waited for; matrix products, arithmetic and copies ran while one was open for 3% of the time, Pallas kernels for 20%

profile of v10, /device:TPU:10, one launch (start us, length us, event | category | flops | bytes accessed | tf_op | source)
XLA Modules:
  0.0 80.1 jit_solution(2251649230829290130)
XLA Ops:
  0.0 1.7 %fusion = (bf16[256,256]{1,0:T(8,128)(2,1)}, bf16[256,256]{1,0:T(8,128)(2,1)}) fusion(bf16[512,256]{1,0:T(8,128)(2,1)} %refs_0_.1), kind=kLoop, calls=%fused_computation.15 | loop fusion | bytes 524288 | tf_op jit(solution)/shard_map/slice | solution.py:336
  1.7 1.6 %collective-permute-start = (bf16[256,256]{1,0:T(8,128)(2,1)}, bf16[256,256]{1,0:T(8,128)(2,1)S(1)}, u32[]{:S(2)}, u32[]{:S(2)}) collective-permute-start(bf16[256,256]{1,0:T(8,128)(2,1)} %get-tuple-element.64), channel_id=1, source_target_pairs={{0,2},{2,4},{4,6},{6,7},{7,5},{5,3},{3,1},{1,0},{8,10},{10,12},{12... | collective-permute-start | bytes 393224 | tf_op jit(solution)/shard_map/ppermute | solution.py:33
  3.3 0.4 collective-permute-start.4
  3.7 1.6 %collective-permute-start.11 = (bf16[256,256]{1,0:T(8,128)(2,1)}, bf16[256,256]{1,0:T(8,128)(2,1)S(1)}, u32[]{:S(2)}, u32[]{:S(2)}) collective-permute-start(bf16[256,256]{1,0:T(8,128)(2,1)} %get-tuple-element.63), channel_id=1, source_target_pairs={{0,2},{2,4},{4,6},{6,7},{7,5},{5,3},{3,1},{1,0},{8,10},{10,12},{12... | collective-permute-start | bytes 393224 | tf_op jit(solution)/shard_map/ppermute | solution.py:33
  5.3 0.4 collective-permute-start.8
  5.8 3.0 %fold_gain.2 = (bf16[2,2048,256]{2,1,0:T(8,128)(2,1)S(1)}, bf16[512,2048]{1,0:T(8,128)(2,1)S(1)}) custom-call(s32[8]{0:T(128)S(1)} %stack.89.at, f32[16,128]{1,0:T(8,128)} %bitcast.19, bf16[3,2048,256]{2,1,0:T(8,128)(2,1)} %w_hbm.3, bf16[512,256]{1,0:T(8,128)(2,1)} %refs_0_.1), custom_call_target="tpu_custom_call" | custom-call | flops 1048576 | bytes 4194304 | tf_op jit(solution)/shard_map/fold_gain/pallas_call | solution.py:95
  8.9 1.6 %collective-permute-start.1 = (bf16[256,256]{1,0:T(8,128)(2,1)S(1)}, bf16[256,256]{1,0:T(8,128)(2,1)S(1)}, u32[]{:S(2)}, u32[]{:S(2)}) collective-permute-start(bf16[256,256]{1,0:T(8,128)(2,1)S(1)} %collective-permute-done.refs_0_), channel_id=1, source_target_pairs={{0,2},{2,4},{4,6},{6,7},{7,5},{5,3},{3,1},{1,0},{8,10},{10,12},{12... | collective-permute-start | bytes 393224 | tf_op jit(solution)/shard_map/ppermute | solution.py:33
  10.5 0.4 collective-permute-start.5
  11.0 3.0 %fold_gain.3.w_ref = bf16[1,2048,256]{2,1,0:T(8,128)(2,1)S(1)} custom-call(s32[8]{0:T(128)S(1)} %stack.89.at, f32[16,128]{1,0:T(8,128)} %bitcast.20, bf16[3,2048,256]{2,1,0:T(8,128)(2,1)} %w_hbm.3), custom_call_target="tpu_custom_call" | custom-call | flops 524288 | bytes 2097152 | tf_op jit(solution)/shard_map/fold_gain/pallas_call | solution.py:95
  13.9 1.6 %collective-permute-start.12 = (bf16[256,256]{1,0:T(8,128)(2,1)S(1)}, bf16[256,256]{1,0:T(8,128)(2,1)S(1)}, u32[]{:S(2)}, u32[]{:S(2)}) collective-permute-start(bf16[256,256]{1,0:T(8,128)(2,1)S(1)} %collective-permute-done.11.refs_3_), channel_id=1, source_target_pairs={{0,2},{2,4},{4,6},{6,7},{7,5},{5,3},{3,1},{1,0},{8,10},{10,12},{12... | collective-permute-start | bytes 393224 | tf_op jit(solution)/shard_map/ppermute | solution.py:33
  15.6 0.4 collective-permute-start.9
  16.0 1.6 %collective-permute-start.2 = (bf16[256,256]{1,0:T(8,128)(2,1)S(1)}, bf16[256,256]{1,0:T(8,128)(2,1)S(1)}, u32[]{:S(2)}, u32[]{:S(2)}) collective-permute-start(bf16[256,256]{1,0:T(8,128)(2,1)S(1)} %collective-permute-done.1.refs_0_), channel_id=1, source_target_pairs={{0,2},{2,4},{4,6},{6,7},{7,5},{5,3},{3,1},{1,0},{8,10},{10,12},{12... | collective-permute-start | bytes 393224 | tf_op jit(solution)/shard_map/ppermute | solution.py:33
  17.6 0.4 collective-permute-start.6
  18.1 3.1 %collective-permute-done.9.refs_2_ = bf16[256,256]{1,0:T(8,128)(2,1)S(1)} collective-permute-done((bf16[256,256]{1,0:T(8,128)(2,1)}, bf16[256,256]{1,0:T(8,128)(2,1)S(1)}, u32[]{:S(2)}, u32[]{:S(2)}) %collective-permute-start.9) | collective-permute-done | bytes 131104 | tf_op jit(solution)/shard_map/ppermute | solution.py:33
  21.1 0.4 collective-permute-start.10
  21.6 1.6 %collective-permute-start.13 = (bf16[256,256]{1,0:T(8,128)(2,1)S(1)}, bf16[256,256]{1,0:T(8,128)(2,1)S(1)}, u32[]{:S(2)}, u32[]{:S(2)}) collective-permute-start(bf16[256,256]{1,0:T(8,128)(2,1)S(1)} %collective-permute-done.12.refs_3_), channel_id=1, source_target_pairs={{0,2},{2,4},{4,6},{6,7},{7,5},{5,3},{3,1},{1,0},{8,10},{10,12},{12... | collective-permute-start | bytes 393224 | tf_op jit(solution)/shard_map/ppermute | solution.py:33
  23.2 1.6 %collective-permute-start.3 = (bf16[256,256]{1,0:T(8,128)(2,1)S(1)}, bf16[256,256]{1,0:T(8,128)(2,1)S(1)}, u32[]{:S(2)}, u32[]{:S(2)}) collective-permute-start(bf16[256,256]{1,0:T(8,128)(2,1)S(1)} %collective-permute-done.2.refs_0_), channel_id=1, source_target_pairs={{0,2},{2,4},{4,6},{6,7},{7,5},{5,3},{3,1},{1,0},{8,10},{10,12},{12... | collective-permute-start | bytes 393224 | tf_op jit(solution)/shard_map/ppermute | solution.py:33
  24.8 0.5 collective-permute-start.7
  25.2 1.0 %place.4.refs_4_ = bf16[512,2048]{1,0:T(8,128)(2,1)S(1)} custom-call(bf16[256,256]{1,0:T(8,128)(2,1)S(1)} %collective-permute-done.refs_0_, bf16[256,256]{1,0:T(8,128)(2,1)S(1)} %collective-permute-done.4.refs_1_, bf16[256,256]{1,0:T(8,128)(2,1)} %collective-permute-done.8.refs_2_, ...), custom_call_target="tpu_custom_call", output_to_operand_aliasing={{}: (4, {})} | custom-call | bytes 1048576 | tf_op jit(solution)/shard_map/place/pallas_call | solution.py:122
  26.7 1.5 %collective-permute-done.3.refs_0_ = bf16[256,256]{1,0:T(8,128)(2,1)S(1)} collective-permute-done((bf16[256,256]{1,0:T(8,128)(2,1)S(1)}, bf16[256,256]{1,0:T(8,128)(2,1)S(1)}, u32[]{:S(2)}, u32[]{:S(2)}) %collective-permute-start.3) | collective-permute-done | bytes 131104 | tf_op jit(solution)/shard_map/ppermute | solution.py:33
  28.1 1.6 %collective-permute-done.7.refs_1_ = bf16[256,256]{1,0:T(8,128)(2,1)S(1)} collective-permute-done((bf16[256,256]{1,0:T(8,128)(2,1)S(1)}, bf16[256,256]{1,0:T(8,128)(2,1)S(1)}, u32[]{:S(2)}, u32[]{:S(2)}) %collective-permute-start.7) | collective-permute-done | bytes 131104 | tf_op jit(solution)/shard_map/ppermute | solution.py:33
  29.8 3.1 %project_kv.1.refs_0_ = bf16[512,512]{1,0:T(8,128)(2,1)} custom-call(f32[2]{0:T(128)} %factor.3, bf16[512,2048]{1,0:T(8,128)(2,1)S(1)} %place.7.wide, bf16[2,2048,256]{2,1,0:T(8,128)(2,1)S(1)} %get-tuple-element.40.w_ref), custom_call_target="tpu_custom_call" | custom-call | flops 1073741824 | bytes 4194304 | tf_op jit(solution)/shard_map/project_kv/pallas_call | solution.py:168
  32.9 0.5 collective-permute-start.15
  33.5 0.8 dynamic_slice.3
  34.2 0.9 %copy.13.id_col = s32[512,1]{1,0:T(8,128)} copy(s32[512,1]{0,1:T(1,128)S(1)} %bitcast.21) | data formatting | bytes 4096 | tf_op jit(solution)/shard_map/broadcast_in_dim | solution.py:327
  35.2 1.7 %project_q.1.q_ref = bf16[512,256]{1,0:T(8,128)(2,1)S(1)} custom-call(f32[2]{0:T(128)} %factor.3, bf16[512,2048]{1,0:T(8,128)(2,1)S(1)} %place.7.wide, bf16[1,2048,256]{2,1,0:T(8,128)(2,1)S(1)} %fold_gain.3.w_ref), custom_call_target="tpu_custom_call" | custom-call | flops 536870912 | bytes 3145728 | tf_op jit(solution)/shard_map/project_q/pallas_call | solution.py:168
  36.9 4.3 %attend.2.refs_1_ = f32[512,512]{1,0:T(8,128)S(1)} custom-call(s32[3]{0:T(128)S(1)} %pad_add_fusion.info, s32[2048]{0:T(1024)} %ids.5, bf16[512,256]{1,0:T(8,128)(2,1)S(1)} %project_q.1.q_ref, s32[512,1]{1,0:T(8,128)S(1)} %copy-done, s32[8,1,256]{2,1,0:T(1,128)} %bitcast.16, bf16[512,512]{1,0:T(8,128)(2,1)} %project_kv.1.refs_0_, ...), custom_call_target="tpu_custom_call" | custom-call | flops 1048576 | bytes 1024 | tf_op jit(solution)/shard_map/attend/pallas_call | solution.py:295
  41.3 6.3 %collective-permute-done.15.refs_0_ = bf16[512,512]{1,0:T(8,128)(2,1)} collective-permute-done((bf16[512,512]{1,0:T(8,128)(2,1)}, bf16[512,512]{1,0:T(8,128)(2,1)}, u32[]{:S(2)}, u32[]{:S(2)}) %collective-permute-start.15) | collective-permute-done | bytes 524320 | tf_op jit(solution)/shard_map/ppermute | solution.py:367
  47.8 2.4 %attend.3.refs_1_ = f32[512,512]{1,0:T(8,128)S(1)} custom-call(s32[2]{0:T(128)S(1)} %pad_add_fusion.1.info, s32[2048]{0:T(1024)} %ids.5, bf16[512,256]{1,0:T(8,128)(2,1)S(1)} %project_q.1.q_ref, s32[512,1]{1,0:T(8,128)S(1)} %copy-done.1, s32[8,1,256]{2,1,0:T(1,128)} %bitcast.17, bf16[512,512]{1,0:T(8,128)(2,1)} %collective-permute-done.15.refs_0_, ...), custom_call_target="tpu_custom_call" | custom-call | flops 1048576 | bytes 1024 | tf_op jit(solution)/shard_map/attend/pallas_call | solution.py:295
  50.2 3.3 %attend_last.1 = (bf16[256,256]{1,0:T(8,128)(2,1)S(1)}, bf16[256,256]{1,0:T(8,128)(2,1)S(1)}, bf16[256,256]{1,0:T(8,128)(2,1)S(1)}, bf16[256,256]{1,0:T(8,128)(2...) custom-call(s32[18]{0:T(128)S(1)} %stack.88.info, ...), custom_call_target="tpu_custom_call" | custom-call | flops 1048576 | bytes 1024 | tf_op jit(solution)/shard_map/attend_last/pallas_call | solution.py:295
  53.5 1.9 %collective-permute-start.27 = (bf16[256,256]{1,0:T(8,128)(2,1)S(1)}, bf16[256,256]{1,0:T(8,128)(2,1)S(1)}, u32[]{:S(2)}, u32[]{:S(2)}) collective-permute-start(bf16[256,256]{1,0:T(8,128)(2,1)S(1)} %get-tuple-element.57), channel_id=1, source_target_pairs={{0,2},{2,4},{4,6},{6,7},{7,5},{5,3},{3,1},{1,0},{8,10},{10,12},{12... | collective-permute-start | bytes 393224 | tf_op jit(solution)/shard_map/ppermute | solution.py:33
  56.0 1.6 %collective-permute-start.17 = (bf16[256,256]{1,0:T(8,128)(2,1)S(1)}, bf16[256,256]{1,0:T(8,128)(2,1)S(1)}, u32[]{:S(2)}, u32[]{:S(2)}) collective-permute-start(bf16[256,256]{1,0:T(8,128)(2,1)S(1)} %get-tuple-element.46), channel_id=1, source_target_pairs={{0,2},{2,4},{4,6},{6,7},{7,5},{5,3},{3,1},{1,0},{8,10},{10,12},{12... | collective-permute-start | bytes 393224 | tf_op jit(solution)/shard_map/ppermute | solution.py:33
  57.6 2.2 %collective-permute-done.27 = bf16[256,256]{1,0:T(8,128)(2,1)S(1)} collective-permute-done((bf16[256,256]{1,0:T(8,128)(2,1)S(1)}, bf16[256,256]{1,0:T(8,128)(2,1)S(1)}, u32[]{:S(2)}, u32[]{:S(2)}) %collective-permute-start.27) | collective-permute-done | bytes 131104 | tf_op jit(solution)/shard_map/ppermute | solution.py:33
  59.9 1.9 %collective-permute-start.28 = (bf16[256,256]{1,0:T(8,128)(2,1)S(1)}, bf16[256,256]{1,0:T(8,128)(2,1)S(1)}, u32[]{:S(2)}, u32[]{:S(2)}) collective-permute-start(bf16[256,256]{1,0:T(8,128)(2,1)S(1)} %add_convert_fusion.4), channel_id=1, source_target_pairs={{0,2},{2,4},{4,6},{6,7},{7,5},{5,3},{3,1},{1,0},{8,10},{10,12},{12... | collective-permute-start | bytes 393224 | tf_op jit(solution)/shard_map/ppermute | solution.py:33
  62.0 2.0 %collective-permute-done.20 = bf16[256,256]{1,0:T(8,128)(2,1)S(1)} collective-permute-done((bf16[256,256]{1,0:T(8,128)(2,1)S(1)}, bf16[256,256]{1,0:T(8,128)(2,1)S(1)}, u32[]{:S(2)}, u32[]{:S(2)}) %collective-permute-start.20) | collective-permute-done | bytes 131104 | tf_op jit(solution)/shard_map/ppermute | solution.py:33
  64.5 1.8 %collective-permute-start.18 = (bf16[256,256]{1,0:T(8,128)(2,1)S(1)}, bf16[256,256]{1,0:T(8,128)(2,1)S(1)}, u32[]{:S(2)}, u32[]{:S(2)}) collective-permute-start(bf16[256,256]{1,0:T(8,128)(2,1)S(1)} %add_convert_fusion.11), channel_id=1, source_target_pairs={{0,2},{2,4},{4,6},{6,7},{7,5},{5,3},{3,1},{1,0},{8,10},{10,12},{12... | collective-permute-start | bytes 393224 | tf_op jit(solution)/shard_map/ppermute | solution.py:33
  66.3 0.8 %collective-permute-start.29 = (bf16[256,256]{1,0:T(8,128)(2,1)S(1)}, bf16[256,256]{1,0:T(8,128)(2,1)S(1)}, u32[]{:S(2)}, u32[]{:S(2)}) collective-permute-start(bf16[256,256]{1,0:T(8,128)(2,1)S(1)} %add_convert_fusion.3), channel_id=1, source_target_pairs={{0,2},{2,4},{4,6},{6,7},{7,5},{5,3},{3,1},{1,0},{8,10},{10,12},{12... | collective-permute-start | bytes 393224 | tf_op jit(solution)/shard_map/ppermute | solution.py:33
  67.1 0.7 collective-permute-done.24
  67.8 0.6 collective-permute-start.25
  68.5 2.1 %collective-permute-done.21 = bf16[256,256]{1,0:T(8,128)(2,1)S(1)} collective-permute-done((bf16[256,256]{1,0:T(8,128)(2,1)S(1)}, bf16[256,256]{1,0:T(8,128)(2,1)S(1)}, u32[]{:S(2)}, u32[]{:S(2)}) %collective-permute-start.21) | collective-permute-done | bytes 131104 | tf_op jit(solution)/shard_map/ppermute | solution.py:33
  70.8 2.1 %collective-permute-start.19 = (bf16[256,256]{1,0:T(8,128)(2,1)S(1)}, bf16[256,256]{1,0:T(8,128)(2,1)S(1)}, u32[]{:S(2)}, u32[]{:S(2)}) collective-permute-start(bf16[256,256]{1,0:T(8,128)(2,1)S(1)} %add_convert_fusion.10), channel_id=1, source_target_pairs={{0,2},{2,4},{4,6},{6,7},{7,5},{5,3},{3,1},{1,0},{8,10},{10,12},{12... | collective-permute-start | bytes 393224 | tf_op jit(solution)/shard_map/ppermute | solution.py:33
  72.9 0.8 collective-permute-start.30
  73.6 0.6 collective-permute-done.25
  74.3 0.7 collective-permute-start.26
  75.0 2.0 %collective-permute-done.22 = bf16[256,256]{1,0:T(8,128)(2,1)S(1)} collective-permute-done((bf16[256,256]{1,0:T(8,128)(2,1)S(1)}, bf16[256,256]{1,0:T(8,128)(2,1)S(1)}, u32[]{:S(2)}, u32[]{:S(2)}) %collective-permute-start.22) | collective-permute-done | bytes 131104 | tf_op jit(solution)/shard_map/ppermute | solution.py:33
  77.1 0.8 %collective-permute-done.30 = bf16[256,256]{1,0:T(8,128)(2,1)S(1)} collective-permute-done((bf16[256,256]{1,0:T(8,128)(2,1)S(1)}, bf16[256,256]{1,0:T(8,128)(2,1)S(1)}, u32[]{:S(2)}, u32[]{:S(2)}) %collective-permute-start.30) | collective-permute-done | bytes 131104 | tf_op jit(solution)/shard_map/ppermute | solution.py:33
  77.9 1.4 %collective-permute-done.26 = bf16[256,256]{1,0:T(8,128)(2,1)S(1)} collective-permute-done((bf16[256,256]{1,0:T(8,128)(2,1)S(1)}, bf16[256,256]{1,0:T(8,128)(2,1)S(1)}, u32[]{:S(2)}, u32[]{:S(2)}) %collective-permute-start.26) | collective-permute-done | bytes 131104 | tf_op jit(solution)/shard_map/ppermute | solution.py:33
  79.4 0.7 pad_maximum_fusion
  (48 shorter events, 2.6 us)
Async XLA Ops:
  1.7 7.2 %collective-permute-start = (bf16[256,256]{1,0:T(8,128)(2,1)}, bf16[256,256]{1,0:T(8,128)(2,1)S(1)}, u32[]{:S(2)}, u32[]{:S(2)}) collective-permute-start(bf16[256,256]{1,0:T(8,128)(2,1)} %get-tuple-element.64), channel_id=1, source_target_pairs={{0,2},{2,4},{4,6},{6,7},{7,5},{5,3},{3,1},{1,0},{8,10},{10,12},{12... | collective-permute-start | bytes 393224 | tf_op jit(solution)/shard_map/ppermute | solution.py:33
  3.3 7.3 %collective-permute-start.4 = (bf16[256,256]{1,0:T(8,128)(2,1)}, bf16[256,256]{1,0:T(8,128)(2,1)S(1)}, u32[]{:S(2)}, u32[]{:S(2)}) collective-permute-start(bf16[256,256]{1,0:T(8,128)(2,1)} %get-tuple-element.63), channel_id=1, source_target_pairs={{0,1},{2,0},{4,2},{6,4},{7,6},{5,7},{3,5},{1,3},{8,9},{10,8},{12,1... | collective-permute-start | bytes 393224 | tf_op jit(solution)/shard_map/ppermute | solution.py:33
  3.7 10.2 %collective-permute-start.11 = (bf16[256,256]{1,0:T(8,128)(2,1)}, bf16[256,256]{1,0:T(8,128)(2,1)S(1)}, u32[]{:S(2)}, u32[]{:S(2)}) collective-permute-start(bf16[256,256]{1,0:T(8,128)(2,1)} %get-tuple-element.63), channel_id=1, source_target_pairs={{0,2},{2,4},{4,6},{6,7},{7,5},{5,3},{3,1},{1,0},{8,10},{10,12},{12... | collective-permute-start | bytes 393224 | tf_op jit(solution)/shard_map/ppermute | solution.py:33
  5.3 10.3 %collective-permute-start.8 = (bf16[256,256]{1,0:T(8,128)(2,1)}, bf16[256,256]{1,0:T(8,128)(2,1)}, u32[]{:S(2)}, u32[]{:S(2)}) collective-permute-start(bf16[256,256]{1,0:T(8,128)(2,1)} %get-tuple-element.64), channel_id=1, source_target_pairs={{0,1},{2,0},{4,2},{6,4},{7,6},{5,7},{3,5},{1,3},{8,9},{10,8},{12,1... | collective-permute-start | bytes 393224 | tf_op jit(solution)/shard_map/ppermute | solution.py:33
  8.9 7.2 %collective-permute-start.1 = (bf16[256,256]{1,0:T(8,128)(2,1)S(1)}, bf16[256,256]{1,0:T(8,128)(2,1)S(1)}, u32[]{:S(2)}, u32[]{:S(2)}) collective-permute-start(bf16[256,256]{1,0:T(8,128)(2,1)S(1)} %collective-permute-done.refs_0_), channel_id=1, source_target_pairs={{0,2},{2,4},{4,6},{6,7},{7,5},{5,3},{3,1},{1,0},{8,10},{10,12},{12... | collective-permute-start | bytes 393224 | tf_op jit(solution)/shard_map/ppermute | solution.py:33
  10.5 7.1 %collective-permute-start.5 = (bf16[256,256]{1,0:T(8,128)(2,1)S(1)}, bf16[256,256]{1,0:T(8,128)(2,1)S(1)}, u32[]{:S(2)}, u32[]{:S(2)}) collective-permute-start(bf16[256,256]{1,0:T(8,128)(2,1)S(1)} %collective-permute-done.4.refs_1_), channel_id=1, source_target_pairs={{0,1},{2,0},{4,2},{6,4},{7,6},{5,7},{3,5},{1,3},{8,9},{10,8},{12,1... | collective-permute-start | bytes 393224 | tf_op jit(solution)/shard_map/ppermute | solution.py:33
  13.9 7.6 %collective-permute-start.12 = (bf16[256,256]{1,0:T(8,128)(2,1)S(1)}, bf16[256,256]{1,0:T(8,128)(2,1)S(1)}, u32[]{:S(2)}, u32[]{:S(2)}) collective-permute-start(bf16[256,256]{1,0:T(8,128)(2,1)S(1)} %collective-permute-done.11.refs_3_), channel_id=1, source_target_pairs={{0,2},{2,4},{4,6},{6,7},{7,5},{5,3},{3,1},{1,0},{8,10},{10,12},{12... | collective-permute-start | bytes 393224 | tf_op jit(solution)/shard_map/ppermute | solution.py:33
  15.6 5.6 %collective-permute-start.9 = (bf16[256,256]{1,0:T(8,128)(2,1)}, bf16[256,256]{1,0:T(8,128)(2,1)S(1)}, u32[]{:S(2)}, u32[]{:S(2)}) collective-permute-start(bf16[256,256]{1,0:T(8,128)(2,1)} %collective-permute-done.8.refs_2_), channel_id=1, source_target_pairs={{0,1},{2,0},{4,2},{6,4},{7,6},{5,7},{3,5},{1,3},{8,9},{10,8},{12,1... | collective-permute-start | bytes 393224 | tf_op jit(solution)/shard_map/ppermute | solution.py:33
  16.0 7.1 %collective-permute-start.2 = (bf16[256,256]{1,0:T(8,128)(2,1)S(1)}, bf16[256,256]{1,0:T(8,128)(2,1)S(1)}, u32[]{:S(2)}, u32[]{:S(2)}) collective-permute-start(bf16[256,256]{1,0:T(8,128)(2,1)S(1)} %collective-permute-done.1.refs_0_), channel_id=1, source_target_pairs={{0,2},{2,4},{4,6},{6,7},{7,5},{5,3},{3,1},{1,0},{8,10},{10,12},{12... | collective-permute-start | bytes 393224 | tf_op jit(solution)/shard_map/ppermute | solution.py:33
  17.6 7.1 %collective-permute-start.6 = (bf16[256,256]{1,0:T(8,128)(2,1)S(1)}, bf16[256,256]{1,0:T(8,128)(2,1)S(1)}, u32[]{:S(2)}, u32[]{:S(2)}) collective-permute-start(bf16[256,256]{1,0:T(8,128)(2,1)S(1)} %collective-permute-done.5.refs_1_), channel_id=1, source_target_pairs={{0,1},{2,0},{4,2},{6,4},{7,6},{5,7},{3,5},{1,3},{8,9},{10,8},{12,1... | collective-permute-start | bytes 393224 | tf_op jit(solution)/shard_map/ppermute | solution.py:33
  21.1 5.2 %collective-permute-start.10 = (bf16[256,256]{1,0:T(8,128)(2,1)S(1)}, bf16[256,256]{1,0:T(8,128)(2,1)S(1)}, u32[]{:S(2)}, u32[]{:S(2)}) collective-permute-start(bf16[256,256]{1,0:T(8,128)(2,1)S(1)} %collective-permute-done.9.refs_2_), channel_id=1, source_target_pairs={{0,1},{2,0},{4,2},{6,4},{7,6},{5,7},{3,5},{1,3},{8,9},{10,8},{12,1... | collective-permute-start | bytes 393224 | tf_op jit(solution)/shard_map/ppermute | solution.py:33
  21.6 5.0 %collective-permute-start.13 = (bf16[256,256]{1,0:T(8,128)(2,1)S(1)}, bf16[256,256]{1,0:T(8,128)(2,1)S(1)}, u32[]{:S(2)}, u32[]{:S(2)}) collective-permute-start(bf16[256,256]{1,0:T(8,128)(2,1)S(1)} %collective-permute-done.12.refs_3_), channel_id=1, source_target_pairs={{0,2},{2,4},{4,6},{6,7},{7,5},{5,3},{3,1},{1,0},{8,10},{10,12},{12... | collective-permute-start | bytes 393224 | tf_op jit(solution)/shard_map/ppermute | solution.py:33
  23.2 5.0 %collective-permute-start.3 = (bf16[256,256]{1,0:T(8,128)(2,1)S(1)}, bf16[256,256]{1,0:T(8,128)(2,1)S(1)}, u32[]{:S(2)}, u32[]{:S(2)}) collective-permute-start(bf16[256,256]{1,0:T(8,128)(2,1)S(1)} %collective-permute-done.2.refs_0_), channel_id=1, source_target_pairs={{0,2},{2,4},{4,6},{6,7},{7,5},{5,3},{3,1},{1,0},{8,10},{10,12},{12... | collective-permute-start | bytes 393224 | tf_op jit(solution)/shard_map/ppermute | solution.py:33
  24.8 5.0 %collective-permute-start.7 = (bf16[256,256]{1,0:T(8,128)(2,1)S(1)}, bf16[256,256]{1,0:T(8,128)(2,1)S(1)}, u32[]{:S(2)}, u32[]{:S(2)}) collective-permute-start(bf16[256,256]{1,0:T(8,128)(2,1)S(1)} %collective-permute-done.6.refs_1_), channel_id=1, source_target_pairs={{0,1},{2,0},{4,2},{6,4},{7,6},{5,7},{3,5},{1,3},{8,9},{10,8},{12,1... | collective-permute-start | bytes 393224 | tf_op jit(solution)/shard_map/ppermute | solution.py:33
  32.9 4.0 %collective-permute-start.14 = (bf16[512,512]{1,0:T(8,128)(2,1)}, bf16[512,512]{1,0:T(8,128)(2,1)}, u32[]{:S(2)}, u32[]{:S(2)}) collective-permute-start(bf16[512,512]{1,0:T(8,128)(2,1)} %project_kv.1.refs_0_), channel_id=1, source_target_pairs={{0,8},{8,0},{16,24},{24,16},{1,9},{9,1},{17,25},{25,17},{2,10},{10... | collective-permute-start | bytes 1572872 | tf_op jit(solution)/shard_map/ppermute | solution.py:39
  32.9 14.7 %collective-permute-start.15 = (bf16[512,512]{1,0:T(8,128)(2,1)}, bf16[512,512]{1,0:T(8,128)(2,1)}, u32[]{:S(2)}, u32[]{:S(2)}) collective-permute-start(bf16[512,512]{1,0:T(8,128)(2,1)} %project_kv.1.refs_0_), channel_id=1, source_target_pairs={{0,16},{8,24},{16,0},{24,8},{1,17},{9,25},{17,1},{25,9},{2,18},{10... | collective-permute-start | bytes 1572872 | tf_op jit(solution)/shard_map/ppermute | solution.py:367
  35.1 1.9 %copy-start = (s32[512,1]{1,0:T(8,128)S(1)}, s32[512,1]{1,0:T(8,128)}, u32[]{:S(2)}) copy-start(s32[512,1]{1,0:T(8,128)} %copy.13.id_col) | copy-start | bytes 6148
  36.9 10.8 %copy-start.1 = (s32[512,1]{1,0:T(8,128)S(1)}, s32[512,1]{1,0:T(8,128)}, u32[]{:S(2)}) copy-start(s32[512,1]{1,0:T(8,128)} %copy.13.id_col) | copy-start | bytes 6148
  47.6 2.6 %collective-permute-start.16 = (bf16[512,512]{1,0:T(8,128)(2,1)}, bf16[512,512]{1,0:T(8,128)(2,1)S(1)}, u32[]{:S(2)}, u32[]{:S(2)}) collective-permute-start(bf16[512,512]{1,0:T(8,128)(2,1)} %collective-permute-done.15.refs_0_), channel_id=1, source_target_pairs={{0,8},{8,0},{16,24},{24,16},{1,9},{9,1},{17,25},{25,17},{2,10},{10... | collective-permute-start | bytes 1572872 | tf_op jit(solution)/shard_map/ppermute | solution.py:39
  53.5 6.3 %collective-permute-start.27 = (bf16[256,256]{1,0:T(8,128)(2,1)S(1)}, bf16[256,256]{1,0:T(8,128)(2,1)S(1)}, u32[]{:S(2)}, u32[]{:S(2)}) collective-permute-start(bf16[256,256]{1,0:T(8,128)(2,1)S(1)} %get-tuple-element.57), channel_id=1, source_target_pairs={{0,2},{2,4},{4,6},{6,7},{7,5},{5,3},{3,1},{1,0},{8,10},{10,12},{12... | collective-permute-start | bytes 393224 | tf_op jit(solution)/shard_map/ppermute | solution.py:33
  55.4 6.4 %collective-permute-start.23 = (bf16[256,256]{1,0:T(8,128)(2,1)S(1)}, bf16[256,256]{1,0:T(8,128)(2,1)S(1)}, u32[]{:S(2)}, u32[]{:S(2)}) collective-permute-start(bf16[256,256]{1,0:T(8,128)(2,1)S(1)} %get-tuple-element.53), channel_id=1, source_target_pairs={{0,1},{2,0},{4,2},{6,4},{7,6},{5,7},{3,5},{1,3},{8,9},{10,8},{12,1... | collective-permute-start | bytes 393224 | tf_op jit(solution)/shard_map/ppermute | solution.py:33
  55.6 8.5 %collective-permute-start.20 = (bf16[256,256]{1,0:T(8,128)(2,1)S(1)}, bf16[256,256]{1,0:T(8,128)(2,1)S(1)}, u32[]{:S(2)}, u32[]{:S(2)}) collective-permute-start(bf16[256,256]{1,0:T(8,128)(2,1)S(1)} %get-tuple-element.49), channel_id=1, source_target_pairs={{0,1},{2,0},{4,2},{6,4},{7,6},{5,7},{3,5},{1,3},{8,9},{10,8},{12,1... | collective-permute-start | bytes 393224 | tf_op jit(solution)/shard_map/ppermute | solution.py:33
  56.0 8.4 %collective-permute-start.17 = (bf16[256,256]{1,0:T(8,128)(2,1)S(1)}, bf16[256,256]{1,0:T(8,128)(2,1)S(1)}, u32[]{:S(2)}, u32[]{:S(2)}) collective-permute-start(bf16[256,256]{1,0:T(8,128)(2,1)S(1)} %get-tuple-element.46), channel_id=1, source_target_pairs={{0,2},{2,4},{4,6},{6,7},{7,5},{5,3},{3,1},{1,0},{8,10},{10,12},{12... | collective-permute-start | bytes 393224 | tf_op jit(solution)/shard_map/ppermute | solution.py:33
  59.9 6.4 %collective-permute-start.28 = (bf16[256,256]{1,0:T(8,128)(2,1)S(1)}, bf16[256,256]{1,0:T(8,128)(2,1)S(1)}, u32[]{:S(2)}, u32[]{:S(2)}) collective-permute-start(bf16[256,256]{1,0:T(8,128)(2,1)S(1)} %add_convert_fusion.4), channel_id=1, source_target_pairs={{0,2},{2,4},{4,6},{6,7},{7,5},{5,3},{3,1},{1,0},{8,10},{10,12},{12... | collective-permute-start | bytes 393224 | tf_op jit(solution)/shard_map/ppermute | solution.py:33
  61.8 6.0 %collective-permute-start.24 = (bf16[256,256]{1,0:T(8,128)(2,1)S(1)}, bf16[256,256]{1,0:T(8,128)(2,1)S(1)}, u32[]{:S(2)}, u32[]{:S(2)}) collective-permute-start(bf16[256,256]{1,0:T(8,128)(2,1)S(1)} %add_convert_fusion.7), channel_id=1, source_target_pairs={{0,1},{2,0},{4,2},{6,4},{7,6},{5,7},{3,5},{1,3},{8,9},{10,8},{12,1... | collective-permute-start | bytes 393224 | tf_op jit(solution)/shard_map/ppermute | solution.py:33
  64.1 6.5 %collective-permute-start.21 = (bf16[256,256]{1,0:T(8,128)(2,1)S(1)}, bf16[256,256]{1,0:T(8,128)(2,1)S(1)}, u32[]{:S(2)}, u32[]{:S(2)}) collective-permute-start(bf16[256,256]{1,0:T(8,128)(2,1)S(1)} %add_convert_fusion.9), channel_id=1, source_target_pairs={{0,1},{2,0},{4,2},{6,4},{7,6},{5,7},{3,5},{1,3},{8,9},{10,8},{12,1... | collective-permute-start | bytes 393224 | tf_op jit(solution)/shard_map/ppermute | solution.py:33
  64.5 6.3 %collective-permute-start.18 = (bf16[256,256]{1,0:T(8,128)(2,1)S(1)}, bf16[256,256]{1,0:T(8,128)(2,1)S(1)}, u32[]{:S(2)}, u32[]{:S(2)}) collective-permute-start(bf16[256,256]{1,0:T(8,128)(2,1)S(1)} %add_convert_fusion.11), channel_id=1, source_target_pairs={{0,2},{2,4},{4,6},{6,7},{7,5},{5,3},{3,1},{1,0},{8,10},{10,12},{12... | collective-permute-start | bytes 393224 | tf_op jit(solution)/shard_map/ppermute | solution.py:33
  66.3 6.5 %collective-permute-start.29 = (bf16[256,256]{1,0:T(8,128)(2,1)S(1)}, bf16[256,256]{1,0:T(8,128)(2,1)S(1)}, u32[]{:S(2)}, u32[]{:S(2)}) collective-permute-start(bf16[256,256]{1,0:T(8,128)(2,1)S(1)} %add_convert_fusion.3), channel_id=1, source_target_pairs={{0,2},{2,4},{4,6},{6,7},{7,5},{5,3},{3,1},{1,0},{8,10},{10,12},{12... | collective-permute-start | bytes 393224 | tf_op jit(solution)/shard_map/ppermute | solution.py:33
  67.8 6.4 %collective-permute-start.25 = (bf16[256,256]{1,0:T(8,128)(2,1)S(1)}, bf16[256,256]{1,0:T(8,128)(2,1)S(1)}, u32[]{:S(2)}, u32[]{:S(2)}) collective-permute-start(bf16[256,256]{1,0:T(8,128)(2,1)S(1)} %add_convert_fusion.6), channel_id=1, source_target_pairs={{0,1},{2,0},{4,2},{6,4},{7,6},{5,7},{3,5},{1,3},{8,9},{10,8},{12,1... | collective-permute-start | bytes 393224 | tf_op jit(solution)/shard_map/ppermute | solution.py:33
  70.6 6.4 %collective-permute-start.22 = (bf16[256,256]{1,0:T(8,128)(2,1)S(1)}, bf16[256,256]{1,0:T(8,128)(2,1)S(1)}, u32[]{:S(2)}, u32[]{:S(2)}) collective-permute-start(bf16[256,256]{1,0:T(8,128)(2,1)S(1)} %add_convert_fusion.8), channel_id=1, source_target_pairs={{0,1},{2,0},{4,2},{6,4},{7,6},{5,7},{3,5},{1,3},{8,9},{10,8},{12,1... | collective-permute-start | bytes 393224 | tf_op jit(solution)/shard_map/ppermute | solution.py:33
  70.8 6.3 %collective-permute-start.19 = (bf16[256,256]{1,0:T(8,128)(2,1)S(1)}, bf16[256,256]{1,0:T(8,128)(2,1)S(1)}, u32[]{:S(2)}, u32[]{:S(2)}) collective-permute-start(bf16[256,256]{1,0:T(8,128)(2,1)S(1)} %add_convert_fusion.10), channel_id=1, source_target_pairs={{0,2},{2,4},{4,6},{6,7},{7,5},{5,3},{3,1},{1,0},{8,10},{10,12},{12... | collective-permute-start | bytes 393224 | tf_op jit(solution)/shard_map/ppermute | solution.py:33
  72.9 5.0 %collective-permute-start.30 = (bf16[256,256]{1,0:T(8,128)(2,1)S(1)}, bf16[256,256]{1,0:T(8,128)(2,1)S(1)}, u32[]{:S(2)}, u32[]{:S(2)}) collective-permute-start(bf16[256,256]{1,0:T(8,128)(2,1)S(1)} %add_convert_fusion.2), channel_id=1, source_target_pairs={{0,2},{2,4},{4,6},{6,7},{7,5},{5,3},{3,1},{1,0},{8,10},{10,12},{12... | collective-permute-start | bytes 393224 | tf_op jit(solution)/shard_map/ppermute | solution.py:33
  74.3 5.0 %collective-permute-start.26 = (bf16[256,256]{1,0:T(8,128)(2,1)S(1)}, bf16[256,256]{1,0:T(8,128)(2,1)S(1)}, u32[]{:S(2)}, u32[]{:S(2)}) collective-permute-start(bf16[256,256]{1,0:T(8,128)(2,1)S(1)} %add_convert_fusion.5), channel_id=1, source_target_pairs={{0,1},{2,0},{4,2},{6,4},{7,6},{5,7},{3,5},{1,3},{8,9},{10,8},{12,1... | collective-permute-start | bytes 393224 | tf_op jit(solution)/shard_map/ppermute | solution.py:33

commit v11 on v8

--- a/solution.py
+++ b/solution.py
@@ -117,7 +117,8 @@
 
 
 def project_kernel(head_size, factor, wide, w_ref, *refs):
-    lasts, (q_ref, kv_ref) = refs[:-2], refs[-2:]
+    count = len(refs) // 2 - 1
+    lasts, (q_ref, kv_ref), pieces = refs[:count], refs[count : count + 2], refs[count + 2 :]
     rows, width = lasts[0].shape
     depth, out_width = w_ref.shape[1:]
     done = depth - width
@@ -145,6 +146,7 @@
             q_ref[here, lanes] = (qh * (q_size * (factor[head] * LOG2E))).astype(BF16)
             kv_ref[here, lanes] = (kh * k_size).astype(BF16)
         kv_ref[here, out_width:] = v.astype(BF16)
+        pieces[stream][...] = kv_ref[here, :]
 
 
 def project(factor, wide, weights, lasts, head_size):
@@ -152,9 +154,13 @@
     groups, depth, out_width = weights.shape
     return pl.pallas_call(
         functools.partial(project_kernel, head_size),
-        out_shape=(pltpu.VMEM((rows, out_width), BF16), pltpu.VMEM((rows, 2 * out_width), BF16)),
+        out_shape=(
+            pltpu.VMEM((rows, out_width), BF16),
+            pltpu.VMEM((rows, 2 * out_width), BF16),
+            *[pltpu.VMEM((rows // len(lasts), 2 * out_width), BF16)] * len(lasts),
+        ),
         in_specs=[SMEM] + [VMEM] * (2 + len(lasts)),
-        out_specs=(VMEM, VMEM),
+        out_specs=(VMEM,) * (2 + len(lasts)),
         compiler_params=pltpu.CompilerParams(vmem_limit_bytes=16 << 20),
         cost_estimate=pl.CostEstimate(
             flops=2 * rows * depth * groups * out_width,
@@ -253,7 +259,7 @@
         ).astype(BF16)
 
 
-def attend(info, ids, queries, id_col, id_row, kvs, head_size, acc=None, w_out=None, streams=0):
+def attend(info, ids, queries, id_col, kvs, head_size, acc=None, w_out=None, streams=0):
     rows, width = queries[0].shape
     total = rows * len(queries)
     keys = kvs[0].shape[0]
@@ -263,7 +269,7 @@
         pltpu.VMEM((heads, keys, 2 * head_size), BF16),
         pltpu.VMEM((total, 2 * width), F32),
     ]
-    operands = [*map(in_vmem, queries), id_col, in_hbm(id_row), *map(in_vmem, kvs)]
+    operands = [*map(in_vmem, queries), id_col, in_hbm(ids.reshape(-1, 1, keys)), *map(in_vmem, kvs)]
     if acc is not None:
         operands.append(in_vmem(acc))
     if count_out:
@@ -284,11 +290,7 @@
         compiler_params=pltpu.CompilerParams(
             vmem_limit_bytes=(16 << 20) + 2 * kvs[0].size * 2 * len(kvs)
         ),
-        cost_estimate=pl.CostEstimate(
-            flops=6 * total * keys * len(kvs) * width + 2 * total * width * width * count_out,
-            bytes_accessed=4 * keys * len(kvs) * width + 8 * total * width,
-            transcendentals=total * keys * len(kvs) * heads,
-        ),
+        cost_estimate=pl.CostEstimate(flops=1 << 20, bytes_accessed=1 << 10, transcendentals=0),
         name="attend_last" if count_out else "attend",
     )(info, in_hbm(ids), *operands)
 
@@ -308,7 +310,6 @@
     chip, core = seq_at // 2, seq_at % 2
     index_at = lambda offset: ring_index((place + offset + ring) % ring, ring)
     numbers = lambda values: jnp.stack(values).astype(jnp.int32)
-    id_row = scale_ids.reshape(-1, 1, rows)
     id_col = lax.dynamic_slice_in_dim(scale_ids, seq_at * rows, rows)[:, None]
     at = [index_at(offset) for offset in range(ring)]
 
@@ -343,7 +344,7 @@
                     targets.append((s * half, (2 * step - 1 + way) * width))
     wide = placed(targets, blocks, wide, (rows, ring * width))
     lasts = [held[0][0], held[1][1]]
-    query, kv = project(head_scale, wide, weights, lasts, head_size)
+    query, kv, *pieces = project(head_scale, wide, weights, lasts, head_size)
 
     far, straight, crossed = [], [], []
     for step in range(outer):
@@ -355,18 +356,21 @@
                 (2 * a + b, 2 * ((a + step) % outer) + b) for a in range(outer) for b in (0, 1)
             ]))
     first = [seq_at * rows]
-    info = numbers(straight[:1] + crossed[:1] + first)
-    keys = [kv, swapped(kv, seqs)]
-    (acc,) = attend(info, scale_ids, [query], id_col, id_row, keys, head_size)
-    acc, far = lax.optimization_barrier((acc, far))
-    far_crossed = [swapped(block, seqs) for block in far]
-    info = numbers(straight[1:] + first)
-    (acc,) = attend(info, scale_ids, [query], id_col, id_row, far, head_size, acc)
+    places = crossed[0] + jnp.arange(len(pieces)) * half
+    near = [(kv, straight[0])], [(swapped(piece, seqs), places[s]) for s, piece in enumerate(pieces)]
+    acc = None
+    for group in (*near, list(zip(far, straight[1:]))):
+        keys = [key for key, place in group]
+        if acc is not None:
+            acc, keys = lax.optimization_barrier((acc, keys))
+        info = numbers([place for key, place in group] + first)
+        far_crossed = [swapped(block, seqs) for block in keys]
+        (acc,) = attend(info, scale_ids, [query], id_col, keys, head_size, acc)
 
     goals = [[*range(up, 0, -1), *range(-down, 0), 0] for up, down in reach]
     info = numbers(crossed[1:] + first + [at[goal % ring] for goal in goals[0] + goals[1]])
     parts = attend(
-        info, scale_ids, [query], id_col, id_row, far_crossed, head_size, acc, w_out, len(streams)
+        info, scale_ids, [query], id_col, far_crossed, head_size, acc, w_out, len(streams)
     )
     parts = [dict(zip(goals[s], parts[s * ring : (s + 1) * ring])) for s in streams]
     sums = [[None, None] for s in streams]

time: 76.9 us -> 72.4 us (0.941)
  waiting for transfers between devices: 27.4 us -> 20.7 us
  Pallas kernels: 15.7 us -> 17.3 us
    ppermute x1, waiting for transfers between devices: 9.13 us -> 2.75 us  [body(): lax.ppermute(kv, 'seq', [(2 * a + b, 2 * ((a + step) % outer) + b) for a...]
    pallas_call x3 -> x4, Pallas kernels: 8.71 us -> 10.2 us  [attend(): pl.pallas_call(functools.partial(attend_kernel, len(queries), len(kvs), h...]
  transfers between devices with their start and end apart: 31 -> 32, of which waited for: 16 -> 15; matrix products, arithmetic and copies ran while one was open for 2% -> 2% of each run, Pallas kernels for 13% -> 16%
where the time goes in v11:
time: 72.4 us; the launch traced here: 71.8 us
  starting transfers between devices  30.1 us (42%)
  waiting for transfers between devices  20.7 us (29%)
  Pallas kernels  17.3 us (24%)
  local copies, waits for them, and re-layouts  2.07 us (3%)
  other arithmetic  1.41 us (2%)
    ppermute x28, starting transfers between devices, along(): lax.ppermute(value, 'head', [(order[p], order[(p + step) % count]) for p...  29.1 us
    ppermute x28, waiting for transfers between devices, along(): lax.ppermute(value, 'head', [(order[p], order[(p + step) % count]) for p...  17.9 us
    pallas_call x4, Pallas kernels, attend(): pl.pallas_call(functools.partial(attend_kernel, len(queries), len(kvs), h...  10.2 us
    pallas_call x1, Pallas kernels, fold_gain(): pl.pallas_call(functools.partial(fold_kernel, order), out_shape=pltpu.VME...  3.01 us
    pallas_call x1, Pallas kernels, project(): pl.pallas_call(functools.partial(project_kernel, head_size), out_shape=(p...  2.88 us
    ppermute x1, waiting for transfers between devices, body(): lax.ppermute(kv, 'seq', [(2 * a + b, 2 * ((a + step) % outer) + b) for a...  2.75 us
  transfers between devices with their start and end apart: 32, of which 15 were waited for; matrix products, arithmetic and copies ran while one was open for 2% of the time, Pallas kernels for 16%

profile of v11, /device:TPU:10, one launch (start us, length us, event | category | flops | bytes accessed | tf_op | source)
XLA Modules:
  0.0 71.8 jit_solution(8135121181111166652)
XLA Ops:
  0.0 1.0 %fusion = (bf16[256,256]{1,0:T(8,128)(2,1)S(1)}, bf16[256,256]{1,0:T(8,128)(2,1)S(1)}) fusion(bf16[512,256]{1,0:T(8,128)(2,1)} %refs_0_.1), kind=kLoop, calls=%fused_computation.17 | loop fusion | bytes 524288 | tf_op jit(solution)/shard_map/slice | solution.py:321
  1.0 0.5 collective-permute-start.9
  1.5 1.6 %collective-permute-start = (bf16[256,256]{1,0:T(8,128)(2,1)S(1)}, bf16[256,256]{1,0:T(8,128)(2,1)S(1)}, u32[]{:S(2)}, u32[]{:S(2)}) collective-permute-start(bf16[256,256]{1,0:T(8,128)(2,1)S(1)} %get-tuple-element.64), channel_id=1, source_target_pairs={{0,2},{2,4},{4,6},{6,7},{7,5},{5,3},{3,1},{1,0},{8,10},{10,12},{12... | collective-permute-start | bytes 393224 | tf_op jit(solution)/shard_map/ppermute | solution.py:33
  3.5 1.6 %collective-permute-start.6 = (bf16[256,256]{1,0:T(8,128)(2,1)S(1)}, bf16[256,256]{1,0:T(8,128)(2,1)S(1)}, u32[]{:S(2)}, u32[]{:S(2)}) collective-permute-start(bf16[256,256]{1,0:T(8,128)(2,1)S(1)} %get-tuple-element.63), channel_id=1, source_target_pairs={{0,2},{2,4},{4,6},{6,7},{7,5},{5,3},{3,1},{1,0},{8,10},{10,12},{12... | collective-permute-start | bytes 393224 | tf_op jit(solution)/shard_map/ppermute | solution.py:33
  5.2 3.0 %fold_gain.1.w_ref = bf16[3,2048,256]{2,1,0:T(8,128)(2,1)S(1)} custom-call(s32[8]{0:T(128)S(1)} %stack.81.at, f32[16,128]{1,0:T(8,128)} %bitcast.20, bf16[3,2048,256]{2,1,0:T(8,128)(2,1)} %w_hbm.1), custom_call_target="tpu_custom_call" | custom-call | flops 1572864 | bytes 6291456 | tf_op jit(solution)/shard_map/fold_gain/pallas_call | solution.py:77
  8.2 0.5 collective-permute-start.10
  8.7 1.6 %collective-permute-start.1 = (bf16[256,256]{1,0:T(8,128)(2,1)S(1)}, bf16[256,256]{1,0:T(8,128)(2,1)S(1)}, u32[]{:S(2)}, u32[]{:S(2)}) collective-permute-start(bf16[256,256]{1,0:T(8,128)(2,1)S(1)} %collective-permute-done.refs_1_), channel_id=1, source_target_pairs={{0,2},{2,4},{4,6},{6,7},{7,5},{5,3},{3,1},{1,0},{8,10},{10,12},{12... | collective-permute-start | bytes 393224 | tf_op jit(solution)/shard_map/ppermute | solution.py:33
  10.7 1.6 %collective-permute-start.7 = (bf16[256,256]{1,0:T(8,128)(2,1)S(1)}, bf16[256,256]{1,0:T(8,128)(2,1)S(1)}, u32[]{:S(2)}, u32[]{:S(2)}) collective-permute-start(bf16[256,256]{1,0:T(8,128)(2,1)S(1)} %collective-permute-done.6.refs_3_), channel_id=1, source_target_pairs={{0,2},{2,4},{4,6},{6,7},{7,5},{5,3},{3,1},{1,0},{8,10},{10,12},{12... | collective-permute-start | bytes 393224 | tf_op jit(solution)/shard_map/ppermute | solution.py:33
  12.3 1.9 %collective-permute-done.10.refs_3_ = bf16[256,256]{1,0:T(8,128)(2,1)S(1)} collective-permute-done((bf16[256,256]{1,0:T(8,128)(2,1)S(1)}, bf16[256,256]{1,0:T(8,128)(2,1)S(1)}, u32[]{:S(2)}, u32[]{:S(2)}) %collective-permute-start.10) | collective-permute-done | bytes 131104 | tf_op jit(solution)/shard_map/ppermute | solution.py:33
  14.7 1.6 %collective-permute-start.2 = (bf16[256,256]{1,0:T(8,128)(2,1)S(1)}, bf16[256,256]{1,0:T(8,128)(2,1)S(1)}, u32[]{:S(2)}, u32[]{:S(2)}) collective-permute-start(bf16[256,256]{1,0:T(8,128)(2,1)S(1)} %collective-permute-done.1.refs_0_), channel_id=1, source_target_pairs={{0,2},{2,4},{4,6},{6,7},{7,5},{5,3},{3,1},{1,0},{8,10},{10,12},{12... | collective-permute-start | bytes 393224 | tf_op jit(solution)/shard_map/ppermute | solution.py:33
  16.3 1.0 %place.3.refs_4_ = bf16[512,2048]{1,0:T(8,128)(2,1)S(1)} custom-call(bf16[512,256]{1,0:T(8,128)(2,1)} %refs_0_.1, bf16[256,256]{1,0:T(8,128)(2,1)S(1)} %collective-permute-done.refs_1_, bf16[256,256]{1,0:T(8,128)(2,1)S(1)} %collective-permute-done.3.refs_2_, bf16[256,256]{1,0:T(8,128)(2,1)S(1)} %collective-permute-done.6.refs_3_, ...), custom_call_target="tpu_custom_call" | custom-call | bytes 1048576 | tf_op jit(solution)/shard_map/place/pallas_call | solution.py:106
  17.3 0.5 collective-permute-start.5
  17.8 1.6 %collective-permute-start.8 = (bf16[256,256]{1,0:T(8,128)(2,1)S(1)}, bf16[256,256]{1,0:T(8,128)(2,1)S(1)}, u32[]{:S(2)}, u32[]{:S(2)}) collective-permute-start(bf16[256,256]{1,0:T(8,128)(2,1)S(1)} %collective-permute-done.7.refs_2_), channel_id=1, source_target_pairs={{0,2},{2,4},{4,6},{6,7},{7,5},{5,3},{3,1},{1,0},{8,10},{10,12},{12... | collective-permute-start | bytes 393224 | tf_op jit(solution)/shard_map/ppermute | solution.py:33
  20.4 1.6 %collective-permute-start.12 = (bf16[256,256]{1,0:T(8,128)(2,1)S(1)}, bf16[256,256]{1,0:T(8,128)(2,1)S(1)}, u32[]{:S(2)}, u32[]{:S(2)}) collective-permute-start(bf16[256,256]{1,0:T(8,128)(2,1)S(1)} %collective-permute-done.2.refs_0_), channel_id=1, source_target_pairs={{0,2},{2,4},{4,6},{6,7},{7,5},{5,3},{3,1},{1,0},{8,10},{10,12},{12... | collective-permute-start | bytes 393224 | tf_op jit(solution)/shard_map/ppermute | solution.py:33
  22.3 0.5 collective-permute-done.8.refs_2_
  22.9 2.0 %collective-permute-done.13.refs_1_ = bf16[256,256]{1,0:T(8,128)(2,1)S(1)} collective-permute-done((bf16[256,256]{1,0:T(8,128)(2,1)S(1)}, bf16[256,256]{1,0:T(8,128)(2,1)S(1)}, u32[]{:S(2)}, u32[]{:S(2)}) %collective-permute-start.13) | collective-permute-done | bytes 131104 | tf_op jit(solution)/shard_map/ppermute | solution.py:33
  25.4 2.9 %project.1 = (bf16[512,256]{1,0:T(8,128)(2,1)S(1)}, bf16[512,512]{1,0:T(8,128)(2,1)S(1)}, bf16[256,512]{1,0:T(8,128)(2,1)S(1)}, bf16[256,512]{1,0:T(8,128)(2,1)S(1)}) custom-call(f32[2]{0:T(128)} %factor.1, bf16[512,2048]{1,0:T(8,128)(2,1)S(1)} %place.5.wide, bf16[3,2048,256]{2,1,0:T(8,128)(2,1)S(1)} %fold_gain.1.w_ref, ...), custom_call_target="tpu_custom_call" | custom-call | flops 1610612736 | bytes 5242880 | tf_op jit(solution)/shard_map/project/pallas_call | solution.py:155
  28.3 0.5 collective-permute-start.16
  28.8 0.5 collective-permute-start.15
  29.3 0.8 %dynamic_slice.3 = s32[512]{0:T(512)S(1)} dynamic-slice(s32[2048]{0:T(1024)} %ids.7, s32[]{:T(128)S(6)} %select_n.111), dynamic_slice_sizes={512} | dynamic-slice | bytes 4100 | tf_op jit(solution)/shard_map/dynamic_slice | solution.py:313
  30.4 2.1 %attend.3.refs_5_ = f32[512,512]{1,0:T(8,128)S(1)} custom-call(s32[2]{0:T(128)S(1)} %pad_add_fusion.1.info, s32[2048]{0:T(1024)} %ids.7, bf16[512,256]{1,0:T(8,128)(2,1)S(1)} %get-tuple-element.38.refs_0_, s32[512,1]{1,0:T(8,128)S(1)} %copy.12.refs_1_, s32[4,1,512]{2,1,0:T(1,128)} %bitcast.16, bf16[512,512]{1,0:T(8,128)(2,1)S(1)} %get-tuple-element.39.refs_3_), custom_call_target="tpu_custom_call" | custom-call | flops 1048576 | bytes 1024 | tf_op jit(solution)/shard_map/attend/pallas_call | solution.py:282
  32.5 2.7 %attend.4.refs_4_ = f32[512,512]{1,0:T(8,128)S(1)} custom-call(s32[3]{0:T(128)S(1)} %pad_add_fusion.info, s32[2048]{0:T(1024)} %ids.7, bf16[512,256]{1,0:T(8,128)(2,1)S(1)} %get-tuple-element.38.refs_0_, s32[512,1]{1,0:T(8,128)S(1)} %copy.12.refs_1_, s32[8,1,256]{2,1,0:T(1,128)} %bitcast.17, bf16[256,512]{1,0:T(8,128)(2,1)S(1)} %collective-permute-done.14.refs_3_, ...), custom_call_target="tpu_custom_call" | custom-call | flops 1048576 | bytes 1024 | tf_op jit(solution)/shard_map/attend/pallas_call | solution.py:282
  35.2 2.8 %collective-permute-done.16.refs_3_ = bf16[512,512]{1,0:T(8,128)(2,1)S(1)} collective-permute-done((bf16[512,512]{1,0:T(8,128)(2,1)S(1)}, bf16[512,512]{1,0:T(8,128)(2,1)S(1)}, u32[]{:S(2)}, u32[]{:S(2)}) %collective-permute-start.16) | collective-permute-done | bytes 524320 | tf_op jit(solution)/shard_map/ppermute | solution.py:355
  38.1 2.1 %attend.5.refs_4_ = f32[512,512]{1,0:T(8,128)S(1)} custom-call(s32[2]{0:T(128)S(1)} %pad_add_fusion.2.info, s32[2048]{0:T(1024)} %ids.7, bf16[512,256]{1,0:T(8,128)(2,1)S(1)} %get-tuple-element.38.refs_0_, s32[512,1]{1,0:T(8,128)S(1)} %copy.12.refs_1_, s32[4,1,512]{2,1,0:T(1,128)} %bitcast.18, bf16[512,512]{1,0:T(8,128)(2,1)S(1)} %collective-permute-done.16.refs_3_, ...), custom_call_target="tpu_custom_call" | custom-call | flops 1048576 | bytes 1024 | tf_op jit(solution)/shard_map/attend/pallas_call | solution.py:282
  40.3 3.3 %attend_last.1 = (bf16[256,256]{1,0:T(8,128)(2,1)S(1)}, bf16[256,256]{1,0:T(8,128)(2,1)S(1)}, bf16[256,256]{1,0:T(8,128)(2,1)S(1)}, bf16[256,256]{1,0:T(8,128)(2...) custom-call(s32[18]{0:T(128)S(1)} %stack.80.info, ...), custom_call_target="tpu_custom_call" | custom-call | flops 1048576 | bytes 1024 | tf_op jit(solution)/shard_map/attend_last/pallas_call | solution.py:282
  43.6 1.6 %collective-permute-start.18 = (bf16[256,256]{1,0:T(8,128)(2,1)S(1)}, bf16[256,256]{1,0:T(8,128)(2,1)S(1)}, u32[]{:S(2)}, u32[]{:S(2)}) collective-permute-start(bf16[256,256]{1,0:T(8,128)(2,1)S(1)} %get-tuple-element.51), channel_id=1, source_target_pairs={{0,2},{2,4},{4,6},{6,7},{7,5},{5,3},{3,1},{1,0},{8,10},{10,12},{12... | collective-permute-start | bytes 393224 | tf_op jit(solution)/shard_map/ppermute | solution.py:33
  45.2 0.5 collective-permute-start.22
  45.7 1.6 %collective-permute-start.25 = (bf16[256,256]{1,0:T(8,128)(2,1)S(1)}, bf16[256,256]{1,0:T(8,128)(2,1)S(1)}, u32[]{:S(2)}, u32[]{:S(2)}) collective-permute-start(bf16[256,256]{1,0:T(8,128)(2,1)S(1)} %get-tuple-element.58), channel_id=1, source_target_pairs={{0,2},{2,4},{4,6},{6,7},{7,5},{5,3},{3,1},{1,0},{8,10},{10,12},{12... | collective-permute-start | bytes 393224 | tf_op jit(solution)/shard_map/ppermute | solution.py:33
  47.2 0.5 collective-permute-start.28
  47.7 2.2 %collective-permute-done.18 = bf16[256,256]{1,0:T(8,128)(2,1)S(1)} collective-permute-done((bf16[256,256]{1,0:T(8,128)(2,1)S(1)}, bf16[256,256]{1,0:T(8,128)(2,1)S(1)}, u32[]{:S(2)}, u32[]{:S(2)}) %collective-permute-start.18) | collective-permute-done | bytes 131104 | tf_op jit(solution)/shard_map/ppermute | solution.py:33
  50.0 1.6 %collective-permute-start.19 = (bf16[256,256]{1,0:T(8,128)(2,1)S(1)}, bf16[256,256]{1,0:T(8,128)(2,1)S(1)}, u32[]{:S(2)}, u32[]{:S(2)}) collective-permute-start(bf16[256,256]{1,0:T(8,128)(2,1)S(1)} %add_convert_fusion.11), channel_id=1, source_target_pairs={{0,2},{2,4},{4,6},{6,7},{7,5},{5,3},{3,1},{1,0},{8,10},{10,12},{12... | collective-permute-start | bytes 393224 | tf_op jit(solution)/shard_map/ppermute | solution.py:33
  51.6 0.5 collective-permute-start.23
  52.1 0.6 collective-permute-done.25
  52.8 1.6 %collective-permute-start.26 = (bf16[256,256]{1,0:T(8,128)(2,1)S(1)}, bf16[256,256]{1,0:T(8,128)(2,1)S(1)}, u32[]{:S(2)}, u32[]{:S(2)}) collective-permute-start(bf16[256,256]{1,0:T(8,128)(2,1)S(1)} %add_convert_fusion.5), channel_id=1, source_target_pairs={{0,2},{2,4},{4,6},{6,7},{7,5},{5,3},{3,1},{1,0},{8,10},{10,12},{12... | collective-permute-start | bytes 393224 | tf_op jit(solution)/shard_map/ppermute | solution.py:33
  54.4 0.5 collective-permute-start.29
  54.9 0.6 collective-permute-done.19
  55.6 1.6 %collective-permute-start.20 = (bf16[256,256]{1,0:T(8,128)(2,1)S(1)}, bf16[256,256]{1,0:T(8,128)(2,1)S(1)}, u32[]{:S(2)}, u32[]{:S(2)}) collective-permute-start(bf16[256,256]{1,0:T(8,128)(2,1)S(1)} %add_convert_fusion.10), channel_id=1, source_target_pairs={{0,2},{2,4},{4,6},{6,7},{7,5},{5,3},{3,1},{1,0},{8,10},{10,12},{12... | collective-permute-start | bytes 393224 | tf_op jit(solution)/shard_map/ppermute | solution.py:33
  57.2 0.5 collective-permute-start.24
  57.7 1.5 %collective-permute-done.26 = bf16[256,256]{1,0:T(8,128)(2,1)S(1)} collective-permute-done((bf16[256,256]{1,0:T(8,128)(2,1)S(1)}, bf16[256,256]{1,0:T(8,128)(2,1)S(1)}, u32[]{:S(2)}, u32[]{:S(2)}) %collective-permute-start.26) | collective-permute-done | bytes 131104 | tf_op jit(solution)/shard_map/ppermute | solution.py:33
  59.3 1.6 %collective-permute-start.27 = (bf16[256,256]{1,0:T(8,128)(2,1)S(1)}, bf16[256,256]{1,0:T(8,128)(2,1)S(1)}, u32[]{:S(2)}, u32[]{:S(2)}) collective-permute-start(bf16[256,256]{1,0:T(8,128)(2,1)S(1)} %add_convert_fusion.4), channel_id=1, source_target_pairs={{0,2},{2,4},{4,6},{6,7},{7,5},{5,3},{3,1},{1,0},{8,10},{10,12},{12... | collective-permute-start | bytes 393224 | tf_op jit(solution)/shard_map/ppermute | solution.py:33
  61.0 0.5 collective-permute-start.30
  61.5 0.6 collective-permute-done.20
  62.1 1.6 %collective-permute-start.21 = (bf16[256,256]{1,0:T(8,128)(2,1)S(1)}, bf16[256,256]{1,0:T(8,128)(2,1)S(1)}, u32[]{:S(2)}, u32[]{:S(2)}) collective-permute-start(bf16[256,256]{1,0:T(8,128)(2,1)S(1)} %add_convert_fusion.9), channel_id=1, source_target_pairs={{0,2},{2,4},{4,6},{6,7},{7,5},{5,3},{3,1},{1,0},{8,10},{10,12},{12... | collective-permute-start | bytes 393224 | tf_op jit(solution)/shard_map/ppermute | solution.py:33
  63.7 2.3 %collective-permute-done.30 = bf16[256,256]{1,0:T(8,128)(2,1)S(1)} collective-permute-done((bf16[256,256]{1,0:T(8,128)(2,1)S(1)}, bf16[256,256]{1,0:T(8,128)(2,1)S(1)}, u32[]{:S(2)}, u32[]{:S(2)}) %collective-permute-start.30) | collective-permute-done | bytes 131104 | tf_op jit(solution)/shard_map/ppermute | solution.py:33
  66.0 0.5 collective-permute-start.31
  66.5 0.6 collective-permute-done.21
  67.2 3.8 %collective-permute-done.31 = bf16[256,256]{1,0:T(8,128)(2,1)S(1)} collective-permute-done((bf16[256,256]{1,0:T(8,128)(2,1)S(1)}, bf16[256,256]{1,0:T(8,128)(2,1)S(1)}, u32[]{:S(2)}, u32[]{:S(2)}) %collective-permute-start.31) | collective-permute-done | bytes 131104 | tf_op jit(solution)/shard_map/ppermute | solution.py:33
  71.1 0.7 %pad_maximum_fusion = bf16[512,256]{1,0:T(8,128)(2,1)} fusion(bf16[256,256]{1,0:T(8,128)(2,1)S(1)} %add_convert_fusion, bf16[256,256]{1,0:T(8,128)(2,1)S(1)} %add_convert_fusion.6), kind=kLoop, calls=%fused_computation | loop fusion | flops 524288 | bytes 524288 | tf_op jit(solution)/shard_map/concatenate | solution.py:385
  (47 shorter events, 4.3 us)
Async XLA Ops:
  1.0 7.2 %collective-permute-start.9 = (bf16[256,256]{1,0:T(8,128)(2,1)S(1)}, bf16[256,256]{1,0:T(8,128)(2,1)S(1)}, u32[]{:S(2)}, u32[]{:S(2)}) collective-permute-start(bf16[256,256]{1,0:T(8,128)(2,1)S(1)} %get-tuple-element.63), channel_id=1, source_target_pairs={{0,1},{2,0},{4,2},{6,4},{7,6},{5,7},{3,5},{1,3},{8,9},{10,8},{12,1... | collective-permute-start | bytes 393224 | tf_op jit(solution)/shard_map/ppermute | solution.py:33
  1.5 7.2 %collective-permute-start = (bf16[256,256]{1,0:T(8,128)(2,1)S(1)}, bf16[256,256]{1,0:T(8,128)(2,1)S(1)}, u32[]{:S(2)}, u32[]{:S(2)}) collective-permute-start(bf16[256,256]{1,0:T(8,128)(2,1)S(1)} %get-tuple-element.64), channel_id=1, source_target_pairs={{0,2},{2,4},{4,6},{6,7},{7,5},{5,3},{3,1},{1,0},{8,10},{10,12},{12... | collective-permute-start | bytes 393224 | tf_op jit(solution)/shard_map/ppermute | solution.py:33
  3.1 7.2 %collective-permute-start.3 = (bf16[256,256]{1,0:T(8,128)(2,1)S(1)}, bf16[256,256]{1,0:T(8,128)(2,1)S(1)}, u32[]{:S(2)}, u32[]{:S(2)}) collective-permute-start(bf16[256,256]{1,0:T(8,128)(2,1)S(1)} %get-tuple-element.64), channel_id=1, source_target_pairs={{0,1},{2,0},{4,2},{6,4},{7,6},{5,7},{3,5},{1,3},{8,9},{10,8},{12,1... | collective-permute-start | bytes 393224 | tf_op jit(solution)/shard_map/ppermute | solution.py:33
  3.5 7.2 %collective-permute-start.6 = (bf16[256,256]{1,0:T(8,128)(2,1)S(1)}, bf16[256,256]{1,0:T(8,128)(2,1)S(1)}, u32[]{:S(2)}, u32[]{:S(2)}) collective-permute-start(bf16[256,256]{1,0:T(8,128)(2,1)S(1)} %get-tuple-element.63), channel_id=1, source_target_pairs={{0,2},{2,4},{4,6},{6,7},{7,5},{5,3},{3,1},{1,0},{8,10},{10,12},{12... | collective-permute-start | bytes 393224 | tf_op jit(solution)/shard_map/ppermute | solution.py:33
  8.2 6.0 %collective-permute-start.10 = (bf16[256,256]{1,0:T(8,128)(2,1)S(1)}, bf16[256,256]{1,0:T(8,128)(2,1)S(1)}, u32[]{:S(2)}, u32[]{:S(2)}) collective-permute-start(bf16[256,256]{1,0:T(8,128)(2,1)S(1)} %collective-permute-done.9.refs_4_), channel_id=1, source_target_pairs={{0,1},{2,0},{4,2},{6,4},{7,6},{5,7},{3,5},{1,3},{8,9},{10,8},{12,1... | collective-permute-start | bytes 393224 | tf_op jit(solution)/shard_map/ppermute | solution.py:33
  8.7 6.0 %collective-permute-start.1 = (bf16[256,256]{1,0:T(8,128)(2,1)S(1)}, bf16[256,256]{1,0:T(8,128)(2,1)S(1)}, u32[]{:S(2)}, u32[]{:S(2)}) collective-permute-start(bf16[256,256]{1,0:T(8,128)(2,1)S(1)} %collective-permute-done.refs_1_), channel_id=1, source_target_pairs={{0,2},{2,4},{4,6},{6,7},{7,5},{5,3},{3,1},{1,0},{8,10},{10,12},{12... | collective-permute-start | bytes 393224 | tf_op jit(solution)/shard_map/ppermute | solution.py:33
  10.3 7.0 %collective-permute-start.4 = (bf16[256,256]{1,0:T(8,128)(2,1)S(1)}, bf16[256,256]{1,0:T(8,128)(2,1)S(1)}, u32[]{:S(2)}, u32[]{:S(2)}) collective-permute-start(bf16[256,256]{1,0:T(8,128)(2,1)S(1)} %collective-permute-done.3.refs_2_), channel_id=1, source_target_pairs={{0,1},{2,0},{4,2},{6,4},{7,6},{5,7},{3,5},{1,3},{8,9},{10,8},{12,1... | collective-permute-start | bytes 393224 | tf_op jit(solution)/shard_map/ppermute | solution.py:33
  10.7 7.1 %collective-permute-start.7 = (bf16[256,256]{1,0:T(8,128)(2,1)S(1)}, bf16[256,256]{1,0:T(8,128)(2,1)S(1)}, u32[]{:S(2)}, u32[]{:S(2)}) collective-permute-start(bf16[256,256]{1,0:T(8,128)(2,1)S(1)} %collective-permute-done.6.refs_3_), channel_id=1, source_target_pairs={{0,2},{2,4},{4,6},{6,7},{7,5},{5,3},{3,1},{1,0},{8,10},{10,12},{12... | collective-permute-start | bytes 393224 | tf_op jit(solution)/shard_map/ppermute | solution.py:33
  14.2 5.7 %collective-permute-start.11 = (bf16[256,256]{1,0:T(8,128)(2,1)S(1)}, bf16[256,256]{1,0:T(8,128)(2,1)S(1)}, u32[]{:S(2)}, u32[]{:S(2)}) collective-permute-start(bf16[256,256]{1,0:T(8,128)(2,1)S(1)} %collective-permute-done.10.refs_3_), channel_id=1, source_target_pairs={{0,1},{2,0},{4,2},{6,4},{7,6},{5,7},{3,5},{1,3},{8,9},{10,8},{12,1... | collective-permute-start | bytes 393224 | tf_op jit(solution)/shard_map/ppermute | solution.py:33
  14.7 5.7 %collective-permute-start.2 = (bf16[256,256]{1,0:T(8,128)(2,1)S(1)}, bf16[256,256]{1,0:T(8,128)(2,1)S(1)}, u32[]{:S(2)}, u32[]{:S(2)}) collective-permute-start(bf16[256,256]{1,0:T(8,128)(2,1)S(1)} %collective-permute-done.1.refs_0_), channel_id=1, source_target_pairs={{0,2},{2,4},{4,6},{6,7},{7,5},{5,3},{3,1},{1,0},{8,10},{10,12},{12... | collective-permute-start | bytes 393224 | tf_op jit(solution)/shard_map/ppermute | solution.py:33
  17.3 5.0 %collective-permute-start.5 = (bf16[256,256]{1,0:T(8,128)(2,1)S(1)}, bf16[256,256]{1,0:T(8,128)(2,1)S(1)}, u32[]{:S(2)}, u32[]{:S(2)}) collective-permute-start(bf16[256,256]{1,0:T(8,128)(2,1)S(1)} %collective-permute-done.4.refs_1_), channel_id=1, source_target_pairs={{0,1},{2,0},{4,2},{6,4},{7,6},{5,7},{3,5},{1,3},{8,9},{10,8},{12,1... | collective-permute-start | bytes 393224 | tf_op jit(solution)/shard_map/ppermute | solution.py:33
  17.8 5.0 %collective-permute-start.8 = (bf16[256,256]{1,0:T(8,128)(2,1)S(1)}, bf16[256,256]{1,0:T(8,128)(2,1)S(1)}, u32[]{:S(2)}, u32[]{:S(2)}) collective-permute-start(bf16[256,256]{1,0:T(8,128)(2,1)S(1)} %collective-permute-done.7.refs_2_), channel_id=1, source_target_pairs={{0,2},{2,4},{4,6},{6,7},{7,5},{5,3},{3,1},{1,0},{8,10},{10,12},{12... | collective-permute-start | bytes 393224 | tf_op jit(solution)/shard_map/ppermute | solution.py:33
  19.9 5.0 %collective-permute-start.13 = (bf16[256,256]{1,0:T(8,128)(2,1)S(1)}, bf16[256,256]{1,0:T(8,128)(2,1)S(1)}, u32[]{:S(2)}, u32[]{:S(2)}) collective-permute-start(bf16[256,256]{1,0:T(8,128)(2,1)S(1)} %collective-permute-done.11.refs_3_), channel_id=1, source_target_pairs={{0,1},{2,0},{4,2},{6,4},{7,6},{5,7},{3,5},{1,3},{8,9},{10,8},{12,1... | collective-permute-start | bytes 393224 | tf_op jit(solution)/shard_map/ppermute | solution.py:33
  20.4 5.0 %collective-permute-start.12 = (bf16[256,256]{1,0:T(8,128)(2,1)S(1)}, bf16[256,256]{1,0:T(8,128)(2,1)S(1)}, u32[]{:S(2)}, u32[]{:S(2)}) collective-permute-start(bf16[256,256]{1,0:T(8,128)(2,1)S(1)} %collective-permute-done.2.refs_0_), channel_id=1, source_target_pairs={{0,2},{2,4},{4,6},{6,7},{7,5},{5,3},{3,1},{1,0},{8,10},{10,12},{12... | collective-permute-start | bytes 393224 | tf_op jit(solution)/shard_map/ppermute | solution.py:33
  28.3 9.7 %collective-permute-start.16 = (bf16[512,512]{1,0:T(8,128)(2,1)S(1)}, bf16[512,512]{1,0:T(8,128)(2,1)S(1)}, u32[]{:S(2)}, u32[]{:S(2)}) collective-permute-start(bf16[512,512]{1,0:T(8,128)(2,1)S(1)} %get-tuple-element.39.refs_3_), channel_id=1, source_target_pairs={{0,16},{8,24},{16,0},{24,8},{1,17},{9,25},{17,1},{25,9},{2,18},{10... | collective-permute-start | bytes 1572872 | tf_op jit(solution)/shard_map/ppermute | solution.py:355
  28.8 3.7 %collective-permute-start.14 = (bf16[256,512]{1,0:T(8,128)(2,1)S(1)}, bf16[256,512]{1,0:T(8,128)(2,1)S(1)}, u32[]{:S(2)}, u32[]{:S(2)}) collective-permute-start(bf16[256,512]{1,0:T(8,128)(2,1)S(1)} %get-tuple-element.40), channel_id=1, source_target_pairs={{0,8},{8,0},{16,24},{24,16},{1,9},{9,1},{17,25},{25,17},{2,10},{10... | collective-permute-start | bytes 786440 | tf_op jit(solution)/shard_map/ppermute | solution.py:39
  28.8 3.7 %collective-permute-start.15 = (bf16[256,512]{1,0:T(8,128)(2,1)S(1)}, bf16[256,512]{1,0:T(8,128)(2,1)S(1)}, u32[]{:S(2)}, u32[]{:S(2)}) collective-permute-start(bf16[256,512]{1,0:T(8,128)(2,1)S(1)} %get-tuple-element.41), channel_id=1, source_target_pairs={{0,8},{8,0},{16,24},{24,16},{1,9},{9,1},{17,25},{25,17},{2,10},{10... | collective-permute-start | bytes 786440 | tf_op jit(solution)/shard_map/ppermute | solution.py:39
  38.0 2.3 %collective-permute-start.17 = (bf16[512,512]{1,0:T(8,128)(2,1)S(1)}, bf16[512,512]{1,0:T(8,128)(2,1)S(1)}, u32[]{:S(2)}, u32[]{:S(2)}) collective-permute-start(bf16[512,512]{1,0:T(8,128)(2,1)S(1)} %collective-permute-done.16.refs_3_), channel_id=1, source_target_pairs={{0,8},{8,0},{16,24},{24,16},{1,9},{9,1},{17,25},{25,17},{2,10},{10... | collective-permute-start | bytes 1572872 | tf_op jit(solution)/shard_map/ppermute | solution.py:39
  43.6 6.3 %collective-permute-start.18 = (bf16[256,256]{1,0:T(8,128)(2,1)S(1)}, bf16[256,256]{1,0:T(8,128)(2,1)S(1)}, u32[]{:S(2)}, u32[]{:S(2)}) collective-permute-start(bf16[256,256]{1,0:T(8,128)(2,1)S(1)} %get-tuple-element.51), channel_id=1, source_target_pairs={{0,2},{2,4},{4,6},{6,7},{7,5},{5,3},{3,1},{1,0},{8,10},{10,12},{12... | collective-permute-start | bytes 393224 | tf_op jit(solution)/shard_map/ppermute | solution.py:33
  45.2 6.4 %collective-permute-start.22 = (bf16[256,256]{1,0:T(8,128)(2,1)S(1)}, bf16[256,256]{1,0:T(8,128)(2,1)S(1)}, u32[]{:S(2)}, u32[]{:S(2)}) collective-permute-start(bf16[256,256]{1,0:T(8,128)(2,1)S(1)} %get-tuple-element.54), channel_id=1, source_target_pairs={{0,1},{2,0},{4,2},{6,4},{7,6},{5,7},{3,5},{1,3},{8,9},{10,8},{12,1... | collective-permute-start | bytes 393224 | tf_op jit(solution)/shard_map/ppermute | solution.py:33
  45.7 7.1 %collective-permute-start.25 = (bf16[256,256]{1,0:T(8,128)(2,1)S(1)}, bf16[256,256]{1,0:T(8,128)(2,1)S(1)}, u32[]{:S(2)}, u32[]{:S(2)}) collective-permute-start(bf16[256,256]{1,0:T(8,128)(2,1)S(1)} %get-tuple-element.58), channel_id=1, source_target_pairs={{0,2},{2,4},{4,6},{6,7},{7,5},{5,3},{3,1},{1,0},{8,10},{10,12},{12... | collective-permute-start | bytes 393224 | tf_op jit(solution)/shard_map/ppermute | solution.py:33
  47.2 7.2 %collective-permute-start.28 = (bf16[256,256]{1,0:T(8,128)(2,1)S(1)}, bf16[256,256]{1,0:T(8,128)(2,1)S(1)}, u32[]{:S(2)}, u32[]{:S(2)}) collective-permute-start(bf16[256,256]{1,0:T(8,128)(2,1)S(1)} %get-tuple-element.62), channel_id=1, source_target_pairs={{0,1},{2,0},{4,2},{6,4},{7,6},{5,7},{3,5},{1,3},{8,9},{10,8},{12,1... | collective-permute-start | bytes 393224 | tf_op jit(solution)/shard_map/ppermute | solution.py:33
  50.0 5.6 %collective-permute-start.19 = (bf16[256,256]{1,0:T(8,128)(2,1)S(1)}, bf16[256,256]{1,0:T(8,128)(2,1)S(1)}, u32[]{:S(2)}, u32[]{:S(2)}) collective-permute-start(bf16[256,256]{1,0:T(8,128)(2,1)S(1)} %add_convert_fusion.11), channel_id=1, source_target_pairs={{0,2},{2,4},{4,6},{6,7},{7,5},{5,3},{3,1},{1,0},{8,10},{10,12},{12... | collective-permute-start | bytes 393224 | tf_op jit(solution)/shard_map/ppermute | solution.py:33
  51.6 5.6 %collective-permute-start.23 = (bf16[256,256]{1,0:T(8,128)(2,1)S(1)}, bf16[256,256]{1,0:T(8,128)(2,1)S(1)}, u32[]{:S(2)}, u32[]{:S(2)}) collective-permute-start(bf16[256,256]{1,0:T(8,128)(2,1)S(1)} %add_convert_fusion.8), channel_id=1, source_target_pairs={{0,1},{2,0},{4,2},{6,4},{7,6},{5,7},{3,5},{1,3},{8,9},{10,8},{12,1... | collective-permute-start | bytes 393224 | tf_op jit(solution)/shard_map/ppermute | solution.py:33
  52.8 6.5 %collective-permute-start.26 = (bf16[256,256]{1,0:T(8,128)(2,1)S(1)}, bf16[256,256]{1,0:T(8,128)(2,1)S(1)}, u32[]{:S(2)}, u32[]{:S(2)}) collective-permute-start(bf16[256,256]{1,0:T(8,128)(2,1)S(1)} %add_convert_fusion.5), channel_id=1, source_target_pairs={{0,2},{2,4},{4,6},{6,7},{7,5},{5,3},{3,1},{1,0},{8,10},{10,12},{12... | collective-permute-start | bytes 393224 | tf_op jit(solution)/shard_map/ppermute | solution.py:33
  54.4 6.5 %collective-permute-start.29 = (bf16[256,256]{1,0:T(8,128)(2,1)S(1)}, bf16[256,256]{1,0:T(8,128)(2,1)S(1)}, u32[]{:S(2)}, u32[]{:S(2)}) collective-permute-start(bf16[256,256]{1,0:T(8,128)(2,1)S(1)} %add_convert_fusion.3), channel_id=1, source_target_pairs={{0,1},{2,0},{4,2},{6,4},{7,6},{5,7},{3,5},{1,3},{8,9},{10,8},{12,1... | collective-permute-start | bytes 393224 | tf_op jit(solution)/shard_map/ppermute | solution.py:33
  55.6 6.5 %collective-permute-start.20 = (bf16[256,256]{1,0:T(8,128)(2,1)S(1)}, bf16[256,256]{1,0:T(8,128)(2,1)S(1)}, u32[]{:S(2)}, u32[]{:S(2)}) collective-permute-start(bf16[256,256]{1,0:T(8,128)(2,1)S(1)} %add_convert_fusion.10), channel_id=1, source_target_pairs={{0,2},{2,4},{4,6},{6,7},{7,5},{5,3},{3,1},{1,0},{8,10},{10,12},{12... | collective-permute-start | bytes 393224 | tf_op jit(solution)/shard_map/ppermute | solution.py:33
  57.2 9.3 %collective-permute-start.24 = (bf16[256,256]{1,0:T(8,128)(2,1)S(1)}, bf16[256,256]{1,0:T(8,128)(2,1)S(1)}, u32[]{:S(2)}, u32[]{:S(2)}) collective-permute-start(bf16[256,256]{1,0:T(8,128)(2,1)S(1)} %add_convert_fusion.7), channel_id=1, source_target_pairs={{0,1},{2,0},{4,2},{6,4},{7,6},{5,7},{3,5},{1,3},{8,9},{10,8},{12,1... | collective-permute-start | bytes 393224 | tf_op jit(solution)/shard_map/ppermute | solution.py:33
  59.3 7.9 %collective-permute-start.27 = (bf16[256,256]{1,0:T(8,128)(2,1)S(1)}, bf16[256,256]{1,0:T(8,128)(2,1)S(1)}, u32[]{:S(2)}, u32[]{:S(2)}) collective-permute-start(bf16[256,256]{1,0:T(8,128)(2,1)S(1)} %add_convert_fusion.4), channel_id=1, source_target_pairs={{0,2},{2,4},{4,6},{6,7},{7,5},{5,3},{3,1},{1,0},{8,10},{10,12},{12... | collective-permute-start | bytes 393224 | tf_op jit(solution)/shard_map/ppermute | solution.py:33
  61.0 5.0 %collective-permute-start.30 = (bf16[256,256]{1,0:T(8,128)(2,1)S(1)}, bf16[256,256]{1,0:T(8,128)(2,1)S(1)}, u32[]{:S(2)}, u32[]{:S(2)}) collective-permute-start(bf16[256,256]{1,0:T(8,128)(2,1)S(1)} %add_convert_fusion.2), channel_id=1, source_target_pairs={{0,1},{2,0},{4,2},{6,4},{7,6},{5,7},{3,5},{1,3},{8,9},{10,8},{12,1... | collective-permute-start | bytes 393224 | tf_op jit(solution)/shard_map/ppermute | solution.py:33
  62.1 5.0 %collective-permute-start.21 = (bf16[256,256]{1,0:T(8,128)(2,1)S(1)}, bf16[256,256]{1,0:T(8,128)(2,1)S(1)}, u32[]{:S(2)}, u32[]{:S(2)}) collective-permute-start(bf16[256,256]{1,0:T(8,128)(2,1)S(1)} %add_convert_fusion.9), channel_id=1, source_target_pairs={{0,2},{2,4},{4,6},{6,7},{7,5},{5,3},{3,1},{1,0},{8,10},{10,12},{12... | collective-permute-start | bytes 393224 | tf_op jit(solution)/shard_map/ppermute | solution.py:33
  66.0 5.0 %collective-permute-start.31 = (bf16[256,256]{1,0:T(8,128)(2,1)S(1)}, bf16[256,256]{1,0:T(8,128)(2,1)S(1)}, u32[]{:S(2)}, u32[]{:S(2)}) collective-permute-start(bf16[256,256]{1,0:T(8,128)(2,1)S(1)} %add_convert_fusion.1), channel_id=1, source_target_pairs={{0,1},{2,0},{4,2},{6,4},{7,6},{5,7},{3,5},{1,3},{8,9},{10,8},{12,1... | collective-permute-start | bytes 393224 | tf_op jit(solution)/shard_map/ppermute | solution.py:33

commit v12 on v11

--- a/solution.py
+++ b/solution.py
@@ -116,59 +116,51 @@
     )(*operands)
 
 
-def project_kernel(head_size, factor, wide, w_ref, *refs):
-    count = len(refs) // 2 - 1
-    lasts, (q_ref, kv_ref), pieces = refs[:count], refs[count : count + 2], refs[count + 2 :]
-    rows, width = lasts[0].shape
+def project_kernel(head_size, groups, count, factor, wide, w_ref, out_ref, *pieces):
+    rows = wide.shape[0] // count
     depth, out_width = w_ref.shape[1:]
-    done = depth - width
-    for stream, last in enumerate(lasts):
-        here = slice(stream * rows, (stream + 1) * rows)
-        q, k, v = (
-            jnp.dot(wide[here, :done], w_ref[group, :done, :], preferred_element_type=F32)
-            + jnp.dot(last[...], w_ref[group, done:, :], preferred_element_type=F32)
-            for group in range(3)
-        )
+    for part in range(count):
+        here = slice(part * rows, (part + 1) * rows)
+        products = [
+            jnp.dot(wide[here, :], w_ref[group], preferred_element_type=F32) for group in groups
+        ]
         power = None
         for lane in range(0, depth, 128):
-            if lane < done:
-                values = wide[here, lane : lane + 128].astype(F32)
-            else:
-                values = last[:, lane - done : lane - done + 128].astype(F32)
+            values = wide[here, lane : lane + 128].astype(F32)
             power = values * values if power is None else power + values * values
         scale = lax.rsqrt(jnp.sum(power, axis=-1, keepdims=True) * (1.0 / depth) + 1e-06)
-        q, k, v = q * scale, k * scale, v * scale
-        for head in range(out_width // head_size):
-            lanes = slice(head * head_size, (head + 1) * head_size)
-            qh, kh = q[:, lanes], k[:, lanes]
-            q_size = lax.rsqrt(jnp.sum(qh * qh, axis=-1, keepdims=True) + 1e-06)
-            k_size = lax.rsqrt(jnp.sum(kh * kh, axis=-1, keepdims=True) + 1e-06)
-            q_ref[here, lanes] = (qh * (q_size * (factor[head] * LOG2E))).astype(BF16)
-            kv_ref[here, lanes] = (kh * k_size).astype(BF16)
-        kv_ref[here, out_width:] = v.astype(BF16)
-        pieces[stream][...] = kv_ref[here, :]
-
-
-def project(factor, wide, weights, lasts, head_size):
+        for number, (group, product) in enumerate(zip(groups, products)):
+            start = number * out_width
+            product = product * scale
+            for head in range(out_width // head_size):
+                value = product[:, head * head_size : (head + 1) * head_size]
+                if group < 2:
+                    size = lax.rsqrt(jnp.sum(value * value, axis=-1, keepdims=True) + 1e-06)
+                    value = value * (size * (factor[head] * LOG2E) if group == 0 else size)
+                lanes = slice(start + head * head_size, start + (head + 1) * head_size)
+                out_ref[here, lanes] = value.astype(BF16)
+        if pieces:
+            pieces[part][...] = out_ref[here, :]
+
+
+def project(factor, wide, weights, groups, count, apart, head_size):
     rows = wide.shape[0]
-    groups, depth, out_width = weights.shape
+    depth, out_width = weights.shape[1:]
+    width = len(groups) * out_width
+    shapes = [(rows, width)] + [(rows // count, width)] * (count if apart else 0)
     return pl.pallas_call(
-        functools.partial(project_kernel, head_size),
-        out_shape=(
-            pltpu.VMEM((rows, out_width), BF16),
-            pltpu.VMEM((rows, 2 * out_width), BF16),
-            *[pltpu.VMEM((rows // len(lasts), 2 * out_width), BF16)] * len(lasts),
-        ),
-        in_specs=[SMEM] + [VMEM] * (2 + len(lasts)),
-        out_specs=(VMEM,) * (2 + len(lasts)),
+        functools.partial(project_kernel, head_size, groups, count),
+        out_shape=tuple(pltpu.VMEM(shape, BF16) for shape in shapes),
+        in_specs=[SMEM] + [VMEM] * 2,
+        out_specs=(VMEM,) * len(shapes),
         compiler_params=pltpu.CompilerParams(vmem_limit_bytes=16 << 20),
         cost_estimate=pl.CostEstimate(
-            flops=2 * rows * depth * groups * out_width,
-            bytes_accessed=2 * depth * (rows + groups * out_width),
+            flops=2 * rows * depth * width,
+            bytes_accessed=2 * depth * (rows + width),
             transcendentals=0,
         ),
-        name="project",
-    )(in_hbm(factor), in_vmem(wide), in_vmem(weights), *map(in_vmem, lasts))
+        name="project_q" if groups == (0,) else "project_kv",
+    )(in_hbm(factor), in_vmem(wide), in_vmem(weights))
 
 
 def attend_blocks(sources, ids, q_first, q_refs, id_col, id_row, kv_refs, v_ones, acc, head_size):
@@ -273,7 +265,7 @@
     if acc is not None:
         operands.append(in_vmem(acc))
     if count_out:
-        operands.append(in_hbm(w_out))
+        operands.append(in_vmem(w_out))
         scratch.append(pltpu.VMEM((total, width), BF16))
         shape = pltpu.VMEM((total // streams, w_out.shape[1] * streams // count_out), BF16)
     else:
@@ -343,8 +335,11 @@
                     blocks.append(in_vmem(held[s][way]))
                     targets.append((s * half, (2 * step - 1 + way) * width))
     wide = placed(targets, blocks, wide, (rows, ring * width))
-    lasts = [held[0][0], held[1][1]]
-    query, kv, *pieces = project(head_scale, wide, weights, lasts, head_size)
+    lasts, column = [held[0][0], held[1][1]], (ring - 1) * width
+    targets = [(s * half, column) for s in streams]
+    wide = placed(targets, [*map(in_vmem, lasts)], wide, (rows, ring * width))
+    kv, *pieces = project(head_scale, wide, weights, (1, 2), len(streams), True, head_size)
+    (query,) = project(head_scale, wide, weights, (0,), len(streams), False, head_size)
 
     far, straight, crossed = [], [], []
     for step in range(outer):

time: 72.4 us -> 74.5 us (1.029)
  local copies, waits for them, and re-layouts: 2.07 us -> 5.18 us
  waiting for transfers between devices: 20.7 us -> 18 us
  Pallas kernels: 17.3 us -> 18.6 us
    unnamed x0 -> x6, local copies, waits for them, and re-layouts: none -> 3.11 us
    ppermute x1, waiting for transfers between devices: 2.75 us -> 0.01 us  [body(): lax.ppermute(kv, 'seq', [(2 * a + b, 2 * ((a + step) % outer) + b) for a...]
    pallas_call x1 -> x2, Pallas kernels: 2.88 us -> 4.27 us  [project(): pl.pallas_call(functools.partial(project_kernel, head_size, groups, count...]
  transfers between devices with their start and end apart: 32 -> 32, of which waited for: 15 -> 15; matrix products, arithmetic and copies ran while one was open for 2% -> 2% of each run, Pallas kernels for 16% -> 18%
where the time goes in v12:
time: 74.5 us; the launch traced here: 73.7 us
  starting transfers between devices  30.3 us (41%)
  Pallas kernels  18.6 us (25%)
  waiting for transfers between devices  18 us (24%)
  local copies, waits for them, and re-layouts  5.18 us (7%)
  other arithmetic  1.39 us (2%)
    ppermute x28, starting transfers between devices, along(): lax.ppermute(value, 'head', [(order[p], order[(p + step) % count]) for p...  29.1 us
    ppermute x28, waiting for transfers between devices, along(): lax.ppermute(value, 'head', [(order[p], order[(p + step) % count]) for p...  18 us
    pallas_call x4, Pallas kernels, attend(): pl.pallas_call(functools.partial(attend_kernel, len(queries), len(kvs), h...  10 us
    pallas_call x2, Pallas kernels, project(): pl.pallas_call(functools.partial(project_kernel, head_size, groups, count...  4.27 us
    unnamed x6, local copies, waits for them, and re-layouts  3.11 us
    pallas_call x1, Pallas kernels, fold_gain(): pl.pallas_call(functools.partial(fold_kernel, order), out_shape=pltpu.VME...  3.01 us
  transfers between devices with their start and end apart: 32, of which 15 were waited for; matrix products, arithmetic and copies ran while one was open for 2% of the time, Pallas kernels for 18%

profile of v12, /device:TPU:10, one launch (start us, length us, event | category | flops | bytes accessed | tf_op | source)
XLA Modules:
  0.0 73.7 jit_solution(8041215518325469046)
XLA Ops:
  0.0 1.0 %fusion = (bf16[256,256]{1,0:T(8,128)(2,1)S(1)}, bf16[256,256]{1,0:T(8,128)(2,1)S(1)}) fusion(bf16[512,256]{1,0:T(8,128)(2,1)} %refs_0_.1), kind=kLoop, calls=%fused_computation.17 | loop fusion | bytes 524288 | tf_op jit(solution)/shard_map/slice | solution.py:313
  1.0 0.5 collective-permute-start.4
  1.5 1.6 %collective-permute-start = (bf16[256,256]{1,0:T(8,128)(2,1)S(1)}, bf16[256,256]{1,0:T(8,128)(2,1)S(1)}, u32[]{:S(2)}, u32[]{:S(2)}) collective-permute-start(bf16[256,256]{1,0:T(8,128)(2,1)S(1)} %get-tuple-element.62), channel_id=1, source_target_pairs={{0,2},{2,4},{4,6},{6,7},{7,5},{5,3},{3,1},{1,0},{8,10},{10,12},{12... | collective-permute-start | bytes 393224 | tf_op jit(solution)/shard_map/ppermute | solution.py:33
  3.1 0.4 collective-permute-start.7
  3.5 1.6 %collective-permute-start.9 = (bf16[256,256]{1,0:T(8,128)(2,1)S(1)}, bf16[256,256]{1,0:T(8,128)(2,1)S(1)}, u32[]{:S(2)}, u32[]{:S(2)}) collective-permute-start(bf16[256,256]{1,0:T(8,128)(2,1)S(1)} %get-tuple-element.61), channel_id=1, source_target_pairs={{0,2},{2,4},{4,6},{6,7},{7,5},{5,3},{3,1},{1,0},{8,10},{10,12},{12... | collective-permute-start | bytes 393224 | tf_op jit(solution)/shard_map/ppermute | solution.py:33
  5.2 3.0 %fold_gain.1.w_ref = bf16[3,2048,256]{2,1,0:T(8,128)(2,1)S(1)} custom-call(s32[8]{0:T(128)S(1)} %stack.81.at, f32[16,128]{1,0:T(8,128)} %bitcast.20, bf16[3,2048,256]{2,1,0:T(8,128)(2,1)} %w_hbm.1), custom_call_target="tpu_custom_call" | custom-call | flops 1572864 | bytes 6291456 | tf_op jit(solution)/shard_map/fold_gain/pallas_call | solution.py:77
  8.2 0.5 collective-permute-start.5
  8.7 1.6 %collective-permute-start.1 = (bf16[256,256]{1,0:T(8,128)(2,1)S(1)}, bf16[256,256]{1,0:T(8,128)(2,1)S(1)}, u32[]{:S(2)}, u32[]{:S(2)}) collective-permute-start(bf16[256,256]{1,0:T(8,128)(2,1)S(1)} %collective-permute-done.refs_1_), channel_id=1, source_target_pairs={{0,2},{2,4},{4,6},{6,7},{7,5},{5,3},{3,1},{1,0},{8,10},{10,12},{12... | collective-permute-start | bytes 393224 | tf_op jit(solution)/shard_map/ppermute | solution.py:33
  10.3 0.5 collective-permute-start.8
  10.8 1.6 %collective-permute-start.10 = (bf16[256,256]{1,0:T(8,128)(2,1)S(1)}, bf16[256,256]{1,0:T(8,128)(2,1)S(1)}, u32[]{:S(2)}, u32[]{:S(2)}) collective-permute-start(bf16[256,256]{1,0:T(8,128)(2,1)S(1)} %collective-permute-done.9.refs_3_), channel_id=1, source_target_pairs={{0,2},{2,4},{4,6},{6,7},{7,5},{5,3},{3,1},{1,0},{8,10},{10,12},{12... | collective-permute-start | bytes 393224 | tf_op jit(solution)/shard_map/ppermute | solution.py:33
  12.3 1.9 %collective-permute-done.5.refs_3_ = bf16[256,256]{1,0:T(8,128)(2,1)S(1)} collective-permute-done((bf16[256,256]{1,0:T(8,128)(2,1)S(1)}, bf16[256,256]{1,0:T(8,128)(2,1)S(1)}, u32[]{:S(2)}, u32[]{:S(2)}) %collective-permute-start.5) | collective-permute-done | bytes 131104 | tf_op jit(solution)/shard_map/ppermute | solution.py:33
  14.3 0.4 collective-permute-start.6
  14.7 1.6 %collective-permute-start.2 = (bf16[256,256]{1,0:T(8,128)(2,1)S(1)}, bf16[256,256]{1,0:T(8,128)(2,1)S(1)}, u32[]{:S(2)}, u32[]{:S(2)}) collective-permute-start(bf16[256,256]{1,0:T(8,128)(2,1)S(1)} %collective-permute-done.1.refs_0_), channel_id=1, source_target_pairs={{0,2},{2,4},{4,6},{6,7},{7,5},{5,3},{3,1},{1,0},{8,10},{10,12},{12... | collective-permute-start | bytes 393224 | tf_op jit(solution)/shard_map/ppermute | solution.py:33
  16.3 1.0 %place.4.refs_4_ = bf16[512,2048]{1,0:T(8,128)(2,1)S(1)} custom-call(bf16[512,256]{1,0:T(8,128)(2,1)} %refs_0_.1, bf16[256,256]{1,0:T(8,128)(2,1)S(1)} %collective-permute-done.refs_1_, bf16[256,256]{1,0:T(8,128)(2,1)S(1)} %collective-permute-done.7.refs_2_, bf16[256,256]{1,0:T(8,128)(2,1)S(1)} %collective-permute-done.9.refs_3_, ...), custom_call_target="tpu_custom_call" | custom-call | bytes 1048576 | tf_op jit(solution)/shard_map/place/pallas_call | solution.py:106
  17.3 0.5 collective-permute-start.12
  17.8 1.6 %collective-permute-start.13 = (bf16[256,256]{1,0:T(8,128)(2,1)S(1)}, bf16[256,256]{1,0:T(8,128)(2,1)S(1)}, u32[]{:S(2)}, u32[]{:S(2)}) collective-permute-start(bf16[256,256]{1,0:T(8,128)(2,1)S(1)} %collective-permute-done.10.refs_2_), channel_id=1, source_target_pairs={{0,2},{2,4},{4,6},{6,7},{7,5},{5,3},{3,1},{1,0},{8,10},{10,12},{12... | collective-permute-start | bytes 393224 | tf_op jit(solution)/shard_map/ppermute | solution.py:33
  19.5 0.5 collective-permute-done.6.refs_3_
  20.4 1.6 %collective-permute-start.3 = (bf16[256,256]{1,0:T(8,128)(2,1)S(1)}, bf16[256,256]{1,0:T(8,128)(2,1)S(1)}, u32[]{:S(2)}, u32[]{:S(2)}) collective-permute-start(bf16[256,256]{1,0:T(8,128)(2,1)S(1)} %collective-permute-done.2.refs_0_), channel_id=1, source_target_pairs={{0,2},{2,4},{4,6},{6,7},{7,5},{5,3},{3,1},{1,0},{8,10},{10,12},{12... | collective-permute-start | bytes 393224 | tf_op jit(solution)/shard_map/ppermute | solution.py:33
  22.3 0.5 collective-permute-done.13.refs_2_
  22.9 2.0 %collective-permute-done.11.refs_1_ = bf16[256,256]{1,0:T(8,128)(2,1)S(1)} collective-permute-done((bf16[256,256]{1,0:T(8,128)(2,1)S(1)}, bf16[256,256]{1,0:T(8,128)(2,1)S(1)}, u32[]{:S(2)}, u32[]{:S(2)}) %collective-permute-start.11) | collective-permute-done | bytes 131104 | tf_op jit(solution)/shard_map/ppermute | solution.py:33
  24.9 0.5 collective-permute-done.3.refs_0_
  25.5 2.5 %project_kv.1 = (bf16[512,512]{1,0:T(8,128)(2,1)S(1)}, bf16[256,512]{1,0:T(8,128)(2,1)}, bf16[256,512]{1,0:T(8,128)(2,1)S(1)}) custom-call(f32[2]{0:T(128)} %factor.3, bf16[512,2048]{1,0:T(8,128)(2,1)S(1)} %place.7.wide, bf16[3,2048,256]{2,1,0:T(8,128)(2,1)S(1)} %fold_gain.1.w_ref), custom_call_target="tpu_custom_call" | custom-call | flops 1073741824 | bytes 4194304 | tf_op jit(solution)/shard_map/project_kv/pallas_call | solution.py:151
  28.0 0.5 collective-permute-start.16
  28.5 0.8 %dynamic_slice.3 = s32[512]{0:T(512)S(1)} dynamic-slice(s32[2048]{0:T(1024)} %ids.7, s32[]{:T(128)S(6)} %select_n.111), dynamic_slice_sizes={512} | dynamic-slice | bytes 4100 | tf_op jit(solution)/shard_map/dynamic_slice | solution.py:305
  29.5 0.5 collective-permute-start.15
  30.1 1.9 %copy-done.1 = bf16[3,2048,256]{2,1,0:T(8,128)(2,1)S(1)} copy-done((bf16[3,2048,256]{2,1,0:T(8,128)(2,1)S(1)}, bf16[3,2048,256]{2,1,0:T(8,128)(2,1)}, u32[]{:S(2)}) %copy-start.1) | copy-done | bytes 3145752
  32.0 1.7 %project_q.1.refs_0_ = bf16[512,256]{1,0:T(8,128)(2,1)S(1)} custom-call(f32[2]{0:T(128)} %factor.3, bf16[512,2048]{1,0:T(8,128)(2,1)S(1)} %place.7.wide, bf16[3,2048,256]{2,1,0:T(8,128)(2,1)S(1)} %copy-done.1), custom_call_target="tpu_custom_call" | custom-call | flops 536870912 | bytes 3145728 | tf_op jit(solution)/shard_map/project_q/pallas_call | solution.py:151
  33.8 2.1 %attend.3.refs_5_ = f32[512,512]{1,0:T(8,128)S(1)} custom-call(s32[2]{0:T(128)S(1)} %pad_add_fusion.1.info, s32[2048]{0:T(1024)} %ids.7, bf16[512,256]{1,0:T(8,128)(2,1)S(1)} %project_q.1.refs_0_, s32[512,1]{1,0:T(8,128)S(1)} %copy.13.refs_1_, s32[4,1,512]{2,1,0:T(1,128)} %bitcast.16, bf16[512,512]{1,0:T(8,128)(2,1)S(1)} %get-tuple-element.37.refs_3_), custom_call_target="tpu_custom_call" | custom-call | flops 1048576 | bytes 1024 | tf_op jit(solution)/shard_map/attend/pallas_call | solution.py:274
  35.9 2.7 %attend.4.refs_4_ = f32[512,512]{1,0:T(8,128)S(1)} custom-call(s32[3]{0:T(128)S(1)} %pad_add_fusion.info, s32[2048]{0:T(1024)} %ids.7, bf16[512,256]{1,0:T(8,128)(2,1)S(1)} %project_q.1.refs_0_, s32[512,1]{1,0:T(8,128)S(1)} %copy.13.refs_1_, s32[8,1,256]{2,1,0:T(1,128)} %bitcast.17, bf16[256,512]{1,0:T(8,128)(2,1)S(1)} %collective-permute-done.14.refs_3_, ...), custom_call_target="tpu_custom_call" | custom-call | flops 1048576 | bytes 1024 | tf_op jit(solution)/shard_map/attend/pallas_call | solution.py:274
  38.9 2.4 %attend.5.refs_4_ = f32[512,512]{1,0:T(8,128)S(1)} custom-call(s32[2]{0:T(128)S(1)} %pad_add_fusion.2.info, s32[2048]{0:T(1024)} %ids.7, bf16[512,256]{1,0:T(8,128)(2,1)S(1)} %project_q.1.refs_0_, s32[512,1]{1,0:T(8,128)S(1)} %copy.13.refs_1_, s32[4,1,512]{2,1,0:T(1,128)} %bitcast.18, bf16[512,512]{1,0:T(8,128)(2,1)} %collective-permute-done.16.refs_3_, ...), custom_call_target="tpu_custom_call" | custom-call | flops 1048576 | bytes 1024 | tf_op jit(solution)/shard_map/attend/pallas_call | solution.py:274
  41.3 1.2 %copy-done.2 = bf16[256,2048]{1,0:T(8,128)(2,1)S(1)} copy-done((bf16[256,2048]{1,0:T(8,128)(2,1)S(1)}, bf16[256,2048]{1,0:T(8,128)(2,1)}, u32[]{:S(2)}) %copy-start.2) | copy-done | bytes 1048600
  42.6 2.8 %attend_last.1 = (bf16[256,256]{1,0:T(8,128)(2,1)S(1)}, bf16[256,256]{1,0:T(8,128)(2,1)S(1)}, bf16[256,256]{1,0:T(8,128)(2,1)S(1)}, bf16[256,256]{1,0:T(8,128)(2...) custom-call(s32[18]{0:T(128)S(1)} %stack.80.info, ...), custom_call_target="tpu_custom_call" | custom-call | flops 1048576 | bytes 1024 | tf_op jit(solution)/shard_map/attend_last/pallas_call | solution.py:274
  45.4 1.7 %collective-permute-start.18 = (bf16[256,256]{1,0:T(8,128)(2,1)S(1)}, bf16[256,256]{1,0:T(8,128)(2,1)S(1)}, u32[]{:S(2)}, u32[]{:S(2)}) collective-permute-start(bf16[256,256]{1,0:T(8,128)(2,1)S(1)} %get-tuple-element.49), channel_id=1, source_target_pairs={{0,2},{2,4},{4,6},{6,7},{7,5},{5,3},{3,1},{1,0},{8,10},{10,12},{12... | collective-permute-start | bytes 393224 | tf_op jit(solution)/shard_map/ppermute | solution.py:33
  47.5 1.6 %collective-permute-start.25 = (bf16[256,256]{1,0:T(8,128)(2,1)S(1)}, bf16[256,256]{1,0:T(8,128)(2,1)S(1)}, u32[]{:S(2)}, u32[]{:S(2)}) collective-permute-start(bf16[256,256]{1,0:T(8,128)(2,1)S(1)} %get-tuple-element.56), channel_id=1, source_target_pairs={{0,2},{2,4},{4,6},{6,7},{7,5},{5,3},{3,1},{1,0},{8,10},{10,12},{12... | collective-permute-start | bytes 393224 | tf_op jit(solution)/shard_map/ppermute | solution.py:33
  49.5 2.2 %collective-permute-done.18 = bf16[256,256]{1,0:T(8,128)(2,1)S(1)} collective-permute-done((bf16[256,256]{1,0:T(8,128)(2,1)S(1)}, bf16[256,256]{1,0:T(8,128)(2,1)S(1)}, u32[]{:S(2)}, u32[]{:S(2)}) %collective-permute-start.18) | collective-permute-done | bytes 131104 | tf_op jit(solution)/shard_map/ppermute | solution.py:33
  51.8 1.7 %collective-permute-start.19 = (bf16[256,256]{1,0:T(8,128)(2,1)S(1)}, bf16[256,256]{1,0:T(8,128)(2,1)S(1)}, u32[]{:S(2)}, u32[]{:S(2)}) collective-permute-start(bf16[256,256]{1,0:T(8,128)(2,1)S(1)} %add_convert_fusion.11), channel_id=1, source_target_pairs={{0,2},{2,4},{4,6},{6,7},{7,5},{5,3},{3,1},{1,0},{8,10},{10,12},{12... | collective-permute-start | bytes 393224 | tf_op jit(solution)/shard_map/ppermute | solution.py:33
  53.9 0.6 collective-permute-done.25
  54.6 1.7 %collective-permute-start.26 = (bf16[256,256]{1,0:T(8,128)(2,1)S(1)}, bf16[256,256]{1,0:T(8,128)(2,1)S(1)}, u32[]{:S(2)}, u32[]{:S(2)}) collective-permute-start(bf16[256,256]{1,0:T(8,128)(2,1)S(1)} %add_convert_fusion.5), channel_id=1, source_target_pairs={{0,2},{2,4},{4,6},{6,7},{7,5},{5,3},{3,1},{1,0},{8,10},{10,12},{12... | collective-permute-start | bytes 393224 | tf_op jit(solution)/shard_map/ppermute | solution.py:33
  56.7 0.6 collective-permute-done.19
  57.4 1.7 %collective-permute-start.20 = (bf16[256,256]{1,0:T(8,128)(2,1)S(1)}, bf16[256,256]{1,0:T(8,128)(2,1)S(1)}, u32[]{:S(2)}, u32[]{:S(2)}) collective-permute-start(bf16[256,256]{1,0:T(8,128)(2,1)S(1)} %add_convert_fusion.10), channel_id=1, source_target_pairs={{0,2},{2,4},{4,6},{6,7},{7,5},{5,3},{3,1},{1,0},{8,10},{10,12},{12... | collective-permute-start | bytes 393224 | tf_op jit(solution)/shard_map/ppermute | solution.py:33
  59.7 1.4 %collective-permute-done.26 = bf16[256,256]{1,0:T(8,128)(2,1)S(1)} collective-permute-done((bf16[256,256]{1,0:T(8,128)(2,1)S(1)}, bf16[256,256]{1,0:T(8,128)(2,1)S(1)}, u32[]{:S(2)}, u32[]{:S(2)}) %collective-permute-start.26) | collective-permute-done | bytes 131104 | tf_op jit(solution)/shard_map/ppermute | solution.py:33
  61.1 1.7 %collective-permute-start.27 = (bf16[256,256]{1,0:T(8,128)(2,1)S(1)}, bf16[256,256]{1,0:T(8,128)(2,1)S(1)}, u32[]{:S(2)}, u32[]{:S(2)}) collective-permute-start(bf16[256,256]{1,0:T(8,128)(2,1)S(1)} %add_convert_fusion.4), channel_id=1, source_target_pairs={{0,2},{2,4},{4,6},{6,7},{7,5},{5,3},{3,1},{1,0},{8,10},{10,12},{12... | collective-permute-start | bytes 393224 | tf_op jit(solution)/shard_map/ppermute | solution.py:33
  63.3 0.6 collective-permute-done.20
  63.9 1.7 %collective-permute-start.21 = (bf16[256,256]{1,0:T(8,128)(2,1)S(1)}, bf16[256,256]{1,0:T(8,128)(2,1)S(1)}, u32[]{:S(2)}, u32[]{:S(2)}) collective-permute-start(bf16[256,256]{1,0:T(8,128)(2,1)S(1)} %add_convert_fusion.9), channel_id=1, source_target_pairs={{0,2},{2,4},{4,6},{6,7},{7,5},{5,3},{3,1},{1,0},{8,10},{10,12},{12... | collective-permute-start | bytes 393224 | tf_op jit(solution)/shard_map/ppermute | solution.py:33
  65.6 2.3 %collective-permute-done.30 = bf16[256,256]{1,0:T(8,128)(2,1)S(1)} collective-permute-done((bf16[256,256]{1,0:T(8,128)(2,1)S(1)}, bf16[256,256]{1,0:T(8,128)(2,1)S(1)}, u32[]{:S(2)}, u32[]{:S(2)}) %collective-permute-start.30) | collective-permute-done | bytes 131104 | tf_op jit(solution)/shard_map/ppermute | solution.py:33
  68.3 0.6 collective-permute-done.21
  69.0 3.9 %collective-permute-done.31 = bf16[256,256]{1,0:T(8,128)(2,1)S(1)} collective-permute-done((bf16[256,256]{1,0:T(8,128)(2,1)S(1)}, bf16[256,256]{1,0:T(8,128)(2,1)S(1)}, u32[]{:S(2)}, u32[]{:S(2)}) %collective-permute-start.31) | collective-permute-done | bytes 131104 | tf_op jit(solution)/shard_map/ppermute | solution.py:33
  73.0 0.7 pad_maximum_fusion
  (55 shorter events, 5.4 us)
Async XLA Ops:
  1.0 7.2 %collective-permute-start.4 = (bf16[256,256]{1,0:T(8,128)(2,1)S(1)}, bf16[256,256]{1,0:T(8,128)(2,1)S(1)}, u32[]{:S(2)}, u32[]{:S(2)}) collective-permute-start(bf16[256,256]{1,0:T(8,128)(2,1)S(1)} %get-tuple-element.61), channel_id=1, source_target_pairs={{0,1},{2,0},{4,2},{6,4},{7,6},{5,7},{3,5},{1,3},{8,9},{10,8},{12,1... | collective-permute-start | bytes 393224 | tf_op jit(solution)/shard_map/ppermute | solution.py:33
  1.5 7.2 %collective-permute-start = (bf16[256,256]{1,0:T(8,128)(2,1)S(1)}, bf16[256,256]{1,0:T(8,128)(2,1)S(1)}, u32[]{:S(2)}, u32[]{:S(2)}) collective-permute-start(bf16[256,256]{1,0:T(8,128)(2,1)S(1)} %get-tuple-element.62), channel_id=1, source_target_pairs={{0,2},{2,4},{4,6},{6,7},{7,5},{5,3},{3,1},{1,0},{8,10},{10,12},{12... | collective-permute-start | bytes 393224 | tf_op jit(solution)/shard_map/ppermute | solution.py:33
  3.1 7.2 %collective-permute-start.7 = (bf16[256,256]{1,0:T(8,128)(2,1)S(1)}, bf16[256,256]{1,0:T(8,128)(2,1)S(1)}, u32[]{:S(2)}, u32[]{:S(2)}) collective-permute-start(bf16[256,256]{1,0:T(8,128)(2,1)S(1)} %get-tuple-element.62), channel_id=1, source_target_pairs={{0,1},{2,0},{4,2},{6,4},{7,6},{5,7},{3,5},{1,3},{8,9},{10,8},{12,1... | collective-permute-start | bytes 393224 | tf_op jit(solution)/shard_map/ppermute | solution.py:33
  3.5 7.2 %collective-permute-start.9 = (bf16[256,256]{1,0:T(8,128)(2,1)S(1)}, bf16[256,256]{1,0:T(8,128)(2,1)S(1)}, u32[]{:S(2)}, u32[]{:S(2)}) collective-permute-start(bf16[256,256]{1,0:T(8,128)(2,1)S(1)} %get-tuple-element.61), channel_id=1, source_target_pairs={{0,2},{2,4},{4,6},{6,7},{7,5},{5,3},{3,1},{1,0},{8,10},{10,12},{12... | collective-permute-start | bytes 393224 | tf_op jit(solution)/shard_map/ppermute | solution.py:33
  8.2 17.2 %copy-start = (bf16[3,2048,256]{2,1,0:T(8,128)(2,1)}, bf16[3,2048,256]{2,1,0:T(8,128)(2,1)S(1)}, u32[]{:S(2)}) copy-start(bf16[3,2048,256]{2,1,0:T(8,128)(2,1)S(1)} %fold_gain.1.w_ref) | copy-start | bytes 9437188
  8.2 6.0 %collective-permute-start.5 = (bf16[256,256]{1,0:T(8,128)(2,1)S(1)}, bf16[256,256]{1,0:T(8,128)(2,1)S(1)}, u32[]{:S(2)}, u32[]{:S(2)}) collective-permute-start(bf16[256,256]{1,0:T(8,128)(2,1)S(1)} %collective-permute-done.4.refs_4_), channel_id=1, source_target_pairs={{0,1},{2,0},{4,2},{6,4},{7,6},{5,7},{3,5},{1,3},{8,9},{10,8},{12,1... | collective-permute-start | bytes 393224 | tf_op jit(solution)/shard_map/ppermute | solution.py:33
  8.7 6.0 %collective-permute-start.1 = (bf16[256,256]{1,0:T(8,128)(2,1)S(1)}, bf16[256,256]{1,0:T(8,128)(2,1)S(1)}, u32[]{:S(2)}, u32[]{:S(2)}) collective-permute-start(bf16[256,256]{1,0:T(8,128)(2,1)S(1)} %collective-permute-done.refs_1_), channel_id=1, source_target_pairs={{0,2},{2,4},{4,6},{6,7},{7,5},{5,3},{3,1},{1,0},{8,10},{10,12},{12... | collective-permute-start | bytes 393224 | tf_op jit(solution)/shard_map/ppermute | solution.py:33
  10.3 7.0 %collective-permute-start.8 = (bf16[256,256]{1,0:T(8,128)(2,1)S(1)}, bf16[256,256]{1,0:T(8,128)(2,1)S(1)}, u32[]{:S(2)}, u32[]{:S(2)}) collective-permute-start(bf16[256,256]{1,0:T(8,128)(2,1)S(1)} %collective-permute-done.7.refs_2_), channel_id=1, source_target_pairs={{0,1},{2,0},{4,2},{6,4},{7,6},{5,7},{3,5},{1,3},{8,9},{10,8},{12,1... | collective-permute-start | bytes 393224 | tf_op jit(solution)/shard_map/ppermute | solution.py:33
  10.8 7.1 %collective-permute-start.10 = (bf16[256,256]{1,0:T(8,128)(2,1)S(1)}, bf16[256,256]{1,0:T(8,128)(2,1)S(1)}, u32[]{:S(2)}, u32[]{:S(2)}) collective-permute-start(bf16[256,256]{1,0:T(8,128)(2,1)S(1)} %collective-permute-done.9.refs_3_), channel_id=1, source_target_pairs={{0,2},{2,4},{4,6},{6,7},{7,5},{5,3},{3,1},{1,0},{8,10},{10,12},{12... | collective-permute-start | bytes 393224 | tf_op jit(solution)/shard_map/ppermute | solution.py:33
  14.3 5.7 %collective-permute-start.6 = (bf16[256,256]{1,0:T(8,128)(2,1)S(1)}, bf16[256,256]{1,0:T(8,128)(2,1)S(1)}, u32[]{:S(2)}, u32[]{:S(2)}) collective-permute-start(bf16[256,256]{1,0:T(8,128)(2,1)S(1)} %collective-permute-done.5.refs_3_), channel_id=1, source_target_pairs={{0,1},{2,0},{4,2},{6,4},{7,6},{5,7},{3,5},{1,3},{8,9},{10,8},{12,1... | collective-permute-start | bytes 393224 | tf_op jit(solution)/shard_map/ppermute | solution.py:33
  14.7 5.7 %collective-permute-start.2 = (bf16[256,256]{1,0:T(8,128)(2,1)S(1)}, bf16[256,256]{1,0:T(8,128)(2,1)S(1)}, u32[]{:S(2)}, u32[]{:S(2)}) collective-permute-start(bf16[256,256]{1,0:T(8,128)(2,1)S(1)} %collective-permute-done.1.refs_0_), channel_id=1, source_target_pairs={{0,2},{2,4},{4,6},{6,7},{7,5},{5,3},{3,1},{1,0},{8,10},{10,12},{12... | collective-permute-start | bytes 393224 | tf_op jit(solution)/shard_map/ppermute | solution.py:33
  17.3 5.0 %collective-permute-start.12 = (bf16[256,256]{1,0:T(8,128)(2,1)S(1)}, bf16[256,256]{1,0:T(8,128)(2,1)S(1)}, u32[]{:S(2)}, u32[]{:S(2)}) collective-permute-start(bf16[256,256]{1,0:T(8,128)(2,1)S(1)} %collective-permute-done.8.refs_1_), channel_id=1, source_target_pairs={{0,1},{2,0},{4,2},{6,4},{7,6},{5,7},{3,5},{1,3},{8,9},{10,8},{12,1... | collective-permute-start | bytes 393224 | tf_op jit(solution)/shard_map/ppermute | solution.py:33
  17.8 5.0 %collective-permute-start.13 = (bf16[256,256]{1,0:T(8,128)(2,1)S(1)}, bf16[256,256]{1,0:T(8,128)(2,1)S(1)}, u32[]{:S(2)}, u32[]{:S(2)}) collective-permute-start(bf16[256,256]{1,0:T(8,128)(2,1)S(1)} %collective-permute-done.10.refs_2_), channel_id=1, source_target_pairs={{0,2},{2,4},{4,6},{6,7},{7,5},{5,3},{3,1},{1,0},{8,10},{10,12},{12... | collective-permute-start | bytes 393224 | tf_op jit(solution)/shard_map/ppermute | solution.py:33
  20.0 5.0 %collective-permute-start.11 = (bf16[256,256]{1,0:T(8,128)(2,1)S(1)}, bf16[256,256]{1,0:T(8,128)(2,1)S(1)}, u32[]{:S(2)}, u32[]{:S(2)}) collective-permute-start(bf16[256,256]{1,0:T(8,128)(2,1)S(1)} %collective-permute-done.6.refs_3_), channel_id=1, source_target_pairs={{0,1},{2,0},{4,2},{6,4},{7,6},{5,7},{3,5},{1,3},{8,9},{10,8},{12,1... | collective-permute-start | bytes 393224 | tf_op jit(solution)/shard_map/ppermute | solution.py:33
  20.4 5.0 %collective-permute-start.3 = (bf16[256,256]{1,0:T(8,128)(2,1)S(1)}, bf16[256,256]{1,0:T(8,128)(2,1)S(1)}, u32[]{:S(2)}, u32[]{:S(2)}) collective-permute-start(bf16[256,256]{1,0:T(8,128)(2,1)S(1)} %collective-permute-done.2.refs_0_), channel_id=1, source_target_pairs={{0,2},{2,4},{4,6},{6,7},{7,5},{5,3},{3,1},{1,0},{8,10},{10,12},{12... | collective-permute-start | bytes 393224 | tf_op jit(solution)/shard_map/ppermute | solution.py:33
  28.0 10.6 %collective-permute-start.16 = (bf16[512,512]{1,0:T(8,128)(2,1)S(1)}, bf16[512,512]{1,0:T(8,128)(2,1)}, u32[]{:S(2)}, u32[]{:S(2)}) collective-permute-start(bf16[512,512]{1,0:T(8,128)(2,1)S(1)} %get-tuple-element.37.refs_3_), channel_id=1, source_target_pairs={{0,16},{8,24},{16,0},{24,8},{1,17},{9,25},{17,1},{25,9},{2,18},{10... | collective-permute-start | bytes 1572872 | tf_op jit(solution)/shard_map/ppermute | solution.py:350
  29.4 6.5 %collective-permute-start.14 = (bf16[256,512]{1,0:T(8,128)(2,1)}, bf16[256,512]{1,0:T(8,128)(2,1)S(1)}, u32[]{:S(2)}, u32[]{:S(2)}) collective-permute-start(bf16[256,512]{1,0:T(8,128)(2,1)} %get-tuple-element.38), channel_id=1, source_target_pairs={{0,8},{8,0},{16,24},{24,16},{1,9},{9,1},{17,25},{25,17},{2,10},{10... | collective-permute-start | bytes 786440 | tf_op jit(solution)/shard_map/ppermute | solution.py:39
  29.5 6.4 %collective-permute-start.15 = (bf16[256,512]{1,0:T(8,128)(2,1)S(1)}, bf16[256,512]{1,0:T(8,128)(2,1)S(1)}, u32[]{:S(2)}, u32[]{:S(2)}) collective-permute-start(bf16[256,512]{1,0:T(8,128)(2,1)S(1)} %get-tuple-element.39), channel_id=1, source_target_pairs={{0,8},{8,0},{16,24},{24,16},{1,9},{9,1},{17,25},{25,17},{2,10},{10... | collective-permute-start | bytes 786440 | tf_op jit(solution)/shard_map/ppermute | solution.py:39
  30.1 1.9 %copy-start.1 = (bf16[3,2048,256]{2,1,0:T(8,128)(2,1)S(1)}, bf16[3,2048,256]{2,1,0:T(8,128)(2,1)}, u32[]{:S(2)}) copy-start(bf16[3,2048,256]{2,1,0:T(8,128)(2,1)} %copy-done) | copy-start | bytes 9437188
  38.6 2.7 %collective-permute-start.17 = (bf16[512,512]{1,0:T(8,128)(2,1)}, bf16[512,512]{1,0:T(8,128)(2,1)S(1)}, u32[]{:S(2)}, u32[]{:S(2)}) collective-permute-start(bf16[512,512]{1,0:T(8,128)(2,1)} %collective-permute-done.16.refs_3_), channel_id=1, source_target_pairs={{0,8},{8,0},{16,24},{24,16},{1,9},{9,1},{17,25},{25,17},{2,10},{10... | collective-permute-start | bytes 1572872 | tf_op jit(solution)/shard_map/ppermute | solution.py:39
  41.3 1.2 %copy-start.2 = (bf16[256,2048]{1,0:T(8,128)(2,1)S(1)}, bf16[256,2048]{1,0:T(8,128)(2,1)}, u32[]{:S(2)}) copy-start(bf16[256,2048]{1,0:T(8,128)(2,1)} %refs_5_.1) | copy-start | bytes 3145732
  45.4 6.3 %collective-permute-start.18 = (bf16[256,256]{1,0:T(8,128)(2,1)S(1)}, bf16[256,256]{1,0:T(8,128)(2,1)S(1)}, u32[]{:S(2)}, u32[]{:S(2)}) collective-permute-start(bf16[256,256]{1,0:T(8,128)(2,1)S(1)} %get-tuple-element.49), channel_id=1, source_target_pairs={{0,2},{2,4},{4,6},{6,7},{7,5},{5,3},{3,1},{1,0},{8,10},{10,12},{12... | collective-permute-start | bytes 393224 | tf_op jit(solution)/shard_map/ppermute | solution.py:33
  47.1 6.4 %collective-permute-start.22 = (bf16[256,256]{1,0:T(8,128)(2,1)S(1)}, bf16[256,256]{1,0:T(8,128)(2,1)S(1)}, u32[]{:S(2)}, u32[]{:S(2)}) collective-permute-start(bf16[256,256]{1,0:T(8,128)(2,1)S(1)} %get-tuple-element.52), channel_id=1, source_target_pairs={{0,1},{2,0},{4,2},{6,4},{7,6},{5,7},{3,5},{1,3},{8,9},{10,8},{12,1... | collective-permute-start | bytes 393224 | tf_op jit(solution)/shard_map/ppermute | solution.py:33
  47.5 7.1 %collective-permute-start.25 = (bf16[256,256]{1,0:T(8,128)(2,1)S(1)}, bf16[256,256]{1,0:T(8,128)(2,1)S(1)}, u32[]{:S(2)}, u32[]{:S(2)}) collective-permute-start(bf16[256,256]{1,0:T(8,128)(2,1)S(1)} %get-tuple-element.56), channel_id=1, source_target_pairs={{0,2},{2,4},{4,6},{6,7},{7,5},{5,3},{3,1},{1,0},{8,10},{10,12},{12... | collective-permute-start | bytes 393224 | tf_op jit(solution)/shard_map/ppermute | solution.py:33
  49.1 7.2 %collective-permute-start.28 = (bf16[256,256]{1,0:T(8,128)(2,1)S(1)}, bf16[256,256]{1,0:T(8,128)(2,1)S(1)}, u32[]{:S(2)}, u32[]{:S(2)}) collective-permute-start(bf16[256,256]{1,0:T(8,128)(2,1)S(1)} %get-tuple-element.60), channel_id=1, source_target_pairs={{0,1},{2,0},{4,2},{6,4},{7,6},{5,7},{3,5},{1,3},{8,9},{10,8},{12,1... | collective-permute-start | bytes 393224 | tf_op jit(solution)/shard_map/ppermute | solution.py:33
  51.8 5.6 %collective-permute-start.19 = (bf16[256,256]{1,0:T(8,128)(2,1)S(1)}, bf16[256,256]{1,0:T(8,128)(2,1)S(1)}, u32[]{:S(2)}, u32[]{:S(2)}) collective-permute-start(bf16[256,256]{1,0:T(8,128)(2,1)S(1)} %add_convert_fusion.11), channel_id=1, source_target_pairs={{0,2},{2,4},{4,6},{6,7},{7,5},{5,3},{3,1},{1,0},{8,10},{10,12},{12... | collective-permute-start | bytes 393224 | tf_op jit(solution)/shard_map/ppermute | solution.py:33
  53.5 5.7 %collective-permute-start.23 = (bf16[256,256]{1,0:T(8,128)(2,1)S(1)}, bf16[256,256]{1,0:T(8,128)(2,1)S(1)}, u32[]{:S(2)}, u32[]{:S(2)}) collective-permute-start(bf16[256,256]{1,0:T(8,128)(2,1)S(1)} %add_convert_fusion.8), channel_id=1, source_target_pairs={{0,1},{2,0},{4,2},{6,4},{7,6},{5,7},{3,5},{1,3},{8,9},{10,8},{12,1... | collective-permute-start | bytes 393224 | tf_op jit(solution)/shard_map/ppermute | solution.py:33
  54.6 6.5 %collective-permute-start.26 = (bf16[256,256]{1,0:T(8,128)(2,1)S(1)}, bf16[256,256]{1,0:T(8,128)(2,1)S(1)}, u32[]{:S(2)}, u32[]{:S(2)}) collective-permute-start(bf16[256,256]{1,0:T(8,128)(2,1)S(1)} %add_convert_fusion.5), channel_id=1, source_target_pairs={{0,2},{2,4},{4,6},{6,7},{7,5},{5,3},{3,1},{1,0},{8,10},{10,12},{12... | collective-permute-start | bytes 393224 | tf_op jit(solution)/shard_map/ppermute | solution.py:33
  56.3 6.5 %collective-permute-start.29 = (bf16[256,256]{1,0:T(8,128)(2,1)S(1)}, bf16[256,256]{1,0:T(8,128)(2,1)S(1)}, u32[]{:S(2)}, u32[]{:S(2)}) collective-permute-start(bf16[256,256]{1,0:T(8,128)(2,1)S(1)} %add_convert_fusion.3), channel_id=1, source_target_pairs={{0,1},{2,0},{4,2},{6,4},{7,6},{5,7},{3,5},{1,3},{8,9},{10,8},{12,1... | collective-permute-start | bytes 393224 | tf_op jit(solution)/shard_map/ppermute | solution.py:33
  57.4 6.5 %collective-permute-start.20 = (bf16[256,256]{1,0:T(8,128)(2,1)S(1)}, bf16[256,256]{1,0:T(8,128)(2,1)S(1)}, u32[]{:S(2)}, u32[]{:S(2)}) collective-permute-start(bf16[256,256]{1,0:T(8,128)(2,1)S(1)} %add_convert_fusion.10), channel_id=1, source_target_pairs={{0,2},{2,4},{4,6},{6,7},{7,5},{5,3},{3,1},{1,0},{8,10},{10,12},{12... | collective-permute-start | bytes 393224 | tf_op jit(solution)/shard_map/ppermute | solution.py:33
  59.2 9.1 %collective-permute-start.24 = (bf16[256,256]{1,0:T(8,128)(2,1)S(1)}, bf16[256,256]{1,0:T(8,128)(2,1)S(1)}, u32[]{:S(2)}, u32[]{:S(2)}) collective-permute-start(bf16[256,256]{1,0:T(8,128)(2,1)S(1)} %add_convert_fusion.7), channel_id=1, source_target_pairs={{0,1},{2,0},{4,2},{6,4},{7,6},{5,7},{3,5},{1,3},{8,9},{10,8},{12,1... | collective-permute-start | bytes 393224 | tf_op jit(solution)/shard_map/ppermute | solution.py:33
  61.1 7.9 %collective-permute-start.27 = (bf16[256,256]{1,0:T(8,128)(2,1)S(1)}, bf16[256,256]{1,0:T(8,128)(2,1)S(1)}, u32[]{:S(2)}, u32[]{:S(2)}) collective-permute-start(bf16[256,256]{1,0:T(8,128)(2,1)S(1)} %add_convert_fusion.4), channel_id=1, source_target_pairs={{0,2},{2,4},{4,6},{6,7},{7,5},{5,3},{3,1},{1,0},{8,10},{10,12},{12... | collective-permute-start | bytes 393224 | tf_op jit(solution)/shard_map/ppermute | solution.py:33
  62.8 5.0 %collective-permute-start.30 = (bf16[256,256]{1,0:T(8,128)(2,1)S(1)}, bf16[256,256]{1,0:T(8,128)(2,1)S(1)}, u32[]{:S(2)}, u32[]{:S(2)}) collective-permute-start(bf16[256,256]{1,0:T(8,128)(2,1)S(1)} %add_convert_fusion.2), channel_id=1, source_target_pairs={{0,1},{2,0},{4,2},{6,4},{7,6},{5,7},{3,5},{1,3},{8,9},{10,8},{12,1... | collective-permute-start | bytes 393224 | tf_op jit(solution)/shard_map/ppermute | solution.py:33
  63.9 5.0 %collective-permute-start.21 = (bf16[256,256]{1,0:T(8,128)(2,1)S(1)}, bf16[256,256]{1,0:T(8,128)(2,1)S(1)}, u32[]{:S(2)}, u32[]{:S(2)}) collective-permute-start(bf16[256,256]{1,0:T(8,128)(2,1)S(1)} %add_convert_fusion.9), channel_id=1, source_target_pairs={{0,2},{2,4},{4,6},{6,7},{7,5},{5,3},{3,1},{1,0},{8,10},{10,12},{12... | collective-permute-start | bytes 393224 | tf_op jit(solution)/shard_map/ppermute | solution.py:33
  67.9 5.0 %collective-permute-start.31 = (bf16[256,256]{1,0:T(8,128)(2,1)S(1)}, bf16[256,256]{1,0:T(8,128)(2,1)S(1)}, u32[]{:S(2)}, u32[]{:S(2)}) collective-permute-start(bf16[256,256]{1,0:T(8,128)(2,1)S(1)} %add_convert_fusion.1), channel_id=1, source_target_pairs={{0,1},{2,0},{4,2},{6,4},{7,6},{5,7},{3,5},{1,3},{8,9},{10,8},{12,1... | collective-permute-start | bytes 393224 | tf_op jit(solution)/shard_map/ppermute | solution.py:33

commit v13 on v11

--- a/solution.py
+++ b/solution.py
@@ -116,14 +116,15 @@
     )(*operands)
 
 
-def project_kernel(head_size, factor, wide, w_ref, *refs):
-    count = len(refs) // 2 - 1
-    lasts, (q_ref, kv_ref), pieces = refs[:count], refs[count : count + 2], refs[count + 2 :]
+def project_kernel(head_size, count, factor, wide, w_ref, *refs):
+    lasts, q_ref = refs[:count], refs[count]
+    halves, pieces = refs[count + 1 : 2 * count + 1], refs[2 * count + 1 :]
     rows, width = lasts[0].shape
     depth, out_width = w_ref.shape[1:]
     done = depth - width
     for stream, last in enumerate(lasts):
         here = slice(stream * rows, (stream + 1) * rows)
+        kv_ref = halves[stream]
         q, k, v = (
             jnp.dot(wide[here, :done], w_ref[group, :done, :], preferred_element_type=F32)
             + jnp.dot(last[...], w_ref[group, done:, :], preferred_element_type=F32)
@@ -144,23 +145,32 @@
             q_size = lax.rsqrt(jnp.sum(qh * qh, axis=-1, keepdims=True) + 1e-06)
             k_size = lax.rsqrt(jnp.sum(kh * kh, axis=-1, keepdims=True) + 1e-06)
             q_ref[here, lanes] = (qh * (q_size * (factor[head] * LOG2E))).astype(BF16)
-            kv_ref[here, lanes] = (kh * k_size).astype(BF16)
-        kv_ref[here, out_width:] = v.astype(BF16)
-        pieces[stream][...] = kv_ref[here, :]
-
-
-def project(factor, wide, weights, lasts, head_size):
+            kv_ref[:, lanes] = (kh * k_size).astype(BF16)
+        kv_ref[:, out_width:] = v.astype(BF16)
+    start = 0
+    for piece in pieces:
+        size = piece.shape[0]
+        for stream, half in enumerate(halves):
+            low, high = max(start, stream * rows), min(start + size, (stream + 1) * rows)
+            if low < high:
+                piece[low - start : high - start, :] = half[low - stream * rows : high - stream * rows, :]
+        start += size
+
+
+def project(factor, wide, weights, lasts, count_pieces, head_size):
     rows = wide.shape[0]
+    units = rows // 16
+    sizes = [16 * ((units + n) // count_pieces) for n in range(count_pieces)]
     groups, depth, out_width = weights.shape
     return pl.pallas_call(
-        functools.partial(project_kernel, head_size),
+        functools.partial(project_kernel, head_size, len(lasts)),
         out_shape=(
             pltpu.VMEM((rows, out_width), BF16),
-            pltpu.VMEM((rows, 2 * out_width), BF16),
             *[pltpu.VMEM((rows // len(lasts), 2 * out_width), BF16)] * len(lasts),
+            *[pltpu.VMEM((size, 2 * out_width), BF16) for size in sizes],
         ),
         in_specs=[SMEM] + [VMEM] * (2 + len(lasts)),
-        out_specs=(VMEM,) * (2 + len(lasts)),
+        out_specs=(VMEM,) * (1 + len(lasts) + count_pieces),
         compiler_params=pltpu.CompilerParams(vmem_limit_bytes=16 << 20),
         cost_estimate=pl.CostEstimate(
             flops=2 * rows * depth * groups * out_width,
@@ -171,109 +181,108 @@
     )(in_hbm(factor), in_vmem(wide), in_vmem(weights), *map(in_vmem, lasts))
 
 
-def attend_blocks(sources, ids, q_first, q_refs, id_col, id_row, kv_refs, v_ones, acc, head_size):
-    heads = q_refs[0].shape[1] // head_size
-    keys = kv_refs[0].shape[0]
-    rows = q_refs[0].shape[0]
-    for number, kv_ref in enumerate(kv_refs):
-        for head in range(heads):
-            start = (heads + head) * head_size
-            v_ones[head, :, :head_size] = kv_ref[:, start : start + head_size]
-            v_ones[head, :, head_size:] = jnp.ones((keys, head_size), BF16)
-        first = sources[number]
-        key_low, key_high = ids[first], ids[first + keys - 1]
-        tile = math.gcd(rows, 256)
-        for chunk, q_ref in enumerate(q_refs):
-
-            @pl.loop(0, rows // tile)
-            def _(index):
-                here = pl.ds(pl.multiple_of(index * tile, tile), tile)
-                base = chunk * rows + index * tile
-                there = pl.ds(pl.multiple_of(base, tile), tile)
-                q_low = ids[q_first + base]
-                q_high = ids[q_first + base + tile - 1]
-
-                def add(masked):
-                    if masked:
-                        allowed = id_row[first // keys] <= id_col[there, :]
-                    for head in range(heads):
-                        lanes = slice(head * head_size, (head + 1) * head_size)
-                        score = lax.dot_general(
-                            q_ref[here, lanes],
-                            kv_ref[:, lanes],
-                            (((1,), (1,)), ((), ())),
-                            preferred_element_type=F32,
-                        )
-                        weight = jnp.exp2(score)
-                        if masked:
-                            weight = jnp.where(allowed, weight, 0.0)
-                        wide = slice(2 * head * head_size, 2 * (head + 1) * head_size)
-                        acc[there, wide] += jnp.dot(
-                            weight.astype(BF16), v_ones[head], preferred_element_type=F32
-                        )
-
-                @pl.when(key_high <= q_low)
-                def _():
-                    add(False)
-
-                @pl.when((key_high > q_low) & (key_low <= q_high))
-                def _():
-                    add(True)
-
-
 def attend_kernel(
-    count_q, count_kv, head_size, has_acc, count_out, count_streams, info, ids, *refs
+    head_size, counts, has_acc, count_out, count_streams, info, ids, q_ref, id_row, *refs
 ):
-    q_refs, rest = refs[:count_q], refs[count_q:]
-    (id_col, id_row), rest = rest[:2], rest[2:]
-    kv_refs, rest = rest[:count_kv], rest[count_kv:]
-    rows, width = q_refs[0].shape
+    count_blocks, count_parts = counts
+    kv_refs, rest = refs[: count_blocks * count_parts], refs[count_blocks * count_parts :]
     if has_acc:
         acc_in, rest = rest[0], rest[1:]
     if count_out:
-        w_ref, outs, (v_ones, acc, attended) = rest[0], rest[1:-3], rest[-3:]
+        w_ref, outs, (k_all, v_ones, acc, attended) = rest[0], rest[1:-4], rest[-4:]
     else:
-        acc_out, v_ones, acc = rest
+        acc_out, k_all, v_ones, acc = rest
     acc[...] = acc_in[...] if has_acc else jnp.zeros_like(acc)
-    sources = [info[number] for number in range(count_kv)]
-    attend_blocks(
-        sources, ids, info[count_kv], q_refs, id_col, id_row, kv_refs, v_ones, acc, head_size
-    )
+    rows, width = q_ref.shape
+    heads = width // head_size
+    keys = k_all.shape[0]
+    tile = id_row.shape[2]
+    q_first = info[count_blocks]
+    v_ones[:, :, head_size:] = jnp.ones((heads, keys, head_size), BF16)
+    for number in range(count_blocks):
+        begin = 0
+        for kv_ref in kv_refs[number * count_parts : (number + 1) * count_parts]:
+            here = slice(begin, begin + kv_ref.shape[0])
+            begin += kv_ref.shape[0]
+            k_all[here, :] = kv_ref[:, :width]
+            for head in range(heads):
+                start = width + head * head_size
+                v_ones[head, here, :head_size] = kv_ref[:, start : start + head_size]
+        first = info[number]
+        key_low, key_high = ids[first], ids[first + keys - 1]
+
+        @pl.loop(0, rows // tile)
+        def _(index):
+            base = pl.multiple_of(index * tile, tile)
+            here = pl.ds(base, tile)
+            q_low, q_high = ids[q_first + base], ids[q_first + base + tile - 1]
+
+            def add(masked):
+                if masked:
+                    key_ids = [id_row[first // tile + n] for n in range(keys // tile)]
+                    own = jnp.broadcast_to(id_row[q_first // tile + index], (8, tile))
+                    allowed = jnp.concatenate(key_ids, axis=1) <= jnp.transpose(own)[:, :1]
+                for head in range(heads):
+                    lanes = slice(head * head_size, (head + 1) * head_size)
+                    score = lax.dot_general(
+                        q_ref[here, lanes],
+                        k_all[:, lanes],
+                        (((1,), (1,)), ((), ())),
+                        preferred_element_type=F32,
+                    )
+                    weight = jnp.exp2(score)
+                    if masked:
+                        weight = jnp.where(allowed, weight, 0.0)
+                    spread = slice(2 * head * head_size, 2 * (head + 1) * head_size)
+                    acc[here, spread] += jnp.dot(
+                        weight.astype(BF16), v_ones[head], preferred_element_type=F32
+                    )
+
+            @pl.when(key_high <= q_low)
+            def _():
+                add(False)
+
+            @pl.when((key_high > q_low) & (key_low <= q_high))
+            def _():
+                add(True)
+
     if not count_out:
         acc_out[...] = acc[...]
         return
-    for head in range(width // head_size):
+    for head in range(heads):
         start = 2 * head * head_size
         attended[:, head * head_size : (head + 1) * head_size] = (
             acc[:, start : start + head_size]
             / acc[:, start + head_size : start + 2 * head_size]
         ).astype(BF16)
-    out_width = outs[0].shape[1]
+    out_rows, out_width = outs[0].shape
     for number, out in enumerate(outs):
-        lane = info[count_kv + 1 + number] * out_width
-        first = number * count_streams // count_out * out.shape[0]
+        lane = info[count_blocks + 1 + number] * out_width
+        first = number * count_streams // count_out * out_rows
         out[...] = jnp.dot(
-            attended[first : first + out.shape[0], :],
+            attended[first : first + out_rows, :],
             w_ref[:, pl.ds(pl.multiple_of(lane, out_width), out_width)],
             preferred_element_type=F32,
         ).astype(BF16)
 
 
-def attend(info, ids, queries, id_col, kvs, head_size, acc=None, w_out=None, streams=0):
-    rows, width = queries[0].shape
-    total = rows * len(queries)
-    keys = kvs[0].shape[0]
+def attend(info, ids, query, blocks, head_size, acc=None, w_out=None, streams=0):
+    total, width = query.shape
+    parts = [part for block in blocks for part in block]
+    keys = sum(part.shape[0] for part in blocks[0])
     heads = width // head_size
     count_out = streams * w_out.shape[1] // width if streams else 0
     scratch = [
+        pltpu.VMEM((keys, width), BF16),
         pltpu.VMEM((heads, keys, 2 * head_size), BF16),
         pltpu.VMEM((total, 2 * width), F32),
     ]
-    operands = [*map(in_vmem, queries), id_col, in_hbm(ids.reshape(-1, 1, keys)), *map(in_vmem, kvs)]
+    operands = [in_vmem(query), in_hbm(ids.reshape(-1, 1, math.gcd(total, 256)))]
+    operands += map(in_vmem, parts)
     if acc is not None:
         operands.append(in_vmem(acc))
     if count_out:
-        operands.append(in_hbm(w_out))
+        operands.append(in_vmem(w_out))
         scratch.append(pltpu.VMEM((total, width), BF16))
         shape = pltpu.VMEM((total // streams, w_out.shape[1] * streams // count_out), BF16)
     else:
@@ -281,18 +290,37 @@
     outs = count_out or 1
     return pl.pallas_call(
         functools.partial(
-            attend_kernel, len(queries), len(kvs), head_size, acc is not None, count_out, streams
+            attend_kernel, head_size, (len(blocks), len(blocks[0])), acc is not None, count_out, streams
         ),
         out_shape=(shape,) * outs,
         in_specs=[SMEM, SMEM] + [VMEM] * len(operands),
         out_specs=(VMEM,) * outs,
         scratch_shapes=scratch,
         compiler_params=pltpu.CompilerParams(
-            vmem_limit_bytes=(16 << 20) + 2 * kvs[0].size * 2 * len(kvs)
+            vmem_limit_bytes=(16 << 20) + 4 * sum(part.size for part in parts)
         ),
         cost_estimate=pl.CostEstimate(flops=1 << 20, bytes_accessed=1 << 10, transcendentals=0),
         name="attend_last" if count_out else "attend",
     )(info, in_hbm(ids), *operands)
+
+
+def load_kernel(source, target, sem):
+    copy = pltpu.make_async_copy(source, target, sem)
+    copy.start()
+    copy.wait()
+
+
+def loaded(value):
+    return pl.pallas_call(
+        load_kernel,
+        out_shape=pltpu.VMEM(value.shape, value.dtype),
+        in_specs=[pl.BlockSpec(memory_space=pltpu.HBM)],
+        out_specs=pl.BlockSpec(memory_space=pl.ANY),
+        scratch_shapes=[pltpu.SemaphoreType.DMA(())],
+        compiler_params=pltpu.CompilerParams(vmem_limit_bytes=1 << 20),
+        cost_estimate=pl.CostEstimate(flops=0, bytes_accessed=1 << 20, transcendentals=0),
+        name="load",
+    )(in_hbm(value))
 
 
 def total_of(*parts):
@@ -310,7 +338,6 @@
     chip, core = seq_at // 2, seq_at % 2
     index_at = lambda offset: ring_index((place + offset + ring) % ring, ring)
     numbers = lambda values: jnp.stack(values).astype(jnp.int32)
-    id_col = lax.dynamic_slice_in_dim(scale_ids, seq_at * rows, rows)[:, None]
     at = [index_at(offset) for offset in range(ring)]
 
     streams, ways = (0, 1), ((0, 1), (1, -1))
@@ -344,7 +371,8 @@
                     targets.append((s * half, (2 * step - 1 + way) * width))
     wide = placed(targets, blocks, wide, (rows, ring * width))
     lasts = [held[0][0], held[1][1]]
-    query, kv, *pieces = project(head_scale, wide, weights, lasts, head_size)
+    query, *kvs = project(head_scale, wide, weights, lasts, 3, head_size)
+    halves, pieces = kvs[:2], kvs[2:]
 
     far, straight, crossed = [], [], []
     for step in range(outer):
@@ -352,25 +380,21 @@
         straight.append((source + core) * rows)
         crossed.append((source + 1 - core) * rows)
         if step:
-            far.append(lax.ppermute(kv, "seq", [
-                (2 * a + b, 2 * ((a + step) % outer) + b) for a in range(outer) for b in (0, 1)
-            ]))
+            shift = [(2 * a + b, 2 * ((a + step) % outer) + b) for a in range(outer) for b in (0, 1)]
+            far.append([lax.ppermute(kv, "seq", shift) for kv in halves])
     first = [seq_at * rows]
-    places = crossed[0] + jnp.arange(len(pieces)) * half
-    near = [(kv, straight[0])], [(swapped(piece, seqs), places[s]) for s, piece in enumerate(pieces)]
-    acc = None
-    for group in (*near, list(zip(far, straight[1:]))):
-        keys = [key for key, place in group]
-        if acc is not None:
-            acc, keys = lax.optimization_barrier((acc, keys))
-        info = numbers([place for key, place in group] + first)
-        far_crossed = [swapped(block, seqs) for block in keys]
-        (acc,) = attend(info, scale_ids, [query], id_col, keys, head_size, acc)
+    (acc,) = attend(numbers(straight[:1] + first), scale_ids, query, [halves], head_size)
+    near = [[swapped(piece, seqs) for piece in pieces]]
+    acc, near = lax.optimization_barrier((acc, near))
+    (acc,) = attend(numbers(crossed[:1] + first), scale_ids, query, near, head_size, acc)
+    acc, far, w_near = lax.optimization_barrier((acc, far, loaded(w_out)))
+    far_crossed = [[swapped(part, seqs) for part in block] for block in far]
+    (acc,) = attend(numbers(straight[1:] + first), scale_ids, query, far, head_size, acc)
 
     goals = [[*range(up, 0, -1), *range(-down, 0), 0] for up, down in reach]
     info = numbers(crossed[1:] + first + [at[goal % ring] for goal in goals[0] + goals[1]])
     parts = attend(
-        info, scale_ids, [query], id_col, far_crossed, head_size, acc, w_out, len(streams)
+        info, scale_ids, query, far_crossed, head_size, acc, w_near, len(streams)
     )
     parts = [dict(zip(goals[s], parts[s * ring : (s + 1) * ring])) for s in streams]
     sums = [[None, None] for s in streams]

time: 72.4 us -> 76 us (1.050)
  local copies, waits for them, and re-layouts: 2.07 us -> 5.92 us
  waiting for transfers between devices: 20.7 us -> 17.9 us
  starting transfers between devices: 30.1 us -> 32.3 us
    unnamed x0 -> x12, local copies, waits for them, and re-layouts: none -> 4.76 us
    ppermute x1 -> x2, waiting for transfers between devices: 2.75 us -> 0.01 us  [body(): far.append([lax.ppermute(kv, 'seq', shift) for kv in halves])]
    ppermute x1 -> x2, starting transfers between devices: 0.53 us -> 2.09 us  [body(): far.append([lax.ppermute(kv, 'seq', shift) for kv in halves])]
    pallas_call x5 -> x6, Pallas kernels: 13.1 us -> 13.6 us  [the longest x4 9.47 us: attend(): pl.pallas_call(functools.partial(attend_kernel, head_size, (len(blocks),...]
  transfers between devices with their start and end apart: 32 -> 35, of which waited for: 15 -> 15; matrix products, arithmetic and copies ran while one was open for 2% -> 1% of each run, Pallas kernels for 16% -> 16%
where the time goes in v13:
time: 76 us; the launch traced here: 75.5 us
  starting transfers between devices  32.3 us (42%)
  waiting for transfers between devices  17.9 us (24%)
  Pallas kernels  17.8 us (23%)
  local copies, waits for them, and re-layouts  5.92 us (8%)
  other arithmetic  1.4 us (2%)
    ppermute x28, starting transfers between devices, along(): lax.ppermute(value, 'head', [(order[p], order[(p + step) % count]) for p...  29.1 us
    ppermute x28, waiting for transfers between devices, along(): lax.ppermute(value, 'head', [(order[p], order[(p + step) % count]) for p...  17.9 us
    pallas_call x4, Pallas kernels, attend(): pl.pallas_call(functools.partial(attend_kernel, head_size, (len(blocks),...  9.47 us
    unnamed x12, local copies, waits for them, and re-layouts  4.76 us
    pallas_call x1, Pallas kernels, fold_gain(): pl.pallas_call(functools.partial(fold_kernel, order), out_shape=pltpu.VME...  3.01 us
    pallas_call x1, Pallas kernels, project(): pl.pallas_call(functools.partial(project_kernel, head_size, len(lasts)),...  2.87 us
    ppermute x2, starting transfers between devices, body(): far.append([lax.ppermute(kv, 'seq', shift) for kv in halves])  2.09 us
  transfers between devices with their start and end apart: 35, of which 15 were waited for; matrix products, arithmetic and copies ran while one was open for 1% of the time, Pallas kernels for 16%

profile of v13, /device:TPU:10, one launch (start us, length us, event | category | flops | bytes accessed | tf_op | source)
XLA Modules:
  0.0 75.5 jit_solution(14598996081862474700)
XLA Ops:
  0.0 1.0 %fusion = (bf16[256,256]{1,0:T(8,128)(2,1)S(1)}, bf16[256,256]{1,0:T(8,128)(2,1)S(1)}) fusion(bf16[512,256]{1,0:T(8,128)(2,1)} %refs_0_.1), kind=kLoop, calls=%fused_computation.16 | loop fusion | bytes 524288 | tf_op jit(solution)/shard_map/slice | solution.py:348
  1.0 0.5 collective-permute-start.9
  1.5 1.6 %collective-permute-start = (bf16[256,256]{1,0:T(8,128)(2,1)S(1)}, bf16[256,256]{1,0:T(8,128)(2,1)S(1)}, u32[]{:S(2)}, u32[]{:S(2)}) collective-permute-start(bf16[256,256]{1,0:T(8,128)(2,1)S(1)} %get-tuple-element.74), channel_id=1, source_target_pairs={{0,2},{2,4},{4,6},{6,7},{7,5},{5,3},{3,1},{1,0},{8,10},{10,12},{12... | collective-permute-start | bytes 393224 | tf_op jit(solution)/shard_map/ppermute | solution.py:33
  3.5 1.6 %collective-permute-start.6 = (bf16[256,256]{1,0:T(8,128)(2,1)S(1)}, bf16[256,256]{1,0:T(8,128)(2,1)S(1)}, u32[]{:S(2)}, u32[]{:S(2)}) collective-permute-start(bf16[256,256]{1,0:T(8,128)(2,1)S(1)} %get-tuple-element.73), channel_id=1, source_target_pairs={{0,2},{2,4},{4,6},{6,7},{7,5},{5,3},{3,1},{1,0},{8,10},{10,12},{12... | collective-permute-start | bytes 393224 | tf_op jit(solution)/shard_map/ppermute | solution.py:33
  5.2 3.0 %fold_gain.1.w_ref = bf16[3,2048,256]{2,1,0:T(8,128)(2,1)S(1)} custom-call(s32[8]{0:T(128)S(1)} %stack.84.at, f32[16,128]{1,0:T(8,128)} %bitcast.19, bf16[3,2048,256]{2,1,0:T(8,128)(2,1)} %w_hbm.1), custom_call_target="tpu_custom_call" | custom-call | flops 1572864 | bytes 6291456 | tf_op jit(solution)/shard_map/fold_gain/pallas_call | solution.py:77
  8.2 0.5 collective-permute-start.10
  8.7 1.6 %collective-permute-start.1 = (bf16[256,256]{1,0:T(8,128)(2,1)S(1)}, bf16[256,256]{1,0:T(8,128)(2,1)S(1)}, u32[]{:S(2)}, u32[]{:S(2)}) collective-permute-start(bf16[256,256]{1,0:T(8,128)(2,1)S(1)} %collective-permute-done.refs_1_), channel_id=1, source_target_pairs={{0,2},{2,4},{4,6},{6,7},{7,5},{5,3},{3,1},{1,0},{8,10},{10,12},{12... | collective-permute-start | bytes 393224 | tf_op jit(solution)/shard_map/ppermute | solution.py:33
  10.7 1.6 %collective-permute-start.7 = (bf16[256,256]{1,0:T(8,128)(2,1)S(1)}, bf16[256,256]{1,0:T(8,128)(2,1)S(1)}, u32[]{:S(2)}, u32[]{:S(2)}) collective-permute-start(bf16[256,256]{1,0:T(8,128)(2,1)S(1)} %collective-permute-done.6.refs_3_), channel_id=1, source_target_pairs={{0,2},{2,4},{4,6},{6,7},{7,5},{5,3},{3,1},{1,0},{8,10},{10,12},{12... | collective-permute-start | bytes 393224 | tf_op jit(solution)/shard_map/ppermute | solution.py:33
  12.3 1.9 %collective-permute-done.10.refs_3_ = bf16[256,256]{1,0:T(8,128)(2,1)S(1)} collective-permute-done((bf16[256,256]{1,0:T(8,128)(2,1)S(1)}, bf16[256,256]{1,0:T(8,128)(2,1)S(1)}, u32[]{:S(2)}, u32[]{:S(2)}) %collective-permute-start.10) | collective-permute-done | bytes 131104 | tf_op jit(solution)/shard_map/ppermute | solution.py:33
  14.7 1.6 %collective-permute-start.2 = (bf16[256,256]{1,0:T(8,128)(2,1)S(1)}, bf16[256,256]{1,0:T(8,128)(2,1)S(1)}, u32[]{:S(2)}, u32[]{:S(2)}) collective-permute-start(bf16[256,256]{1,0:T(8,128)(2,1)S(1)} %collective-permute-done.1.refs_0_), channel_id=1, source_target_pairs={{0,2},{2,4},{4,6},{6,7},{7,5},{5,3},{3,1},{1,0},{8,10},{10,12},{12... | collective-permute-start | bytes 393224 | tf_op jit(solution)/shard_map/ppermute | solution.py:33
  16.3 1.0 %place.3.refs_4_ = bf16[512,2048]{1,0:T(8,128)(2,1)S(1)} custom-call(bf16[512,256]{1,0:T(8,128)(2,1)} %refs_0_.1, bf16[256,256]{1,0:T(8,128)(2,1)S(1)} %collective-permute-done.refs_1_, bf16[256,256]{1,0:T(8,128)(2,1)S(1)} %collective-permute-done.3.refs_2_, bf16[256,256]{1,0:T(8,128)(2,1)S(1)} %collective-permute-done.6.refs_3_, ...), custom_call_target="tpu_custom_call" | custom-call | bytes 1048576 | tf_op jit(solution)/shard_map/place/pallas_call | solution.py:106
  17.3 0.5 collective-permute-start.5
  17.8 1.6 %collective-permute-start.8 = (bf16[256,256]{1,0:T(8,128)(2,1)S(1)}, bf16[256,256]{1,0:T(8,128)(2,1)S(1)}, u32[]{:S(2)}, u32[]{:S(2)}) collective-permute-start(bf16[256,256]{1,0:T(8,128)(2,1)S(1)} %collective-permute-done.7.refs_2_), channel_id=1, source_target_pairs={{0,2},{2,4},{4,6},{6,7},{7,5},{5,3},{3,1},{1,0},{8,10},{10,12},{12... | collective-permute-start | bytes 393224 | tf_op jit(solution)/shard_map/ppermute | solution.py:33
  20.4 1.6 %collective-permute-start.12 = (bf16[256,256]{1,0:T(8,128)(2,1)S(1)}, bf16[256,256]{1,0:T(8,128)(2,1)S(1)}, u32[]{:S(2)}, u32[]{:S(2)}) collective-permute-start(bf16[256,256]{1,0:T(8,128)(2,1)S(1)} %collective-permute-done.2.refs_0_), channel_id=1, source_target_pairs={{0,2},{2,4},{4,6},{6,7},{7,5},{5,3},{3,1},{1,0},{8,10},{10,12},{12... | collective-permute-start | bytes 393224 | tf_op jit(solution)/shard_map/ppermute | solution.py:33
  22.9 2.0 %collective-permute-done.13.refs_1_ = bf16[256,256]{1,0:T(8,128)(2,1)S(1)} collective-permute-done((bf16[256,256]{1,0:T(8,128)(2,1)S(1)}, bf16[256,256]{1,0:T(8,128)(2,1)S(1)}, u32[]{:S(2)}, u32[]{:S(2)}) %collective-permute-start.13) | collective-permute-done | bytes 131104 | tf_op jit(solution)/shard_map/ppermute | solution.py:33
  25.4 2.9 %project.1 = (bf16[512,256]{1,0:T(8,128)(2,1)S(1)}, bf16[256,512]{1,0:T(8,128)(2,1)S(1)}, bf16[256,512]{1,0:T(8,128)(2,1)S(1)}, bf16[160,512]{1,0:T(8,128)(2,1)}...) custom-call(f32[2]{0:T(128)} %factor.1, bf16[512,2048]{1,0:T(8,128)(2,1)S(1)} %place.5.wide, ...), custom_call_target="tpu_custom_call" | custom-call | flops 1610612736 | bytes 5242880 | tf_op jit(solution)/shard_map/project/pallas_call | solution.py:165
  28.2 0.5 collective-permute-start.17
  28.8 1.6 %collective-permute-start.18 = (bf16[256,512]{1,0:T(8,128)(2,1)S(1)}, bf16[256,512]{1,0:T(8,128)(2,1)S(1)}, u32[]{:S(2)}, u32[]{:S(2)}) collective-permute-start(bf16[256,512]{1,0:T(8,128)(2,1)S(1)} %get-tuple-element.45.refs_1_), channel_id=1, source_target_pairs={{0,16},{8,24},{16,0},{24,8},{1,17},{9,25},{17,1},{25,9},{2,18},{10... | collective-permute-start | bytes 786440 | tf_op jit(solution)/shard_map/ppermute | solution.py:384
  30.3 0.5 collective-permute-start.16
  30.9 1.2 %load.1.refs_3_ = bf16[256,2048]{1,0:T(8,128)(2,1)S(1)} custom-call(bf16[256,2048]{1,0:T(8,128)(2,1)} %source.1), custom_call_target="tpu_custom_call" | custom-call | bytes 1048576 | tf_op jit(solution)/shard_map/load/pallas_call | solution.py:314
  32.2 2.2 %attend.3.refs_3_ = f32[512,512]{1,0:T(8,128)S(1)} custom-call(s32[2]{0:T(128)S(1)} %pad_add_fusion.1.info, s32[2048]{0:T(1024)} %ids.7, bf16[512,256]{1,0:T(8,128)(2,1)S(1)} %get-tuple-element.43.q_ref, s32[8,1,256]{2,1,0:T(1,128)} %bitcast.15, bf16[256,512]{1,0:T(8,128)(2,1)S(1)} %get-tuple-element.44.refs_0_, bf16[256,512]{1,0:T(8,128)(2,1)S(1)} %get-tuple-element.45.refs_1_), custom_call_target="tpu_custom_call" | custom-call | flops 1048576 | bytes 1024 | tf_op jit(solution)/shard_map/attend/pallas_call | solution.py:291
  34.5 0.7 copy-done.4
  35.2 0.7 copy-done
  35.8 0.7 copy-done.2
  36.5 0.9 %copy-done.1 = bf16[176,512]{1,0:T(8,128)(2,1)S(1)} copy-done((bf16[176,512]{1,0:T(8,128)(2,1)S(1)}, bf16[176,512]{1,0:T(8,128)(2,1)}, u32[]{:S(2)}) %copy-start.1) | copy-done | bytes 180248
  37.4 0.9 %copy-done.3 = bf16[176,512]{1,0:T(8,128)(2,1)S(1)} copy-done((bf16[176,512]{1,0:T(8,128)(2,1)S(1)}, bf16[176,512]{1,0:T(8,128)(2,1)}, u32[]{:S(2)}) %copy-start.3) | copy-done | bytes 180248
  38.4 0.9 %copy-done.5 = bf16[160,512]{1,0:T(8,128)(2,1)S(1)} copy-done((bf16[160,512]{1,0:T(8,128)(2,1)S(1)}, bf16[160,512]{1,0:T(8,128)(2,1)}, u32[]{:S(2)}) %copy-start.5) | copy-done | bytes 163864
  39.3 2.2 %attend.4.refs_2_ = f32[512,512]{1,0:T(8,128)S(1)} custom-call(s32[2]{0:T(128)S(1)} %pad_add_fusion.info, s32[2048]{0:T(1024)} %ids.7, bf16[512,256]{1,0:T(8,128)(2,1)S(1)} %get-tuple-element.43.q_ref, s32[8,1,256]{2,1,0:T(1,128)} %bitcast.16, bf16[160,512]{1,0:T(8,128)(2,1)S(1)} %copy-done.5, bf16[176,512]{1,0:T(8,128)(2,1)S(1)} %copy-done.1, ...), custom_call_target="tpu_custom_call" | custom-call | flops 1048576 | bytes 1024 | tf_op jit(solution)/shard_map/attend/pallas_call | solution.py:291
  42.3 2.1 %attend.5.refs_2_ = f32[512,512]{1,0:T(8,128)S(1)} custom-call(s32[2]{0:T(128)S(1)} %pad_add_fusion.2.info, s32[2048]{0:T(1024)} %ids.7, bf16[512,256]{1,0:T(8,128)(2,1)S(1)} %get-tuple-element.43.q_ref, s32[8,1,256]{2,1,0:T(1,128)} %bitcast.17, bf16[256,512]{1,0:T(8,128)(2,1)S(1)} %collective-permute-done.17.refs_0_, ...), custom_call_target="tpu_custom_call" | custom-call | flops 1048576 | bytes 1024 | tf_op jit(solution)/shard_map/attend/pallas_call | solution.py:291
  44.5 2.9 %attend_last.1 = (bf16[256,256]{1,0:T(8,128)(2,1)S(1)}, bf16[256,256]{1,0:T(8,128)(2,1)S(1)}, bf16[256,256]{1,0:T(8,128)(2,1)S(1)}, bf16[256,256]{1,0:T(8,128)(2...) custom-call(s32[18]{0:T(128)S(1)} %stack.83.info, ...), custom_call_target="tpu_custom_call" | custom-call | flops 1048576 | bytes 1024 | tf_op jit(solution)/shard_map/attend_last/pallas_call | solution.py:291
  47.3 1.6 %collective-permute-start.21 = (bf16[256,256]{1,0:T(8,128)(2,1)S(1)}, bf16[256,256]{1,0:T(8,128)(2,1)S(1)}, u32[]{:S(2)}, u32[]{:S(2)}) collective-permute-start(bf16[256,256]{1,0:T(8,128)(2,1)S(1)} %get-tuple-element.61), channel_id=1, source_target_pairs={{0,2},{2,4},{4,6},{6,7},{7,5},{5,3},{3,1},{1,0},{8,10},{10,12},{12... | collective-permute-start | bytes 393224 | tf_op jit(solution)/shard_map/ppermute | solution.py:33
  49.4 1.6 %collective-permute-start.28 = (bf16[256,256]{1,0:T(8,128)(2,1)S(1)}, bf16[256,256]{1,0:T(8,128)(2,1)S(1)}, u32[]{:S(2)}, u32[]{:S(2)}) collective-permute-start(bf16[256,256]{1,0:T(8,128)(2,1)S(1)} %get-tuple-element.68), channel_id=1, source_target_pairs={{0,2},{2,4},{4,6},{6,7},{7,5},{5,3},{3,1},{1,0},{8,10},{10,12},{12... | collective-permute-start | bytes 393224 | tf_op jit(solution)/shard_map/ppermute | solution.py:33
  51.4 2.3 %collective-permute-done.21 = bf16[256,256]{1,0:T(8,128)(2,1)S(1)} collective-permute-done((bf16[256,256]{1,0:T(8,128)(2,1)S(1)}, bf16[256,256]{1,0:T(8,128)(2,1)S(1)}, u32[]{:S(2)}, u32[]{:S(2)}) %collective-permute-start.21) | collective-permute-done | bytes 131104 | tf_op jit(solution)/shard_map/ppermute | solution.py:33
  53.7 1.6 %collective-permute-start.22 = (bf16[256,256]{1,0:T(8,128)(2,1)S(1)}, bf16[256,256]{1,0:T(8,128)(2,1)S(1)}, u32[]{:S(2)}, u32[]{:S(2)}) collective-permute-start(bf16[256,256]{1,0:T(8,128)(2,1)S(1)} %add_convert_fusion.11), channel_id=1, source_target_pairs={{0,2},{2,4},{4,6},{6,7},{7,5},{5,3},{3,1},{1,0},{8,10},{10,12},{12... | collective-permute-start | bytes 393224 | tf_op jit(solution)/shard_map/ppermute | solution.py:33
  55.4 0.5 collective-permute-start.26
  55.9 0.6 collective-permute-done.28
  56.5 1.6 %collective-permute-start.29 = (bf16[256,256]{1,0:T(8,128)(2,1)S(1)}, bf16[256,256]{1,0:T(8,128)(2,1)S(1)}, u32[]{:S(2)}, u32[]{:S(2)}) collective-permute-start(bf16[256,256]{1,0:T(8,128)(2,1)S(1)} %add_convert_fusion.5), channel_id=1, source_target_pairs={{0,2},{2,4},{4,6},{6,7},{7,5},{5,3},{3,1},{1,0},{8,10},{10,12},{12... | collective-permute-start | bytes 393224 | tf_op jit(solution)/shard_map/ppermute | solution.py:33
  58.7 0.7 collective-permute-done.22
  59.5 1.6 %collective-permute-start.23 = (bf16[256,256]{1,0:T(8,128)(2,1)S(1)}, bf16[256,256]{1,0:T(8,128)(2,1)S(1)}, u32[]{:S(2)}, u32[]{:S(2)}) collective-permute-start(bf16[256,256]{1,0:T(8,128)(2,1)S(1)} %add_convert_fusion.10), channel_id=1, source_target_pairs={{0,2},{2,4},{4,6},{6,7},{7,5},{5,3},{3,1},{1,0},{8,10},{10,12},{12... | collective-permute-start | bytes 393224 | tf_op jit(solution)/shard_map/ppermute | solution.py:33
  62.0 1.0 %collective-permute-done.29 = bf16[256,256]{1,0:T(8,128)(2,1)S(1)} collective-permute-done((bf16[256,256]{1,0:T(8,128)(2,1)S(1)}, bf16[256,256]{1,0:T(8,128)(2,1)S(1)}, u32[]{:S(2)}, u32[]{:S(2)}) %collective-permute-start.29) | collective-permute-done | bytes 131104 | tf_op jit(solution)/shard_map/ppermute | solution.py:33
  63.0 1.6 %collective-permute-start.30 = (bf16[256,256]{1,0:T(8,128)(2,1)S(1)}, bf16[256,256]{1,0:T(8,128)(2,1)S(1)}, u32[]{:S(2)}, u32[]{:S(2)}) collective-permute-start(bf16[256,256]{1,0:T(8,128)(2,1)S(1)} %add_convert_fusion.4), channel_id=1, source_target_pairs={{0,2},{2,4},{4,6},{6,7},{7,5},{5,3},{3,1},{1,0},{8,10},{10,12},{12... | collective-permute-start | bytes 393224 | tf_op jit(solution)/shard_map/ppermute | solution.py:33
  65.2 0.6 collective-permute-done.23
  65.8 1.6 %collective-permute-start.24 = (bf16[256,256]{1,0:T(8,128)(2,1)S(1)}, bf16[256,256]{1,0:T(8,128)(2,1)S(1)}, u32[]{:S(2)}, u32[]{:S(2)}) collective-permute-start(bf16[256,256]{1,0:T(8,128)(2,1)S(1)} %add_convert_fusion.9), channel_id=1, source_target_pairs={{0,2},{2,4},{4,6},{6,7},{7,5},{5,3},{3,1},{1,0},{8,10},{10,12},{12... | collective-permute-start | bytes 393224 | tf_op jit(solution)/shard_map/ppermute | solution.py:33
  67.5 2.2 %collective-permute-done.33 = bf16[256,256]{1,0:T(8,128)(2,1)S(1)} collective-permute-done((bf16[256,256]{1,0:T(8,128)(2,1)S(1)}, bf16[256,256]{1,0:T(8,128)(2,1)S(1)}, u32[]{:S(2)}, u32[]{:S(2)}) %collective-permute-start.33) | collective-permute-done | bytes 131104 | tf_op jit(solution)/shard_map/ppermute | solution.py:33
  69.7 0.5 collective-permute-start.34
  70.2 0.6 collective-permute-done.24
  70.9 3.8 %collective-permute-done.34 = bf16[256,256]{1,0:T(8,128)(2,1)S(1)} collective-permute-done((bf16[256,256]{1,0:T(8,128)(2,1)S(1)}, bf16[256,256]{1,0:T(8,128)(2,1)S(1)}, u32[]{:S(2)}, u32[]{:S(2)}) %collective-permute-start.34) | collective-permute-done | bytes 131104 | tf_op jit(solution)/shard_map/ppermute | solution.py:33
  74.8 0.7 pad_maximum_fusion
  (63 shorter events, 7.9 us)
Async XLA Ops:
  1.0 7.2 %collective-permute-start.9 = (bf16[256,256]{1,0:T(8,128)(2,1)S(1)}, bf16[256,256]{1,0:T(8,128)(2,1)S(1)}, u32[]{:S(2)}, u32[]{:S(2)}) collective-permute-start(bf16[256,256]{1,0:T(8,128)(2,1)S(1)} %get-tuple-element.73), channel_id=1, source_target_pairs={{0,1},{2,0},{4,2},{6,4},{7,6},{5,7},{3,5},{1,3},{8,9},{10,8},{12,1... | collective-permute-start | bytes 393224 | tf_op jit(solution)/shard_map/ppermute | solution.py:33
  1.5 7.2 %collective-permute-start = (bf16[256,256]{1,0:T(8,128)(2,1)S(1)}, bf16[256,256]{1,0:T(8,128)(2,1)S(1)}, u32[]{:S(2)}, u32[]{:S(2)}) collective-permute-start(bf16[256,256]{1,0:T(8,128)(2,1)S(1)} %get-tuple-element.74), channel_id=1, source_target_pairs={{0,2},{2,4},{4,6},{6,7},{7,5},{5,3},{3,1},{1,0},{8,10},{10,12},{12... | collective-permute-start | bytes 393224 | tf_op jit(solution)/shard_map/ppermute | solution.py:33
  3.1 7.2 %collective-permute-start.3 = (bf16[256,256]{1,0:T(8,128)(2,1)S(1)}, bf16[256,256]{1,0:T(8,128)(2,1)S(1)}, u32[]{:S(2)}, u32[]{:S(2)}) collective-permute-start(bf16[256,256]{1,0:T(8,128)(2,1)S(1)} %get-tuple-element.74), channel_id=1, source_target_pairs={{0,1},{2,0},{4,2},{6,4},{7,6},{5,7},{3,5},{1,3},{8,9},{10,8},{12,1... | collective-permute-start | bytes 393224 | tf_op jit(solution)/shard_map/ppermute | solution.py:33
  3.5 7.2 %collective-permute-start.6 = (bf16[256,256]{1,0:T(8,128)(2,1)S(1)}, bf16[256,256]{1,0:T(8,128)(2,1)S(1)}, u32[]{:S(2)}, u32[]{:S(2)}) collective-permute-start(bf16[256,256]{1,0:T(8,128)(2,1)S(1)} %get-tuple-element.73), channel_id=1, source_target_pairs={{0,2},{2,4},{4,6},{6,7},{7,5},{5,3},{3,1},{1,0},{8,10},{10,12},{12... | collective-permute-start | bytes 393224 | tf_op jit(solution)/shard_map/ppermute | solution.py:33
  8.2 6.0 %collective-permute-start.10 = (bf16[256,256]{1,0:T(8,128)(2,1)S(1)}, bf16[256,256]{1,0:T(8,128)(2,1)S(1)}, u32[]{:S(2)}, u32[]{:S(2)}) collective-permute-start(bf16[256,256]{1,0:T(8,128)(2,1)S(1)} %collective-permute-done.9.refs_4_), channel_id=1, source_target_pairs={{0,1},{2,0},{4,2},{6,4},{7,6},{5,7},{3,5},{1,3},{8,9},{10,8},{12,1... | collective-permute-start | bytes 393224 | tf_op jit(solution)/shard_map/ppermute | solution.py:33
  8.7 6.0 %collective-permute-start.1 = (bf16[256,256]{1,0:T(8,128)(2,1)S(1)}, bf16[256,256]{1,0:T(8,128)(2,1)S(1)}, u32[]{:S(2)}, u32[]{:S(2)}) collective-permute-start(bf16[256,256]{1,0:T(8,128)(2,1)S(1)} %collective-permute-done.refs_1_), channel_id=1, source_target_pairs={{0,2},{2,4},{4,6},{6,7},{7,5},{5,3},{3,1},{1,0},{8,10},{10,12},{12... | collective-permute-start | bytes 393224 | tf_op jit(solution)/shard_map/ppermute | solution.py:33
  10.3 7.0 %collective-permute-start.4 = (bf16[256,256]{1,0:T(8,128)(2,1)S(1)}, bf16[256,256]{1,0:T(8,128)(2,1)S(1)}, u32[]{:S(2)}, u32[]{:S(2)}) collective-permute-start(bf16[256,256]{1,0:T(8,128)(2,1)S(1)} %collective-permute-done.3.refs_2_), channel_id=1, source_target_pairs={{0,1},{2,0},{4,2},{6,4},{7,6},{5,7},{3,5},{1,3},{8,9},{10,8},{12,1... | collective-permute-start | bytes 393224 | tf_op jit(solution)/shard_map/ppermute | solution.py:33
  10.7 7.1 %collective-permute-start.7 = (bf16[256,256]{1,0:T(8,128)(2,1)S(1)}, bf16[256,256]{1,0:T(8,128)(2,1)S(1)}, u32[]{:S(2)}, u32[]{:S(2)}) collective-permute-start(bf16[256,256]{1,0:T(8,128)(2,1)S(1)} %collective-permute-done.6.refs_3_), channel_id=1, source_target_pairs={{0,2},{2,4},{4,6},{6,7},{7,5},{5,3},{3,1},{1,0},{8,10},{10,12},{12... | collective-permute-start | bytes 393224 | tf_op jit(solution)/shard_map/ppermute | solution.py:33
  14.2 5.7 %collective-permute-start.11 = (bf16[256,256]{1,0:T(8,128)(2,1)S(1)}, bf16[256,256]{1,0:T(8,128)(2,1)S(1)}, u32[]{:S(2)}, u32[]{:S(2)}) collective-permute-start(bf16[256,256]{1,0:T(8,128)(2,1)S(1)} %collective-permute-done.10.refs_3_), channel_id=1, source_target_pairs={{0,1},{2,0},{4,2},{6,4},{7,6},{5,7},{3,5},{1,3},{8,9},{10,8},{12,1... | collective-permute-start | bytes 393224 | tf_op jit(solution)/shard_map/ppermute | solution.py:33
  14.7 5.7 %collective-permute-start.2 = (bf16[256,256]{1,0:T(8,128)(2,1)S(1)}, bf16[256,256]{1,0:T(8,128)(2,1)S(1)}, u32[]{:S(2)}, u32[]{:S(2)}) collective-permute-start(bf16[256,256]{1,0:T(8,128)(2,1)S(1)} %collective-permute-done.1.refs_0_), channel_id=1, source_target_pairs={{0,2},{2,4},{4,6},{6,7},{7,5},{5,3},{3,1},{1,0},{8,10},{10,12},{12... | collective-permute-start | bytes 393224 | tf_op jit(solution)/shard_map/ppermute | solution.py:33
  17.3 5.0 %collective-permute-start.5 = (bf16[256,256]{1,0:T(8,128)(2,1)S(1)}, bf16[256,256]{1,0:T(8,128)(2,1)S(1)}, u32[]{:S(2)}, u32[]{:S(2)}) collective-permute-start(bf16[256,256]{1,0:T(8,128)(2,1)S(1)} %collective-permute-done.4.refs_1_), channel_id=1, source_target_pairs={{0,1},{2,0},{4,2},{6,4},{7,6},{5,7},{3,5},{1,3},{8,9},{10,8},{12,1... | collective-permute-start | bytes 393224 | tf_op jit(solution)/shard_map/ppermute | solution.py:33
  17.8 5.0 %collective-permute-start.8 = (bf16[256,256]{1,0:T(8,128)(2,1)S(1)}, bf16[256,256]{1,0:T(8,128)(2,1)S(1)}, u32[]{:S(2)}, u32[]{:S(2)}) collective-permute-start(bf16[256,256]{1,0:T(8,128)(2,1)S(1)} %collective-permute-done.7.refs_2_), channel_id=1, source_target_pairs={{0,2},{2,4},{4,6},{6,7},{7,5},{5,3},{3,1},{1,0},{8,10},{10,12},{12... | collective-permute-start | bytes 393224 | tf_op jit(solution)/shard_map/ppermute | solution.py:33
  19.9 5.0 %collective-permute-start.13 = (bf16[256,256]{1,0:T(8,128)(2,1)S(1)}, bf16[256,256]{1,0:T(8,128)(2,1)S(1)}, u32[]{:S(2)}, u32[]{:S(2)}) collective-permute-start(bf16[256,256]{1,0:T(8,128)(2,1)S(1)} %collective-permute-done.11.refs_3_), channel_id=1, source_target_pairs={{0,1},{2,0},{4,2},{6,4},{7,6},{5,7},{3,5},{1,3},{8,9},{10,8},{12,1... | collective-permute-start | bytes 393224 | tf_op jit(solution)/shard_map/ppermute | solution.py:33
  20.4 5.0 %collective-permute-start.12 = (bf16[256,256]{1,0:T(8,128)(2,1)S(1)}, bf16[256,256]{1,0:T(8,128)(2,1)S(1)}, u32[]{:S(2)}, u32[]{:S(2)}) collective-permute-start(bf16[256,256]{1,0:T(8,128)(2,1)S(1)} %collective-permute-done.2.refs_0_), channel_id=1, source_target_pairs={{0,2},{2,4},{4,6},{6,7},{7,5},{5,3},{3,1},{1,0},{8,10},{10,12},{12... | collective-permute-start | bytes 393224 | tf_op jit(solution)/shard_map/ppermute | solution.py:33
  28.2 13.3 %collective-permute-start.17 = (bf16[256,512]{1,0:T(8,128)(2,1)S(1)}, bf16[256,512]{1,0:T(8,128)(2,1)S(1)}, u32[]{:S(2)}, u32[]{:S(2)}) collective-permute-start(bf16[256,512]{1,0:T(8,128)(2,1)S(1)} %get-tuple-element.44.refs_0_), channel_id=1, source_target_pairs={{0,16},{8,24},{16,0},{24,8},{1,17},{9,25},{17,1},{25,9},{2,18},{10... | collective-permute-start | bytes 786440 | tf_op jit(solution)/shard_map/ppermute | solution.py:384
  28.8 12.8 %collective-permute-start.18 = (bf16[256,512]{1,0:T(8,128)(2,1)S(1)}, bf16[256,512]{1,0:T(8,128)(2,1)S(1)}, u32[]{:S(2)}, u32[]{:S(2)}) collective-permute-start(bf16[256,512]{1,0:T(8,128)(2,1)S(1)} %get-tuple-element.45.refs_1_), channel_id=1, source_target_pairs={{0,16},{8,24},{16,0},{24,8},{1,17},{9,25},{17,1},{25,9},{2,18},{10... | collective-permute-start | bytes 786440 | tf_op jit(solution)/shard_map/ppermute | solution.py:384
  30.3 4.8 %collective-permute-start.15 = (bf16[176,512]{1,0:T(8,128)(2,1)S(1)}, bf16[176,512]{1,0:T(8,128)(2,1)S(1)}, u32[]{:S(2)}, u32[]{:S(2)}) collective-permute-start(bf16[176,512]{1,0:T(8,128)(2,1)S(1)} %get-tuple-element.47), channel_id=1, source_target_pairs={{0,8},{8,0},{16,24},{24,16},{1,9},{9,1},{17,25},{25,17},{2,10},{10... | collective-permute-start | bytes 540680 | tf_op jit(solution)/shard_map/ppermute | solution.py:39
  30.3 5.5 %collective-permute-start.16 = (bf16[176,512]{1,0:T(8,128)(2,1)S(1)}, bf16[176,512]{1,0:T(8,128)(2,1)S(1)}, u32[]{:S(2)}, u32[]{:S(2)}) collective-permute-start(bf16[176,512]{1,0:T(8,128)(2,1)S(1)} %get-tuple-element.48), channel_id=1, source_target_pairs={{0,8},{8,0},{16,24},{24,16},{1,9},{9,1},{17,25},{25,17},{2,10},{10... | collective-permute-start | bytes 540680 | tf_op jit(solution)/shard_map/ppermute | solution.py:39
  30.8 3.6 %collective-permute-start.14 = (bf16[160,512]{1,0:T(8,128)(2,1)}, bf16[160,512]{1,0:T(8,128)(2,1)S(1)}, u32[]{:S(2)}, u32[]{:S(2)}) collective-permute-start(bf16[160,512]{1,0:T(8,128)(2,1)} %get-tuple-element.46), channel_id=1, source_target_pairs={{0,8},{8,0},{16,24},{24,16},{1,9},{9,1},{17,25},{25,17},{2,10},{10... | collective-permute-start | bytes 491528 | tf_op jit(solution)/shard_map/ppermute | solution.py:39
  34.5 0.7 copy-start.4
  35.2 0.7 copy-start
  35.8 0.7 copy-start.2
  36.5 0.9 %copy-start.1 = (bf16[176,512]{1,0:T(8,128)(2,1)S(1)}, bf16[176,512]{1,0:T(8,128)(2,1)}, u32[]{:S(2)}) copy-start(bf16[176,512]{1,0:T(8,128)(2,1)} %copy-done) | copy-start | bytes 540676
  37.4 0.9 %copy-start.3 = (bf16[176,512]{1,0:T(8,128)(2,1)S(1)}, bf16[176,512]{1,0:T(8,128)(2,1)}, u32[]{:S(2)}) copy-start(bf16[176,512]{1,0:T(8,128)(2,1)} %copy-done.2) | copy-start | bytes 540676
  38.4 0.9 %copy-start.5 = (bf16[160,512]{1,0:T(8,128)(2,1)S(1)}, bf16[160,512]{1,0:T(8,128)(2,1)}, u32[]{:S(2)}) copy-start(bf16[160,512]{1,0:T(8,128)(2,1)} %copy-done.4) | copy-start | bytes 491524
  41.5 2.9 %collective-permute-start.19 = (bf16[256,512]{1,0:T(8,128)(2,1)S(1)}, bf16[256,512]{1,0:T(8,128)(2,1)S(1)}, u32[]{:S(2)}, u32[]{:S(2)}) collective-permute-start(bf16[256,512]{1,0:T(8,128)(2,1)S(1)} %collective-permute-done.17.refs_0_), channel_id=1, source_target_pairs={{0,8},{8,0},{16,24},{24,16},{1,9},{9,1},{17,25},{25,17},{2,10},{10... | collective-permute-start | bytes 786440 | tf_op jit(solution)/shard_map/ppermute | solution.py:39
  41.9 2.5 %collective-permute-start.20 = (bf16[256,512]{1,0:T(8,128)(2,1)S(1)}, bf16[256,512]{1,0:T(8,128)(2,1)S(1)}, u32[]{:S(2)}, u32[]{:S(2)}) collective-permute-start(bf16[256,512]{1,0:T(8,128)(2,1)S(1)} %collective-permute-done.18.refs_1_), channel_id=1, source_target_pairs={{0,8},{8,0},{16,24},{24,16},{1,9},{9,1},{17,25},{25,17},{2,10},{10... | collective-permute-start | bytes 786440 | tf_op jit(solution)/shard_map/ppermute | solution.py:39
  47.3 6.4 %collective-permute-start.21 = (bf16[256,256]{1,0:T(8,128)(2,1)S(1)}, bf16[256,256]{1,0:T(8,128)(2,1)S(1)}, u32[]{:S(2)}, u32[]{:S(2)}) collective-permute-start(bf16[256,256]{1,0:T(8,128)(2,1)S(1)} %get-tuple-element.61), channel_id=1, source_target_pairs={{0,2},{2,4},{4,6},{6,7},{7,5},{5,3},{3,1},{1,0},{8,10},{10,12},{12... | collective-permute-start | bytes 393224 | tf_op jit(solution)/shard_map/ppermute | solution.py:33
  49.0 6.4 %collective-permute-start.25 = (bf16[256,256]{1,0:T(8,128)(2,1)S(1)}, bf16[256,256]{1,0:T(8,128)(2,1)S(1)}, u32[]{:S(2)}, u32[]{:S(2)}) collective-permute-start(bf16[256,256]{1,0:T(8,128)(2,1)S(1)} %get-tuple-element.64), channel_id=1, source_target_pairs={{0,1},{2,0},{4,2},{6,4},{7,6},{5,7},{3,5},{1,3},{8,9},{10,8},{12,1... | collective-permute-start | bytes 393224 | tf_op jit(solution)/shard_map/ppermute | solution.py:33
  49.4 7.1 %collective-permute-start.28 = (bf16[256,256]{1,0:T(8,128)(2,1)S(1)}, bf16[256,256]{1,0:T(8,128)(2,1)S(1)}, u32[]{:S(2)}, u32[]{:S(2)}) collective-permute-start(bf16[256,256]{1,0:T(8,128)(2,1)S(1)} %get-tuple-element.68), channel_id=1, source_target_pairs={{0,2},{2,4},{4,6},{6,7},{7,5},{5,3},{3,1},{1,0},{8,10},{10,12},{12... | collective-permute-start | bytes 393224 | tf_op jit(solution)/shard_map/ppermute | solution.py:33
  51.0 7.2 %collective-permute-start.31 = (bf16[256,256]{1,0:T(8,128)(2,1)S(1)}, bf16[256,256]{1,0:T(8,128)(2,1)S(1)}, u32[]{:S(2)}, u32[]{:S(2)}) collective-permute-start(bf16[256,256]{1,0:T(8,128)(2,1)S(1)} %get-tuple-element.72), channel_id=1, source_target_pairs={{0,1},{2,0},{4,2},{6,4},{7,6},{5,7},{3,5},{1,3},{8,9},{10,8},{12,1... | collective-permute-start | bytes 393224 | tf_op jit(solution)/shard_map/ppermute | solution.py:33
  53.7 5.7 %collective-permute-start.22 = (bf16[256,256]{1,0:T(8,128)(2,1)S(1)}, bf16[256,256]{1,0:T(8,128)(2,1)S(1)}, u32[]{:S(2)}, u32[]{:S(2)}) collective-permute-start(bf16[256,256]{1,0:T(8,128)(2,1)S(1)} %add_convert_fusion.11), channel_id=1, source_target_pairs={{0,2},{2,4},{4,6},{6,7},{7,5},{5,3},{3,1},{1,0},{8,10},{10,12},{12... | collective-permute-start | bytes 393224 | tf_op jit(solution)/shard_map/ppermute | solution.py:33
  55.4 6.0 %collective-permute-start.26 = (bf16[256,256]{1,0:T(8,128)(2,1)S(1)}, bf16[256,256]{1,0:T(8,128)(2,1)S(1)}, u32[]{:S(2)}, u32[]{:S(2)}) collective-permute-start(bf16[256,256]{1,0:T(8,128)(2,1)S(1)} %add_convert_fusion.8), channel_id=1, source_target_pairs={{0,1},{2,0},{4,2},{6,4},{7,6},{5,7},{3,5},{1,3},{8,9},{10,8},{12,1... | collective-permute-start | bytes 393224 | tf_op jit(solution)/shard_map/ppermute | solution.py:33
  56.5 6.4 %collective-permute-start.29 = (bf16[256,256]{1,0:T(8,128)(2,1)S(1)}, bf16[256,256]{1,0:T(8,128)(2,1)S(1)}, u32[]{:S(2)}, u32[]{:S(2)}) collective-permute-start(bf16[256,256]{1,0:T(8,128)(2,1)S(1)} %add_convert_fusion.5), channel_id=1, source_target_pairs={{0,2},{2,4},{4,6},{6,7},{7,5},{5,3},{3,1},{1,0},{8,10},{10,12},{12... | collective-permute-start | bytes 393224 | tf_op jit(solution)/shard_map/ppermute | solution.py:33
  58.2 6.4 %collective-permute-start.32 = (bf16[256,256]{1,0:T(8,128)(2,1)S(1)}, bf16[256,256]{1,0:T(8,128)(2,1)S(1)}, u32[]{:S(2)}, u32[]{:S(2)}) collective-permute-start(bf16[256,256]{1,0:T(8,128)(2,1)S(1)} %add_convert_fusion.3), channel_id=1, source_target_pairs={{0,1},{2,0},{4,2},{6,4},{7,6},{5,7},{3,5},{1,3},{8,9},{10,8},{12,1... | collective-permute-start | bytes 393224 | tf_op jit(solution)/shard_map/ppermute | solution.py:33
  59.5 6.3 %collective-permute-start.23 = (bf16[256,256]{1,0:T(8,128)(2,1)S(1)}, bf16[256,256]{1,0:T(8,128)(2,1)S(1)}, u32[]{:S(2)}, u32[]{:S(2)}) collective-permute-start(bf16[256,256]{1,0:T(8,128)(2,1)S(1)} %add_convert_fusion.10), channel_id=1, source_target_pairs={{0,2},{2,4},{4,6},{6,7},{7,5},{5,3},{3,1},{1,0},{8,10},{10,12},{12... | collective-permute-start | bytes 393224 | tf_op jit(solution)/shard_map/ppermute | solution.py:33
  61.5 8.7 %collective-permute-start.27 = (bf16[256,256]{1,0:T(8,128)(2,1)S(1)}, bf16[256,256]{1,0:T(8,128)(2,1)S(1)}, u32[]{:S(2)}, u32[]{:S(2)}) collective-permute-start(bf16[256,256]{1,0:T(8,128)(2,1)S(1)} %add_convert_fusion.7), channel_id=1, source_target_pairs={{0,1},{2,0},{4,2},{6,4},{7,6},{5,7},{3,5},{1,3},{8,9},{10,8},{12,1... | collective-permute-start | bytes 393224 | tf_op jit(solution)/shard_map/ppermute | solution.py:33
  63.0 7.9 %collective-permute-start.30 = (bf16[256,256]{1,0:T(8,128)(2,1)S(1)}, bf16[256,256]{1,0:T(8,128)(2,1)S(1)}, u32[]{:S(2)}, u32[]{:S(2)}) collective-permute-start(bf16[256,256]{1,0:T(8,128)(2,1)S(1)} %add_convert_fusion.4), channel_id=1, source_target_pairs={{0,2},{2,4},{4,6},{6,7},{7,5},{5,3},{3,1},{1,0},{8,10},{10,12},{12... | collective-permute-start | bytes 393224 | tf_op jit(solution)/shard_map/ppermute | solution.py:33
  64.7 5.0 %collective-permute-start.33 = (bf16[256,256]{1,0:T(8,128)(2,1)S(1)}, bf16[256,256]{1,0:T(8,128)(2,1)S(1)}, u32[]{:S(2)}, u32[]{:S(2)}) collective-permute-start(bf16[256,256]{1,0:T(8,128)(2,1)S(1)} %add_convert_fusion.2), channel_id=1, source_target_pairs={{0,1},{2,0},{4,2},{6,4},{7,6},{5,7},{3,5},{1,3},{8,9},{10,8},{12,1... | collective-permute-start | bytes 393224 | tf_op jit(solution)/shard_map/ppermute | solution.py:33
  65.8 5.0 %collective-permute-start.24 = (bf16[256,256]{1,0:T(8,128)(2,1)S(1)}, bf16[256,256]{1,0:T(8,128)(2,1)S(1)}, u32[]{:S(2)}, u32[]{:S(2)}) collective-permute-start(bf16[256,256]{1,0:T(8,128)(2,1)S(1)} %add_convert_fusion.9), channel_id=1, source_target_pairs={{0,2},{2,4},{4,6},{6,7},{7,5},{5,3},{3,1},{1,0},{8,10},{10,12},{12... | collective-permute-start | bytes 393224 | tf_op jit(solution)/shard_map/ppermute | solution.py:33
  69.7 5.0 %collective-permute-start.34 = (bf16[256,256]{1,0:T(8,128)(2,1)S(1)}, bf16[256,256]{1,0:T(8,128)(2,1)S(1)}, u32[]{:S(2)}, u32[]{:S(2)}) collective-permute-start(bf16[256,256]{1,0:T(8,128)(2,1)S(1)} %add_convert_fusion.1), channel_id=1, source_target_pairs={{0,1},{2,0},{4,2},{6,4},{7,6},{5,7},{3,5},{1,3},{8,9},{10,8},{12,1... | collective-permute-start | bytes 393224 | tf_op jit(solution)/shard_map/ppermute | solution.py:33

commit v14 on v13

--- a/solution.py
+++ b/solution.py
@@ -116,27 +116,40 @@
     )(*operands)
 
 
-def project_kernel(head_size, count, factor, wide, w_ref, *refs):
-    lasts, q_ref = refs[:count], refs[count]
-    halves, pieces = refs[count + 1 : 2 * count + 1], refs[2 * count + 1 :]
+def begin_kernel(blocks, wide, w_ref, state):
+    rows, depth = wide.shape
+    out_width = w_ref.shape[2]
+    done = depth - depth // blocks
+    tile = math.gcd(rows, 256)
+    for first in range(0, rows, tile):
+        here = slice(first, first + tile)
+        for group in range(3):
+            state[here, group * out_width : (group + 1) * out_width] = jnp.dot(
+                wide[here, :done], w_ref[group, :done, :], preferred_element_type=F32
+            )
+        power = None
+        for lane in range(0, done, 128):
+            values = wide[here, lane : lane + 128].astype(F32)
+            power = values * values if power is None else power + values * values
+        state[here, 3 * out_width :] = power
+
+
+def finish_kernel(head_size, factor, state, w_ref, *refs):
+    count = (len(refs) - 2) // 2
+    lasts, (q_ref, kv_ref), pieces = refs[:count], refs[count : count + 2], refs[count + 2 :]
     rows, width = lasts[0].shape
     depth, out_width = w_ref.shape[1:]
-    done = depth - width
     for stream, last in enumerate(lasts):
         here = slice(stream * rows, (stream + 1) * rows)
-        kv_ref = halves[stream]
         q, k, v = (
-            jnp.dot(wide[here, :done], w_ref[group, :done, :], preferred_element_type=F32)
-            + jnp.dot(last[...], w_ref[group, done:, :], preferred_element_type=F32)
+            state[here, group * out_width : (group + 1) * out_width]
+            + jnp.dot(last[...], w_ref[group, depth - width :, :], preferred_element_type=F32)
             for group in range(3)
         )
-        power = None
-        for lane in range(0, depth, 128):
-            if lane < done:
-                values = wide[here, lane : lane + 128].astype(F32)
-            else:
-                values = last[:, lane - done : lane - done + 128].astype(F32)
-            power = values * values if power is None else power + values * values
+        power = state[here, 3 * out_width :]
+        for lane in range(0, width, 128):
+            values = last[:, lane : lane + 128].astype(F32)
+            power += values * values
         scale = lax.rsqrt(jnp.sum(power, axis=-1, keepdims=True) * (1.0 / depth) + 1e-06)
         q, k, v = q * scale, k * scale, v * scale
         for head in range(out_width // head_size):
@@ -145,40 +158,48 @@
             q_size = lax.rsqrt(jnp.sum(qh * qh, axis=-1, keepdims=True) + 1e-06)
             k_size = lax.rsqrt(jnp.sum(kh * kh, axis=-1, keepdims=True) + 1e-06)
             q_ref[here, lanes] = (qh * (q_size * (factor[head] * LOG2E))).astype(BF16)
-            kv_ref[:, lanes] = (kh * k_size).astype(BF16)
-        kv_ref[:, out_width:] = v.astype(BF16)
-    start = 0
-    for piece in pieces:
-        size = piece.shape[0]
-        for stream, half in enumerate(halves):
-            low, high = max(start, stream * rows), min(start + size, (stream + 1) * rows)
-            if low < high:
-                piece[low - start : high - start, :] = half[low - stream * rows : high - stream * rows, :]
-        start += size
-
-
-def project(factor, wide, weights, lasts, count_pieces, head_size):
-    rows = wide.shape[0]
-    units = rows // 16
-    sizes = [16 * ((units + n) // count_pieces) for n in range(count_pieces)]
-    groups, depth, out_width = weights.shape
-    return pl.pallas_call(
-        functools.partial(project_kernel, head_size, len(lasts)),
-        out_shape=(
-            pltpu.VMEM((rows, out_width), BF16),
-            *[pltpu.VMEM((rows // len(lasts), 2 * out_width), BF16)] * len(lasts),
-            *[pltpu.VMEM((size, 2 * out_width), BF16) for size in sizes],
-        ),
-        in_specs=[SMEM] + [VMEM] * (2 + len(lasts)),
-        out_specs=(VMEM,) * (1 + len(lasts) + count_pieces),
+            kv_ref[here, lanes] = (kh * k_size).astype(BF16)
+        kv_ref[here, out_width:] = v.astype(BF16)
+        pieces[stream][...] = kv_ref[here, :]
+
+
+def project_begin(wide, weights, blocks):
+    rows, depth = wide.shape
+    groups, _, out_width = weights.shape
+    return pl.pallas_call(
+        functools.partial(begin_kernel, blocks),
+        out_shape=pltpu.VMEM((rows, groups * out_width + 128), F32),
+        in_specs=[VMEM] * 2,
+        out_specs=VMEM,
         compiler_params=pltpu.CompilerParams(vmem_limit_bytes=16 << 20),
         cost_estimate=pl.CostEstimate(
             flops=2 * rows * depth * groups * out_width,
             bytes_accessed=2 * depth * (rows + groups * out_width),
             transcendentals=0,
         ),
-        name="project",
-    )(in_hbm(factor), in_vmem(wide), in_vmem(weights), *map(in_vmem, lasts))
+        name="project_begin",
+    )(in_vmem(wide), in_vmem(weights))
+
+
+def project_finish(factor, state, weights, lasts, head_size):
+    rows, width = lasts[0].shape
+    out_width = weights.shape[2]
+    total = rows * len(lasts)
+    return pl.pallas_call(
+        functools.partial(finish_kernel, head_size),
+        out_shape=(
+            pltpu.VMEM((total, out_width), BF16),
+            pltpu.VMEM((total, 2 * out_width), BF16),
+            *[pltpu.VMEM((rows, 2 * out_width), BF16)] * len(lasts),
+        ),
+        in_specs=[SMEM] + [VMEM] * (2 + len(lasts)),
+        out_specs=(VMEM,) * (2 + len(lasts)),
+        compiler_params=pltpu.CompilerParams(vmem_limit_bytes=16 << 20),
+        cost_estimate=pl.CostEstimate(
+            flops=6 * total * width * out_width, bytes_accessed=8 * total * out_width, transcendentals=0
+        ),
+        name="project_finish",
+    )(in_hbm(factor), in_vmem(state), in_vmem(weights), *map(in_vmem, lasts))
 
 
 def attend_kernel(
@@ -371,8 +392,8 @@
                     targets.append((s * half, (2 * step - 1 + way) * width))
     wide = placed(targets, blocks, wide, (rows, ring * width))
     lasts = [held[0][0], held[1][1]]
-    query, *kvs = project(head_scale, wide, weights, lasts, 3, head_size)
-    halves, pieces = kvs[:2], kvs[2:]
+    state = project_begin(wide, weights, ring)
+    query, kv, *pieces = project_finish(head_scale, state, weights, lasts, head_size)
 
     far, straight, crossed = [], [], []
     for step in range(outer):
@@ -381,9 +402,9 @@
         crossed.append((source + 1 - core) * rows)
         if step:
             shift = [(2 * a + b, 2 * ((a + step) % outer) + b) for a in range(outer) for b in (0, 1)]
-            far.append([lax.ppermute(kv, "seq", shift) for kv in halves])
+            far.append([lax.ppermute(kv, "seq", shift)])
     first = [seq_at * rows]
-    (acc,) = attend(numbers(straight[:1] + first), scale_ids, query, [halves], head_size)
+    (acc,) = attend(numbers(straight[:1] + first), scale_ids, query, [[kv]], head_size)
     near = [[swapped(piece, seqs) for piece in pieces]]
     acc, near = lax.optimization_barrier((acc, near))
     (acc,) = attend(numbers(crossed[:1] + first), scale_ids, query, near, head_size, acc)

time: 76 us -> 72.3 us (0.951)
  starting transfers between devices: 32.3 us -> 30.1 us
  waiting for transfers between devices: 17.9 us -> 16.4 us
  local copies, waits for them, and re-layouts: 5.92 us -> 4.46 us
  Pallas kernels: 17.8 us -> 18.7 us
    ppermute x2 -> x1, starting transfers between devices: 2.09 us -> 0.46 us  [body(): far.append([lax.ppermute(kv, 'seq', shift)])]
    ppermute x28, waiting for transfers between devices: 17.9 us -> 16.4 us  [along(): lax.ppermute(value, 'head', [(order[p], order[(p + step) % count]) for p...]
    unnamed x12 -> x8, local copies, waits for them, and re-layouts: 4.76 us -> 3.3 us
    pallas_call x1 -> x2, Pallas kernels: 2.87 us -> 3.75 us  [the longest x1 1.91 us: project_begin(): pl.pallas_call(functools.partial(begin_kernel, blocks), out_shape=pltpu.V...]
  transfers between devices with their start and end apart: 35 -> 32, of which waited for: 15 -> 14; matrix products, arithmetic and copies ran while one was open for 1% -> 1% of each run, Pallas kernels for 16% -> 20%
where the time goes in v14:
time: 72.3 us; the launch traced here: 71.4 us
  starting transfers between devices  30.1 us (42%)
  Pallas kernels  18.7 us (26%)
  waiting for transfers between devices  16.4 us (23%)
  local copies, waits for them, and re-layouts  4.46 us (6%)
  other arithmetic  1.4 us (2%)
    ppermute x28, starting transfers between devices, along(): lax.ppermute(value, 'head', [(order[p], order[(p + step) % count]) for p...  29.1 us
    ppermute x28, waiting for transfers between devices, along(): lax.ppermute(value, 'head', [(order[p], order[(p + step) % count]) for p...  16.4 us
    pallas_call x4, Pallas kernels, attend(): pl.pallas_call(functools.partial(attend_kernel, head_size, (len(blocks),...  9.47 us
    unnamed x8, local copies, waits for them, and re-layouts  3.3 us
    pallas_call x1, Pallas kernels, fold_gain(): pl.pallas_call(functools.partial(fold_kernel, order), out_shape=pltpu.VME...  3.01 us
    pallas_call x1, Pallas kernels, project_begin(): pl.pallas_call(functools.partial(begin_kernel, blocks), out_shape=pltpu.V...  1.91 us
    pallas_call x1, Pallas kernels, project_finish(): pl.pallas_call(functools.partial(finish_kernel, head_size), out_shape=(pl...  1.84 us
  transfers between devices with their start and end apart: 32, of which 14 were waited for; matrix products, arithmetic and copies ran while one was open for 1% of the time, Pallas kernels for 20%

profile of v14, /device:TPU:10, one launch (start us, length us, event | category | flops | bytes accessed | tf_op | source)
XLA Modules:
  0.0 71.4 jit_solution(6444478025980176597)
XLA Ops:
  0.0 1.0 %fusion = (bf16[256,256]{1,0:T(8,128)(2,1)S(1)}, bf16[256,256]{1,0:T(8,128)(2,1)S(1)}) fusion(bf16[512,256]{1,0:T(8,128)(2,1)} %refs_0_.1), kind=kLoop, calls=%fused_computation.16 | loop fusion | bytes 524288 | tf_op jit(solution)/shard_map/slice | solution.py:369
  1.0 0.5 collective-permute-start.9
  1.5 1.6 %collective-permute-start = (bf16[256,256]{1,0:T(8,128)(2,1)S(1)}, bf16[256,256]{1,0:T(8,128)(2,1)S(1)}, u32[]{:S(2)}, u32[]{:S(2)}) collective-permute-start(bf16[256,256]{1,0:T(8,128)(2,1)S(1)} %get-tuple-element.66), channel_id=1, source_target_pairs={{0,2},{2,4},{4,6},{6,7},{7,5},{5,3},{3,1},{1,0},{8,10},{10,12},{12... | collective-permute-start | bytes 393224 | tf_op jit(solution)/shard_map/ppermute | solution.py:33
  3.1 0.4 collective-permute-start.3
  3.5 1.6 %collective-permute-start.6 = (bf16[256,256]{1,0:T(8,128)(2,1)S(1)}, bf16[256,256]{1,0:T(8,128)(2,1)S(1)}, u32[]{:S(2)}, u32[]{:S(2)}) collective-permute-start(bf16[256,256]{1,0:T(8,128)(2,1)S(1)} %get-tuple-element.65), channel_id=1, source_target_pairs={{0,2},{2,4},{4,6},{6,7},{7,5},{5,3},{3,1},{1,0},{8,10},{10,12},{12... | collective-permute-start | bytes 393224 | tf_op jit(solution)/shard_map/ppermute | solution.py:33
  5.2 3.0 %fold_gain.1.w_ref = bf16[3,2048,256]{2,1,0:T(8,128)(2,1)S(1)} custom-call(s32[8]{0:T(128)S(1)} %stack.84.at, f32[16,128]{1,0:T(8,128)} %bitcast.19, bf16[3,2048,256]{2,1,0:T(8,128)(2,1)} %w_hbm.1), custom_call_target="tpu_custom_call" | custom-call | flops 1572864 | bytes 6291456 | tf_op jit(solution)/shard_map/fold_gain/pallas_call | solution.py:77
  8.2 0.5 collective-permute-start.10
  8.7 1.6 %collective-permute-start.1 = (bf16[256,256]{1,0:T(8,128)(2,1)S(1)}, bf16[256,256]{1,0:T(8,128)(2,1)S(1)}, u32[]{:S(2)}, u32[]{:S(2)}) collective-permute-start(bf16[256,256]{1,0:T(8,128)(2,1)S(1)} %collective-permute-done.refs_1_), channel_id=1, source_target_pairs={{0,2},{2,4},{4,6},{6,7},{7,5},{5,3},{3,1},{1,0},{8,10},{10,12},{12... | collective-permute-start | bytes 393224 | tf_op jit(solution)/shard_map/ppermute | solution.py:33
  10.3 0.5 collective-permute-start.4
  10.7 1.6 %collective-permute-start.7 = (bf16[256,256]{1,0:T(8,128)(2,1)S(1)}, bf16[256,256]{1,0:T(8,128)(2,1)S(1)}, u32[]{:S(2)}, u32[]{:S(2)}) collective-permute-start(bf16[256,256]{1,0:T(8,128)(2,1)S(1)} %collective-permute-done.6.refs_3_), channel_id=1, source_target_pairs={{0,2},{2,4},{4,6},{6,7},{7,5},{5,3},{3,1},{1,0},{8,10},{10,12},{12... | collective-permute-start | bytes 393224 | tf_op jit(solution)/shard_map/ppermute | solution.py:33
  12.3 1.9 %collective-permute-done.10.refs_3_ = bf16[256,256]{1,0:T(8,128)(2,1)S(1)} collective-permute-done((bf16[256,256]{1,0:T(8,128)(2,1)S(1)}, bf16[256,256]{1,0:T(8,128)(2,1)S(1)}, u32[]{:S(2)}, u32[]{:S(2)}) %collective-permute-start.10) | collective-permute-done | bytes 131104 | tf_op jit(solution)/shard_map/ppermute | solution.py:33
  14.7 1.6 %collective-permute-start.2 = (bf16[256,256]{1,0:T(8,128)(2,1)S(1)}, bf16[256,256]{1,0:T(8,128)(2,1)S(1)}, u32[]{:S(2)}, u32[]{:S(2)}) collective-permute-start(bf16[256,256]{1,0:T(8,128)(2,1)S(1)} %collective-permute-done.1.refs_0_), channel_id=1, source_target_pairs={{0,2},{2,4},{4,6},{6,7},{7,5},{5,3},{3,1},{1,0},{8,10},{10,12},{12... | collective-permute-start | bytes 393224 | tf_op jit(solution)/shard_map/ppermute | solution.py:33
  16.3 0.8 %collective-permute-done.4.refs_1_ = bf16[256,256]{1,0:T(8,128)(2,1)S(1)} collective-permute-done((bf16[256,256]{1,0:T(8,128)(2,1)S(1)}, bf16[256,256]{1,0:T(8,128)(2,1)S(1)}, u32[]{:S(2)}, u32[]{:S(2)}) %collective-permute-start.4) | collective-permute-done | bytes 131104 | tf_op jit(solution)/shard_map/ppermute | solution.py:33
  17.5 1.6 %collective-permute-start.8 = (bf16[256,256]{1,0:T(8,128)(2,1)S(1)}, bf16[256,256]{1,0:T(8,128)(2,1)S(1)}, u32[]{:S(2)}, u32[]{:S(2)}) collective-permute-start(bf16[256,256]{1,0:T(8,128)(2,1)S(1)} %collective-permute-done.7.refs_2_), channel_id=1, source_target_pairs={{0,2},{2,4},{4,6},{6,7},{7,5},{5,3},{3,1},{1,0},{8,10},{10,12},{12... | collective-permute-start | bytes 393224 | tf_op jit(solution)/shard_map/ppermute | solution.py:33
  19.1 1.0 %place.3.refs_4_ = bf16[512,2048]{1,0:T(8,128)(2,1)S(1)} custom-call(bf16[512,256]{1,0:T(8,128)(2,1)} %refs_0_.1, bf16[256,256]{1,0:T(8,128)(2,1)S(1)} %collective-permute-done.refs_1_, bf16[256,256]{1,0:T(8,128)(2,1)S(1)} %collective-permute-done.3.refs_2_, bf16[256,256]{1,0:T(8,128)(2,1)S(1)} %collective-permute-done.6.refs_3_, ...), custom_call_target="tpu_custom_call" | custom-call | bytes 1048576 | tf_op jit(solution)/shard_map/place/pallas_call | solution.py:106
  20.2 0.5 collective-permute-start.13
  20.7 1.6 %collective-permute-start.12 = (bf16[256,256]{1,0:T(8,128)(2,1)S(1)}, bf16[256,256]{1,0:T(8,128)(2,1)S(1)}, u32[]{:S(2)}, u32[]{:S(2)}) collective-permute-start(bf16[256,256]{1,0:T(8,128)(2,1)S(1)} %collective-permute-done.2.refs_0_), channel_id=1, source_target_pairs={{0,2},{2,4},{4,6},{6,7},{7,5},{5,3},{3,1},{1,0},{8,10},{10,12},{12... | collective-permute-start | bytes 393224 | tf_op jit(solution)/shard_map/ppermute | solution.py:33
  22.6 1.9 %project_begin.1.state = f32[512,896]{1,0:T(8,128)S(1)} custom-call(bf16[512,2048]{1,0:T(8,128)(2,1)S(1)} %place.5.wide, bf16[3,2048,256]{2,1,0:T(8,128)(2,1)S(1)} %fold_gain.1.w_ref), custom_call_target="tpu_custom_call" | custom-call | flops 1610612736 | bytes 5242880 | tf_op jit(solution)/shard_map/project_begin/pallas_call | solution.py:169
  24.5 0.7 %collective-permute-done.13.refs_1_ = bf16[256,256]{1,0:T(8,128)(2,1)S(1)} collective-permute-done((bf16[256,256]{1,0:T(8,128)(2,1)S(1)}, bf16[256,256]{1,0:T(8,128)(2,1)S(1)}, u32[]{:S(2)}, u32[]{:S(2)}) %collective-permute-start.13) | collective-permute-done | bytes 131104 | tf_op jit(solution)/shard_map/ppermute | solution.py:33
  25.2 0.5 collective-permute-done.12.refs_0_
  25.7 1.8 %project_finish.1 = (bf16[512,256]{1,0:T(8,128)(2,1)S(1)}, bf16[512,512]{1,0:T(8,128)(2,1)S(1)}, bf16[256,512]{1,0:T(8,128)(2,1)}, bf16[256,512]{1,0:T(8,128)(2,1)S(1)}) custom-call(f32[2]{0:T(128)} %factor.1, f32[512,896]{1,0:T(8,128)S(1)} %project_begin.1.state, bf16[3,2048,256]{2,1,0:T(8,128)(2,1)S(1)} %fold_gain.1.w_ref, ...), custom_call_target="tpu_custom_call" | custom-call | flops 201326592 | bytes 1048576 | tf_op jit(solution)/shard_map/project_finish/pallas_call | solution.py:188
  27.5 0.5 collective-permute-start.16
  28.0 0.5 collective-permute-start.15
  28.5 1.2 %load.1.refs_2_ = bf16[256,2048]{1,0:T(8,128)(2,1)S(1)} custom-call(bf16[256,2048]{1,0:T(8,128)(2,1)} %source.1), custom_call_target="tpu_custom_call" | custom-call | bytes 1048576 | tf_op jit(solution)/shard_map/load/pallas_call | solution.py:335
  29.9 2.2 %attend.3.refs_2_ = f32[512,512]{1,0:T(8,128)S(1)} custom-call(s32[2]{0:T(128)S(1)} %pad_add_fusion.1.info, s32[2048]{0:T(1024)} %ids.7, bf16[512,256]{1,0:T(8,128)(2,1)S(1)} %get-tuple-element.39.q_ref, s32[8,1,256]{2,1,0:T(1,128)} %bitcast.15, bf16[512,512]{1,0:T(8,128)(2,1)S(1)} %get-tuple-element.40.refs_0_), custom_call_target="tpu_custom_call" | custom-call | flops 1048576 | bytes 1024 | tf_op jit(solution)/shard_map/attend/pallas_call | solution.py:312
  32.2 0.7 copy-done
  32.9 0.7 copy-done.2
  33.6 0.9 %copy-done.1 = bf16[256,512]{1,0:T(8,128)(2,1)S(1)} copy-done((bf16[256,512]{1,0:T(8,128)(2,1)S(1)}, bf16[256,512]{1,0:T(8,128)(2,1)}, u32[]{:S(2)}) %copy-start.1) | copy-done | bytes 262168
  34.5 0.9 %copy-done.3 = bf16[256,512]{1,0:T(8,128)(2,1)S(1)} copy-done((bf16[256,512]{1,0:T(8,128)(2,1)S(1)}, bf16[256,512]{1,0:T(8,128)(2,1)}, u32[]{:S(2)}) %copy-start.3) | copy-done | bytes 262168
  35.5 2.2 %attend.4.refs_1_ = f32[512,512]{1,0:T(8,128)S(1)} custom-call(s32[2]{0:T(128)S(1)} %pad_add_fusion.info, s32[2048]{0:T(1024)} %ids.7, bf16[512,256]{1,0:T(8,128)(2,1)S(1)} %get-tuple-element.39.q_ref, s32[8,1,256]{2,1,0:T(1,128)} %bitcast.16, bf16[256,512]{1,0:T(8,128)(2,1)S(1)} %copy-done.1, bf16[256,512]{1,0:T(8,128)(2,1)S(1)} %copy-done.3, ...), custom_call_target="tpu_custom_call" | custom-call | flops 1048576 | bytes 1024 | tf_op jit(solution)/shard_map/attend/pallas_call | solution.py:312
  38.0 2.1 %attend.5.refs_1_ = f32[512,512]{1,0:T(8,128)S(1)} custom-call(s32[2]{0:T(128)S(1)} %pad_add_fusion.2.info, s32[2048]{0:T(1024)} %ids.7, bf16[512,256]{1,0:T(8,128)(2,1)S(1)} %get-tuple-element.39.q_ref, s32[8,1,256]{2,1,0:T(1,128)} %bitcast.17, bf16[512,512]{1,0:T(8,128)(2,1)S(1)} %collective-permute-done.16.refs_0_, f32[512,512]{1,0:T(8,128)S(1)} %attend.4.refs_1_), custom_call_target="tpu_custom_call" | custom-call | flops 1048576 | bytes 1024 | tf_op jit(solution)/shard_map/attend/pallas_call | solution.py:312
  40.2 2.9 %attend_last.1 = (bf16[256,256]{1,0:T(8,128)(2,1)S(1)}, bf16[256,256]{1,0:T(8,128)(2,1)S(1)}, bf16[256,256]{1,0:T(8,128)(2,1)S(1)}, bf16[256,256]{1,0:T(8,128)(2...) custom-call(s32[18]{0:T(128)S(1)} %stack.83.info, ...), custom_call_target="tpu_custom_call" | custom-call | flops 1048576 | bytes 1024 | tf_op jit(solution)/shard_map/attend_last/pallas_call | solution.py:312
  43.0 1.7 %collective-permute-start.18 = (bf16[256,256]{1,0:T(8,128)(2,1)S(1)}, bf16[256,256]{1,0:T(8,128)(2,1)S(1)}, u32[]{:S(2)}, u32[]{:S(2)}) collective-permute-start(bf16[256,256]{1,0:T(8,128)(2,1)S(1)} %get-tuple-element.53), channel_id=1, source_target_pairs={{0,2},{2,4},{4,6},{6,7},{7,5},{5,3},{3,1},{1,0},{8,10},{10,12},{12... | collective-permute-start | bytes 393224 | tf_op jit(solution)/shard_map/ppermute | solution.py:33
  45.1 1.6 %collective-permute-start.25 = (bf16[256,256]{1,0:T(8,128)(2,1)S(1)}, bf16[256,256]{1,0:T(8,128)(2,1)S(1)}, u32[]{:S(2)}, u32[]{:S(2)}) collective-permute-start(bf16[256,256]{1,0:T(8,128)(2,1)S(1)} %get-tuple-element.60), channel_id=1, source_target_pairs={{0,2},{2,4},{4,6},{6,7},{7,5},{5,3},{3,1},{1,0},{8,10},{10,12},{12... | collective-permute-start | bytes 393224 | tf_op jit(solution)/shard_map/ppermute | solution.py:33
  47.1 2.2 %collective-permute-done.18 = bf16[256,256]{1,0:T(8,128)(2,1)S(1)} collective-permute-done((bf16[256,256]{1,0:T(8,128)(2,1)S(1)}, bf16[256,256]{1,0:T(8,128)(2,1)S(1)}, u32[]{:S(2)}, u32[]{:S(2)}) %collective-permute-start.18) | collective-permute-done | bytes 131104 | tf_op jit(solution)/shard_map/ppermute | solution.py:33
  49.4 1.7 %collective-permute-start.19 = (bf16[256,256]{1,0:T(8,128)(2,1)S(1)}, bf16[256,256]{1,0:T(8,128)(2,1)S(1)}, u32[]{:S(2)}, u32[]{:S(2)}) collective-permute-start(bf16[256,256]{1,0:T(8,128)(2,1)S(1)} %add_convert_fusion.11), channel_id=1, source_target_pairs={{0,2},{2,4},{4,6},{6,7},{7,5},{5,3},{3,1},{1,0},{8,10},{10,12},{12... | collective-permute-start | bytes 393224 | tf_op jit(solution)/shard_map/ppermute | solution.py:33
  51.6 0.6 collective-permute-done.25
  52.2 1.7 %collective-permute-start.26 = (bf16[256,256]{1,0:T(8,128)(2,1)S(1)}, bf16[256,256]{1,0:T(8,128)(2,1)S(1)}, u32[]{:S(2)}, u32[]{:S(2)}) collective-permute-start(bf16[256,256]{1,0:T(8,128)(2,1)S(1)} %add_convert_fusion.5), channel_id=1, source_target_pairs={{0,2},{2,4},{4,6},{6,7},{7,5},{5,3},{3,1},{1,0},{8,10},{10,12},{12... | collective-permute-start | bytes 393224 | tf_op jit(solution)/shard_map/ppermute | solution.py:33
  54.4 0.6 collective-permute-done.19
  55.1 1.7 %collective-permute-start.20 = (bf16[256,256]{1,0:T(8,128)(2,1)S(1)}, bf16[256,256]{1,0:T(8,128)(2,1)S(1)}, u32[]{:S(2)}, u32[]{:S(2)}) collective-permute-start(bf16[256,256]{1,0:T(8,128)(2,1)S(1)} %add_convert_fusion.10), channel_id=1, source_target_pairs={{0,2},{2,4},{4,6},{6,7},{7,5},{5,3},{3,1},{1,0},{8,10},{10,12},{12... | collective-permute-start | bytes 393224 | tf_op jit(solution)/shard_map/ppermute | solution.py:33
  57.3 1.4 %collective-permute-done.26 = bf16[256,256]{1,0:T(8,128)(2,1)S(1)} collective-permute-done((bf16[256,256]{1,0:T(8,128)(2,1)S(1)}, bf16[256,256]{1,0:T(8,128)(2,1)S(1)}, u32[]{:S(2)}, u32[]{:S(2)}) %collective-permute-start.26) | collective-permute-done | bytes 131104 | tf_op jit(solution)/shard_map/ppermute | solution.py:33
  58.8 1.7 %collective-permute-start.27 = (bf16[256,256]{1,0:T(8,128)(2,1)S(1)}, bf16[256,256]{1,0:T(8,128)(2,1)S(1)}, u32[]{:S(2)}, u32[]{:S(2)}) collective-permute-start(bf16[256,256]{1,0:T(8,128)(2,1)S(1)} %add_convert_fusion.4), channel_id=1, source_target_pairs={{0,2},{2,4},{4,6},{6,7},{7,5},{5,3},{3,1},{1,0},{8,10},{10,12},{12... | collective-permute-start | bytes 393224 | tf_op jit(solution)/shard_map/ppermute | solution.py:33
  60.9 0.6 collective-permute-done.20
  61.6 1.7 %collective-permute-start.21 = (bf16[256,256]{1,0:T(8,128)(2,1)S(1)}, bf16[256,256]{1,0:T(8,128)(2,1)S(1)}, u32[]{:S(2)}, u32[]{:S(2)}) collective-permute-start(bf16[256,256]{1,0:T(8,128)(2,1)S(1)} %add_convert_fusion.9), channel_id=1, source_target_pairs={{0,2},{2,4},{4,6},{6,7},{7,5},{5,3},{3,1},{1,0},{8,10},{10,12},{12... | collective-permute-start | bytes 393224 | tf_op jit(solution)/shard_map/ppermute | solution.py:33
  63.3 2.3 %collective-permute-done.30 = bf16[256,256]{1,0:T(8,128)(2,1)S(1)} collective-permute-done((bf16[256,256]{1,0:T(8,128)(2,1)S(1)}, bf16[256,256]{1,0:T(8,128)(2,1)S(1)}, u32[]{:S(2)}, u32[]{:S(2)}) %collective-permute-start.30) | collective-permute-done | bytes 131104 | tf_op jit(solution)/shard_map/ppermute | solution.py:33
  66.0 0.6 collective-permute-done.21
  66.7 3.9 %collective-permute-done.31 = bf16[256,256]{1,0:T(8,128)(2,1)S(1)} collective-permute-done((bf16[256,256]{1,0:T(8,128)(2,1)S(1)}, bf16[256,256]{1,0:T(8,128)(2,1)S(1)}, u32[]{:S(2)}, u32[]{:S(2)}) %collective-permute-start.31) | collective-permute-done | bytes 131104 | tf_op jit(solution)/shard_map/ppermute | solution.py:33
  70.6 0.7 %pad_maximum_fusion = bf16[512,256]{1,0:T(8,128)(2,1)} fusion(bf16[256,256]{1,0:T(8,128)(2,1)S(1)} %add_convert_fusion, bf16[256,256]{1,0:T(8,128)(2,1)S(1)} %add_convert_fusion.6), kind=kLoop, calls=%fused_computation | loop fusion | flops 524288 | bytes 524288 | tf_op jit(solution)/shard_map/concatenate | solution.py:430
  (54 shorter events, 5.3 us)
Async XLA Ops:
  1.0 7.2 %collective-permute-start.9 = (bf16[256,256]{1,0:T(8,128)(2,1)S(1)}, bf16[256,256]{1,0:T(8,128)(2,1)S(1)}, u32[]{:S(2)}, u32[]{:S(2)}) collective-permute-start(bf16[256,256]{1,0:T(8,128)(2,1)S(1)} %get-tuple-element.65), channel_id=1, source_target_pairs={{0,1},{2,0},{4,2},{6,4},{7,6},{5,7},{3,5},{1,3},{8,9},{10,8},{12,1... | collective-permute-start | bytes 393224 | tf_op jit(solution)/shard_map/ppermute | solution.py:33
  1.5 7.2 %collective-permute-start = (bf16[256,256]{1,0:T(8,128)(2,1)S(1)}, bf16[256,256]{1,0:T(8,128)(2,1)S(1)}, u32[]{:S(2)}, u32[]{:S(2)}) collective-permute-start(bf16[256,256]{1,0:T(8,128)(2,1)S(1)} %get-tuple-element.66), channel_id=1, source_target_pairs={{0,2},{2,4},{4,6},{6,7},{7,5},{5,3},{3,1},{1,0},{8,10},{10,12},{12... | collective-permute-start | bytes 393224 | tf_op jit(solution)/shard_map/ppermute | solution.py:33
  3.1 7.2 %collective-permute-start.3 = (bf16[256,256]{1,0:T(8,128)(2,1)S(1)}, bf16[256,256]{1,0:T(8,128)(2,1)S(1)}, u32[]{:S(2)}, u32[]{:S(2)}) collective-permute-start(bf16[256,256]{1,0:T(8,128)(2,1)S(1)} %get-tuple-element.66), channel_id=1, source_target_pairs={{0,1},{2,0},{4,2},{6,4},{7,6},{5,7},{3,5},{1,3},{8,9},{10,8},{12,1... | collective-permute-start | bytes 393224 | tf_op jit(solution)/shard_map/ppermute | solution.py:33
  3.5 7.2 %collective-permute-start.6 = (bf16[256,256]{1,0:T(8,128)(2,1)S(1)}, bf16[256,256]{1,0:T(8,128)(2,1)S(1)}, u32[]{:S(2)}, u32[]{:S(2)}) collective-permute-start(bf16[256,256]{1,0:T(8,128)(2,1)S(1)} %get-tuple-element.65), channel_id=1, source_target_pairs={{0,2},{2,4},{4,6},{6,7},{7,5},{5,3},{3,1},{1,0},{8,10},{10,12},{12... | collective-permute-start | bytes 393224 | tf_op jit(solution)/shard_map/ppermute | solution.py:33
  8.2 6.0 %collective-permute-start.10 = (bf16[256,256]{1,0:T(8,128)(2,1)S(1)}, bf16[256,256]{1,0:T(8,128)(2,1)S(1)}, u32[]{:S(2)}, u32[]{:S(2)}) collective-permute-start(bf16[256,256]{1,0:T(8,128)(2,1)S(1)} %collective-permute-done.9.refs_4_), channel_id=1, source_target_pairs={{0,1},{2,0},{4,2},{6,4},{7,6},{5,7},{3,5},{1,3},{8,9},{10,8},{12,1... | collective-permute-start | bytes 393224 | tf_op jit(solution)/shard_map/ppermute | solution.py:33
  8.7 6.0 %collective-permute-start.1 = (bf16[256,256]{1,0:T(8,128)(2,1)S(1)}, bf16[256,256]{1,0:T(8,128)(2,1)S(1)}, u32[]{:S(2)}, u32[]{:S(2)}) collective-permute-start(bf16[256,256]{1,0:T(8,128)(2,1)S(1)} %collective-permute-done.refs_1_), channel_id=1, source_target_pairs={{0,2},{2,4},{4,6},{6,7},{7,5},{5,3},{3,1},{1,0},{8,10},{10,12},{12... | collective-permute-start | bytes 393224 | tf_op jit(solution)/shard_map/ppermute | solution.py:33
  10.3 6.8 %collective-permute-start.4 = (bf16[256,256]{1,0:T(8,128)(2,1)S(1)}, bf16[256,256]{1,0:T(8,128)(2,1)S(1)}, u32[]{:S(2)}, u32[]{:S(2)}) collective-permute-start(bf16[256,256]{1,0:T(8,128)(2,1)S(1)} %collective-permute-done.3.refs_2_), channel_id=1, source_target_pairs={{0,1},{2,0},{4,2},{6,4},{7,6},{5,7},{3,5},{1,3},{8,9},{10,8},{12,1... | collective-permute-start | bytes 393224 | tf_op jit(solution)/shard_map/ppermute | solution.py:33
  10.7 6.8 %collective-permute-start.7 = (bf16[256,256]{1,0:T(8,128)(2,1)S(1)}, bf16[256,256]{1,0:T(8,128)(2,1)S(1)}, u32[]{:S(2)}, u32[]{:S(2)}) collective-permute-start(bf16[256,256]{1,0:T(8,128)(2,1)S(1)} %collective-permute-done.6.refs_3_), channel_id=1, source_target_pairs={{0,2},{2,4},{4,6},{6,7},{7,5},{5,3},{3,1},{1,0},{8,10},{10,12},{12... | collective-permute-start | bytes 393224 | tf_op jit(solution)/shard_map/ppermute | solution.py:33
  14.2 6.0 %collective-permute-start.11 = (bf16[256,256]{1,0:T(8,128)(2,1)S(1)}, bf16[256,256]{1,0:T(8,128)(2,1)S(1)}, u32[]{:S(2)}, u32[]{:S(2)}) collective-permute-start(bf16[256,256]{1,0:T(8,128)(2,1)S(1)} %collective-permute-done.10.refs_3_), channel_id=1, source_target_pairs={{0,1},{2,0},{4,2},{6,4},{7,6},{5,7},{3,5},{1,3},{8,9},{10,8},{12,1... | collective-permute-start | bytes 393224 | tf_op jit(solution)/shard_map/ppermute | solution.py:33
  14.7 6.0 %collective-permute-start.2 = (bf16[256,256]{1,0:T(8,128)(2,1)S(1)}, bf16[256,256]{1,0:T(8,128)(2,1)S(1)}, u32[]{:S(2)}, u32[]{:S(2)}) collective-permute-start(bf16[256,256]{1,0:T(8,128)(2,1)S(1)} %collective-permute-done.1.refs_0_), channel_id=1, source_target_pairs={{0,2},{2,4},{4,6},{6,7},{7,5},{5,3},{3,1},{1,0},{8,10},{10,12},{12... | collective-permute-start | bytes 393224 | tf_op jit(solution)/shard_map/ppermute | solution.py:33
  17.1 5.3 %collective-permute-start.5 = (bf16[256,256]{1,0:T(8,128)(2,1)S(1)}, bf16[256,256]{1,0:T(8,128)(2,1)S(1)}, u32[]{:S(2)}, u32[]{:S(2)}) collective-permute-start(bf16[256,256]{1,0:T(8,128)(2,1)S(1)} %collective-permute-done.4.refs_1_), channel_id=1, source_target_pairs={{0,1},{2,0},{4,2},{6,4},{7,6},{5,7},{3,5},{1,3},{8,9},{10,8},{12,1... | collective-permute-start | bytes 393224 | tf_op jit(solution)/shard_map/ppermute | solution.py:33
  17.5 5.0 %collective-permute-start.8 = (bf16[256,256]{1,0:T(8,128)(2,1)S(1)}, bf16[256,256]{1,0:T(8,128)(2,1)S(1)}, u32[]{:S(2)}, u32[]{:S(2)}) collective-permute-start(bf16[256,256]{1,0:T(8,128)(2,1)S(1)} %collective-permute-done.7.refs_2_), channel_id=1, source_target_pairs={{0,2},{2,4},{4,6},{6,7},{7,5},{5,3},{3,1},{1,0},{8,10},{10,12},{12... | collective-permute-start | bytes 393224 | tf_op jit(solution)/shard_map/ppermute | solution.py:33
  20.2 5.0 %collective-permute-start.13 = (bf16[256,256]{1,0:T(8,128)(2,1)S(1)}, bf16[256,256]{1,0:T(8,128)(2,1)S(1)}, u32[]{:S(2)}, u32[]{:S(2)}) collective-permute-start(bf16[256,256]{1,0:T(8,128)(2,1)S(1)} %collective-permute-done.11.refs_3_), channel_id=1, source_target_pairs={{0,1},{2,0},{4,2},{6,4},{7,6},{5,7},{3,5},{1,3},{8,9},{10,8},{12,1... | collective-permute-start | bytes 393224 | tf_op jit(solution)/shard_map/ppermute | solution.py:33
  20.7 5.0 %collective-permute-start.12 = (bf16[256,256]{1,0:T(8,128)(2,1)S(1)}, bf16[256,256]{1,0:T(8,128)(2,1)S(1)}, u32[]{:S(2)}, u32[]{:S(2)}) collective-permute-start(bf16[256,256]{1,0:T(8,128)(2,1)S(1)} %collective-permute-done.2.refs_0_), channel_id=1, source_target_pairs={{0,2},{2,4},{4,6},{6,7},{7,5},{5,3},{3,1},{1,0},{8,10},{10,12},{12... | collective-permute-start | bytes 393224 | tf_op jit(solution)/shard_map/ppermute | solution.py:33
  27.5 10.2 %collective-permute-start.16 = (bf16[512,512]{1,0:T(8,128)(2,1)S(1)}, bf16[512,512]{1,0:T(8,128)(2,1)S(1)}, u32[]{:S(2)}, u32[]{:S(2)}) collective-permute-start(bf16[512,512]{1,0:T(8,128)(2,1)S(1)} %get-tuple-element.40.refs_0_), channel_id=1, source_target_pairs={{0,16},{8,24},{16,0},{24,8},{1,17},{9,25},{17,1},{25,9},{2,18},{10... | collective-permute-start | bytes 1572872 | tf_op jit(solution)/shard_map/ppermute | solution.py:405
  28.0 4.2 %collective-permute-start.14 = (bf16[256,512]{1,0:T(8,128)(2,1)}, bf16[256,512]{1,0:T(8,128)(2,1)S(1)}, u32[]{:S(2)}, u32[]{:S(2)}) collective-permute-start(bf16[256,512]{1,0:T(8,128)(2,1)} %get-tuple-element.41), channel_id=1, source_target_pairs={{0,8},{8,0},{16,24},{24,16},{1,9},{9,1},{17,25},{25,17},{2,10},{10... | collective-permute-start | bytes 786440 | tf_op jit(solution)/shard_map/ppermute | solution.py:39
  28.0 4.9 %collective-permute-start.15 = (bf16[256,512]{1,0:T(8,128)(2,1)S(1)}, bf16[256,512]{1,0:T(8,128)(2,1)S(1)}, u32[]{:S(2)}, u32[]{:S(2)}) collective-permute-start(bf16[256,512]{1,0:T(8,128)(2,1)S(1)} %get-tuple-element.42), channel_id=1, source_target_pairs={{0,8},{8,0},{16,24},{24,16},{1,9},{9,1},{17,25},{25,17},{2,10},{10... | collective-permute-start | bytes 786440 | tf_op jit(solution)/shard_map/ppermute | solution.py:39
  32.2 0.7 copy-start
  32.9 0.7 copy-start.2
  33.6 0.9 %copy-start.1 = (bf16[256,512]{1,0:T(8,128)(2,1)S(1)}, bf16[256,512]{1,0:T(8,128)(2,1)}, u32[]{:S(2)}) copy-start(bf16[256,512]{1,0:T(8,128)(2,1)} %copy-done) | copy-start | bytes 786436
  34.5 0.9 %copy-start.3 = (bf16[256,512]{1,0:T(8,128)(2,1)S(1)}, bf16[256,512]{1,0:T(8,128)(2,1)}, u32[]{:S(2)}) copy-start(bf16[256,512]{1,0:T(8,128)(2,1)} %copy-done.2) | copy-start | bytes 786436
  37.7 2.4 %collective-permute-start.17 = (bf16[512,512]{1,0:T(8,128)(2,1)S(1)}, bf16[512,512]{1,0:T(8,128)(2,1)S(1)}, u32[]{:S(2)}, u32[]{:S(2)}) collective-permute-start(bf16[512,512]{1,0:T(8,128)(2,1)S(1)} %collective-permute-done.16.refs_0_), channel_id=1, source_target_pairs={{0,8},{8,0},{16,24},{24,16},{1,9},{9,1},{17,25},{25,17},{2,10},{10... | collective-permute-start | bytes 1572872 | tf_op jit(solution)/shard_map/ppermute | solution.py:39
  43.0 6.4 %collective-permute-start.18 = (bf16[256,256]{1,0:T(8,128)(2,1)S(1)}, bf16[256,256]{1,0:T(8,128)(2,1)S(1)}, u32[]{:S(2)}, u32[]{:S(2)}) collective-permute-start(bf16[256,256]{1,0:T(8,128)(2,1)S(1)} %get-tuple-element.53), channel_id=1, source_target_pairs={{0,2},{2,4},{4,6},{6,7},{7,5},{5,3},{3,1},{1,0},{8,10},{10,12},{12... | collective-permute-start | bytes 393224 | tf_op jit(solution)/shard_map/ppermute | solution.py:33
  44.7 6.4 %collective-permute-start.22 = (bf16[256,256]{1,0:T(8,128)(2,1)S(1)}, bf16[256,256]{1,0:T(8,128)(2,1)S(1)}, u32[]{:S(2)}, u32[]{:S(2)}) collective-permute-start(bf16[256,256]{1,0:T(8,128)(2,1)S(1)} %get-tuple-element.56), channel_id=1, source_target_pairs={{0,1},{2,0},{4,2},{6,4},{7,6},{5,7},{3,5},{1,3},{8,9},{10,8},{12,1... | collective-permute-start | bytes 393224 | tf_op jit(solution)/shard_map/ppermute | solution.py:33
  45.1 7.1 %collective-permute-start.25 = (bf16[256,256]{1,0:T(8,128)(2,1)S(1)}, bf16[256,256]{1,0:T(8,128)(2,1)S(1)}, u32[]{:S(2)}, u32[]{:S(2)}) collective-permute-start(bf16[256,256]{1,0:T(8,128)(2,1)S(1)} %get-tuple-element.60), channel_id=1, source_target_pairs={{0,2},{2,4},{4,6},{6,7},{7,5},{5,3},{3,1},{1,0},{8,10},{10,12},{12... | collective-permute-start | bytes 393224 | tf_op jit(solution)/shard_map/ppermute | solution.py:33
  46.8 7.2 %collective-permute-start.28 = (bf16[256,256]{1,0:T(8,128)(2,1)S(1)}, bf16[256,256]{1,0:T(8,128)(2,1)S(1)}, u32[]{:S(2)}, u32[]{:S(2)}) collective-permute-start(bf16[256,256]{1,0:T(8,128)(2,1)S(1)} %get-tuple-element.64), channel_id=1, source_target_pairs={{0,1},{2,0},{4,2},{6,4},{7,6},{5,7},{3,5},{1,3},{8,9},{10,8},{12,1... | collective-permute-start | bytes 393224 | tf_op jit(solution)/shard_map/ppermute | solution.py:33
  49.4 5.6 %collective-permute-start.19 = (bf16[256,256]{1,0:T(8,128)(2,1)S(1)}, bf16[256,256]{1,0:T(8,128)(2,1)S(1)}, u32[]{:S(2)}, u32[]{:S(2)}) collective-permute-start(bf16[256,256]{1,0:T(8,128)(2,1)S(1)} %add_convert_fusion.11), channel_id=1, source_target_pairs={{0,2},{2,4},{4,6},{6,7},{7,5},{5,3},{3,1},{1,0},{8,10},{10,12},{12... | collective-permute-start | bytes 393224 | tf_op jit(solution)/shard_map/ppermute | solution.py:33
  51.2 5.6 %collective-permute-start.23 = (bf16[256,256]{1,0:T(8,128)(2,1)S(1)}, bf16[256,256]{1,0:T(8,128)(2,1)S(1)}, u32[]{:S(2)}, u32[]{:S(2)}) collective-permute-start(bf16[256,256]{1,0:T(8,128)(2,1)S(1)} %add_convert_fusion.8), channel_id=1, source_target_pairs={{0,1},{2,0},{4,2},{6,4},{7,6},{5,7},{3,5},{1,3},{8,9},{10,8},{12,1... | collective-permute-start | bytes 393224 | tf_op jit(solution)/shard_map/ppermute | solution.py:33
  52.2 6.5 %collective-permute-start.26 = (bf16[256,256]{1,0:T(8,128)(2,1)S(1)}, bf16[256,256]{1,0:T(8,128)(2,1)S(1)}, u32[]{:S(2)}, u32[]{:S(2)}) collective-permute-start(bf16[256,256]{1,0:T(8,128)(2,1)S(1)} %add_convert_fusion.5), channel_id=1, source_target_pairs={{0,2},{2,4},{4,6},{6,7},{7,5},{5,3},{3,1},{1,0},{8,10},{10,12},{12... | collective-permute-start | bytes 393224 | tf_op jit(solution)/shard_map/ppermute | solution.py:33
  54.0 6.5 %collective-permute-start.29 = (bf16[256,256]{1,0:T(8,128)(2,1)S(1)}, bf16[256,256]{1,0:T(8,128)(2,1)S(1)}, u32[]{:S(2)}, u32[]{:S(2)}) collective-permute-start(bf16[256,256]{1,0:T(8,128)(2,1)S(1)} %add_convert_fusion.3), channel_id=1, source_target_pairs={{0,1},{2,0},{4,2},{6,4},{7,6},{5,7},{3,5},{1,3},{8,9},{10,8},{12,1... | collective-permute-start | bytes 393224 | tf_op jit(solution)/shard_map/ppermute | solution.py:33
  55.1 6.5 %collective-permute-start.20 = (bf16[256,256]{1,0:T(8,128)(2,1)S(1)}, bf16[256,256]{1,0:T(8,128)(2,1)S(1)}, u32[]{:S(2)}, u32[]{:S(2)}) collective-permute-start(bf16[256,256]{1,0:T(8,128)(2,1)S(1)} %add_convert_fusion.10), channel_id=1, source_target_pairs={{0,2},{2,4},{4,6},{6,7},{7,5},{5,3},{3,1},{1,0},{8,10},{10,12},{12... | collective-permute-start | bytes 393224 | tf_op jit(solution)/shard_map/ppermute | solution.py:33
  56.8 9.2 %collective-permute-start.24 = (bf16[256,256]{1,0:T(8,128)(2,1)S(1)}, bf16[256,256]{1,0:T(8,128)(2,1)S(1)}, u32[]{:S(2)}, u32[]{:S(2)}) collective-permute-start(bf16[256,256]{1,0:T(8,128)(2,1)S(1)} %add_convert_fusion.7), channel_id=1, source_target_pairs={{0,1},{2,0},{4,2},{6,4},{7,6},{5,7},{3,5},{1,3},{8,9},{10,8},{12,1... | collective-permute-start | bytes 393224 | tf_op jit(solution)/shard_map/ppermute | solution.py:33
  58.8 7.9 %collective-permute-start.27 = (bf16[256,256]{1,0:T(8,128)(2,1)S(1)}, bf16[256,256]{1,0:T(8,128)(2,1)S(1)}, u32[]{:S(2)}, u32[]{:S(2)}) collective-permute-start(bf16[256,256]{1,0:T(8,128)(2,1)S(1)} %add_convert_fusion.4), channel_id=1, source_target_pairs={{0,2},{2,4},{4,6},{6,7},{7,5},{5,3},{3,1},{1,0},{8,10},{10,12},{12... | collective-permute-start | bytes 393224 | tf_op jit(solution)/shard_map/ppermute | solution.py:33
  60.5 5.0 %collective-permute-start.30 = (bf16[256,256]{1,0:T(8,128)(2,1)S(1)}, bf16[256,256]{1,0:T(8,128)(2,1)S(1)}, u32[]{:S(2)}, u32[]{:S(2)}) collective-permute-start(bf16[256,256]{1,0:T(8,128)(2,1)S(1)} %add_convert_fusion.2), channel_id=1, source_target_pairs={{0,1},{2,0},{4,2},{6,4},{7,6},{5,7},{3,5},{1,3},{8,9},{10,8},{12,1... | collective-permute-start | bytes 393224 | tf_op jit(solution)/shard_map/ppermute | solution.py:33
  61.6 5.0 %collective-permute-start.21 = (bf16[256,256]{1,0:T(8,128)(2,1)S(1)}, bf16[256,256]{1,0:T(8,128)(2,1)S(1)}, u32[]{:S(2)}, u32[]{:S(2)}) collective-permute-start(bf16[256,256]{1,0:T(8,128)(2,1)S(1)} %add_convert_fusion.9), channel_id=1, source_target_pairs={{0,2},{2,4},{4,6},{6,7},{7,5},{5,3},{3,1},{1,0},{8,10},{10,12},{12... | collective-permute-start | bytes 393224 | tf_op jit(solution)/shard_map/ppermute | solution.py:33
  65.6 5.0 %collective-permute-start.31 = (bf16[256,256]{1,0:T(8,128)(2,1)S(1)}, bf16[256,256]{1,0:T(8,128)(2,1)S(1)}, u32[]{:S(2)}, u32[]{:S(2)}) collective-permute-start(bf16[256,256]{1,0:T(8,128)(2,1)S(1)} %add_convert_fusion.1), channel_id=1, source_target_pairs={{0,1},{2,0},{4,2},{6,4},{7,6},{5,7},{3,5},{1,3},{8,9},{10,8},{12,1... | collective-permute-start | bytes 393224 | tf_op jit(solution)/shard_map/ppermute | solution.py:33

commit v15 on v14

--- a/solution.py
+++ b/solution.py
@@ -135,8 +135,9 @@
 
 
 def finish_kernel(head_size, factor, state, w_ref, *refs):
-    count = (len(refs) - 2) // 2
-    lasts, (q_ref, kv_ref), pieces = refs[:count], refs[count : count + 2], refs[count + 2 :]
+    count = 2
+    lasts, (q_ref, kv_ref), rest = refs[:count], refs[count : count + 2], refs[count + 2 :]
+    halves, pieces = rest[:count], rest[count:]
     rows, width = lasts[0].shape
     depth, out_width = w_ref.shape[1:]
     for stream, last in enumerate(lasts):
@@ -160,7 +161,11 @@
             q_ref[here, lanes] = (qh * (q_size * (factor[head] * LOG2E))).astype(BF16)
             kv_ref[here, lanes] = (kh * k_size).astype(BF16)
         kv_ref[here, out_width:] = v.astype(BF16)
-        pieces[stream][...] = kv_ref[here, :]
+        halves[stream][...] = kv_ref[here, :]
+    start = 0
+    for piece in pieces:
+        piece[...] = kv_ref[start : start + piece.shape[0], :]
+        start += piece.shape[0]
 
 
 def project_begin(wide, weights, blocks):
@@ -181,19 +186,22 @@
     )(in_vmem(wide), in_vmem(weights))
 
 
-def project_finish(factor, state, weights, lasts, head_size):
+def project_finish(factor, state, weights, lasts, count_pieces, head_size):
     rows, width = lasts[0].shape
     out_width = weights.shape[2]
     total = rows * len(lasts)
+    units = total // 16
+    sizes = [rows] * len(lasts)
+    sizes += [16 * ((units + n) // count_pieces) for n in range(count_pieces)]
     return pl.pallas_call(
         functools.partial(finish_kernel, head_size),
         out_shape=(
             pltpu.VMEM((total, out_width), BF16),
             pltpu.VMEM((total, 2 * out_width), BF16),
-            *[pltpu.VMEM((rows, 2 * out_width), BF16)] * len(lasts),
+            *[pltpu.VMEM((size, 2 * out_width), BF16) for size in sizes],
         ),
         in_specs=[SMEM] + [VMEM] * (2 + len(lasts)),
-        out_specs=(VMEM,) * (2 + len(lasts)),
+        out_specs=(VMEM,) * (2 + len(sizes)),
         compiler_params=pltpu.CompilerParams(vmem_limit_bytes=16 << 20),
         cost_estimate=pl.CostEstimate(
             flops=6 * total * width * out_width, bytes_accessed=8 * total * out_width, transcendentals=0
@@ -303,7 +311,7 @@
     if acc is not None:
         operands.append(in_vmem(acc))
     if count_out:
-        operands.append(in_vmem(w_out))
+        operands.append(in_hbm(w_out))
         scratch.append(pltpu.VMEM((total, width), BF16))
         shape = pltpu.VMEM((total // streams, w_out.shape[1] * streams // count_out), BF16)
     else:
@@ -323,25 +331,6 @@
         cost_estimate=pl.CostEstimate(flops=1 << 20, bytes_accessed=1 << 10, transcendentals=0),
         name="attend_last" if count_out else "attend",
     )(info, in_hbm(ids), *operands)
-
-
-def load_kernel(source, target, sem):
-    copy = pltpu.make_async_copy(source, target, sem)
-    copy.start()
-    copy.wait()
-
-
-def loaded(value):
-    return pl.pallas_call(
-        load_kernel,
-        out_shape=pltpu.VMEM(value.shape, value.dtype),
-        in_specs=[pl.BlockSpec(memory_space=pltpu.HBM)],
-        out_specs=pl.BlockSpec(memory_space=pl.ANY),
-        scratch_shapes=[pltpu.SemaphoreType.DMA(())],
-        compiler_params=pltpu.CompilerParams(vmem_limit_bytes=1 << 20),
-        cost_estimate=pl.CostEstimate(flops=0, bytes_accessed=1 << 20, transcendentals=0),
-        name="load",
-    )(in_hbm(value))
 
 
 def total_of(*parts):
@@ -393,7 +382,8 @@
     wide = placed(targets, blocks, wide, (rows, ring * width))
     lasts = [held[0][0], held[1][1]]
     state = project_begin(wide, weights, ring)
-    query, kv, *pieces = project_finish(head_scale, state, weights, lasts, head_size)
+    query, kv, *parts = project_finish(head_scale, state, weights, lasts, 3, head_size)
+    halves, pieces = parts[:2], parts[2:]
 
     far, straight, crossed = [], [], []
     for step in range(outer):
@@ -402,20 +392,20 @@
         crossed.append((source + 1 - core) * rows)
         if step:
             shift = [(2 * a + b, 2 * ((a + step) % outer) + b) for a in range(outer) for b in (0, 1)]
-            far.append([lax.ppermute(kv, "seq", shift)])
+            far.append([lax.ppermute(part, "seq", shift) for part in halves])
     first = [seq_at * rows]
     (acc,) = attend(numbers(straight[:1] + first), scale_ids, query, [[kv]], head_size)
     near = [[swapped(piece, seqs) for piece in pieces]]
     acc, near = lax.optimization_barrier((acc, near))
     (acc,) = attend(numbers(crossed[:1] + first), scale_ids, query, near, head_size, acc)
-    acc, far, w_near = lax.optimization_barrier((acc, far, loaded(w_out)))
+    acc, far = lax.optimization_barrier((acc, far))
     far_crossed = [[swapped(part, seqs) for part in block] for block in far]
     (acc,) = attend(numbers(straight[1:] + first), scale_ids, query, far, head_size, acc)
 
     goals = [[*range(up, 0, -1), *range(-down, 0), 0] for up, down in reach]
     info = numbers(crossed[1:] + first + [at[goal % ring] for goal in goals[0] + goals[1]])
     parts = attend(
-        info, scale_ids, query, far_crossed, head_size, acc, w_near, len(streams)
+        info, scale_ids, query, far_crossed, head_size, acc, w_out, len(streams)
     )
     parts = [dict(zip(goals[s], parts[s * ring : (s + 1) * ring])) for s in streams]
     sums = [[None, None] for s in streams]

time: 72.3 us -> 72.2 us (level)
  local copies, waits for them, and re-layouts: 4.46 us -> 1.16 us
  waiting for transfers between devices: 16.4 us -> 19.3 us
  starting transfers between devices: 30.1 us -> 32.2 us
  Pallas kernels: 18.7 us -> 17.4 us
    unnamed x8 -> x0, local copies, waits for them, and re-layouts: 3.3 us -> none
    ppermute x1 -> x2, waiting for transfers between devices: 0.01 us -> 2.08 us  [body(): far.append([lax.ppermute(part, 'seq', shift) for part in halves])]
    ppermute x1 -> x2, starting transfers between devices: 0.46 us -> 2.09 us  [body(): far.append([lax.ppermute(part, 'seq', shift) for part in halves])]
    pallas_call x1 -> x0, Pallas kernels: 1.23 us -> none  [loaded(): pl.pallas_call(load_kernel, out_shape=pltpu.VMEM(value.shape, value.dtype...]
    ppermute x28, waiting for transfers between devices: 16.4 us -> 17.2 us  [along(): lax.ppermute(value, 'head', [(order[p], order[(p + step) % count]) for p...]
  transfers between devices with their start and end apart: 32 -> 35, of which waited for: 14 -> 13; matrix products, arithmetic and copies ran while one was open for 1% -> 1% of each run, Pallas kernels for 20% -> 18%
where the time goes in v15:
time: 72.2 us; the launch traced here: 71.7 us
  starting transfers between devices  32.2 us (45%)
  waiting for transfers between devices  19.3 us (27%)
  Pallas kernels  17.4 us (24%)
  other arithmetic  1.39 us (2%)
  local copies, waits for them, and re-layouts  1.16 us (2%)
    ppermute x28, starting transfers between devices, along(): lax.ppermute(value, 'head', [(order[p], order[(p + step) % count]) for p...  29.1 us
    ppermute x28, waiting for transfers between devices, along(): lax.ppermute(value, 'head', [(order[p], order[(p + step) % count]) for p...  17.2 us
    pallas_call x4, Pallas kernels, attend(): pl.pallas_call(functools.partial(attend_kernel, head_size, (len(blocks),...  9.92 us
    pallas_call x1, Pallas kernels, fold_gain(): pl.pallas_call(functools.partial(fold_kernel, order), out_shape=pltpu.VME...  3.01 us
    ppermute x2, starting transfers between devices, body(): far.append([lax.ppermute(part, 'seq', shift) for part in halves])  2.09 us
    ppermute x2, waiting for transfers between devices, body(): far.append([lax.ppermute(part, 'seq', shift) for part in halves])  2.08 us
    pallas_call x1, Pallas kernels, project_begin(): pl.pallas_call(functools.partial(begin_kernel, blocks), out_shape=pltpu.V...  1.91 us
  transfers between devices with their start and end apart: 35, of which 13 were waited for; matrix products, arithmetic and copies ran while one was open for 1% of the time, Pallas kernels for 18%

profile of v15, /device:TPU:10, one launch (start us, length us, event | category | flops | bytes accessed | tf_op | source)
XLA Modules:
  0.0 71.7 jit_solution(5756022166392965977)
XLA Ops:
  0.0 1.0 %fusion = (bf16[256,256]{1,0:T(8,128)(2,1)S(1)}, bf16[256,256]{1,0:T(8,128)(2,1)S(1)}) fusion(bf16[512,256]{1,0:T(8,128)(2,1)} %refs_0_.1), kind=kLoop, calls=%fused_computation.16 | loop fusion | bytes 524288 | tf_op jit(solution)/shard_map/slice | solution.py:358
  1.0 0.5 collective-permute-start.9
  1.5 1.6 %collective-permute-start = (bf16[256,256]{1,0:T(8,128)(2,1)S(1)}, bf16[256,256]{1,0:T(8,128)(2,1)S(1)}, u32[]{:S(2)}, u32[]{:S(2)}) collective-permute-start(bf16[256,256]{1,0:T(8,128)(2,1)S(1)} %get-tuple-element.74), channel_id=1, source_target_pairs={{0,2},{2,4},{4,6},{6,7},{7,5},{5,3},{3,1},{1,0},{8,10},{10,12},{12... | collective-permute-start | bytes 393224 | tf_op jit(solution)/shard_map/ppermute | solution.py:33
  3.5 1.6 %collective-permute-start.6 = (bf16[256,256]{1,0:T(8,128)(2,1)S(1)}, bf16[256,256]{1,0:T(8,128)(2,1)S(1)}, u32[]{:S(2)}, u32[]{:S(2)}) collective-permute-start(bf16[256,256]{1,0:T(8,128)(2,1)S(1)} %get-tuple-element.73), channel_id=1, source_target_pairs={{0,2},{2,4},{4,6},{6,7},{7,5},{5,3},{3,1},{1,0},{8,10},{10,12},{12... | collective-permute-start | bytes 393224 | tf_op jit(solution)/shard_map/ppermute | solution.py:33
  5.2 3.0 %fold_gain.1.w_ref = bf16[3,2048,256]{2,1,0:T(8,128)(2,1)S(1)} custom-call(s32[8]{0:T(128)S(1)} %stack.84.at, f32[16,128]{1,0:T(8,128)} %bitcast.19, bf16[3,2048,256]{2,1,0:T(8,128)(2,1)} %w_hbm.1), custom_call_target="tpu_custom_call" | custom-call | flops 1572864 | bytes 6291456 | tf_op jit(solution)/shard_map/fold_gain/pallas_call | solution.py:77
  8.2 0.5 collective-permute-start.10
  8.7 1.6 %collective-permute-start.1 = (bf16[256,256]{1,0:T(8,128)(2,1)S(1)}, bf16[256,256]{1,0:T(8,128)(2,1)S(1)}, u32[]{:S(2)}, u32[]{:S(2)}) collective-permute-start(bf16[256,256]{1,0:T(8,128)(2,1)S(1)} %collective-permute-done.refs_1_), channel_id=1, source_target_pairs={{0,2},{2,4},{4,6},{6,7},{7,5},{5,3},{3,1},{1,0},{8,10},{10,12},{12... | collective-permute-start | bytes 393224 | tf_op jit(solution)/shard_map/ppermute | solution.py:33
  10.7 1.6 %collective-permute-start.7 = (bf16[256,256]{1,0:T(8,128)(2,1)S(1)}, bf16[256,256]{1,0:T(8,128)(2,1)S(1)}, u32[]{:S(2)}, u32[]{:S(2)}) collective-permute-start(bf16[256,256]{1,0:T(8,128)(2,1)S(1)} %collective-permute-done.6.refs_3_), channel_id=1, source_target_pairs={{0,2},{2,4},{4,6},{6,7},{7,5},{5,3},{3,1},{1,0},{8,10},{10,12},{12... | collective-permute-start | bytes 393224 | tf_op jit(solution)/shard_map/ppermute | solution.py:33
  12.3 1.9 %collective-permute-done.10.refs_3_ = bf16[256,256]{1,0:T(8,128)(2,1)S(1)} collective-permute-done((bf16[256,256]{1,0:T(8,128)(2,1)S(1)}, bf16[256,256]{1,0:T(8,128)(2,1)S(1)}, u32[]{:S(2)}, u32[]{:S(2)}) %collective-permute-start.10) | collective-permute-done | bytes 131104 | tf_op jit(solution)/shard_map/ppermute | solution.py:33
  14.7 1.6 %collective-permute-start.2 = (bf16[256,256]{1,0:T(8,128)(2,1)S(1)}, bf16[256,256]{1,0:T(8,128)(2,1)S(1)}, u32[]{:S(2)}, u32[]{:S(2)}) collective-permute-start(bf16[256,256]{1,0:T(8,128)(2,1)S(1)} %collective-permute-done.1.refs_0_), channel_id=1, source_target_pairs={{0,2},{2,4},{4,6},{6,7},{7,5},{5,3},{3,1},{1,0},{8,10},{10,12},{12... | collective-permute-start | bytes 393224 | tf_op jit(solution)/shard_map/ppermute | solution.py:33
  16.3 0.8 %collective-permute-done.4.refs_1_ = bf16[256,256]{1,0:T(8,128)(2,1)S(1)} collective-permute-done((bf16[256,256]{1,0:T(8,128)(2,1)S(1)}, bf16[256,256]{1,0:T(8,128)(2,1)S(1)}, u32[]{:S(2)}, u32[]{:S(2)}) %collective-permute-start.4) | collective-permute-done | bytes 131104 | tf_op jit(solution)/shard_map/ppermute | solution.py:33
  17.5 1.6 %collective-permute-start.8 = (bf16[256,256]{1,0:T(8,128)(2,1)S(1)}, bf16[256,256]{1,0:T(8,128)(2,1)S(1)}, u32[]{:S(2)}, u32[]{:S(2)}) collective-permute-start(bf16[256,256]{1,0:T(8,128)(2,1)S(1)} %collective-permute-done.7.refs_2_), channel_id=1, source_target_pairs={{0,2},{2,4},{4,6},{6,7},{7,5},{5,3},{3,1},{1,0},{8,10},{10,12},{12... | collective-permute-start | bytes 393224 | tf_op jit(solution)/shard_map/ppermute | solution.py:33
  19.1 1.0 %place.3.refs_4_ = bf16[512,2048]{1,0:T(8,128)(2,1)S(1)} custom-call(bf16[512,256]{1,0:T(8,128)(2,1)} %refs_0_.1, bf16[256,256]{1,0:T(8,128)(2,1)S(1)} %collective-permute-done.refs_1_, bf16[256,256]{1,0:T(8,128)(2,1)S(1)} %collective-permute-done.3.refs_2_, bf16[256,256]{1,0:T(8,128)(2,1)S(1)} %collective-permute-done.6.refs_3_, ...), custom_call_target="tpu_custom_call" | custom-call | bytes 1048576 | tf_op jit(solution)/shard_map/place/pallas_call | solution.py:106
  20.2 0.5 collective-permute-start.13
  20.7 1.6 %collective-permute-start.12 = (bf16[256,256]{1,0:T(8,128)(2,1)S(1)}, bf16[256,256]{1,0:T(8,128)(2,1)S(1)}, u32[]{:S(2)}, u32[]{:S(2)}) collective-permute-start(bf16[256,256]{1,0:T(8,128)(2,1)S(1)} %collective-permute-done.2.refs_0_), channel_id=1, source_target_pairs={{0,2},{2,4},{4,6},{6,7},{7,5},{5,3},{3,1},{1,0},{8,10},{10,12},{12... | collective-permute-start | bytes 393224 | tf_op jit(solution)/shard_map/ppermute | solution.py:33
  22.6 1.9 %project_begin.1.state = f32[512,896]{1,0:T(8,128)S(1)} custom-call(bf16[512,2048]{1,0:T(8,128)(2,1)S(1)} %place.5.wide, bf16[3,2048,256]{2,1,0:T(8,128)(2,1)S(1)} %fold_gain.1.w_ref), custom_call_target="tpu_custom_call" | custom-call | flops 1610612736 | bytes 5242880 | tf_op jit(solution)/shard_map/project_begin/pallas_call | solution.py:174
  24.5 0.7 %collective-permute-done.13.refs_1_ = bf16[256,256]{1,0:T(8,128)(2,1)S(1)} collective-permute-done((bf16[256,256]{1,0:T(8,128)(2,1)S(1)}, bf16[256,256]{1,0:T(8,128)(2,1)S(1)}, u32[]{:S(2)}, u32[]{:S(2)}) %collective-permute-start.13) | collective-permute-done | bytes 131104 | tf_op jit(solution)/shard_map/ppermute | solution.py:33
  25.2 0.5 collective-permute-done.12.refs_0_
  25.7 1.3 %project_finish.1 = (bf16[512,256]{1,0:T(8,128)(2,1)S(1)}, bf16[512,512]{1,0:T(8,128)(2,1)S(1)}, bf16[256,512]{1,0:T(8,128)(2,1)S(1)}, bf16[256,512]{1,0:T(8,128...) custom-call(f32[2]{0:T(128)} %factor.1, ...), custom_call_target="tpu_custom_call" | custom-call | flops 201326592 | bytes 1048576 | tf_op jit(solution)/shard_map/project_finish/pallas_call | solution.py:196
  27.0 0.5 collective-permute-start.17
  27.5 1.6 %collective-permute-start.18 = (bf16[256,512]{1,0:T(8,128)(2,1)S(1)}, bf16[256,512]{1,0:T(8,128)(2,1)S(1)}, u32[]{:S(2)}, u32[]{:S(2)}) collective-permute-start(bf16[256,512]{1,0:T(8,128)(2,1)S(1)} %get-tuple-element.53), channel_id=1, source_target_pairs={{0,16},{8,24},{16,0},{24,8},{1,17},{9,25},{17,1},{25,9},{2,18},{10... | collective-permute-start | bytes 786440 | tf_op jit(solution)/shard_map/ppermute | solution.py:395
  29.1 0.5 collective-permute-start.16
  29.8 2.2 %attend.3.refs_3_ = f32[512,512]{1,0:T(8,128)S(1)} custom-call(s32[2]{0:T(128)S(1)} %pad_add_fusion.1.info, s32[2048]{0:T(1024)} %ids.7, bf16[512,256]{1,0:T(8,128)(2,1)S(1)} %get-tuple-element.43.q_ref, s32[8,1,256]{2,1,0:T(1,128)} %bitcast.15, bf16[512,512]{1,0:T(8,128)(2,1)S(1)} %get-tuple-element.44.refs_0_), custom_call_target="tpu_custom_call" | custom-call | flops 1048576 | bytes 1024 | tf_op jit(solution)/shard_map/attend/pallas_call | solution.py:320
  32.0 2.2 %attend.4.refs_2_ = f32[512,512]{1,0:T(8,128)S(1)} custom-call(s32[2]{0:T(128)S(1)} %pad_add_fusion.info, s32[2048]{0:T(1024)} %ids.7, bf16[512,256]{1,0:T(8,128)(2,1)S(1)} %get-tuple-element.43.q_ref, s32[8,1,256]{2,1,0:T(1,128)} %bitcast.16, bf16[160,512]{1,0:T(8,128)(2,1)S(1)} %collective-permute-done.14.refs_0_, ...), custom_call_target="tpu_custom_call" | custom-call | flops 1048576 | bytes 1024 | tf_op jit(solution)/shard_map/attend/pallas_call | solution.py:320
  34.3 2.1 %collective-permute-done.18.refs_1_ = bf16[256,512]{1,0:T(8,128)(2,1)S(1)} collective-permute-done((bf16[256,512]{1,0:T(8,128)(2,1)S(1)}, bf16[256,512]{1,0:T(8,128)(2,1)S(1)}, u32[]{:S(2)}, u32[]{:S(2)}) %collective-permute-start.18) | collective-permute-done | bytes 262176 | tf_op jit(solution)/shard_map/ppermute | solution.py:395
  36.4 0.5 collective-permute-start.20
  37.1 2.1 %attend.5.refs_2_ = f32[512,512]{1,0:T(8,128)S(1)} custom-call(s32[2]{0:T(128)S(1)} %pad_add_fusion.2.info, s32[2048]{0:T(1024)} %ids.7, bf16[512,256]{1,0:T(8,128)(2,1)S(1)} %get-tuple-element.43.q_ref, s32[8,1,256]{2,1,0:T(1,128)} %bitcast.17, bf16[256,512]{1,0:T(8,128)(2,1)S(1)} %collective-permute-done.17.refs_0_, ...), custom_call_target="tpu_custom_call" | custom-call | flops 1048576 | bytes 1024 | tf_op jit(solution)/shard_map/attend/pallas_call | solution.py:320
  39.2 3.3 %attend_last.1 = (bf16[256,256]{1,0:T(8,128)(2,1)S(1)}, bf16[256,256]{1,0:T(8,128)(2,1)S(1)}, bf16[256,256]{1,0:T(8,128)(2,1)S(1)}, bf16[256,256]{1,0:T(8,128)(2...) custom-call(s32[18]{0:T(128)S(1)} %stack.83.info, ...), custom_call_target="tpu_custom_call" | custom-call | flops 1048576 | bytes 1024 | tf_op jit(solution)/shard_map/attend_last/pallas_call | solution.py:320
  42.5 1.6 %collective-permute-start.21 = (bf16[256,256]{1,0:T(8,128)(2,1)S(1)}, bf16[256,256]{1,0:T(8,128)(2,1)S(1)}, u32[]{:S(2)}, u32[]{:S(2)}) collective-permute-start(bf16[256,256]{1,0:T(8,128)(2,1)S(1)} %get-tuple-element.61), channel_id=1, source_target_pairs={{0,2},{2,4},{4,6},{6,7},{7,5},{5,3},{3,1},{1,0},{8,10},{10,12},{12... | collective-permute-start | bytes 393224 | tf_op jit(solution)/shard_map/ppermute | solution.py:33
  44.6 1.6 %collective-permute-start.28 = (bf16[256,256]{1,0:T(8,128)(2,1)S(1)}, bf16[256,256]{1,0:T(8,128)(2,1)S(1)}, u32[]{:S(2)}, u32[]{:S(2)}) collective-permute-start(bf16[256,256]{1,0:T(8,128)(2,1)S(1)} %get-tuple-element.68), channel_id=1, source_target_pairs={{0,2},{2,4},{4,6},{6,7},{7,5},{5,3},{3,1},{1,0},{8,10},{10,12},{12... | collective-permute-start | bytes 393224 | tf_op jit(solution)/shard_map/ppermute | solution.py:33
  46.7 2.3 %collective-permute-done.21 = bf16[256,256]{1,0:T(8,128)(2,1)S(1)} collective-permute-done((bf16[256,256]{1,0:T(8,128)(2,1)S(1)}, bf16[256,256]{1,0:T(8,128)(2,1)S(1)}, u32[]{:S(2)}, u32[]{:S(2)}) %collective-permute-start.21) | collective-permute-done | bytes 131104 | tf_op jit(solution)/shard_map/ppermute | solution.py:33
  49.0 1.6 %collective-permute-start.22 = (bf16[256,256]{1,0:T(8,128)(2,1)S(1)}, bf16[256,256]{1,0:T(8,128)(2,1)S(1)}, u32[]{:S(2)}, u32[]{:S(2)}) collective-permute-start(bf16[256,256]{1,0:T(8,128)(2,1)S(1)} %add_convert_fusion.11), channel_id=1, source_target_pairs={{0,2},{2,4},{4,6},{6,7},{7,5},{5,3},{3,1},{1,0},{8,10},{10,12},{12... | collective-permute-start | bytes 393224 | tf_op jit(solution)/shard_map/ppermute | solution.py:33
  50.7 0.5 collective-permute-start.26
  51.2 0.6 collective-permute-done.28
  51.8 1.6 %collective-permute-start.29 = (bf16[256,256]{1,0:T(8,128)(2,1)S(1)}, bf16[256,256]{1,0:T(8,128)(2,1)S(1)}, u32[]{:S(2)}, u32[]{:S(2)}) collective-permute-start(bf16[256,256]{1,0:T(8,128)(2,1)S(1)} %add_convert_fusion.5), channel_id=1, source_target_pairs={{0,2},{2,4},{4,6},{6,7},{7,5},{5,3},{3,1},{1,0},{8,10},{10,12},{12... | collective-permute-start | bytes 393224 | tf_op jit(solution)/shard_map/ppermute | solution.py:33
  53.5 0.5 collective-permute-start.32
  54.0 1.4 %collective-permute-done.22 = bf16[256,256]{1,0:T(8,128)(2,1)S(1)} collective-permute-done((bf16[256,256]{1,0:T(8,128)(2,1)S(1)}, bf16[256,256]{1,0:T(8,128)(2,1)S(1)}, u32[]{:S(2)}, u32[]{:S(2)}) %collective-permute-start.22) | collective-permute-done | bytes 131104 | tf_op jit(solution)/shard_map/ppermute | solution.py:33
  55.4 1.6 %collective-permute-start.23 = (bf16[256,256]{1,0:T(8,128)(2,1)S(1)}, bf16[256,256]{1,0:T(8,128)(2,1)S(1)}, u32[]{:S(2)}, u32[]{:S(2)}) collective-permute-start(bf16[256,256]{1,0:T(8,128)(2,1)S(1)} %add_convert_fusion.10), channel_id=1, source_target_pairs={{0,2},{2,4},{4,6},{6,7},{7,5},{5,3},{3,1},{1,0},{8,10},{10,12},{12... | collective-permute-start | bytes 393224 | tf_op jit(solution)/shard_map/ppermute | solution.py:33
  57.1 0.5 collective-permute-start.27
  57.6 0.6 collective-permute-done.29
  58.3 1.6 %collective-permute-start.30 = (bf16[256,256]{1,0:T(8,128)(2,1)S(1)}, bf16[256,256]{1,0:T(8,128)(2,1)S(1)}, u32[]{:S(2)}, u32[]{:S(2)}) collective-permute-start(bf16[256,256]{1,0:T(8,128)(2,1)S(1)} %add_convert_fusion.4), channel_id=1, source_target_pairs={{0,2},{2,4},{4,6},{6,7},{7,5},{5,3},{3,1},{1,0},{8,10},{10,12},{12... | collective-permute-start | bytes 393224 | tf_op jit(solution)/shard_map/ppermute | solution.py:33
  59.9 0.5 collective-permute-start.33
  60.4 0.6 collective-permute-done.23
  61.1 1.6 %collective-permute-start.24 = (bf16[256,256]{1,0:T(8,128)(2,1)S(1)}, bf16[256,256]{1,0:T(8,128)(2,1)S(1)}, u32[]{:S(2)}, u32[]{:S(2)}) collective-permute-start(bf16[256,256]{1,0:T(8,128)(2,1)S(1)} %add_convert_fusion.9), channel_id=1, source_target_pairs={{0,2},{2,4},{4,6},{6,7},{7,5},{5,3},{3,1},{1,0},{8,10},{10,12},{12... | collective-permute-start | bytes 393224 | tf_op jit(solution)/shard_map/ppermute | solution.py:33
  62.7 3.1 %collective-permute-done.33 = bf16[256,256]{1,0:T(8,128)(2,1)S(1)} collective-permute-done((bf16[256,256]{1,0:T(8,128)(2,1)S(1)}, bf16[256,256]{1,0:T(8,128)(2,1)S(1)}, u32[]{:S(2)}, u32[]{:S(2)}) %collective-permute-start.33) | collective-permute-done | bytes 131104 | tf_op jit(solution)/shard_map/ppermute | solution.py:33
  65.9 0.5 collective-permute-start.34
  66.4 4.4 %collective-permute-done.34 = bf16[256,256]{1,0:T(8,128)(2,1)S(1)} collective-permute-done((bf16[256,256]{1,0:T(8,128)(2,1)S(1)}, bf16[256,256]{1,0:T(8,128)(2,1)S(1)}, u32[]{:S(2)}, u32[]{:S(2)}) %collective-permute-start.34) | collective-permute-done | bytes 131104 | tf_op jit(solution)/shard_map/ppermute | solution.py:33
  70.9 0.7 %pad_maximum_fusion = bf16[512,256]{1,0:T(8,128)(2,1)} fusion(bf16[256,256]{1,0:T(8,128)(2,1)S(1)} %add_convert_fusion, bf16[256,256]{1,0:T(8,128)(2,1)S(1)} %add_convert_fusion.6), kind=kLoop, calls=%fused_computation | loop fusion | flops 524288 | bytes 524288 | tf_op jit(solution)/shard_map/concatenate | solution.py:420
  (51 shorter events, 4.0 us)
Async XLA Ops:
  1.0 7.2 %collective-permute-start.9 = (bf16[256,256]{1,0:T(8,128)(2,1)S(1)}, bf16[256,256]{1,0:T(8,128)(2,1)S(1)}, u32[]{:S(2)}, u32[]{:S(2)}) collective-permute-start(bf16[256,256]{1,0:T(8,128)(2,1)S(1)} %get-tuple-element.73), channel_id=1, source_target_pairs={{0,1},{2,0},{4,2},{6,4},{7,6},{5,7},{3,5},{1,3},{8,9},{10,8},{12,1... | collective-permute-start | bytes 393224 | tf_op jit(solution)/shard_map/ppermute | solution.py:33
  1.5 7.2 %collective-permute-start = (bf16[256,256]{1,0:T(8,128)(2,1)S(1)}, bf16[256,256]{1,0:T(8,128)(2,1)S(1)}, u32[]{:S(2)}, u32[]{:S(2)}) collective-permute-start(bf16[256,256]{1,0:T(8,128)(2,1)S(1)} %get-tuple-element.74), channel_id=1, source_target_pairs={{0,2},{2,4},{4,6},{6,7},{7,5},{5,3},{3,1},{1,0},{8,10},{10,12},{12... | collective-permute-start | bytes 393224 | tf_op jit(solution)/shard_map/ppermute | solution.py:33
  3.1 7.2 %collective-permute-start.3 = (bf16[256,256]{1,0:T(8,128)(2,1)S(1)}, bf16[256,256]{1,0:T(8,128)(2,1)S(1)}, u32[]{:S(2)}, u32[]{:S(2)}) collective-permute-start(bf16[256,256]{1,0:T(8,128)(2,1)S(1)} %get-tuple-element.74), channel_id=1, source_target_pairs={{0,1},{2,0},{4,2},{6,4},{7,6},{5,7},{3,5},{1,3},{8,9},{10,8},{12,1... | collective-permute-start | bytes 393224 | tf_op jit(solution)/shard_map/ppermute | solution.py:33
  3.5 7.2 %collective-permute-start.6 = (bf16[256,256]{1,0:T(8,128)(2,1)S(1)}, bf16[256,256]{1,0:T(8,128)(2,1)S(1)}, u32[]{:S(2)}, u32[]{:S(2)}) collective-permute-start(bf16[256,256]{1,0:T(8,128)(2,1)S(1)} %get-tuple-element.73), channel_id=1, source_target_pairs={{0,2},{2,4},{4,6},{6,7},{7,5},{5,3},{3,1},{1,0},{8,10},{10,12},{12... | collective-permute-start | bytes 393224 | tf_op jit(solution)/shard_map/ppermute | solution.py:33
  8.2 6.0 %collective-permute-start.10 = (bf16[256,256]{1,0:T(8,128)(2,1)S(1)}, bf16[256,256]{1,0:T(8,128)(2,1)S(1)}, u32[]{:S(2)}, u32[]{:S(2)}) collective-permute-start(bf16[256,256]{1,0:T(8,128)(2,1)S(1)} %collective-permute-done.9.refs_4_), channel_id=1, source_target_pairs={{0,1},{2,0},{4,2},{6,4},{7,6},{5,7},{3,5},{1,3},{8,9},{10,8},{12,1... | collective-permute-start | bytes 393224 | tf_op jit(solution)/shard_map/ppermute | solution.py:33
  8.7 6.0 %collective-permute-start.1 = (bf16[256,256]{1,0:T(8,128)(2,1)S(1)}, bf16[256,256]{1,0:T(8,128)(2,1)S(1)}, u32[]{:S(2)}, u32[]{:S(2)}) collective-permute-start(bf16[256,256]{1,0:T(8,128)(2,1)S(1)} %collective-permute-done.refs_1_), channel_id=1, source_target_pairs={{0,2},{2,4},{4,6},{6,7},{7,5},{5,3},{3,1},{1,0},{8,10},{10,12},{12... | collective-permute-start | bytes 393224 | tf_op jit(solution)/shard_map/ppermute | solution.py:33
  10.3 6.8 %collective-permute-start.4 = (bf16[256,256]{1,0:T(8,128)(2,1)S(1)}, bf16[256,256]{1,0:T(8,128)(2,1)S(1)}, u32[]{:S(2)}, u32[]{:S(2)}) collective-permute-start(bf16[256,256]{1,0:T(8,128)(2,1)S(1)} %collective-permute-done.3.refs_2_), channel_id=1, source_target_pairs={{0,1},{2,0},{4,2},{6,4},{7,6},{5,7},{3,5},{1,3},{8,9},{10,8},{12,1... | collective-permute-start | bytes 393224 | tf_op jit(solution)/shard_map/ppermute | solution.py:33
  10.7 6.8 %collective-permute-start.7 = (bf16[256,256]{1,0:T(8,128)(2,1)S(1)}, bf16[256,256]{1,0:T(8,128)(2,1)S(1)}, u32[]{:S(2)}, u32[]{:S(2)}) collective-permute-start(bf16[256,256]{1,0:T(8,128)(2,1)S(1)} %collective-permute-done.6.refs_3_), channel_id=1, source_target_pairs={{0,2},{2,4},{4,6},{6,7},{7,5},{5,3},{3,1},{1,0},{8,10},{10,12},{12... | collective-permute-start | bytes 393224 | tf_op jit(solution)/shard_map/ppermute | solution.py:33
  14.2 6.0 %collective-permute-start.11 = (bf16[256,256]{1,0:T(8,128)(2,1)S(1)}, bf16[256,256]{1,0:T(8,128)(2,1)S(1)}, u32[]{:S(2)}, u32[]{:S(2)}) collective-permute-start(bf16[256,256]{1,0:T(8,128)(2,1)S(1)} %collective-permute-done.10.refs_3_), channel_id=1, source_target_pairs={{0,1},{2,0},{4,2},{6,4},{7,6},{5,7},{3,5},{1,3},{8,9},{10,8},{12,1... | collective-permute-start | bytes 393224 | tf_op jit(solution)/shard_map/ppermute | solution.py:33
  14.7 6.0 %collective-permute-start.2 = (bf16[256,256]{1,0:T(8,128)(2,1)S(1)}, bf16[256,256]{1,0:T(8,128)(2,1)S(1)}, u32[]{:S(2)}, u32[]{:S(2)}) collective-permute-start(bf16[256,256]{1,0:T(8,128)(2,1)S(1)} %collective-permute-done.1.refs_0_), channel_id=1, source_target_pairs={{0,2},{2,4},{4,6},{6,7},{7,5},{5,3},{3,1},{1,0},{8,10},{10,12},{12... | collective-permute-start | bytes 393224 | tf_op jit(solution)/shard_map/ppermute | solution.py:33
  17.1 5.3 %collective-permute-start.5 = (bf16[256,256]{1,0:T(8,128)(2,1)S(1)}, bf16[256,256]{1,0:T(8,128)(2,1)S(1)}, u32[]{:S(2)}, u32[]{:S(2)}) collective-permute-start(bf16[256,256]{1,0:T(8,128)(2,1)S(1)} %collective-permute-done.4.refs_1_), channel_id=1, source_target_pairs={{0,1},{2,0},{4,2},{6,4},{7,6},{5,7},{3,5},{1,3},{8,9},{10,8},{12,1... | collective-permute-start | bytes 393224 | tf_op jit(solution)/shard_map/ppermute | solution.py:33
  17.5 5.0 %collective-permute-start.8 = (bf16[256,256]{1,0:T(8,128)(2,1)S(1)}, bf16[256,256]{1,0:T(8,128)(2,1)S(1)}, u32[]{:S(2)}, u32[]{:S(2)}) collective-permute-start(bf16[256,256]{1,0:T(8,128)(2,1)S(1)} %collective-permute-done.7.refs_2_), channel_id=1, source_target_pairs={{0,2},{2,4},{4,6},{6,7},{7,5},{5,3},{3,1},{1,0},{8,10},{10,12},{12... | collective-permute-start | bytes 393224 | tf_op jit(solution)/shard_map/ppermute | solution.py:33
  20.2 5.0 %collective-permute-start.13 = (bf16[256,256]{1,0:T(8,128)(2,1)S(1)}, bf16[256,256]{1,0:T(8,128)(2,1)S(1)}, u32[]{:S(2)}, u32[]{:S(2)}) collective-permute-start(bf16[256,256]{1,0:T(8,128)(2,1)S(1)} %collective-permute-done.11.refs_3_), channel_id=1, source_target_pairs={{0,1},{2,0},{4,2},{6,4},{7,6},{5,7},{3,5},{1,3},{8,9},{10,8},{12,1... | collective-permute-start | bytes 393224 | tf_op jit(solution)/shard_map/ppermute | solution.py:33
  20.7 5.0 %collective-permute-start.12 = (bf16[256,256]{1,0:T(8,128)(2,1)S(1)}, bf16[256,256]{1,0:T(8,128)(2,1)S(1)}, u32[]{:S(2)}, u32[]{:S(2)}) collective-permute-start(bf16[256,256]{1,0:T(8,128)(2,1)S(1)} %collective-permute-done.2.refs_0_), channel_id=1, source_target_pairs={{0,2},{2,4},{4,6},{6,7},{7,5},{5,3},{3,1},{1,0},{8,10},{10,12},{12... | collective-permute-start | bytes 393224 | tf_op jit(solution)/shard_map/ppermute | solution.py:33
  27.0 7.3 %collective-permute-start.17 = (bf16[256,512]{1,0:T(8,128)(2,1)S(1)}, bf16[256,512]{1,0:T(8,128)(2,1)S(1)}, u32[]{:S(2)}, u32[]{:S(2)}) collective-permute-start(bf16[256,512]{1,0:T(8,128)(2,1)S(1)} %get-tuple-element.52), channel_id=1, source_target_pairs={{0,16},{8,24},{16,0},{24,8},{1,17},{9,25},{17,1},{25,9},{2,18},{10... | collective-permute-start | bytes 786440 | tf_op jit(solution)/shard_map/ppermute | solution.py:395
  27.5 8.9 %collective-permute-start.18 = (bf16[256,512]{1,0:T(8,128)(2,1)S(1)}, bf16[256,512]{1,0:T(8,128)(2,1)S(1)}, u32[]{:S(2)}, u32[]{:S(2)}) collective-permute-start(bf16[256,512]{1,0:T(8,128)(2,1)S(1)} %get-tuple-element.53), channel_id=1, source_target_pairs={{0,16},{8,24},{16,0},{24,8},{1,17},{9,25},{17,1},{25,9},{2,18},{10... | collective-permute-start | bytes 786440 | tf_op jit(solution)/shard_map/ppermute | solution.py:395
  29.1 2.9 %collective-permute-start.15 = (bf16[176,512]{1,0:T(8,128)(2,1)S(1)}, bf16[176,512]{1,0:T(8,128)(2,1)S(1)}, u32[]{:S(2)}, u32[]{:S(2)}) collective-permute-start(bf16[176,512]{1,0:T(8,128)(2,1)S(1)} %get-tuple-element.46), channel_id=1, source_target_pairs={{0,8},{8,0},{16,24},{24,16},{1,9},{9,1},{17,25},{25,17},{2,10},{10... | collective-permute-start | bytes 540680 | tf_op jit(solution)/shard_map/ppermute | solution.py:39
  29.1 2.9 %collective-permute-start.16 = (bf16[176,512]{1,0:T(8,128)(2,1)S(1)}, bf16[176,512]{1,0:T(8,128)(2,1)S(1)}, u32[]{:S(2)}, u32[]{:S(2)}) collective-permute-start(bf16[176,512]{1,0:T(8,128)(2,1)S(1)} %get-tuple-element.47), channel_id=1, source_target_pairs={{0,8},{8,0},{16,24},{24,16},{1,9},{9,1},{17,25},{25,17},{2,10},{10... | collective-permute-start | bytes 540680 | tf_op jit(solution)/shard_map/ppermute | solution.py:39
  29.6 2.4 %collective-permute-start.14 = (bf16[160,512]{1,0:T(8,128)(2,1)S(1)}, bf16[160,512]{1,0:T(8,128)(2,1)S(1)}, u32[]{:S(2)}, u32[]{:S(2)}) collective-permute-start(bf16[160,512]{1,0:T(8,128)(2,1)S(1)} %get-tuple-element.45), channel_id=1, source_target_pairs={{0,8},{8,0},{16,24},{24,16},{1,9},{9,1},{17,25},{25,17},{2,10},{10... | collective-permute-start | bytes 491528 | tf_op jit(solution)/shard_map/ppermute | solution.py:39
  36.4 2.8 %collective-permute-start.19 = (bf16[256,512]{1,0:T(8,128)(2,1)S(1)}, bf16[256,512]{1,0:T(8,128)(2,1)S(1)}, u32[]{:S(2)}, u32[]{:S(2)}) collective-permute-start(bf16[256,512]{1,0:T(8,128)(2,1)S(1)} %collective-permute-done.17.refs_0_), channel_id=1, source_target_pairs={{0,8},{8,0},{16,24},{24,16},{1,9},{9,1},{17,25},{25,17},{2,10},{10... | collective-permute-start | bytes 786440 | tf_op jit(solution)/shard_map/ppermute | solution.py:39
  36.4 2.8 %collective-permute-start.20 = (bf16[256,512]{1,0:T(8,128)(2,1)S(1)}, bf16[256,512]{1,0:T(8,128)(2,1)S(1)}, u32[]{:S(2)}, u32[]{:S(2)}) collective-permute-start(bf16[256,512]{1,0:T(8,128)(2,1)S(1)} %collective-permute-done.18.refs_1_), channel_id=1, source_target_pairs={{0,8},{8,0},{16,24},{24,16},{1,9},{9,1},{17,25},{25,17},{2,10},{10... | collective-permute-start | bytes 786440 | tf_op jit(solution)/shard_map/ppermute | solution.py:39
  42.5 6.4 %collective-permute-start.21 = (bf16[256,256]{1,0:T(8,128)(2,1)S(1)}, bf16[256,256]{1,0:T(8,128)(2,1)S(1)}, u32[]{:S(2)}, u32[]{:S(2)}) collective-permute-start(bf16[256,256]{1,0:T(8,128)(2,1)S(1)} %get-tuple-element.61), channel_id=1, source_target_pairs={{0,2},{2,4},{4,6},{6,7},{7,5},{5,3},{3,1},{1,0},{8,10},{10,12},{12... | collective-permute-start | bytes 393224 | tf_op jit(solution)/shard_map/ppermute | solution.py:33
  44.2 6.5 %collective-permute-start.25 = (bf16[256,256]{1,0:T(8,128)(2,1)S(1)}, bf16[256,256]{1,0:T(8,128)(2,1)S(1)}, u32[]{:S(2)}, u32[]{:S(2)}) collective-permute-start(bf16[256,256]{1,0:T(8,128)(2,1)S(1)} %get-tuple-element.64), channel_id=1, source_target_pairs={{0,1},{2,0},{4,2},{6,4},{7,6},{5,7},{3,5},{1,3},{8,9},{10,8},{12,1... | collective-permute-start | bytes 393224 | tf_op jit(solution)/shard_map/ppermute | solution.py:33
  44.6 7.1 %collective-permute-start.28 = (bf16[256,256]{1,0:T(8,128)(2,1)S(1)}, bf16[256,256]{1,0:T(8,128)(2,1)S(1)}, u32[]{:S(2)}, u32[]{:S(2)}) collective-permute-start(bf16[256,256]{1,0:T(8,128)(2,1)S(1)} %get-tuple-element.68), channel_id=1, source_target_pairs={{0,2},{2,4},{4,6},{6,7},{7,5},{5,3},{3,1},{1,0},{8,10},{10,12},{12... | collective-permute-start | bytes 393224 | tf_op jit(solution)/shard_map/ppermute | solution.py:33
  46.2 7.2 %collective-permute-start.31 = (bf16[256,256]{1,0:T(8,128)(2,1)S(1)}, bf16[256,256]{1,0:T(8,128)(2,1)S(1)}, u32[]{:S(2)}, u32[]{:S(2)}) collective-permute-start(bf16[256,256]{1,0:T(8,128)(2,1)S(1)} %get-tuple-element.72), channel_id=1, source_target_pairs={{0,1},{2,0},{4,2},{6,4},{7,6},{5,7},{3,5},{1,3},{8,9},{10,8},{12,1... | collective-permute-start | bytes 393224 | tf_op jit(solution)/shard_map/ppermute | solution.py:33
  49.0 6.4 %collective-permute-start.22 = (bf16[256,256]{1,0:T(8,128)(2,1)S(1)}, bf16[256,256]{1,0:T(8,128)(2,1)S(1)}, u32[]{:S(2)}, u32[]{:S(2)}) collective-permute-start(bf16[256,256]{1,0:T(8,128)(2,1)S(1)} %add_convert_fusion.11), channel_id=1, source_target_pairs={{0,2},{2,4},{4,6},{6,7},{7,5},{5,3},{3,1},{1,0},{8,10},{10,12},{12... | collective-permute-start | bytes 393224 | tf_op jit(solution)/shard_map/ppermute | solution.py:33
  50.7 6.4 %collective-permute-start.26 = (bf16[256,256]{1,0:T(8,128)(2,1)S(1)}, bf16[256,256]{1,0:T(8,128)(2,1)S(1)}, u32[]{:S(2)}, u32[]{:S(2)}) collective-permute-start(bf16[256,256]{1,0:T(8,128)(2,1)S(1)} %add_convert_fusion.8), channel_id=1, source_target_pairs={{0,1},{2,0},{4,2},{6,4},{7,6},{5,7},{3,5},{1,3},{8,9},{10,8},{12,1... | collective-permute-start | bytes 393224 | tf_op jit(solution)/shard_map/ppermute | solution.py:33
  51.8 6.4 %collective-permute-start.29 = (bf16[256,256]{1,0:T(8,128)(2,1)S(1)}, bf16[256,256]{1,0:T(8,128)(2,1)S(1)}, u32[]{:S(2)}, u32[]{:S(2)}) collective-permute-start(bf16[256,256]{1,0:T(8,128)(2,1)S(1)} %add_convert_fusion.5), channel_id=1, source_target_pairs={{0,2},{2,4},{4,6},{6,7},{7,5},{5,3},{3,1},{1,0},{8,10},{10,12},{12... | collective-permute-start | bytes 393224 | tf_op jit(solution)/shard_map/ppermute | solution.py:33
  53.5 6.4 %collective-permute-start.32 = (bf16[256,256]{1,0:T(8,128)(2,1)S(1)}, bf16[256,256]{1,0:T(8,128)(2,1)S(1)}, u32[]{:S(2)}, u32[]{:S(2)}) collective-permute-start(bf16[256,256]{1,0:T(8,128)(2,1)S(1)} %add_convert_fusion.3), channel_id=1, source_target_pairs={{0,1},{2,0},{4,2},{6,4},{7,6},{5,7},{3,5},{1,3},{8,9},{10,8},{12,1... | collective-permute-start | bytes 393224 | tf_op jit(solution)/shard_map/ppermute | solution.py:33
  55.4 5.6 %collective-permute-start.23 = (bf16[256,256]{1,0:T(8,128)(2,1)S(1)}, bf16[256,256]{1,0:T(8,128)(2,1)S(1)}, u32[]{:S(2)}, u32[]{:S(2)}) collective-permute-start(bf16[256,256]{1,0:T(8,128)(2,1)S(1)} %add_convert_fusion.10), channel_id=1, source_target_pairs={{0,2},{2,4},{4,6},{6,7},{7,5},{5,3},{3,1},{1,0},{8,10},{10,12},{12... | collective-permute-start | bytes 393224 | tf_op jit(solution)/shard_map/ppermute | solution.py:33
  57.1 9.2 %collective-permute-start.27 = (bf16[256,256]{1,0:T(8,128)(2,1)S(1)}, bf16[256,256]{1,0:T(8,128)(2,1)S(1)}, u32[]{:S(2)}, u32[]{:S(2)}) collective-permute-start(bf16[256,256]{1,0:T(8,128)(2,1)S(1)} %add_convert_fusion.7), channel_id=1, source_target_pairs={{0,1},{2,0},{4,2},{6,4},{7,6},{5,7},{3,5},{1,3},{8,9},{10,8},{12,1... | collective-permute-start | bytes 393224 | tf_op jit(solution)/shard_map/ppermute | solution.py:33
  58.3 8.2 %collective-permute-start.30 = (bf16[256,256]{1,0:T(8,128)(2,1)S(1)}, bf16[256,256]{1,0:T(8,128)(2,1)S(1)}, u32[]{:S(2)}, u32[]{:S(2)}) collective-permute-start(bf16[256,256]{1,0:T(8,128)(2,1)S(1)} %add_convert_fusion.4), channel_id=1, source_target_pairs={{0,2},{2,4},{4,6},{6,7},{7,5},{5,3},{3,1},{1,0},{8,10},{10,12},{12... | collective-permute-start | bytes 393224 | tf_op jit(solution)/shard_map/ppermute | solution.py:33
  59.9 5.9 %collective-permute-start.33 = (bf16[256,256]{1,0:T(8,128)(2,1)S(1)}, bf16[256,256]{1,0:T(8,128)(2,1)S(1)}, u32[]{:S(2)}, u32[]{:S(2)}) collective-permute-start(bf16[256,256]{1,0:T(8,128)(2,1)S(1)} %add_convert_fusion.2), channel_id=1, source_target_pairs={{0,1},{2,0},{4,2},{6,4},{7,6},{5,7},{3,5},{1,3},{8,9},{10,8},{12,1... | collective-permute-start | bytes 393224 | tf_op jit(solution)/shard_map/ppermute | solution.py:33
  61.1 5.3 %collective-permute-start.24 = (bf16[256,256]{1,0:T(8,128)(2,1)S(1)}, bf16[256,256]{1,0:T(8,128)(2,1)S(1)}, u32[]{:S(2)}, u32[]{:S(2)}) collective-permute-start(bf16[256,256]{1,0:T(8,128)(2,1)S(1)} %add_convert_fusion.9), channel_id=1, source_target_pairs={{0,2},{2,4},{4,6},{6,7},{7,5},{5,3},{3,1},{1,0},{8,10},{10,12},{12... | collective-permute-start | bytes 393224 | tf_op jit(solution)/shard_map/ppermute | solution.py:33
  65.9 5.0 %collective-permute-start.34 = (bf16[256,256]{1,0:T(8,128)(2,1)S(1)}, bf16[256,256]{1,0:T(8,128)(2,1)S(1)}, u32[]{:S(2)}, u32[]{:S(2)}) collective-permute-start(bf16[256,256]{1,0:T(8,128)(2,1)S(1)} %add_convert_fusion.1), channel_id=1, source_target_pairs={{0,1},{2,0},{4,2},{6,4},{7,6},{5,7},{3,5},{1,3},{8,9},{10,8},{12,1... | collective-permute-start | bytes 393224 | tf_op jit(solution)/shard_map/ppermute | solution.py:33

commit v16 on v15

--- a/solution.py
+++ b/solution.py
@@ -47,7 +47,7 @@
     return pltpu.with_memory_space_constraint(value, pltpu.VMEM)
 
 
-def fold_kernel(order, at, gain_ref, w_hbm, out_ref, sems):
+def fold_kernel(order, at, gain_ref, w_hbm, tokens, out_ref, wide, sems):
     lanes = gain_ref.shape[1]
     size = w_hbm.shape[1] // len(order)
     per = size // lanes
@@ -55,11 +55,15 @@
     def fetch(n):
         start = pl.multiple_of(at[order[n]] * size, size)
         return pltpu.make_async_copy(
-            w_hbm.at[:, pl.ds(start, size), :], out_ref.at[:, n * size : (n + 1) * size, :], sems.at[n]
+            w_hbm.at[:, pl.ds(start, size), :],
+            out_ref.at[:, n * size : (n + 1) * size, :],
+            sems.at[n],
         )
 
     for n in range(len(order)):
         fetch(n).start()
+    own = pltpu.make_async_copy(tokens, wide.at[:, : tokens.shape[1]], sems.at[len(order)])
+    own.start()
     for n in range(len(order)):
         columns = jnp.transpose(gain_ref[pl.ds(at[order[n]] * per, per), :])
         fetch(n).wait()
@@ -69,23 +73,25 @@
                 here = (group, slice(first, first + lanes), slice(None))
                 scaled = out_ref[here].astype(F32) * columns[:, piece : piece + 1]
                 out_ref[here] = scaled.astype(BF16)
-
-
-def fold_gain(order, at, gain, weights):
+    own.wait()
+
+
+def fold_gain(order, at, gain, weights, tokens):
     depth = weights.shape[1]
     lanes = math.gcd(depth // len(order), 128)
+    hbm = pl.BlockSpec(memory_space=pltpu.HBM)
     return pl.pallas_call(
         functools.partial(fold_kernel, order),
-        out_shape=pltpu.VMEM(weights.shape, BF16),
-        in_specs=[SMEM, VMEM, pl.BlockSpec(memory_space=pltpu.HBM)],
-        out_specs=VMEM,
-        scratch_shapes=[pltpu.SemaphoreType.DMA((len(order),))],
+        out_shape=(pltpu.VMEM(weights.shape, BF16), pltpu.VMEM((tokens.shape[0], depth), BF16)),
+        in_specs=[SMEM, VMEM, hbm, hbm],
+        out_specs=(VMEM, pl.BlockSpec(memory_space=pl.ANY)),
+        scratch_shapes=[pltpu.SemaphoreType.DMA((len(order) + 1,))],
         compiler_params=pltpu.CompilerParams(vmem_limit_bytes=16 << 20),
         cost_estimate=pl.CostEstimate(
             flops=weights.size, bytes_accessed=4 * weights.size, transcendentals=0
         ),
         name="fold_gain",
-    )(at, in_hbm(gain.reshape(depth // lanes, lanes)), in_hbm(weights))
+    )(at, in_hbm(gain.reshape(depth // lanes, lanes)), in_hbm(weights), in_hbm(tokens))
 
 
 def place_kernel(targets, *refs):
@@ -101,15 +107,15 @@
         copy.wait()
 
 
-def placed(targets, blocks, wide, shape):
-    operands = [*blocks] + ([] if wide is None else [in_vmem(wide)])
+def placed(targets, blocks, wide):
+    operands = [*map(in_vmem, blocks), in_vmem(wide)]
     return pl.pallas_call(
         functools.partial(place_kernel, targets),
-        out_shape=pltpu.VMEM(shape, BF16),
+        out_shape=pltpu.VMEM(wide.shape, BF16),
         in_specs=[pl.BlockSpec(memory_space=pl.ANY)] * len(operands),
         out_specs=pl.BlockSpec(memory_space=pl.ANY),
         scratch_shapes=[pltpu.SemaphoreType.DMA((len(targets),))],
-        input_output_aliases={} if wide is None else {len(blocks): 0},
+        input_output_aliases={len(blocks): 0},
         compiler_params=pltpu.CompilerParams(vmem_limit_bytes=1 << 20),
         cost_estimate=pl.CostEstimate(flops=0, bytes_accessed=1 << 20, transcendentals=0),
         name="place",
@@ -248,24 +254,29 @@
 
             def add(masked):
                 if masked:
-                    key_ids = [id_row[first // tile + n] for n in range(keys // tile)]
                     own = jnp.broadcast_to(id_row[q_first // tile + index], (8, tile))
-                    allowed = jnp.concatenate(key_ids, axis=1) <= jnp.transpose(own)[:, :1]
+                    own = jnp.transpose(own)[:, :1]
+                    allowed = [id_row[first // tile + n] <= own for n in range(keys // tile)]
                 for head in range(heads):
                     lanes = slice(head * head_size, (head + 1) * head_size)
-                    score = lax.dot_general(
-                        q_ref[here, lanes],
-                        k_all[:, lanes],
-                        (((1,), (1,)), ((), ())),
-                        preferred_element_type=F32,
-                    )
-                    weight = jnp.exp2(score)
-                    if masked:
-                        weight = jnp.where(allowed, weight, 0.0)
                     spread = slice(2 * head * head_size, 2 * (head + 1) * head_size)
-                    acc[here, spread] += jnp.dot(
-                        weight.astype(BF16), v_ones[head], preferred_element_type=F32
-                    )
+                    total = acc[here, spread]
+                    for low in range(0, keys, tile):
+                        score = lax.dot_general(
+                            q_ref[here, lanes],
+                            k_all[low : low + tile, lanes],
+                            (((1,), (1,)), ((), ())),
+                            preferred_element_type=F32,
+                        )
+                        weight = jnp.exp2(score)
+                        if masked:
+                            weight = jnp.where(allowed[low // tile], weight, 0.0)
+                        total += jnp.dot(
+                            weight.astype(BF16),
+                            v_ones[head, low : low + tile, :],
+                            preferred_element_type=F32,
+                        )
+                    acc[here, spread] = total
 
             @pl.when(key_high <= q_low)
             def _():
@@ -356,30 +367,30 @@
 
     order = [0] + [sign * step % ring for step in range(1, farthest) for sign in (-1, 1)] + [farthest]
     held = [[tokens[s * half : (s + 1) * half]] * 2 for s in streams]
-    wide, blocks, targets = None, [in_hbm(tokens)], [(0, 0)]
+    blocks, targets = [], []
     for step in range(1, farthest + 1):
         for s in streams:
             for way, sign in ways:
                 if step <= reach[s][way]:
                     held[s][way] = along(held[s][way], sign, ring)
         if step == 1:
-            held[1][1], weights = lax.optimization_barrier(
-                (held[1][1], fold_gain(order, numbers(at), norm_gain, w_qkv))
+            held[1][1], (weights, wide) = lax.optimization_barrier(
+                (held[1][1], fold_gain(order, numbers(at), norm_gain, w_qkv, tokens))
             )
         elif step == 2:
-            wide = placed(targets, blocks, wide, (rows, ring * width))
+            wide = placed(targets, blocks, wide)
             blocks, targets = [], []
         elif step == 3:
             held[1][1], wide = lax.optimization_barrier(
-                (held[1][1], placed(targets, blocks, wide, (rows, ring * width)))
+                (held[1][1], placed(targets, blocks, wide))
             )
             blocks, targets = [], []
         if step < farthest:
             for s in streams:
                 for way, sign in ways:
-                    blocks.append(in_vmem(held[s][way]))
+                    blocks.append(held[s][way])
                     targets.append((s * half, (2 * step - 1 + way) * width))
-    wide = placed(targets, blocks, wide, (rows, ring * width))
+    wide = placed(targets, blocks, wide)
     lasts = [held[0][0], held[1][1]]
     state = project_begin(wide, weights, ring)
     query, kv, *parts = project_finish(head_scale, state, weights, lasts, 3, head_size)

time: 72.2 us -> 72.2 us (level)
  Pallas kernels: 17.4 us -> 16.5 us
  waiting for transfers between devices: 19.3 us -> 20.2 us
    pallas_call x3, Pallas kernels: 1.22 us -> 0.34 us  [placed(): pl.pallas_call(functools.partial(place_kernel, targets), out_shape=pltpu....]
  transfers between devices with their start and end apart: 35 -> 35, of which waited for: 13 -> 15; matrix products, arithmetic and copies ran while one was open for 1% -> 1% of each run, Pallas kernels for 18% -> 17%
where the time goes in v16:
time: 72.2 us; the launch traced here: 71.6 us
  starting transfers between devices  32.2 us (45%)
  waiting for transfers between devices  20.2 us (28%)
  Pallas kernels  16.5 us (23%)
  other arithmetic  1.39 us (2%)
  local copies, waits for them, and re-layouts  1.16 us (2%)
    ppermute x28, starting transfers between devices, along(): lax.ppermute(value, 'head', [(order[p], order[(p + step) % count]) for p...  29 us
    ppermute x28, waiting for transfers between devices, along(): lax.ppermute(value, 'head', [(order[p], order[(p + step) % count]) for p...  17.8 us
    pallas_call x4, Pallas kernels, attend(): pl.pallas_call(functools.partial(attend_kernel, head_size, (len(blocks),...  9.92 us
    pallas_call x1, Pallas kernels, fold_gain(): pl.pallas_call(functools.partial(fold_kernel, order), out_shape=(pltpu.VM...  3.02 us
    ppermute x2, waiting for transfers between devices, body(): far.append([lax.ppermute(part, 'seq', shift) for part in halves])  2.41 us
    ppermute x2, starting transfers between devices, body(): far.append([lax.ppermute(part, 'seq', shift) for part in halves])  2.09 us
    pallas_call x1, Pallas kernels, project_begin(): pl.pallas_call(functools.partial(begin_kernel, blocks), out_shape=pltpu.V...  1.91 us
  transfers between devices with their start and end apart: 35, of which 15 were waited for; matrix products, arithmetic and copies ran while one was open for 1% of the time, Pallas kernels for 17%

profile of v16, /device:TPU:10, one launch (start us, length us, event | category | flops | bytes accessed | tf_op | source)
XLA Modules:
  0.0 71.6 jit_solution(11794653062016872319)
XLA Ops:
  0.0 1.0 %fusion = (bf16[256,256]{1,0:T(8,128)(2,1)S(1)}, bf16[256,256]{1,0:T(8,128)(2,1)S(1)}) fusion(bf16[512,256]{1,0:T(8,128)(2,1)} %tokens.1), kind=kLoop, calls=%fused_computation.16 | loop fusion | bytes 524288 | tf_op jit(solution)/shard_map/slice | solution.py:369
  1.0 0.5 collective-permute-start.9
  1.5 1.6 %collective-permute-start = (bf16[256,256]{1,0:T(8,128)(2,1)S(1)}, bf16[256,256]{1,0:T(8,128)(2,1)S(1)}, u32[]{:S(2)}, u32[]{:S(2)}) collective-permute-start(bf16[256,256]{1,0:T(8,128)(2,1)S(1)} %get-tuple-element.80), channel_id=1, source_target_pairs={{0,2},{2,4},{4,6},{6,7},{7,5},{5,3},{3,1},{1,0},{8,10},{10,12},{12... | collective-permute-start | bytes 393224 | tf_op jit(solution)/shard_map/ppermute | solution.py:33
  3.5 1.6 %collective-permute-start.6 = (bf16[256,256]{1,0:T(8,128)(2,1)S(1)}, bf16[256,256]{1,0:T(8,128)(2,1)S(1)}, u32[]{:S(2)}, u32[]{:S(2)}) collective-permute-start(bf16[256,256]{1,0:T(8,128)(2,1)S(1)} %get-tuple-element.79), channel_id=1, source_target_pairs={{0,2},{2,4},{4,6},{6,7},{7,5},{5,3},{3,1},{1,0},{8,10},{10,12},{12... | collective-permute-start | bytes 393224 | tf_op jit(solution)/shard_map/ppermute | solution.py:33
  5.2 3.0 %fold_gain.1 = (bf16[3,2048,256]{2,1,0:T(8,128)(2,1)S(1)}, bf16[512,2048]{1,0:T(8,128)(2,1)S(1)}) custom-call(s32[8]{0:T(128)S(1)} %stack.84.at, f32[16,128]{1,0:T(8,128)} %bitcast.19, bf16[3,2048,256]{2,1,0:T(8,128)(2,1)} %w_hbm.1, bf16[512,256]{1,0:T(8,128)(2,1)} %tokens.1), custom_call_target="tpu_custom_call" | custom-call | flops 1572864 | bytes 6291456 | tf_op jit(solution)/shard_map/fold_gain/pallas_call | solution.py:83
  8.2 0.5 collective-permute-start.10
  8.7 1.6 %collective-permute-start.1 = (bf16[256,256]{1,0:T(8,128)(2,1)S(1)}, bf16[256,256]{1,0:T(8,128)(2,1)S(1)}, u32[]{:S(2)}, u32[]{:S(2)}) collective-permute-start(bf16[256,256]{1,0:T(8,128)(2,1)S(1)} %collective-permute-done.refs_0_), channel_id=1, source_target_pairs={{0,2},{2,4},{4,6},{6,7},{7,5},{5,3},{3,1},{1,0},{8,10},{10,12},{12... | collective-permute-start | bytes 393224 | tf_op jit(solution)/shard_map/ppermute | solution.py:33
  10.8 1.6 %collective-permute-start.7 = (bf16[256,256]{1,0:T(8,128)(2,1)S(1)}, bf16[256,256]{1,0:T(8,128)(2,1)S(1)}, u32[]{:S(2)}, u32[]{:S(2)}) collective-permute-start(bf16[256,256]{1,0:T(8,128)(2,1)S(1)} %collective-permute-done.6.refs_2_), channel_id=1, source_target_pairs={{0,2},{2,4},{4,6},{6,7},{7,5},{5,3},{3,1},{1,0},{8,10},{10,12},{12... | collective-permute-start | bytes 393224 | tf_op jit(solution)/shard_map/ppermute | solution.py:33
  12.3 1.9 %collective-permute-done.10.refs_3_ = bf16[256,256]{1,0:T(8,128)(2,1)S(1)} collective-permute-done((bf16[256,256]{1,0:T(8,128)(2,1)S(1)}, bf16[256,256]{1,0:T(8,128)(2,1)S(1)}, u32[]{:S(2)}, u32[]{:S(2)}) %collective-permute-start.10) | collective-permute-done | bytes 131104 | tf_op jit(solution)/shard_map/ppermute | solution.py:33
  14.7 1.6 %collective-permute-start.2 = (bf16[256,256]{1,0:T(8,128)(2,1)S(1)}, bf16[256,256]{1,0:T(8,128)(2,1)S(1)}, u32[]{:S(2)}, u32[]{:S(2)}) collective-permute-start(bf16[256,256]{1,0:T(8,128)(2,1)S(1)} %collective-permute-done.1.refs_0_), channel_id=1, source_target_pairs={{0,2},{2,4},{4,6},{6,7},{7,5},{5,3},{3,1},{1,0},{8,10},{10,12},{12... | collective-permute-start | bytes 393224 | tf_op jit(solution)/shard_map/ppermute | solution.py:33
  16.3 0.8 %collective-permute-done.4.refs_1_ = bf16[256,256]{1,0:T(8,128)(2,1)S(1)} collective-permute-done((bf16[256,256]{1,0:T(8,128)(2,1)S(1)}, bf16[256,256]{1,0:T(8,128)(2,1)S(1)}, u32[]{:S(2)}, u32[]{:S(2)}) %collective-permute-start.4) | collective-permute-done | bytes 131104 | tf_op jit(solution)/shard_map/ppermute | solution.py:33
  17.5 1.6 %collective-permute-start.8 = (bf16[256,256]{1,0:T(8,128)(2,1)S(1)}, bf16[256,256]{1,0:T(8,128)(2,1)S(1)}, u32[]{:S(2)}, u32[]{:S(2)}) collective-permute-start(bf16[256,256]{1,0:T(8,128)(2,1)S(1)} %collective-permute-done.7.refs_2_), channel_id=1, source_target_pairs={{0,2},{2,4},{4,6},{6,7},{7,5},{5,3},{3,1},{1,0},{8,10},{10,12},{12... | collective-permute-start | bytes 393224 | tf_op jit(solution)/shard_map/ppermute | solution.py:33
  19.3 0.6 collective-permute-done.11.refs_3_
  20.4 1.6 %collective-permute-start.12 = (bf16[256,256]{1,0:T(8,128)(2,1)S(1)}, bf16[256,256]{1,0:T(8,128)(2,1)S(1)}, u32[]{:S(2)}, u32[]{:S(2)}) collective-permute-start(bf16[256,256]{1,0:T(8,128)(2,1)S(1)} %collective-permute-done.2.refs_0_), channel_id=1, source_target_pairs={{0,2},{2,4},{4,6},{6,7},{7,5},{5,3},{3,1},{1,0},{8,10},{10,12},{12... | collective-permute-start | bytes 393224 | tf_op jit(solution)/shard_map/ppermute | solution.py:33
  22.6 1.9 %project_begin.1.state = f32[512,896]{1,0:T(8,128)S(1)} custom-call(bf16[512,2048]{1,0:T(8,128)(2,1)S(1)} %place.5.wide, bf16[3,2048,256]{2,1,0:T(8,128)(2,1)S(1)} %get-tuple-element.48.w_ref), custom_call_target="tpu_custom_call" | custom-call | flops 1610612736 | bytes 5242880 | tf_op jit(solution)/shard_map/project_begin/pallas_call | solution.py:180
  24.9 0.5 collective-permute-done.12.refs_0_
  25.4 1.3 %project_finish.1 = (bf16[512,256]{1,0:T(8,128)(2,1)S(1)}, bf16[512,512]{1,0:T(8,128)(2,1)S(1)}, bf16[256,512]{1,0:T(8,128)(2,1)S(1)}, bf16[256,512]{1,0:T(8,128...) custom-call(f32[2]{0:T(128)} %factor.1, ...), custom_call_target="tpu_custom_call" | custom-call | flops 201326592 | bytes 1048576 | tf_op jit(solution)/shard_map/project_finish/pallas_call | solution.py:202
  26.7 0.5 collective-permute-start.17
  27.2 1.6 %collective-permute-start.18 = (bf16[256,512]{1,0:T(8,128)(2,1)S(1)}, bf16[256,512]{1,0:T(8,128)(2,1)S(1)}, u32[]{:S(2)}, u32[]{:S(2)}) collective-permute-start(bf16[256,512]{1,0:T(8,128)(2,1)S(1)} %get-tuple-element.59), channel_id=1, source_target_pairs={{0,16},{8,24},{16,0},{24,8},{1,17},{9,25},{17,1},{25,9},{2,18},{10... | collective-permute-start | bytes 786440 | tf_op jit(solution)/shard_map/ppermute | solution.py:406
  28.8 0.5 collective-permute-start.16
  29.4 2.2 %attend.3.refs_3_ = f32[512,512]{1,0:T(8,128)S(1)} custom-call(s32[2]{0:T(128)S(1)} %pad_add_fusion.1.info, s32[2048]{0:T(1024)} %ids.7, bf16[512,256]{1,0:T(8,128)(2,1)S(1)} %get-tuple-element.49.q_ref, s32[8,1,256]{2,1,0:T(1,128)} %bitcast.15, bf16[512,512]{1,0:T(8,128)(2,1)S(1)} %get-tuple-element.50.refs_0_), custom_call_target="tpu_custom_call" | custom-call | flops 1048576 | bytes 1024 | tf_op jit(solution)/shard_map/attend/pallas_call | solution.py:331
  31.7 2.2 %attend.4.refs_2_ = f32[512,512]{1,0:T(8,128)S(1)} custom-call(s32[2]{0:T(128)S(1)} %pad_add_fusion.info, s32[2048]{0:T(1024)} %ids.7, bf16[512,256]{1,0:T(8,128)(2,1)S(1)} %get-tuple-element.49.q_ref, s32[8,1,256]{2,1,0:T(1,128)} %bitcast.16, bf16[160,512]{1,0:T(8,128)(2,1)S(1)} %collective-permute-done.14.refs_0_, ...), custom_call_target="tpu_custom_call" | custom-call | flops 1048576 | bytes 1024 | tf_op jit(solution)/shard_map/attend/pallas_call | solution.py:331
  34.0 2.4 %collective-permute-done.18.refs_1_ = bf16[256,512]{1,0:T(8,128)(2,1)S(1)} collective-permute-done((bf16[256,512]{1,0:T(8,128)(2,1)S(1)}, bf16[256,512]{1,0:T(8,128)(2,1)S(1)}, u32[]{:S(2)}, u32[]{:S(2)}) %collective-permute-start.18) | collective-permute-done | bytes 262176 | tf_op jit(solution)/shard_map/ppermute | solution.py:406
  36.4 0.5 collective-permute-start.20
  37.1 2.1 %attend.5.refs_2_ = f32[512,512]{1,0:T(8,128)S(1)} custom-call(s32[2]{0:T(128)S(1)} %pad_add_fusion.2.info, s32[2048]{0:T(1024)} %ids.7, bf16[512,256]{1,0:T(8,128)(2,1)S(1)} %get-tuple-element.49.q_ref, s32[8,1,256]{2,1,0:T(1,128)} %bitcast.17, bf16[256,512]{1,0:T(8,128)(2,1)S(1)} %collective-permute-done.17.refs_0_, ...), custom_call_target="tpu_custom_call" | custom-call | flops 1048576 | bytes 1024 | tf_op jit(solution)/shard_map/attend/pallas_call | solution.py:331
  39.3 3.3 %attend_last.1 = (bf16[256,256]{1,0:T(8,128)(2,1)S(1)}, bf16[256,256]{1,0:T(8,128)(2,1)S(1)}, bf16[256,256]{1,0:T(8,128)(2,1)S(1)}, bf16[256,256]{1,0:T(8,128)(2...) custom-call(s32[18]{0:T(128)S(1)} %stack.83.info, ...), custom_call_target="tpu_custom_call" | custom-call | flops 1048576 | bytes 1024 | tf_op jit(solution)/shard_map/attend_last/pallas_call | solution.py:331
  42.6 1.6 %collective-permute-start.21 = (bf16[256,256]{1,0:T(8,128)(2,1)S(1)}, bf16[256,256]{1,0:T(8,128)(2,1)S(1)}, u32[]{:S(2)}, u32[]{:S(2)}) collective-permute-start(bf16[256,256]{1,0:T(8,128)(2,1)S(1)} %get-tuple-element.67), channel_id=1, source_target_pairs={{0,2},{2,4},{4,6},{6,7},{7,5},{5,3},{3,1},{1,0},{8,10},{10,12},{12... | collective-permute-start | bytes 393224 | tf_op jit(solution)/shard_map/ppermute | solution.py:33
  44.2 0.5 collective-permute-start.25
  44.6 1.6 %collective-permute-start.28 = (bf16[256,256]{1,0:T(8,128)(2,1)S(1)}, bf16[256,256]{1,0:T(8,128)(2,1)S(1)}, u32[]{:S(2)}, u32[]{:S(2)}) collective-permute-start(bf16[256,256]{1,0:T(8,128)(2,1)S(1)} %get-tuple-element.74), channel_id=1, source_target_pairs={{0,2},{2,4},{4,6},{6,7},{7,5},{5,3},{3,1},{1,0},{8,10},{10,12},{12... | collective-permute-start | bytes 393224 | tf_op jit(solution)/shard_map/ppermute | solution.py:33
  46.2 0.5 collective-permute-start.31
  46.7 2.3 %collective-permute-done.21 = bf16[256,256]{1,0:T(8,128)(2,1)S(1)} collective-permute-done((bf16[256,256]{1,0:T(8,128)(2,1)S(1)}, bf16[256,256]{1,0:T(8,128)(2,1)S(1)}, u32[]{:S(2)}, u32[]{:S(2)}) %collective-permute-start.21) | collective-permute-done | bytes 131104 | tf_op jit(solution)/shard_map/ppermute | solution.py:33
  49.0 1.6 %collective-permute-start.22 = (bf16[256,256]{1,0:T(8,128)(2,1)S(1)}, bf16[256,256]{1,0:T(8,128)(2,1)S(1)}, u32[]{:S(2)}, u32[]{:S(2)}) collective-permute-start(bf16[256,256]{1,0:T(8,128)(2,1)S(1)} %add_convert_fusion.11), channel_id=1, source_target_pairs={{0,2},{2,4},{4,6},{6,7},{7,5},{5,3},{3,1},{1,0},{8,10},{10,12},{12... | collective-permute-start | bytes 393224 | tf_op jit(solution)/shard_map/ppermute | solution.py:33
  50.7 0.5 collective-permute-start.26
  51.2 0.6 collective-permute-done.28
  51.8 1.6 %collective-permute-start.29 = (bf16[256,256]{1,0:T(8,128)(2,1)S(1)}, bf16[256,256]{1,0:T(8,128)(2,1)S(1)}, u32[]{:S(2)}, u32[]{:S(2)}) collective-permute-start(bf16[256,256]{1,0:T(8,128)(2,1)S(1)} %add_convert_fusion.5), channel_id=1, source_target_pairs={{0,2},{2,4},{4,6},{6,7},{7,5},{5,3},{3,1},{1,0},{8,10},{10,12},{12... | collective-permute-start | bytes 393224 | tf_op jit(solution)/shard_map/ppermute | solution.py:33
  53.5 0.5 collective-permute-start.32
  54.0 1.4 %collective-permute-done.22 = bf16[256,256]{1,0:T(8,128)(2,1)S(1)} collective-permute-done((bf16[256,256]{1,0:T(8,128)(2,1)S(1)}, bf16[256,256]{1,0:T(8,128)(2,1)S(1)}, u32[]{:S(2)}, u32[]{:S(2)}) %collective-permute-start.22) | collective-permute-done | bytes 131104 | tf_op jit(solution)/shard_map/ppermute | solution.py:33
  55.4 1.6 %collective-permute-start.23 = (bf16[256,256]{1,0:T(8,128)(2,1)S(1)}, bf16[256,256]{1,0:T(8,128)(2,1)S(1)}, u32[]{:S(2)}, u32[]{:S(2)}) collective-permute-start(bf16[256,256]{1,0:T(8,128)(2,1)S(1)} %add_convert_fusion.10), channel_id=1, source_target_pairs={{0,2},{2,4},{4,6},{6,7},{7,5},{5,3},{3,1},{1,0},{8,10},{10,12},{12... | collective-permute-start | bytes 393224 | tf_op jit(solution)/shard_map/ppermute | solution.py:33
  57.1 0.5 collective-permute-start.27
  57.6 0.6 collective-permute-done.29
  58.3 1.6 %collective-permute-start.30 = (bf16[256,256]{1,0:T(8,128)(2,1)S(1)}, bf16[256,256]{1,0:T(8,128)(2,1)S(1)}, u32[]{:S(2)}, u32[]{:S(2)}) collective-permute-start(bf16[256,256]{1,0:T(8,128)(2,1)S(1)} %add_convert_fusion.4), channel_id=1, source_target_pairs={{0,2},{2,4},{4,6},{6,7},{7,5},{5,3},{3,1},{1,0},{8,10},{10,12},{12... | collective-permute-start | bytes 393224 | tf_op jit(solution)/shard_map/ppermute | solution.py:33
  59.9 0.5 collective-permute-start.33
  60.5 0.6 collective-permute-done.23
  61.1 1.6 %collective-permute-start.24 = (bf16[256,256]{1,0:T(8,128)(2,1)S(1)}, bf16[256,256]{1,0:T(8,128)(2,1)S(1)}, u32[]{:S(2)}, u32[]{:S(2)}) collective-permute-start(bf16[256,256]{1,0:T(8,128)(2,1)S(1)} %add_convert_fusion.9), channel_id=1, source_target_pairs={{0,2},{2,4},{4,6},{6,7},{7,5},{5,3},{3,1},{1,0},{8,10},{10,12},{12... | collective-permute-start | bytes 393224 | tf_op jit(solution)/shard_map/ppermute | solution.py:33
  62.7 3.1 %collective-permute-done.33 = bf16[256,256]{1,0:T(8,128)(2,1)S(1)} collective-permute-done((bf16[256,256]{1,0:T(8,128)(2,1)S(1)}, bf16[256,256]{1,0:T(8,128)(2,1)S(1)}, u32[]{:S(2)}, u32[]{:S(2)}) %collective-permute-start.33) | collective-permute-done | bytes 131104 | tf_op jit(solution)/shard_map/ppermute | solution.py:33
  65.8 0.5 collective-permute-start.34
  66.4 4.4 %collective-permute-done.34 = bf16[256,256]{1,0:T(8,128)(2,1)S(1)} collective-permute-done((bf16[256,256]{1,0:T(8,128)(2,1)S(1)}, bf16[256,256]{1,0:T(8,128)(2,1)S(1)}, u32[]{:S(2)}, u32[]{:S(2)}) %collective-permute-start.34) | collective-permute-done | bytes 131104 | tf_op jit(solution)/shard_map/ppermute | solution.py:33
  70.9 0.7 %pad_maximum_fusion = bf16[512,256]{1,0:T(8,128)(2,1)} fusion(bf16[256,256]{1,0:T(8,128)(2,1)S(1)} %add_convert_fusion, bf16[256,256]{1,0:T(8,128)(2,1)S(1)} %add_convert_fusion.6), kind=kLoop, calls=%fused_computation | loop fusion | flops 524288 | bytes 524288 | tf_op jit(solution)/shard_map/concatenate | solution.py:431
  (51 shorter events, 4.4 us)
Async XLA Ops:
  1.0 7.2 %collective-permute-start.9 = (bf16[256,256]{1,0:T(8,128)(2,1)S(1)}, bf16[256,256]{1,0:T(8,128)(2,1)S(1)}, u32[]{:S(2)}, u32[]{:S(2)}) collective-permute-start(bf16[256,256]{1,0:T(8,128)(2,1)S(1)} %get-tuple-element.79), channel_id=1, source_target_pairs={{0,1},{2,0},{4,2},{6,4},{7,6},{5,7},{3,5},{1,3},{8,9},{10,8},{12,1... | collective-permute-start | bytes 393224 | tf_op jit(solution)/shard_map/ppermute | solution.py:33
  1.5 7.2 %collective-permute-start = (bf16[256,256]{1,0:T(8,128)(2,1)S(1)}, bf16[256,256]{1,0:T(8,128)(2,1)S(1)}, u32[]{:S(2)}, u32[]{:S(2)}) collective-permute-start(bf16[256,256]{1,0:T(8,128)(2,1)S(1)} %get-tuple-element.80), channel_id=1, source_target_pairs={{0,2},{2,4},{4,6},{6,7},{7,5},{5,3},{3,1},{1,0},{8,10},{10,12},{12... | collective-permute-start | bytes 393224 | tf_op jit(solution)/shard_map/ppermute | solution.py:33
  3.1 7.2 %collective-permute-start.3 = (bf16[256,256]{1,0:T(8,128)(2,1)S(1)}, bf16[256,256]{1,0:T(8,128)(2,1)S(1)}, u32[]{:S(2)}, u32[]{:S(2)}) collective-permute-start(bf16[256,256]{1,0:T(8,128)(2,1)S(1)} %get-tuple-element.80), channel_id=1, source_target_pairs={{0,1},{2,0},{4,2},{6,4},{7,6},{5,7},{3,5},{1,3},{8,9},{10,8},{12,1... | collective-permute-start | bytes 393224 | tf_op jit(solution)/shard_map/ppermute | solution.py:33
  3.5 7.2 %collective-permute-start.6 = (bf16[256,256]{1,0:T(8,128)(2,1)S(1)}, bf16[256,256]{1,0:T(8,128)(2,1)S(1)}, u32[]{:S(2)}, u32[]{:S(2)}) collective-permute-start(bf16[256,256]{1,0:T(8,128)(2,1)S(1)} %get-tuple-element.79), channel_id=1, source_target_pairs={{0,2},{2,4},{4,6},{6,7},{7,5},{5,3},{3,1},{1,0},{8,10},{10,12},{12... | collective-permute-start | bytes 393224 | tf_op jit(solution)/shard_map/ppermute | solution.py:33
  8.2 6.0 %collective-permute-start.10 = (bf16[256,256]{1,0:T(8,128)(2,1)S(1)}, bf16[256,256]{1,0:T(8,128)(2,1)S(1)}, u32[]{:S(2)}, u32[]{:S(2)}) collective-permute-start(bf16[256,256]{1,0:T(8,128)(2,1)S(1)} %collective-permute-done.9.refs_3_), channel_id=1, source_target_pairs={{0,1},{2,0},{4,2},{6,4},{7,6},{5,7},{3,5},{1,3},{8,9},{10,8},{12,1... | collective-permute-start | bytes 393224 | tf_op jit(solution)/shard_map/ppermute | solution.py:33
  8.7 6.0 %collective-permute-start.1 = (bf16[256,256]{1,0:T(8,128)(2,1)S(1)}, bf16[256,256]{1,0:T(8,128)(2,1)S(1)}, u32[]{:S(2)}, u32[]{:S(2)}) collective-permute-start(bf16[256,256]{1,0:T(8,128)(2,1)S(1)} %collective-permute-done.refs_0_), channel_id=1, source_target_pairs={{0,2},{2,4},{4,6},{6,7},{7,5},{5,3},{3,1},{1,0},{8,10},{10,12},{12... | collective-permute-start | bytes 393224 | tf_op jit(solution)/shard_map/ppermute | solution.py:33
  10.3 6.8 %collective-permute-start.4 = (bf16[256,256]{1,0:T(8,128)(2,1)S(1)}, bf16[256,256]{1,0:T(8,128)(2,1)S(1)}, u32[]{:S(2)}, u32[]{:S(2)}) collective-permute-start(bf16[256,256]{1,0:T(8,128)(2,1)S(1)} %collective-permute-done.3.refs_1_), channel_id=1, source_target_pairs={{0,1},{2,0},{4,2},{6,4},{7,6},{5,7},{3,5},{1,3},{8,9},{10,8},{12,1... | collective-permute-start | bytes 393224 | tf_op jit(solution)/shard_map/ppermute | solution.py:33
  10.8 6.8 %collective-permute-start.7 = (bf16[256,256]{1,0:T(8,128)(2,1)S(1)}, bf16[256,256]{1,0:T(8,128)(2,1)S(1)}, u32[]{:S(2)}, u32[]{:S(2)}) collective-permute-start(bf16[256,256]{1,0:T(8,128)(2,1)S(1)} %collective-permute-done.6.refs_2_), channel_id=1, source_target_pairs={{0,2},{2,4},{4,6},{6,7},{7,5},{5,3},{3,1},{1,0},{8,10},{10,12},{12... | collective-permute-start | bytes 393224 | tf_op jit(solution)/shard_map/ppermute | solution.py:33
  14.3 5.7 %collective-permute-start.11 = (bf16[256,256]{1,0:T(8,128)(2,1)S(1)}, bf16[256,256]{1,0:T(8,128)(2,1)S(1)}, u32[]{:S(2)}, u32[]{:S(2)}) collective-permute-start(bf16[256,256]{1,0:T(8,128)(2,1)S(1)} %collective-permute-done.10.refs_3_), channel_id=1, source_target_pairs={{0,1},{2,0},{4,2},{6,4},{7,6},{5,7},{3,5},{1,3},{8,9},{10,8},{12,1... | collective-permute-start | bytes 393224 | tf_op jit(solution)/shard_map/ppermute | solution.py:33
  14.7 5.7 %collective-permute-start.2 = (bf16[256,256]{1,0:T(8,128)(2,1)S(1)}, bf16[256,256]{1,0:T(8,128)(2,1)S(1)}, u32[]{:S(2)}, u32[]{:S(2)}) collective-permute-start(bf16[256,256]{1,0:T(8,128)(2,1)S(1)} %collective-permute-done.1.refs_0_), channel_id=1, source_target_pairs={{0,2},{2,4},{4,6},{6,7},{7,5},{5,3},{3,1},{1,0},{8,10},{10,12},{12... | collective-permute-start | bytes 393224 | tf_op jit(solution)/shard_map/ppermute | solution.py:33
  17.1 5.2 %collective-permute-start.5 = (bf16[256,256]{1,0:T(8,128)(2,1)S(1)}, bf16[256,256]{1,0:T(8,128)(2,1)S(1)}, u32[]{:S(2)}, u32[]{:S(2)}) collective-permute-start(bf16[256,256]{1,0:T(8,128)(2,1)S(1)} %collective-permute-done.4.refs_1_), channel_id=1, source_target_pairs={{0,1},{2,0},{4,2},{6,4},{7,6},{5,7},{3,5},{1,3},{8,9},{10,8},{12,1... | collective-permute-start | bytes 393224 | tf_op jit(solution)/shard_map/ppermute | solution.py:33
  17.5 5.0 %collective-permute-start.8 = (bf16[256,256]{1,0:T(8,128)(2,1)S(1)}, bf16[256,256]{1,0:T(8,128)(2,1)S(1)}, u32[]{:S(2)}, u32[]{:S(2)}) collective-permute-start(bf16[256,256]{1,0:T(8,128)(2,1)S(1)} %collective-permute-done.7.refs_2_), channel_id=1, source_target_pairs={{0,2},{2,4},{4,6},{6,7},{7,5},{5,3},{3,1},{1,0},{8,10},{10,12},{12... | collective-permute-start | bytes 393224 | tf_op jit(solution)/shard_map/ppermute | solution.py:33
  20.0 5.0 %collective-permute-start.13 = (bf16[256,256]{1,0:T(8,128)(2,1)S(1)}, bf16[256,256]{1,0:T(8,128)(2,1)S(1)}, u32[]{:S(2)}, u32[]{:S(2)}) collective-permute-start(bf16[256,256]{1,0:T(8,128)(2,1)S(1)} %collective-permute-done.11.refs_3_), channel_id=1, source_target_pairs={{0,1},{2,0},{4,2},{6,4},{7,6},{5,7},{3,5},{1,3},{8,9},{10,8},{12,1... | collective-permute-start | bytes 393224 | tf_op jit(solution)/shard_map/ppermute | solution.py:33
  20.4 5.0 %collective-permute-start.12 = (bf16[256,256]{1,0:T(8,128)(2,1)S(1)}, bf16[256,256]{1,0:T(8,128)(2,1)S(1)}, u32[]{:S(2)}, u32[]{:S(2)}) collective-permute-start(bf16[256,256]{1,0:T(8,128)(2,1)S(1)} %collective-permute-done.2.refs_0_), channel_id=1, source_target_pairs={{0,2},{2,4},{4,6},{6,7},{7,5},{5,3},{3,1},{1,0},{8,10},{10,12},{12... | collective-permute-start | bytes 393224 | tf_op jit(solution)/shard_map/ppermute | solution.py:33
  26.7 7.3 %collective-permute-start.17 = (bf16[256,512]{1,0:T(8,128)(2,1)S(1)}, bf16[256,512]{1,0:T(8,128)(2,1)S(1)}, u32[]{:S(2)}, u32[]{:S(2)}) collective-permute-start(bf16[256,512]{1,0:T(8,128)(2,1)S(1)} %get-tuple-element.58), channel_id=1, source_target_pairs={{0,16},{8,24},{16,0},{24,8},{1,17},{9,25},{17,1},{25,9},{2,18},{10... | collective-permute-start | bytes 786440 | tf_op jit(solution)/shard_map/ppermute | solution.py:406
  27.2 9.2 %collective-permute-start.18 = (bf16[256,512]{1,0:T(8,128)(2,1)S(1)}, bf16[256,512]{1,0:T(8,128)(2,1)S(1)}, u32[]{:S(2)}, u32[]{:S(2)}) collective-permute-start(bf16[256,512]{1,0:T(8,128)(2,1)S(1)} %get-tuple-element.59), channel_id=1, source_target_pairs={{0,16},{8,24},{16,0},{24,8},{1,17},{9,25},{17,1},{25,9},{2,18},{10... | collective-permute-start | bytes 786440 | tf_op jit(solution)/shard_map/ppermute | solution.py:406
  28.8 2.9 %collective-permute-start.15 = (bf16[176,512]{1,0:T(8,128)(2,1)S(1)}, bf16[176,512]{1,0:T(8,128)(2,1)S(1)}, u32[]{:S(2)}, u32[]{:S(2)}) collective-permute-start(bf16[176,512]{1,0:T(8,128)(2,1)S(1)} %get-tuple-element.52), channel_id=1, source_target_pairs={{0,8},{8,0},{16,24},{24,16},{1,9},{9,1},{17,25},{25,17},{2,10},{10... | collective-permute-start | bytes 540680 | tf_op jit(solution)/shard_map/ppermute | solution.py:39
  28.8 2.9 %collective-permute-start.16 = (bf16[176,512]{1,0:T(8,128)(2,1)S(1)}, bf16[176,512]{1,0:T(8,128)(2,1)S(1)}, u32[]{:S(2)}, u32[]{:S(2)}) collective-permute-start(bf16[176,512]{1,0:T(8,128)(2,1)S(1)} %get-tuple-element.53), channel_id=1, source_target_pairs={{0,8},{8,0},{16,24},{24,16},{1,9},{9,1},{17,25},{25,17},{2,10},{10... | collective-permute-start | bytes 540680 | tf_op jit(solution)/shard_map/ppermute | solution.py:39
  29.3 2.4 %collective-permute-start.14 = (bf16[160,512]{1,0:T(8,128)(2,1)S(1)}, bf16[160,512]{1,0:T(8,128)(2,1)S(1)}, u32[]{:S(2)}, u32[]{:S(2)}) collective-permute-start(bf16[160,512]{1,0:T(8,128)(2,1)S(1)} %get-tuple-element.51), channel_id=1, source_target_pairs={{0,8},{8,0},{16,24},{24,16},{1,9},{9,1},{17,25},{25,17},{2,10},{10... | collective-permute-start | bytes 491528 | tf_op jit(solution)/shard_map/ppermute | solution.py:39
  36.4 2.8 %collective-permute-start.19 = (bf16[256,512]{1,0:T(8,128)(2,1)S(1)}, bf16[256,512]{1,0:T(8,128)(2,1)S(1)}, u32[]{:S(2)}, u32[]{:S(2)}) collective-permute-start(bf16[256,512]{1,0:T(8,128)(2,1)S(1)} %collective-permute-done.17.refs_0_), channel_id=1, source_target_pairs={{0,8},{8,0},{16,24},{24,16},{1,9},{9,1},{17,25},{25,17},{2,10},{10... | collective-permute-start | bytes 786440 | tf_op jit(solution)/shard_map/ppermute | solution.py:39
  36.4 2.8 %collective-permute-start.20 = (bf16[256,512]{1,0:T(8,128)(2,1)S(1)}, bf16[256,512]{1,0:T(8,128)(2,1)S(1)}, u32[]{:S(2)}, u32[]{:S(2)}) collective-permute-start(bf16[256,512]{1,0:T(8,128)(2,1)S(1)} %collective-permute-done.18.refs_1_), channel_id=1, source_target_pairs={{0,8},{8,0},{16,24},{24,16},{1,9},{9,1},{17,25},{25,17},{2,10},{10... | collective-permute-start | bytes 786440 | tf_op jit(solution)/shard_map/ppermute | solution.py:39
  42.6 6.4 %collective-permute-start.21 = (bf16[256,256]{1,0:T(8,128)(2,1)S(1)}, bf16[256,256]{1,0:T(8,128)(2,1)S(1)}, u32[]{:S(2)}, u32[]{:S(2)}) collective-permute-start(bf16[256,256]{1,0:T(8,128)(2,1)S(1)} %get-tuple-element.67), channel_id=1, source_target_pairs={{0,2},{2,4},{4,6},{6,7},{7,5},{5,3},{3,1},{1,0},{8,10},{10,12},{12... | collective-permute-start | bytes 393224 | tf_op jit(solution)/shard_map/ppermute | solution.py:33
  44.2 6.5 %collective-permute-start.25 = (bf16[256,256]{1,0:T(8,128)(2,1)S(1)}, bf16[256,256]{1,0:T(8,128)(2,1)S(1)}, u32[]{:S(2)}, u32[]{:S(2)}) collective-permute-start(bf16[256,256]{1,0:T(8,128)(2,1)S(1)} %get-tuple-element.70), channel_id=1, source_target_pairs={{0,1},{2,0},{4,2},{6,4},{7,6},{5,7},{3,5},{1,3},{8,9},{10,8},{12,1... | collective-permute-start | bytes 393224 | tf_op jit(solution)/shard_map/ppermute | solution.py:33
  44.6 7.1 %collective-permute-start.28 = (bf16[256,256]{1,0:T(8,128)(2,1)S(1)}, bf16[256,256]{1,0:T(8,128)(2,1)S(1)}, u32[]{:S(2)}, u32[]{:S(2)}) collective-permute-start(bf16[256,256]{1,0:T(8,128)(2,1)S(1)} %get-tuple-element.74), channel_id=1, source_target_pairs={{0,2},{2,4},{4,6},{6,7},{7,5},{5,3},{3,1},{1,0},{8,10},{10,12},{12... | collective-permute-start | bytes 393224 | tf_op jit(solution)/shard_map/ppermute | solution.py:33
  46.2 7.2 %collective-permute-start.31 = (bf16[256,256]{1,0:T(8,128)(2,1)S(1)}, bf16[256,256]{1,0:T(8,128)(2,1)S(1)}, u32[]{:S(2)}, u32[]{:S(2)}) collective-permute-start(bf16[256,256]{1,0:T(8,128)(2,1)S(1)} %get-tuple-element.78), channel_id=1, source_target_pairs={{0,1},{2,0},{4,2},{6,4},{7,6},{5,7},{3,5},{1,3},{8,9},{10,8},{12,1... | collective-permute-start | bytes 393224 | tf_op jit(solution)/shard_map/ppermute | solution.py:33
  49.0 6.4 %collective-permute-start.22 = (bf16[256,256]{1,0:T(8,128)(2,1)S(1)}, bf16[256,256]{1,0:T(8,128)(2,1)S(1)}, u32[]{:S(2)}, u32[]{:S(2)}) collective-permute-start(bf16[256,256]{1,0:T(8,128)(2,1)S(1)} %add_convert_fusion.11), channel_id=1, source_target_pairs={{0,2},{2,4},{4,6},{6,7},{7,5},{5,3},{3,1},{1,0},{8,10},{10,12},{12... | collective-permute-start | bytes 393224 | tf_op jit(solution)/shard_map/ppermute | solution.py:33
  50.7 6.4 %collective-permute-start.26 = (bf16[256,256]{1,0:T(8,128)(2,1)S(1)}, bf16[256,256]{1,0:T(8,128)(2,1)S(1)}, u32[]{:S(2)}, u32[]{:S(2)}) collective-permute-start(bf16[256,256]{1,0:T(8,128)(2,1)S(1)} %add_convert_fusion.8), channel_id=1, source_target_pairs={{0,1},{2,0},{4,2},{6,4},{7,6},{5,7},{3,5},{1,3},{8,9},{10,8},{12,1... | collective-permute-start | bytes 393224 | tf_op jit(solution)/shard_map/ppermute | solution.py:33
  51.8 6.4 %collective-permute-start.29 = (bf16[256,256]{1,0:T(8,128)(2,1)S(1)}, bf16[256,256]{1,0:T(8,128)(2,1)S(1)}, u32[]{:S(2)}, u32[]{:S(2)}) collective-permute-start(bf16[256,256]{1,0:T(8,128)(2,1)S(1)} %add_convert_fusion.5), channel_id=1, source_target_pairs={{0,2},{2,4},{4,6},{6,7},{7,5},{5,3},{3,1},{1,0},{8,10},{10,12},{12... | collective-permute-start | bytes 393224 | tf_op jit(solution)/shard_map/ppermute | solution.py:33
  53.5 6.4 %collective-permute-start.32 = (bf16[256,256]{1,0:T(8,128)(2,1)S(1)}, bf16[256,256]{1,0:T(8,128)(2,1)S(1)}, u32[]{:S(2)}, u32[]{:S(2)}) collective-permute-start(bf16[256,256]{1,0:T(8,128)(2,1)S(1)} %add_convert_fusion.3), channel_id=1, source_target_pairs={{0,1},{2,0},{4,2},{6,4},{7,6},{5,7},{3,5},{1,3},{8,9},{10,8},{12,1... | collective-permute-start | bytes 393224 | tf_op jit(solution)/shard_map/ppermute | solution.py:33
  55.4 5.6 %collective-permute-start.23 = (bf16[256,256]{1,0:T(8,128)(2,1)S(1)}, bf16[256,256]{1,0:T(8,128)(2,1)S(1)}, u32[]{:S(2)}, u32[]{:S(2)}) collective-permute-start(bf16[256,256]{1,0:T(8,128)(2,1)S(1)} %add_convert_fusion.10), channel_id=1, source_target_pairs={{0,2},{2,4},{4,6},{6,7},{7,5},{5,3},{3,1},{1,0},{8,10},{10,12},{12... | collective-permute-start | bytes 393224 | tf_op jit(solution)/shard_map/ppermute | solution.py:33
  57.1 9.2 %collective-permute-start.27 = (bf16[256,256]{1,0:T(8,128)(2,1)S(1)}, bf16[256,256]{1,0:T(8,128)(2,1)S(1)}, u32[]{:S(2)}, u32[]{:S(2)}) collective-permute-start(bf16[256,256]{1,0:T(8,128)(2,1)S(1)} %add_convert_fusion.7), channel_id=1, source_target_pairs={{0,1},{2,0},{4,2},{6,4},{7,6},{5,7},{3,5},{1,3},{8,9},{10,8},{12,1... | collective-permute-start | bytes 393224 | tf_op jit(solution)/shard_map/ppermute | solution.py:33
  58.3 8.1 %collective-permute-start.30 = (bf16[256,256]{1,0:T(8,128)(2,1)S(1)}, bf16[256,256]{1,0:T(8,128)(2,1)S(1)}, u32[]{:S(2)}, u32[]{:S(2)}) collective-permute-start(bf16[256,256]{1,0:T(8,128)(2,1)S(1)} %add_convert_fusion.4), channel_id=1, source_target_pairs={{0,2},{2,4},{4,6},{6,7},{7,5},{5,3},{3,1},{1,0},{8,10},{10,12},{12... | collective-permute-start | bytes 393224 | tf_op jit(solution)/shard_map/ppermute | solution.py:33
  59.9 5.9 %collective-permute-start.33 = (bf16[256,256]{1,0:T(8,128)(2,1)S(1)}, bf16[256,256]{1,0:T(8,128)(2,1)S(1)}, u32[]{:S(2)}, u32[]{:S(2)}) collective-permute-start(bf16[256,256]{1,0:T(8,128)(2,1)S(1)} %add_convert_fusion.2), channel_id=1, source_target_pairs={{0,1},{2,0},{4,2},{6,4},{7,6},{5,7},{3,5},{1,3},{8,9},{10,8},{12,1... | collective-permute-start | bytes 393224 | tf_op jit(solution)/shard_map/ppermute | solution.py:33
  61.1 5.3 %collective-permute-start.24 = (bf16[256,256]{1,0:T(8,128)(2,1)S(1)}, bf16[256,256]{1,0:T(8,128)(2,1)S(1)}, u32[]{:S(2)}, u32[]{:S(2)}) collective-permute-start(bf16[256,256]{1,0:T(8,128)(2,1)S(1)} %add_convert_fusion.9), channel_id=1, source_target_pairs={{0,2},{2,4},{4,6},{6,7},{7,5},{5,3},{3,1},{1,0},{8,10},{10,12},{12... | collective-permute-start | bytes 393224 | tf_op jit(solution)/shard_map/ppermute | solution.py:33
  65.8 5.0 %collective-permute-start.34 = (bf16[256,256]{1,0:T(8,128)(2,1)S(1)}, bf16[256,256]{1,0:T(8,128)(2,1)S(1)}, u32[]{:S(2)}, u32[]{:S(2)}) collective-permute-start(bf16[256,256]{1,0:T(8,128)(2,1)S(1)} %add_convert_fusion.1), channel_id=1, source_target_pairs={{0,1},{2,0},{4,2},{6,4},{7,6},{5,7},{3,5},{1,3},{8,9},{10,8},{12,1... | collective-permute-start | bytes 393224 | tf_op jit(solution)/shard_map/ppermute | solution.py:33

commit v17 on v16

--- a/solution.py
+++ b/solution.py
@@ -204,7 +204,8 @@
         out_shape=(
             pltpu.VMEM((total, out_width), BF16),
             pltpu.VMEM((total, 2 * out_width), BF16),
-            *[pltpu.VMEM((size, 2 * out_width), BF16) for size in sizes],
+            *[pltpu.HBM((size, 2 * out_width), BF16) for size in sizes[: len(lasts)]],
+            *[pltpu.VMEM((size, 2 * out_width), BF16) for size in sizes[len(lasts) :]],
         ),
         in_specs=[SMEM] + [VMEM] * (2 + len(lasts)),
         out_specs=(VMEM,) * (2 + len(sizes)),
@@ -361,7 +362,8 @@
     numbers = lambda values: jnp.stack(values).astype(jnp.int32)
     at = [index_at(offset) for offset in range(ring)]
 
-    streams, ways = (0, 1), ((0, 1), (1, -1))
+    streams = (0, 1)
+    lanes = ((0, 0, 1), (1, 1, -1), (0, 1, -1), (1, 0, 1))
     farthest = ring // 2
     reach = [(farthest, farthest - 1), (farthest - 1, farthest)]
 
@@ -369,13 +371,12 @@
     held = [[tokens[s * half : (s + 1) * half]] * 2 for s in streams]
     blocks, targets = [], []
     for step in range(1, farthest + 1):
-        for s in streams:
-            for way, sign in ways:
-                if step <= reach[s][way]:
-                    held[s][way] = along(held[s][way], sign, ring)
+        for s, way, sign in lanes:
+            if step <= reach[s][way]:
+                held[s][way] = along(held[s][way], sign, ring)
         if step == 1:
-            held[1][1], (weights, wide) = lax.optimization_barrier(
-                (held[1][1], fold_gain(order, numbers(at), norm_gain, w_qkv, tokens))
+            held[0][0], (weights, wide) = lax.optimization_barrier(
+                (held[0][0], fold_gain(order, numbers(at), norm_gain, w_qkv, tokens))
             )
         elif step == 2:
             wide = placed(targets, blocks, wide)
@@ -386,10 +387,9 @@
             )
             blocks, targets = [], []
         if step < farthest:
-            for s in streams:
-                for way, sign in ways:
-                    blocks.append(held[s][way])
-                    targets.append((s * half, (2 * step - 1 + way) * width))
+            for s, way, sign in lanes:
+                blocks.append(held[s][way])
+                targets.append((s * half, (2 * step - 1 + way) * width))
     wide = placed(targets, blocks, wide)
     lasts = [held[0][0], held[1][1]]
     state = project_begin(wide, weights, ring)
@@ -421,13 +421,15 @@
     parts = [dict(zip(goals[s], parts[s * ring : (s + 1) * ring])) for s in streams]
     sums = [[None, None] for s in streams]
     for step in range(farthest, 0, -1):
-        for s in streams:
-            for way, sign in ways:
-                if step <= reach[s][way]:
-                    part = parts[s][sign * step]
-                    if sums[s][way] is not None:
-                        part = total_of(part, sums[s][way])
-                    sums[s][way] = along(part, sign, ring)
+        for s, way, sign in lanes:
+            if step <= reach[s][way]:
+                part = parts[s][sign * step]
+                if sums[s][way] is not None:
+                    part = total_of(part, sums[s][way])
+                sums[s][way] = along(part, sign, ring)
+    ends = lax.optimization_barrier([sums[s][way] for s, way, sign in lanes[::-1]])
+    for (s, way, sign), end in zip(lanes[::-1], ends):
+        sums[s][way] = end
     return jnp.concatenate([total_of(parts[s][0], *sums[s]) for s in streams])
 
 

time: 72.2 us -> 70.7 us (0.979)
  waiting for transfers between devices: 20.2 us -> 17 us
  starting transfers between devices: 32.2 us -> 33 us
    ppermute x28, waiting for transfers between devices: 17.8 us -> 14.3 us  [along(): lax.ppermute(value, 'head', [(order[p], order[(p + step) % count]) for p...]
    ppermute x28, starting transfers between devices: 29 us -> 29.9 us  [along(): lax.ppermute(value, 'head', [(order[p], order[(p + step) % count]) for p...]
  transfers between devices with their start and end apart: 35 -> 35, of which waited for: 15 -> 14; matrix products, arithmetic and copies ran while one was open for 1% -> 1% of each run, Pallas kernels for 17% -> 17%
where the time goes in v17:
time: 70.7 us; the launch traced here: 69.9 us
  starting transfers between devices  33 us (47%)
  Pallas kernels  17.2 us (24%)
  waiting for transfers between devices  17 us (24%)
  other arithmetic  1.39 us (2%)
  local copies, waits for them, and re-layouts  1.16 us (2%)
    ppermute x28, starting transfers between devices, along(): lax.ppermute(value, 'head', [(order[p], order[(p + step) % count]) for p...  29.9 us
    ppermute x28, waiting for transfers between devices, along(): lax.ppermute(value, 'head', [(order[p], order[(p + step) % count]) for p...  14.3 us
    pallas_call x4, Pallas kernels, attend(): pl.pallas_call(functools.partial(attend_kernel, head_size, (len(blocks),...  9.92 us
    pallas_call x1, Pallas kernels, fold_gain(): pl.pallas_call(functools.partial(fold_kernel, order), out_shape=(pltpu.VM...  3.02 us
    ppermute x2, waiting for transfers between devices, body(): far.append([lax.ppermute(part, 'seq', shift) for part in halves])  2.62 us
    ppermute x2, starting transfers between devices, body(): far.append([lax.ppermute(part, 'seq', shift) for part in halves])  2.03 us
    pallas_call x1, Pallas kernels, project_finish(): pl.pallas_call(functools.partial(finish_kernel, head_size), out_shape=(pl...  2.01 us
    pallas_call x1, Pallas kernels, project_begin(): pl.pallas_call(functools.partial(begin_kernel, blocks), out_shape=pltpu.V...  1.92 us
  transfers between devices with their start and end apart: 35, of which 14 were waited for; matrix products, arithmetic and copies ran while one was open for 1% of the time, Pallas kernels for 17%

profile of v17, /device:TPU:10, one launch (start us, length us, event | category | flops | bytes accessed | tf_op | source)
XLA Modules:
  0.0 69.9 jit_solution(17567560828180443326)
XLA Ops:
  0.0 1.0 %fusion = (bf16[256,256]{1,0:T(8,128)(2,1)S(1)}, bf16[256,256]{1,0:T(8,128)(2,1)S(1)}) fusion(bf16[512,256]{1,0:T(8,128)(2,1)} %tokens.1), kind=kLoop, calls=%fused_computation.16 | loop fusion | bytes 524288 | tf_op jit(solution)/shard_map/slice | solution.py:371
  1.0 0.5 collective-permute-start.3
  1.5 1.6 %collective-permute-start = (bf16[256,256]{1,0:T(8,128)(2,1)S(1)}, bf16[256,256]{1,0:T(8,128)(2,1)S(1)}, u32[]{:S(2)}, u32[]{:S(2)}) collective-permute-start(bf16[256,256]{1,0:T(8,128)(2,1)S(1)} %get-tuple-element.88), channel_id=1, source_target_pairs={{0,2},{2,4},{4,6},{6,7},{7,5},{5,3},{3,1},{1,0},{8,10},{10,12},{12... | collective-permute-start | bytes 393224 | tf_op jit(solution)/shard_map/ppermute | solution.py:33
  3.1 0.4 collective-permute-start.6
  3.5 1.6 %collective-permute-start.8 = (bf16[256,256]{1,0:T(8,128)(2,1)S(1)}, bf16[256,256]{1,0:T(8,128)(2,1)S(1)}, u32[]{:S(2)}, u32[]{:S(2)}) collective-permute-start(bf16[256,256]{1,0:T(8,128)(2,1)S(1)} %get-tuple-element.87), channel_id=1, source_target_pairs={{0,2},{2,4},{4,6},{6,7},{7,5},{5,3},{3,1},{1,0},{8,10},{10,12},{12... | collective-permute-start | bytes 393224 | tf_op jit(solution)/shard_map/ppermute | solution.py:33
  5.2 3.0 %fold_gain.1 = (bf16[3,2048,256]{2,1,0:T(8,128)(2,1)S(1)}, bf16[512,2048]{1,0:T(8,128)(2,1)S(1)}) custom-call(s32[8]{0:T(128)S(1)} %stack.84.at, f32[16,128]{1,0:T(8,128)} %bitcast.19, bf16[3,2048,256]{2,1,0:T(8,128)(2,1)} %w_hbm.1, bf16[512,256]{1,0:T(8,128)(2,1)} %tokens.1), custom_call_target="tpu_custom_call" | custom-call | flops 1572864 | bytes 6291456 | tf_op jit(solution)/shard_map/fold_gain/pallas_call | solution.py:83
  8.2 0.5 collective-permute-start.4
  8.7 1.6 %collective-permute-start.1 = (bf16[256,256]{1,0:T(8,128)(2,1)S(1)}, bf16[256,256]{1,0:T(8,128)(2,1)S(1)}, u32[]{:S(2)}, u32[]{:S(2)}) collective-permute-start(bf16[256,256]{1,0:T(8,128)(2,1)S(1)} %collective-permute-done.refs_0_), channel_id=1, source_target_pairs={{0,2},{2,4},{4,6},{6,7},{7,5},{5,3},{3,1},{1,0},{8,10},{10,12},{12... | collective-permute-start | bytes 393224 | tf_op jit(solution)/shard_map/ppermute | solution.py:33
  10.3 0.5 collective-permute-start.7
  10.8 1.6 %collective-permute-start.9 = (bf16[256,256]{1,0:T(8,128)(2,1)S(1)}, bf16[256,256]{1,0:T(8,128)(2,1)S(1)}, u32[]{:S(2)}, u32[]{:S(2)}) collective-permute-start(bf16[256,256]{1,0:T(8,128)(2,1)S(1)} %collective-permute-done.8.refs_3_), channel_id=1, source_target_pairs={{0,2},{2,4},{4,6},{6,7},{7,5},{5,3},{3,1},{1,0},{8,10},{10,12},{12... | collective-permute-start | bytes 393224 | tf_op jit(solution)/shard_map/ppermute | solution.py:33
  12.3 1.9 %collective-permute-done.4.refs_1_ = bf16[256,256]{1,0:T(8,128)(2,1)S(1)} collective-permute-done((bf16[256,256]{1,0:T(8,128)(2,1)S(1)}, bf16[256,256]{1,0:T(8,128)(2,1)S(1)}, u32[]{:S(2)}, u32[]{:S(2)}) %collective-permute-start.4) | collective-permute-done | bytes 131104 | tf_op jit(solution)/shard_map/ppermute | solution.py:33
  14.7 1.6 %collective-permute-start.2 = (bf16[256,256]{1,0:T(8,128)(2,1)S(1)}, bf16[256,256]{1,0:T(8,128)(2,1)S(1)}, u32[]{:S(2)}, u32[]{:S(2)}) collective-permute-start(bf16[256,256]{1,0:T(8,128)(2,1)S(1)} %collective-permute-done.1.refs_0_), channel_id=1, source_target_pairs={{0,2},{2,4},{4,6},{6,7},{7,5},{5,3},{3,1},{1,0},{8,10},{10,12},{12... | collective-permute-start | bytes 393224 | tf_op jit(solution)/shard_map/ppermute | solution.py:33
  16.3 0.8 %collective-permute-done.7.refs_2_ = bf16[256,256]{1,0:T(8,128)(2,1)S(1)} collective-permute-done((bf16[256,256]{1,0:T(8,128)(2,1)S(1)}, bf16[256,256]{1,0:T(8,128)(2,1)S(1)}, u32[]{:S(2)}, u32[]{:S(2)}) %collective-permute-start.7) | collective-permute-done | bytes 131104 | tf_op jit(solution)/shard_map/ppermute | solution.py:33
  17.1 0.4 collective-permute-start.10
  17.5 1.6 %collective-permute-start.11 = (bf16[256,256]{1,0:T(8,128)(2,1)S(1)}, bf16[256,256]{1,0:T(8,128)(2,1)S(1)}, u32[]{:S(2)}, u32[]{:S(2)}) collective-permute-start(bf16[256,256]{1,0:T(8,128)(2,1)S(1)} %collective-permute-done.9.refs_3_), channel_id=1, source_target_pairs={{0,2},{2,4},{4,6},{6,7},{7,5},{5,3},{3,1},{1,0},{8,10},{10,12},{12... | collective-permute-start | bytes 393224 | tf_op jit(solution)/shard_map/ppermute | solution.py:33
  19.3 0.6 collective-permute-done.5.refs_1_
  20.4 1.6 %collective-permute-start.12 = (bf16[256,256]{1,0:T(8,128)(2,1)S(1)}, bf16[256,256]{1,0:T(8,128)(2,1)S(1)}, u32[]{:S(2)}, u32[]{:S(2)}) collective-permute-start(bf16[256,256]{1,0:T(8,128)(2,1)S(1)} %collective-permute-done.2.refs_0_), channel_id=1, source_target_pairs={{0,2},{2,4},{4,6},{6,7},{7,5},{5,3},{3,1},{1,0},{8,10},{10,12},{12... | collective-permute-start | bytes 393224 | tf_op jit(solution)/shard_map/ppermute | solution.py:33
  22.6 1.9 %project_begin.1.state = f32[512,896]{1,0:T(8,128)S(1)} custom-call(bf16[512,2048]{1,0:T(8,128)(2,1)S(1)} %place.5.wide, bf16[3,2048,256]{2,1,0:T(8,128)(2,1)S(1)} %get-tuple-element.52.w_ref), custom_call_target="tpu_custom_call" | custom-call | flops 1610612736 | bytes 5242880 | tf_op jit(solution)/shard_map/project_begin/pallas_call | solution.py:180
  24.9 0.5 collective-permute-done.12.refs_0_
  25.4 2.0 %project_finish.1 = (bf16[512,256]{1,0:T(8,128)(2,1)S(1)}, bf16[512,512]{1,0:T(8,128)(2,1)S(1)}, bf16[256,512]{1,0:T(8,128)(2,1)}, bf16[256,512]{1,0:T(8,128)(2,...) custom-call(f32[2]{0:T(128)} %factor.1, ...), custom_call_target="tpu_custom_call" | custom-call | flops 201326592 | bytes 1048576 | tf_op jit(solution)/shard_map/project_finish/pallas_call | solution.py:202
  27.4 0.5 collective-permute-start.17
  27.9 1.6 %collective-permute-start.18 = (bf16[256,512]{1,0:T(8,128)(2,1)}, bf16[256,512]{1,0:T(8,128)(2,1)S(1)}, u32[]{:S(2)}, u32[]{:S(2)}) collective-permute-start(bf16[256,512]{1,0:T(8,128)(2,1)} %get-tuple-element.63), channel_id=1, source_target_pairs={{0,16},{8,24},{16,0},{24,8},{1,17},{9,25},{17,1},{25,9},{2,18},{10... | collective-permute-start | bytes 786440 | tf_op jit(solution)/shard_map/ppermute | solution.py:406
  29.4 0.5 collective-permute-start.16
  30.1 2.2 %attend.3.refs_3_ = f32[512,512]{1,0:T(8,128)S(1)} custom-call(s32[2]{0:T(128)S(1)} %pad_add_fusion.1.info, s32[2048]{0:T(1024)} %ids.7, bf16[512,256]{1,0:T(8,128)(2,1)S(1)} %get-tuple-element.53.q_ref, s32[8,1,256]{2,1,0:T(1,128)} %bitcast.15, bf16[512,512]{1,0:T(8,128)(2,1)S(1)} %get-tuple-element.54.refs_0_), custom_call_target="tpu_custom_call" | custom-call | flops 1048576 | bytes 1024 | tf_op jit(solution)/shard_map/attend/pallas_call | solution.py:332
  32.4 2.2 %attend.4.refs_2_ = f32[512,512]{1,0:T(8,128)S(1)} custom-call(s32[2]{0:T(128)S(1)} %pad_add_fusion.info, s32[2048]{0:T(1024)} %ids.7, bf16[512,256]{1,0:T(8,128)(2,1)S(1)} %get-tuple-element.53.q_ref, s32[8,1,256]{2,1,0:T(1,128)} %bitcast.16, bf16[160,512]{1,0:T(8,128)(2,1)S(1)} %collective-permute-done.14.refs_0_, ...), custom_call_target="tpu_custom_call" | custom-call | flops 1048576 | bytes 1024 | tf_op jit(solution)/shard_map/attend/pallas_call | solution.py:332
  34.6 2.6 %collective-permute-done.18.refs_1_ = bf16[256,512]{1,0:T(8,128)(2,1)S(1)} collective-permute-done((bf16[256,512]{1,0:T(8,128)(2,1)}, bf16[256,512]{1,0:T(8,128)(2,1)S(1)}, u32[]{:S(2)}, u32[]{:S(2)}) %collective-permute-start.18) | collective-permute-done | bytes 262176 | tf_op jit(solution)/shard_map/ppermute | solution.py:406
  37.2 0.5 collective-permute-start.20
  37.9 2.1 %attend.5.refs_2_ = f32[512,512]{1,0:T(8,128)S(1)} custom-call(s32[2]{0:T(128)S(1)} %pad_add_fusion.2.info, s32[2048]{0:T(1024)} %ids.7, bf16[512,256]{1,0:T(8,128)(2,1)S(1)} %get-tuple-element.53.q_ref, s32[8,1,256]{2,1,0:T(1,128)} %bitcast.17, bf16[256,512]{1,0:T(8,128)(2,1)S(1)} %collective-permute-done.17.refs_0_, ...), custom_call_target="tpu_custom_call" | custom-call | flops 1048576 | bytes 1024 | tf_op jit(solution)/shard_map/attend/pallas_call | solution.py:332
  40.1 3.3 %attend_last.1 = (bf16[256,256]{1,0:T(8,128)(2,1)S(1)}, bf16[256,256]{1,0:T(8,128)(2,1)S(1)}, bf16[256,256]{1,0:T(8,128)(2,1)S(1)}, bf16[256,256]{1,0:T(8,128)(2...) custom-call(s32[18]{0:T(128)S(1)} %stack.83.info, ...), custom_call_target="tpu_custom_call" | custom-call | flops 1048576 | bytes 1024 | tf_op jit(solution)/shard_map/attend_last/pallas_call | solution.py:332
  43.4 1.6 %collective-permute-start.31 = (bf16[256,256]{1,0:T(8,128)(2,1)S(1)}, bf16[256,256]{1,0:T(8,128)(2,1)S(1)}, u32[]{:S(2)}, u32[]{:S(2)}) collective-permute-start(bf16[256,256]{1,0:T(8,128)(2,1)S(1)} %get-tuple-element.81), channel_id=1, source_target_pairs={{0,2},{2,4},{4,6},{6,7},{7,5},{5,3},{3,1},{1,0},{8,10},{10,12},{12... | collective-permute-start | bytes 393224 | tf_op jit(solution)/shard_map/ppermute | solution.py:33
  45.5 1.5 %collective-permute-start.24 = (bf16[256,256]{1,0:T(8,128)(2,1)S(1)}, bf16[256,256]{1,0:T(8,128)(2,1)S(1)}, u32[]{:S(2)}, u32[]{:S(2)}) collective-permute-start(bf16[256,256]{1,0:T(8,128)(2,1)S(1)} %get-tuple-element.73), channel_id=1, source_target_pairs={{0,1},{2,0},{4,2},{6,4},{7,6},{5,7},{3,5},{1,3},{8,9},{10,8},{12,1... | collective-permute-start | bytes 393224 | tf_op jit(solution)/shard_map/ppermute | solution.py:33
  47.0 0.5 collective-permute-start.21
  47.5 1.4 %collective-permute-done.31 = bf16[256,256]{1,0:T(8,128)(2,1)S(1)} collective-permute-done((bf16[256,256]{1,0:T(8,128)(2,1)S(1)}, bf16[256,256]{1,0:T(8,128)(2,1)S(1)}, u32[]{:S(2)}, u32[]{:S(2)}) %collective-permute-start.31) | collective-permute-done | bytes 131104 | tf_op jit(solution)/shard_map/ppermute | solution.py:33
  48.9 2.5 %collective-permute-start.32 = (bf16[256,256]{1,0:T(8,128)(2,1)S(1)}, bf16[256,256]{1,0:T(8,128)(2,1)S(1)}, u32[]{:S(2)}, u32[]{:S(2)}) collective-permute-start(bf16[256,256]{1,0:T(8,128)(2,1)S(1)} %add_convert_fusion.4), channel_id=1, source_target_pairs={{0,2},{2,4},{4,6},{6,7},{7,5},{5,3},{3,1},{1,0},{8,10},{10,12},{12... | collective-permute-start | bytes 393224 | tf_op jit(solution)/shard_map/ppermute | solution.py:33
  51.5 0.5 collective-permute-start.28
  52.0 1.8 %collective-permute-done.24 = bf16[256,256]{1,0:T(8,128)(2,1)S(1)} collective-permute-done((bf16[256,256]{1,0:T(8,128)(2,1)S(1)}, bf16[256,256]{1,0:T(8,128)(2,1)S(1)}, u32[]{:S(2)}, u32[]{:S(2)}) %collective-permute-start.24) | collective-permute-done | bytes 131104 | tf_op jit(solution)/shard_map/ppermute | solution.py:33
  53.8 0.5 collective-permute-start.25
  54.3 1.6 %collective-permute-start.22 = (bf16[256,256]{1,0:T(8,128)(2,1)S(1)}, bf16[256,256]{1,0:T(8,128)(2,1)S(1)}, u32[]{:S(2)}, u32[]{:S(2)}) collective-permute-start(bf16[256,256]{1,0:T(8,128)(2,1)S(1)} %add_convert_fusion.11), channel_id=1, source_target_pairs={{0,2},{2,4},{4,6},{6,7},{7,5},{5,3},{3,1},{1,0},{8,10},{10,12},{12... | collective-permute-start | bytes 393224 | tf_op jit(solution)/shard_map/ppermute | solution.py:33
  56.0 1.6 %collective-permute-start.33 = (bf16[256,256]{1,0:T(8,128)(2,1)S(1)}, bf16[256,256]{1,0:T(8,128)(2,1)S(1)}, u32[]{:S(2)}, u32[]{:S(2)}) collective-permute-start(bf16[256,256]{1,0:T(8,128)(2,1)S(1)} %add_convert_fusion.3), channel_id=1, source_target_pairs={{0,2},{2,4},{4,6},{6,7},{7,5},{5,3},{3,1},{1,0},{8,10},{10,12},{12... | collective-permute-start | bytes 393224 | tf_op jit(solution)/shard_map/ppermute | solution.py:33
  57.7 0.5 collective-permute-start.29
  58.2 1.9 %collective-permute-done.25 = bf16[256,256]{1,0:T(8,128)(2,1)S(1)} collective-permute-done((bf16[256,256]{1,0:T(8,128)(2,1)S(1)}, bf16[256,256]{1,0:T(8,128)(2,1)S(1)}, u32[]{:S(2)}, u32[]{:S(2)}) %collective-permute-start.25) | collective-permute-done | bytes 131104 | tf_op jit(solution)/shard_map/ppermute | solution.py:33
  60.6 1.8 %collective-permute-start.23 = (bf16[256,256]{1,0:T(8,128)(2,1)S(1)}, bf16[256,256]{1,0:T(8,128)(2,1)S(1)}, u32[]{:S(2)}, u32[]{:S(2)}) collective-permute-start(bf16[256,256]{1,0:T(8,128)(2,1)S(1)} %add_convert_fusion.10), channel_id=1, source_target_pairs={{0,2},{2,4},{4,6},{6,7},{7,5},{5,3},{3,1},{1,0},{8,10},{10,12},{12... | collective-permute-start | bytes 393224 | tf_op jit(solution)/shard_map/ppermute | solution.py:33
  62.4 1.6 %collective-permute-start.34 = (bf16[256,256]{1,0:T(8,128)(2,1)S(1)}, bf16[256,256]{1,0:T(8,128)(2,1)S(1)}, u32[]{:S(2)}, u32[]{:S(2)}) collective-permute-start(bf16[256,256]{1,0:T(8,128)(2,1)S(1)} %add_convert_fusion.2), channel_id=1, source_target_pairs={{0,2},{2,4},{4,6},{6,7},{7,5},{5,3},{3,1},{1,0},{8,10},{10,12},{12... | collective-permute-start | bytes 393224 | tf_op jit(solution)/shard_map/ppermute | solution.py:33
  64.0 0.5 collective-permute-start.30
  64.5 1.3 %collective-permute-done.26 = bf16[256,256]{1,0:T(8,128)(2,1)S(1)} collective-permute-done((bf16[256,256]{1,0:T(8,128)(2,1)S(1)}, bf16[256,256]{1,0:T(8,128)(2,1)S(1)}, u32[]{:S(2)}, u32[]{:S(2)}) %collective-permute-start.26) | collective-permute-done | bytes 131104 | tf_op jit(solution)/shard_map/ppermute | solution.py:33
  65.9 1.5 %collective-permute-done.34 = bf16[256,256]{1,0:T(8,128)(2,1)S(1)} collective-permute-done((bf16[256,256]{1,0:T(8,128)(2,1)S(1)}, bf16[256,256]{1,0:T(8,128)(2,1)S(1)}, u32[]{:S(2)}, u32[]{:S(2)}) %collective-permute-start.34) | collective-permute-done | bytes 131104 | tf_op jit(solution)/shard_map/ppermute | solution.py:33
  67.4 1.7 %collective-permute-done.30 = bf16[256,256]{1,0:T(8,128)(2,1)S(1)} collective-permute-done((bf16[256,256]{1,0:T(8,128)(2,1)S(1)}, bf16[256,256]{1,0:T(8,128)(2,1)S(1)}, u32[]{:S(2)}, u32[]{:S(2)}) %collective-permute-start.30) | collective-permute-done | bytes 131104 | tf_op jit(solution)/shard_map/ppermute | solution.py:33
  69.2 0.7 %pad_maximum_fusion = bf16[512,256]{1,0:T(8,128)(2,1)} fusion(bf16[256,256]{1,0:T(8,128)(2,1)S(1)} %get-tuple-element.89, bf16[256,256]{1,0:T(8,128)(2,1)S(1)} %get-tuple-element.90), kind=kLoop, calls=%fused_computation | loop fusion | flops 524288 | bytes 524288 | tf_op jit(solution)/shard_map/concatenate | solution.py:433
  (50 shorter events, 3.8 us)
Async XLA Ops:
  1.0 7.2 %collective-permute-start.3 = (bf16[256,256]{1,0:T(8,128)(2,1)S(1)}, bf16[256,256]{1,0:T(8,128)(2,1)S(1)}, u32[]{:S(2)}, u32[]{:S(2)}) collective-permute-start(bf16[256,256]{1,0:T(8,128)(2,1)S(1)} %get-tuple-element.87), channel_id=1, source_target_pairs={{0,1},{2,0},{4,2},{6,4},{7,6},{5,7},{3,5},{1,3},{8,9},{10,8},{12,1... | collective-permute-start | bytes 393224 | tf_op jit(solution)/shard_map/ppermute | solution.py:33
  1.5 7.2 %collective-permute-start = (bf16[256,256]{1,0:T(8,128)(2,1)S(1)}, bf16[256,256]{1,0:T(8,128)(2,1)S(1)}, u32[]{:S(2)}, u32[]{:S(2)}) collective-permute-start(bf16[256,256]{1,0:T(8,128)(2,1)S(1)} %get-tuple-element.88), channel_id=1, source_target_pairs={{0,2},{2,4},{4,6},{6,7},{7,5},{5,3},{3,1},{1,0},{8,10},{10,12},{12... | collective-permute-start | bytes 393224 | tf_op jit(solution)/shard_map/ppermute | solution.py:33
  3.1 7.2 %collective-permute-start.6 = (bf16[256,256]{1,0:T(8,128)(2,1)S(1)}, bf16[256,256]{1,0:T(8,128)(2,1)S(1)}, u32[]{:S(2)}, u32[]{:S(2)}) collective-permute-start(bf16[256,256]{1,0:T(8,128)(2,1)S(1)} %get-tuple-element.88), channel_id=1, source_target_pairs={{0,1},{2,0},{4,2},{6,4},{7,6},{5,7},{3,5},{1,3},{8,9},{10,8},{12,1... | collective-permute-start | bytes 393224 | tf_op jit(solution)/shard_map/ppermute | solution.py:33
  3.5 7.2 %collective-permute-start.8 = (bf16[256,256]{1,0:T(8,128)(2,1)S(1)}, bf16[256,256]{1,0:T(8,128)(2,1)S(1)}, u32[]{:S(2)}, u32[]{:S(2)}) collective-permute-start(bf16[256,256]{1,0:T(8,128)(2,1)S(1)} %get-tuple-element.87), channel_id=1, source_target_pairs={{0,2},{2,4},{4,6},{6,7},{7,5},{5,3},{3,1},{1,0},{8,10},{10,12},{12... | collective-permute-start | bytes 393224 | tf_op jit(solution)/shard_map/ppermute | solution.py:33
  8.2 6.0 %collective-permute-start.4 = (bf16[256,256]{1,0:T(8,128)(2,1)S(1)}, bf16[256,256]{1,0:T(8,128)(2,1)S(1)}, u32[]{:S(2)}, u32[]{:S(2)}) collective-permute-start(bf16[256,256]{1,0:T(8,128)(2,1)S(1)} %collective-permute-done.3.refs_1_), channel_id=1, source_target_pairs={{0,1},{2,0},{4,2},{6,4},{7,6},{5,7},{3,5},{1,3},{8,9},{10,8},{12,1... | collective-permute-start | bytes 393224 | tf_op jit(solution)/shard_map/ppermute | solution.py:33
  8.7 6.0 %collective-permute-start.1 = (bf16[256,256]{1,0:T(8,128)(2,1)S(1)}, bf16[256,256]{1,0:T(8,128)(2,1)S(1)}, u32[]{:S(2)}, u32[]{:S(2)}) collective-permute-start(bf16[256,256]{1,0:T(8,128)(2,1)S(1)} %collective-permute-done.refs_0_), channel_id=1, source_target_pairs={{0,2},{2,4},{4,6},{6,7},{7,5},{5,3},{3,1},{1,0},{8,10},{10,12},{12... | collective-permute-start | bytes 393224 | tf_op jit(solution)/shard_map/ppermute | solution.py:33
  10.3 6.8 %collective-permute-start.7 = (bf16[256,256]{1,0:T(8,128)(2,1)S(1)}, bf16[256,256]{1,0:T(8,128)(2,1)S(1)}, u32[]{:S(2)}, u32[]{:S(2)}) collective-permute-start(bf16[256,256]{1,0:T(8,128)(2,1)S(1)} %collective-permute-done.6.refs_2_), channel_id=1, source_target_pairs={{0,1},{2,0},{4,2},{6,4},{7,6},{5,7},{3,5},{1,3},{8,9},{10,8},{12,1... | collective-permute-start | bytes 393224 | tf_op jit(solution)/shard_map/ppermute | solution.py:33
  10.8 6.8 %collective-permute-start.9 = (bf16[256,256]{1,0:T(8,128)(2,1)S(1)}, bf16[256,256]{1,0:T(8,128)(2,1)S(1)}, u32[]{:S(2)}, u32[]{:S(2)}) collective-permute-start(bf16[256,256]{1,0:T(8,128)(2,1)S(1)} %collective-permute-done.8.refs_3_), channel_id=1, source_target_pairs={{0,2},{2,4},{4,6},{6,7},{7,5},{5,3},{3,1},{1,0},{8,10},{10,12},{12... | collective-permute-start | bytes 393224 | tf_op jit(solution)/shard_map/ppermute | solution.py:33
  14.3 5.7 %collective-permute-start.5 = (bf16[256,256]{1,0:T(8,128)(2,1)S(1)}, bf16[256,256]{1,0:T(8,128)(2,1)S(1)}, u32[]{:S(2)}, u32[]{:S(2)}) collective-permute-start(bf16[256,256]{1,0:T(8,128)(2,1)S(1)} %collective-permute-done.4.refs_1_), channel_id=1, source_target_pairs={{0,1},{2,0},{4,2},{6,4},{7,6},{5,7},{3,5},{1,3},{8,9},{10,8},{12,1... | collective-permute-start | bytes 393224 | tf_op jit(solution)/shard_map/ppermute | solution.py:33
  14.7 5.7 %collective-permute-start.2 = (bf16[256,256]{1,0:T(8,128)(2,1)S(1)}, bf16[256,256]{1,0:T(8,128)(2,1)S(1)}, u32[]{:S(2)}, u32[]{:S(2)}) collective-permute-start(bf16[256,256]{1,0:T(8,128)(2,1)S(1)} %collective-permute-done.1.refs_0_), channel_id=1, source_target_pairs={{0,2},{2,4},{4,6},{6,7},{7,5},{5,3},{3,1},{1,0},{8,10},{10,12},{12... | collective-permute-start | bytes 393224 | tf_op jit(solution)/shard_map/ppermute | solution.py:33
  17.1 5.2 %collective-permute-start.10 = (bf16[256,256]{1,0:T(8,128)(2,1)S(1)}, bf16[256,256]{1,0:T(8,128)(2,1)S(1)}, u32[]{:S(2)}, u32[]{:S(2)}) collective-permute-start(bf16[256,256]{1,0:T(8,128)(2,1)S(1)} %collective-permute-done.7.refs_2_), channel_id=1, source_target_pairs={{0,1},{2,0},{4,2},{6,4},{7,6},{5,7},{3,5},{1,3},{8,9},{10,8},{12,1... | collective-permute-start | bytes 393224 | tf_op jit(solution)/shard_map/ppermute | solution.py:33
  17.5 5.0 %collective-permute-start.11 = (bf16[256,256]{1,0:T(8,128)(2,1)S(1)}, bf16[256,256]{1,0:T(8,128)(2,1)S(1)}, u32[]{:S(2)}, u32[]{:S(2)}) collective-permute-start(bf16[256,256]{1,0:T(8,128)(2,1)S(1)} %collective-permute-done.9.refs_3_), channel_id=1, source_target_pairs={{0,2},{2,4},{4,6},{6,7},{7,5},{5,3},{3,1},{1,0},{8,10},{10,12},{12... | collective-permute-start | bytes 393224 | tf_op jit(solution)/shard_map/ppermute | solution.py:33
  20.0 5.0 %collective-permute-start.13 = (bf16[256,256]{1,0:T(8,128)(2,1)S(1)}, bf16[256,256]{1,0:T(8,128)(2,1)S(1)}, u32[]{:S(2)}, u32[]{:S(2)}) collective-permute-start(bf16[256,256]{1,0:T(8,128)(2,1)S(1)} %collective-permute-done.5.refs_1_), channel_id=1, source_target_pairs={{0,1},{2,0},{4,2},{6,4},{7,6},{5,7},{3,5},{1,3},{8,9},{10,8},{12,1... | collective-permute-start | bytes 393224 | tf_op jit(solution)/shard_map/ppermute | solution.py:33
  20.4 5.0 %collective-permute-start.12 = (bf16[256,256]{1,0:T(8,128)(2,1)S(1)}, bf16[256,256]{1,0:T(8,128)(2,1)S(1)}, u32[]{:S(2)}, u32[]{:S(2)}) collective-permute-start(bf16[256,256]{1,0:T(8,128)(2,1)S(1)} %collective-permute-done.2.refs_0_), channel_id=1, source_target_pairs={{0,2},{2,4},{4,6},{6,7},{7,5},{5,3},{3,1},{1,0},{8,10},{10,12},{12... | collective-permute-start | bytes 393224 | tf_op jit(solution)/shard_map/ppermute | solution.py:33
  27.4 7.2 %collective-permute-start.17 = (bf16[256,512]{1,0:T(8,128)(2,1)}, bf16[256,512]{1,0:T(8,128)(2,1)S(1)}, u32[]{:S(2)}, u32[]{:S(2)}) collective-permute-start(bf16[256,512]{1,0:T(8,128)(2,1)} %get-tuple-element.62), channel_id=1, source_target_pairs={{0,16},{8,24},{16,0},{24,8},{1,17},{9,25},{17,1},{25,9},{2,18},{10... | collective-permute-start | bytes 786440 | tf_op jit(solution)/shard_map/ppermute | solution.py:406
  27.9 9.4 %collective-permute-start.18 = (bf16[256,512]{1,0:T(8,128)(2,1)}, bf16[256,512]{1,0:T(8,128)(2,1)S(1)}, u32[]{:S(2)}, u32[]{:S(2)}) collective-permute-start(bf16[256,512]{1,0:T(8,128)(2,1)} %get-tuple-element.63), channel_id=1, source_target_pairs={{0,16},{8,24},{16,0},{24,8},{1,17},{9,25},{17,1},{25,9},{2,18},{10... | collective-permute-start | bytes 786440 | tf_op jit(solution)/shard_map/ppermute | solution.py:406
  29.4 2.9 %collective-permute-start.15 = (bf16[176,512]{1,0:T(8,128)(2,1)S(1)}, bf16[176,512]{1,0:T(8,128)(2,1)S(1)}, u32[]{:S(2)}, u32[]{:S(2)}) collective-permute-start(bf16[176,512]{1,0:T(8,128)(2,1)S(1)} %get-tuple-element.56), channel_id=1, source_target_pairs={{0,8},{8,0},{16,24},{24,16},{1,9},{9,1},{17,25},{25,17},{2,10},{10... | collective-permute-start | bytes 540680 | tf_op jit(solution)/shard_map/ppermute | solution.py:39
  29.4 2.9 %collective-permute-start.16 = (bf16[176,512]{1,0:T(8,128)(2,1)S(1)}, bf16[176,512]{1,0:T(8,128)(2,1)S(1)}, u32[]{:S(2)}, u32[]{:S(2)}) collective-permute-start(bf16[176,512]{1,0:T(8,128)(2,1)S(1)} %get-tuple-element.57), channel_id=1, source_target_pairs={{0,8},{8,0},{16,24},{24,16},{1,9},{9,1},{17,25},{25,17},{2,10},{10... | collective-permute-start | bytes 540680 | tf_op jit(solution)/shard_map/ppermute | solution.py:39
  29.9 2.4 %collective-permute-start.14 = (bf16[160,512]{1,0:T(8,128)(2,1)S(1)}, bf16[160,512]{1,0:T(8,128)(2,1)S(1)}, u32[]{:S(2)}, u32[]{:S(2)}) collective-permute-start(bf16[160,512]{1,0:T(8,128)(2,1)S(1)} %get-tuple-element.55), channel_id=1, source_target_pairs={{0,8},{8,0},{16,24},{24,16},{1,9},{9,1},{17,25},{25,17},{2,10},{10... | collective-permute-start | bytes 491528 | tf_op jit(solution)/shard_map/ppermute | solution.py:39
  37.2 2.8 %collective-permute-start.19 = (bf16[256,512]{1,0:T(8,128)(2,1)S(1)}, bf16[256,512]{1,0:T(8,128)(2,1)S(1)}, u32[]{:S(2)}, u32[]{:S(2)}) collective-permute-start(bf16[256,512]{1,0:T(8,128)(2,1)S(1)} %collective-permute-done.17.refs_0_), channel_id=1, source_target_pairs={{0,8},{8,0},{16,24},{24,16},{1,9},{9,1},{17,25},{25,17},{2,10},{10... | collective-permute-start | bytes 786440 | tf_op jit(solution)/shard_map/ppermute | solution.py:39
  37.2 2.8 %collective-permute-start.20 = (bf16[256,512]{1,0:T(8,128)(2,1)S(1)}, bf16[256,512]{1,0:T(8,128)(2,1)S(1)}, u32[]{:S(2)}, u32[]{:S(2)}) collective-permute-start(bf16[256,512]{1,0:T(8,128)(2,1)S(1)} %collective-permute-done.18.refs_1_), channel_id=1, source_target_pairs={{0,8},{8,0},{16,24},{24,16},{1,9},{9,1},{17,25},{25,17},{2,10},{10... | collective-permute-start | bytes 786440 | tf_op jit(solution)/shard_map/ppermute | solution.py:39
  43.4 5.5 %collective-permute-start.31 = (bf16[256,256]{1,0:T(8,128)(2,1)S(1)}, bf16[256,256]{1,0:T(8,128)(2,1)S(1)}, u32[]{:S(2)}, u32[]{:S(2)}) collective-permute-start(bf16[256,256]{1,0:T(8,128)(2,1)S(1)} %get-tuple-element.81), channel_id=1, source_target_pairs={{0,2},{2,4},{4,6},{6,7},{7,5},{5,3},{3,1},{1,0},{8,10},{10,12},{12... | collective-permute-start | bytes 393224 | tf_op jit(solution)/shard_map/ppermute | solution.py:33
  45.0 6.5 %collective-permute-start.27 = (bf16[256,256]{1,0:T(8,128)(2,1)S(1)}, bf16[256,256]{1,0:T(8,128)(2,1)S(1)}, u32[]{:S(2)}, u32[]{:S(2)}) collective-permute-start(bf16[256,256]{1,0:T(8,128)(2,1)S(1)} %get-tuple-element.77), channel_id=1, source_target_pairs={{0,1},{2,0},{4,2},{6,4},{7,6},{5,7},{3,5},{1,3},{8,9},{10,8},{12,1... | collective-permute-start | bytes 393224 | tf_op jit(solution)/shard_map/ppermute | solution.py:33
  45.5 8.3 %collective-permute-start.24 = (bf16[256,256]{1,0:T(8,128)(2,1)S(1)}, bf16[256,256]{1,0:T(8,128)(2,1)S(1)}, u32[]{:S(2)}, u32[]{:S(2)}) collective-permute-start(bf16[256,256]{1,0:T(8,128)(2,1)S(1)} %get-tuple-element.73), channel_id=1, source_target_pairs={{0,1},{2,0},{4,2},{6,4},{7,6},{5,7},{3,5},{1,3},{8,9},{10,8},{12,1... | collective-permute-start | bytes 393224 | tf_op jit(solution)/shard_map/ppermute | solution.py:33
  47.0 7.3 %collective-permute-start.21 = (bf16[256,256]{1,0:T(8,128)(2,1)S(1)}, bf16[256,256]{1,0:T(8,128)(2,1)S(1)}, u32[]{:S(2)}, u32[]{:S(2)}) collective-permute-start(bf16[256,256]{1,0:T(8,128)(2,1)S(1)} %get-tuple-element.70), channel_id=1, source_target_pairs={{0,2},{2,4},{4,6},{6,7},{7,5},{5,3},{3,1},{1,0},{8,10},{10,12},{12... | collective-permute-start | bytes 393224 | tf_op jit(solution)/shard_map/ppermute | solution.py:33
  48.9 7.0 %collective-permute-start.32 = (bf16[256,256]{1,0:T(8,128)(2,1)S(1)}, bf16[256,256]{1,0:T(8,128)(2,1)S(1)}, u32[]{:S(2)}, u32[]{:S(2)}) collective-permute-start(bf16[256,256]{1,0:T(8,128)(2,1)S(1)} %add_convert_fusion.4), channel_id=1, source_target_pairs={{0,2},{2,4},{4,6},{6,7},{7,5},{5,3},{3,1},{1,0},{8,10},{10,12},{12... | collective-permute-start | bytes 393224 | tf_op jit(solution)/shard_map/ppermute | solution.py:33
  51.5 6.1 %collective-permute-start.28 = (bf16[256,256]{1,0:T(8,128)(2,1)S(1)}, bf16[256,256]{1,0:T(8,128)(2,1)S(1)}, u32[]{:S(2)}, u32[]{:S(2)}) collective-permute-start(bf16[256,256]{1,0:T(8,128)(2,1)S(1)} %add_convert_fusion.7), channel_id=1, source_target_pairs={{0,1},{2,0},{4,2},{6,4},{7,6},{5,7},{3,5},{1,3},{8,9},{10,8},{12,1... | collective-permute-start | bytes 393224 | tf_op jit(solution)/shard_map/ppermute | solution.py:33
  53.8 6.3 %collective-permute-start.25 = (bf16[256,256]{1,0:T(8,128)(2,1)S(1)}, bf16[256,256]{1,0:T(8,128)(2,1)S(1)}, u32[]{:S(2)}, u32[]{:S(2)}) collective-permute-start(bf16[256,256]{1,0:T(8,128)(2,1)S(1)} %add_convert_fusion.9), channel_id=1, source_target_pairs={{0,1},{2,0},{4,2},{6,4},{7,6},{5,7},{3,5},{1,3},{8,9},{10,8},{12,1... | collective-permute-start | bytes 393224 | tf_op jit(solution)/shard_map/ppermute | solution.py:33
  54.3 6.2 %collective-permute-start.22 = (bf16[256,256]{1,0:T(8,128)(2,1)S(1)}, bf16[256,256]{1,0:T(8,128)(2,1)S(1)}, u32[]{:S(2)}, u32[]{:S(2)}) collective-permute-start(bf16[256,256]{1,0:T(8,128)(2,1)S(1)} %add_convert_fusion.11), channel_id=1, source_target_pairs={{0,2},{2,4},{4,6},{6,7},{7,5},{5,3},{3,1},{1,0},{8,10},{10,12},{12... | collective-permute-start | bytes 393224 | tf_op jit(solution)/shard_map/ppermute | solution.py:33
  56.0 6.3 %collective-permute-start.33 = (bf16[256,256]{1,0:T(8,128)(2,1)S(1)}, bf16[256,256]{1,0:T(8,128)(2,1)S(1)}, u32[]{:S(2)}, u32[]{:S(2)}) collective-permute-start(bf16[256,256]{1,0:T(8,128)(2,1)S(1)} %add_convert_fusion.3), channel_id=1, source_target_pairs={{0,2},{2,4},{4,6},{6,7},{7,5},{5,3},{3,1},{1,0},{8,10},{10,12},{12... | collective-permute-start | bytes 393224 | tf_op jit(solution)/shard_map/ppermute | solution.py:33
  57.7 6.3 %collective-permute-start.29 = (bf16[256,256]{1,0:T(8,128)(2,1)S(1)}, bf16[256,256]{1,0:T(8,128)(2,1)S(1)}, u32[]{:S(2)}, u32[]{:S(2)}) collective-permute-start(bf16[256,256]{1,0:T(8,128)(2,1)S(1)} %add_convert_fusion.6), channel_id=1, source_target_pairs={{0,1},{2,0},{4,2},{6,4},{7,6},{5,7},{3,5},{1,3},{8,9},{10,8},{12,1... | collective-permute-start | bytes 393224 | tf_op jit(solution)/shard_map/ppermute | solution.py:33
  60.2 5.7 %collective-permute-start.26 = (bf16[256,256]{1,0:T(8,128)(2,1)S(1)}, bf16[256,256]{1,0:T(8,128)(2,1)S(1)}, u32[]{:S(2)}, u32[]{:S(2)}) collective-permute-start(bf16[256,256]{1,0:T(8,128)(2,1)S(1)} %add_convert_fusion.8), channel_id=1, source_target_pairs={{0,1},{2,0},{4,2},{6,4},{7,6},{5,7},{3,5},{1,3},{8,9},{10,8},{12,1... | collective-permute-start | bytes 393224 | tf_op jit(solution)/shard_map/ppermute | solution.py:33
  60.6 5.3 %collective-permute-start.23 = (bf16[256,256]{1,0:T(8,128)(2,1)S(1)}, bf16[256,256]{1,0:T(8,128)(2,1)S(1)}, u32[]{:S(2)}, u32[]{:S(2)}) collective-permute-start(bf16[256,256]{1,0:T(8,128)(2,1)S(1)} %add_convert_fusion.10), channel_id=1, source_target_pairs={{0,2},{2,4},{4,6},{6,7},{7,5},{5,3},{3,1},{1,0},{8,10},{10,12},{12... | collective-permute-start | bytes 393224 | tf_op jit(solution)/shard_map/ppermute | solution.py:33
  62.4 5.0 %collective-permute-start.34 = (bf16[256,256]{1,0:T(8,128)(2,1)S(1)}, bf16[256,256]{1,0:T(8,128)(2,1)S(1)}, u32[]{:S(2)}, u32[]{:S(2)}) collective-permute-start(bf16[256,256]{1,0:T(8,128)(2,1)S(1)} %add_convert_fusion.2), channel_id=1, source_target_pairs={{0,2},{2,4},{4,6},{6,7},{7,5},{5,3},{3,1},{1,0},{8,10},{10,12},{12... | collective-permute-start | bytes 393224 | tf_op jit(solution)/shard_map/ppermute | solution.py:33
  64.0 5.0 %collective-permute-start.30 = (bf16[256,256]{1,0:T(8,128)(2,1)S(1)}, bf16[256,256]{1,0:T(8,128)(2,1)S(1)}, u32[]{:S(2)}, u32[]{:S(2)}) collective-permute-start(bf16[256,256]{1,0:T(8,128)(2,1)S(1)} %add_convert_fusion.5), channel_id=1, source_target_pairs={{0,1},{2,0},{4,2},{6,4},{7,6},{5,7},{3,5},{1,3},{8,9},{10,8},{12,1... | collective-permute-start | bytes 393224 | tf_op jit(solution)/shard_map/ppermute | solution.py:33

commit v18 on v17

--- a/solution.py
+++ b/solution.py
@@ -47,7 +47,7 @@
     return pltpu.with_memory_space_constraint(value, pltpu.VMEM)
 
 
-def fold_kernel(order, at, gain_ref, w_hbm, tokens, out_ref, wide, sems):
+def fold_kernel(order, at, gain_hbm, w_hbm, tokens, out_ref, wide, gain_ref, sems):
     lanes = gain_ref.shape[1]
     size = w_hbm.shape[1] // len(order)
     per = size // lanes
@@ -60,10 +60,13 @@
             sems.at[n],
         )
 
+    gains = pltpu.make_async_copy(gain_hbm, gain_ref, sems.at[len(order) + 1])
+    gains.start()
     for n in range(len(order)):
         fetch(n).start()
     own = pltpu.make_async_copy(tokens, wide.at[:, : tokens.shape[1]], sems.at[len(order)])
     own.start()
+    gains.wait()
     for n in range(len(order)):
         columns = jnp.transpose(gain_ref[pl.ds(at[order[n]] * per, per), :])
         fetch(n).wait()
@@ -83,9 +86,12 @@
     return pl.pallas_call(
         functools.partial(fold_kernel, order),
         out_shape=(pltpu.VMEM(weights.shape, BF16), pltpu.VMEM((tokens.shape[0], depth), BF16)),
-        in_specs=[SMEM, VMEM, hbm, hbm],
+        in_specs=[SMEM, hbm, hbm, hbm],
         out_specs=(VMEM, pl.BlockSpec(memory_space=pl.ANY)),
-        scratch_shapes=[pltpu.SemaphoreType.DMA((len(order) + 1,))],
+        scratch_shapes=[
+            pltpu.VMEM((depth // lanes, lanes), F32),
+            pltpu.SemaphoreType.DMA((len(order) + 2,)),
+        ],
         compiler_params=pltpu.CompilerParams(vmem_limit_bytes=16 << 20),
         cost_estimate=pl.CostEstimate(
             flops=weights.size, bytes_accessed=4 * weights.size, transcendentals=0
@@ -164,7 +170,7 @@
             qh, kh = q[:, lanes], k[:, lanes]
             q_size = lax.rsqrt(jnp.sum(qh * qh, axis=-1, keepdims=True) + 1e-06)
             k_size = lax.rsqrt(jnp.sum(kh * kh, axis=-1, keepdims=True) + 1e-06)
-            q_ref[here, lanes] = (qh * (q_size * (factor[head] * LOG2E))).astype(BF16)
+            q_ref[here, lanes] = (qh * (q_size * factor[head])).astype(BF16)
             kv_ref[here, lanes] = (kh * k_size).astype(BF16)
         kv_ref[here, out_width:] = v.astype(BF16)
         halves[stream][...] = kv_ref[here, :]
@@ -204,8 +210,7 @@
         out_shape=(
             pltpu.VMEM((total, out_width), BF16),
             pltpu.VMEM((total, 2 * out_width), BF16),
-            *[pltpu.HBM((size, 2 * out_width), BF16) for size in sizes[: len(lasts)]],
-            *[pltpu.VMEM((size, 2 * out_width), BF16) for size in sizes[len(lasts) :]],
+            *[pltpu.VMEM((size, 2 * out_width), BF16) for size in sizes],
         ),
         in_specs=[SMEM] + [VMEM] * (2 + len(lasts)),
         out_specs=(VMEM,) * (2 + len(sizes)),
@@ -214,18 +219,23 @@
             flops=6 * total * width * out_width, bytes_accessed=8 * total * out_width, transcendentals=0
         ),
         name="project_finish",
-    )(in_hbm(factor), in_vmem(state), in_vmem(weights), *map(in_vmem, lasts))
+    )(factor, in_vmem(state), in_vmem(weights), *map(in_vmem, lasts))
 
 
 def attend_kernel(
-    head_size, counts, has_acc, count_out, count_streams, info, ids, q_ref, id_row, *refs
+    head_size, counts, has_acc, count_out, count_streams, info, ids_hbm, rows_hbm, q_ref, *refs
 ):
+    refs, (ids, id_row, sems) = refs[:-3], refs[-3:]
+    fetch_ids = pltpu.make_async_copy(ids_hbm, ids, sems.at[0])
+    fetch_ids.start()
     count_blocks, count_parts = counts
     kv_refs, rest = refs[: count_blocks * count_parts], refs[count_blocks * count_parts :]
     if has_acc:
         acc_in, rest = rest[0], rest[1:]
     if count_out:
-        w_ref, outs, (k_all, v_ones, acc, attended) = rest[0], rest[1:-4], rest[-4:]
+        w_hbm, outs, (k_all, v_ones, acc, attended, w_ref) = rest[0], rest[1:-5], rest[-5:]
+        fetch_w = pltpu.make_async_copy(w_hbm, w_ref, sems.at[1])
+        fetch_w.start()
     else:
         acc_out, k_all, v_ones, acc = rest
     acc[...] = acc_in[...] if has_acc else jnp.zeros_like(acc)
@@ -244,6 +254,8 @@
             for head in range(heads):
                 start = width + head * head_size
                 v_ones[head, here, :head_size] = kv_ref[:, start : start + head_size]
+        if number == 0:
+            fetch_ids.wait()
         first = info[number]
         key_low, key_high = ids[first], ids[first + keys - 1]
 
@@ -255,6 +267,9 @@
 
             def add(masked):
                 if masked:
+                    fetch_rows = pltpu.make_async_copy(rows_hbm, id_row, sems.at[2])
+                    fetch_rows.start()
+                    fetch_rows.wait()
                     own = jnp.broadcast_to(id_row[q_first // tile + index], (8, tile))
                     own = jnp.transpose(own)[:, :1]
                     allowed = [id_row[first // tile + n] <= own for n in range(keys // tile)]
@@ -297,6 +312,7 @@
             / acc[:, start + head_size : start + 2 * head_size]
         ).astype(BF16)
     out_rows, out_width = outs[0].shape
+    fetch_w.wait()
     for number, out in enumerate(outs):
         lane = info[count_blocks + 1 + number] * out_width
         first = number * count_streams // count_out * out_rows
@@ -318,23 +334,32 @@
         pltpu.VMEM((heads, keys, 2 * head_size), BF16),
         pltpu.VMEM((total, 2 * width), F32),
     ]
-    operands = [in_vmem(query), in_hbm(ids.reshape(-1, 1, math.gcd(total, 256)))]
-    operands += map(in_vmem, parts)
+    id_rows = ids.reshape(-1, 1, math.gcd(total, 256))
+    operands = [in_vmem(query), *map(in_vmem, parts)]
     if acc is not None:
         operands.append(in_vmem(acc))
     if count_out:
         operands.append(in_hbm(w_out))
-        scratch.append(pltpu.VMEM((total, width), BF16))
+        scratch += [pltpu.VMEM((total, width), BF16), pltpu.VMEM(w_out.shape, BF16)]
         shape = pltpu.VMEM((total // streams, w_out.shape[1] * streams // count_out), BF16)
     else:
         shape = pltpu.VMEM((total, 2 * width), F32)
     outs = count_out or 1
+    scratch += [
+        pltpu.SMEM(ids.shape, jnp.int32),
+        pltpu.VMEM(id_rows.shape, jnp.int32),
+        pltpu.SemaphoreType.DMA((3,)),
+    ]
+    hbm = pl.BlockSpec(memory_space=pltpu.HBM)
+    in_specs = [SMEM, hbm, hbm] + [VMEM] * len(operands)
+    if count_out:
+        in_specs[-1] = hbm
     return pl.pallas_call(
         functools.partial(
             attend_kernel, head_size, (len(blocks), len(blocks[0])), acc is not None, count_out, streams
         ),
         out_shape=(shape,) * outs,
-        in_specs=[SMEM, SMEM] + [VMEM] * len(operands),
+        in_specs=in_specs,
         out_specs=(VMEM,) * outs,
         scratch_shapes=scratch,
         compiler_params=pltpu.CompilerParams(
@@ -342,7 +367,7 @@
         ),
         cost_estimate=pl.CostEstimate(flops=1 << 20, bytes_accessed=1 << 10, transcendentals=0),
         name="attend_last" if count_out else "attend",
-    )(info, in_hbm(ids), *operands)
+    )(info, in_hbm(ids), in_hbm(id_rows), *operands)
 
 
 def total_of(*parts):
@@ -392,8 +417,8 @@
                 targets.append((s * half, (2 * step - 1 + way) * width))
     wide = placed(targets, blocks, wide)
     lasts = [held[0][0], held[1][1]]
-    state = project_begin(wide, weights, ring)
-    query, kv, *parts = project_finish(head_scale, state, weights, lasts, 3, head_size)
+    state, factor = lax.optimization_barrier((project_begin(wide, weights, ring), head_scale * LOG2E))
+    query, kv, *parts = project_finish(factor, state, weights, lasts, 3, head_size)
     halves, pieces = parts[:2], parts[2:]
 
     far, straight, crossed = [], [], []

time: 70.7 us -> 71.1 us (level)
  Pallas kernels: 17.2 us -> 18.8 us
  starting transfers between devices: 33 us -> 32.1 us
    pallas_call x4, Pallas kernels: 9.92 us -> 12.5 us  [attend(): pl.pallas_call(functools.partial(attend_kernel, head_size, (len(blocks),...]
    ppermute x2, waiting for transfers between devices: 2.62 us -> 0.39 us  [body(): far.append([lax.ppermute(part, 'seq', shift) for part in halves])]
    ppermute x28, waiting for transfers between devices: 14.3 us -> 16.1 us  [along(): lax.ppermute(value, 'head', [(order[p], order[(p + step) % count]) for p...]
    ppermute x28, starting transfers between devices: 29.9 us -> 29 us  [along(): lax.ppermute(value, 'head', [(order[p], order[(p + step) % count]) for p...]
    pallas_call x1, Pallas kernels: 2.01 us -> 1.18 us  [project_finish(): pl.pallas_call(functools.partial(finish_kernel, head_size), out_shape=(pl...]
  transfers between devices with their start and end apart: 35 -> 35, of which waited for: 14 -> 16; matrix products, arithmetic and copies ran while one was open for 1% -> 1% of each run, Pallas kernels for 17% -> 20%
where the time goes in v18:
time: 71.1 us; the launch traced here: 70.2 us
  starting transfers between devices  32.1 us (45%)
  Pallas kernels  18.8 us (26%)
  waiting for transfers between devices  16.5 us (23%)
  other arithmetic  1.4 us (2%)
  local copies, waits for them, and re-layouts  1.18 us (2%)
    ppermute x28, starting transfers between devices, along(): lax.ppermute(value, 'head', [(order[p], order[(p + step) % count]) for p...  29 us
    ppermute x28, waiting for transfers between devices, along(): lax.ppermute(value, 'head', [(order[p], order[(p + step) % count]) for p...  16.1 us
    pallas_call x4, Pallas kernels, attend(): pl.pallas_call(functools.partial(attend_kernel, head_size, (len(blocks),...  12.5 us
    pallas_call x1, Pallas kernels, fold_gain(): pl.pallas_call(functools.partial(fold_kernel, order), out_shape=(pltpu.VM...  2.88 us
    ppermute x2, starting transfers between devices, body(): far.append([lax.ppermute(part, 'seq', shift) for part in halves])  2.09 us
    pallas_call x1, Pallas kernels, project_begin(): pl.pallas_call(functools.partial(begin_kernel, blocks), out_shape=pltpu.V...  1.91 us
  transfers between devices with their start and end apart: 35, of which 16 were waited for; matrix products, arithmetic and copies ran while one was open for 1% of the time, Pallas kernels for 20%

profile of v18, /device:TPU:10, one launch (start us, length us, event | category | flops | bytes accessed | tf_op | source)
XLA Modules:
  0.0 70.2 jit_solution(12946620239909212297)
XLA Ops:
  0.0 1.0 %fusion = (bf16[256,256]{1,0:T(8,128)(2,1)S(1)}, bf16[256,256]{1,0:T(8,128)(2,1)S(1)}) fusion(bf16[512,256]{1,0:T(8,128)(2,1)} %tokens.1), kind=kLoop, calls=%fused_computation.17 | loop fusion | bytes 524288 | tf_op jit(solution)/shard_map/slice | solution.py:396
  1.0 1.6 %collective-permute-start = (bf16[256,256]{1,0:T(8,128)(2,1)S(1)}, bf16[256,256]{1,0:T(8,128)(2,1)S(1)}, u32[]{:S(2)}, u32[]{:S(2)}) collective-permute-start(bf16[256,256]{1,0:T(8,128)(2,1)S(1)} %get-tuple-element.92), channel_id=1, source_target_pairs={{0,2},{2,4},{4,6},{6,7},{7,5},{5,3},{3,1},{1,0},{8,10},{10,12},{12... | collective-permute-start | bytes 393224 | tf_op jit(solution)/shard_map/ppermute | solution.py:33
  2.6 0.4 collective-permute-start.3
  3.1 0.4 collective-permute-start.6
  3.5 1.6 %collective-permute-start.8 = (bf16[256,256]{1,0:T(8,128)(2,1)S(1)}, bf16[256,256]{1,0:T(8,128)(2,1)S(1)}, u32[]{:S(2)}, u32[]{:S(2)}) collective-permute-start(bf16[256,256]{1,0:T(8,128)(2,1)S(1)} %get-tuple-element.91), channel_id=1, source_target_pairs={{0,2},{2,4},{4,6},{6,7},{7,5},{5,3},{3,1},{1,0},{8,10},{10,12},{12... | collective-permute-start | bytes 393224 | tf_op jit(solution)/shard_map/ppermute | solution.py:33
  5.2 2.9 %fold_gain.1 = (bf16[3,2048,256]{2,1,0:T(8,128)(2,1)S(1)}, bf16[512,2048]{1,0:T(8,128)(2,1)S(1)}) custom-call(s32[8]{0:T(128)S(1)} %stack.84.at, f32[16,128]{1,0:T(8,128)} %bitcast.19, bf16[3,2048,256]{2,1,0:T(8,128)(2,1)} %w_hbm.1, bf16[512,256]{1,0:T(8,128)(2,1)} %tokens.1), custom_call_target="tpu_custom_call" | custom-call | flops 1572864 | bytes 6291456 | tf_op jit(solution)/shard_map/fold_gain/pallas_call | solution.py:86
  8.1 0.9 %collective-permute-done.3.refs_1_ = bf16[256,256]{1,0:T(8,128)(2,1)S(1)} collective-permute-done((bf16[256,256]{1,0:T(8,128)(2,1)S(1)}, bf16[256,256]{1,0:T(8,128)(2,1)S(1)}, u32[]{:S(2)}, u32[]{:S(2)}) %collective-permute-start.3) | collective-permute-done | bytes 131104 | tf_op jit(solution)/shard_map/ppermute | solution.py:33
  9.0 0.4 collective-permute-start.4
  9.4 1.6 %collective-permute-start.1 = (bf16[256,256]{1,0:T(8,128)(2,1)S(1)}, bf16[256,256]{1,0:T(8,128)(2,1)S(1)}, u32[]{:S(2)}, u32[]{:S(2)}) collective-permute-start(bf16[256,256]{1,0:T(8,128)(2,1)S(1)} %collective-permute-done.refs_0_), channel_id=1, source_target_pairs={{0,2},{2,4},{4,6},{6,7},{7,5},{5,3},{3,1},{1,0},{8,10},{10,12},{12... | collective-permute-start | bytes 393224 | tf_op jit(solution)/shard_map/ppermute | solution.py:33
  11.7 1.6 %collective-permute-start.9 = (bf16[256,256]{1,0:T(8,128)(2,1)S(1)}, bf16[256,256]{1,0:T(8,128)(2,1)S(1)}, u32[]{:S(2)}, u32[]{:S(2)}) collective-permute-start(bf16[256,256]{1,0:T(8,128)(2,1)S(1)} %collective-permute-done.8.refs_3_), channel_id=1, source_target_pairs={{0,2},{2,4},{4,6},{6,7},{7,5},{5,3},{3,1},{1,0},{8,10},{10,12},{12... | collective-permute-start | bytes 393224 | tf_op jit(solution)/shard_map/ppermute | solution.py:33
  13.3 1.6 %collective-permute-done.4.refs_1_ = bf16[256,256]{1,0:T(8,128)(2,1)S(1)} collective-permute-done((bf16[256,256]{1,0:T(8,128)(2,1)S(1)}, bf16[256,256]{1,0:T(8,128)(2,1)S(1)}, u32[]{:S(2)}, u32[]{:S(2)}) %collective-permute-start.4) | collective-permute-done | bytes 131104 | tf_op jit(solution)/shard_map/ppermute | solution.py:33
  15.4 1.6 %collective-permute-start.2 = (bf16[256,256]{1,0:T(8,128)(2,1)S(1)}, bf16[256,256]{1,0:T(8,128)(2,1)S(1)}, u32[]{:S(2)}, u32[]{:S(2)}) collective-permute-start(bf16[256,256]{1,0:T(8,128)(2,1)S(1)} %collective-permute-done.1.refs_0_), channel_id=1, source_target_pairs={{0,2},{2,4},{4,6},{6,7},{7,5},{5,3},{3,1},{1,0},{8,10},{10,12},{12... | collective-permute-start | bytes 393224 | tf_op jit(solution)/shard_map/ppermute | solution.py:33
  17.0 0.8 %collective-permute-done.7.refs_2_ = bf16[256,256]{1,0:T(8,128)(2,1)S(1)} collective-permute-done((bf16[256,256]{1,0:T(8,128)(2,1)S(1)}, bf16[256,256]{1,0:T(8,128)(2,1)S(1)}, u32[]{:S(2)}, u32[]{:S(2)}) %collective-permute-start.7) | collective-permute-done | bytes 131104 | tf_op jit(solution)/shard_map/ppermute | solution.py:33
  18.2 1.6 %collective-permute-start.11 = (bf16[256,256]{1,0:T(8,128)(2,1)S(1)}, bf16[256,256]{1,0:T(8,128)(2,1)S(1)}, u32[]{:S(2)}, u32[]{:S(2)}) collective-permute-start(bf16[256,256]{1,0:T(8,128)(2,1)S(1)} %collective-permute-done.9.refs_3_), channel_id=1, source_target_pairs={{0,2},{2,4},{4,6},{6,7},{7,5},{5,3},{3,1},{1,0},{8,10},{10,12},{12... | collective-permute-start | bytes 393224 | tf_op jit(solution)/shard_map/ppermute | solution.py:33
  20.0 0.6 collective-permute-done.5.refs_1_
  21.1 1.6 %collective-permute-start.12 = (bf16[256,256]{1,0:T(8,128)(2,1)S(1)}, bf16[256,256]{1,0:T(8,128)(2,1)S(1)}, u32[]{:S(2)}, u32[]{:S(2)}) collective-permute-start(bf16[256,256]{1,0:T(8,128)(2,1)S(1)} %collective-permute-done.2.refs_0_), channel_id=1, source_target_pairs={{0,2},{2,4},{4,6},{6,7},{7,5},{5,3},{3,1},{1,0},{8,10},{10,12},{12... | collective-permute-start | bytes 393224 | tf_op jit(solution)/shard_map/ppermute | solution.py:33
  23.3 1.9 %project_begin.1.state = f32[512,896]{1,0:T(8,128)S(1)} custom-call(bf16[512,2048]{1,0:T(8,128)(2,1)S(1)} %place.5.wide, bf16[3,2048,256]{2,1,0:T(8,128)(2,1)S(1)} %get-tuple-element.54.w_ref), custom_call_target="tpu_custom_call" | custom-call | flops 1610612736 | bytes 5242880 | tf_op jit(solution)/shard_map/project_begin/pallas_call | solution.py:186
  25.6 0.5 collective-permute-done.12.refs_0_
  26.0 1.2 %project_finish.1 = (bf16[512,256]{1,0:T(8,128)(2,1)S(1)}, bf16[512,512]{1,0:T(8,128)(2,1)S(1)}, bf16[256,512]{1,0:T(8,128)(2,1)S(1)}, bf16[256,512]{1,0:T(8,128...) custom-call(f32[2]{0:T(128)S(1)} %broadcast_multiply_fusion.factor, ...), custom_call_target="tpu_custom_call" | custom-call | flops 201326592 | bytes 1048576 | tf_op jit(solution)/shard_map/project_finish/pallas_call | solution.py:208
  27.2 0.6 collective-permute-start.17
  27.8 1.5 %collective-permute-start.18 = (bf16[256,512]{1,0:T(8,128)(2,1)S(1)}, bf16[256,512]{1,0:T(8,128)(2,1)S(1)}, u32[]{:S(2)}, u32[]{:S(2)}) collective-permute-start(bf16[256,512]{1,0:T(8,128)(2,1)S(1)} %get-tuple-element.67), channel_id=1, source_target_pairs={{0,16},{8,24},{16,0},{24,8},{1,17},{9,25},{17,1},{25,9},{2,18},{10... | collective-permute-start | bytes 786440 | tf_op jit(solution)/shard_map/ppermute | solution.py:431
  29.3 0.5 collective-permute-start.16
  30.0 3.3 %attend.3.refs_3_ = f32[512,512]{1,0:T(8,128)S(1)} custom-call(s32[2]{0:T(128)S(1)} %pad_add_fusion.1.info, s32[2048]{0:T(1024)} %ids_hbm.7, s32[8,1,256]{2,1,0:T(1,128)} %bitcast.15, bf16[512,256]{1,0:T(8,128)(2,1)S(1)} %get-tuple-element.57.q_ref, bf16[512,512]{1,0:T(8,128)(2,1)S(1)} %get-tuple-element.58.refs_0_), custom_call_target="tpu_custom_call" | custom-call | flops 1048576 | bytes 1024 | tf_op jit(solution)/shard_map/attend/pallas_call | solution.py:357
  33.4 3.3 %attend.4.refs_2_ = f32[512,512]{1,0:T(8,128)S(1)} custom-call(s32[2]{0:T(128)S(1)} %pad_add_fusion.info, s32[2048]{0:T(1024)} %ids_hbm.7, s32[8,1,256]{2,1,0:T(1,128)} %bitcast.16, bf16[512,256]{1,0:T(8,128)(2,1)S(1)} %get-tuple-element.57.q_ref, bf16[160,512]{1,0:T(8,128)(2,1)S(1)} %collective-permute-done.14.refs_0_, ...), custom_call_target="tpu_custom_call" | custom-call | flops 1048576 | bytes 1024 | tf_op jit(solution)/shard_map/attend/pallas_call | solution.py:357
  37.1 0.5 collective-permute-start.20
  37.8 2.5 %attend.5.refs_2_ = f32[512,512]{1,0:T(8,128)S(1)} custom-call(s32[2]{0:T(128)S(1)} %pad_add_fusion.2.info, s32[2048]{0:T(1024)} %ids_hbm.7, s32[8,1,256]{2,1,0:T(1,128)} %bitcast.17, bf16[512,256]{1,0:T(8,128)(2,1)S(1)} %get-tuple-element.57.q_ref, bf16[256,512]{1,0:T(8,128)(2,1)S(1)} %collective-permute-done.17.refs_0_, ...), custom_call_target="tpu_custom_call" | custom-call | flops 1048576 | bytes 1024 | tf_op jit(solution)/shard_map/attend/pallas_call | solution.py:357
  40.3 3.3 %attend_last.1 = (bf16[256,256]{1,0:T(8,128)(2,1)S(1)}, bf16[256,256]{1,0:T(8,128)(2,1)S(1)}, bf16[256,256]{1,0:T(8,128)(2,1)S(1)}, bf16[256,256]{1,0:T(8,128)(2...) custom-call(s32[18]{0:T(128)S(1)} %stack.83.info, ...), custom_call_target="tpu_custom_call" | custom-call | flops 1048576 | bytes 1024 | tf_op jit(solution)/shard_map/attend_last/pallas_call | solution.py:357
  43.7 1.6 %collective-permute-start.31 = (bf16[256,256]{1,0:T(8,128)(2,1)S(1)}, bf16[256,256]{1,0:T(8,128)(2,1)S(1)}, u32[]{:S(2)}, u32[]{:S(2)}) collective-permute-start(bf16[256,256]{1,0:T(8,128)(2,1)S(1)} %get-tuple-element.85), channel_id=1, source_target_pairs={{0,2},{2,4},{4,6},{6,7},{7,5},{5,3},{3,1},{1,0},{8,10},{10,12},{12... | collective-permute-start | bytes 393224 | tf_op jit(solution)/shard_map/ppermute | solution.py:33
  45.3 0.4 collective-permute-start.27
  45.7 0.6 collective-permute-start.24
  46.3 1.5 %collective-permute-start.21 = (bf16[256,256]{1,0:T(8,128)(2,1)S(1)}, bf16[256,256]{1,0:T(8,128)(2,1)S(1)}, u32[]{:S(2)}, u32[]{:S(2)}) collective-permute-start(bf16[256,256]{1,0:T(8,128)(2,1)S(1)} %get-tuple-element.74), channel_id=1, source_target_pairs={{0,2},{2,4},{4,6},{6,7},{7,5},{5,3},{3,1},{1,0},{8,10},{10,12},{12... | collective-permute-start | bytes 393224 | tf_op jit(solution)/shard_map/ppermute | solution.py:33
  47.8 2.3 %collective-permute-done.31 = bf16[256,256]{1,0:T(8,128)(2,1)S(1)} collective-permute-done((bf16[256,256]{1,0:T(8,128)(2,1)S(1)}, bf16[256,256]{1,0:T(8,128)(2,1)S(1)}, u32[]{:S(2)}, u32[]{:S(2)}) %collective-permute-start.31) | collective-permute-done | bytes 131104 | tf_op jit(solution)/shard_map/ppermute | solution.py:33
  50.1 1.6 %collective-permute-start.32 = (bf16[256,256]{1,0:T(8,128)(2,1)S(1)}, bf16[256,256]{1,0:T(8,128)(2,1)S(1)}, u32[]{:S(2)}, u32[]{:S(2)}) collective-permute-start(bf16[256,256]{1,0:T(8,128)(2,1)S(1)} %add_convert_fusion.4), channel_id=1, source_target_pairs={{0,2},{2,4},{4,6},{6,7},{7,5},{5,3},{3,1},{1,0},{8,10},{10,12},{12... | collective-permute-start | bytes 393224 | tf_op jit(solution)/shard_map/ppermute | solution.py:33
  51.8 0.5 collective-permute-start.28
  52.3 1.7 %collective-permute-done.24 = bf16[256,256]{1,0:T(8,128)(2,1)S(1)} collective-permute-done((bf16[256,256]{1,0:T(8,128)(2,1)S(1)}, bf16[256,256]{1,0:T(8,128)(2,1)S(1)}, u32[]{:S(2)}, u32[]{:S(2)}) %collective-permute-start.24) | collective-permute-done | bytes 131104 | tf_op jit(solution)/shard_map/ppermute | solution.py:33
  54.1 0.5 collective-permute-start.25
  54.6 1.6 %collective-permute-start.22 = (bf16[256,256]{1,0:T(8,128)(2,1)S(1)}, bf16[256,256]{1,0:T(8,128)(2,1)S(1)}, u32[]{:S(2)}, u32[]{:S(2)}) collective-permute-start(bf16[256,256]{1,0:T(8,128)(2,1)S(1)} %add_convert_fusion.11), channel_id=1, source_target_pairs={{0,2},{2,4},{4,6},{6,7},{7,5},{5,3},{3,1},{1,0},{8,10},{10,12},{12... | collective-permute-start | bytes 393224 | tf_op jit(solution)/shard_map/ppermute | solution.py:33
  56.3 1.6 %collective-permute-start.33 = (bf16[256,256]{1,0:T(8,128)(2,1)S(1)}, bf16[256,256]{1,0:T(8,128)(2,1)S(1)}, u32[]{:S(2)}, u32[]{:S(2)}) collective-permute-start(bf16[256,256]{1,0:T(8,128)(2,1)S(1)} %add_convert_fusion.3), channel_id=1, source_target_pairs={{0,2},{2,4},{4,6},{6,7},{7,5},{5,3},{3,1},{1,0},{8,10},{10,12},{12... | collective-permute-start | bytes 393224 | tf_op jit(solution)/shard_map/ppermute | solution.py:33
  57.9 0.5 collective-permute-start.29
  58.5 2.0 %collective-permute-done.25 = bf16[256,256]{1,0:T(8,128)(2,1)S(1)} collective-permute-done((bf16[256,256]{1,0:T(8,128)(2,1)S(1)}, bf16[256,256]{1,0:T(8,128)(2,1)S(1)}, u32[]{:S(2)}, u32[]{:S(2)}) %collective-permute-start.25) | collective-permute-done | bytes 131104 | tf_op jit(solution)/shard_map/ppermute | solution.py:33
  60.5 0.5 collective-permute-start.26
  61.0 1.7 %collective-permute-start.23 = (bf16[256,256]{1,0:T(8,128)(2,1)S(1)}, bf16[256,256]{1,0:T(8,128)(2,1)S(1)}, u32[]{:S(2)}, u32[]{:S(2)}) collective-permute-start(bf16[256,256]{1,0:T(8,128)(2,1)S(1)} %add_convert_fusion.10), channel_id=1, source_target_pairs={{0,2},{2,4},{4,6},{6,7},{7,5},{5,3},{3,1},{1,0},{8,10},{10,12},{12... | collective-permute-start | bytes 393224 | tf_op jit(solution)/shard_map/ppermute | solution.py:33
  62.7 1.6 %collective-permute-start.34 = (bf16[256,256]{1,0:T(8,128)(2,1)S(1)}, bf16[256,256]{1,0:T(8,128)(2,1)S(1)}, u32[]{:S(2)}, u32[]{:S(2)}) collective-permute-start(bf16[256,256]{1,0:T(8,128)(2,1)S(1)} %add_convert_fusion.2), channel_id=1, source_target_pairs={{0,2},{2,4},{4,6},{6,7},{7,5},{5,3},{3,1},{1,0},{8,10},{10,12},{12... | collective-permute-start | bytes 393224 | tf_op jit(solution)/shard_map/ppermute | solution.py:33
  64.4 0.5 collective-permute-start.30
  64.9 1.3 %collective-permute-done.26 = bf16[256,256]{1,0:T(8,128)(2,1)S(1)} collective-permute-done((bf16[256,256]{1,0:T(8,128)(2,1)S(1)}, bf16[256,256]{1,0:T(8,128)(2,1)S(1)}, u32[]{:S(2)}, u32[]{:S(2)}) %collective-permute-start.26) | collective-permute-done | bytes 131104 | tf_op jit(solution)/shard_map/ppermute | solution.py:33
  66.1 1.6 %collective-permute-done.34 = bf16[256,256]{1,0:T(8,128)(2,1)S(1)} collective-permute-done((bf16[256,256]{1,0:T(8,128)(2,1)S(1)}, bf16[256,256]{1,0:T(8,128)(2,1)S(1)}, u32[]{:S(2)}, u32[]{:S(2)}) %collective-permute-start.34) | collective-permute-done | bytes 131104 | tf_op jit(solution)/shard_map/ppermute | solution.py:33
  67.7 1.7 %collective-permute-done.30 = bf16[256,256]{1,0:T(8,128)(2,1)S(1)} collective-permute-done((bf16[256,256]{1,0:T(8,128)(2,1)S(1)}, bf16[256,256]{1,0:T(8,128)(2,1)S(1)}, u32[]{:S(2)}, u32[]{:S(2)}) %collective-permute-start.30) | collective-permute-done | bytes 131104 | tf_op jit(solution)/shard_map/ppermute | solution.py:33
  69.5 0.7 %pad_maximum_fusion = bf16[512,256]{1,0:T(8,128)(2,1)} fusion(bf16[256,256]{1,0:T(8,128)(2,1)S(1)} %get-tuple-element.93, bf16[256,256]{1,0:T(8,128)(2,1)S(1)} %get-tuple-element.94), kind=kLoop, calls=%fused_computation | loop fusion | flops 524288 | bytes 524288 | tf_op jit(solution)/shard_map/concatenate | solution.py:458
  (53 shorter events, 4.6 us)
Async XLA Ops:
  0.0 19.8 %copy-start = (f32[2]{0:T(128)S(1)}, f32[2]{0:T(128)}, u32[]{:S(2)}) copy-start(f32[2]{0:T(128)} %param.9) | copy-start | bytes 28
  1.0 7.1 %collective-permute-start = (bf16[256,256]{1,0:T(8,128)(2,1)S(1)}, bf16[256,256]{1,0:T(8,128)(2,1)S(1)}, u32[]{:S(2)}, u32[]{:S(2)}) collective-permute-start(bf16[256,256]{1,0:T(8,128)(2,1)S(1)} %get-tuple-element.92), channel_id=1, source_target_pairs={{0,2},{2,4},{4,6},{6,7},{7,5},{5,3},{3,1},{1,0},{8,10},{10,12},{12... | collective-permute-start | bytes 393224 | tf_op jit(solution)/shard_map/ppermute | solution.py:33
  2.6 6.4 %collective-permute-start.3 = (bf16[256,256]{1,0:T(8,128)(2,1)S(1)}, bf16[256,256]{1,0:T(8,128)(2,1)S(1)}, u32[]{:S(2)}, u32[]{:S(2)}) collective-permute-start(bf16[256,256]{1,0:T(8,128)(2,1)S(1)} %get-tuple-element.91), channel_id=1, source_target_pairs={{0,1},{2,0},{4,2},{6,4},{7,6},{5,7},{3,5},{1,3},{8,9},{10,8},{12,1... | collective-permute-start | bytes 393224 | tf_op jit(solution)/shard_map/ppermute | solution.py:33
  3.1 8.2 %collective-permute-start.6 = (bf16[256,256]{1,0:T(8,128)(2,1)S(1)}, bf16[256,256]{1,0:T(8,128)(2,1)S(1)}, u32[]{:S(2)}, u32[]{:S(2)}) collective-permute-start(bf16[256,256]{1,0:T(8,128)(2,1)S(1)} %get-tuple-element.92), channel_id=1, source_target_pairs={{0,1},{2,0},{4,2},{6,4},{7,6},{5,7},{3,5},{1,3},{8,9},{10,8},{12,1... | collective-permute-start | bytes 393224 | tf_op jit(solution)/shard_map/ppermute | solution.py:33
  3.5 8.2 %collective-permute-start.8 = (bf16[256,256]{1,0:T(8,128)(2,1)S(1)}, bf16[256,256]{1,0:T(8,128)(2,1)S(1)}, u32[]{:S(2)}, u32[]{:S(2)}) collective-permute-start(bf16[256,256]{1,0:T(8,128)(2,1)S(1)} %get-tuple-element.91), channel_id=1, source_target_pairs={{0,2},{2,4},{4,6},{6,7},{7,5},{5,3},{3,1},{1,0},{8,10},{10,12},{12... | collective-permute-start | bytes 393224 | tf_op jit(solution)/shard_map/ppermute | solution.py:33
  9.0 5.9 %collective-permute-start.4 = (bf16[256,256]{1,0:T(8,128)(2,1)S(1)}, bf16[256,256]{1,0:T(8,128)(2,1)S(1)}, u32[]{:S(2)}, u32[]{:S(2)}) collective-permute-start(bf16[256,256]{1,0:T(8,128)(2,1)S(1)} %collective-permute-done.3.refs_1_), channel_id=1, source_target_pairs={{0,1},{2,0},{4,2},{6,4},{7,6},{5,7},{3,5},{1,3},{8,9},{10,8},{12,1... | collective-permute-start | bytes 393224 | tf_op jit(solution)/shard_map/ppermute | solution.py:33
  9.4 5.9 %collective-permute-start.1 = (bf16[256,256]{1,0:T(8,128)(2,1)S(1)}, bf16[256,256]{1,0:T(8,128)(2,1)S(1)}, u32[]{:S(2)}, u32[]{:S(2)}) collective-permute-start(bf16[256,256]{1,0:T(8,128)(2,1)S(1)} %collective-permute-done.refs_0_), channel_id=1, source_target_pairs={{0,2},{2,4},{4,6},{6,7},{7,5},{5,3},{3,1},{1,0},{8,10},{10,12},{12... | collective-permute-start | bytes 393224 | tf_op jit(solution)/shard_map/ppermute | solution.py:33
  11.3 6.5 %collective-permute-start.7 = (bf16[256,256]{1,0:T(8,128)(2,1)S(1)}, bf16[256,256]{1,0:T(8,128)(2,1)S(1)}, u32[]{:S(2)}, u32[]{:S(2)}) collective-permute-start(bf16[256,256]{1,0:T(8,128)(2,1)S(1)} %collective-permute-done.6.refs_2_), channel_id=1, source_target_pairs={{0,1},{2,0},{4,2},{6,4},{7,6},{5,7},{3,5},{1,3},{8,9},{10,8},{12,1... | collective-permute-start | bytes 393224 | tf_op jit(solution)/shard_map/ppermute | solution.py:33
  11.7 6.5 %collective-permute-start.9 = (bf16[256,256]{1,0:T(8,128)(2,1)S(1)}, bf16[256,256]{1,0:T(8,128)(2,1)S(1)}, u32[]{:S(2)}, u32[]{:S(2)}) collective-permute-start(bf16[256,256]{1,0:T(8,128)(2,1)S(1)} %collective-permute-done.8.refs_3_), channel_id=1, source_target_pairs={{0,2},{2,4},{4,6},{6,7},{7,5},{5,3},{3,1},{1,0},{8,10},{10,12},{12... | collective-permute-start | bytes 393224 | tf_op jit(solution)/shard_map/ppermute | solution.py:33
  14.9 5.7 %collective-permute-start.5 = (bf16[256,256]{1,0:T(8,128)(2,1)S(1)}, bf16[256,256]{1,0:T(8,128)(2,1)S(1)}, u32[]{:S(2)}, u32[]{:S(2)}) collective-permute-start(bf16[256,256]{1,0:T(8,128)(2,1)S(1)} %collective-permute-done.4.refs_1_), channel_id=1, source_target_pairs={{0,1},{2,0},{4,2},{6,4},{7,6},{5,7},{3,5},{1,3},{8,9},{10,8},{12,1... | collective-permute-start | bytes 393224 | tf_op jit(solution)/shard_map/ppermute | solution.py:33
  15.4 5.7 %collective-permute-start.2 = (bf16[256,256]{1,0:T(8,128)(2,1)S(1)}, bf16[256,256]{1,0:T(8,128)(2,1)S(1)}, u32[]{:S(2)}, u32[]{:S(2)}) collective-permute-start(bf16[256,256]{1,0:T(8,128)(2,1)S(1)} %collective-permute-done.1.refs_0_), channel_id=1, source_target_pairs={{0,2},{2,4},{4,6},{6,7},{7,5},{5,3},{3,1},{1,0},{8,10},{10,12},{12... | collective-permute-start | bytes 393224 | tf_op jit(solution)/shard_map/ppermute | solution.py:33
  17.7 5.3 %collective-permute-start.10 = (bf16[256,256]{1,0:T(8,128)(2,1)S(1)}, bf16[256,256]{1,0:T(8,128)(2,1)S(1)}, u32[]{:S(2)}, u32[]{:S(2)}) collective-permute-start(bf16[256,256]{1,0:T(8,128)(2,1)S(1)} %collective-permute-done.7.refs_2_), channel_id=1, source_target_pairs={{0,1},{2,0},{4,2},{6,4},{7,6},{5,7},{3,5},{1,3},{8,9},{10,8},{12,1... | collective-permute-start | bytes 393224 | tf_op jit(solution)/shard_map/ppermute | solution.py:33
  18.2 5.0 %collective-permute-start.11 = (bf16[256,256]{1,0:T(8,128)(2,1)S(1)}, bf16[256,256]{1,0:T(8,128)(2,1)S(1)}, u32[]{:S(2)}, u32[]{:S(2)}) collective-permute-start(bf16[256,256]{1,0:T(8,128)(2,1)S(1)} %collective-permute-done.9.refs_3_), channel_id=1, source_target_pairs={{0,2},{2,4},{4,6},{6,7},{7,5},{5,3},{3,1},{1,0},{8,10},{10,12},{12... | collective-permute-start | bytes 393224 | tf_op jit(solution)/shard_map/ppermute | solution.py:33
  20.6 5.0 %collective-permute-start.13 = (bf16[256,256]{1,0:T(8,128)(2,1)S(1)}, bf16[256,256]{1,0:T(8,128)(2,1)S(1)}, u32[]{:S(2)}, u32[]{:S(2)}) collective-permute-start(bf16[256,256]{1,0:T(8,128)(2,1)S(1)} %collective-permute-done.5.refs_1_), channel_id=1, source_target_pairs={{0,1},{2,0},{4,2},{6,4},{7,6},{5,7},{3,5},{1,3},{8,9},{10,8},{12,1... | collective-permute-start | bytes 393224 | tf_op jit(solution)/shard_map/ppermute | solution.py:33
  21.1 5.0 %collective-permute-start.12 = (bf16[256,256]{1,0:T(8,128)(2,1)S(1)}, bf16[256,256]{1,0:T(8,128)(2,1)S(1)}, u32[]{:S(2)}, u32[]{:S(2)}) collective-permute-start(bf16[256,256]{1,0:T(8,128)(2,1)S(1)} %collective-permute-done.2.refs_0_), channel_id=1, source_target_pairs={{0,2},{2,4},{4,6},{6,7},{7,5},{5,3},{3,1},{1,0},{8,10},{10,12},{12... | collective-permute-start | bytes 393224 | tf_op jit(solution)/shard_map/ppermute | solution.py:33
  27.2 9.5 %collective-permute-start.17 = (bf16[256,512]{1,0:T(8,128)(2,1)S(1)}, bf16[256,512]{1,0:T(8,128)(2,1)S(1)}, u32[]{:S(2)}, u32[]{:S(2)}) collective-permute-start(bf16[256,512]{1,0:T(8,128)(2,1)S(1)} %get-tuple-element.66), channel_id=1, source_target_pairs={{0,16},{8,24},{16,0},{24,8},{1,17},{9,25},{17,1},{25,9},{2,18},{10... | collective-permute-start | bytes 786440 | tf_op jit(solution)/shard_map/ppermute | solution.py:431
  27.8 9.3 %collective-permute-start.18 = (bf16[256,512]{1,0:T(8,128)(2,1)S(1)}, bf16[256,512]{1,0:T(8,128)(2,1)S(1)}, u32[]{:S(2)}, u32[]{:S(2)}) collective-permute-start(bf16[256,512]{1,0:T(8,128)(2,1)S(1)} %get-tuple-element.67), channel_id=1, source_target_pairs={{0,16},{8,24},{16,0},{24,8},{1,17},{9,25},{17,1},{25,9},{2,18},{10... | collective-permute-start | bytes 786440 | tf_op jit(solution)/shard_map/ppermute | solution.py:431
  29.3 4.0 %collective-permute-start.15 = (bf16[176,512]{1,0:T(8,128)(2,1)S(1)}, bf16[176,512]{1,0:T(8,128)(2,1)S(1)}, u32[]{:S(2)}, u32[]{:S(2)}) collective-permute-start(bf16[176,512]{1,0:T(8,128)(2,1)S(1)} %get-tuple-element.60), channel_id=1, source_target_pairs={{0,8},{8,0},{16,24},{24,16},{1,9},{9,1},{17,25},{25,17},{2,10},{10... | collective-permute-start | bytes 540680 | tf_op jit(solution)/shard_map/ppermute | solution.py:39
  29.3 4.0 %collective-permute-start.16 = (bf16[176,512]{1,0:T(8,128)(2,1)S(1)}, bf16[176,512]{1,0:T(8,128)(2,1)S(1)}, u32[]{:S(2)}, u32[]{:S(2)}) collective-permute-start(bf16[176,512]{1,0:T(8,128)(2,1)S(1)} %get-tuple-element.61), channel_id=1, source_target_pairs={{0,8},{8,0},{16,24},{24,16},{1,9},{9,1},{17,25},{25,17},{2,10},{10... | collective-permute-start | bytes 540680 | tf_op jit(solution)/shard_map/ppermute | solution.py:39
  29.8 3.5 %collective-permute-start.14 = (bf16[160,512]{1,0:T(8,128)(2,1)S(1)}, bf16[160,512]{1,0:T(8,128)(2,1)S(1)}, u32[]{:S(2)}, u32[]{:S(2)}) collective-permute-start(bf16[160,512]{1,0:T(8,128)(2,1)S(1)} %get-tuple-element.59), channel_id=1, source_target_pairs={{0,8},{8,0},{16,24},{24,16},{1,9},{9,1},{17,25},{25,17},{2,10},{10... | collective-permute-start | bytes 491528 | tf_op jit(solution)/shard_map/ppermute | solution.py:39
  37.1 3.2 %collective-permute-start.19 = (bf16[256,512]{1,0:T(8,128)(2,1)S(1)}, bf16[256,512]{1,0:T(8,128)(2,1)S(1)}, u32[]{:S(2)}, u32[]{:S(2)}) collective-permute-start(bf16[256,512]{1,0:T(8,128)(2,1)S(1)} %collective-permute-done.17.refs_0_), channel_id=1, source_target_pairs={{0,8},{8,0},{16,24},{24,16},{1,9},{9,1},{17,25},{25,17},{2,10},{10... | collective-permute-start | bytes 786440 | tf_op jit(solution)/shard_map/ppermute | solution.py:39
  37.1 3.2 %collective-permute-start.20 = (bf16[256,512]{1,0:T(8,128)(2,1)S(1)}, bf16[256,512]{1,0:T(8,128)(2,1)S(1)}, u32[]{:S(2)}, u32[]{:S(2)}) collective-permute-start(bf16[256,512]{1,0:T(8,128)(2,1)S(1)} %collective-permute-done.18.refs_1_), channel_id=1, source_target_pairs={{0,8},{8,0},{16,24},{24,16},{1,9},{9,1},{17,25},{25,17},{2,10},{10... | collective-permute-start | bytes 786440 | tf_op jit(solution)/shard_map/ppermute | solution.py:39
  43.7 6.4 %collective-permute-start.31 = (bf16[256,256]{1,0:T(8,128)(2,1)S(1)}, bf16[256,256]{1,0:T(8,128)(2,1)S(1)}, u32[]{:S(2)}, u32[]{:S(2)}) collective-permute-start(bf16[256,256]{1,0:T(8,128)(2,1)S(1)} %get-tuple-element.85), channel_id=1, source_target_pairs={{0,2},{2,4},{4,6},{6,7},{7,5},{5,3},{3,1},{1,0},{8,10},{10,12},{12... | collective-permute-start | bytes 393224 | tf_op jit(solution)/shard_map/ppermute | solution.py:33
  45.3 6.5 %collective-permute-start.27 = (bf16[256,256]{1,0:T(8,128)(2,1)S(1)}, bf16[256,256]{1,0:T(8,128)(2,1)S(1)}, u32[]{:S(2)}, u32[]{:S(2)}) collective-permute-start(bf16[256,256]{1,0:T(8,128)(2,1)S(1)} %get-tuple-element.81), channel_id=1, source_target_pairs={{0,1},{2,0},{4,2},{6,4},{7,6},{5,7},{3,5},{1,3},{8,9},{10,8},{12,1... | collective-permute-start | bytes 393224 | tf_op jit(solution)/shard_map/ppermute | solution.py:33
  45.7 8.3 %collective-permute-start.24 = (bf16[256,256]{1,0:T(8,128)(2,1)S(1)}, bf16[256,256]{1,0:T(8,128)(2,1)S(1)}, u32[]{:S(2)}, u32[]{:S(2)}) collective-permute-start(bf16[256,256]{1,0:T(8,128)(2,1)S(1)} %get-tuple-element.77), channel_id=1, source_target_pairs={{0,1},{2,0},{4,2},{6,4},{7,6},{5,7},{3,5},{1,3},{8,9},{10,8},{12,1... | collective-permute-start | bytes 393224 | tf_op jit(solution)/shard_map/ppermute | solution.py:33
  46.3 8.3 %collective-permute-start.21 = (bf16[256,256]{1,0:T(8,128)(2,1)S(1)}, bf16[256,256]{1,0:T(8,128)(2,1)S(1)}, u32[]{:S(2)}, u32[]{:S(2)}) collective-permute-start(bf16[256,256]{1,0:T(8,128)(2,1)S(1)} %get-tuple-element.74), channel_id=1, source_target_pairs={{0,2},{2,4},{4,6},{6,7},{7,5},{5,3},{3,1},{1,0},{8,10},{10,12},{12... | collective-permute-start | bytes 393224 | tf_op jit(solution)/shard_map/ppermute | solution.py:33
  50.1 6.1 %collective-permute-start.32 = (bf16[256,256]{1,0:T(8,128)(2,1)S(1)}, bf16[256,256]{1,0:T(8,128)(2,1)S(1)}, u32[]{:S(2)}, u32[]{:S(2)}) collective-permute-start(bf16[256,256]{1,0:T(8,128)(2,1)S(1)} %add_convert_fusion.4), channel_id=1, source_target_pairs={{0,2},{2,4},{4,6},{6,7},{7,5},{5,3},{3,1},{1,0},{8,10},{10,12},{12... | collective-permute-start | bytes 393224 | tf_op jit(solution)/shard_map/ppermute | solution.py:33
  51.8 6.1 %collective-permute-start.28 = (bf16[256,256]{1,0:T(8,128)(2,1)S(1)}, bf16[256,256]{1,0:T(8,128)(2,1)S(1)}, u32[]{:S(2)}, u32[]{:S(2)}) collective-permute-start(bf16[256,256]{1,0:T(8,128)(2,1)S(1)} %add_convert_fusion.7), channel_id=1, source_target_pairs={{0,1},{2,0},{4,2},{6,4},{7,6},{5,7},{3,5},{1,3},{8,9},{10,8},{12,1... | collective-permute-start | bytes 393224 | tf_op jit(solution)/shard_map/ppermute | solution.py:33
  54.1 6.4 %collective-permute-start.25 = (bf16[256,256]{1,0:T(8,128)(2,1)S(1)}, bf16[256,256]{1,0:T(8,128)(2,1)S(1)}, u32[]{:S(2)}, u32[]{:S(2)}) collective-permute-start(bf16[256,256]{1,0:T(8,128)(2,1)S(1)} %add_convert_fusion.9), channel_id=1, source_target_pairs={{0,1},{2,0},{4,2},{6,4},{7,6},{5,7},{3,5},{1,3},{8,9},{10,8},{12,1... | collective-permute-start | bytes 393224 | tf_op jit(solution)/shard_map/ppermute | solution.py:33
  54.6 6.3 %collective-permute-start.22 = (bf16[256,256]{1,0:T(8,128)(2,1)S(1)}, bf16[256,256]{1,0:T(8,128)(2,1)S(1)}, u32[]{:S(2)}, u32[]{:S(2)}) collective-permute-start(bf16[256,256]{1,0:T(8,128)(2,1)S(1)} %add_convert_fusion.11), channel_id=1, source_target_pairs={{0,2},{2,4},{4,6},{6,7},{7,5},{5,3},{3,1},{1,0},{8,10},{10,12},{12... | collective-permute-start | bytes 393224 | tf_op jit(solution)/shard_map/ppermute | solution.py:33
  56.3 6.4 %collective-permute-start.33 = (bf16[256,256]{1,0:T(8,128)(2,1)S(1)}, bf16[256,256]{1,0:T(8,128)(2,1)S(1)}, u32[]{:S(2)}, u32[]{:S(2)}) collective-permute-start(bf16[256,256]{1,0:T(8,128)(2,1)S(1)} %add_convert_fusion.3), channel_id=1, source_target_pairs={{0,2},{2,4},{4,6},{6,7},{7,5},{5,3},{3,1},{1,0},{8,10},{10,12},{12... | collective-permute-start | bytes 393224 | tf_op jit(solution)/shard_map/ppermute | solution.py:33
  57.9 6.4 %collective-permute-start.29 = (bf16[256,256]{1,0:T(8,128)(2,1)S(1)}, bf16[256,256]{1,0:T(8,128)(2,1)S(1)}, u32[]{:S(2)}, u32[]{:S(2)}) collective-permute-start(bf16[256,256]{1,0:T(8,128)(2,1)S(1)} %add_convert_fusion.6), channel_id=1, source_target_pairs={{0,1},{2,0},{4,2},{6,4},{7,6},{5,7},{3,5},{1,3},{8,9},{10,8},{12,1... | collective-permute-start | bytes 393224 | tf_op jit(solution)/shard_map/ppermute | solution.py:33
  60.5 5.6 %collective-permute-start.26 = (bf16[256,256]{1,0:T(8,128)(2,1)S(1)}, bf16[256,256]{1,0:T(8,128)(2,1)S(1)}, u32[]{:S(2)}, u32[]{:S(2)}) collective-permute-start(bf16[256,256]{1,0:T(8,128)(2,1)S(1)} %add_convert_fusion.8), channel_id=1, source_target_pairs={{0,1},{2,0},{4,2},{6,4},{7,6},{5,7},{3,5},{1,3},{8,9},{10,8},{12,1... | collective-permute-start | bytes 393224 | tf_op jit(solution)/shard_map/ppermute | solution.py:33
  61.0 5.1 %collective-permute-start.23 = (bf16[256,256]{1,0:T(8,128)(2,1)S(1)}, bf16[256,256]{1,0:T(8,128)(2,1)S(1)}, u32[]{:S(2)}, u32[]{:S(2)}) collective-permute-start(bf16[256,256]{1,0:T(8,128)(2,1)S(1)} %add_convert_fusion.10), channel_id=1, source_target_pairs={{0,2},{2,4},{4,6},{6,7},{7,5},{5,3},{3,1},{1,0},{8,10},{10,12},{12... | collective-permute-start | bytes 393224 | tf_op jit(solution)/shard_map/ppermute | solution.py:33
  62.7 5.0 %collective-permute-start.34 = (bf16[256,256]{1,0:T(8,128)(2,1)S(1)}, bf16[256,256]{1,0:T(8,128)(2,1)S(1)}, u32[]{:S(2)}, u32[]{:S(2)}) collective-permute-start(bf16[256,256]{1,0:T(8,128)(2,1)S(1)} %add_convert_fusion.2), channel_id=1, source_target_pairs={{0,2},{2,4},{4,6},{6,7},{7,5},{5,3},{3,1},{1,0},{8,10},{10,12},{12... | collective-permute-start | bytes 393224 | tf_op jit(solution)/shard_map/ppermute | solution.py:33
  64.4 5.0 %collective-permute-start.30 = (bf16[256,256]{1,0:T(8,128)(2,1)S(1)}, bf16[256,256]{1,0:T(8,128)(2,1)S(1)}, u32[]{:S(2)}, u32[]{:S(2)}) collective-permute-start(bf16[256,256]{1,0:T(8,128)(2,1)S(1)} %add_convert_fusion.5), channel_id=1, source_target_pairs={{0,1},{2,0},{4,2},{6,4},{7,6},{5,7},{3,5},{1,3},{8,9},{10,8},{12,1... | collective-permute-start | bytes 393224 | tf_op jit(solution)/shard_map/ppermute | solution.py:33

commit v19 on v18

--- a/solution.py
+++ b/solution.py
@@ -223,18 +223,15 @@
 
 
 def attend_kernel(
-    head_size, counts, has_acc, count_out, count_streams, info, ids_hbm, rows_hbm, q_ref, *refs
+    head_size, counts, has_acc, count_out, count_streams, info, ids, id_row, q_ref, *refs
 ):
-    refs, (ids, id_row, sems) = refs[:-3], refs[-3:]
-    fetch_ids = pltpu.make_async_copy(ids_hbm, ids, sems.at[0])
-    fetch_ids.start()
     count_blocks, count_parts = counts
     kv_refs, rest = refs[: count_blocks * count_parts], refs[count_blocks * count_parts :]
     if has_acc:
         acc_in, rest = rest[0], rest[1:]
     if count_out:
-        w_hbm, outs, (k_all, v_ones, acc, attended, w_ref) = rest[0], rest[1:-5], rest[-5:]
-        fetch_w = pltpu.make_async_copy(w_hbm, w_ref, sems.at[1])
+        w_hbm, outs, (k_all, v_ones, acc, attended, w_ref, sem) = rest[0], rest[1:-6], rest[-6:]
+        fetch_w = pltpu.make_async_copy(w_hbm, w_ref, sem)
         fetch_w.start()
     else:
         acc_out, k_all, v_ones, acc = rest
@@ -254,8 +251,6 @@
             for head in range(heads):
                 start = width + head * head_size
                 v_ones[head, here, :head_size] = kv_ref[:, start : start + head_size]
-        if number == 0:
-            fetch_ids.wait()
         first = info[number]
         key_low, key_high = ids[first], ids[first + keys - 1]
 
@@ -267,9 +262,6 @@
 
             def add(masked):
                 if masked:
-                    fetch_rows = pltpu.make_async_copy(rows_hbm, id_row, sems.at[2])
-                    fetch_rows.start()
-                    fetch_rows.wait()
                     own = jnp.broadcast_to(id_row[q_first // tile + index], (8, tile))
                     own = jnp.transpose(own)[:, :1]
                     allowed = [id_row[first // tile + n] <= own for n in range(keys // tile)]
@@ -340,20 +332,18 @@
         operands.append(in_vmem(acc))
     if count_out:
         operands.append(in_hbm(w_out))
-        scratch += [pltpu.VMEM((total, width), BF16), pltpu.VMEM(w_out.shape, BF16)]
+        scratch += [
+            pltpu.VMEM((total, width), BF16),
+            pltpu.VMEM(w_out.shape, BF16),
+            pltpu.SemaphoreType.DMA(()),
+        ]
         shape = pltpu.VMEM((total // streams, w_out.shape[1] * streams // count_out), BF16)
     else:
         shape = pltpu.VMEM((total, 2 * width), F32)
     outs = count_out or 1
-    scratch += [
-        pltpu.SMEM(ids.shape, jnp.int32),
-        pltpu.VMEM(id_rows.shape, jnp.int32),
-        pltpu.SemaphoreType.DMA((3,)),
-    ]
-    hbm = pl.BlockSpec(memory_space=pltpu.HBM)
-    in_specs = [SMEM, hbm, hbm] + [VMEM] * len(operands)
+    in_specs = [SMEM, SMEM, VMEM] + [VMEM] * len(operands)
     if count_out:
-        in_specs[-1] = hbm
+        in_specs[-1] = pl.BlockSpec(memory_space=pltpu.HBM)
     return pl.pallas_call(
         functools.partial(
             attend_kernel, head_size, (len(blocks), len(blocks[0])), acc is not None, count_out, streams

time: 71.1 us -> 70.2 us (0.987)
  Pallas kernels: 18.8 us -> 15.9 us
  waiting for transfers between devices: 16.5 us -> 18.7 us
    pallas_call x4, Pallas kernels: 12.5 us -> 9.55 us  [attend(): pl.pallas_call(functools.partial(attend_kernel, head_size, (len(blocks),...]
    ppermute x2, waiting for transfers between devices: 0.39 us -> 2.57 us  [body(): far.append([lax.ppermute(part, 'seq', shift) for part in halves])]
  transfers between devices with their start and end apart: 35 -> 35, of which waited for: 16 -> 16; matrix products, arithmetic and copies ran while one was open for 1% -> 1% of each run, Pallas kernels for 20% -> 17%
where the time goes in v19:
time: 70.2 us; the launch traced here: 69.4 us
  starting transfers between devices  32.1 us (46%)
  waiting for transfers between devices  18.7 us (27%)
  Pallas kernels  15.9 us (23%)
  other arithmetic  1.4 us (2%)
  local copies, waits for them, and re-layouts  1.18 us (2%)
    ppermute x28, starting transfers between devices, along(): lax.ppermute(value, 'head', [(order[p], order[(p + step) % count]) for p...  29 us
    ppermute x28, waiting for transfers between devices, along(): lax.ppermute(value, 'head', [(order[p], order[(p + step) % count]) for p...  16.1 us
    pallas_call x4, Pallas kernels, attend(): pl.pallas_call(functools.partial(attend_kernel, head_size, (len(blocks),...  9.55 us
    pallas_call x1, Pallas kernels, fold_gain(): pl.pallas_call(functools.partial(fold_kernel, order), out_shape=(pltpu.VM...  2.88 us
    ppermute x2, waiting for transfers between devices, body(): far.append([lax.ppermute(part, 'seq', shift) for part in halves])  2.57 us
    ppermute x2, starting transfers between devices, body(): far.append([lax.ppermute(part, 'seq', shift) for part in halves])  2.09 us
    pallas_call x1, Pallas kernels, project_begin(): pl.pallas_call(functools.partial(begin_kernel, blocks), out_shape=pltpu.V...  1.91 us
  transfers between devices with their start and end apart: 35, of which 16 were waited for; matrix products, arithmetic and copies ran while one was open for 1% of the time, Pallas kernels for 17%

profile of v19, /device:TPU:10, one launch (start us, length us, event | category | flops | bytes accessed | tf_op | source)
XLA Modules:
  0.0 69.4 jit_solution(16005149512467119651)
XLA Ops:
  0.0 1.0 %fusion = (bf16[256,256]{1,0:T(8,128)(2,1)S(1)}, bf16[256,256]{1,0:T(8,128)(2,1)S(1)}) fusion(bf16[512,256]{1,0:T(8,128)(2,1)} %tokens.1), kind=kLoop, calls=%fused_computation.17 | loop fusion | bytes 524288 | tf_op jit(solution)/shard_map/slice | solution.py:386
  1.0 1.6 %collective-permute-start = (bf16[256,256]{1,0:T(8,128)(2,1)S(1)}, bf16[256,256]{1,0:T(8,128)(2,1)S(1)}, u32[]{:S(2)}, u32[]{:S(2)}) collective-permute-start(bf16[256,256]{1,0:T(8,128)(2,1)S(1)} %get-tuple-element.92), channel_id=1, source_target_pairs={{0,2},{2,4},{4,6},{6,7},{7,5},{5,3},{3,1},{1,0},{8,10},{10,12},{12... | collective-permute-start | bytes 393224 | tf_op jit(solution)/shard_map/ppermute | solution.py:33
  3.1 0.4 collective-permute-start.6
  3.5 1.6 %collective-permute-start.8 = (bf16[256,256]{1,0:T(8,128)(2,1)S(1)}, bf16[256,256]{1,0:T(8,128)(2,1)S(1)}, u32[]{:S(2)}, u32[]{:S(2)}) collective-permute-start(bf16[256,256]{1,0:T(8,128)(2,1)S(1)} %get-tuple-element.91), channel_id=1, source_target_pairs={{0,2},{2,4},{4,6},{6,7},{7,5},{5,3},{3,1},{1,0},{8,10},{10,12},{12... | collective-permute-start | bytes 393224 | tf_op jit(solution)/shard_map/ppermute | solution.py:33
  5.2 2.9 %fold_gain.1 = (bf16[3,2048,256]{2,1,0:T(8,128)(2,1)S(1)}, bf16[512,2048]{1,0:T(8,128)(2,1)S(1)}) custom-call(s32[8]{0:T(128)S(1)} %stack.84.at, f32[16,128]{1,0:T(8,128)} %bitcast.19, bf16[3,2048,256]{2,1,0:T(8,128)(2,1)} %w_hbm.1, bf16[512,256]{1,0:T(8,128)(2,1)} %tokens.1), custom_call_target="tpu_custom_call" | custom-call | flops 1572864 | bytes 6291456 | tf_op jit(solution)/shard_map/fold_gain/pallas_call | solution.py:86
  8.1 0.9 %collective-permute-done.3.refs_1_ = bf16[256,256]{1,0:T(8,128)(2,1)S(1)} collective-permute-done((bf16[256,256]{1,0:T(8,128)(2,1)S(1)}, bf16[256,256]{1,0:T(8,128)(2,1)S(1)}, u32[]{:S(2)}, u32[]{:S(2)}) %collective-permute-start.3) | collective-permute-done | bytes 131104 | tf_op jit(solution)/shard_map/ppermute | solution.py:33
  9.0 0.4 collective-permute-start.4
  9.4 1.6 %collective-permute-start.1 = (bf16[256,256]{1,0:T(8,128)(2,1)S(1)}, bf16[256,256]{1,0:T(8,128)(2,1)S(1)}, u32[]{:S(2)}, u32[]{:S(2)}) collective-permute-start(bf16[256,256]{1,0:T(8,128)(2,1)S(1)} %collective-permute-done.refs_0_), channel_id=1, source_target_pairs={{0,2},{2,4},{4,6},{6,7},{7,5},{5,3},{3,1},{1,0},{8,10},{10,12},{12... | collective-permute-start | bytes 393224 | tf_op jit(solution)/shard_map/ppermute | solution.py:33
  11.7 1.6 %collective-permute-start.9 = (bf16[256,256]{1,0:T(8,128)(2,1)S(1)}, bf16[256,256]{1,0:T(8,128)(2,1)S(1)}, u32[]{:S(2)}, u32[]{:S(2)}) collective-permute-start(bf16[256,256]{1,0:T(8,128)(2,1)S(1)} %collective-permute-done.8.refs_3_), channel_id=1, source_target_pairs={{0,2},{2,4},{4,6},{6,7},{7,5},{5,3},{3,1},{1,0},{8,10},{10,12},{12... | collective-permute-start | bytes 393224 | tf_op jit(solution)/shard_map/ppermute | solution.py:33
  13.3 1.6 %collective-permute-done.4.refs_1_ = bf16[256,256]{1,0:T(8,128)(2,1)S(1)} collective-permute-done((bf16[256,256]{1,0:T(8,128)(2,1)S(1)}, bf16[256,256]{1,0:T(8,128)(2,1)S(1)}, u32[]{:S(2)}, u32[]{:S(2)}) %collective-permute-start.4) | collective-permute-done | bytes 131104 | tf_op jit(solution)/shard_map/ppermute | solution.py:33
  15.4 1.6 %collective-permute-start.2 = (bf16[256,256]{1,0:T(8,128)(2,1)S(1)}, bf16[256,256]{1,0:T(8,128)(2,1)S(1)}, u32[]{:S(2)}, u32[]{:S(2)}) collective-permute-start(bf16[256,256]{1,0:T(8,128)(2,1)S(1)} %collective-permute-done.1.refs_0_), channel_id=1, source_target_pairs={{0,2},{2,4},{4,6},{6,7},{7,5},{5,3},{3,1},{1,0},{8,10},{10,12},{12... | collective-permute-start | bytes 393224 | tf_op jit(solution)/shard_map/ppermute | solution.py:33
  17.0 0.8 %collective-permute-done.7.refs_2_ = bf16[256,256]{1,0:T(8,128)(2,1)S(1)} collective-permute-done((bf16[256,256]{1,0:T(8,128)(2,1)S(1)}, bf16[256,256]{1,0:T(8,128)(2,1)S(1)}, u32[]{:S(2)}, u32[]{:S(2)}) %collective-permute-start.7) | collective-permute-done | bytes 131104 | tf_op jit(solution)/shard_map/ppermute | solution.py:33
  17.7 0.4 collective-permute-start.10
  18.2 1.6 %collective-permute-start.11 = (bf16[256,256]{1,0:T(8,128)(2,1)S(1)}, bf16[256,256]{1,0:T(8,128)(2,1)S(1)}, u32[]{:S(2)}, u32[]{:S(2)}) collective-permute-start(bf16[256,256]{1,0:T(8,128)(2,1)S(1)} %collective-permute-done.9.refs_3_), channel_id=1, source_target_pairs={{0,2},{2,4},{4,6},{6,7},{7,5},{5,3},{3,1},{1,0},{8,10},{10,12},{12... | collective-permute-start | bytes 393224 | tf_op jit(solution)/shard_map/ppermute | solution.py:33
  20.0 0.6 collective-permute-done.5.refs_1_
  21.1 1.6 %collective-permute-start.12 = (bf16[256,256]{1,0:T(8,128)(2,1)S(1)}, bf16[256,256]{1,0:T(8,128)(2,1)S(1)}, u32[]{:S(2)}, u32[]{:S(2)}) collective-permute-start(bf16[256,256]{1,0:T(8,128)(2,1)S(1)} %collective-permute-done.2.refs_0_), channel_id=1, source_target_pairs={{0,2},{2,4},{4,6},{6,7},{7,5},{5,3},{3,1},{1,0},{8,10},{10,12},{12... | collective-permute-start | bytes 393224 | tf_op jit(solution)/shard_map/ppermute | solution.py:33
  23.3 1.9 %project_begin.1.state = f32[512,896]{1,0:T(8,128)S(1)} custom-call(bf16[512,2048]{1,0:T(8,128)(2,1)S(1)} %place.5.wide, bf16[3,2048,256]{2,1,0:T(8,128)(2,1)S(1)} %get-tuple-element.54.w_ref), custom_call_target="tpu_custom_call" | custom-call | flops 1610612736 | bytes 5242880 | tf_op jit(solution)/shard_map/project_begin/pallas_call | solution.py:186
  25.6 0.5 collective-permute-done.12.refs_0_
  26.0 1.2 %project_finish.1 = (bf16[512,256]{1,0:T(8,128)(2,1)S(1)}, bf16[512,512]{1,0:T(8,128)(2,1)S(1)}, bf16[256,512]{1,0:T(8,128)(2,1)S(1)}, bf16[256,512]{1,0:T(8,128...) custom-call(f32[2]{0:T(128)S(1)} %broadcast_multiply_fusion.factor, ...), custom_call_target="tpu_custom_call" | custom-call | flops 201326592 | bytes 1048576 | tf_op jit(solution)/shard_map/project_finish/pallas_call | solution.py:208
  27.2 0.6 collective-permute-start.17
  27.8 1.5 %collective-permute-start.18 = (bf16[256,512]{1,0:T(8,128)(2,1)S(1)}, bf16[256,512]{1,0:T(8,128)(2,1)S(1)}, u32[]{:S(2)}, u32[]{:S(2)}) collective-permute-start(bf16[256,512]{1,0:T(8,128)(2,1)S(1)} %get-tuple-element.67), channel_id=1, source_target_pairs={{0,16},{8,24},{16,0},{24,8},{1,17},{9,25},{17,1},{25,9},{2,18},{10... | collective-permute-start | bytes 786440 | tf_op jit(solution)/shard_map/ppermute | solution.py:421
  29.3 0.5 collective-permute-start.16
  30.0 2.2 %attend.3.refs_3_ = f32[512,512]{1,0:T(8,128)S(1)} custom-call(s32[2]{0:T(128)S(1)} %pad_add_fusion.1.info, s32[2048]{0:T(1024)} %ids.7, s32[8,1,256]{2,1,0:T(1,128)} %bitcast.15, bf16[512,256]{1,0:T(8,128)(2,1)S(1)} %get-tuple-element.57.q_ref, bf16[512,512]{1,0:T(8,128)(2,1)S(1)} %get-tuple-element.58.refs_0_), custom_call_target="tpu_custom_call" | custom-call | flops 1048576 | bytes 1024 | tf_op jit(solution)/shard_map/attend/pallas_call | solution.py:347
  32.3 2.2 %attend.4.refs_2_ = f32[512,512]{1,0:T(8,128)S(1)} custom-call(s32[2]{0:T(128)S(1)} %pad_add_fusion.info, s32[2048]{0:T(1024)} %ids.7, s32[8,1,256]{2,1,0:T(1,128)} %bitcast.16, bf16[512,256]{1,0:T(8,128)(2,1)S(1)} %get-tuple-element.57.q_ref, bf16[160,512]{1,0:T(8,128)(2,1)S(1)} %collective-permute-done.14.refs_0_, ...), custom_call_target="tpu_custom_call" | custom-call | flops 1048576 | bytes 1024 | tf_op jit(solution)/shard_map/attend/pallas_call | solution.py:347
  34.5 2.6 %collective-permute-done.18.refs_1_ = bf16[256,512]{1,0:T(8,128)(2,1)S(1)} collective-permute-done((bf16[256,512]{1,0:T(8,128)(2,1)S(1)}, bf16[256,512]{1,0:T(8,128)(2,1)S(1)}, u32[]{:S(2)}, u32[]{:S(2)}) %collective-permute-start.18) | collective-permute-done | bytes 262176 | tf_op jit(solution)/shard_map/ppermute | solution.py:421
  37.1 0.5 collective-permute-start.20
  37.8 2.1 %attend.5.refs_2_ = f32[512,512]{1,0:T(8,128)S(1)} custom-call(s32[2]{0:T(128)S(1)} %pad_add_fusion.2.info, s32[2048]{0:T(1024)} %ids.7, s32[8,1,256]{2,1,0:T(1,128)} %bitcast.17, bf16[512,256]{1,0:T(8,128)(2,1)S(1)} %get-tuple-element.57.q_ref, bf16[256,512]{1,0:T(8,128)(2,1)S(1)} %collective-permute-done.17.refs_0_, ...), custom_call_target="tpu_custom_call" | custom-call | flops 1048576 | bytes 1024 | tf_op jit(solution)/shard_map/attend/pallas_call | solution.py:347
  39.9 2.9 %attend_last.1 = (bf16[256,256]{1,0:T(8,128)(2,1)S(1)}, bf16[256,256]{1,0:T(8,128)(2,1)S(1)}, bf16[256,256]{1,0:T(8,128)(2,1)S(1)}, bf16[256,256]{1,0:T(8,128)(2...) custom-call(s32[18]{0:T(128)S(1)} %stack.83.info, ...), custom_call_target="tpu_custom_call" | custom-call | flops 1048576 | bytes 1024 | tf_op jit(solution)/shard_map/attend_last/pallas_call | solution.py:347
  42.9 1.6 %collective-permute-start.31 = (bf16[256,256]{1,0:T(8,128)(2,1)S(1)}, bf16[256,256]{1,0:T(8,128)(2,1)S(1)}, u32[]{:S(2)}, u32[]{:S(2)}) collective-permute-start(bf16[256,256]{1,0:T(8,128)(2,1)S(1)} %get-tuple-element.85), channel_id=1, source_target_pairs={{0,2},{2,4},{4,6},{6,7},{7,5},{5,3},{3,1},{1,0},{8,10},{10,12},{12... | collective-permute-start | bytes 393224 | tf_op jit(solution)/shard_map/ppermute | solution.py:33
  45.0 0.6 collective-permute-start.24
  45.5 1.5 %collective-permute-start.21 = (bf16[256,256]{1,0:T(8,128)(2,1)S(1)}, bf16[256,256]{1,0:T(8,128)(2,1)S(1)}, u32[]{:S(2)}, u32[]{:S(2)}) collective-permute-start(bf16[256,256]{1,0:T(8,128)(2,1)S(1)} %get-tuple-element.74), channel_id=1, source_target_pairs={{0,2},{2,4},{4,6},{6,7},{7,5},{5,3},{3,1},{1,0},{8,10},{10,12},{12... | collective-permute-start | bytes 393224 | tf_op jit(solution)/shard_map/ppermute | solution.py:33
  47.0 2.3 %collective-permute-done.31 = bf16[256,256]{1,0:T(8,128)(2,1)S(1)} collective-permute-done((bf16[256,256]{1,0:T(8,128)(2,1)S(1)}, bf16[256,256]{1,0:T(8,128)(2,1)S(1)}, u32[]{:S(2)}, u32[]{:S(2)}) %collective-permute-start.31) | collective-permute-done | bytes 131104 | tf_op jit(solution)/shard_map/ppermute | solution.py:33
  49.3 1.6 %collective-permute-start.32 = (bf16[256,256]{1,0:T(8,128)(2,1)S(1)}, bf16[256,256]{1,0:T(8,128)(2,1)S(1)}, u32[]{:S(2)}, u32[]{:S(2)}) collective-permute-start(bf16[256,256]{1,0:T(8,128)(2,1)S(1)} %add_convert_fusion.4), channel_id=1, source_target_pairs={{0,2},{2,4},{4,6},{6,7},{7,5},{5,3},{3,1},{1,0},{8,10},{10,12},{12... | collective-permute-start | bytes 393224 | tf_op jit(solution)/shard_map/ppermute | solution.py:33
  51.0 0.5 collective-permute-start.28
  51.5 1.8 %collective-permute-done.24 = bf16[256,256]{1,0:T(8,128)(2,1)S(1)} collective-permute-done((bf16[256,256]{1,0:T(8,128)(2,1)S(1)}, bf16[256,256]{1,0:T(8,128)(2,1)S(1)}, u32[]{:S(2)}, u32[]{:S(2)}) %collective-permute-start.24) | collective-permute-done | bytes 131104 | tf_op jit(solution)/shard_map/ppermute | solution.py:33
  53.3 0.5 collective-permute-start.25
  53.8 1.6 %collective-permute-start.22 = (bf16[256,256]{1,0:T(8,128)(2,1)S(1)}, bf16[256,256]{1,0:T(8,128)(2,1)S(1)}, u32[]{:S(2)}, u32[]{:S(2)}) collective-permute-start(bf16[256,256]{1,0:T(8,128)(2,1)S(1)} %add_convert_fusion.11), channel_id=1, source_target_pairs={{0,2},{2,4},{4,6},{6,7},{7,5},{5,3},{3,1},{1,0},{8,10},{10,12},{12... | collective-permute-start | bytes 393224 | tf_op jit(solution)/shard_map/ppermute | solution.py:33
  55.5 1.6 %collective-permute-start.33 = (bf16[256,256]{1,0:T(8,128)(2,1)S(1)}, bf16[256,256]{1,0:T(8,128)(2,1)S(1)}, u32[]{:S(2)}, u32[]{:S(2)}) collective-permute-start(bf16[256,256]{1,0:T(8,128)(2,1)S(1)} %add_convert_fusion.3), channel_id=1, source_target_pairs={{0,2},{2,4},{4,6},{6,7},{7,5},{5,3},{3,1},{1,0},{8,10},{10,12},{12... | collective-permute-start | bytes 393224 | tf_op jit(solution)/shard_map/ppermute | solution.py:33
  57.1 0.6 collective-permute-start.29
  57.7 2.0 %collective-permute-done.25 = bf16[256,256]{1,0:T(8,128)(2,1)S(1)} collective-permute-done((bf16[256,256]{1,0:T(8,128)(2,1)S(1)}, bf16[256,256]{1,0:T(8,128)(2,1)S(1)}, u32[]{:S(2)}, u32[]{:S(2)}) %collective-permute-start.25) | collective-permute-done | bytes 131104 | tf_op jit(solution)/shard_map/ppermute | solution.py:33
  59.7 0.5 collective-permute-start.26
  60.2 1.7 %collective-permute-start.23 = (bf16[256,256]{1,0:T(8,128)(2,1)S(1)}, bf16[256,256]{1,0:T(8,128)(2,1)S(1)}, u32[]{:S(2)}, u32[]{:S(2)}) collective-permute-start(bf16[256,256]{1,0:T(8,128)(2,1)S(1)} %add_convert_fusion.10), channel_id=1, source_target_pairs={{0,2},{2,4},{4,6},{6,7},{7,5},{5,3},{3,1},{1,0},{8,10},{10,12},{12... | collective-permute-start | bytes 393224 | tf_op jit(solution)/shard_map/ppermute | solution.py:33
  61.9 1.6 %collective-permute-start.34 = (bf16[256,256]{1,0:T(8,128)(2,1)S(1)}, bf16[256,256]{1,0:T(8,128)(2,1)S(1)}, u32[]{:S(2)}, u32[]{:S(2)}) collective-permute-start(bf16[256,256]{1,0:T(8,128)(2,1)S(1)} %add_convert_fusion.2), channel_id=1, source_target_pairs={{0,2},{2,4},{4,6},{6,7},{7,5},{5,3},{3,1},{1,0},{8,10},{10,12},{12... | collective-permute-start | bytes 393224 | tf_op jit(solution)/shard_map/ppermute | solution.py:33
  63.6 0.5 collective-permute-start.30
  64.1 1.2 %collective-permute-done.26 = bf16[256,256]{1,0:T(8,128)(2,1)S(1)} collective-permute-done((bf16[256,256]{1,0:T(8,128)(2,1)S(1)}, bf16[256,256]{1,0:T(8,128)(2,1)S(1)}, u32[]{:S(2)}, u32[]{:S(2)}) %collective-permute-start.26) | collective-permute-done | bytes 131104 | tf_op jit(solution)/shard_map/ppermute | solution.py:33
  65.3 1.6 %collective-permute-done.34 = bf16[256,256]{1,0:T(8,128)(2,1)S(1)} collective-permute-done((bf16[256,256]{1,0:T(8,128)(2,1)S(1)}, bf16[256,256]{1,0:T(8,128)(2,1)S(1)}, u32[]{:S(2)}, u32[]{:S(2)}) %collective-permute-start.34) | collective-permute-done | bytes 131104 | tf_op jit(solution)/shard_map/ppermute | solution.py:33
  66.9 1.7 %collective-permute-done.30 = bf16[256,256]{1,0:T(8,128)(2,1)S(1)} collective-permute-done((bf16[256,256]{1,0:T(8,128)(2,1)S(1)}, bf16[256,256]{1,0:T(8,128)(2,1)S(1)}, u32[]{:S(2)}, u32[]{:S(2)}) %collective-permute-start.30) | collective-permute-done | bytes 131104 | tf_op jit(solution)/shard_map/ppermute | solution.py:33
  68.7 0.7 %pad_maximum_fusion = bf16[512,256]{1,0:T(8,128)(2,1)} fusion(bf16[256,256]{1,0:T(8,128)(2,1)S(1)} %get-tuple-element.93, bf16[256,256]{1,0:T(8,128)(2,1)S(1)} %get-tuple-element.94), kind=kLoop, calls=%fused_computation | loop fusion | flops 524288 | bytes 524288 | tf_op jit(solution)/shard_map/concatenate | solution.py:448
  (53 shorter events, 4.6 us)
Async XLA Ops:
  0.0 19.8 %copy-start = (f32[2]{0:T(128)S(1)}, f32[2]{0:T(128)}, u32[]{:S(2)}) copy-start(f32[2]{0:T(128)} %param.9) | copy-start | bytes 28
  1.0 7.1 %collective-permute-start = (bf16[256,256]{1,0:T(8,128)(2,1)S(1)}, bf16[256,256]{1,0:T(8,128)(2,1)S(1)}, u32[]{:S(2)}, u32[]{:S(2)}) collective-permute-start(bf16[256,256]{1,0:T(8,128)(2,1)S(1)} %get-tuple-element.92), channel_id=1, source_target_pairs={{0,2},{2,4},{4,6},{6,7},{7,5},{5,3},{3,1},{1,0},{8,10},{10,12},{12... | collective-permute-start | bytes 393224 | tf_op jit(solution)/shard_map/ppermute | solution.py:33
  2.6 6.4 %collective-permute-start.3 = (bf16[256,256]{1,0:T(8,128)(2,1)S(1)}, bf16[256,256]{1,0:T(8,128)(2,1)S(1)}, u32[]{:S(2)}, u32[]{:S(2)}) collective-permute-start(bf16[256,256]{1,0:T(8,128)(2,1)S(1)} %get-tuple-element.91), channel_id=1, source_target_pairs={{0,1},{2,0},{4,2},{6,4},{7,6},{5,7},{3,5},{1,3},{8,9},{10,8},{12,1... | collective-permute-start | bytes 393224 | tf_op jit(solution)/shard_map/ppermute | solution.py:33
  3.1 8.2 %collective-permute-start.6 = (bf16[256,256]{1,0:T(8,128)(2,1)S(1)}, bf16[256,256]{1,0:T(8,128)(2,1)S(1)}, u32[]{:S(2)}, u32[]{:S(2)}) collective-permute-start(bf16[256,256]{1,0:T(8,128)(2,1)S(1)} %get-tuple-element.92), channel_id=1, source_target_pairs={{0,1},{2,0},{4,2},{6,4},{7,6},{5,7},{3,5},{1,3},{8,9},{10,8},{12,1... | collective-permute-start | bytes 393224 | tf_op jit(solution)/shard_map/ppermute | solution.py:33
  3.5 8.2 %collective-permute-start.8 = (bf16[256,256]{1,0:T(8,128)(2,1)S(1)}, bf16[256,256]{1,0:T(8,128)(2,1)S(1)}, u32[]{:S(2)}, u32[]{:S(2)}) collective-permute-start(bf16[256,256]{1,0:T(8,128)(2,1)S(1)} %get-tuple-element.91), channel_id=1, source_target_pairs={{0,2},{2,4},{4,6},{6,7},{7,5},{5,3},{3,1},{1,0},{8,10},{10,12},{12... | collective-permute-start | bytes 393224 | tf_op jit(solution)/shard_map/ppermute | solution.py:33
  9.0 5.9 %collective-permute-start.4 = (bf16[256,256]{1,0:T(8,128)(2,1)S(1)}, bf16[256,256]{1,0:T(8,128)(2,1)S(1)}, u32[]{:S(2)}, u32[]{:S(2)}) collective-permute-start(bf16[256,256]{1,0:T(8,128)(2,1)S(1)} %collective-permute-done.3.refs_1_), channel_id=1, source_target_pairs={{0,1},{2,0},{4,2},{6,4},{7,6},{5,7},{3,5},{1,3},{8,9},{10,8},{12,1... | collective-permute-start | bytes 393224 | tf_op jit(solution)/shard_map/ppermute | solution.py:33
  9.4 5.9 %collective-permute-start.1 = (bf16[256,256]{1,0:T(8,128)(2,1)S(1)}, bf16[256,256]{1,0:T(8,128)(2,1)S(1)}, u32[]{:S(2)}, u32[]{:S(2)}) collective-permute-start(bf16[256,256]{1,0:T(8,128)(2,1)S(1)} %collective-permute-done.refs_0_), channel_id=1, source_target_pairs={{0,2},{2,4},{4,6},{6,7},{7,5},{5,3},{3,1},{1,0},{8,10},{10,12},{12... | collective-permute-start | bytes 393224 | tf_op jit(solution)/shard_map/ppermute | solution.py:33
  11.3 6.5 %collective-permute-start.7 = (bf16[256,256]{1,0:T(8,128)(2,1)S(1)}, bf16[256,256]{1,0:T(8,128)(2,1)S(1)}, u32[]{:S(2)}, u32[]{:S(2)}) collective-permute-start(bf16[256,256]{1,0:T(8,128)(2,1)S(1)} %collective-permute-done.6.refs_2_), channel_id=1, source_target_pairs={{0,1},{2,0},{4,2},{6,4},{7,6},{5,7},{3,5},{1,3},{8,9},{10,8},{12,1... | collective-permute-start | bytes 393224 | tf_op jit(solution)/shard_map/ppermute | solution.py:33
  11.7 6.5 %collective-permute-start.9 = (bf16[256,256]{1,0:T(8,128)(2,1)S(1)}, bf16[256,256]{1,0:T(8,128)(2,1)S(1)}, u32[]{:S(2)}, u32[]{:S(2)}) collective-permute-start(bf16[256,256]{1,0:T(8,128)(2,1)S(1)} %collective-permute-done.8.refs_3_), channel_id=1, source_target_pairs={{0,2},{2,4},{4,6},{6,7},{7,5},{5,3},{3,1},{1,0},{8,10},{10,12},{12... | collective-permute-start | bytes 393224 | tf_op jit(solution)/shard_map/ppermute | solution.py:33
  14.9 5.7 %collective-permute-start.5 = (bf16[256,256]{1,0:T(8,128)(2,1)S(1)}, bf16[256,256]{1,0:T(8,128)(2,1)S(1)}, u32[]{:S(2)}, u32[]{:S(2)}) collective-permute-start(bf16[256,256]{1,0:T(8,128)(2,1)S(1)} %collective-permute-done.4.refs_1_), channel_id=1, source_target_pairs={{0,1},{2,0},{4,2},{6,4},{7,6},{5,7},{3,5},{1,3},{8,9},{10,8},{12,1... | collective-permute-start | bytes 393224 | tf_op jit(solution)/shard_map/ppermute | solution.py:33
  15.4 5.7 %collective-permute-start.2 = (bf16[256,256]{1,0:T(8,128)(2,1)S(1)}, bf16[256,256]{1,0:T(8,128)(2,1)S(1)}, u32[]{:S(2)}, u32[]{:S(2)}) collective-permute-start(bf16[256,256]{1,0:T(8,128)(2,1)S(1)} %collective-permute-done.1.refs_0_), channel_id=1, source_target_pairs={{0,2},{2,4},{4,6},{6,7},{7,5},{5,3},{3,1},{1,0},{8,10},{10,12},{12... | collective-permute-start | bytes 393224 | tf_op jit(solution)/shard_map/ppermute | solution.py:33
  17.7 5.3 %collective-permute-start.10 = (bf16[256,256]{1,0:T(8,128)(2,1)S(1)}, bf16[256,256]{1,0:T(8,128)(2,1)S(1)}, u32[]{:S(2)}, u32[]{:S(2)}) collective-permute-start(bf16[256,256]{1,0:T(8,128)(2,1)S(1)} %collective-permute-done.7.refs_2_), channel_id=1, source_target_pairs={{0,1},{2,0},{4,2},{6,4},{7,6},{5,7},{3,5},{1,3},{8,9},{10,8},{12,1... | collective-permute-start | bytes 393224 | tf_op jit(solution)/shard_map/ppermute | solution.py:33
  18.2 5.0 %collective-permute-start.11 = (bf16[256,256]{1,0:T(8,128)(2,1)S(1)}, bf16[256,256]{1,0:T(8,128)(2,1)S(1)}, u32[]{:S(2)}, u32[]{:S(2)}) collective-permute-start(bf16[256,256]{1,0:T(8,128)(2,1)S(1)} %collective-permute-done.9.refs_3_), channel_id=1, source_target_pairs={{0,2},{2,4},{4,6},{6,7},{7,5},{5,3},{3,1},{1,0},{8,10},{10,12},{12... | collective-permute-start | bytes 393224 | tf_op jit(solution)/shard_map/ppermute | solution.py:33
  20.6 5.0 %collective-permute-start.13 = (bf16[256,256]{1,0:T(8,128)(2,1)S(1)}, bf16[256,256]{1,0:T(8,128)(2,1)S(1)}, u32[]{:S(2)}, u32[]{:S(2)}) collective-permute-start(bf16[256,256]{1,0:T(8,128)(2,1)S(1)} %collective-permute-done.5.refs_1_), channel_id=1, source_target_pairs={{0,1},{2,0},{4,2},{6,4},{7,6},{5,7},{3,5},{1,3},{8,9},{10,8},{12,1... | collective-permute-start | bytes 393224 | tf_op jit(solution)/shard_map/ppermute | solution.py:33
  21.1 5.0 %collective-permute-start.12 = (bf16[256,256]{1,0:T(8,128)(2,1)S(1)}, bf16[256,256]{1,0:T(8,128)(2,1)S(1)}, u32[]{:S(2)}, u32[]{:S(2)}) collective-permute-start(bf16[256,256]{1,0:T(8,128)(2,1)S(1)} %collective-permute-done.2.refs_0_), channel_id=1, source_target_pairs={{0,2},{2,4},{4,6},{6,7},{7,5},{5,3},{3,1},{1,0},{8,10},{10,12},{12... | collective-permute-start | bytes 393224 | tf_op jit(solution)/shard_map/ppermute | solution.py:33
  27.2 7.3 %collective-permute-start.17 = (bf16[256,512]{1,0:T(8,128)(2,1)S(1)}, bf16[256,512]{1,0:T(8,128)(2,1)S(1)}, u32[]{:S(2)}, u32[]{:S(2)}) collective-permute-start(bf16[256,512]{1,0:T(8,128)(2,1)S(1)} %get-tuple-element.66), channel_id=1, source_target_pairs={{0,16},{8,24},{16,0},{24,8},{1,17},{9,25},{17,1},{25,9},{2,18},{10... | collective-permute-start | bytes 786440 | tf_op jit(solution)/shard_map/ppermute | solution.py:421
  27.8 9.3 %collective-permute-start.18 = (bf16[256,512]{1,0:T(8,128)(2,1)S(1)}, bf16[256,512]{1,0:T(8,128)(2,1)S(1)}, u32[]{:S(2)}, u32[]{:S(2)}) collective-permute-start(bf16[256,512]{1,0:T(8,128)(2,1)S(1)} %get-tuple-element.67), channel_id=1, source_target_pairs={{0,16},{8,24},{16,0},{24,8},{1,17},{9,25},{17,1},{25,9},{2,18},{10... | collective-permute-start | bytes 786440 | tf_op jit(solution)/shard_map/ppermute | solution.py:421
  29.3 2.9 %collective-permute-start.15 = (bf16[176,512]{1,0:T(8,128)(2,1)S(1)}, bf16[176,512]{1,0:T(8,128)(2,1)S(1)}, u32[]{:S(2)}, u32[]{:S(2)}) collective-permute-start(bf16[176,512]{1,0:T(8,128)(2,1)S(1)} %get-tuple-element.60), channel_id=1, source_target_pairs={{0,8},{8,0},{16,24},{24,16},{1,9},{9,1},{17,25},{25,17},{2,10},{10... | collective-permute-start | bytes 540680 | tf_op jit(solution)/shard_map/ppermute | solution.py:39
  29.3 2.9 %collective-permute-start.16 = (bf16[176,512]{1,0:T(8,128)(2,1)S(1)}, bf16[176,512]{1,0:T(8,128)(2,1)S(1)}, u32[]{:S(2)}, u32[]{:S(2)}) collective-permute-start(bf16[176,512]{1,0:T(8,128)(2,1)S(1)} %get-tuple-element.61), channel_id=1, source_target_pairs={{0,8},{8,0},{16,24},{24,16},{1,9},{9,1},{17,25},{25,17},{2,10},{10... | collective-permute-start | bytes 540680 | tf_op jit(solution)/shard_map/ppermute | solution.py:39
  29.8 2.4 %collective-permute-start.14 = (bf16[160,512]{1,0:T(8,128)(2,1)S(1)}, bf16[160,512]{1,0:T(8,128)(2,1)S(1)}, u32[]{:S(2)}, u32[]{:S(2)}) collective-permute-start(bf16[160,512]{1,0:T(8,128)(2,1)S(1)} %get-tuple-element.59), channel_id=1, source_target_pairs={{0,8},{8,0},{16,24},{24,16},{1,9},{9,1},{17,25},{25,17},{2,10},{10... | collective-permute-start | bytes 491528 | tf_op jit(solution)/shard_map/ppermute | solution.py:39
  37.1 2.8 %collective-permute-start.19 = (bf16[256,512]{1,0:T(8,128)(2,1)S(1)}, bf16[256,512]{1,0:T(8,128)(2,1)S(1)}, u32[]{:S(2)}, u32[]{:S(2)}) collective-permute-start(bf16[256,512]{1,0:T(8,128)(2,1)S(1)} %collective-permute-done.17.refs_0_), channel_id=1, source_target_pairs={{0,8},{8,0},{16,24},{24,16},{1,9},{9,1},{17,25},{25,17},{2,10},{10... | collective-permute-start | bytes 786440 | tf_op jit(solution)/shard_map/ppermute | solution.py:39
  37.1 2.8 %collective-permute-start.20 = (bf16[256,512]{1,0:T(8,128)(2,1)S(1)}, bf16[256,512]{1,0:T(8,128)(2,1)S(1)}, u32[]{:S(2)}, u32[]{:S(2)}) collective-permute-start(bf16[256,512]{1,0:T(8,128)(2,1)S(1)} %collective-permute-done.18.refs_1_), channel_id=1, source_target_pairs={{0,8},{8,0},{16,24},{24,16},{1,9},{9,1},{17,25},{25,17},{2,10},{10... | collective-permute-start | bytes 786440 | tf_op jit(solution)/shard_map/ppermute | solution.py:39
  42.9 6.4 %collective-permute-start.31 = (bf16[256,256]{1,0:T(8,128)(2,1)S(1)}, bf16[256,256]{1,0:T(8,128)(2,1)S(1)}, u32[]{:S(2)}, u32[]{:S(2)}) collective-permute-start(bf16[256,256]{1,0:T(8,128)(2,1)S(1)} %get-tuple-element.85), channel_id=1, source_target_pairs={{0,2},{2,4},{4,6},{6,7},{7,5},{5,3},{3,1},{1,0},{8,10},{10,12},{12... | collective-permute-start | bytes 393224 | tf_op jit(solution)/shard_map/ppermute | solution.py:33
  44.5 6.5 %collective-permute-start.27 = (bf16[256,256]{1,0:T(8,128)(2,1)S(1)}, bf16[256,256]{1,0:T(8,128)(2,1)S(1)}, u32[]{:S(2)}, u32[]{:S(2)}) collective-permute-start(bf16[256,256]{1,0:T(8,128)(2,1)S(1)} %get-tuple-element.81), channel_id=1, source_target_pairs={{0,1},{2,0},{4,2},{6,4},{7,6},{5,7},{3,5},{1,3},{8,9},{10,8},{12,1... | collective-permute-start | bytes 393224 | tf_op jit(solution)/shard_map/ppermute | solution.py:33
  45.0 8.3 %collective-permute-start.24 = (bf16[256,256]{1,0:T(8,128)(2,1)S(1)}, bf16[256,256]{1,0:T(8,128)(2,1)S(1)}, u32[]{:S(2)}, u32[]{:S(2)}) collective-permute-start(bf16[256,256]{1,0:T(8,128)(2,1)S(1)} %get-tuple-element.77), channel_id=1, source_target_pairs={{0,1},{2,0},{4,2},{6,4},{7,6},{5,7},{3,5},{1,3},{8,9},{10,8},{12,1... | collective-permute-start | bytes 393224 | tf_op jit(solution)/shard_map/ppermute | solution.py:33
  45.5 8.3 %collective-permute-start.21 = (bf16[256,256]{1,0:T(8,128)(2,1)S(1)}, bf16[256,256]{1,0:T(8,128)(2,1)S(1)}, u32[]{:S(2)}, u32[]{:S(2)}) collective-permute-start(bf16[256,256]{1,0:T(8,128)(2,1)S(1)} %get-tuple-element.74), channel_id=1, source_target_pairs={{0,2},{2,4},{4,6},{6,7},{7,5},{5,3},{3,1},{1,0},{8,10},{10,12},{12... | collective-permute-start | bytes 393224 | tf_op jit(solution)/shard_map/ppermute | solution.py:33
  49.3 6.1 %collective-permute-start.32 = (bf16[256,256]{1,0:T(8,128)(2,1)S(1)}, bf16[256,256]{1,0:T(8,128)(2,1)S(1)}, u32[]{:S(2)}, u32[]{:S(2)}) collective-permute-start(bf16[256,256]{1,0:T(8,128)(2,1)S(1)} %add_convert_fusion.4), channel_id=1, source_target_pairs={{0,2},{2,4},{4,6},{6,7},{7,5},{5,3},{3,1},{1,0},{8,10},{10,12},{12... | collective-permute-start | bytes 393224 | tf_op jit(solution)/shard_map/ppermute | solution.py:33
  51.0 6.1 %collective-permute-start.28 = (bf16[256,256]{1,0:T(8,128)(2,1)S(1)}, bf16[256,256]{1,0:T(8,128)(2,1)S(1)}, u32[]{:S(2)}, u32[]{:S(2)}) collective-permute-start(bf16[256,256]{1,0:T(8,128)(2,1)S(1)} %add_convert_fusion.7), channel_id=1, source_target_pairs={{0,1},{2,0},{4,2},{6,4},{7,6},{5,7},{3,5},{1,3},{8,9},{10,8},{12,1... | collective-permute-start | bytes 393224 | tf_op jit(solution)/shard_map/ppermute | solution.py:33
  53.3 6.4 %collective-permute-start.25 = (bf16[256,256]{1,0:T(8,128)(2,1)S(1)}, bf16[256,256]{1,0:T(8,128)(2,1)S(1)}, u32[]{:S(2)}, u32[]{:S(2)}) collective-permute-start(bf16[256,256]{1,0:T(8,128)(2,1)S(1)} %add_convert_fusion.9), channel_id=1, source_target_pairs={{0,1},{2,0},{4,2},{6,4},{7,6},{5,7},{3,5},{1,3},{8,9},{10,8},{12,1... | collective-permute-start | bytes 393224 | tf_op jit(solution)/shard_map/ppermute | solution.py:33
  53.8 6.3 %collective-permute-start.22 = (bf16[256,256]{1,0:T(8,128)(2,1)S(1)}, bf16[256,256]{1,0:T(8,128)(2,1)S(1)}, u32[]{:S(2)}, u32[]{:S(2)}) collective-permute-start(bf16[256,256]{1,0:T(8,128)(2,1)S(1)} %add_convert_fusion.11), channel_id=1, source_target_pairs={{0,2},{2,4},{4,6},{6,7},{7,5},{5,3},{3,1},{1,0},{8,10},{10,12},{12... | collective-permute-start | bytes 393224 | tf_op jit(solution)/shard_map/ppermute | solution.py:33
  55.5 6.4 %collective-permute-start.33 = (bf16[256,256]{1,0:T(8,128)(2,1)S(1)}, bf16[256,256]{1,0:T(8,128)(2,1)S(1)}, u32[]{:S(2)}, u32[]{:S(2)}) collective-permute-start(bf16[256,256]{1,0:T(8,128)(2,1)S(1)} %add_convert_fusion.3), channel_id=1, source_target_pairs={{0,2},{2,4},{4,6},{6,7},{7,5},{5,3},{3,1},{1,0},{8,10},{10,12},{12... | collective-permute-start | bytes 393224 | tf_op jit(solution)/shard_map/ppermute | solution.py:33
  57.1 6.4 %collective-permute-start.29 = (bf16[256,256]{1,0:T(8,128)(2,1)S(1)}, bf16[256,256]{1,0:T(8,128)(2,1)S(1)}, u32[]{:S(2)}, u32[]{:S(2)}) collective-permute-start(bf16[256,256]{1,0:T(8,128)(2,1)S(1)} %add_convert_fusion.6), channel_id=1, source_target_pairs={{0,1},{2,0},{4,2},{6,4},{7,6},{5,7},{3,5},{1,3},{8,9},{10,8},{12,1... | collective-permute-start | bytes 393224 | tf_op jit(solution)/shard_map/ppermute | solution.py:33
  59.7 5.6 %collective-permute-start.26 = (bf16[256,256]{1,0:T(8,128)(2,1)S(1)}, bf16[256,256]{1,0:T(8,128)(2,1)S(1)}, u32[]{:S(2)}, u32[]{:S(2)}) collective-permute-start(bf16[256,256]{1,0:T(8,128)(2,1)S(1)} %add_convert_fusion.8), channel_id=1, source_target_pairs={{0,1},{2,0},{4,2},{6,4},{7,6},{5,7},{3,5},{1,3},{8,9},{10,8},{12,1... | collective-permute-start | bytes 393224 | tf_op jit(solution)/shard_map/ppermute | solution.py:33
  60.2 5.1 %collective-permute-start.23 = (bf16[256,256]{1,0:T(8,128)(2,1)S(1)}, bf16[256,256]{1,0:T(8,128)(2,1)S(1)}, u32[]{:S(2)}, u32[]{:S(2)}) collective-permute-start(bf16[256,256]{1,0:T(8,128)(2,1)S(1)} %add_convert_fusion.10), channel_id=1, source_target_pairs={{0,2},{2,4},{4,6},{6,7},{7,5},{5,3},{3,1},{1,0},{8,10},{10,12},{12... | collective-permute-start | bytes 393224 | tf_op jit(solution)/shard_map/ppermute | solution.py:33
  61.9 5.0 %collective-permute-start.34 = (bf16[256,256]{1,0:T(8,128)(2,1)S(1)}, bf16[256,256]{1,0:T(8,128)(2,1)S(1)}, u32[]{:S(2)}, u32[]{:S(2)}) collective-permute-start(bf16[256,256]{1,0:T(8,128)(2,1)S(1)} %add_convert_fusion.2), channel_id=1, source_target_pairs={{0,2},{2,4},{4,6},{6,7},{7,5},{5,3},{3,1},{1,0},{8,10},{10,12},{12... | collective-permute-start | bytes 393224 | tf_op jit(solution)/shard_map/ppermute | solution.py:33
  63.6 5.0 %collective-permute-start.30 = (bf16[256,256]{1,0:T(8,128)(2,1)S(1)}, bf16[256,256]{1,0:T(8,128)(2,1)S(1)}, u32[]{:S(2)}, u32[]{:S(2)}) collective-permute-start(bf16[256,256]{1,0:T(8,128)(2,1)S(1)} %add_convert_fusion.5), channel_id=1, source_target_pairs={{0,1},{2,0},{4,2},{6,4},{7,6},{5,7},{3,5},{1,3},{8,9},{10,8},{12,1... | collective-permute-start | bytes 393224 | tf_op jit(solution)/shard_map/ppermute | solution.py:33

commit v20 on v19

--- a/solution.py
+++ b/solution.py
@@ -148,12 +148,13 @@
 
 def finish_kernel(head_size, factor, state, w_ref, *refs):
     count = 2
-    lasts, (q_ref, kv_ref), rest = refs[:count], refs[count : count + 2], refs[count + 2 :]
-    halves, pieces = rest[:count], rest[count:]
+    lasts, q_ref = refs[:count], refs[count]
+    halves, pieces = refs[count + 1 : 2 * count + 1], refs[2 * count + 1 :]
     rows, width = lasts[0].shape
     depth, out_width = w_ref.shape[1:]
     for stream, last in enumerate(lasts):
         here = slice(stream * rows, (stream + 1) * rows)
+        kv_ref = halves[stream]
         q, k, v = (
             state[here, group * out_width : (group + 1) * out_width]
             + jnp.dot(last[...], w_ref[group, depth - width :, :], preferred_element_type=F32)
@@ -170,14 +171,18 @@
             qh, kh = q[:, lanes], k[:, lanes]
             q_size = lax.rsqrt(jnp.sum(qh * qh, axis=-1, keepdims=True) + 1e-06)
             k_size = lax.rsqrt(jnp.sum(kh * kh, axis=-1, keepdims=True) + 1e-06)
-            q_ref[here, lanes] = (qh * (q_size * factor[head])).astype(BF16)
-            kv_ref[here, lanes] = (kh * k_size).astype(BF16)
-        kv_ref[here, out_width:] = v.astype(BF16)
-        halves[stream][...] = kv_ref[here, :]
+            q_ref[here, lanes] = (qh * (q_size * (factor[head] * LOG2E))).astype(BF16)
+            kv_ref[:, lanes] = (kh * k_size).astype(BF16)
+        kv_ref[:, out_width:] = v.astype(BF16)
     start = 0
     for piece in pieces:
-        piece[...] = kv_ref[start : start + piece.shape[0], :]
-        start += piece.shape[0]
+        end = start + piece.shape[0]
+        for stream, half in enumerate(halves):
+            base = stream * rows
+            low, high = max(start, base), min(end, base + rows)
+            if low < high:
+                piece[low - start : high - start, :] = half[low - base : high - base, :]
+        start = end
 
 
 def project_begin(wide, weights, blocks):
@@ -209,17 +214,16 @@
         functools.partial(finish_kernel, head_size),
         out_shape=(
             pltpu.VMEM((total, out_width), BF16),
-            pltpu.VMEM((total, 2 * out_width), BF16),
             *[pltpu.VMEM((size, 2 * out_width), BF16) for size in sizes],
         ),
         in_specs=[SMEM] + [VMEM] * (2 + len(lasts)),
-        out_specs=(VMEM,) * (2 + len(sizes)),
+        out_specs=(VMEM,) * (1 + len(sizes)),
         compiler_params=pltpu.CompilerParams(vmem_limit_bytes=16 << 20),
         cost_estimate=pl.CostEstimate(
             flops=6 * total * width * out_width, bytes_accessed=8 * total * out_width, transcendentals=0
         ),
         name="project_finish",
-    )(factor, in_vmem(state), in_vmem(weights), *map(in_vmem, lasts))
+    )(in_hbm(factor), in_vmem(state), in_vmem(weights), *map(in_vmem, lasts))
 
 
 def attend_kernel(
@@ -407,8 +411,8 @@
                 targets.append((s * half, (2 * step - 1 + way) * width))
     wide = placed(targets, blocks, wide)
     lasts = [held[0][0], held[1][1]]
-    state, factor = lax.optimization_barrier((project_begin(wide, weights, ring), head_scale * LOG2E))
-    query, kv, *parts = project_finish(factor, state, weights, lasts, 3, head_size)
+    state = project_begin(wide, weights, ring)
+    query, *parts = project_finish(head_scale, state, weights, lasts, 3, head_size)
     halves, pieces = parts[:2], parts[2:]
 
     far, straight, crossed = [], [], []
@@ -420,7 +424,7 @@
             shift = [(2 * a + b, 2 * ((a + step) % outer) + b) for a in range(outer) for b in (0, 1)]
             far.append([lax.ppermute(part, "seq", shift) for part in halves])
     first = [seq_at * rows]
-    (acc,) = attend(numbers(straight[:1] + first), scale_ids, query, [[kv]], head_size)
+    (acc,) = attend(numbers(straight[:1] + first), scale_ids, query, [halves], head_size)
     near = [[swapped(piece, seqs) for piece in pieces]]
     acc, near = lax.optimization_barrier((acc, near))
     (acc,) = attend(numbers(crossed[:1] + first), scale_ids, query, near, head_size, acc)

time: 70.2 us -> 69.4 us (0.989)
  waiting for transfers between devices: 18.7 us -> 16.8 us
  starting transfers between devices: 32.1 us -> 33 us
    ppermute x28, waiting for transfers between devices: 16.1 us -> 14.4 us  [along(): lax.ppermute(value, 'head', [(order[p], order[(p + step) % count]) for p...]
    ppermute x28, starting transfers between devices: 29 us -> 29.9 us  [along(): lax.ppermute(value, 'head', [(order[p], order[(p + step) % count]) for p...]
  transfers between devices with their start and end apart: 35 -> 35, of which waited for: 16 -> 14; matrix products, arithmetic and copies ran while one was open for 1% -> 1% of each run, Pallas kernels for 17% -> 17%
where the time goes in v20:
time: 69.4 us; the launch traced here: 68.5 us
  starting transfers between devices  33 us (48%)
  waiting for transfers between devices  16.8 us (24%)
  Pallas kernels  16 us (23%)
  other arithmetic  1.39 us (2%)
  local copies, waits for them, and re-layouts  1.16 us (2%)
    ppermute x28, starting transfers between devices, along(): lax.ppermute(value, 'head', [(order[p], order[(p + step) % count]) for p...  29.9 us
    ppermute x28, waiting for transfers between devices, along(): lax.ppermute(value, 'head', [(order[p], order[(p + step) % count]) for p...  14.4 us
    pallas_call x4, Pallas kernels, attend(): pl.pallas_call(functools.partial(attend_kernel, head_size, (len(blocks),...  9.55 us
    pallas_call x1, Pallas kernels, fold_gain(): pl.pallas_call(functools.partial(fold_kernel, order), out_shape=(pltpu.VM...  2.88 us
    ppermute x2, waiting for transfers between devices, body(): far.append([lax.ppermute(part, 'seq', shift) for part in halves])  2.42 us
    ppermute x2, starting transfers between devices, body(): far.append([lax.ppermute(part, 'seq', shift) for part in halves])  2.09 us
    pallas_call x1, Pallas kernels, project_begin(): pl.pallas_call(functools.partial(begin_kernel, blocks), out_shape=pltpu.V...  1.91 us
  transfers between devices with their start and end apart: 35, of which 14 were waited for; matrix products, arithmetic and copies ran while one was open for 1% of the time, Pallas kernels for 17%

profile of v20, /device:TPU:10, one launch (start us, length us, event | category | flops | bytes accessed | tf_op | source)
XLA Modules:
  0.0 68.5 jit_solution(16279975382156080005)
XLA Ops:
  0.0 1.0 %fusion = (bf16[256,256]{1,0:T(8,128)(2,1)S(1)}, bf16[256,256]{1,0:T(8,128)(2,1)S(1)}) fusion(bf16[512,256]{1,0:T(8,128)(2,1)} %tokens.1), kind=kLoop, calls=%fused_computation.16 | loop fusion | bytes 524288 | tf_op jit(solution)/shard_map/slice | solution.py:390
  1.0 0.5 collective-permute-start.3
  1.5 1.6 %collective-permute-start = (bf16[256,256]{1,0:T(8,128)(2,1)S(1)}, bf16[256,256]{1,0:T(8,128)(2,1)S(1)}, u32[]{:S(2)}, u32[]{:S(2)}) collective-permute-start(bf16[256,256]{1,0:T(8,128)(2,1)S(1)} %get-tuple-element.86), channel_id=1, source_target_pairs={{0,2},{2,4},{4,6},{6,7},{7,5},{5,3},{3,1},{1,0},{8,10},{10,12},{12... | collective-permute-start | bytes 393224 | tf_op jit(solution)/shard_map/ppermute | solution.py:33
  3.1 0.4 collective-permute-start.6
  3.5 1.6 %collective-permute-start.8 = (bf16[256,256]{1,0:T(8,128)(2,1)S(1)}, bf16[256,256]{1,0:T(8,128)(2,1)S(1)}, u32[]{:S(2)}, u32[]{:S(2)}) collective-permute-start(bf16[256,256]{1,0:T(8,128)(2,1)S(1)} %get-tuple-element.85), channel_id=1, source_target_pairs={{0,2},{2,4},{4,6},{6,7},{7,5},{5,3},{3,1},{1,0},{8,10},{10,12},{12... | collective-permute-start | bytes 393224 | tf_op jit(solution)/shard_map/ppermute | solution.py:33
  5.2 2.9 %fold_gain.1 = (bf16[3,2048,256]{2,1,0:T(8,128)(2,1)S(1)}, bf16[512,2048]{1,0:T(8,128)(2,1)S(1)}) custom-call(s32[8]{0:T(128)S(1)} %stack.84.at, f32[16,128]{1,0:T(8,128)} %bitcast.19, bf16[3,2048,256]{2,1,0:T(8,128)(2,1)} %w_hbm.1, bf16[512,256]{1,0:T(8,128)(2,1)} %tokens.1), custom_call_target="tpu_custom_call" | custom-call | flops 1572864 | bytes 6291456 | tf_op jit(solution)/shard_map/fold_gain/pallas_call | solution.py:86
  8.1 0.5 collective-permute-start.4
  8.6 1.6 %collective-permute-start.1 = (bf16[256,256]{1,0:T(8,128)(2,1)S(1)}, bf16[256,256]{1,0:T(8,128)(2,1)S(1)}, u32[]{:S(2)}, u32[]{:S(2)}) collective-permute-start(bf16[256,256]{1,0:T(8,128)(2,1)S(1)} %collective-permute-done.refs_0_), channel_id=1, source_target_pairs={{0,2},{2,4},{4,6},{6,7},{7,5},{5,3},{3,1},{1,0},{8,10},{10,12},{12... | collective-permute-start | bytes 393224 | tf_op jit(solution)/shard_map/ppermute | solution.py:33
  10.2 0.5 collective-permute-start.7
  10.6 1.6 %collective-permute-start.9 = (bf16[256,256]{1,0:T(8,128)(2,1)S(1)}, bf16[256,256]{1,0:T(8,128)(2,1)S(1)}, u32[]{:S(2)}, u32[]{:S(2)}) collective-permute-start(bf16[256,256]{1,0:T(8,128)(2,1)S(1)} %collective-permute-done.8.refs_3_), channel_id=1, source_target_pairs={{0,2},{2,4},{4,6},{6,7},{7,5},{5,3},{3,1},{1,0},{8,10},{10,12},{12... | collective-permute-start | bytes 393224 | tf_op jit(solution)/shard_map/ppermute | solution.py:33
  12.2 1.9 %collective-permute-done.4.refs_1_ = bf16[256,256]{1,0:T(8,128)(2,1)S(1)} collective-permute-done((bf16[256,256]{1,0:T(8,128)(2,1)S(1)}, bf16[256,256]{1,0:T(8,128)(2,1)S(1)}, u32[]{:S(2)}, u32[]{:S(2)}) %collective-permute-start.4) | collective-permute-done | bytes 131104 | tf_op jit(solution)/shard_map/ppermute | solution.py:33
  14.6 1.6 %collective-permute-start.2 = (bf16[256,256]{1,0:T(8,128)(2,1)S(1)}, bf16[256,256]{1,0:T(8,128)(2,1)S(1)}, u32[]{:S(2)}, u32[]{:S(2)}) collective-permute-start(bf16[256,256]{1,0:T(8,128)(2,1)S(1)} %collective-permute-done.1.refs_0_), channel_id=1, source_target_pairs={{0,2},{2,4},{4,6},{6,7},{7,5},{5,3},{3,1},{1,0},{8,10},{10,12},{12... | collective-permute-start | bytes 393224 | tf_op jit(solution)/shard_map/ppermute | solution.py:33
  16.1 0.8 %collective-permute-done.7.refs_2_ = bf16[256,256]{1,0:T(8,128)(2,1)S(1)} collective-permute-done((bf16[256,256]{1,0:T(8,128)(2,1)S(1)}, bf16[256,256]{1,0:T(8,128)(2,1)S(1)}, u32[]{:S(2)}, u32[]{:S(2)}) %collective-permute-start.7) | collective-permute-done | bytes 131104 | tf_op jit(solution)/shard_map/ppermute | solution.py:33
  17.4 1.6 %collective-permute-start.11 = (bf16[256,256]{1,0:T(8,128)(2,1)S(1)}, bf16[256,256]{1,0:T(8,128)(2,1)S(1)}, u32[]{:S(2)}, u32[]{:S(2)}) collective-permute-start(bf16[256,256]{1,0:T(8,128)(2,1)S(1)} %collective-permute-done.9.refs_3_), channel_id=1, source_target_pairs={{0,2},{2,4},{4,6},{6,7},{7,5},{5,3},{3,1},{1,0},{8,10},{10,12},{12... | collective-permute-start | bytes 393224 | tf_op jit(solution)/shard_map/ppermute | solution.py:33
  19.2 0.6 collective-permute-done.5.refs_1_
  20.3 1.6 %collective-permute-start.12 = (bf16[256,256]{1,0:T(8,128)(2,1)S(1)}, bf16[256,256]{1,0:T(8,128)(2,1)S(1)}, u32[]{:S(2)}, u32[]{:S(2)}) collective-permute-start(bf16[256,256]{1,0:T(8,128)(2,1)S(1)} %collective-permute-done.2.refs_0_), channel_id=1, source_target_pairs={{0,2},{2,4},{4,6},{6,7},{7,5},{5,3},{3,1},{1,0},{8,10},{10,12},{12... | collective-permute-start | bytes 393224 | tf_op jit(solution)/shard_map/ppermute | solution.py:33
  22.5 1.9 %project_begin.1.state = f32[512,896]{1,0:T(8,128)S(1)} custom-call(bf16[512,2048]{1,0:T(8,128)(2,1)S(1)} %place.5.wide, bf16[3,2048,256]{2,1,0:T(8,128)(2,1)S(1)} %get-tuple-element.51.w_ref), custom_call_target="tpu_custom_call" | custom-call | flops 1610612736 | bytes 5242880 | tf_op jit(solution)/shard_map/project_begin/pallas_call | solution.py:191
  24.8 0.5 collective-permute-done.12.refs_0_
  25.2 1.3 %project_finish.1 = (bf16[512,256]{1,0:T(8,128)(2,1)S(1)}, bf16[256,512]{1,0:T(8,128)(2,1)S(1)}, bf16[256,512]{1,0:T(8,128)(2,1)S(1)}, bf16[160,512]{1,0:T(8,128...) custom-call(f32[2]{0:T(128)} %factor.1, f32[512,896]{1,0:T(8,128)S(1)} %project_begin.1.state, ...), custom_call_target="tpu_custom_call" | custom-call | flops 201326592 | bytes 1048576 | tf_op jit(solution)/shard_map/project_finish/pallas_call | solution.py:213
  26.5 0.5 collective-permute-start.17
  27.1 1.6 %collective-permute-start.18 = (bf16[256,512]{1,0:T(8,128)(2,1)S(1)}, bf16[256,512]{1,0:T(8,128)(2,1)S(1)}, u32[]{:S(2)}, u32[]{:S(2)}) collective-permute-start(bf16[256,512]{1,0:T(8,128)(2,1)S(1)} %get-tuple-element.54.refs_1_), channel_id=1, source_target_pairs={{0,16},{8,24},{16,0},{24,8},{1,17},{9,25},{17,1},{25,9},{2,18},{10... | collective-permute-start | bytes 786440 | tf_op jit(solution)/shard_map/ppermute | solution.py:425
  28.6 0.5 collective-permute-start.16
  29.3 2.2 %attend.3.refs_3_ = f32[512,512]{1,0:T(8,128)S(1)} custom-call(s32[2]{0:T(128)S(1)} %pad_add_fusion.1.info, s32[2048]{0:T(1024)} %ids.7, s32[8,1,256]{2,1,0:T(1,128)} %bitcast.15, bf16[512,256]{1,0:T(8,128)(2,1)S(1)} %get-tuple-element.52.q_ref, bf16[256,512]{1,0:T(8,128)(2,1)S(1)} %get-tuple-element.53.refs_0_, bf16[256,512]{1,0:T(8,128)(2,1)S(1)} %get-tuple-element.54.refs_1_), custom_call_target="tpu_custom_call" | custom-call | flops 1048576 | bytes 1024 | tf_op jit(solution)/shard_map/attend/pallas_call | solution.py:351
  31.6 2.2 %attend.4.refs_2_ = f32[512,512]{1,0:T(8,128)S(1)} custom-call(s32[2]{0:T(128)S(1)} %pad_add_fusion.info, s32[2048]{0:T(1024)} %ids.7, s32[8,1,256]{2,1,0:T(1,128)} %bitcast.16, bf16[512,256]{1,0:T(8,128)(2,1)S(1)} %get-tuple-element.52.q_ref, bf16[160,512]{1,0:T(8,128)(2,1)S(1)} %collective-permute-done.14.refs_0_, ...), custom_call_target="tpu_custom_call" | custom-call | flops 1048576 | bytes 1024 | tf_op jit(solution)/shard_map/attend/pallas_call | solution.py:351
  33.8 2.4 %collective-permute-done.18.refs_1_ = bf16[256,512]{1,0:T(8,128)(2,1)S(1)} collective-permute-done((bf16[256,512]{1,0:T(8,128)(2,1)S(1)}, bf16[256,512]{1,0:T(8,128)(2,1)S(1)}, u32[]{:S(2)}, u32[]{:S(2)}) %collective-permute-start.18) | collective-permute-done | bytes 262176 | tf_op jit(solution)/shard_map/ppermute | solution.py:425
  36.3 0.5 collective-permute-start.20
  36.9 2.1 %attend.5.refs_2_ = f32[512,512]{1,0:T(8,128)S(1)} custom-call(s32[2]{0:T(128)S(1)} %pad_add_fusion.2.info, s32[2048]{0:T(1024)} %ids.7, s32[8,1,256]{2,1,0:T(1,128)} %bitcast.17, bf16[512,256]{1,0:T(8,128)(2,1)S(1)} %get-tuple-element.52.q_ref, bf16[256,512]{1,0:T(8,128)(2,1)S(1)} %collective-permute-done.17.refs_0_, ...), custom_call_target="tpu_custom_call" | custom-call | flops 1048576 | bytes 1024 | tf_op jit(solution)/shard_map/attend/pallas_call | solution.py:351
  39.1 2.9 %attend_last.1 = (bf16[256,256]{1,0:T(8,128)(2,1)S(1)}, bf16[256,256]{1,0:T(8,128)(2,1)S(1)}, bf16[256,256]{1,0:T(8,128)(2,1)S(1)}, bf16[256,256]{1,0:T(8,128)(2...) custom-call(s32[18]{0:T(128)S(1)} %stack.83.info, ...), custom_call_target="tpu_custom_call" | custom-call | flops 1048576 | bytes 1024 | tf_op jit(solution)/shard_map/attend_last/pallas_call | solution.py:351
  42.0 1.6 %collective-permute-start.31 = (bf16[256,256]{1,0:T(8,128)(2,1)S(1)}, bf16[256,256]{1,0:T(8,128)(2,1)S(1)}, u32[]{:S(2)}, u32[]{:S(2)}) collective-permute-start(bf16[256,256]{1,0:T(8,128)(2,1)S(1)} %get-tuple-element.79), channel_id=1, source_target_pairs={{0,2},{2,4},{4,6},{6,7},{7,5},{5,3},{3,1},{1,0},{8,10},{10,12},{12... | collective-permute-start | bytes 393224 | tf_op jit(solution)/shard_map/ppermute | solution.py:33
  43.7 0.5 collective-permute-start.27
  44.1 1.5 %collective-permute-start.24 = (bf16[256,256]{1,0:T(8,128)(2,1)S(1)}, bf16[256,256]{1,0:T(8,128)(2,1)S(1)}, u32[]{:S(2)}, u32[]{:S(2)}) collective-permute-start(bf16[256,256]{1,0:T(8,128)(2,1)S(1)} %get-tuple-element.71), channel_id=1, source_target_pairs={{0,1},{2,0},{4,2},{6,4},{7,6},{5,7},{3,5},{1,3},{8,9},{10,8},{12,1... | collective-permute-start | bytes 393224 | tf_op jit(solution)/shard_map/ppermute | solution.py:33
  45.6 0.5 collective-permute-start.21
  46.1 1.4 %collective-permute-done.31 = bf16[256,256]{1,0:T(8,128)(2,1)S(1)} collective-permute-done((bf16[256,256]{1,0:T(8,128)(2,1)S(1)}, bf16[256,256]{1,0:T(8,128)(2,1)S(1)}, u32[]{:S(2)}, u32[]{:S(2)}) %collective-permute-start.31) | collective-permute-done | bytes 131104 | tf_op jit(solution)/shard_map/ppermute | solution.py:33
  47.6 2.5 %collective-permute-start.32 = (bf16[256,256]{1,0:T(8,128)(2,1)S(1)}, bf16[256,256]{1,0:T(8,128)(2,1)S(1)}, u32[]{:S(2)}, u32[]{:S(2)}) collective-permute-start(bf16[256,256]{1,0:T(8,128)(2,1)S(1)} %add_convert_fusion.4), channel_id=1, source_target_pairs={{0,2},{2,4},{4,6},{6,7},{7,5},{5,3},{3,1},{1,0},{8,10},{10,12},{12... | collective-permute-start | bytes 393224 | tf_op jit(solution)/shard_map/ppermute | solution.py:33
  50.2 0.5 collective-permute-start.28
  50.6 1.8 %collective-permute-done.24 = bf16[256,256]{1,0:T(8,128)(2,1)S(1)} collective-permute-done((bf16[256,256]{1,0:T(8,128)(2,1)S(1)}, bf16[256,256]{1,0:T(8,128)(2,1)S(1)}, u32[]{:S(2)}, u32[]{:S(2)}) %collective-permute-start.24) | collective-permute-done | bytes 131104 | tf_op jit(solution)/shard_map/ppermute | solution.py:33
  52.4 0.5 collective-permute-start.25
  53.0 1.6 %collective-permute-start.22 = (bf16[256,256]{1,0:T(8,128)(2,1)S(1)}, bf16[256,256]{1,0:T(8,128)(2,1)S(1)}, u32[]{:S(2)}, u32[]{:S(2)}) collective-permute-start(bf16[256,256]{1,0:T(8,128)(2,1)S(1)} %add_convert_fusion.11), channel_id=1, source_target_pairs={{0,2},{2,4},{4,6},{6,7},{7,5},{5,3},{3,1},{1,0},{8,10},{10,12},{12... | collective-permute-start | bytes 393224 | tf_op jit(solution)/shard_map/ppermute | solution.py:33
  54.7 1.6 %collective-permute-start.33 = (bf16[256,256]{1,0:T(8,128)(2,1)S(1)}, bf16[256,256]{1,0:T(8,128)(2,1)S(1)}, u32[]{:S(2)}, u32[]{:S(2)}) collective-permute-start(bf16[256,256]{1,0:T(8,128)(2,1)S(1)} %add_convert_fusion.3), channel_id=1, source_target_pairs={{0,2},{2,4},{4,6},{6,7},{7,5},{5,3},{3,1},{1,0},{8,10},{10,12},{12... | collective-permute-start | bytes 393224 | tf_op jit(solution)/shard_map/ppermute | solution.py:33
  56.3 0.5 collective-permute-start.29
  56.8 1.9 %collective-permute-done.25 = bf16[256,256]{1,0:T(8,128)(2,1)S(1)} collective-permute-done((bf16[256,256]{1,0:T(8,128)(2,1)S(1)}, bf16[256,256]{1,0:T(8,128)(2,1)S(1)}, u32[]{:S(2)}, u32[]{:S(2)}) %collective-permute-start.25) | collective-permute-done | bytes 131104 | tf_op jit(solution)/shard_map/ppermute | solution.py:33
  59.2 1.8 %collective-permute-start.23 = (bf16[256,256]{1,0:T(8,128)(2,1)S(1)}, bf16[256,256]{1,0:T(8,128)(2,1)S(1)}, u32[]{:S(2)}, u32[]{:S(2)}) collective-permute-start(bf16[256,256]{1,0:T(8,128)(2,1)S(1)} %add_convert_fusion.10), channel_id=1, source_target_pairs={{0,2},{2,4},{4,6},{6,7},{7,5},{5,3},{3,1},{1,0},{8,10},{10,12},{12... | collective-permute-start | bytes 393224 | tf_op jit(solution)/shard_map/ppermute | solution.py:33
  61.0 1.6 %collective-permute-start.34 = (bf16[256,256]{1,0:T(8,128)(2,1)S(1)}, bf16[256,256]{1,0:T(8,128)(2,1)S(1)}, u32[]{:S(2)}, u32[]{:S(2)}) collective-permute-start(bf16[256,256]{1,0:T(8,128)(2,1)S(1)} %add_convert_fusion.2), channel_id=1, source_target_pairs={{0,2},{2,4},{4,6},{6,7},{7,5},{5,3},{3,1},{1,0},{8,10},{10,12},{12... | collective-permute-start | bytes 393224 | tf_op jit(solution)/shard_map/ppermute | solution.py:33
  62.7 0.5 collective-permute-start.30
  63.2 1.3 %collective-permute-done.26 = bf16[256,256]{1,0:T(8,128)(2,1)S(1)} collective-permute-done((bf16[256,256]{1,0:T(8,128)(2,1)S(1)}, bf16[256,256]{1,0:T(8,128)(2,1)S(1)}, u32[]{:S(2)}, u32[]{:S(2)}) %collective-permute-start.26) | collective-permute-done | bytes 131104 | tf_op jit(solution)/shard_map/ppermute | solution.py:33
  64.5 1.6 %collective-permute-done.34 = bf16[256,256]{1,0:T(8,128)(2,1)S(1)} collective-permute-done((bf16[256,256]{1,0:T(8,128)(2,1)S(1)}, bf16[256,256]{1,0:T(8,128)(2,1)S(1)}, u32[]{:S(2)}, u32[]{:S(2)}) %collective-permute-start.34) | collective-permute-done | bytes 131104 | tf_op jit(solution)/shard_map/ppermute | solution.py:33
  66.0 1.7 %collective-permute-done.30 = bf16[256,256]{1,0:T(8,128)(2,1)S(1)} collective-permute-done((bf16[256,256]{1,0:T(8,128)(2,1)S(1)}, bf16[256,256]{1,0:T(8,128)(2,1)S(1)}, u32[]{:S(2)}, u32[]{:S(2)}) %collective-permute-start.30) | collective-permute-done | bytes 131104 | tf_op jit(solution)/shard_map/ppermute | solution.py:33
  67.8 0.7 %pad_maximum_fusion = bf16[512,256]{1,0:T(8,128)(2,1)} fusion(bf16[256,256]{1,0:T(8,128)(2,1)S(1)} %get-tuple-element.87, bf16[256,256]{1,0:T(8,128)(2,1)S(1)} %get-tuple-element.88), kind=kLoop, calls=%fused_computation | loop fusion | flops 524288 | bytes 524288 | tf_op jit(solution)/shard_map/concatenate | solution.py:452
  (50 shorter events, 3.9 us)
Async XLA Ops:
  1.0 7.1 %collective-permute-start.3 = (bf16[256,256]{1,0:T(8,128)(2,1)S(1)}, bf16[256,256]{1,0:T(8,128)(2,1)S(1)}, u32[]{:S(2)}, u32[]{:S(2)}) collective-permute-start(bf16[256,256]{1,0:T(8,128)(2,1)S(1)} %get-tuple-element.85), channel_id=1, source_target_pairs={{0,1},{2,0},{4,2},{6,4},{7,6},{5,7},{3,5},{1,3},{8,9},{10,8},{12,1... | collective-permute-start | bytes 393224 | tf_op jit(solution)/shard_map/ppermute | solution.py:33
  1.5 7.1 %collective-permute-start = (bf16[256,256]{1,0:T(8,128)(2,1)S(1)}, bf16[256,256]{1,0:T(8,128)(2,1)S(1)}, u32[]{:S(2)}, u32[]{:S(2)}) collective-permute-start(bf16[256,256]{1,0:T(8,128)(2,1)S(1)} %get-tuple-element.86), channel_id=1, source_target_pairs={{0,2},{2,4},{4,6},{6,7},{7,5},{5,3},{3,1},{1,0},{8,10},{10,12},{12... | collective-permute-start | bytes 393224 | tf_op jit(solution)/shard_map/ppermute | solution.py:33
  3.1 7.1 %collective-permute-start.6 = (bf16[256,256]{1,0:T(8,128)(2,1)S(1)}, bf16[256,256]{1,0:T(8,128)(2,1)S(1)}, u32[]{:S(2)}, u32[]{:S(2)}) collective-permute-start(bf16[256,256]{1,0:T(8,128)(2,1)S(1)} %get-tuple-element.86), channel_id=1, source_target_pairs={{0,1},{2,0},{4,2},{6,4},{7,6},{5,7},{3,5},{1,3},{8,9},{10,8},{12,1... | collective-permute-start | bytes 393224 | tf_op jit(solution)/shard_map/ppermute | solution.py:33
  3.5 7.1 %collective-permute-start.8 = (bf16[256,256]{1,0:T(8,128)(2,1)S(1)}, bf16[256,256]{1,0:T(8,128)(2,1)S(1)}, u32[]{:S(2)}, u32[]{:S(2)}) collective-permute-start(bf16[256,256]{1,0:T(8,128)(2,1)S(1)} %get-tuple-element.85), channel_id=1, source_target_pairs={{0,2},{2,4},{4,6},{6,7},{7,5},{5,3},{3,1},{1,0},{8,10},{10,12},{12... | collective-permute-start | bytes 393224 | tf_op jit(solution)/shard_map/ppermute | solution.py:33
  8.1 6.0 %collective-permute-start.4 = (bf16[256,256]{1,0:T(8,128)(2,1)S(1)}, bf16[256,256]{1,0:T(8,128)(2,1)S(1)}, u32[]{:S(2)}, u32[]{:S(2)}) collective-permute-start(bf16[256,256]{1,0:T(8,128)(2,1)S(1)} %collective-permute-done.3.refs_1_), channel_id=1, source_target_pairs={{0,1},{2,0},{4,2},{6,4},{7,6},{5,7},{3,5},{1,3},{8,9},{10,8},{12,1... | collective-permute-start | bytes 393224 | tf_op jit(solution)/shard_map/ppermute | solution.py:33
  8.6 6.0 %collective-permute-start.1 = (bf16[256,256]{1,0:T(8,128)(2,1)S(1)}, bf16[256,256]{1,0:T(8,128)(2,1)S(1)}, u32[]{:S(2)}, u32[]{:S(2)}) collective-permute-start(bf16[256,256]{1,0:T(8,128)(2,1)S(1)} %collective-permute-done.refs_0_), channel_id=1, source_target_pairs={{0,2},{2,4},{4,6},{6,7},{7,5},{5,3},{3,1},{1,0},{8,10},{10,12},{12... | collective-permute-start | bytes 393224 | tf_op jit(solution)/shard_map/ppermute | solution.py:33
  10.2 6.8 %collective-permute-start.7 = (bf16[256,256]{1,0:T(8,128)(2,1)S(1)}, bf16[256,256]{1,0:T(8,128)(2,1)S(1)}, u32[]{:S(2)}, u32[]{:S(2)}) collective-permute-start(bf16[256,256]{1,0:T(8,128)(2,1)S(1)} %collective-permute-done.6.refs_2_), channel_id=1, source_target_pairs={{0,1},{2,0},{4,2},{6,4},{7,6},{5,7},{3,5},{1,3},{8,9},{10,8},{12,1... | collective-permute-start | bytes 393224 | tf_op jit(solution)/shard_map/ppermute | solution.py:33
  10.6 6.8 %collective-permute-start.9 = (bf16[256,256]{1,0:T(8,128)(2,1)S(1)}, bf16[256,256]{1,0:T(8,128)(2,1)S(1)}, u32[]{:S(2)}, u32[]{:S(2)}) collective-permute-start(bf16[256,256]{1,0:T(8,128)(2,1)S(1)} %collective-permute-done.8.refs_3_), channel_id=1, source_target_pairs={{0,2},{2,4},{4,6},{6,7},{7,5},{5,3},{3,1},{1,0},{8,10},{10,12},{12... | collective-permute-start | bytes 393224 | tf_op jit(solution)/shard_map/ppermute | solution.py:33
  14.1 5.7 %collective-permute-start.5 = (bf16[256,256]{1,0:T(8,128)(2,1)S(1)}, bf16[256,256]{1,0:T(8,128)(2,1)S(1)}, u32[]{:S(2)}, u32[]{:S(2)}) collective-permute-start(bf16[256,256]{1,0:T(8,128)(2,1)S(1)} %collective-permute-done.4.refs_1_), channel_id=1, source_target_pairs={{0,1},{2,0},{4,2},{6,4},{7,6},{5,7},{3,5},{1,3},{8,9},{10,8},{12,1... | collective-permute-start | bytes 393224 | tf_op jit(solution)/shard_map/ppermute | solution.py:33
  14.6 5.7 %collective-permute-start.2 = (bf16[256,256]{1,0:T(8,128)(2,1)S(1)}, bf16[256,256]{1,0:T(8,128)(2,1)S(1)}, u32[]{:S(2)}, u32[]{:S(2)}) collective-permute-start(bf16[256,256]{1,0:T(8,128)(2,1)S(1)} %collective-permute-done.1.refs_0_), channel_id=1, source_target_pairs={{0,2},{2,4},{4,6},{6,7},{7,5},{5,3},{3,1},{1,0},{8,10},{10,12},{12... | collective-permute-start | bytes 393224 | tf_op jit(solution)/shard_map/ppermute | solution.py:33
  16.9 5.2 %collective-permute-start.10 = (bf16[256,256]{1,0:T(8,128)(2,1)S(1)}, bf16[256,256]{1,0:T(8,128)(2,1)S(1)}, u32[]{:S(2)}, u32[]{:S(2)}) collective-permute-start(bf16[256,256]{1,0:T(8,128)(2,1)S(1)} %collective-permute-done.7.refs_2_), channel_id=1, source_target_pairs={{0,1},{2,0},{4,2},{6,4},{7,6},{5,7},{3,5},{1,3},{8,9},{10,8},{12,1... | collective-permute-start | bytes 393224 | tf_op jit(solution)/shard_map/ppermute | solution.py:33
  17.4 5.0 %collective-permute-start.11 = (bf16[256,256]{1,0:T(8,128)(2,1)S(1)}, bf16[256,256]{1,0:T(8,128)(2,1)S(1)}, u32[]{:S(2)}, u32[]{:S(2)}) collective-permute-start(bf16[256,256]{1,0:T(8,128)(2,1)S(1)} %collective-permute-done.9.refs_3_), channel_id=1, source_target_pairs={{0,2},{2,4},{4,6},{6,7},{7,5},{5,3},{3,1},{1,0},{8,10},{10,12},{12... | collective-permute-start | bytes 393224 | tf_op jit(solution)/shard_map/ppermute | solution.py:33
  19.8 5.0 %collective-permute-start.13 = (bf16[256,256]{1,0:T(8,128)(2,1)S(1)}, bf16[256,256]{1,0:T(8,128)(2,1)S(1)}, u32[]{:S(2)}, u32[]{:S(2)}) collective-permute-start(bf16[256,256]{1,0:T(8,128)(2,1)S(1)} %collective-permute-done.5.refs_1_), channel_id=1, source_target_pairs={{0,1},{2,0},{4,2},{6,4},{7,6},{5,7},{3,5},{1,3},{8,9},{10,8},{12,1... | collective-permute-start | bytes 393224 | tf_op jit(solution)/shard_map/ppermute | solution.py:33
  20.3 5.0 %collective-permute-start.12 = (bf16[256,256]{1,0:T(8,128)(2,1)S(1)}, bf16[256,256]{1,0:T(8,128)(2,1)S(1)}, u32[]{:S(2)}, u32[]{:S(2)}) collective-permute-start(bf16[256,256]{1,0:T(8,128)(2,1)S(1)} %collective-permute-done.2.refs_0_), channel_id=1, source_target_pairs={{0,2},{2,4},{4,6},{6,7},{7,5},{5,3},{3,1},{1,0},{8,10},{10,12},{12... | collective-permute-start | bytes 393224 | tf_op jit(solution)/shard_map/ppermute | solution.py:33
  26.5 7.3 %collective-permute-start.17 = (bf16[256,512]{1,0:T(8,128)(2,1)S(1)}, bf16[256,512]{1,0:T(8,128)(2,1)S(1)}, u32[]{:S(2)}, u32[]{:S(2)}) collective-permute-start(bf16[256,512]{1,0:T(8,128)(2,1)S(1)} %get-tuple-element.53.refs_0_), channel_id=1, source_target_pairs={{0,16},{8,24},{16,0},{24,8},{1,17},{9,25},{17,1},{25,9},{2,18},{10... | collective-permute-start | bytes 786440 | tf_op jit(solution)/shard_map/ppermute | solution.py:425
  27.1 9.2 %collective-permute-start.18 = (bf16[256,512]{1,0:T(8,128)(2,1)S(1)}, bf16[256,512]{1,0:T(8,128)(2,1)S(1)}, u32[]{:S(2)}, u32[]{:S(2)}) collective-permute-start(bf16[256,512]{1,0:T(8,128)(2,1)S(1)} %get-tuple-element.54.refs_1_), channel_id=1, source_target_pairs={{0,16},{8,24},{16,0},{24,8},{1,17},{9,25},{17,1},{25,9},{2,18},{10... | collective-permute-start | bytes 786440 | tf_op jit(solution)/shard_map/ppermute | solution.py:425
  28.6 2.9 %collective-permute-start.15 = (bf16[176,512]{1,0:T(8,128)(2,1)S(1)}, bf16[176,512]{1,0:T(8,128)(2,1)S(1)}, u32[]{:S(2)}, u32[]{:S(2)}) collective-permute-start(bf16[176,512]{1,0:T(8,128)(2,1)S(1)} %get-tuple-element.56), channel_id=1, source_target_pairs={{0,8},{8,0},{16,24},{24,16},{1,9},{9,1},{17,25},{25,17},{2,10},{10... | collective-permute-start | bytes 540680 | tf_op jit(solution)/shard_map/ppermute | solution.py:39
  28.6 2.9 %collective-permute-start.16 = (bf16[176,512]{1,0:T(8,128)(2,1)S(1)}, bf16[176,512]{1,0:T(8,128)(2,1)S(1)}, u32[]{:S(2)}, u32[]{:S(2)}) collective-permute-start(bf16[176,512]{1,0:T(8,128)(2,1)S(1)} %get-tuple-element.57), channel_id=1, source_target_pairs={{0,8},{8,0},{16,24},{24,16},{1,9},{9,1},{17,25},{25,17},{2,10},{10... | collective-permute-start | bytes 540680 | tf_op jit(solution)/shard_map/ppermute | solution.py:39
  29.1 2.4 %collective-permute-start.14 = (bf16[160,512]{1,0:T(8,128)(2,1)S(1)}, bf16[160,512]{1,0:T(8,128)(2,1)S(1)}, u32[]{:S(2)}, u32[]{:S(2)}) collective-permute-start(bf16[160,512]{1,0:T(8,128)(2,1)S(1)} %get-tuple-element.55), channel_id=1, source_target_pairs={{0,8},{8,0},{16,24},{24,16},{1,9},{9,1},{17,25},{25,17},{2,10},{10... | collective-permute-start | bytes 491528 | tf_op jit(solution)/shard_map/ppermute | solution.py:39
  36.2 2.8 %collective-permute-start.19 = (bf16[256,512]{1,0:T(8,128)(2,1)S(1)}, bf16[256,512]{1,0:T(8,128)(2,1)S(1)}, u32[]{:S(2)}, u32[]{:S(2)}) collective-permute-start(bf16[256,512]{1,0:T(8,128)(2,1)S(1)} %collective-permute-done.17.refs_0_), channel_id=1, source_target_pairs={{0,8},{8,0},{16,24},{24,16},{1,9},{9,1},{17,25},{25,17},{2,10},{10... | collective-permute-start | bytes 786440 | tf_op jit(solution)/shard_map/ppermute | solution.py:39
  36.3 2.8 %collective-permute-start.20 = (bf16[256,512]{1,0:T(8,128)(2,1)S(1)}, bf16[256,512]{1,0:T(8,128)(2,1)S(1)}, u32[]{:S(2)}, u32[]{:S(2)}) collective-permute-start(bf16[256,512]{1,0:T(8,128)(2,1)S(1)} %collective-permute-done.18.refs_1_), channel_id=1, source_target_pairs={{0,8},{8,0},{16,24},{24,16},{1,9},{9,1},{17,25},{25,17},{2,10},{10... | collective-permute-start | bytes 786440 | tf_op jit(solution)/shard_map/ppermute | solution.py:39
  42.0 5.5 %collective-permute-start.31 = (bf16[256,256]{1,0:T(8,128)(2,1)S(1)}, bf16[256,256]{1,0:T(8,128)(2,1)S(1)}, u32[]{:S(2)}, u32[]{:S(2)}) collective-permute-start(bf16[256,256]{1,0:T(8,128)(2,1)S(1)} %get-tuple-element.79), channel_id=1, source_target_pairs={{0,2},{2,4},{4,6},{6,7},{7,5},{5,3},{3,1},{1,0},{8,10},{10,12},{12... | collective-permute-start | bytes 393224 | tf_op jit(solution)/shard_map/ppermute | solution.py:33
  43.7 6.5 %collective-permute-start.27 = (bf16[256,256]{1,0:T(8,128)(2,1)S(1)}, bf16[256,256]{1,0:T(8,128)(2,1)S(1)}, u32[]{:S(2)}, u32[]{:S(2)}) collective-permute-start(bf16[256,256]{1,0:T(8,128)(2,1)S(1)} %get-tuple-element.75), channel_id=1, source_target_pairs={{0,1},{2,0},{4,2},{6,4},{7,6},{5,7},{3,5},{1,3},{8,9},{10,8},{12,1... | collective-permute-start | bytes 393224 | tf_op jit(solution)/shard_map/ppermute | solution.py:33
  44.1 8.3 %collective-permute-start.24 = (bf16[256,256]{1,0:T(8,128)(2,1)S(1)}, bf16[256,256]{1,0:T(8,128)(2,1)S(1)}, u32[]{:S(2)}, u32[]{:S(2)}) collective-permute-start(bf16[256,256]{1,0:T(8,128)(2,1)S(1)} %get-tuple-element.71), channel_id=1, source_target_pairs={{0,1},{2,0},{4,2},{6,4},{7,6},{5,7},{3,5},{1,3},{8,9},{10,8},{12,1... | collective-permute-start | bytes 393224 | tf_op jit(solution)/shard_map/ppermute | solution.py:33
  45.6 7.3 %collective-permute-start.21 = (bf16[256,256]{1,0:T(8,128)(2,1)S(1)}, bf16[256,256]{1,0:T(8,128)(2,1)S(1)}, u32[]{:S(2)}, u32[]{:S(2)}) collective-permute-start(bf16[256,256]{1,0:T(8,128)(2,1)S(1)} %get-tuple-element.68), channel_id=1, source_target_pairs={{0,2},{2,4},{4,6},{6,7},{7,5},{5,3},{3,1},{1,0},{8,10},{10,12},{12... | collective-permute-start | bytes 393224 | tf_op jit(solution)/shard_map/ppermute | solution.py:33
  47.6 7.0 %collective-permute-start.32 = (bf16[256,256]{1,0:T(8,128)(2,1)S(1)}, bf16[256,256]{1,0:T(8,128)(2,1)S(1)}, u32[]{:S(2)}, u32[]{:S(2)}) collective-permute-start(bf16[256,256]{1,0:T(8,128)(2,1)S(1)} %add_convert_fusion.4), channel_id=1, source_target_pairs={{0,2},{2,4},{4,6},{6,7},{7,5},{5,3},{3,1},{1,0},{8,10},{10,12},{12... | collective-permute-start | bytes 393224 | tf_op jit(solution)/shard_map/ppermute | solution.py:33
  50.2 6.1 %collective-permute-start.28 = (bf16[256,256]{1,0:T(8,128)(2,1)S(1)}, bf16[256,256]{1,0:T(8,128)(2,1)S(1)}, u32[]{:S(2)}, u32[]{:S(2)}) collective-permute-start(bf16[256,256]{1,0:T(8,128)(2,1)S(1)} %add_convert_fusion.7), channel_id=1, source_target_pairs={{0,1},{2,0},{4,2},{6,4},{7,6},{5,7},{3,5},{1,3},{8,9},{10,8},{12,1... | collective-permute-start | bytes 393224 | tf_op jit(solution)/shard_map/ppermute | solution.py:33
  52.4 6.3 %collective-permute-start.25 = (bf16[256,256]{1,0:T(8,128)(2,1)S(1)}, bf16[256,256]{1,0:T(8,128)(2,1)S(1)}, u32[]{:S(2)}, u32[]{:S(2)}) collective-permute-start(bf16[256,256]{1,0:T(8,128)(2,1)S(1)} %add_convert_fusion.9), channel_id=1, source_target_pairs={{0,1},{2,0},{4,2},{6,4},{7,6},{5,7},{3,5},{1,3},{8,9},{10,8},{12,1... | collective-permute-start | bytes 393224 | tf_op jit(solution)/shard_map/ppermute | solution.py:33
  53.0 6.2 %collective-permute-start.22 = (bf16[256,256]{1,0:T(8,128)(2,1)S(1)}, bf16[256,256]{1,0:T(8,128)(2,1)S(1)}, u32[]{:S(2)}, u32[]{:S(2)}) collective-permute-start(bf16[256,256]{1,0:T(8,128)(2,1)S(1)} %add_convert_fusion.11), channel_id=1, source_target_pairs={{0,2},{2,4},{4,6},{6,7},{7,5},{5,3},{3,1},{1,0},{8,10},{10,12},{12... | collective-permute-start | bytes 393224 | tf_op jit(solution)/shard_map/ppermute | solution.py:33
  54.7 6.3 %collective-permute-start.33 = (bf16[256,256]{1,0:T(8,128)(2,1)S(1)}, bf16[256,256]{1,0:T(8,128)(2,1)S(1)}, u32[]{:S(2)}, u32[]{:S(2)}) collective-permute-start(bf16[256,256]{1,0:T(8,128)(2,1)S(1)} %add_convert_fusion.3), channel_id=1, source_target_pairs={{0,2},{2,4},{4,6},{6,7},{7,5},{5,3},{3,1},{1,0},{8,10},{10,12},{12... | collective-permute-start | bytes 393224 | tf_op jit(solution)/shard_map/ppermute | solution.py:33
  56.3 6.3 %collective-permute-start.29 = (bf16[256,256]{1,0:T(8,128)(2,1)S(1)}, bf16[256,256]{1,0:T(8,128)(2,1)S(1)}, u32[]{:S(2)}, u32[]{:S(2)}) collective-permute-start(bf16[256,256]{1,0:T(8,128)(2,1)S(1)} %add_convert_fusion.6), channel_id=1, source_target_pairs={{0,1},{2,0},{4,2},{6,4},{7,6},{5,7},{3,5},{1,3},{8,9},{10,8},{12,1... | collective-permute-start | bytes 393224 | tf_op jit(solution)/shard_map/ppermute | solution.py:33
  58.8 5.7 %collective-permute-start.26 = (bf16[256,256]{1,0:T(8,128)(2,1)S(1)}, bf16[256,256]{1,0:T(8,128)(2,1)S(1)}, u32[]{:S(2)}, u32[]{:S(2)}) collective-permute-start(bf16[256,256]{1,0:T(8,128)(2,1)S(1)} %add_convert_fusion.8), channel_id=1, source_target_pairs={{0,1},{2,0},{4,2},{6,4},{7,6},{5,7},{3,5},{1,3},{8,9},{10,8},{12,1... | collective-permute-start | bytes 393224 | tf_op jit(solution)/shard_map/ppermute | solution.py:33
  59.2 5.3 %collective-permute-start.23 = (bf16[256,256]{1,0:T(8,128)(2,1)S(1)}, bf16[256,256]{1,0:T(8,128)(2,1)S(1)}, u32[]{:S(2)}, u32[]{:S(2)}) collective-permute-start(bf16[256,256]{1,0:T(8,128)(2,1)S(1)} %add_convert_fusion.10), channel_id=1, source_target_pairs={{0,2},{2,4},{4,6},{6,7},{7,5},{5,3},{3,1},{1,0},{8,10},{10,12},{12... | collective-permute-start | bytes 393224 | tf_op jit(solution)/shard_map/ppermute | solution.py:33
  61.0 5.0 %collective-permute-start.34 = (bf16[256,256]{1,0:T(8,128)(2,1)S(1)}, bf16[256,256]{1,0:T(8,128)(2,1)S(1)}, u32[]{:S(2)}, u32[]{:S(2)}) collective-permute-start(bf16[256,256]{1,0:T(8,128)(2,1)S(1)} %add_convert_fusion.2), channel_id=1, source_target_pairs={{0,2},{2,4},{4,6},{6,7},{7,5},{5,3},{3,1},{1,0},{8,10},{10,12},{12... | collective-permute-start | bytes 393224 | tf_op jit(solution)/shard_map/ppermute | solution.py:33
  62.7 5.0 %collective-permute-start.30 = (bf16[256,256]{1,0:T(8,128)(2,1)S(1)}, bf16[256,256]{1,0:T(8,128)(2,1)S(1)}, u32[]{:S(2)}, u32[]{:S(2)}) collective-permute-start(bf16[256,256]{1,0:T(8,128)(2,1)S(1)} %add_convert_fusion.5), channel_id=1, source_target_pairs={{0,1},{2,0},{4,2},{6,4},{7,6},{5,7},{3,5},{1,3},{8,9},{10,8},{12,1... | collective-permute-start | bytes 393224 | tf_op jit(solution)/shard_map/ppermute | solution.py:33

commit v21 on v20

--- a/solution.py
+++ b/solution.py
@@ -47,57 +47,47 @@
     return pltpu.with_memory_space_constraint(value, pltpu.VMEM)
 
 
-def fold_kernel(order, at, gain_hbm, w_hbm, tokens, out_ref, wide, gain_ref, sems):
-    lanes = gain_ref.shape[1]
+def load_kernel(order, at, w_hbm, tokens, out_ref, wide, sems):
     size = w_hbm.shape[1] // len(order)
-    per = size // lanes
-
-    def fetch(n):
+    copies = [pltpu.make_async_copy(tokens, wide.at[:, : tokens.shape[1]], sems.at[len(order)])]
+    for n in range(len(order)):
         start = pl.multiple_of(at[order[n]] * size, size)
-        return pltpu.make_async_copy(
-            w_hbm.at[:, pl.ds(start, size), :],
-            out_ref.at[:, n * size : (n + 1) * size, :],
-            sems.at[n],
+        copies.append(
+            pltpu.make_async_copy(
+                w_hbm.at[:, pl.ds(start, size), :],
+                out_ref.at[:, n * size : (n + 1) * size, :],
+                sems.at[n],
+            )
         )
-
-    gains = pltpu.make_async_copy(gain_hbm, gain_ref, sems.at[len(order) + 1])
-    gains.start()
-    for n in range(len(order)):
-        fetch(n).start()
-    own = pltpu.make_async_copy(tokens, wide.at[:, : tokens.shape[1]], sems.at[len(order)])
-    own.start()
-    gains.wait()
-    for n in range(len(order)):
-        columns = jnp.transpose(gain_ref[pl.ds(at[order[n]] * per, per), :])
-        fetch(n).wait()
-        for piece in range(per):
-            first = n * size + piece * lanes
-            for group in range(w_hbm.shape[0]):
-                here = (group, slice(first, first + lanes), slice(None))
-                scaled = out_ref[here].astype(F32) * columns[:, piece : piece + 1]
-                out_ref[here] = scaled.astype(BF16)
-    own.wait()
-
-
-def fold_gain(order, at, gain, weights, tokens):
-    depth = weights.shape[1]
-    lanes = math.gcd(depth // len(order), 128)
+    for copy in copies:
+        copy.start()
+    for copy in copies:
+        copy.wait()
+
+
+def loaded(order, at, weights, tokens):
     hbm = pl.BlockSpec(memory_space=pltpu.HBM)
     return pl.pallas_call(
-        functools.partial(fold_kernel, order),
-        out_shape=(pltpu.VMEM(weights.shape, BF16), pltpu.VMEM((tokens.shape[0], depth), BF16)),
-        in_specs=[SMEM, hbm, hbm, hbm],
-        out_specs=(VMEM, pl.BlockSpec(memory_space=pl.ANY)),
-        scratch_shapes=[
-            pltpu.VMEM((depth // lanes, lanes), F32),
-            pltpu.SemaphoreType.DMA((len(order) + 2,)),
-        ],
-        compiler_params=pltpu.CompilerParams(vmem_limit_bytes=16 << 20),
+        functools.partial(load_kernel, order),
+        out_shape=(
+            pltpu.VMEM(weights.shape, BF16),
+            pltpu.VMEM((tokens.shape[0], weights.shape[1]), BF16),
+        ),
+        in_specs=[SMEM, hbm, hbm],
+        out_specs=(pl.BlockSpec(memory_space=pl.ANY),) * 2,
+        scratch_shapes=[pltpu.SemaphoreType.DMA((len(order) + 1,))],
+        compiler_params=pltpu.CompilerParams(vmem_limit_bytes=1 << 20),
         cost_estimate=pl.CostEstimate(
             flops=weights.size, bytes_accessed=4 * weights.size, transcendentals=0
         ),
-        name="fold_gain",
-    )(at, in_hbm(gain.reshape(depth // lanes, lanes)), in_hbm(weights), in_hbm(tokens))
+        name="load",
+    )(at, in_hbm(weights), in_hbm(tokens))
+
+
+def gain_of(gain_ref, offset, ring, part, parts):
+    place = ring_place(lax.axis_index("head"), ring)
+    index = ring_index((place + offset) % ring, ring)
+    return gain_ref[pl.ds(index * parts + part, 1), :]
 
 
 def place_kernel(targets, *refs):
@@ -128,25 +118,28 @@
     )(*operands)
 
 
-def begin_kernel(blocks, wide, w_ref, state):
+def begin_kernel(order, gain_ref, wide, w_ref, state, scaled):
     rows, depth = wide.shape
-    out_width = w_ref.shape[2]
-    done = depth - depth // blocks
-    tile = math.gcd(rows, 256)
+    ring = len(order)
+    out_width, parts = w_ref.shape[2], depth // ring // 128
+    tile, done = scaled.shape
     for first in range(0, rows, tile):
         here = slice(first, first + tile)
+        power = None
+        for lane in range(0, done, 128):
+            n, part = lane // 128 // parts, lane // 128 % parts
+            values = wide[here, lane : lane + 128].astype(F32)
+            power = values * values if power is None else power + values * values
+            row = gain_of(gain_ref, order[n], ring, part, parts)
+            scaled[:, lane : lane + 128] = (values * row).astype(BF16)
+        state[here, 3 * out_width :] = power
         for group in range(3):
             state[here, group * out_width : (group + 1) * out_width] = jnp.dot(
-                wide[here, :done], w_ref[group, :done, :], preferred_element_type=F32
+                scaled[...], w_ref[group, :done, :], preferred_element_type=F32
             )
-        power = None
-        for lane in range(0, done, 128):
-            values = wide[here, lane : lane + 128].astype(F32)
-            power = values * values if power is None else power + values * values
-        state[here, 3 * out_width :] = power
-
-
-def finish_kernel(head_size, factor, state, w_ref, *refs):
+
+
+def finish_kernel(head_size, order, factor, gain_ref, state, w_ref, *refs):
     count = 2
     lasts, q_ref = refs[:count], refs[count]
     halves, pieces = refs[count + 1 : 2 * count + 1], refs[2 * count + 1 :]
@@ -155,15 +148,19 @@
     for stream, last in enumerate(lasts):
         here = slice(stream * rows, (stream + 1) * rows)
         kv_ref = halves[stream]
+        power = state[here, 3 * out_width :]
+        scaled = []
+        for part in range(width // 128):
+            values = last[:, part * 128 : (part + 1) * 128].astype(F32)
+            power += values * values
+            row = gain_of(gain_ref, order[-1], len(order), part, width // 128)
+            scaled.append((values * row).astype(BF16))
+        scaled = jnp.concatenate(scaled, axis=1)
         q, k, v = (
             state[here, group * out_width : (group + 1) * out_width]
-            + jnp.dot(last[...], w_ref[group, depth - width :, :], preferred_element_type=F32)
+            + jnp.dot(scaled, w_ref[group, depth - width :, :], preferred_element_type=F32)
             for group in range(3)
         )
-        power = state[here, 3 * out_width :]
-        for lane in range(0, width, 128):
-            values = last[:, lane : lane + 128].astype(F32)
-            power += values * values
         scale = lax.rsqrt(jnp.sum(power, axis=-1, keepdims=True) * (1.0 / depth) + 1e-06)
         q, k, v = q * scale, k * scale, v * scale
         for head in range(out_width // head_size):
@@ -185,14 +182,16 @@
         start = end
 
 
-def project_begin(wide, weights, blocks):
+def project_begin(gain, wide, weights, order):
     rows, depth = wide.shape
+    done = depth - depth // len(order)
     groups, _, out_width = weights.shape
     return pl.pallas_call(
-        functools.partial(begin_kernel, blocks),
+        functools.partial(begin_kernel, order),
         out_shape=pltpu.VMEM((rows, groups * out_width + 128), F32),
-        in_specs=[VMEM] * 2,
+        in_specs=[VMEM] * 3,
         out_specs=VMEM,
+        scratch_shapes=[pltpu.VMEM((math.gcd(rows, 256), done), BF16)],
         compiler_params=pltpu.CompilerParams(vmem_limit_bytes=16 << 20),
         cost_estimate=pl.CostEstimate(
             flops=2 * rows * depth * groups * out_width,
@@ -200,10 +199,10 @@
             transcendentals=0,
         ),
         name="project_begin",
-    )(in_vmem(wide), in_vmem(weights))
-
-
-def project_finish(factor, state, weights, lasts, count_pieces, head_size):
+    )(in_hbm(gain), in_vmem(wide), in_vmem(weights))
+
+
+def project_finish(factor, gain, state, weights, lasts, count_pieces, order, head_size):
     rows, width = lasts[0].shape
     out_width = weights.shape[2]
     total = rows * len(lasts)
@@ -211,19 +210,19 @@
     sizes = [rows] * len(lasts)
     sizes += [16 * ((units + n) // count_pieces) for n in range(count_pieces)]
     return pl.pallas_call(
-        functools.partial(finish_kernel, head_size),
+        functools.partial(finish_kernel, head_size, order),
         out_shape=(
             pltpu.VMEM((total, out_width), BF16),
             *[pltpu.VMEM((size, 2 * out_width), BF16) for size in sizes],
         ),
-        in_specs=[SMEM] + [VMEM] * (2 + len(lasts)),
+        in_specs=[SMEM] + [VMEM] * (3 + len(lasts)),
         out_specs=(VMEM,) * (1 + len(sizes)),
         compiler_params=pltpu.CompilerParams(vmem_limit_bytes=16 << 20),
         cost_estimate=pl.CostEstimate(
             flops=6 * total * width * out_width, bytes_accessed=8 * total * out_width, transcendentals=0
         ),
         name="project_finish",
-    )(in_hbm(factor), in_vmem(state), in_vmem(weights), *map(in_vmem, lasts))
+    )(in_hbm(factor), in_hbm(gain), in_vmem(state), in_vmem(weights), *map(in_vmem, lasts))
 
 
 def attend_kernel(
@@ -395,7 +394,7 @@
                 held[s][way] = along(held[s][way], sign, ring)
         if step == 1:
             held[0][0], (weights, wide) = lax.optimization_barrier(
-                (held[0][0], fold_gain(order, numbers(at), norm_gain, w_qkv, tokens))
+                (held[0][0], loaded(order, numbers(at), w_qkv, tokens))
             )
         elif step == 2:
             wide = placed(targets, blocks, wide)
@@ -411,8 +410,9 @@
                 targets.append((s * half, (2 * step - 1 + way) * width))
     wide = placed(targets, blocks, wide)
     lasts = [held[0][0], held[1][1]]
-    state = project_begin(wide, weights, ring)
-    query, *parts = project_finish(head_scale, state, weights, lasts, 3, head_size)
+    gain = norm_gain.reshape(-1, 128)
+    state = project_begin(gain, wide, weights, order)
+    query, *parts = project_finish(head_scale, gain, state, weights, lasts, 3, order, head_size)
     halves, pieces = parts[:2], parts[2:]
 
     far, straight, crossed = [], [], []

time: 69.4 us -> 69.3 us (level)
  transfers between devices with their start and end apart: 35 -> 35, of which waited for: 14 -> 15; matrix products, arithmetic and copies ran while one was open for 1% -> 1% of each run, Pallas kernels for 17% -> 17%
where the time goes in v21:
time: 69.3 us; the launch traced here: 68.4 us
  starting transfers between devices  32.9 us (47%)
  waiting for transfers between devices  16.7 us (24%)
  Pallas kernels  16 us (23%)
  other arithmetic  1.39 us (2%)
  local copies, waits for them, and re-layouts  1.16 us (2%)
    ppermute x28, starting transfers between devices, along(): lax.ppermute(value, 'head', [(order[p], order[(p + step) % count]) for p...  29.8 us
    ppermute x28, waiting for transfers between devices, along(): lax.ppermute(value, 'head', [(order[p], order[(p + step) % count]) for p...  14.2 us
    pallas_call x4, Pallas kernels, attend(): pl.pallas_call(functools.partial(attend_kernel, head_size, (len(blocks),...  9.53 us
    pallas_call x1, Pallas kernels, loaded(): pl.pallas_call(functools.partial(load_kernel, order), out_shape=(pltpu.VM...  2.53 us
    ppermute x2, waiting for transfers between devices, body(): far.append([lax.ppermute(part, 'seq', shift) for part in halves])  2.47 us
    pallas_call x1, Pallas kernels, project_begin(): pl.pallas_call(functools.partial(begin_kernel, order), out_shape=pltpu.VM...  2.3 us
    ppermute x2, starting transfers between devices, body(): far.append([lax.ppermute(part, 'seq', shift) for part in halves])  2.09 us
  transfers between devices with their start and end apart: 35, of which 15 were waited for; matrix products, arithmetic and copies ran while one was open for 1% of the time, Pallas kernels for 17%

profile of v21, /device:TPU:10, one launch (start us, length us, event | category | flops | bytes accessed | tf_op | source)
XLA Modules:
  0.0 68.4 jit_solution(7218592078827205235)
XLA Ops:
  0.0 1.0 %fusion = (bf16[256,256]{1,0:T(8,128)(2,1)S(1)}, bf16[256,256]{1,0:T(8,128)(2,1)S(1)}) fusion(bf16[512,256]{1,0:T(8,128)(2,1)} %tokens.1), kind=kLoop, calls=%fused_computation.16 | loop fusion | bytes 524288 | tf_op jit(solution)/shard_map/slice | solution.py:389
  1.0 0.5 collective-permute-start.3
  1.5 1.6 %collective-permute-start = (bf16[256,256]{1,0:T(8,128)(2,1)S(1)}, bf16[256,256]{1,0:T(8,128)(2,1)S(1)}, u32[]{:S(2)}, u32[]{:S(2)}) collective-permute-start(bf16[256,256]{1,0:T(8,128)(2,1)S(1)} %get-tuple-element.86), channel_id=1, source_target_pairs={{0,2},{2,4},{4,6},{6,7},{7,5},{5,3},{3,1},{1,0},{8,10},{10,12},{12... | collective-permute-start | bytes 393224 | tf_op jit(solution)/shard_map/ppermute | solution.py:33
  3.1 0.4 collective-permute-start.6
  3.5 1.6 %collective-permute-start.8 = (bf16[256,256]{1,0:T(8,128)(2,1)S(1)}, bf16[256,256]{1,0:T(8,128)(2,1)S(1)}, u32[]{:S(2)}, u32[]{:S(2)}) collective-permute-start(bf16[256,256]{1,0:T(8,128)(2,1)S(1)} %get-tuple-element.85), channel_id=1, source_target_pairs={{0,2},{2,4},{4,6},{6,7},{7,5},{5,3},{3,1},{1,0},{8,10},{10,12},{12... | collective-permute-start | bytes 393224 | tf_op jit(solution)/shard_map/ppermute | solution.py:33
  5.2 2.5 %load.1 = (bf16[3,2048,256]{2,1,0:T(8,128)(2,1)S(1)}, bf16[512,2048]{1,0:T(8,128)(2,1)S(1)}) custom-call(s32[8]{0:T(128)S(1)} %stack.84.at, bf16[3,2048,256]{2,1,0:T(8,128)(2,1)} %w_hbm.1, bf16[512,256]{1,0:T(8,128)(2,1)} %tokens.1), custom_call_target="tpu_custom_call" | custom-call | flops 1572864 | bytes 6291456 | tf_op jit(solution)/shard_map/load/pallas_call | solution.py:70
  7.7 0.5 collective-permute-start.4
  8.2 1.6 %collective-permute-start.1 = (bf16[256,256]{1,0:T(8,128)(2,1)S(1)}, bf16[256,256]{1,0:T(8,128)(2,1)S(1)}, u32[]{:S(2)}, u32[]{:S(2)}) collective-permute-start(bf16[256,256]{1,0:T(8,128)(2,1)S(1)} %collective-permute-done.refs_0_), channel_id=1, source_target_pairs={{0,2},{2,4},{4,6},{6,7},{7,5},{5,3},{3,1},{1,0},{8,10},{10,12},{12... | collective-permute-start | bytes 393224 | tf_op jit(solution)/shard_map/ppermute | solution.py:33
  9.8 0.5 collective-permute-start.7
  10.3 1.6 %collective-permute-start.9 = (bf16[256,256]{1,0:T(8,128)(2,1)S(1)}, bf16[256,256]{1,0:T(8,128)(2,1)S(1)}, u32[]{:S(2)}, u32[]{:S(2)}) collective-permute-start(bf16[256,256]{1,0:T(8,128)(2,1)S(1)} %collective-permute-done.8.refs_3_), channel_id=1, source_target_pairs={{0,2},{2,4},{4,6},{6,7},{7,5},{5,3},{3,1},{1,0},{8,10},{10,12},{12... | collective-permute-start | bytes 393224 | tf_op jit(solution)/shard_map/ppermute | solution.py:33
  11.8 2.1 %collective-permute-done.4.refs_1_ = bf16[256,256]{1,0:T(8,128)(2,1)S(1)} collective-permute-done((bf16[256,256]{1,0:T(8,128)(2,1)S(1)}, bf16[256,256]{1,0:T(8,128)(2,1)S(1)}, u32[]{:S(2)}, u32[]{:S(2)}) %collective-permute-start.4) | collective-permute-done | bytes 131104 | tf_op jit(solution)/shard_map/ppermute | solution.py:33
  13.9 0.3 collective-permute-start.5
  14.2 1.7 %collective-permute-start.2 = (bf16[256,256]{1,0:T(8,128)(2,1)S(1)}, bf16[256,256]{1,0:T(8,128)(2,1)S(1)}, u32[]{:S(2)}, u32[]{:S(2)}) collective-permute-start(bf16[256,256]{1,0:T(8,128)(2,1)S(1)} %collective-permute-done.1.refs_0_), channel_id=1, source_target_pairs={{0,2},{2,4},{4,6},{6,7},{7,5},{5,3},{3,1},{1,0},{8,10},{10,12},{12... | collective-permute-start | bytes 393224 | tf_op jit(solution)/shard_map/ppermute | solution.py:33
  16.0 0.8 %collective-permute-done.7.refs_2_ = bf16[256,256]{1,0:T(8,128)(2,1)S(1)} collective-permute-done((bf16[256,256]{1,0:T(8,128)(2,1)S(1)}, bf16[256,256]{1,0:T(8,128)(2,1)S(1)}, u32[]{:S(2)}, u32[]{:S(2)}) %collective-permute-start.7) | collective-permute-done | bytes 131104 | tf_op jit(solution)/shard_map/ppermute | solution.py:33
  17.0 1.7 %collective-permute-start.11 = (bf16[256,256]{1,0:T(8,128)(2,1)S(1)}, bf16[256,256]{1,0:T(8,128)(2,1)S(1)}, u32[]{:S(2)}, u32[]{:S(2)}) collective-permute-start(bf16[256,256]{1,0:T(8,128)(2,1)S(1)} %collective-permute-done.9.refs_3_), channel_id=1, source_target_pairs={{0,2},{2,4},{4,6},{6,7},{7,5},{5,3},{3,1},{1,0},{8,10},{10,12},{12... | collective-permute-start | bytes 393224 | tf_op jit(solution)/shard_map/ppermute | solution.py:33
  19.0 0.6 collective-permute-done.5.refs_1_
  19.9 1.8 %collective-permute-start.12 = (bf16[256,256]{1,0:T(8,128)(2,1)S(1)}, bf16[256,256]{1,0:T(8,128)(2,1)S(1)}, u32[]{:S(2)}, u32[]{:S(2)}) collective-permute-start(bf16[256,256]{1,0:T(8,128)(2,1)S(1)} %collective-permute-done.2.refs_0_), channel_id=1, source_target_pairs={{0,2},{2,4},{4,6},{6,7},{7,5},{5,3},{3,1},{1,0},{8,10},{10,12},{12... | collective-permute-start | bytes 393224 | tf_op jit(solution)/shard_map/ppermute | solution.py:33
  22.2 2.3 %project_begin.1.state = f32[512,896]{1,0:T(8,128)S(1)} custom-call(f32[16,128]{1,0:T(8,128)} %bitcast.19, bf16[512,2048]{1,0:T(8,128)(2,1)S(1)} %place.5.wide, bf16[3,2048,256]{2,1,0:T(8,128)(2,1)S(1)} %get-tuple-element.51.w_ref), custom_call_target="tpu_custom_call" | custom-call | flops 1610612736 | bytes 5242880 | tf_op jit(solution)/shard_map/project_begin/pallas_call | solution.py:189
  24.9 1.3 %project_finish.1 = (bf16[512,256]{1,0:T(8,128)(2,1)S(1)}, bf16[256,512]{1,0:T(8,128)(2,1)S(1)}, bf16[256,512]{1,0:T(8,128)(2,1)S(1)}, bf16[160,512]{1,0:T(8,128...) custom-call(f32[2]{0:T(128)} %factor.1, f32[16,128]{1,0:T(8,128)} %bitcast.20, ...), custom_call_target="tpu_custom_call" | custom-call | flops 201326592 | bytes 1048576 | tf_op jit(solution)/shard_map/project_finish/pallas_call | solution.py:212
  26.2 0.6 collective-permute-start.17
  26.8 1.5 %collective-permute-start.18 = (bf16[256,512]{1,0:T(8,128)(2,1)S(1)}, bf16[256,512]{1,0:T(8,128)(2,1)S(1)}, u32[]{:S(2)}, u32[]{:S(2)}) collective-permute-start(bf16[256,512]{1,0:T(8,128)(2,1)S(1)} %get-tuple-element.54.refs_1_), channel_id=1, source_target_pairs={{0,16},{8,24},{16,0},{24,8},{1,17},{9,25},{17,1},{25,9},{2,18},{10... | collective-permute-start | bytes 786440 | tf_op jit(solution)/shard_map/ppermute | solution.py:425
  28.3 0.5 collective-permute-start.16
  29.0 2.2 %attend.3.refs_3_ = f32[512,512]{1,0:T(8,128)S(1)} custom-call(s32[2]{0:T(128)S(1)} %pad_add_fusion.1.info, s32[2048]{0:T(1024)} %ids.7, s32[8,1,256]{2,1,0:T(1,128)} %bitcast.15, bf16[512,256]{1,0:T(8,128)(2,1)S(1)} %get-tuple-element.52.q_ref, bf16[256,512]{1,0:T(8,128)(2,1)S(1)} %get-tuple-element.53.refs_0_, bf16[256,512]{1,0:T(8,128)(2,1)S(1)} %get-tuple-element.54.refs_1_), custom_call_target="tpu_custom_call" | custom-call | flops 1048576 | bytes 1024 | tf_op jit(solution)/shard_map/attend/pallas_call | solution.py:350
  31.3 2.2 %attend.4.refs_2_ = f32[512,512]{1,0:T(8,128)S(1)} custom-call(s32[2]{0:T(128)S(1)} %pad_add_fusion.info, s32[2048]{0:T(1024)} %ids.7, s32[8,1,256]{2,1,0:T(1,128)} %bitcast.16, bf16[512,256]{1,0:T(8,128)(2,1)S(1)} %get-tuple-element.52.q_ref, bf16[160,512]{1,0:T(8,128)(2,1)S(1)} %collective-permute-done.14.refs_0_, ...), custom_call_target="tpu_custom_call" | custom-call | flops 1048576 | bytes 1024 | tf_op jit(solution)/shard_map/attend/pallas_call | solution.py:350
  33.5 2.5 %collective-permute-done.18.refs_1_ = bf16[256,512]{1,0:T(8,128)(2,1)S(1)} collective-permute-done((bf16[256,512]{1,0:T(8,128)(2,1)S(1)}, bf16[256,512]{1,0:T(8,128)(2,1)S(1)}, u32[]{:S(2)}, u32[]{:S(2)}) %collective-permute-start.18) | collective-permute-done | bytes 262176 | tf_op jit(solution)/shard_map/ppermute | solution.py:425
  36.0 0.5 collective-permute-start.20
  36.7 2.1 %attend.5.refs_2_ = f32[512,512]{1,0:T(8,128)S(1)} custom-call(s32[2]{0:T(128)S(1)} %pad_add_fusion.2.info, s32[2048]{0:T(1024)} %ids.7, s32[8,1,256]{2,1,0:T(1,128)} %bitcast.17, bf16[512,256]{1,0:T(8,128)(2,1)S(1)} %get-tuple-element.52.q_ref, bf16[256,512]{1,0:T(8,128)(2,1)S(1)} %collective-permute-done.17.refs_0_, ...), custom_call_target="tpu_custom_call" | custom-call | flops 1048576 | bytes 1024 | tf_op jit(solution)/shard_map/attend/pallas_call | solution.py:350
  38.9 2.9 %attend_last.1 = (bf16[256,256]{1,0:T(8,128)(2,1)S(1)}, bf16[256,256]{1,0:T(8,128)(2,1)S(1)}, bf16[256,256]{1,0:T(8,128)(2,1)S(1)}, bf16[256,256]{1,0:T(8,128)(2...) custom-call(s32[18]{0:T(128)S(1)} %stack.83.info, ...), custom_call_target="tpu_custom_call" | custom-call | flops 1048576 | bytes 1024 | tf_op jit(solution)/shard_map/attend_last/pallas_call | solution.py:350
  41.8 1.8 %collective-permute-start.31 = (bf16[256,256]{1,0:T(8,128)(2,1)S(1)}, bf16[256,256]{1,0:T(8,128)(2,1)S(1)}, u32[]{:S(2)}, u32[]{:S(2)}) collective-permute-start(bf16[256,256]{1,0:T(8,128)(2,1)S(1)} %get-tuple-element.79), channel_id=1, source_target_pairs={{0,2},{2,4},{4,6},{6,7},{7,5},{5,3},{3,1},{1,0},{8,10},{10,12},{12... | collective-permute-start | bytes 393224 | tf_op jit(solution)/shard_map/ppermute | solution.py:33
  43.5 0.3 collective-permute-start.27
  43.9 1.6 %collective-permute-start.24 = (bf16[256,256]{1,0:T(8,128)(2,1)S(1)}, bf16[256,256]{1,0:T(8,128)(2,1)S(1)}, u32[]{:S(2)}, u32[]{:S(2)}) collective-permute-start(bf16[256,256]{1,0:T(8,128)(2,1)S(1)} %get-tuple-element.71), channel_id=1, source_target_pairs={{0,1},{2,0},{4,2},{6,4},{7,6},{5,7},{3,5},{1,3},{8,9},{10,8},{12,1... | collective-permute-start | bytes 393224 | tf_op jit(solution)/shard_map/ppermute | solution.py:33
  45.4 0.5 collective-permute-start.21
  45.9 1.5 %collective-permute-done.31 = bf16[256,256]{1,0:T(8,128)(2,1)S(1)} collective-permute-done((bf16[256,256]{1,0:T(8,128)(2,1)S(1)}, bf16[256,256]{1,0:T(8,128)(2,1)S(1)}, u32[]{:S(2)}, u32[]{:S(2)}) %collective-permute-start.31) | collective-permute-done | bytes 131104 | tf_op jit(solution)/shard_map/ppermute | solution.py:33
  47.5 2.5 %collective-permute-start.32 = (bf16[256,256]{1,0:T(8,128)(2,1)S(1)}, bf16[256,256]{1,0:T(8,128)(2,1)S(1)}, u32[]{:S(2)}, u32[]{:S(2)}) collective-permute-start(bf16[256,256]{1,0:T(8,128)(2,1)S(1)} %add_convert_fusion.4), channel_id=1, source_target_pairs={{0,2},{2,4},{4,6},{6,7},{7,5},{5,3},{3,1},{1,0},{8,10},{10,12},{12... | collective-permute-start | bytes 393224 | tf_op jit(solution)/shard_map/ppermute | solution.py:33
  50.0 0.3 collective-permute-start.28
  50.4 1.9 %collective-permute-done.24 = bf16[256,256]{1,0:T(8,128)(2,1)S(1)} collective-permute-done((bf16[256,256]{1,0:T(8,128)(2,1)S(1)}, bf16[256,256]{1,0:T(8,128)(2,1)S(1)}, u32[]{:S(2)}, u32[]{:S(2)}) %collective-permute-start.24) | collective-permute-done | bytes 131104 | tf_op jit(solution)/shard_map/ppermute | solution.py:33
  52.3 0.4 collective-permute-start.25
  52.7 1.8 %collective-permute-start.22 = (bf16[256,256]{1,0:T(8,128)(2,1)S(1)}, bf16[256,256]{1,0:T(8,128)(2,1)S(1)}, u32[]{:S(2)}, u32[]{:S(2)}) collective-permute-start(bf16[256,256]{1,0:T(8,128)(2,1)S(1)} %add_convert_fusion.11), channel_id=1, source_target_pairs={{0,2},{2,4},{4,6},{6,7},{7,5},{5,3},{3,1},{1,0},{8,10},{10,12},{12... | collective-permute-start | bytes 393224 | tf_op jit(solution)/shard_map/ppermute | solution.py:33
  54.5 1.6 %collective-permute-start.33 = (bf16[256,256]{1,0:T(8,128)(2,1)S(1)}, bf16[256,256]{1,0:T(8,128)(2,1)S(1)}, u32[]{:S(2)}, u32[]{:S(2)}) collective-permute-start(bf16[256,256]{1,0:T(8,128)(2,1)S(1)} %add_convert_fusion.3), channel_id=1, source_target_pairs={{0,2},{2,4},{4,6},{6,7},{7,5},{5,3},{3,1},{1,0},{8,10},{10,12},{12... | collective-permute-start | bytes 393224 | tf_op jit(solution)/shard_map/ppermute | solution.py:33
  56.2 0.5 collective-permute-start.29
  56.7 2.0 %collective-permute-done.25 = bf16[256,256]{1,0:T(8,128)(2,1)S(1)} collective-permute-done((bf16[256,256]{1,0:T(8,128)(2,1)S(1)}, bf16[256,256]{1,0:T(8,128)(2,1)S(1)}, u32[]{:S(2)}, u32[]{:S(2)}) %collective-permute-start.25) | collective-permute-done | bytes 131104 | tf_op jit(solution)/shard_map/ppermute | solution.py:33
  58.9 1.9 %collective-permute-start.23 = (bf16[256,256]{1,0:T(8,128)(2,1)S(1)}, bf16[256,256]{1,0:T(8,128)(2,1)S(1)}, u32[]{:S(2)}, u32[]{:S(2)}) collective-permute-start(bf16[256,256]{1,0:T(8,128)(2,1)S(1)} %add_convert_fusion.10), channel_id=1, source_target_pairs={{0,2},{2,4},{4,6},{6,7},{7,5},{5,3},{3,1},{1,0},{8,10},{10,12},{12... | collective-permute-start | bytes 393224 | tf_op jit(solution)/shard_map/ppermute | solution.py:33
  61.0 1.5 %collective-permute-start.34 = (bf16[256,256]{1,0:T(8,128)(2,1)S(1)}, bf16[256,256]{1,0:T(8,128)(2,1)S(1)}, u32[]{:S(2)}, u32[]{:S(2)}) collective-permute-start(bf16[256,256]{1,0:T(8,128)(2,1)S(1)} %add_convert_fusion.2), channel_id=1, source_target_pairs={{0,2},{2,4},{4,6},{6,7},{7,5},{5,3},{3,1},{1,0},{8,10},{10,12},{12... | collective-permute-start | bytes 393224 | tf_op jit(solution)/shard_map/ppermute | solution.py:33
  62.5 0.6 collective-permute-start.30
  63.1 1.2 %collective-permute-done.26 = bf16[256,256]{1,0:T(8,128)(2,1)S(1)} collective-permute-done((bf16[256,256]{1,0:T(8,128)(2,1)S(1)}, bf16[256,256]{1,0:T(8,128)(2,1)S(1)}, u32[]{:S(2)}, u32[]{:S(2)}) %collective-permute-start.26) | collective-permute-done | bytes 131104 | tf_op jit(solution)/shard_map/ppermute | solution.py:33
  64.4 1.6 %collective-permute-done.34 = bf16[256,256]{1,0:T(8,128)(2,1)S(1)} collective-permute-done((bf16[256,256]{1,0:T(8,128)(2,1)S(1)}, bf16[256,256]{1,0:T(8,128)(2,1)S(1)}, u32[]{:S(2)}, u32[]{:S(2)}) %collective-permute-start.34) | collective-permute-done | bytes 131104 | tf_op jit(solution)/shard_map/ppermute | solution.py:33
  66.0 1.6 %collective-permute-done.30 = bf16[256,256]{1,0:T(8,128)(2,1)S(1)} collective-permute-done((bf16[256,256]{1,0:T(8,128)(2,1)S(1)}, bf16[256,256]{1,0:T(8,128)(2,1)S(1)}, u32[]{:S(2)}, u32[]{:S(2)}) %collective-permute-start.30) | collective-permute-done | bytes 131104 | tf_op jit(solution)/shard_map/ppermute | solution.py:33
  67.7 0.7 %pad_maximum_fusion = bf16[512,256]{1,0:T(8,128)(2,1)} fusion(bf16[256,256]{1,0:T(8,128)(2,1)S(1)} %get-tuple-element.87, bf16[256,256]{1,0:T(8,128)(2,1)S(1)} %get-tuple-element.88), kind=kLoop, calls=%fused_computation | loop fusion | flops 524288 | bytes 524288 | tf_op jit(solution)/shard_map/concatenate | solution.py:452
  (50 shorter events, 2.9 us)
Async XLA Ops:
  1.0 6.7 %collective-permute-start.3 = (bf16[256,256]{1,0:T(8,128)(2,1)S(1)}, bf16[256,256]{1,0:T(8,128)(2,1)S(1)}, u32[]{:S(2)}, u32[]{:S(2)}) collective-permute-start(bf16[256,256]{1,0:T(8,128)(2,1)S(1)} %get-tuple-element.85), channel_id=1, source_target_pairs={{0,1},{2,0},{4,2},{6,4},{7,6},{5,7},{3,5},{1,3},{8,9},{10,8},{12,1... | collective-permute-start | bytes 393224 | tf_op jit(solution)/shard_map/ppermute | solution.py:33
  1.5 6.7 %collective-permute-start = (bf16[256,256]{1,0:T(8,128)(2,1)S(1)}, bf16[256,256]{1,0:T(8,128)(2,1)S(1)}, u32[]{:S(2)}, u32[]{:S(2)}) collective-permute-start(bf16[256,256]{1,0:T(8,128)(2,1)S(1)} %get-tuple-element.86), channel_id=1, source_target_pairs={{0,2},{2,4},{4,6},{6,7},{7,5},{5,3},{3,1},{1,0},{8,10},{10,12},{12... | collective-permute-start | bytes 393224 | tf_op jit(solution)/shard_map/ppermute | solution.py:33
  3.1 6.7 %collective-permute-start.6 = (bf16[256,256]{1,0:T(8,128)(2,1)S(1)}, bf16[256,256]{1,0:T(8,128)(2,1)S(1)}, u32[]{:S(2)}, u32[]{:S(2)}) collective-permute-start(bf16[256,256]{1,0:T(8,128)(2,1)S(1)} %get-tuple-element.86), channel_id=1, source_target_pairs={{0,1},{2,0},{4,2},{6,4},{7,6},{5,7},{3,5},{1,3},{8,9},{10,8},{12,1... | collective-permute-start | bytes 393224 | tf_op jit(solution)/shard_map/ppermute | solution.py:33
  3.5 6.7 %collective-permute-start.8 = (bf16[256,256]{1,0:T(8,128)(2,1)S(1)}, bf16[256,256]{1,0:T(8,128)(2,1)S(1)}, u32[]{:S(2)}, u32[]{:S(2)}) collective-permute-start(bf16[256,256]{1,0:T(8,128)(2,1)S(1)} %get-tuple-element.85), channel_id=1, source_target_pairs={{0,2},{2,4},{4,6},{6,7},{7,5},{5,3},{3,1},{1,0},{8,10},{10,12},{12... | collective-permute-start | bytes 393224 | tf_op jit(solution)/shard_map/ppermute | solution.py:33
  7.7 6.2 %collective-permute-start.4 = (bf16[256,256]{1,0:T(8,128)(2,1)S(1)}, bf16[256,256]{1,0:T(8,128)(2,1)S(1)}, u32[]{:S(2)}, u32[]{:S(2)}) collective-permute-start(bf16[256,256]{1,0:T(8,128)(2,1)S(1)} %collective-permute-done.3.refs_1_), channel_id=1, source_target_pairs={{0,1},{2,0},{4,2},{6,4},{7,6},{5,7},{3,5},{1,3},{8,9},{10,8},{12,1... | collective-permute-start | bytes 393224 | tf_op jit(solution)/shard_map/ppermute | solution.py:33
  8.2 6.0 %collective-permute-start.1 = (bf16[256,256]{1,0:T(8,128)(2,1)S(1)}, bf16[256,256]{1,0:T(8,128)(2,1)S(1)}, u32[]{:S(2)}, u32[]{:S(2)}) collective-permute-start(bf16[256,256]{1,0:T(8,128)(2,1)S(1)} %collective-permute-done.refs_0_), channel_id=1, source_target_pairs={{0,2},{2,4},{4,6},{6,7},{7,5},{5,3},{3,1},{1,0},{8,10},{10,12},{12... | collective-permute-start | bytes 393224 | tf_op jit(solution)/shard_map/ppermute | solution.py:33
  9.8 6.9 %collective-permute-start.7 = (bf16[256,256]{1,0:T(8,128)(2,1)S(1)}, bf16[256,256]{1,0:T(8,128)(2,1)S(1)}, u32[]{:S(2)}, u32[]{:S(2)}) collective-permute-start(bf16[256,256]{1,0:T(8,128)(2,1)S(1)} %collective-permute-done.6.refs_2_), channel_id=1, source_target_pairs={{0,1},{2,0},{4,2},{6,4},{7,6},{5,7},{3,5},{1,3},{8,9},{10,8},{12,1... | collective-permute-start | bytes 393224 | tf_op jit(solution)/shard_map/ppermute | solution.py:33
  10.3 6.8 %collective-permute-start.9 = (bf16[256,256]{1,0:T(8,128)(2,1)S(1)}, bf16[256,256]{1,0:T(8,128)(2,1)S(1)}, u32[]{:S(2)}, u32[]{:S(2)}) collective-permute-start(bf16[256,256]{1,0:T(8,128)(2,1)S(1)} %collective-permute-done.8.refs_3_), channel_id=1, source_target_pairs={{0,2},{2,4},{4,6},{6,7},{7,5},{5,3},{3,1},{1,0},{8,10},{10,12},{12... | collective-permute-start | bytes 393224 | tf_op jit(solution)/shard_map/ppermute | solution.py:33
  13.9 5.7 %collective-permute-start.5 = (bf16[256,256]{1,0:T(8,128)(2,1)S(1)}, bf16[256,256]{1,0:T(8,128)(2,1)S(1)}, u32[]{:S(2)}, u32[]{:S(2)}) collective-permute-start(bf16[256,256]{1,0:T(8,128)(2,1)S(1)} %collective-permute-done.4.refs_1_), channel_id=1, source_target_pairs={{0,1},{2,0},{4,2},{6,4},{7,6},{5,7},{3,5},{1,3},{8,9},{10,8},{12,1... | collective-permute-start | bytes 393224 | tf_op jit(solution)/shard_map/ppermute | solution.py:33
  14.2 5.7 %collective-permute-start.2 = (bf16[256,256]{1,0:T(8,128)(2,1)S(1)}, bf16[256,256]{1,0:T(8,128)(2,1)S(1)}, u32[]{:S(2)}, u32[]{:S(2)}) collective-permute-start(bf16[256,256]{1,0:T(8,128)(2,1)S(1)} %collective-permute-done.1.refs_0_), channel_id=1, source_target_pairs={{0,2},{2,4},{4,6},{6,7},{7,5},{5,3},{3,1},{1,0},{8,10},{10,12},{12... | collective-permute-start | bytes 393224 | tf_op jit(solution)/shard_map/ppermute | solution.py:33
  16.7 5.1 %collective-permute-start.10 = (bf16[256,256]{1,0:T(8,128)(2,1)S(1)}, bf16[256,256]{1,0:T(8,128)(2,1)S(1)}, u32[]{:S(2)}, u32[]{:S(2)}) collective-permute-start(bf16[256,256]{1,0:T(8,128)(2,1)S(1)} %collective-permute-done.7.refs_2_), channel_id=1, source_target_pairs={{0,1},{2,0},{4,2},{6,4},{7,6},{5,7},{3,5},{1,3},{8,9},{10,8},{12,1... | collective-permute-start | bytes 393224 | tf_op jit(solution)/shard_map/ppermute | solution.py:33
  17.0 5.0 %collective-permute-start.11 = (bf16[256,256]{1,0:T(8,128)(2,1)S(1)}, bf16[256,256]{1,0:T(8,128)(2,1)S(1)}, u32[]{:S(2)}, u32[]{:S(2)}) collective-permute-start(bf16[256,256]{1,0:T(8,128)(2,1)S(1)} %collective-permute-done.9.refs_3_), channel_id=1, source_target_pairs={{0,2},{2,4},{4,6},{6,7},{7,5},{5,3},{3,1},{1,0},{8,10},{10,12},{12... | collective-permute-start | bytes 393224 | tf_op jit(solution)/shard_map/ppermute | solution.py:33
  19.7 5.0 %collective-permute-start.13 = (bf16[256,256]{1,0:T(8,128)(2,1)S(1)}, bf16[256,256]{1,0:T(8,128)(2,1)S(1)}, u32[]{:S(2)}, u32[]{:S(2)}) collective-permute-start(bf16[256,256]{1,0:T(8,128)(2,1)S(1)} %collective-permute-done.5.refs_1_), channel_id=1, source_target_pairs={{0,1},{2,0},{4,2},{6,4},{7,6},{5,7},{3,5},{1,3},{8,9},{10,8},{12,1... | collective-permute-start | bytes 393224 | tf_op jit(solution)/shard_map/ppermute | solution.py:33
  19.9 5.0 %collective-permute-start.12 = (bf16[256,256]{1,0:T(8,128)(2,1)S(1)}, bf16[256,256]{1,0:T(8,128)(2,1)S(1)}, u32[]{:S(2)}, u32[]{:S(2)}) collective-permute-start(bf16[256,256]{1,0:T(8,128)(2,1)S(1)} %collective-permute-done.2.refs_0_), channel_id=1, source_target_pairs={{0,2},{2,4},{4,6},{6,7},{7,5},{5,3},{3,1},{1,0},{8,10},{10,12},{12... | collective-permute-start | bytes 393224 | tf_op jit(solution)/shard_map/ppermute | solution.py:33
  26.2 7.3 %collective-permute-start.17 = (bf16[256,512]{1,0:T(8,128)(2,1)S(1)}, bf16[256,512]{1,0:T(8,128)(2,1)S(1)}, u32[]{:S(2)}, u32[]{:S(2)}) collective-permute-start(bf16[256,512]{1,0:T(8,128)(2,1)S(1)} %get-tuple-element.53.refs_0_), channel_id=1, source_target_pairs={{0,16},{8,24},{16,0},{24,8},{1,17},{9,25},{17,1},{25,9},{2,18},{10... | collective-permute-start | bytes 786440 | tf_op jit(solution)/shard_map/ppermute | solution.py:425
  26.8 9.2 %collective-permute-start.18 = (bf16[256,512]{1,0:T(8,128)(2,1)S(1)}, bf16[256,512]{1,0:T(8,128)(2,1)S(1)}, u32[]{:S(2)}, u32[]{:S(2)}) collective-permute-start(bf16[256,512]{1,0:T(8,128)(2,1)S(1)} %get-tuple-element.54.refs_1_), channel_id=1, source_target_pairs={{0,16},{8,24},{16,0},{24,8},{1,17},{9,25},{17,1},{25,9},{2,18},{10... | collective-permute-start | bytes 786440 | tf_op jit(solution)/shard_map/ppermute | solution.py:425
  28.3 2.9 %collective-permute-start.15 = (bf16[176,512]{1,0:T(8,128)(2,1)S(1)}, bf16[176,512]{1,0:T(8,128)(2,1)S(1)}, u32[]{:S(2)}, u32[]{:S(2)}) collective-permute-start(bf16[176,512]{1,0:T(8,128)(2,1)S(1)} %get-tuple-element.56), channel_id=1, source_target_pairs={{0,8},{8,0},{16,24},{24,16},{1,9},{9,1},{17,25},{25,17},{2,10},{10... | collective-permute-start | bytes 540680 | tf_op jit(solution)/shard_map/ppermute | solution.py:39
  28.3 2.9 %collective-permute-start.16 = (bf16[176,512]{1,0:T(8,128)(2,1)S(1)}, bf16[176,512]{1,0:T(8,128)(2,1)S(1)}, u32[]{:S(2)}, u32[]{:S(2)}) collective-permute-start(bf16[176,512]{1,0:T(8,128)(2,1)S(1)} %get-tuple-element.57), channel_id=1, source_target_pairs={{0,8},{8,0},{16,24},{24,16},{1,9},{9,1},{17,25},{25,17},{2,10},{10... | collective-permute-start | bytes 540680 | tf_op jit(solution)/shard_map/ppermute | solution.py:39
  28.8 2.4 %collective-permute-start.14 = (bf16[160,512]{1,0:T(8,128)(2,1)S(1)}, bf16[160,512]{1,0:T(8,128)(2,1)S(1)}, u32[]{:S(2)}, u32[]{:S(2)}) collective-permute-start(bf16[160,512]{1,0:T(8,128)(2,1)S(1)} %get-tuple-element.55), channel_id=1, source_target_pairs={{0,8},{8,0},{16,24},{24,16},{1,9},{9,1},{17,25},{25,17},{2,10},{10... | collective-permute-start | bytes 491528 | tf_op jit(solution)/shard_map/ppermute | solution.py:39
  36.0 2.8 %collective-permute-start.19 = (bf16[256,512]{1,0:T(8,128)(2,1)S(1)}, bf16[256,512]{1,0:T(8,128)(2,1)S(1)}, u32[]{:S(2)}, u32[]{:S(2)}) collective-permute-start(bf16[256,512]{1,0:T(8,128)(2,1)S(1)} %collective-permute-done.17.refs_0_), channel_id=1, source_target_pairs={{0,8},{8,0},{16,24},{24,16},{1,9},{9,1},{17,25},{25,17},{2,10},{10... | collective-permute-start | bytes 786440 | tf_op jit(solution)/shard_map/ppermute | solution.py:39
  36.0 2.8 %collective-permute-start.20 = (bf16[256,512]{1,0:T(8,128)(2,1)S(1)}, bf16[256,512]{1,0:T(8,128)(2,1)S(1)}, u32[]{:S(2)}, u32[]{:S(2)}) collective-permute-start(bf16[256,512]{1,0:T(8,128)(2,1)S(1)} %collective-permute-done.18.refs_1_), channel_id=1, source_target_pairs={{0,8},{8,0},{16,24},{24,16},{1,9},{9,1},{17,25},{25,17},{2,10},{10... | collective-permute-start | bytes 786440 | tf_op jit(solution)/shard_map/ppermute | solution.py:39
  41.8 5.6 %collective-permute-start.31 = (bf16[256,256]{1,0:T(8,128)(2,1)S(1)}, bf16[256,256]{1,0:T(8,128)(2,1)S(1)}, u32[]{:S(2)}, u32[]{:S(2)}) collective-permute-start(bf16[256,256]{1,0:T(8,128)(2,1)S(1)} %get-tuple-element.79), channel_id=1, source_target_pairs={{0,2},{2,4},{4,6},{6,7},{7,5},{5,3},{3,1},{1,0},{8,10},{10,12},{12... | collective-permute-start | bytes 393224 | tf_op jit(solution)/shard_map/ppermute | solution.py:33
  43.5 6.5 %collective-permute-start.27 = (bf16[256,256]{1,0:T(8,128)(2,1)S(1)}, bf16[256,256]{1,0:T(8,128)(2,1)S(1)}, u32[]{:S(2)}, u32[]{:S(2)}) collective-permute-start(bf16[256,256]{1,0:T(8,128)(2,1)S(1)} %get-tuple-element.75), channel_id=1, source_target_pairs={{0,1},{2,0},{4,2},{6,4},{7,6},{5,7},{3,5},{1,3},{8,9},{10,8},{12,1... | collective-permute-start | bytes 393224 | tf_op jit(solution)/shard_map/ppermute | solution.py:33
  43.9 8.4 %collective-permute-start.24 = (bf16[256,256]{1,0:T(8,128)(2,1)S(1)}, bf16[256,256]{1,0:T(8,128)(2,1)S(1)}, u32[]{:S(2)}, u32[]{:S(2)}) collective-permute-start(bf16[256,256]{1,0:T(8,128)(2,1)S(1)} %get-tuple-element.71), channel_id=1, source_target_pairs={{0,1},{2,0},{4,2},{6,4},{7,6},{5,7},{3,5},{1,3},{8,9},{10,8},{12,1... | collective-permute-start | bytes 393224 | tf_op jit(solution)/shard_map/ppermute | solution.py:33
  45.4 7.3 %collective-permute-start.21 = (bf16[256,256]{1,0:T(8,128)(2,1)S(1)}, bf16[256,256]{1,0:T(8,128)(2,1)S(1)}, u32[]{:S(2)}, u32[]{:S(2)}) collective-permute-start(bf16[256,256]{1,0:T(8,128)(2,1)S(1)} %get-tuple-element.68), channel_id=1, source_target_pairs={{0,2},{2,4},{4,6},{6,7},{7,5},{5,3},{3,1},{1,0},{8,10},{10,12},{12... | collective-permute-start | bytes 393224 | tf_op jit(solution)/shard_map/ppermute | solution.py:33
  47.5 7.0 %collective-permute-start.32 = (bf16[256,256]{1,0:T(8,128)(2,1)S(1)}, bf16[256,256]{1,0:T(8,128)(2,1)S(1)}, u32[]{:S(2)}, u32[]{:S(2)}) collective-permute-start(bf16[256,256]{1,0:T(8,128)(2,1)S(1)} %add_convert_fusion.4), channel_id=1, source_target_pairs={{0,2},{2,4},{4,6},{6,7},{7,5},{5,3},{3,1},{1,0},{8,10},{10,12},{12... | collective-permute-start | bytes 393224 | tf_op jit(solution)/shard_map/ppermute | solution.py:33
  50.0 6.1 %collective-permute-start.28 = (bf16[256,256]{1,0:T(8,128)(2,1)S(1)}, bf16[256,256]{1,0:T(8,128)(2,1)S(1)}, u32[]{:S(2)}, u32[]{:S(2)}) collective-permute-start(bf16[256,256]{1,0:T(8,128)(2,1)S(1)} %add_convert_fusion.7), channel_id=1, source_target_pairs={{0,1},{2,0},{4,2},{6,4},{7,6},{5,7},{3,5},{1,3},{8,9},{10,8},{12,1... | collective-permute-start | bytes 393224 | tf_op jit(solution)/shard_map/ppermute | solution.py:33
  52.3 6.3 %collective-permute-start.25 = (bf16[256,256]{1,0:T(8,128)(2,1)S(1)}, bf16[256,256]{1,0:T(8,128)(2,1)S(1)}, u32[]{:S(2)}, u32[]{:S(2)}) collective-permute-start(bf16[256,256]{1,0:T(8,128)(2,1)S(1)} %add_convert_fusion.9), channel_id=1, source_target_pairs={{0,1},{2,0},{4,2},{6,4},{7,6},{5,7},{3,5},{1,3},{8,9},{10,8},{12,1... | collective-permute-start | bytes 393224 | tf_op jit(solution)/shard_map/ppermute | solution.py:33
  52.7 6.2 %collective-permute-start.22 = (bf16[256,256]{1,0:T(8,128)(2,1)S(1)}, bf16[256,256]{1,0:T(8,128)(2,1)S(1)}, u32[]{:S(2)}, u32[]{:S(2)}) collective-permute-start(bf16[256,256]{1,0:T(8,128)(2,1)S(1)} %add_convert_fusion.11), channel_id=1, source_target_pairs={{0,2},{2,4},{4,6},{6,7},{7,5},{5,3},{3,1},{1,0},{8,10},{10,12},{12... | collective-permute-start | bytes 393224 | tf_op jit(solution)/shard_map/ppermute | solution.py:33
  54.5 6.4 %collective-permute-start.33 = (bf16[256,256]{1,0:T(8,128)(2,1)S(1)}, bf16[256,256]{1,0:T(8,128)(2,1)S(1)}, u32[]{:S(2)}, u32[]{:S(2)}) collective-permute-start(bf16[256,256]{1,0:T(8,128)(2,1)S(1)} %add_convert_fusion.3), channel_id=1, source_target_pairs={{0,2},{2,4},{4,6},{6,7},{7,5},{5,3},{3,1},{1,0},{8,10},{10,12},{12... | collective-permute-start | bytes 393224 | tf_op jit(solution)/shard_map/ppermute | solution.py:33
  56.2 6.3 %collective-permute-start.29 = (bf16[256,256]{1,0:T(8,128)(2,1)S(1)}, bf16[256,256]{1,0:T(8,128)(2,1)S(1)}, u32[]{:S(2)}, u32[]{:S(2)}) collective-permute-start(bf16[256,256]{1,0:T(8,128)(2,1)S(1)} %add_convert_fusion.6), channel_id=1, source_target_pairs={{0,1},{2,0},{4,2},{6,4},{7,6},{5,7},{3,5},{1,3},{8,9},{10,8},{12,1... | collective-permute-start | bytes 393224 | tf_op jit(solution)/shard_map/ppermute | solution.py:33
  58.7 5.7 %collective-permute-start.26 = (bf16[256,256]{1,0:T(8,128)(2,1)S(1)}, bf16[256,256]{1,0:T(8,128)(2,1)S(1)}, u32[]{:S(2)}, u32[]{:S(2)}) collective-permute-start(bf16[256,256]{1,0:T(8,128)(2,1)S(1)} %add_convert_fusion.8), channel_id=1, source_target_pairs={{0,1},{2,0},{4,2},{6,4},{7,6},{5,7},{3,5},{1,3},{8,9},{10,8},{12,1... | collective-permute-start | bytes 393224 | tf_op jit(solution)/shard_map/ppermute | solution.py:33
  58.9 5.4 %collective-permute-start.23 = (bf16[256,256]{1,0:T(8,128)(2,1)S(1)}, bf16[256,256]{1,0:T(8,128)(2,1)S(1)}, u32[]{:S(2)}, u32[]{:S(2)}) collective-permute-start(bf16[256,256]{1,0:T(8,128)(2,1)S(1)} %add_convert_fusion.10), channel_id=1, source_target_pairs={{0,2},{2,4},{4,6},{6,7},{7,5},{5,3},{3,1},{1,0},{8,10},{10,12},{12... | collective-permute-start | bytes 393224 | tf_op jit(solution)/shard_map/ppermute | solution.py:33
  61.0 5.0 %collective-permute-start.34 = (bf16[256,256]{1,0:T(8,128)(2,1)S(1)}, bf16[256,256]{1,0:T(8,128)(2,1)S(1)}, u32[]{:S(2)}, u32[]{:S(2)}) collective-permute-start(bf16[256,256]{1,0:T(8,128)(2,1)S(1)} %add_convert_fusion.2), channel_id=1, source_target_pairs={{0,2},{2,4},{4,6},{6,7},{7,5},{5,3},{3,1},{1,0},{8,10},{10,12},{12... | collective-permute-start | bytes 393224 | tf_op jit(solution)/shard_map/ppermute | solution.py:33
  62.5 5.0 %collective-permute-start.30 = (bf16[256,256]{1,0:T(8,128)(2,1)S(1)}, bf16[256,256]{1,0:T(8,128)(2,1)S(1)}, u32[]{:S(2)}, u32[]{:S(2)}) collective-permute-start(bf16[256,256]{1,0:T(8,128)(2,1)S(1)} %add_convert_fusion.5), channel_id=1, source_target_pairs={{0,1},{2,0},{4,2},{6,4},{7,6},{5,7},{3,5},{1,3},{8,9},{10,8},{12,1... | collective-permute-start | bytes 393224 | tf_op jit(solution)/shard_map/ppermute | solution.py:33

commit v22 on v21

--- a/solution.py
+++ b/solution.py
@@ -47,14 +47,18 @@
     return pltpu.with_memory_space_constraint(value, pltpu.VMEM)
 
 
-def load_kernel(order, at, w_hbm, tokens, out_ref, wide, sems):
+def load_kernel(order, groups, at, w_hbm, *refs):
     size = w_hbm.shape[1] // len(order)
-    copies = [pltpu.make_async_copy(tokens, wide.at[:, : tokens.shape[1]], sems.at[len(order)])]
+    sems, copies, out_ref = refs[-1], [], refs[len(refs) // 2 - 1]
+    if len(refs) > 2:
+        tokens, wide = refs[0], refs[2]
+        place = wide.at[:, : tokens.shape[1]]
+        copies.append(pltpu.make_async_copy(tokens, place, sems.at[len(order)]))
     for n in range(len(order)):
         start = pl.multiple_of(at[order[n]] * size, size)
         copies.append(
             pltpu.make_async_copy(
-                w_hbm.at[:, pl.ds(start, size), :],
+                w_hbm.at[groups[0] : groups[-1] + 1, pl.ds(start, size), :],
                 out_ref.at[:, n * size : (n + 1) * size, :],
                 sems.at[n],
             )
@@ -65,23 +69,25 @@
         copy.wait()
 
 
-def loaded(order, at, weights, tokens):
-    hbm = pl.BlockSpec(memory_space=pltpu.HBM)
+def loaded(order, groups, at, weights, tokens=None):
+    hbm, spot = pl.BlockSpec(memory_space=pltpu.HBM), pl.BlockSpec(memory_space=pl.ANY)
+    depth, width = weights.shape[1:]
+    operands = [at, in_hbm(weights)]
+    shapes = [pltpu.VMEM((len(groups), depth, width), BF16)]
+    if tokens is not None:
+        operands.append(in_hbm(tokens))
+        shapes.append(pltpu.VMEM((tokens.shape[0], depth), BF16))
+    size = len(groups) * depth * width
     return pl.pallas_call(
-        functools.partial(load_kernel, order),
-        out_shape=(
-            pltpu.VMEM(weights.shape, BF16),
-            pltpu.VMEM((tokens.shape[0], weights.shape[1]), BF16),
-        ),
-        in_specs=[SMEM, hbm, hbm],
-        out_specs=(pl.BlockSpec(memory_space=pl.ANY),) * 2,
+        functools.partial(load_kernel, order, groups),
+        out_shape=tuple(shapes),
+        in_specs=[SMEM] + [hbm] * (len(operands) - 1),
+        out_specs=(spot,) * len(shapes),
         scratch_shapes=[pltpu.SemaphoreType.DMA((len(order) + 1,))],
         compiler_params=pltpu.CompilerParams(vmem_limit_bytes=1 << 20),
-        cost_estimate=pl.CostEstimate(
-            flops=weights.size, bytes_accessed=4 * weights.size, transcendentals=0
-        ),
+        cost_estimate=pl.CostEstimate(flops=size, bytes_accessed=4 * size, transcendentals=0),
         name="load",
-    )(at, in_hbm(weights), in_hbm(tokens))
+    )(*operands)
 
 
 def gain_of(gain_ref, offset, ring, part, parts):
@@ -118,10 +124,11 @@
     )(*operands)
 
 
-def begin_kernel(order, gain_ref, wide, w_ref, state, scaled):
+def begin_kernel(order, gain_ref, wide, wq_ref, wkv_ref, state, scaled):
     rows, depth = wide.shape
     ring = len(order)
-    out_width, parts = w_ref.shape[2], depth // ring // 128
+    out_width, parts = wq_ref.shape[2], depth // ring // 128
+    weights = [wq_ref.at[0], wkv_ref.at[0], wkv_ref.at[1]]
     tile, done = scaled.shape
     for first in range(0, rows, tile):
         here = slice(first, first + tile)
@@ -135,16 +142,17 @@
         state[here, 3 * out_width :] = power
         for group in range(3):
             state[here, group * out_width : (group + 1) * out_width] = jnp.dot(
-                scaled[...], w_ref[group, :done, :], preferred_element_type=F32
+                scaled[...], weights[group][:done, :], preferred_element_type=F32
             )
 
 
-def finish_kernel(head_size, order, factor, gain_ref, state, w_ref, *refs):
+def finish_kernel(head_size, order, factor, gain_ref, state, wq_ref, wkv_ref, *refs):
     count = 2
     lasts, q_ref = refs[:count], refs[count]
     halves, pieces = refs[count + 1 : 2 * count + 1], refs[2 * count + 1 :]
     rows, width = lasts[0].shape
-    depth, out_width = w_ref.shape[1:]
+    depth, out_width = wq_ref.shape[1:]
+    weights = [wq_ref.at[0], wkv_ref.at[0], wkv_ref.at[1]]
     for stream, last in enumerate(lasts):
         here = slice(stream * rows, (stream + 1) * rows)
         kv_ref = halves[stream]
@@ -158,7 +166,7 @@
         scaled = jnp.concatenate(scaled, axis=1)
         q, k, v = (
             state[here, group * out_width : (group + 1) * out_width]
-            + jnp.dot(scaled, w_ref[group, depth - width :, :], preferred_element_type=F32)
+            + jnp.dot(scaled, weights[group][depth - width :, :], preferred_element_type=F32)
             for group in range(3)
         )
         scale = lax.rsqrt(jnp.sum(power, axis=-1, keepdims=True) * (1.0 / depth) + 1e-06)
@@ -182,14 +190,14 @@
         start = end
 
 
-def project_begin(gain, wide, weights, order):
+def project_begin(gain, wide, w_q, w_kv, order):
     rows, depth = wide.shape
     done = depth - depth // len(order)
-    groups, _, out_width = weights.shape
+    groups, out_width = 3, w_q.shape[2]
     return pl.pallas_call(
         functools.partial(begin_kernel, order),
         out_shape=pltpu.VMEM((rows, groups * out_width + 128), F32),
-        in_specs=[VMEM] * 3,
+        in_specs=[VMEM] * 4,
         out_specs=VMEM,
         scratch_shapes=[pltpu.VMEM((math.gcd(rows, 256), done), BF16)],
         compiler_params=pltpu.CompilerParams(vmem_limit_bytes=16 << 20),
@@ -199,12 +207,12 @@
             transcendentals=0,
         ),
         name="project_begin",
-    )(in_hbm(gain), in_vmem(wide), in_vmem(weights))
-
-
-def project_finish(factor, gain, state, weights, lasts, count_pieces, order, head_size):
+    )(in_hbm(gain), in_vmem(wide), in_vmem(w_q), in_vmem(w_kv))
+
+
+def project_finish(factor, gain, state, w_q, w_kv, lasts, count_pieces, order, head_size):
     rows, width = lasts[0].shape
-    out_width = weights.shape[2]
+    out_width = w_q.shape[2]
     total = rows * len(lasts)
     units = total // 16
     sizes = [rows] * len(lasts)
@@ -215,20 +223,22 @@
             pltpu.VMEM((total, out_width), BF16),
             *[pltpu.VMEM((size, 2 * out_width), BF16) for size in sizes],
         ),
-        in_specs=[SMEM] + [VMEM] * (3 + len(lasts)),
+        in_specs=[SMEM] + [VMEM] * (4 + len(lasts)),
         out_specs=(VMEM,) * (1 + len(sizes)),
         compiler_params=pltpu.CompilerParams(vmem_limit_bytes=16 << 20),
         cost_estimate=pl.CostEstimate(
             flops=6 * total * width * out_width, bytes_accessed=8 * total * out_width, transcendentals=0
         ),
         name="project_finish",
-    )(in_hbm(factor), in_hbm(gain), in_vmem(state), in_vmem(weights), *map(in_vmem, lasts))
+    )(in_hbm(factor), in_hbm(gain), *map(in_vmem, (state, w_q, w_kv)), *map(in_vmem, lasts))
 
 
 def attend_kernel(
-    head_size, counts, has_acc, count_out, count_streams, info, ids, id_row, q_ref, *refs
+    head_size, counts, has_acc, goals, info, ids, id_row, q_ref, *refs
 ):
     count_blocks, count_parts = counts
+    count_streams = len(goals)
+    count_out = sum(map(len, goals))
     kv_refs, rest = refs[: count_blocks * count_parts], refs[count_blocks * count_parts :]
     if has_acc:
         acc_in, rest = rest[0], rest[1:]
@@ -308,22 +318,26 @@
         ).astype(BF16)
     out_rows, out_width = outs[0].shape
     fetch_w.wait()
-    for number, out in enumerate(outs):
-        lane = info[count_blocks + 1 + number] * out_width
-        first = number * count_streams // count_out * out_rows
-        out[...] = jnp.dot(
-            attended[first : first + out_rows, :],
+    per = count_out // count_streams
+    for offset in range(per):
+        picks = [own.index(offset) for own in goals]
+        lane = info[count_blocks + 1 + picks[0]] * out_width
+        product = jnp.dot(
+            attended[...],
             w_ref[:, pl.ds(pl.multiple_of(lane, out_width), out_width)],
             preferred_element_type=F32,
-        ).astype(BF16)
-
-
-def attend(info, ids, query, blocks, head_size, acc=None, w_out=None, streams=0):
+        )
+        for stream, pick in enumerate(picks):
+            rows_of = slice(stream * out_rows, (stream + 1) * out_rows)
+            outs[stream * per + pick][...] = product[rows_of, :].astype(BF16)
+
+
+def attend(info, ids, query, blocks, head_size, acc=None, w_out=None, goals=()):
     total, width = query.shape
     parts = [part for block in blocks for part in block]
     keys = sum(part.shape[0] for part in blocks[0])
     heads = width // head_size
-    count_out = streams * w_out.shape[1] // width if streams else 0
+    streams, count_out = len(goals), sum(map(len, goals))
     scratch = [
         pltpu.VMEM((keys, width), BF16),
         pltpu.VMEM((heads, keys, 2 * head_size), BF16),
@@ -349,7 +363,7 @@
         in_specs[-1] = pl.BlockSpec(memory_space=pltpu.HBM)
     return pl.pallas_call(
         functools.partial(
-            attend_kernel, head_size, (len(blocks), len(blocks[0])), acc is not None, count_out, streams
+            attend_kernel, head_size, (len(blocks), len(blocks[0])), acc is not None, goals
         ),
         out_shape=(shape,) * outs,
         in_specs=in_specs,
@@ -393,10 +407,13 @@
             if step <= reach[s][way]:
                 held[s][way] = along(held[s][way], sign, ring)
         if step == 1:
-            held[0][0], (weights, wide) = lax.optimization_barrier(
-                (held[0][0], loaded(order, numbers(at), w_qkv, tokens))
+            held[0][0], (w_q, wide) = lax.optimization_barrier(
+                (held[0][0], loaded(order, (0,), numbers(at), w_qkv, tokens))
             )
         elif step == 2:
+            held[1][1], (w_kv,) = lax.optimization_barrier(
+                (held[1][1], loaded(order, (1, 2), numbers(at), w_qkv))
+            )
             wide = placed(targets, blocks, wide)
             blocks, targets = [], []
         elif step == 3:
@@ -411,8 +428,8 @@
     wide = placed(targets, blocks, wide)
     lasts = [held[0][0], held[1][1]]
     gain = norm_gain.reshape(-1, 128)
-    state = project_begin(gain, wide, weights, order)
-    query, *parts = project_finish(head_scale, gain, state, weights, lasts, 3, order, head_size)
+    state = project_begin(gain, wide, w_q, w_kv, order)
+    query, *parts = project_finish(head_scale, gain, state, w_q, w_kv, lasts, 3, order, head_size)
     halves, pieces = parts[:2], parts[2:]
 
     far, straight, crossed = [], [], []
@@ -435,7 +452,8 @@
     goals = [[*range(up, 0, -1), *range(-down, 0), 0] for up, down in reach]
     info = numbers(crossed[1:] + first + [at[goal % ring] for goal in goals[0] + goals[1]])
     parts = attend(
-        info, scale_ids, query, far_crossed, head_size, acc, w_out, len(streams)
+        info, scale_ids, query, far_crossed, head_size, acc, w_out,
+        [[goal % ring for goal in goals[s]] for s in streams],
     )
     parts = [dict(zip(goals[s], parts[s * ring : (s + 1) * ring])) for s in streams]
     sums = [[None, None] for s in streams]

time: 69.3 us -> 70.4 us (1.016)
  Pallas kernels: 16 us -> 17.6 us
  waiting for transfers between devices: 16.7 us -> 15.9 us
    ppermute x28, waiting for transfers between devices: 14.2 us -> 12.1 us  [along(): lax.ppermute(value, 'head', [(order[p], order[(p + step) % count]) for p...]
    pallas_call x1 -> x2, Pallas kernels: 2.53 us -> 4.06 us  [loaded(): pl.pallas_call(functools.partial(load_kernel, order, groups), out_shape=t...]
    ppermute x2, waiting for transfers between devices: 2.47 us -> 3.72 us  [body(): far.append([lax.ppermute(part, 'seq', shift) for part in halves])]
  transfers between devices with their start and end apart: 35 -> 35, of which waited for: 15 -> 13; matrix products, arithmetic and copies ran while one was open for 1% -> 1% of each run, Pallas kernels for 17% -> 19%
where the time goes in v22:
time: 70.4 us; the launch traced here: 69.2 us
  starting transfers between devices  33 us (47%)
  Pallas kernels  17.6 us (25%)
  waiting for transfers between devices  15.9 us (23%)
  other arithmetic  1.39 us (2%)
  local copies, waits for them, and re-layouts  1.16 us (2%)
    ppermute x28, starting transfers between devices, along(): lax.ppermute(value, 'head', [(order[p], order[(p + step) % count]) for p...  29.9 us
    ppermute x28, waiting for transfers between devices, along(): lax.ppermute(value, 'head', [(order[p], order[(p + step) % count]) for p...  12.1 us
    pallas_call x4, Pallas kernels, attend(): pl.pallas_call(functools.partial(attend_kernel, head_size, (len(blocks),...  9.54 us
    pallas_call x2, Pallas kernels, loaded(): pl.pallas_call(functools.partial(load_kernel, order, groups), out_shape=t...  4.06 us
    ppermute x2, waiting for transfers between devices, body(): far.append([lax.ppermute(part, 'seq', shift) for part in halves])  3.72 us
    pallas_call x1, Pallas kernels, project_begin(): pl.pallas_call(functools.partial(begin_kernel, order), out_shape=pltpu.VM...  2.3 us
    ppermute x2, starting transfers between devices, body(): far.append([lax.ppermute(part, 'seq', shift) for part in halves])  2.09 us
  transfers between devices with their start and end apart: 35, of which 13 were waited for; matrix products, arithmetic and copies ran while one was open for 1% of the time, Pallas kernels for 19%

profile of v22, /device:TPU:10, one launch (start us, length us, event | category | flops | bytes accessed | tf_op | source)
XLA Modules:
  0.0 69.2 jit_solution(8328832079267314897)
XLA Ops:
  0.0 1.0 %fusion = (bf16[256,256]{1,0:T(8,128)(2,1)S(1)}, bf16[256,256]{1,0:T(8,128)(2,1)S(1)}) fusion(bf16[512,256]{1,0:T(8,128)(2,1)} %refs_0_.1), kind=kLoop, calls=%fused_computation.16 | loop fusion | bytes 524288 | tf_op jit(solution)/shard_map/slice | solution.py:403
  1.0 0.5 collective-permute-start.3
  1.5 1.6 %collective-permute-start = (bf16[256,256]{1,0:T(8,128)(2,1)S(1)}, bf16[256,256]{1,0:T(8,128)(2,1)S(1)}, u32[]{:S(2)}, u32[]{:S(2)}) collective-permute-start(bf16[256,256]{1,0:T(8,128)(2,1)S(1)} %get-tuple-element.90), channel_id=1, source_target_pairs={{0,2},{2,4},{4,6},{6,7},{7,5},{5,3},{3,1},{1,0},{8,10},{10,12},{12... | collective-permute-start | bytes 393224 | tf_op jit(solution)/shard_map/ppermute | solution.py:33
  3.1 0.4 collective-permute-start.6
  3.5 1.6 %collective-permute-start.8 = (bf16[256,256]{1,0:T(8,128)(2,1)S(1)}, bf16[256,256]{1,0:T(8,128)(2,1)S(1)}, u32[]{:S(2)}, u32[]{:S(2)}) collective-permute-start(bf16[256,256]{1,0:T(8,128)(2,1)S(1)} %get-tuple-element.89), channel_id=1, source_target_pairs={{0,2},{2,4},{4,6},{6,7},{7,5},{5,3},{3,1},{1,0},{8,10},{10,12},{12... | collective-permute-start | bytes 393224 | tf_op jit(solution)/shard_map/ppermute | solution.py:33
  5.2 1.9 %load.2 = (bf16[1,2048,256]{2,1,0:T(8,128)(2,1)S(1)}, bf16[512,2048]{1,0:T(8,128)(2,1)S(1)}) custom-call(s32[8]{0:T(128)S(1)} %stack.93.at, bf16[3,2048,256]{2,1,0:T(8,128)(2,1)} %w_hbm.3, bf16[512,256]{1,0:T(8,128)(2,1)} %refs_0_.1), custom_call_target="tpu_custom_call" | custom-call | flops 524288 | bytes 2097152 | tf_op jit(solution)/shard_map/load/pallas_call | solution.py:81
  7.4 0.4 collective-permute-start.4
  7.9 1.6 %collective-permute-start.1 = (bf16[256,256]{1,0:T(8,128)(2,1)S(1)}, bf16[256,256]{1,0:T(8,128)(2,1)S(1)}, u32[]{:S(2)}, u32[]{:S(2)}) collective-permute-start(bf16[256,256]{1,0:T(8,128)(2,1)S(1)} %collective-permute-done.refs_0_), channel_id=1, source_target_pairs={{0,2},{2,4},{4,6},{6,7},{7,5},{5,3},{3,1},{1,0},{8,10},{10,12},{12... | collective-permute-start | bytes 393224 | tf_op jit(solution)/shard_map/ppermute | solution.py:33
  9.6 0.4 collective-permute-start.7
  10.1 1.6 %collective-permute-start.9 = (bf16[256,256]{1,0:T(8,128)(2,1)S(1)}, bf16[256,256]{1,0:T(8,128)(2,1)S(1)}, u32[]{:S(2)}, u32[]{:S(2)}) collective-permute-start(bf16[256,256]{1,0:T(8,128)(2,1)S(1)} %collective-permute-done.8.refs_3_), channel_id=1, source_target_pairs={{0,2},{2,4},{4,6},{6,7},{7,5},{5,3},{3,1},{1,0},{8,10},{10,12},{12... | collective-permute-start | bytes 393224 | tf_op jit(solution)/shard_map/ppermute | solution.py:33
  11.6 2.1 %load.3.wkv_ref = bf16[2,2048,256]{2,1,0:T(8,128)(2,1)S(1)} custom-call(s32[8]{0:T(128)S(1)} %stack.93.at, bf16[3,2048,256]{2,1,0:T(8,128)(2,1)} %w_hbm.3), custom_call_target="tpu_custom_call" | custom-call | flops 1048576 | bytes 4194304 | tf_op jit(solution)/shard_map/load/pallas_call | solution.py:81
  13.8 0.5 collective-permute-start.5
  14.3 1.6 %collective-permute-start.2 = (bf16[256,256]{1,0:T(8,128)(2,1)S(1)}, bf16[256,256]{1,0:T(8,128)(2,1)S(1)}, u32[]{:S(2)}, u32[]{:S(2)}) collective-permute-start(bf16[256,256]{1,0:T(8,128)(2,1)S(1)} %collective-permute-done.1.refs_0_), channel_id=1, source_target_pairs={{0,2},{2,4},{4,6},{6,7},{7,5},{5,3},{3,1},{1,0},{8,10},{10,12},{12... | collective-permute-start | bytes 393224 | tf_op jit(solution)/shard_map/ppermute | solution.py:33
  15.9 0.5 collective-permute-start.10
  16.3 1.6 %collective-permute-start.11 = (bf16[256,256]{1,0:T(8,128)(2,1)S(1)}, bf16[256,256]{1,0:T(8,128)(2,1)S(1)}, u32[]{:S(2)}, u32[]{:S(2)}) collective-permute-start(bf16[256,256]{1,0:T(8,128)(2,1)S(1)} %collective-permute-done.9.refs_3_), channel_id=1, source_target_pairs={{0,2},{2,4},{4,6},{6,7},{7,5},{5,3},{3,1},{1,0},{8,10},{10,12},{12... | collective-permute-start | bytes 393224 | tf_op jit(solution)/shard_map/ppermute | solution.py:33
  18.2 1.3 %collective-permute-done.5.refs_1_ = bf16[256,256]{1,0:T(8,128)(2,1)S(1)} collective-permute-done((bf16[256,256]{1,0:T(8,128)(2,1)S(1)}, bf16[256,256]{1,0:T(8,128)(2,1)S(1)}, u32[]{:S(2)}, u32[]{:S(2)}) %collective-permute-start.5) | collective-permute-done | bytes 131104 | tf_op jit(solution)/shard_map/ppermute | solution.py:33
  19.6 1.9 %collective-permute-start.12 = (bf16[256,256]{1,0:T(8,128)(2,1)S(1)}, bf16[256,256]{1,0:T(8,128)(2,1)S(1)}, u32[]{:S(2)}, u32[]{:S(2)}) collective-permute-start(bf16[256,256]{1,0:T(8,128)(2,1)S(1)} %collective-permute-done.2.refs_0_), channel_id=1, source_target_pairs={{0,2},{2,4},{4,6},{6,7},{7,5},{5,3},{3,1},{1,0},{8,10},{10,12},{12... | collective-permute-start | bytes 393224 | tf_op jit(solution)/shard_map/ppermute | solution.py:33
  22.2 2.3 %project_begin.1.state = f32[512,896]{1,0:T(8,128)S(1)} custom-call(f32[16,128]{1,0:T(8,128)} %bitcast.19, bf16[512,2048]{1,0:T(8,128)(2,1)S(1)} %place.5.wide, bf16[1,2048,256]{2,1,0:T(8,128)(2,1)S(1)} %get-tuple-element.54.wq_ref, bf16[2,2048,256]{2,1,0:T(8,128)(2,1)S(1)} %load.3.wkv_ref), custom_call_target="tpu_custom_call" | custom-call | flops 1610612736 | bytes 5242880 | tf_op jit(solution)/shard_map/project_begin/pallas_call | solution.py:197
  24.5 1.4 %project_finish.1 = (bf16[512,256]{1,0:T(8,128)(2,1)S(1)}, bf16[256,512]{1,0:T(8,128)(2,1)S(1)}, bf16[256,512]{1,0:T(8,128)(2,1)S(1)}, bf16[160,512]{1,0:T(8,128...) custom-call(f32[2]{0:T(128)} %factor.1, f32[16,128]{1,0:T(8,128)} %bitcast.20, ...), custom_call_target="tpu_custom_call" | custom-call | flops 201326592 | bytes 1048576 | tf_op jit(solution)/shard_map/project_finish/pallas_call | solution.py:220
  25.9 0.8 %collective-permute-start.17 = (bf16[256,512]{1,0:T(8,128)(2,1)S(1)}, bf16[256,512]{1,0:T(8,128)(2,1)S(1)}, u32[]{:S(2)}, u32[]{:S(2)}) collective-permute-start(bf16[256,512]{1,0:T(8,128)(2,1)S(1)} %get-tuple-element.57.refs_0_), channel_id=1, source_target_pairs={{0,16},{8,24},{16,0},{24,8},{1,17},{9,25},{17,1},{25,9},{2,18},{10... | collective-permute-start | bytes 786440 | tf_op jit(solution)/shard_map/ppermute | solution.py:442
  26.7 1.3 %collective-permute-start.18 = (bf16[256,512]{1,0:T(8,128)(2,1)S(1)}, bf16[256,512]{1,0:T(8,128)(2,1)S(1)}, u32[]{:S(2)}, u32[]{:S(2)}) collective-permute-start(bf16[256,512]{1,0:T(8,128)(2,1)S(1)} %get-tuple-element.58.refs_1_), channel_id=1, source_target_pairs={{0,16},{8,24},{16,0},{24,8},{1,17},{9,25},{17,1},{25,9},{2,18},{10... | collective-permute-start | bytes 786440 | tf_op jit(solution)/shard_map/ppermute | solution.py:442
  28.0 0.5 collective-permute-start.16
  28.6 2.2 %attend.3.refs_3_ = f32[512,512]{1,0:T(8,128)S(1)} custom-call(s32[2]{0:T(128)S(1)} %pad_add_fusion.1.info, s32[2048]{0:T(1024)} %ids.7, s32[8,1,256]{2,1,0:T(1,128)} %bitcast.15, bf16[512,256]{1,0:T(8,128)(2,1)S(1)} %get-tuple-element.56.q_ref, bf16[256,512]{1,0:T(8,128)(2,1)S(1)} %get-tuple-element.57.refs_0_, bf16[256,512]{1,0:T(8,128)(2,1)S(1)} %get-tuple-element.58.refs_1_), custom_call_target="tpu_custom_call" | custom-call | flops 1048576 | bytes 1024 | tf_op jit(solution)/shard_map/attend/pallas_call | solution.py:364
  30.9 2.2 %attend.4.refs_2_ = f32[512,512]{1,0:T(8,128)S(1)} custom-call(s32[2]{0:T(128)S(1)} %pad_add_fusion.info, s32[2048]{0:T(1024)} %ids.7, s32[8,1,256]{2,1,0:T(1,128)} %bitcast.16, bf16[512,256]{1,0:T(8,128)(2,1)S(1)} %get-tuple-element.56.q_ref, bf16[160,512]{1,0:T(8,128)(2,1)S(1)} %collective-permute-done.14.refs_0_, ...), custom_call_target="tpu_custom_call" | custom-call | flops 1048576 | bytes 1024 | tf_op jit(solution)/shard_map/attend/pallas_call | solution.py:364
  33.2 0.9 %collective-permute-done.17.refs_0_ = bf16[256,512]{1,0:T(8,128)(2,1)S(1)} collective-permute-done((bf16[256,512]{1,0:T(8,128)(2,1)S(1)}, bf16[256,512]{1,0:T(8,128)(2,1)S(1)}, u32[]{:S(2)}, u32[]{:S(2)}) %collective-permute-start.17) | collective-permute-done | bytes 262176 | tf_op jit(solution)/shard_map/ppermute | solution.py:442
  34.1 2.8 %collective-permute-done.18.refs_1_ = bf16[256,512]{1,0:T(8,128)(2,1)S(1)} collective-permute-done((bf16[256,512]{1,0:T(8,128)(2,1)S(1)}, bf16[256,512]{1,0:T(8,128)(2,1)S(1)}, u32[]{:S(2)}, u32[]{:S(2)}) %collective-permute-start.18) | collective-permute-done | bytes 262176 | tf_op jit(solution)/shard_map/ppermute | solution.py:442
  36.9 0.5 collective-permute-start.20
  37.6 2.1 %attend.5.refs_2_ = f32[512,512]{1,0:T(8,128)S(1)} custom-call(s32[2]{0:T(128)S(1)} %pad_add_fusion.2.info, s32[2048]{0:T(1024)} %ids.7, s32[8,1,256]{2,1,0:T(1,128)} %bitcast.17, bf16[512,256]{1,0:T(8,128)(2,1)S(1)} %get-tuple-element.56.q_ref, bf16[256,512]{1,0:T(8,128)(2,1)S(1)} %collective-permute-done.17.refs_0_, ...), custom_call_target="tpu_custom_call" | custom-call | flops 1048576 | bytes 1024 | tf_op jit(solution)/shard_map/attend/pallas_call | solution.py:364
  39.8 2.9 %attend_last.1 = (bf16[256,256]{1,0:T(8,128)(2,1)S(1)}, bf16[256,256]{1,0:T(8,128)(2,1)S(1)}, bf16[256,256]{1,0:T(8,128)(2,1)S(1)}, bf16[256,256]{1,0:T(8,128)(2...) custom-call(s32[18]{0:T(128)S(1)} %stack.92.info, ...), custom_call_target="tpu_custom_call" | custom-call | flops 1048576 | bytes 1024 | tf_op jit(solution)/shard_map/attend_last/pallas_call | solution.py:364
  42.7 1.6 %collective-permute-start.31 = (bf16[256,256]{1,0:T(8,128)(2,1)S(1)}, bf16[256,256]{1,0:T(8,128)(2,1)S(1)}, u32[]{:S(2)}, u32[]{:S(2)}) collective-permute-start(bf16[256,256]{1,0:T(8,128)(2,1)S(1)} %get-tuple-element.83), channel_id=1, source_target_pairs={{0,2},{2,4},{4,6},{6,7},{7,5},{5,3},{3,1},{1,0},{8,10},{10,12},{12... | collective-permute-start | bytes 393224 | tf_op jit(solution)/shard_map/ppermute | solution.py:33
  44.3 0.4 collective-permute-start.27
  44.8 1.5 %collective-permute-start.24 = (bf16[256,256]{1,0:T(8,128)(2,1)S(1)}, bf16[256,256]{1,0:T(8,128)(2,1)S(1)}, u32[]{:S(2)}, u32[]{:S(2)}) collective-permute-start(bf16[256,256]{1,0:T(8,128)(2,1)S(1)} %get-tuple-element.75), channel_id=1, source_target_pairs={{0,1},{2,0},{4,2},{6,4},{7,6},{5,7},{3,5},{1,3},{8,9},{10,8},{12,1... | collective-permute-start | bytes 393224 | tf_op jit(solution)/shard_map/ppermute | solution.py:33
  46.2 0.6 collective-permute-start.21
  46.8 1.4 %collective-permute-done.31 = bf16[256,256]{1,0:T(8,128)(2,1)S(1)} collective-permute-done((bf16[256,256]{1,0:T(8,128)(2,1)S(1)}, bf16[256,256]{1,0:T(8,128)(2,1)S(1)}, u32[]{:S(2)}, u32[]{:S(2)}) %collective-permute-start.31) | collective-permute-done | bytes 131104 | tf_op jit(solution)/shard_map/ppermute | solution.py:33
  48.2 2.5 %collective-permute-start.32 = (bf16[256,256]{1,0:T(8,128)(2,1)S(1)}, bf16[256,256]{1,0:T(8,128)(2,1)S(1)}, u32[]{:S(2)}, u32[]{:S(2)}) collective-permute-start(bf16[256,256]{1,0:T(8,128)(2,1)S(1)} %add_convert_fusion.4), channel_id=1, source_target_pairs={{0,2},{2,4},{4,6},{6,7},{7,5},{5,3},{3,1},{1,0},{8,10},{10,12},{12... | collective-permute-start | bytes 393224 | tf_op jit(solution)/shard_map/ppermute | solution.py:33
  51.2 1.8 %collective-permute-done.24 = bf16[256,256]{1,0:T(8,128)(2,1)S(1)} collective-permute-done((bf16[256,256]{1,0:T(8,128)(2,1)S(1)}, bf16[256,256]{1,0:T(8,128)(2,1)S(1)}, u32[]{:S(2)}, u32[]{:S(2)}) %collective-permute-start.24) | collective-permute-done | bytes 131104 | tf_op jit(solution)/shard_map/ppermute | solution.py:33
  53.1 0.5 collective-permute-start.25
  53.6 1.6 %collective-permute-start.22 = (bf16[256,256]{1,0:T(8,128)(2,1)S(1)}, bf16[256,256]{1,0:T(8,128)(2,1)S(1)}, u32[]{:S(2)}, u32[]{:S(2)}) collective-permute-start(bf16[256,256]{1,0:T(8,128)(2,1)S(1)} %add_convert_fusion.11), channel_id=1, source_target_pairs={{0,2},{2,4},{4,6},{6,7},{7,5},{5,3},{3,1},{1,0},{8,10},{10,12},{12... | collective-permute-start | bytes 393224 | tf_op jit(solution)/shard_map/ppermute | solution.py:33
  55.3 1.6 %collective-permute-start.33 = (bf16[256,256]{1,0:T(8,128)(2,1)S(1)}, bf16[256,256]{1,0:T(8,128)(2,1)S(1)}, u32[]{:S(2)}, u32[]{:S(2)}) collective-permute-start(bf16[256,256]{1,0:T(8,128)(2,1)S(1)} %add_convert_fusion.3), channel_id=1, source_target_pairs={{0,2},{2,4},{4,6},{6,7},{7,5},{5,3},{3,1},{1,0},{8,10},{10,12},{12... | collective-permute-start | bytes 393224 | tf_op jit(solution)/shard_map/ppermute | solution.py:33
  57.0 0.5 collective-permute-start.29
  57.5 1.9 %collective-permute-done.25 = bf16[256,256]{1,0:T(8,128)(2,1)S(1)} collective-permute-done((bf16[256,256]{1,0:T(8,128)(2,1)S(1)}, bf16[256,256]{1,0:T(8,128)(2,1)S(1)}, u32[]{:S(2)}, u32[]{:S(2)}) %collective-permute-start.25) | collective-permute-done | bytes 131104 | tf_op jit(solution)/shard_map/ppermute | solution.py:33
  59.9 1.8 %collective-permute-start.23 = (bf16[256,256]{1,0:T(8,128)(2,1)S(1)}, bf16[256,256]{1,0:T(8,128)(2,1)S(1)}, u32[]{:S(2)}, u32[]{:S(2)}) collective-permute-start(bf16[256,256]{1,0:T(8,128)(2,1)S(1)} %add_convert_fusion.10), channel_id=1, source_target_pairs={{0,2},{2,4},{4,6},{6,7},{7,5},{5,3},{3,1},{1,0},{8,10},{10,12},{12... | collective-permute-start | bytes 393224 | tf_op jit(solution)/shard_map/ppermute | solution.py:33
  61.7 1.7 %collective-permute-start.34 = (bf16[256,256]{1,0:T(8,128)(2,1)S(1)}, bf16[256,256]{1,0:T(8,128)(2,1)S(1)}, u32[]{:S(2)}, u32[]{:S(2)}) collective-permute-start(bf16[256,256]{1,0:T(8,128)(2,1)S(1)} %add_convert_fusion.2), channel_id=1, source_target_pairs={{0,2},{2,4},{4,6},{6,7},{7,5},{5,3},{3,1},{1,0},{8,10},{10,12},{12... | collective-permute-start | bytes 393224 | tf_op jit(solution)/shard_map/ppermute | solution.py:33
  63.4 0.5 collective-permute-start.30
  63.8 1.3 %collective-permute-done.26 = bf16[256,256]{1,0:T(8,128)(2,1)S(1)} collective-permute-done((bf16[256,256]{1,0:T(8,128)(2,1)S(1)}, bf16[256,256]{1,0:T(8,128)(2,1)S(1)}, u32[]{:S(2)}, u32[]{:S(2)}) %collective-permute-start.26) | collective-permute-done | bytes 131104 | tf_op jit(solution)/shard_map/ppermute | solution.py:33
  65.1 1.6 %collective-permute-done.34 = bf16[256,256]{1,0:T(8,128)(2,1)S(1)} collective-permute-done((bf16[256,256]{1,0:T(8,128)(2,1)S(1)}, bf16[256,256]{1,0:T(8,128)(2,1)S(1)}, u32[]{:S(2)}, u32[]{:S(2)}) %collective-permute-start.34) | collective-permute-done | bytes 131104 | tf_op jit(solution)/shard_map/ppermute | solution.py:33
  66.7 1.7 %collective-permute-done.30 = bf16[256,256]{1,0:T(8,128)(2,1)S(1)} collective-permute-done((bf16[256,256]{1,0:T(8,128)(2,1)S(1)}, bf16[256,256]{1,0:T(8,128)(2,1)S(1)}, u32[]{:S(2)}, u32[]{:S(2)}) %collective-permute-start.30) | collective-permute-done | bytes 131104 | tf_op jit(solution)/shard_map/ppermute | solution.py:33
  68.5 0.7 %pad_maximum_fusion = bf16[512,256]{1,0:T(8,128)(2,1)} fusion(bf16[256,256]{1,0:T(8,128)(2,1)S(1)} %get-tuple-element.91, bf16[256,256]{1,0:T(8,128)(2,1)S(1)} %get-tuple-element.92), kind=kLoop, calls=%fused_computation | loop fusion | flops 524288 | bytes 524288 | tf_op jit(solution)/shard_map/concatenate | solution.py:470
  (51 shorter events, 3.3 us)
Async XLA Ops:
  1.0 6.4 %collective-permute-start.3 = (bf16[256,256]{1,0:T(8,128)(2,1)S(1)}, bf16[256,256]{1,0:T(8,128)(2,1)S(1)}, u32[]{:S(2)}, u32[]{:S(2)}) collective-permute-start(bf16[256,256]{1,0:T(8,128)(2,1)S(1)} %get-tuple-element.89), channel_id=1, source_target_pairs={{0,1},{2,0},{4,2},{6,4},{7,6},{5,7},{3,5},{1,3},{8,9},{10,8},{12,1... | collective-permute-start | bytes 393224 | tf_op jit(solution)/shard_map/ppermute | solution.py:33
  1.5 6.4 %collective-permute-start = (bf16[256,256]{1,0:T(8,128)(2,1)S(1)}, bf16[256,256]{1,0:T(8,128)(2,1)S(1)}, u32[]{:S(2)}, u32[]{:S(2)}) collective-permute-start(bf16[256,256]{1,0:T(8,128)(2,1)S(1)} %get-tuple-element.90), channel_id=1, source_target_pairs={{0,2},{2,4},{4,6},{6,7},{7,5},{5,3},{3,1},{1,0},{8,10},{10,12},{12... | collective-permute-start | bytes 393224 | tf_op jit(solution)/shard_map/ppermute | solution.py:33
  3.1 6.6 %collective-permute-start.6 = (bf16[256,256]{1,0:T(8,128)(2,1)S(1)}, bf16[256,256]{1,0:T(8,128)(2,1)S(1)}, u32[]{:S(2)}, u32[]{:S(2)}) collective-permute-start(bf16[256,256]{1,0:T(8,128)(2,1)S(1)} %get-tuple-element.90), channel_id=1, source_target_pairs={{0,1},{2,0},{4,2},{6,4},{7,6},{5,7},{3,5},{1,3},{8,9},{10,8},{12,1... | collective-permute-start | bytes 393224 | tf_op jit(solution)/shard_map/ppermute | solution.py:33
  3.5 6.6 %collective-permute-start.8 = (bf16[256,256]{1,0:T(8,128)(2,1)S(1)}, bf16[256,256]{1,0:T(8,128)(2,1)S(1)}, u32[]{:S(2)}, u32[]{:S(2)}) collective-permute-start(bf16[256,256]{1,0:T(8,128)(2,1)S(1)} %get-tuple-element.89), channel_id=1, source_target_pairs={{0,2},{2,4},{4,6},{6,7},{7,5},{5,3},{3,1},{1,0},{8,10},{10,12},{12... | collective-permute-start | bytes 393224 | tf_op jit(solution)/shard_map/ppermute | solution.py:33
  7.4 6.4 %collective-permute-start.4 = (bf16[256,256]{1,0:T(8,128)(2,1)S(1)}, bf16[256,256]{1,0:T(8,128)(2,1)S(1)}, u32[]{:S(2)}, u32[]{:S(2)}) collective-permute-start(bf16[256,256]{1,0:T(8,128)(2,1)S(1)} %collective-permute-done.3.refs_1_), channel_id=1, source_target_pairs={{0,1},{2,0},{4,2},{6,4},{7,6},{5,7},{3,5},{1,3},{8,9},{10,8},{12,1... | collective-permute-start | bytes 393224 | tf_op jit(solution)/shard_map/ppermute | solution.py:33
  7.9 6.4 %collective-permute-start.1 = (bf16[256,256]{1,0:T(8,128)(2,1)S(1)}, bf16[256,256]{1,0:T(8,128)(2,1)S(1)}, u32[]{:S(2)}, u32[]{:S(2)}) collective-permute-start(bf16[256,256]{1,0:T(8,128)(2,1)S(1)} %collective-permute-done.refs_0_), channel_id=1, source_target_pairs={{0,2},{2,4},{4,6},{6,7},{7,5},{5,3},{3,1},{1,0},{8,10},{10,12},{12... | collective-permute-start | bytes 393224 | tf_op jit(solution)/shard_map/ppermute | solution.py:33
  9.6 6.3 %collective-permute-start.7 = (bf16[256,256]{1,0:T(8,128)(2,1)S(1)}, bf16[256,256]{1,0:T(8,128)(2,1)S(1)}, u32[]{:S(2)}, u32[]{:S(2)}) collective-permute-start(bf16[256,256]{1,0:T(8,128)(2,1)S(1)} %collective-permute-done.6.refs_2_), channel_id=1, source_target_pairs={{0,1},{2,0},{4,2},{6,4},{7,6},{5,7},{3,5},{1,3},{8,9},{10,8},{12,1... | collective-permute-start | bytes 393224 | tf_op jit(solution)/shard_map/ppermute | solution.py:33
  10.1 6.3 %collective-permute-start.9 = (bf16[256,256]{1,0:T(8,128)(2,1)S(1)}, bf16[256,256]{1,0:T(8,128)(2,1)S(1)}, u32[]{:S(2)}, u32[]{:S(2)}) collective-permute-start(bf16[256,256]{1,0:T(8,128)(2,1)S(1)} %collective-permute-done.8.refs_3_), channel_id=1, source_target_pairs={{0,2},{2,4},{4,6},{6,7},{7,5},{5,3},{3,1},{1,0},{8,10},{10,12},{12... | collective-permute-start | bytes 393224 | tf_op jit(solution)/shard_map/ppermute | solution.py:33
  13.8 5.6 %collective-permute-start.5 = (bf16[256,256]{1,0:T(8,128)(2,1)S(1)}, bf16[256,256]{1,0:T(8,128)(2,1)S(1)}, u32[]{:S(2)}, u32[]{:S(2)}) collective-permute-start(bf16[256,256]{1,0:T(8,128)(2,1)S(1)} %collective-permute-done.4.refs_1_), channel_id=1, source_target_pairs={{0,1},{2,0},{4,2},{6,4},{7,6},{5,7},{3,5},{1,3},{8,9},{10,8},{12,1... | collective-permute-start | bytes 393224 | tf_op jit(solution)/shard_map/ppermute | solution.py:33
  14.3 5.3 %collective-permute-start.2 = (bf16[256,256]{1,0:T(8,128)(2,1)S(1)}, bf16[256,256]{1,0:T(8,128)(2,1)S(1)}, u32[]{:S(2)}, u32[]{:S(2)}) collective-permute-start(bf16[256,256]{1,0:T(8,128)(2,1)S(1)} %collective-permute-done.1.refs_0_), channel_id=1, source_target_pairs={{0,2},{2,4},{4,6},{6,7},{7,5},{5,3},{3,1},{1,0},{8,10},{10,12},{12... | collective-permute-start | bytes 393224 | tf_op jit(solution)/shard_map/ppermute | solution.py:33
  15.9 6.0 %collective-permute-start.10 = (bf16[256,256]{1,0:T(8,128)(2,1)S(1)}, bf16[256,256]{1,0:T(8,128)(2,1)S(1)}, u32[]{:S(2)}, u32[]{:S(2)}) collective-permute-start(bf16[256,256]{1,0:T(8,128)(2,1)S(1)} %collective-permute-done.7.refs_2_), channel_id=1, source_target_pairs={{0,1},{2,0},{4,2},{6,4},{7,6},{5,7},{3,5},{1,3},{8,9},{10,8},{12,1... | collective-permute-start | bytes 393224 | tf_op jit(solution)/shard_map/ppermute | solution.py:33
  16.3 5.7 %collective-permute-start.11 = (bf16[256,256]{1,0:T(8,128)(2,1)S(1)}, bf16[256,256]{1,0:T(8,128)(2,1)S(1)}, u32[]{:S(2)}, u32[]{:S(2)}) collective-permute-start(bf16[256,256]{1,0:T(8,128)(2,1)S(1)} %collective-permute-done.9.refs_3_), channel_id=1, source_target_pairs={{0,2},{2,4},{4,6},{6,7},{7,5},{5,3},{3,1},{1,0},{8,10},{10,12},{12... | collective-permute-start | bytes 393224 | tf_op jit(solution)/shard_map/ppermute | solution.py:33
  19.4 5.1 %collective-permute-start.13 = (bf16[256,256]{1,0:T(8,128)(2,1)S(1)}, bf16[256,256]{1,0:T(8,128)(2,1)S(1)}, u32[]{:S(2)}, u32[]{:S(2)}) collective-permute-start(bf16[256,256]{1,0:T(8,128)(2,1)S(1)} %collective-permute-done.5.refs_1_), channel_id=1, source_target_pairs={{0,1},{2,0},{4,2},{6,4},{7,6},{5,7},{3,5},{1,3},{8,9},{10,8},{12,1... | collective-permute-start | bytes 393224 | tf_op jit(solution)/shard_map/ppermute | solution.py:33
  19.6 5.0 %collective-permute-start.12 = (bf16[256,256]{1,0:T(8,128)(2,1)S(1)}, bf16[256,256]{1,0:T(8,128)(2,1)S(1)}, u32[]{:S(2)}, u32[]{:S(2)}) collective-permute-start(bf16[256,256]{1,0:T(8,128)(2,1)S(1)} %collective-permute-done.2.refs_0_), channel_id=1, source_target_pairs={{0,2},{2,4},{4,6},{6,7},{7,5},{5,3},{3,1},{1,0},{8,10},{10,12},{12... | collective-permute-start | bytes 393224 | tf_op jit(solution)/shard_map/ppermute | solution.py:33
  25.9 8.2 %collective-permute-start.17 = (bf16[256,512]{1,0:T(8,128)(2,1)S(1)}, bf16[256,512]{1,0:T(8,128)(2,1)S(1)}, u32[]{:S(2)}, u32[]{:S(2)}) collective-permute-start(bf16[256,512]{1,0:T(8,128)(2,1)S(1)} %get-tuple-element.57.refs_0_), channel_id=1, source_target_pairs={{0,16},{8,24},{16,0},{24,8},{1,17},{9,25},{17,1},{25,9},{2,18},{10... | collective-permute-start | bytes 786440 | tf_op jit(solution)/shard_map/ppermute | solution.py:442
  26.7 10.2 %collective-permute-start.18 = (bf16[256,512]{1,0:T(8,128)(2,1)S(1)}, bf16[256,512]{1,0:T(8,128)(2,1)S(1)}, u32[]{:S(2)}, u32[]{:S(2)}) collective-permute-start(bf16[256,512]{1,0:T(8,128)(2,1)S(1)} %get-tuple-element.58.refs_1_), channel_id=1, source_target_pairs={{0,16},{8,24},{16,0},{24,8},{1,17},{9,25},{17,1},{25,9},{2,18},{10... | collective-permute-start | bytes 786440 | tf_op jit(solution)/shard_map/ppermute | solution.py:442
  28.0 2.9 %collective-permute-start.15 = (bf16[176,512]{1,0:T(8,128)(2,1)S(1)}, bf16[176,512]{1,0:T(8,128)(2,1)S(1)}, u32[]{:S(2)}, u32[]{:S(2)}) collective-permute-start(bf16[176,512]{1,0:T(8,128)(2,1)S(1)} %get-tuple-element.60), channel_id=1, source_target_pairs={{0,8},{8,0},{16,24},{24,16},{1,9},{9,1},{17,25},{25,17},{2,10},{10... | collective-permute-start | bytes 540680 | tf_op jit(solution)/shard_map/ppermute | solution.py:39
  28.0 2.9 %collective-permute-start.16 = (bf16[176,512]{1,0:T(8,128)(2,1)S(1)}, bf16[176,512]{1,0:T(8,128)(2,1)S(1)}, u32[]{:S(2)}, u32[]{:S(2)}) collective-permute-start(bf16[176,512]{1,0:T(8,128)(2,1)S(1)} %get-tuple-element.61), channel_id=1, source_target_pairs={{0,8},{8,0},{16,24},{24,16},{1,9},{9,1},{17,25},{25,17},{2,10},{10... | collective-permute-start | bytes 540680 | tf_op jit(solution)/shard_map/ppermute | solution.py:39
  28.5 2.4 %collective-permute-start.14 = (bf16[160,512]{1,0:T(8,128)(2,1)S(1)}, bf16[160,512]{1,0:T(8,128)(2,1)S(1)}, u32[]{:S(2)}, u32[]{:S(2)}) collective-permute-start(bf16[160,512]{1,0:T(8,128)(2,1)S(1)} %get-tuple-element.59), channel_id=1, source_target_pairs={{0,8},{8,0},{16,24},{24,16},{1,9},{9,1},{17,25},{25,17},{2,10},{10... | collective-permute-start | bytes 491528 | tf_op jit(solution)/shard_map/ppermute | solution.py:39
  36.9 2.8 %collective-permute-start.19 = (bf16[256,512]{1,0:T(8,128)(2,1)S(1)}, bf16[256,512]{1,0:T(8,128)(2,1)S(1)}, u32[]{:S(2)}, u32[]{:S(2)}) collective-permute-start(bf16[256,512]{1,0:T(8,128)(2,1)S(1)} %collective-permute-done.17.refs_0_), channel_id=1, source_target_pairs={{0,8},{8,0},{16,24},{24,16},{1,9},{9,1},{17,25},{25,17},{2,10},{10... | collective-permute-start | bytes 786440 | tf_op jit(solution)/shard_map/ppermute | solution.py:39
  36.9 2.8 %collective-permute-start.20 = (bf16[256,512]{1,0:T(8,128)(2,1)S(1)}, bf16[256,512]{1,0:T(8,128)(2,1)S(1)}, u32[]{:S(2)}, u32[]{:S(2)}) collective-permute-start(bf16[256,512]{1,0:T(8,128)(2,1)S(1)} %collective-permute-done.18.refs_1_), channel_id=1, source_target_pairs={{0,8},{8,0},{16,24},{24,16},{1,9},{9,1},{17,25},{25,17},{2,10},{10... | collective-permute-start | bytes 786440 | tf_op jit(solution)/shard_map/ppermute | solution.py:39
  42.7 5.5 %collective-permute-start.31 = (bf16[256,256]{1,0:T(8,128)(2,1)S(1)}, bf16[256,256]{1,0:T(8,128)(2,1)S(1)}, u32[]{:S(2)}, u32[]{:S(2)}) collective-permute-start(bf16[256,256]{1,0:T(8,128)(2,1)S(1)} %get-tuple-element.83), channel_id=1, source_target_pairs={{0,2},{2,4},{4,6},{6,7},{7,5},{5,3},{3,1},{1,0},{8,10},{10,12},{12... | collective-permute-start | bytes 393224 | tf_op jit(solution)/shard_map/ppermute | solution.py:33
  44.3 6.5 %collective-permute-start.27 = (bf16[256,256]{1,0:T(8,128)(2,1)S(1)}, bf16[256,256]{1,0:T(8,128)(2,1)S(1)}, u32[]{:S(2)}, u32[]{:S(2)}) collective-permute-start(bf16[256,256]{1,0:T(8,128)(2,1)S(1)} %get-tuple-element.79), channel_id=1, source_target_pairs={{0,1},{2,0},{4,2},{6,4},{7,6},{5,7},{3,5},{1,3},{8,9},{10,8},{12,1... | collective-permute-start | bytes 393224 | tf_op jit(solution)/shard_map/ppermute | solution.py:33
  44.8 8.3 %collective-permute-start.24 = (bf16[256,256]{1,0:T(8,128)(2,1)S(1)}, bf16[256,256]{1,0:T(8,128)(2,1)S(1)}, u32[]{:S(2)}, u32[]{:S(2)}) collective-permute-start(bf16[256,256]{1,0:T(8,128)(2,1)S(1)} %get-tuple-element.75), channel_id=1, source_target_pairs={{0,1},{2,0},{4,2},{6,4},{7,6},{5,7},{3,5},{1,3},{8,9},{10,8},{12,1... | collective-permute-start | bytes 393224 | tf_op jit(solution)/shard_map/ppermute | solution.py:33
  46.2 7.4 %collective-permute-start.21 = (bf16[256,256]{1,0:T(8,128)(2,1)S(1)}, bf16[256,256]{1,0:T(8,128)(2,1)S(1)}, u32[]{:S(2)}, u32[]{:S(2)}) collective-permute-start(bf16[256,256]{1,0:T(8,128)(2,1)S(1)} %get-tuple-element.72), channel_id=1, source_target_pairs={{0,2},{2,4},{4,6},{6,7},{7,5},{5,3},{3,1},{1,0},{8,10},{10,12},{12... | collective-permute-start | bytes 393224 | tf_op jit(solution)/shard_map/ppermute | solution.py:33
  48.2 7.0 %collective-permute-start.32 = (bf16[256,256]{1,0:T(8,128)(2,1)S(1)}, bf16[256,256]{1,0:T(8,128)(2,1)S(1)}, u32[]{:S(2)}, u32[]{:S(2)}) collective-permute-start(bf16[256,256]{1,0:T(8,128)(2,1)S(1)} %add_convert_fusion.4), channel_id=1, source_target_pairs={{0,2},{2,4},{4,6},{6,7},{7,5},{5,3},{3,1},{1,0},{8,10},{10,12},{12... | collective-permute-start | bytes 393224 | tf_op jit(solution)/shard_map/ppermute | solution.py:33
  50.8 6.1 %collective-permute-start.28 = (bf16[256,256]{1,0:T(8,128)(2,1)S(1)}, bf16[256,256]{1,0:T(8,128)(2,1)S(1)}, u32[]{:S(2)}, u32[]{:S(2)}) collective-permute-start(bf16[256,256]{1,0:T(8,128)(2,1)S(1)} %add_convert_fusion.7), channel_id=1, source_target_pairs={{0,1},{2,0},{4,2},{6,4},{7,6},{5,7},{3,5},{1,3},{8,9},{10,8},{12,1... | collective-permute-start | bytes 393224 | tf_op jit(solution)/shard_map/ppermute | solution.py:33
  53.1 6.3 %collective-permute-start.25 = (bf16[256,256]{1,0:T(8,128)(2,1)S(1)}, bf16[256,256]{1,0:T(8,128)(2,1)S(1)}, u32[]{:S(2)}, u32[]{:S(2)}) collective-permute-start(bf16[256,256]{1,0:T(8,128)(2,1)S(1)} %add_convert_fusion.9), channel_id=1, source_target_pairs={{0,1},{2,0},{4,2},{6,4},{7,6},{5,7},{3,5},{1,3},{8,9},{10,8},{12,1... | collective-permute-start | bytes 393224 | tf_op jit(solution)/shard_map/ppermute | solution.py:33
  53.6 6.2 %collective-permute-start.22 = (bf16[256,256]{1,0:T(8,128)(2,1)S(1)}, bf16[256,256]{1,0:T(8,128)(2,1)S(1)}, u32[]{:S(2)}, u32[]{:S(2)}) collective-permute-start(bf16[256,256]{1,0:T(8,128)(2,1)S(1)} %add_convert_fusion.11), channel_id=1, source_target_pairs={{0,2},{2,4},{4,6},{6,7},{7,5},{5,3},{3,1},{1,0},{8,10},{10,12},{12... | collective-permute-start | bytes 393224 | tf_op jit(solution)/shard_map/ppermute | solution.py:33
  55.3 6.3 %collective-permute-start.33 = (bf16[256,256]{1,0:T(8,128)(2,1)S(1)}, bf16[256,256]{1,0:T(8,128)(2,1)S(1)}, u32[]{:S(2)}, u32[]{:S(2)}) collective-permute-start(bf16[256,256]{1,0:T(8,128)(2,1)S(1)} %add_convert_fusion.3), channel_id=1, source_target_pairs={{0,2},{2,4},{4,6},{6,7},{7,5},{5,3},{3,1},{1,0},{8,10},{10,12},{12... | collective-permute-start | bytes 393224 | tf_op jit(solution)/shard_map/ppermute | solution.py:33
  57.0 6.4 %collective-permute-start.29 = (bf16[256,256]{1,0:T(8,128)(2,1)S(1)}, bf16[256,256]{1,0:T(8,128)(2,1)S(1)}, u32[]{:S(2)}, u32[]{:S(2)}) collective-permute-start(bf16[256,256]{1,0:T(8,128)(2,1)S(1)} %add_convert_fusion.6), channel_id=1, source_target_pairs={{0,1},{2,0},{4,2},{6,4},{7,6},{5,7},{3,5},{1,3},{8,9},{10,8},{12,1... | collective-permute-start | bytes 393224 | tf_op jit(solution)/shard_map/ppermute | solution.py:33
  59.5 5.7 %collective-permute-start.26 = (bf16[256,256]{1,0:T(8,128)(2,1)S(1)}, bf16[256,256]{1,0:T(8,128)(2,1)S(1)}, u32[]{:S(2)}, u32[]{:S(2)}) collective-permute-start(bf16[256,256]{1,0:T(8,128)(2,1)S(1)} %add_convert_fusion.8), channel_id=1, source_target_pairs={{0,1},{2,0},{4,2},{6,4},{7,6},{5,7},{3,5},{1,3},{8,9},{10,8},{12,1... | collective-permute-start | bytes 393224 | tf_op jit(solution)/shard_map/ppermute | solution.py:33
  59.9 5.3 %collective-permute-start.23 = (bf16[256,256]{1,0:T(8,128)(2,1)S(1)}, bf16[256,256]{1,0:T(8,128)(2,1)S(1)}, u32[]{:S(2)}, u32[]{:S(2)}) collective-permute-start(bf16[256,256]{1,0:T(8,128)(2,1)S(1)} %add_convert_fusion.10), channel_id=1, source_target_pairs={{0,2},{2,4},{4,6},{6,7},{7,5},{5,3},{3,1},{1,0},{8,10},{10,12},{12... | collective-permute-start | bytes 393224 | tf_op jit(solution)/shard_map/ppermute | solution.py:33
  61.7 5.0 %collective-permute-start.34 = (bf16[256,256]{1,0:T(8,128)(2,1)S(1)}, bf16[256,256]{1,0:T(8,128)(2,1)S(1)}, u32[]{:S(2)}, u32[]{:S(2)}) collective-permute-start(bf16[256,256]{1,0:T(8,128)(2,1)S(1)} %add_convert_fusion.2), channel_id=1, source_target_pairs={{0,2},{2,4},{4,6},{6,7},{7,5},{5,3},{3,1},{1,0},{8,10},{10,12},{12... | collective-permute-start | bytes 393224 | tf_op jit(solution)/shard_map/ppermute | solution.py:33
  63.4 5.0 %collective-permute-start.30 = (bf16[256,256]{1,0:T(8,128)(2,1)S(1)}, bf16[256,256]{1,0:T(8,128)(2,1)S(1)}, u32[]{:S(2)}, u32[]{:S(2)}) collective-permute-start(bf16[256,256]{1,0:T(8,128)(2,1)S(1)} %add_convert_fusion.5), channel_id=1, source_target_pairs={{0,1},{2,0},{4,2},{6,4},{7,6},{5,7},{3,5},{1,3},{8,9},{10,8},{12,1... | collective-permute-start | bytes 393224 | tf_op jit(solution)/shard_map/ppermute | solution.py:33

commit v23 on v20

--- a/solution.py
+++ b/solution.py
@@ -330,7 +330,7 @@
         pltpu.VMEM((heads, keys, 2 * head_size), BF16),
         pltpu.VMEM((total, 2 * width), F32),
     ]
-    id_rows = ids.reshape(-1, 1, math.gcd(total, 256))
+    id_rows = ids.reshape(-1, 1, math.gcd(total, 512))
     operands = [in_vmem(query), *map(in_vmem, parts)]
     if acc is not None:
         operands.append(in_vmem(acc))

time: 69.4 us -> 69.7 us (level)
  the two profiles are of different devices: /device:TPU:10 before, /device:TPU:0 now
where the time goes in v23:
time: 69.7 us; the launch traced here: 69.1 us
  starting transfers between devices  34.9 us (50%)
  waiting for transfers between devices  17.2 us (25%)
  Pallas kernels  14.3 us (21%)
  other arithmetic  1.39 us (2%)
  local copies, waits for them, and re-layouts  1.16 us (2%)
    ppermute x28, starting transfers between devices, along(): lax.ppermute(value, 'head', [(order[p], order[(p + step) % count]) for p...  31.8 us
    ppermute x28, waiting for transfers between devices, along(): lax.ppermute(value, 'head', [(order[p], order[(p + step) % count]) for p...  14.2 us
    pallas_call x4, Pallas kernels, attend(): pl.pallas_call(functools.partial(attend_kernel, head_size, (len(blocks),...  7.85 us
    pallas_call x1, Pallas kernels, fold_gain(): pl.pallas_call(functools.partial(fold_kernel, order), out_shape=(pltpu.VM...  2.88 us
    ppermute x2, waiting for transfers between devices, body(): far.append([lax.ppermute(part, 'seq', shift) for part in halves])  2.87 us
    ppermute x2, starting transfers between devices, body(): far.append([lax.ppermute(part, 'seq', shift) for part in halves])  2.09 us
    pallas_call x1, Pallas kernels, project_begin(): pl.pallas_call(functools.partial(begin_kernel, blocks), out_shape=pltpu.V...  1.92 us
  transfers between devices with their start and end apart: 35, of which 18 were waited for; matrix products, arithmetic and copies ran while one was open for 1% of the time, Pallas kernels for 15%

profile of v23, /device:TPU:0, one launch (start us, length us, event | category | flops | bytes accessed | tf_op | source)
XLA Modules:
  0.0 69.1 jit_solution(13770353387468096341)
XLA Ops:
  0.0 1.0 %fusion = (bf16[256,256]{1,0:T(8,128)(2,1)S(1)}, bf16[256,256]{1,0:T(8,128)(2,1)S(1)}) fusion(bf16[512,256]{1,0:T(8,128)(2,1)} %tokens.1), kind=kLoop, calls=%fused_computation.16 | loop fusion | bytes 524288 | tf_op jit(solution)/shard_map/slice | solution.py:390
  1.0 3.0 %collective-permute-start.3 = (bf16[256,256]{1,0:T(8,128)(2,1)S(1)}, bf16[256,256]{1,0:T(8,128)(2,1)S(1)}, u32[]{:S(2)}, u32[]{:S(2)}) collective-permute-start(bf16[256,256]{1,0:T(8,128)(2,1)S(1)} %get-tuple-element.85), channel_id=1, source_target_pairs={{0,1},{2,0},{4,2},{6,4},{7,6},{5,7},{3,5},{1,3},{8,9},{10,8},{12,1... | collective-permute-start | bytes 393224 | tf_op jit(solution)/shard_map/ppermute | solution.py:33
  4.1 1.9 %collective-permute-start.6 = (bf16[256,256]{1,0:T(8,128)(2,1)S(1)}, bf16[256,256]{1,0:T(8,128)(2,1)S(1)}, u32[]{:S(2)}, u32[]{:S(2)}) collective-permute-start(bf16[256,256]{1,0:T(8,128)(2,1)S(1)} %get-tuple-element.86), channel_id=1, source_target_pairs={{0,1},{2,0},{4,2},{6,4},{7,6},{5,7},{3,5},{1,3},{8,9},{10,8},{12,1... | collective-permute-start | bytes 393224 | tf_op jit(solution)/shard_map/ppermute | solution.py:33
  6.2 2.9 %fold_gain.1 = (bf16[3,2048,256]{2,1,0:T(8,128)(2,1)S(1)}, bf16[512,2048]{1,0:T(8,128)(2,1)S(1)}) custom-call(s32[8]{0:T(128)S(1)} %stack.84.at, f32[16,128]{1,0:T(8,128)} %bitcast.19, bf16[3,2048,256]{2,1,0:T(8,128)(2,1)} %w_hbm.1, bf16[512,256]{1,0:T(8,128)(2,1)} %tokens.1), custom_call_target="tpu_custom_call" | custom-call | flops 1572864 | bytes 6291456 | tf_op jit(solution)/shard_map/fold_gain/pallas_call | solution.py:86
  9.1 2.0 %collective-permute-start.4 = (bf16[256,256]{1,0:T(8,128)(2,1)S(1)}, bf16[256,256]{1,0:T(8,128)(2,1)S(1)}, u32[]{:S(2)}, u32[]{:S(2)}) collective-permute-start(bf16[256,256]{1,0:T(8,128)(2,1)S(1)} %collective-permute-done.3.refs_1_), channel_id=1, source_target_pairs={{0,1},{2,0},{4,2},{6,4},{7,6},{5,7},{3,5},{1,3},{8,9},{10,8},{12,1... | collective-permute-start | bytes 393224 | tf_op jit(solution)/shard_map/ppermute | solution.py:33
  11.2 1.9 %collective-permute-start.7 = (bf16[256,256]{1,0:T(8,128)(2,1)S(1)}, bf16[256,256]{1,0:T(8,128)(2,1)S(1)}, u32[]{:S(2)}, u32[]{:S(2)}) collective-permute-start(bf16[256,256]{1,0:T(8,128)(2,1)S(1)} %collective-permute-done.6.refs_2_), channel_id=1, source_target_pairs={{0,1},{2,0},{4,2},{6,4},{7,6},{5,7},{3,5},{1,3},{8,9},{10,8},{12,1... | collective-permute-start | bytes 393224 | tf_op jit(solution)/shard_map/ppermute | solution.py:33
  13.3 2.2 %collective-permute-done.4.refs_1_ = bf16[256,256]{1,0:T(8,128)(2,1)S(1)} collective-permute-done((bf16[256,256]{1,0:T(8,128)(2,1)S(1)}, bf16[256,256]{1,0:T(8,128)(2,1)S(1)}, u32[]{:S(2)}, u32[]{:S(2)}) %collective-permute-start.4) | collective-permute-done | bytes 131104 | tf_op jit(solution)/shard_map/ppermute | solution.py:33
  15.5 1.6 %collective-permute-start.5 = (bf16[256,256]{1,0:T(8,128)(2,1)S(1)}, bf16[256,256]{1,0:T(8,128)(2,1)S(1)}, u32[]{:S(2)}, u32[]{:S(2)}) collective-permute-start(bf16[256,256]{1,0:T(8,128)(2,1)S(1)} %collective-permute-done.4.refs_1_), channel_id=1, source_target_pairs={{0,1},{2,0},{4,2},{6,4},{7,6},{5,7},{3,5},{1,3},{8,9},{10,8},{12,1... | collective-permute-start | bytes 393224 | tf_op jit(solution)/shard_map/ppermute | solution.py:33
  17.5 0.8 %collective-permute-done.7.refs_2_ = bf16[256,256]{1,0:T(8,128)(2,1)S(1)} collective-permute-done((bf16[256,256]{1,0:T(8,128)(2,1)S(1)}, bf16[256,256]{1,0:T(8,128)(2,1)S(1)}, u32[]{:S(2)}, u32[]{:S(2)}) %collective-permute-start.7) | collective-permute-done | bytes 131104 | tf_op jit(solution)/shard_map/ppermute | solution.py:33
  18.3 1.6 %collective-permute-start.10 = (bf16[256,256]{1,0:T(8,128)(2,1)S(1)}, bf16[256,256]{1,0:T(8,128)(2,1)S(1)}, u32[]{:S(2)}, u32[]{:S(2)}) collective-permute-start(bf16[256,256]{1,0:T(8,128)(2,1)S(1)} %collective-permute-done.7.refs_2_), channel_id=1, source_target_pairs={{0,1},{2,0},{4,2},{6,4},{7,6},{5,7},{3,5},{1,3},{8,9},{10,8},{12,1... | collective-permute-start | bytes 393224 | tf_op jit(solution)/shard_map/ppermute | solution.py:33
  20.6 0.6 collective-permute-done.5.refs_1_
  21.2 1.6 %collective-permute-start.13 = (bf16[256,256]{1,0:T(8,128)(2,1)S(1)}, bf16[256,256]{1,0:T(8,128)(2,1)S(1)}, u32[]{:S(2)}, u32[]{:S(2)}) collective-permute-start(bf16[256,256]{1,0:T(8,128)(2,1)S(1)} %collective-permute-done.5.refs_1_), channel_id=1, source_target_pairs={{0,1},{2,0},{4,2},{6,4},{7,6},{5,7},{3,5},{1,3},{8,9},{10,8},{12,1... | collective-permute-start | bytes 393224 | tf_op jit(solution)/shard_map/ppermute | solution.py:33
  22.8 0.4 collective-permute-start.12
  23.5 1.4 %collective-permute-done.11.refs_3_ = bf16[256,256]{1,0:T(8,128)(2,1)S(1)} collective-permute-done((bf16[256,256]{1,0:T(8,128)(2,1)S(1)}, bf16[256,256]{1,0:T(8,128)(2,1)S(1)}, u32[]{:S(2)}, u32[]{:S(2)}) %collective-permute-start.11) | collective-permute-done | bytes 131104 | tf_op jit(solution)/shard_map/ppermute | solution.py:33
  25.0 1.9 %project_begin.1.state = f32[512,896]{1,0:T(8,128)S(1)} custom-call(bf16[512,2048]{1,0:T(8,128)(2,1)S(1)} %place.5.wide, bf16[3,2048,256]{2,1,0:T(8,128)(2,1)S(1)} %get-tuple-element.51.w_ref), custom_call_target="tpu_custom_call" | custom-call | flops 1610612736 | bytes 5242880 | tf_op jit(solution)/shard_map/project_begin/pallas_call | solution.py:191
  26.9 0.8 %collective-permute-done.12.refs_0_ = bf16[256,256]{1,0:T(8,128)(2,1)S(1)} collective-permute-done((bf16[256,256]{1,0:T(8,128)(2,1)S(1)}, bf16[256,256]{1,0:T(8,128)(2,1)S(1)}, u32[]{:S(2)}, u32[]{:S(2)}) %collective-permute-start.12) | collective-permute-done | bytes 131104 | tf_op jit(solution)/shard_map/ppermute | solution.py:33
  27.8 1.3 %project_finish.1 = (bf16[512,256]{1,0:T(8,128)(2,1)S(1)}, bf16[256,512]{1,0:T(8,128)(2,1)S(1)}, bf16[256,512]{1,0:T(8,128)(2,1)S(1)}, bf16[160,512]{1,0:T(8,128...) custom-call(f32[2]{0:T(128)} %factor.1, f32[512,896]{1,0:T(8,128)S(1)} %project_begin.1.state, ...), custom_call_target="tpu_custom_call" | custom-call | flops 201326592 | bytes 1048576 | tf_op jit(solution)/shard_map/project_finish/pallas_call | solution.py:213
  29.1 1.6 %collective-permute-start.17 = (bf16[256,512]{1,0:T(8,128)(2,1)S(1)}, bf16[256,512]{1,0:T(8,128)(2,1)S(1)}, u32[]{:S(2)}, u32[]{:S(2)}) collective-permute-start(bf16[256,512]{1,0:T(8,128)(2,1)S(1)} %get-tuple-element.53.refs_0_), channel_id=1, source_target_pairs={{0,16},{8,24},{16,0},{24,8},{1,17},{9,25},{17,1},{25,9},{2,18},{10... | collective-permute-start | bytes 786440 | tf_op jit(solution)/shard_map/ppermute | solution.py:425
  30.6 0.5 collective-permute-start.18
  31.1 0.5 collective-permute-start.16
  31.8 2.0 %attend.3.refs_3_ = f32[512,512]{1,0:T(8,128)S(1)} custom-call(s32[2]{0:T(128)S(1)} %pad_add_fusion.1.info, s32[2048]{0:T(1024)} %ids.7, s32[4,1,512]{2,1,0:T(1,128)} %bitcast.15, bf16[512,256]{1,0:T(8,128)(2,1)S(1)} %get-tuple-element.52.q_ref, bf16[256,512]{1,0:T(8,128)(2,1)S(1)} %get-tuple-element.53.refs_0_, bf16[256,512]{1,0:T(8,128)(2,1)S(1)} %get-tuple-element.54.refs_1_), custom_call_target="tpu_custom_call" | custom-call | flops 1048576 | bytes 1024 | tf_op jit(solution)/shard_map/attend/pallas_call | solution.py:351
  33.9 2.0 %attend.4.refs_2_ = f32[512,512]{1,0:T(8,128)S(1)} custom-call(s32[2]{0:T(128)S(1)} %pad_add_fusion.info, s32[2048]{0:T(1024)} %ids.7, s32[4,1,512]{2,1,0:T(1,128)} %bitcast.16, bf16[512,256]{1,0:T(8,128)(2,1)S(1)} %get-tuple-element.52.q_ref, bf16[160,512]{1,0:T(8,128)(2,1)S(1)} %collective-permute-done.14.refs_0_, ...), custom_call_target="tpu_custom_call" | custom-call | flops 1048576 | bytes 1024 | tf_op jit(solution)/shard_map/attend/pallas_call | solution.py:351
  36.0 2.8 %collective-permute-done.18.refs_1_ = bf16[256,512]{1,0:T(8,128)(2,1)S(1)} collective-permute-done((bf16[256,512]{1,0:T(8,128)(2,1)S(1)}, bf16[256,512]{1,0:T(8,128)(2,1)S(1)}, u32[]{:S(2)}, u32[]{:S(2)}) %collective-permute-start.18) | collective-permute-done | bytes 262176 | tf_op jit(solution)/shard_map/ppermute | solution.py:425
  38.8 0.5 collective-permute-start.20
  39.5 1.0 %attend.5.refs_2_ = f32[512,512]{1,0:T(8,128)S(1)} custom-call(s32[2]{0:T(128)S(1)} %pad_add_fusion.2.info, s32[2048]{0:T(1024)} %ids.7, s32[4,1,512]{2,1,0:T(1,128)} %bitcast.17, bf16[512,256]{1,0:T(8,128)(2,1)S(1)} %get-tuple-element.52.q_ref, bf16[256,512]{1,0:T(8,128)(2,1)S(1)} %collective-permute-done.17.refs_0_, ...), custom_call_target="tpu_custom_call" | custom-call | flops 1048576 | bytes 1024 | tf_op jit(solution)/shard_map/attend/pallas_call | solution.py:351
  40.7 2.8 %attend_last.1 = (bf16[256,256]{1,0:T(8,128)(2,1)S(1)}, bf16[256,256]{1,0:T(8,128)(2,1)S(1)}, bf16[256,256]{1,0:T(8,128)(2,1)S(1)}, bf16[256,256]{1,0:T(8,128)(2...) custom-call(s32[18]{0:T(128)S(1)} %stack.83.info, ...), custom_call_target="tpu_custom_call" | custom-call | flops 1048576 | bytes 1024 | tf_op jit(solution)/shard_map/attend_last/pallas_call | solution.py:351
  43.5 0.5 collective-permute-start.31
  44.0 1.5 %collective-permute-start.27 = (bf16[256,256]{1,0:T(8,128)(2,1)S(1)}, bf16[256,256]{1,0:T(8,128)(2,1)S(1)}, u32[]{:S(2)}, u32[]{:S(2)}) collective-permute-start(bf16[256,256]{1,0:T(8,128)(2,1)S(1)} %get-tuple-element.75), channel_id=1, source_target_pairs={{0,1},{2,0},{4,2},{6,4},{7,6},{5,7},{3,5},{1,3},{8,9},{10,8},{12,1... | collective-permute-start | bytes 393224 | tf_op jit(solution)/shard_map/ppermute | solution.py:33
  45.5 1.6 %collective-permute-start.24 = (bf16[256,256]{1,0:T(8,128)(2,1)S(1)}, bf16[256,256]{1,0:T(8,128)(2,1)S(1)}, u32[]{:S(2)}, u32[]{:S(2)}) collective-permute-start(bf16[256,256]{1,0:T(8,128)(2,1)S(1)} %get-tuple-element.71), channel_id=1, source_target_pairs={{0,1},{2,0},{4,2},{6,4},{7,6},{5,7},{3,5},{1,3},{8,9},{10,8},{12,1... | collective-permute-start | bytes 393224 | tf_op jit(solution)/shard_map/ppermute | solution.py:33
  47.1 0.4 collective-permute-start.21
  47.6 1.7 %collective-permute-done.31 = bf16[256,256]{1,0:T(8,128)(2,1)S(1)} collective-permute-done((bf16[256,256]{1,0:T(8,128)(2,1)S(1)}, bf16[256,256]{1,0:T(8,128)(2,1)S(1)}, u32[]{:S(2)}, u32[]{:S(2)}) %collective-permute-start.31) | collective-permute-done | bytes 131104 | tf_op jit(solution)/shard_map/ppermute | solution.py:33
  49.3 0.6 collective-permute-start.32
  49.8 0.5 collective-permute-done.27
  50.4 1.6 %collective-permute-start.28 = (bf16[256,256]{1,0:T(8,128)(2,1)S(1)}, bf16[256,256]{1,0:T(8,128)(2,1)S(1)}, u32[]{:S(2)}, u32[]{:S(2)}) collective-permute-start(bf16[256,256]{1,0:T(8,128)(2,1)S(1)} %add_convert_fusion.7), channel_id=1, source_target_pairs={{0,1},{2,0},{4,2},{6,4},{7,6},{5,7},{3,5},{1,3},{8,9},{10,8},{12,1... | collective-permute-start | bytes 393224 | tf_op jit(solution)/shard_map/ppermute | solution.py:33
  52.0 0.7 %collective-permute-done.24 = bf16[256,256]{1,0:T(8,128)(2,1)S(1)} collective-permute-done((bf16[256,256]{1,0:T(8,128)(2,1)S(1)}, bf16[256,256]{1,0:T(8,128)(2,1)S(1)}, u32[]{:S(2)}, u32[]{:S(2)}) %collective-permute-start.24) | collective-permute-done | bytes 131104 | tf_op jit(solution)/shard_map/ppermute | solution.py:33
  52.7 1.6 %collective-permute-start.25 = (bf16[256,256]{1,0:T(8,128)(2,1)S(1)}, bf16[256,256]{1,0:T(8,128)(2,1)S(1)}, u32[]{:S(2)}, u32[]{:S(2)}) collective-permute-start(bf16[256,256]{1,0:T(8,128)(2,1)S(1)} %add_convert_fusion.9), channel_id=1, source_target_pairs={{0,1},{2,0},{4,2},{6,4},{7,6},{5,7},{3,5},{1,3},{8,9},{10,8},{12,1... | collective-permute-start | bytes 393224 | tf_op jit(solution)/shard_map/ppermute | solution.py:33
  54.4 0.5 collective-permute-start.22
  55.0 1.6 %collective-permute-start.33 = (bf16[256,256]{1,0:T(8,128)(2,1)S(1)}, bf16[256,256]{1,0:T(8,128)(2,1)S(1)}, u32[]{:S(2)}, u32[]{:S(2)}) collective-permute-start(bf16[256,256]{1,0:T(8,128)(2,1)S(1)} %add_convert_fusion.3), channel_id=1, source_target_pairs={{0,2},{2,4},{4,6},{6,7},{7,5},{5,3},{3,1},{1,0},{8,10},{10,12},{12... | collective-permute-start | bytes 393224 | tf_op jit(solution)/shard_map/ppermute | solution.py:33
  56.8 1.6 %collective-permute-start.29 = (bf16[256,256]{1,0:T(8,128)(2,1)S(1)}, bf16[256,256]{1,0:T(8,128)(2,1)S(1)}, u32[]{:S(2)}, u32[]{:S(2)}) collective-permute-start(bf16[256,256]{1,0:T(8,128)(2,1)S(1)} %add_convert_fusion.6), channel_id=1, source_target_pairs={{0,1},{2,0},{4,2},{6,4},{7,6},{5,7},{3,5},{1,3},{8,9},{10,8},{12,1... | collective-permute-start | bytes 393224 | tf_op jit(solution)/shard_map/ppermute | solution.py:33
  58.4 0.9 %collective-permute-done.25 = bf16[256,256]{1,0:T(8,128)(2,1)S(1)} collective-permute-done((bf16[256,256]{1,0:T(8,128)(2,1)S(1)}, bf16[256,256]{1,0:T(8,128)(2,1)S(1)}, u32[]{:S(2)}, u32[]{:S(2)}) %collective-permute-start.25) | collective-permute-done | bytes 131104 | tf_op jit(solution)/shard_map/ppermute | solution.py:33
  59.3 1.6 %collective-permute-start.26 = (bf16[256,256]{1,0:T(8,128)(2,1)S(1)}, bf16[256,256]{1,0:T(8,128)(2,1)S(1)}, u32[]{:S(2)}, u32[]{:S(2)}) collective-permute-start(bf16[256,256]{1,0:T(8,128)(2,1)S(1)} %add_convert_fusion.8), channel_id=1, source_target_pairs={{0,1},{2,0},{4,2},{6,4},{7,6},{5,7},{3,5},{1,3},{8,9},{10,8},{12,1... | collective-permute-start | bytes 393224 | tf_op jit(solution)/shard_map/ppermute | solution.py:33
  60.9 0.5 collective-permute-start.23
  61.5 1.8 %collective-permute-start.34 = (bf16[256,256]{1,0:T(8,128)(2,1)S(1)}, bf16[256,256]{1,0:T(8,128)(2,1)S(1)}, u32[]{:S(2)}, u32[]{:S(2)}) collective-permute-start(bf16[256,256]{1,0:T(8,128)(2,1)S(1)} %add_convert_fusion.2), channel_id=1, source_target_pairs={{0,2},{2,4},{4,6},{6,7},{7,5},{5,3},{3,1},{1,0},{8,10},{10,12},{12... | collective-permute-start | bytes 393224 | tf_op jit(solution)/shard_map/ppermute | solution.py:33
  63.3 0.9 %collective-permute-start.30 = (bf16[256,256]{1,0:T(8,128)(2,1)S(1)}, bf16[256,256]{1,0:T(8,128)(2,1)S(1)}, u32[]{:S(2)}, u32[]{:S(2)}) collective-permute-start(bf16[256,256]{1,0:T(8,128)(2,1)S(1)} %add_convert_fusion.5), channel_id=1, source_target_pairs={{0,1},{2,0},{4,2},{6,4},{7,6},{5,7},{3,5},{1,3},{8,9},{10,8},{12,1... | collective-permute-start | bytes 393224 | tf_op jit(solution)/shard_map/ppermute | solution.py:33
  64.2 1.4 %collective-permute-done.26 = bf16[256,256]{1,0:T(8,128)(2,1)S(1)} collective-permute-done((bf16[256,256]{1,0:T(8,128)(2,1)S(1)}, bf16[256,256]{1,0:T(8,128)(2,1)S(1)}, u32[]{:S(2)}, u32[]{:S(2)}) %collective-permute-start.26) | collective-permute-done | bytes 131104 | tf_op jit(solution)/shard_map/ppermute | solution.py:33
  65.9 1.4 %collective-permute-done.34 = bf16[256,256]{1,0:T(8,128)(2,1)S(1)} collective-permute-done((bf16[256,256]{1,0:T(8,128)(2,1)S(1)}, bf16[256,256]{1,0:T(8,128)(2,1)S(1)}, u32[]{:S(2)}, u32[]{:S(2)}) %collective-permute-start.34) | collective-permute-done | bytes 131104 | tf_op jit(solution)/shard_map/ppermute | solution.py:33
  67.3 1.0 %collective-permute-done.30 = bf16[256,256]{1,0:T(8,128)(2,1)S(1)} collective-permute-done((bf16[256,256]{1,0:T(8,128)(2,1)S(1)}, bf16[256,256]{1,0:T(8,128)(2,1)S(1)}, u32[]{:S(2)}, u32[]{:S(2)}) %collective-permute-start.30) | collective-permute-done | bytes 131104 | tf_op jit(solution)/shard_map/ppermute | solution.py:33
  68.4 0.7 %pad_maximum_fusion = bf16[512,256]{1,0:T(8,128)(2,1)} fusion(bf16[256,256]{1,0:T(8,128)(2,1)S(1)} %get-tuple-element.87, bf16[256,256]{1,0:T(8,128)(2,1)S(1)} %get-tuple-element.88), kind=kLoop, calls=%fused_computation | loop fusion | flops 524288 | bytes 524288 | tf_op jit(solution)/shard_map/concatenate | solution.py:452
  (50 shorter events, 3.6 us)
Async XLA Ops:
  1.0 8.1 %collective-permute-start.3 = (bf16[256,256]{1,0:T(8,128)(2,1)S(1)}, bf16[256,256]{1,0:T(8,128)(2,1)S(1)}, u32[]{:S(2)}, u32[]{:S(2)}) collective-permute-start(bf16[256,256]{1,0:T(8,128)(2,1)S(1)} %get-tuple-element.85), channel_id=1, source_target_pairs={{0,1},{2,0},{4,2},{6,4},{7,6},{5,7},{3,5},{1,3},{8,9},{10,8},{12,1... | collective-permute-start | bytes 393224 | tf_op jit(solution)/shard_map/ppermute | solution.py:33
  4.0 7.1 %collective-permute-start = (bf16[256,256]{1,0:T(8,128)(2,1)S(1)}, bf16[256,256]{1,0:T(8,128)(2,1)S(1)}, u32[]{:S(2)}, u32[]{:S(2)}) collective-permute-start(bf16[256,256]{1,0:T(8,128)(2,1)S(1)} %get-tuple-element.86), channel_id=1, source_target_pairs={{0,2},{2,4},{4,6},{6,7},{7,5},{5,3},{3,1},{1,0},{8,10},{10,12},{12... | collective-permute-start | bytes 393224 | tf_op jit(solution)/shard_map/ppermute | solution.py:33
  4.1 7.1 %collective-permute-start.6 = (bf16[256,256]{1,0:T(8,128)(2,1)S(1)}, bf16[256,256]{1,0:T(8,128)(2,1)S(1)}, u32[]{:S(2)}, u32[]{:S(2)}) collective-permute-start(bf16[256,256]{1,0:T(8,128)(2,1)S(1)} %get-tuple-element.86), channel_id=1, source_target_pairs={{0,1},{2,0},{4,2},{6,4},{7,6},{5,7},{3,5},{1,3},{8,9},{10,8},{12,1... | collective-permute-start | bytes 393224 | tf_op jit(solution)/shard_map/ppermute | solution.py:33
  6.0 7.1 %collective-permute-start.8 = (bf16[256,256]{1,0:T(8,128)(2,1)S(1)}, bf16[256,256]{1,0:T(8,128)(2,1)S(1)}, u32[]{:S(2)}, u32[]{:S(2)}) collective-permute-start(bf16[256,256]{1,0:T(8,128)(2,1)S(1)} %get-tuple-element.85), channel_id=1, source_target_pairs={{0,2},{2,4},{4,6},{6,7},{7,5},{5,3},{3,1},{1,0},{8,10},{10,12},{12... | collective-permute-start | bytes 393224 | tf_op jit(solution)/shard_map/ppermute | solution.py:33
  9.1 6.4 %collective-permute-start.4 = (bf16[256,256]{1,0:T(8,128)(2,1)S(1)}, bf16[256,256]{1,0:T(8,128)(2,1)S(1)}, u32[]{:S(2)}, u32[]{:S(2)}) collective-permute-start(bf16[256,256]{1,0:T(8,128)(2,1)S(1)} %collective-permute-done.3.refs_1_), channel_id=1, source_target_pairs={{0,1},{2,0},{4,2},{6,4},{7,6},{5,7},{3,5},{1,3},{8,9},{10,8},{12,1... | collective-permute-start | bytes 393224 | tf_op jit(solution)/shard_map/ppermute | solution.py:33
  11.1 6.0 %collective-permute-start.1 = (bf16[256,256]{1,0:T(8,128)(2,1)S(1)}, bf16[256,256]{1,0:T(8,128)(2,1)S(1)}, u32[]{:S(2)}, u32[]{:S(2)}) collective-permute-start(bf16[256,256]{1,0:T(8,128)(2,1)S(1)} %collective-permute-done.refs_0_), channel_id=1, source_target_pairs={{0,2},{2,4},{4,6},{6,7},{7,5},{5,3},{3,1},{1,0},{8,10},{10,12},{12... | collective-permute-start | bytes 393224 | tf_op jit(solution)/shard_map/ppermute | solution.py:33
  11.2 7.1 %collective-permute-start.7 = (bf16[256,256]{1,0:T(8,128)(2,1)S(1)}, bf16[256,256]{1,0:T(8,128)(2,1)S(1)}, u32[]{:S(2)}, u32[]{:S(2)}) collective-permute-start(bf16[256,256]{1,0:T(8,128)(2,1)S(1)} %collective-permute-done.6.refs_2_), channel_id=1, source_target_pairs={{0,1},{2,0},{4,2},{6,4},{7,6},{5,7},{3,5},{1,3},{8,9},{10,8},{12,1... | collective-permute-start | bytes 393224 | tf_op jit(solution)/shard_map/ppermute | solution.py:33
  13.1 6.8 %collective-permute-start.9 = (bf16[256,256]{1,0:T(8,128)(2,1)S(1)}, bf16[256,256]{1,0:T(8,128)(2,1)S(1)}, u32[]{:S(2)}, u32[]{:S(2)}) collective-permute-start(bf16[256,256]{1,0:T(8,128)(2,1)S(1)} %collective-permute-done.8.refs_3_), channel_id=1, source_target_pairs={{0,2},{2,4},{4,6},{6,7},{7,5},{5,3},{3,1},{1,0},{8,10},{10,12},{12... | collective-permute-start | bytes 393224 | tf_op jit(solution)/shard_map/ppermute | solution.py:33
  15.5 5.7 %collective-permute-start.5 = (bf16[256,256]{1,0:T(8,128)(2,1)S(1)}, bf16[256,256]{1,0:T(8,128)(2,1)S(1)}, u32[]{:S(2)}, u32[]{:S(2)}) collective-permute-start(bf16[256,256]{1,0:T(8,128)(2,1)S(1)} %collective-permute-done.4.refs_1_), channel_id=1, source_target_pairs={{0,1},{2,0},{4,2},{6,4},{7,6},{5,7},{3,5},{1,3},{8,9},{10,8},{12,1... | collective-permute-start | bytes 393224 | tf_op jit(solution)/shard_map/ppermute | solution.py:33
  17.1 5.7 %collective-permute-start.2 = (bf16[256,256]{1,0:T(8,128)(2,1)S(1)}, bf16[256,256]{1,0:T(8,128)(2,1)S(1)}, u32[]{:S(2)}, u32[]{:S(2)}) collective-permute-start(bf16[256,256]{1,0:T(8,128)(2,1)S(1)} %collective-permute-done.1.refs_0_), channel_id=1, source_target_pairs={{0,2},{2,4},{4,6},{6,7},{7,5},{5,3},{3,1},{1,0},{8,10},{10,12},{12... | collective-permute-start | bytes 393224 | tf_op jit(solution)/shard_map/ppermute | solution.py:33
  18.3 5.2 %collective-permute-start.10 = (bf16[256,256]{1,0:T(8,128)(2,1)S(1)}, bf16[256,256]{1,0:T(8,128)(2,1)S(1)}, u32[]{:S(2)}, u32[]{:S(2)}) collective-permute-start(bf16[256,256]{1,0:T(8,128)(2,1)S(1)} %collective-permute-done.7.refs_2_), channel_id=1, source_target_pairs={{0,1},{2,0},{4,2},{6,4},{7,6},{5,7},{3,5},{1,3},{8,9},{10,8},{12,1... | collective-permute-start | bytes 393224 | tf_op jit(solution)/shard_map/ppermute | solution.py:33
  19.9 5.0 %collective-permute-start.11 = (bf16[256,256]{1,0:T(8,128)(2,1)S(1)}, bf16[256,256]{1,0:T(8,128)(2,1)S(1)}, u32[]{:S(2)}, u32[]{:S(2)}) collective-permute-start(bf16[256,256]{1,0:T(8,128)(2,1)S(1)} %collective-permute-done.9.refs_3_), channel_id=1, source_target_pairs={{0,2},{2,4},{4,6},{6,7},{7,5},{5,3},{3,1},{1,0},{8,10},{10,12},{12... | collective-permute-start | bytes 393224 | tf_op jit(solution)/shard_map/ppermute | solution.py:33
  21.2 5.7 %collective-permute-start.13 = (bf16[256,256]{1,0:T(8,128)(2,1)S(1)}, bf16[256,256]{1,0:T(8,128)(2,1)S(1)}, u32[]{:S(2)}, u32[]{:S(2)}) collective-permute-start(bf16[256,256]{1,0:T(8,128)(2,1)S(1)} %collective-permute-done.5.refs_1_), channel_id=1, source_target_pairs={{0,1},{2,0},{4,2},{6,4},{7,6},{5,7},{3,5},{1,3},{8,9},{10,8},{12,1... | collective-permute-start | bytes 393224 | tf_op jit(solution)/shard_map/ppermute | solution.py:33
  22.8 5.0 %collective-permute-start.12 = (bf16[256,256]{1,0:T(8,128)(2,1)S(1)}, bf16[256,256]{1,0:T(8,128)(2,1)S(1)}, u32[]{:S(2)}, u32[]{:S(2)}) collective-permute-start(bf16[256,256]{1,0:T(8,128)(2,1)S(1)} %collective-permute-done.2.refs_0_), channel_id=1, source_target_pairs={{0,2},{2,4},{4,6},{6,7},{7,5},{5,3},{3,1},{1,0},{8,10},{10,12},{12... | collective-permute-start | bytes 393224 | tf_op jit(solution)/shard_map/ppermute | solution.py:33
  29.1 6.9 %collective-permute-start.17 = (bf16[256,512]{1,0:T(8,128)(2,1)S(1)}, bf16[256,512]{1,0:T(8,128)(2,1)S(1)}, u32[]{:S(2)}, u32[]{:S(2)}) collective-permute-start(bf16[256,512]{1,0:T(8,128)(2,1)S(1)} %get-tuple-element.53.refs_0_), channel_id=1, source_target_pairs={{0,16},{8,24},{16,0},{24,8},{1,17},{9,25},{17,1},{25,9},{2,18},{10... | collective-permute-start | bytes 786440 | tf_op jit(solution)/shard_map/ppermute | solution.py:425
  30.6 8.2 %collective-permute-start.18 = (bf16[256,512]{1,0:T(8,128)(2,1)S(1)}, bf16[256,512]{1,0:T(8,128)(2,1)S(1)}, u32[]{:S(2)}, u32[]{:S(2)}) collective-permute-start(bf16[256,512]{1,0:T(8,128)(2,1)S(1)} %get-tuple-element.54.refs_1_), channel_id=1, source_target_pairs={{0,16},{8,24},{16,0},{24,8},{1,17},{9,25},{17,1},{25,9},{2,18},{10... | collective-permute-start | bytes 786440 | tf_op jit(solution)/shard_map/ppermute | solution.py:425
  31.1 2.7 %collective-permute-start.15 = (bf16[176,512]{1,0:T(8,128)(2,1)S(1)}, bf16[176,512]{1,0:T(8,128)(2,1)S(1)}, u32[]{:S(2)}, u32[]{:S(2)}) collective-permute-start(bf16[176,512]{1,0:T(8,128)(2,1)S(1)} %get-tuple-element.56), channel_id=1, source_target_pairs={{0,8},{8,0},{16,24},{24,16},{1,9},{9,1},{17,25},{25,17},{2,10},{10... | collective-permute-start | bytes 540680 | tf_op jit(solution)/shard_map/ppermute | solution.py:39
  31.1 2.7 %collective-permute-start.16 = (bf16[176,512]{1,0:T(8,128)(2,1)S(1)}, bf16[176,512]{1,0:T(8,128)(2,1)S(1)}, u32[]{:S(2)}, u32[]{:S(2)}) collective-permute-start(bf16[176,512]{1,0:T(8,128)(2,1)S(1)} %get-tuple-element.57), channel_id=1, source_target_pairs={{0,8},{8,0},{16,24},{24,16},{1,9},{9,1},{17,25},{25,17},{2,10},{10... | collective-permute-start | bytes 540680 | tf_op jit(solution)/shard_map/ppermute | solution.py:39
  31.7 2.2 %collective-permute-start.14 = (bf16[160,512]{1,0:T(8,128)(2,1)S(1)}, bf16[160,512]{1,0:T(8,128)(2,1)S(1)}, u32[]{:S(2)}, u32[]{:S(2)}) collective-permute-start(bf16[160,512]{1,0:T(8,128)(2,1)S(1)} %get-tuple-element.55), channel_id=1, source_target_pairs={{0,8},{8,0},{16,24},{24,16},{1,9},{9,1},{17,25},{25,17},{2,10},{10... | collective-permute-start | bytes 491528 | tf_op jit(solution)/shard_map/ppermute | solution.py:39
  38.8 1.7 %collective-permute-start.19 = (bf16[256,512]{1,0:T(8,128)(2,1)S(1)}, bf16[256,512]{1,0:T(8,128)(2,1)S(1)}, u32[]{:S(2)}, u32[]{:S(2)}) collective-permute-start(bf16[256,512]{1,0:T(8,128)(2,1)S(1)} %collective-permute-done.17.refs_0_), channel_id=1, source_target_pairs={{0,8},{8,0},{16,24},{24,16},{1,9},{9,1},{17,25},{25,17},{2,10},{10... | collective-permute-start | bytes 786440 | tf_op jit(solution)/shard_map/ppermute | solution.py:39
  38.8 1.9 %collective-permute-start.20 = (bf16[256,512]{1,0:T(8,128)(2,1)S(1)}, bf16[256,512]{1,0:T(8,128)(2,1)S(1)}, u32[]{:S(2)}, u32[]{:S(2)}) collective-permute-start(bf16[256,512]{1,0:T(8,128)(2,1)S(1)} %collective-permute-done.18.refs_1_), channel_id=1, source_target_pairs={{0,8},{8,0},{16,24},{24,16},{1,9},{9,1},{17,25},{25,17},{2,10},{10... | collective-permute-start | bytes 786440 | tf_op jit(solution)/shard_map/ppermute | solution.py:39
  43.5 5.8 %collective-permute-start.31 = (bf16[256,256]{1,0:T(8,128)(2,1)S(1)}, bf16[256,256]{1,0:T(8,128)(2,1)S(1)}, u32[]{:S(2)}, u32[]{:S(2)}) collective-permute-start(bf16[256,256]{1,0:T(8,128)(2,1)S(1)} %get-tuple-element.79), channel_id=1, source_target_pairs={{0,2},{2,4},{4,6},{6,7},{7,5},{5,3},{3,1},{1,0},{8,10},{10,12},{12... | collective-permute-start | bytes 393224 | tf_op jit(solution)/shard_map/ppermute | solution.py:33
  44.0 6.4 %collective-permute-start.27 = (bf16[256,256]{1,0:T(8,128)(2,1)S(1)}, bf16[256,256]{1,0:T(8,128)(2,1)S(1)}, u32[]{:S(2)}, u32[]{:S(2)}) collective-permute-start(bf16[256,256]{1,0:T(8,128)(2,1)S(1)} %get-tuple-element.75), channel_id=1, source_target_pairs={{0,1},{2,0},{4,2},{6,4},{7,6},{5,7},{3,5},{1,3},{8,9},{10,8},{12,1... | collective-permute-start | bytes 393224 | tf_op jit(solution)/shard_map/ppermute | solution.py:33
  45.5 7.2 %collective-permute-start.24 = (bf16[256,256]{1,0:T(8,128)(2,1)S(1)}, bf16[256,256]{1,0:T(8,128)(2,1)S(1)}, u32[]{:S(2)}, u32[]{:S(2)}) collective-permute-start(bf16[256,256]{1,0:T(8,128)(2,1)S(1)} %get-tuple-element.71), channel_id=1, source_target_pairs={{0,1},{2,0},{4,2},{6,4},{7,6},{5,7},{3,5},{1,3},{8,9},{10,8},{12,1... | collective-permute-start | bytes 393224 | tf_op jit(solution)/shard_map/ppermute | solution.py:33
  47.1 7.2 %collective-permute-start.21 = (bf16[256,256]{1,0:T(8,128)(2,1)S(1)}, bf16[256,256]{1,0:T(8,128)(2,1)S(1)}, u32[]{:S(2)}, u32[]{:S(2)}) collective-permute-start(bf16[256,256]{1,0:T(8,128)(2,1)S(1)} %get-tuple-element.68), channel_id=1, source_target_pairs={{0,2},{2,4},{4,6},{6,7},{7,5},{5,3},{3,1},{1,0},{8,10},{10,12},{12... | collective-permute-start | bytes 393224 | tf_op jit(solution)/shard_map/ppermute | solution.py:33
  49.3 5.7 %collective-permute-start.32 = (bf16[256,256]{1,0:T(8,128)(2,1)S(1)}, bf16[256,256]{1,0:T(8,128)(2,1)S(1)}, u32[]{:S(2)}, u32[]{:S(2)}) collective-permute-start(bf16[256,256]{1,0:T(8,128)(2,1)S(1)} %add_convert_fusion.4), channel_id=1, source_target_pairs={{0,2},{2,4},{4,6},{6,7},{7,5},{5,3},{3,1},{1,0},{8,10},{10,12},{12... | collective-permute-start | bytes 393224 | tf_op jit(solution)/shard_map/ppermute | solution.py:33
  50.4 6.3 %collective-permute-start.28 = (bf16[256,256]{1,0:T(8,128)(2,1)S(1)}, bf16[256,256]{1,0:T(8,128)(2,1)S(1)}, u32[]{:S(2)}, u32[]{:S(2)}) collective-permute-start(bf16[256,256]{1,0:T(8,128)(2,1)S(1)} %add_convert_fusion.7), channel_id=1, source_target_pairs={{0,1},{2,0},{4,2},{6,4},{7,6},{5,7},{3,5},{1,3},{8,9},{10,8},{12,1... | collective-permute-start | bytes 393224 | tf_op jit(solution)/shard_map/ppermute | solution.py:33
  52.7 6.5 %collective-permute-start.25 = (bf16[256,256]{1,0:T(8,128)(2,1)S(1)}, bf16[256,256]{1,0:T(8,128)(2,1)S(1)}, u32[]{:S(2)}, u32[]{:S(2)}) collective-permute-start(bf16[256,256]{1,0:T(8,128)(2,1)S(1)} %add_convert_fusion.9), channel_id=1, source_target_pairs={{0,1},{2,0},{4,2},{6,4},{7,6},{5,7},{3,5},{1,3},{8,9},{10,8},{12,1... | collective-permute-start | bytes 393224 | tf_op jit(solution)/shard_map/ppermute | solution.py:33
  54.4 6.5 %collective-permute-start.22 = (bf16[256,256]{1,0:T(8,128)(2,1)S(1)}, bf16[256,256]{1,0:T(8,128)(2,1)S(1)}, u32[]{:S(2)}, u32[]{:S(2)}) collective-permute-start(bf16[256,256]{1,0:T(8,128)(2,1)S(1)} %add_convert_fusion.11), channel_id=1, source_target_pairs={{0,2},{2,4},{4,6},{6,7},{7,5},{5,3},{3,1},{1,0},{8,10},{10,12},{12... | collective-permute-start | bytes 393224 | tf_op jit(solution)/shard_map/ppermute | solution.py:33
  55.0 6.5 %collective-permute-start.33 = (bf16[256,256]{1,0:T(8,128)(2,1)S(1)}, bf16[256,256]{1,0:T(8,128)(2,1)S(1)}, u32[]{:S(2)}, u32[]{:S(2)}) collective-permute-start(bf16[256,256]{1,0:T(8,128)(2,1)S(1)} %add_convert_fusion.3), channel_id=1, source_target_pairs={{0,2},{2,4},{4,6},{6,7},{7,5},{5,3},{3,1},{1,0},{8,10},{10,12},{12... | collective-permute-start | bytes 393224 | tf_op jit(solution)/shard_map/ppermute | solution.py:33
  56.8 6.5 %collective-permute-start.29 = (bf16[256,256]{1,0:T(8,128)(2,1)S(1)}, bf16[256,256]{1,0:T(8,128)(2,1)S(1)}, u32[]{:S(2)}, u32[]{:S(2)}) collective-permute-start(bf16[256,256]{1,0:T(8,128)(2,1)S(1)} %add_convert_fusion.6), channel_id=1, source_target_pairs={{0,1},{2,0},{4,2},{6,4},{7,6},{5,7},{3,5},{1,3},{8,9},{10,8},{12,1... | collective-permute-start | bytes 393224 | tf_op jit(solution)/shard_map/ppermute | solution.py:33
  59.3 6.3 %collective-permute-start.26 = (bf16[256,256]{1,0:T(8,128)(2,1)S(1)}, bf16[256,256]{1,0:T(8,128)(2,1)S(1)}, u32[]{:S(2)}, u32[]{:S(2)}) collective-permute-start(bf16[256,256]{1,0:T(8,128)(2,1)S(1)} %add_convert_fusion.8), channel_id=1, source_target_pairs={{0,1},{2,0},{4,2},{6,4},{7,6},{5,7},{3,5},{1,3},{8,9},{10,8},{12,1... | collective-permute-start | bytes 393224 | tf_op jit(solution)/shard_map/ppermute | solution.py:33
  60.9 5.0 %collective-permute-start.23 = (bf16[256,256]{1,0:T(8,128)(2,1)S(1)}, bf16[256,256]{1,0:T(8,128)(2,1)S(1)}, u32[]{:S(2)}, u32[]{:S(2)}) collective-permute-start(bf16[256,256]{1,0:T(8,128)(2,1)S(1)} %add_convert_fusion.10), channel_id=1, source_target_pairs={{0,2},{2,4},{4,6},{6,7},{7,5},{5,3},{3,1},{1,0},{8,10},{10,12},{12... | collective-permute-start | bytes 393224 | tf_op jit(solution)/shard_map/ppermute | solution.py:33
  61.5 5.9 %collective-permute-start.34 = (bf16[256,256]{1,0:T(8,128)(2,1)S(1)}, bf16[256,256]{1,0:T(8,128)(2,1)S(1)}, u32[]{:S(2)}, u32[]{:S(2)}) collective-permute-start(bf16[256,256]{1,0:T(8,128)(2,1)S(1)} %add_convert_fusion.2), channel_id=1, source_target_pairs={{0,2},{2,4},{4,6},{6,7},{7,5},{5,3},{3,1},{1,0},{8,10},{10,12},{12... | collective-permute-start | bytes 393224 | tf_op jit(solution)/shard_map/ppermute | solution.py:33
  63.3 5.0 %collective-permute-start.30 = (bf16[256,256]{1,0:T(8,128)(2,1)S(1)}, bf16[256,256]{1,0:T(8,128)(2,1)S(1)}, u32[]{:S(2)}, u32[]{:S(2)}) collective-permute-start(bf16[256,256]{1,0:T(8,128)(2,1)S(1)} %add_convert_fusion.5), channel_id=1, source_target_pairs={{0,1},{2,0},{4,2},{6,4},{7,6},{5,7},{3,5},{1,3},{8,9},{10,8},{12,1... | collective-permute-start | bytes 393224 | tf_op jit(solution)/shard_map/ppermute | solution.py:33

commit v24 on v23

--- a/solution.py
+++ b/solution.py
@@ -319,7 +319,7 @@
         ).astype(BF16)
 
 
-def attend(info, ids, query, blocks, head_size, acc=None, w_out=None, streams=0):
+def attend(info, ids, query, blocks, head_size, acc=None, w_out=None, streams=0, tile=512):
     total, width = query.shape
     parts = [part for block in blocks for part in block]
     keys = sum(part.shape[0] for part in blocks[0])
@@ -330,7 +330,7 @@
         pltpu.VMEM((heads, keys, 2 * head_size), BF16),
         pltpu.VMEM((total, 2 * width), F32),
     ]
-    id_rows = ids.reshape(-1, 1, math.gcd(total, 512))
+    id_rows = ids.reshape(-1, 1, math.gcd(total, tile))
     operands = [in_vmem(query), *map(in_vmem, parts)]
     if acc is not None:
         operands.append(in_vmem(acc))
@@ -424,10 +424,10 @@
             shift = [(2 * a + b, 2 * ((a + step) % outer) + b) for a in range(outer) for b in (0, 1)]
             far.append([lax.ppermute(part, "seq", shift) for part in halves])
     first = [seq_at * rows]
-    (acc,) = attend(numbers(straight[:1] + first), scale_ids, query, [halves], head_size)
+    (acc,) = attend(numbers(straight[:1] + first), scale_ids, query, [halves], head_size, tile=256)
     near = [[swapped(piece, seqs) for piece in pieces]]
     acc, near = lax.optimization_barrier((acc, near))
-    (acc,) = attend(numbers(crossed[:1] + first), scale_ids, query, near, head_size, acc)
+    (acc,) = attend(numbers(crossed[:1] + first), scale_ids, query, near, head_size, acc, tile=256)
     acc, far = lax.optimization_barrier((acc, far))
     far_crossed = [[swapped(part, seqs) for part in block] for block in far]
     (acc,) = attend(numbers(straight[1:] + first), scale_ids, query, far, head_size, acc)

time: 69.7 us -> 69.7 us (level)
  transfers between devices with their start and end apart: 35 -> 35, of which waited for: 18 -> 17; matrix products, arithmetic and copies ran while one was open for 1% -> 1% of each run, Pallas kernels for 15% -> 15%
where the time goes in v24:
time: 69.7 us; the launch traced here: 69.1 us
  starting transfers between devices  34.9 us (50%)
  waiting for transfers between devices  17.2 us (25%)
  Pallas kernels  14.3 us (21%)
  other arithmetic  1.39 us (2%)
  local copies, waits for them, and re-layouts  1.16 us (2%)
    ppermute x28, starting transfers between devices, along(): lax.ppermute(value, 'head', [(order[p], order[(p + step) % count]) for p...  31.8 us
    ppermute x28, waiting for transfers between devices, along(): lax.ppermute(value, 'head', [(order[p], order[(p + step) % count]) for p...  14.2 us
    pallas_call x4, Pallas kernels, attend(): pl.pallas_call(functools.partial(attend_kernel, head_size, (len(blocks),...  7.87 us
    pallas_call x1, Pallas kernels, fold_gain(): pl.pallas_call(functools.partial(fold_kernel, order), out_shape=(pltpu.VM...  2.88 us
    ppermute x2, waiting for transfers between devices, body(): far.append([lax.ppermute(part, 'seq', shift) for part in halves])  2.86 us
    ppermute x2, starting transfers between devices, body(): far.append([lax.ppermute(part, 'seq', shift) for part in halves])  2.09 us
    pallas_call x1, Pallas kernels, project_begin(): pl.pallas_call(functools.partial(begin_kernel, blocks), out_shape=pltpu.V...  1.92 us
  transfers between devices with their start and end apart: 35, of which 17 were waited for; matrix products, arithmetic and copies ran while one was open for 1% of the time, Pallas kernels for 15%

profile of v24, /device:TPU:0, one launch (start us, length us, event | category | flops | bytes accessed | tf_op | source)
XLA Modules:
  0.0 69.1 jit_solution(13227944288778824001)
XLA Ops:
  0.0 1.0 %fusion = (bf16[256,256]{1,0:T(8,128)(2,1)S(1)}, bf16[256,256]{1,0:T(8,128)(2,1)S(1)}) fusion(bf16[512,256]{1,0:T(8,128)(2,1)} %tokens.1), kind=kLoop, calls=%fused_computation.16 | loop fusion | bytes 524288 | tf_op jit(solution)/shard_map/slice | solution.py:390
  1.0 3.0 %collective-permute-start.3 = (bf16[256,256]{1,0:T(8,128)(2,1)S(1)}, bf16[256,256]{1,0:T(8,128)(2,1)S(1)}, u32[]{:S(2)}, u32[]{:S(2)}) collective-permute-start(bf16[256,256]{1,0:T(8,128)(2,1)S(1)} %get-tuple-element.85), channel_id=1, source_target_pairs={{0,1},{2,0},{4,2},{6,4},{7,6},{5,7},{3,5},{1,3},{8,9},{10,8},{12,1... | collective-permute-start | bytes 393224 | tf_op jit(solution)/shard_map/ppermute | solution.py:33
  4.1 1.9 %collective-permute-start.6 = (bf16[256,256]{1,0:T(8,128)(2,1)S(1)}, bf16[256,256]{1,0:T(8,128)(2,1)S(1)}, u32[]{:S(2)}, u32[]{:S(2)}) collective-permute-start(bf16[256,256]{1,0:T(8,128)(2,1)S(1)} %get-tuple-element.86), channel_id=1, source_target_pairs={{0,1},{2,0},{4,2},{6,4},{7,6},{5,7},{3,5},{1,3},{8,9},{10,8},{12,1... | collective-permute-start | bytes 393224 | tf_op jit(solution)/shard_map/ppermute | solution.py:33
  6.2 2.9 %fold_gain.1 = (bf16[3,2048,256]{2,1,0:T(8,128)(2,1)S(1)}, bf16[512,2048]{1,0:T(8,128)(2,1)S(1)}) custom-call(s32[8]{0:T(128)S(1)} %stack.84.at, f32[16,128]{1,0:T(8,128)} %bitcast.20, bf16[3,2048,256]{2,1,0:T(8,128)(2,1)} %w_hbm.1, bf16[512,256]{1,0:T(8,128)(2,1)} %tokens.1), custom_call_target="tpu_custom_call" | custom-call | flops 1572864 | bytes 6291456 | tf_op jit(solution)/shard_map/fold_gain/pallas_call | solution.py:86
  9.1 2.0 %collective-permute-start.4 = (bf16[256,256]{1,0:T(8,128)(2,1)S(1)}, bf16[256,256]{1,0:T(8,128)(2,1)S(1)}, u32[]{:S(2)}, u32[]{:S(2)}) collective-permute-start(bf16[256,256]{1,0:T(8,128)(2,1)S(1)} %collective-permute-done.3.refs_1_), channel_id=1, source_target_pairs={{0,1},{2,0},{4,2},{6,4},{7,6},{5,7},{3,5},{1,3},{8,9},{10,8},{12,1... | collective-permute-start | bytes 393224 | tf_op jit(solution)/shard_map/ppermute | solution.py:33
  11.2 1.9 %collective-permute-start.7 = (bf16[256,256]{1,0:T(8,128)(2,1)S(1)}, bf16[256,256]{1,0:T(8,128)(2,1)S(1)}, u32[]{:S(2)}, u32[]{:S(2)}) collective-permute-start(bf16[256,256]{1,0:T(8,128)(2,1)S(1)} %collective-permute-done.6.refs_2_), channel_id=1, source_target_pairs={{0,1},{2,0},{4,2},{6,4},{7,6},{5,7},{3,5},{1,3},{8,9},{10,8},{12,1... | collective-permute-start | bytes 393224 | tf_op jit(solution)/shard_map/ppermute | solution.py:33
  13.3 2.2 %collective-permute-done.4.refs_1_ = bf16[256,256]{1,0:T(8,128)(2,1)S(1)} collective-permute-done((bf16[256,256]{1,0:T(8,128)(2,1)S(1)}, bf16[256,256]{1,0:T(8,128)(2,1)S(1)}, u32[]{:S(2)}, u32[]{:S(2)}) %collective-permute-start.4) | collective-permute-done | bytes 131104 | tf_op jit(solution)/shard_map/ppermute | solution.py:33
  15.5 1.6 %collective-permute-start.5 = (bf16[256,256]{1,0:T(8,128)(2,1)S(1)}, bf16[256,256]{1,0:T(8,128)(2,1)S(1)}, u32[]{:S(2)}, u32[]{:S(2)}) collective-permute-start(bf16[256,256]{1,0:T(8,128)(2,1)S(1)} %collective-permute-done.4.refs_1_), channel_id=1, source_target_pairs={{0,1},{2,0},{4,2},{6,4},{7,6},{5,7},{3,5},{1,3},{8,9},{10,8},{12,1... | collective-permute-start | bytes 393224 | tf_op jit(solution)/shard_map/ppermute | solution.py:33
  17.5 0.8 %collective-permute-done.7.refs_2_ = bf16[256,256]{1,0:T(8,128)(2,1)S(1)} collective-permute-done((bf16[256,256]{1,0:T(8,128)(2,1)S(1)}, bf16[256,256]{1,0:T(8,128)(2,1)S(1)}, u32[]{:S(2)}, u32[]{:S(2)}) %collective-permute-start.7) | collective-permute-done | bytes 131104 | tf_op jit(solution)/shard_map/ppermute | solution.py:33
  18.3 1.6 %collective-permute-start.10 = (bf16[256,256]{1,0:T(8,128)(2,1)S(1)}, bf16[256,256]{1,0:T(8,128)(2,1)S(1)}, u32[]{:S(2)}, u32[]{:S(2)}) collective-permute-start(bf16[256,256]{1,0:T(8,128)(2,1)S(1)} %collective-permute-done.7.refs_2_), channel_id=1, source_target_pairs={{0,1},{2,0},{4,2},{6,4},{7,6},{5,7},{3,5},{1,3},{8,9},{10,8},{12,1... | collective-permute-start | bytes 393224 | tf_op jit(solution)/shard_map/ppermute | solution.py:33
  20.6 0.6 collective-permute-done.5.refs_1_
  21.2 1.6 %collective-permute-start.13 = (bf16[256,256]{1,0:T(8,128)(2,1)S(1)}, bf16[256,256]{1,0:T(8,128)(2,1)S(1)}, u32[]{:S(2)}, u32[]{:S(2)}) collective-permute-start(bf16[256,256]{1,0:T(8,128)(2,1)S(1)} %collective-permute-done.5.refs_1_), channel_id=1, source_target_pairs={{0,1},{2,0},{4,2},{6,4},{7,6},{5,7},{3,5},{1,3},{8,9},{10,8},{12,1... | collective-permute-start | bytes 393224 | tf_op jit(solution)/shard_map/ppermute | solution.py:33
  22.8 0.4 collective-permute-start.12
  23.5 1.4 %collective-permute-done.11.refs_3_ = bf16[256,256]{1,0:T(8,128)(2,1)S(1)} collective-permute-done((bf16[256,256]{1,0:T(8,128)(2,1)S(1)}, bf16[256,256]{1,0:T(8,128)(2,1)S(1)}, u32[]{:S(2)}, u32[]{:S(2)}) %collective-permute-start.11) | collective-permute-done | bytes 131104 | tf_op jit(solution)/shard_map/ppermute | solution.py:33
  25.0 1.9 %project_begin.1.state = f32[512,896]{1,0:T(8,128)S(1)} custom-call(bf16[512,2048]{1,0:T(8,128)(2,1)S(1)} %place.5.wide, bf16[3,2048,256]{2,1,0:T(8,128)(2,1)S(1)} %get-tuple-element.51.w_ref), custom_call_target="tpu_custom_call" | custom-call | flops 1610612736 | bytes 5242880 | tf_op jit(solution)/shard_map/project_begin/pallas_call | solution.py:191
  26.9 0.8 %collective-permute-done.12.refs_0_ = bf16[256,256]{1,0:T(8,128)(2,1)S(1)} collective-permute-done((bf16[256,256]{1,0:T(8,128)(2,1)S(1)}, bf16[256,256]{1,0:T(8,128)(2,1)S(1)}, u32[]{:S(2)}, u32[]{:S(2)}) %collective-permute-start.12) | collective-permute-done | bytes 131104 | tf_op jit(solution)/shard_map/ppermute | solution.py:33
  27.8 1.3 %project_finish.1 = (bf16[512,256]{1,0:T(8,128)(2,1)S(1)}, bf16[256,512]{1,0:T(8,128)(2,1)S(1)}, bf16[256,512]{1,0:T(8,128)(2,1)S(1)}, bf16[160,512]{1,0:T(8,128...) custom-call(f32[2]{0:T(128)} %factor.1, f32[512,896]{1,0:T(8,128)S(1)} %project_begin.1.state, ...), custom_call_target="tpu_custom_call" | custom-call | flops 201326592 | bytes 1048576 | tf_op jit(solution)/shard_map/project_finish/pallas_call | solution.py:213
  29.1 1.6 %collective-permute-start.17 = (bf16[256,512]{1,0:T(8,128)(2,1)S(1)}, bf16[256,512]{1,0:T(8,128)(2,1)S(1)}, u32[]{:S(2)}, u32[]{:S(2)}) collective-permute-start(bf16[256,512]{1,0:T(8,128)(2,1)S(1)} %get-tuple-element.53.refs_0_), channel_id=1, source_target_pairs={{0,16},{8,24},{16,0},{24,8},{1,17},{9,25},{17,1},{25,9},{2,18},{10... | collective-permute-start | bytes 786440 | tf_op jit(solution)/shard_map/ppermute | solution.py:425
  30.6 0.5 collective-permute-start.18
  31.1 0.5 collective-permute-start.16
  31.8 2.3 %attend.3.refs_3_ = f32[512,512]{1,0:T(8,128)S(1)} custom-call(s32[2]{0:T(128)S(1)} %pad_add_fusion.1.info, s32[2048]{0:T(1024)} %ids.7, s32[8,1,256]{2,1,0:T(1,128)} %bitcast.16, bf16[512,256]{1,0:T(8,128)(2,1)S(1)} %get-tuple-element.52.q_ref, bf16[256,512]{1,0:T(8,128)(2,1)S(1)} %get-tuple-element.53.refs_0_, bf16[256,512]{1,0:T(8,128)(2,1)S(1)} %get-tuple-element.54.refs_1_), custom_call_target="tpu_custom_call" | custom-call | flops 1048576 | bytes 1024 | tf_op jit(solution)/shard_map/attend/pallas_call | solution.py:351
  34.2 1.7 %attend.4.refs_2_ = f32[512,512]{1,0:T(8,128)S(1)} custom-call(s32[2]{0:T(128)S(1)} %pad_add_fusion.info, s32[2048]{0:T(1024)} %ids.7, s32[8,1,256]{2,1,0:T(1,128)} %bitcast.17, bf16[512,256]{1,0:T(8,128)(2,1)S(1)} %get-tuple-element.52.q_ref, bf16[160,512]{1,0:T(8,128)(2,1)S(1)} %collective-permute-done.14.refs_0_, ...), custom_call_target="tpu_custom_call" | custom-call | flops 1048576 | bytes 1024 | tf_op jit(solution)/shard_map/attend/pallas_call | solution.py:351
  36.0 2.8 %collective-permute-done.18.refs_1_ = bf16[256,512]{1,0:T(8,128)(2,1)S(1)} collective-permute-done((bf16[256,512]{1,0:T(8,128)(2,1)S(1)}, bf16[256,512]{1,0:T(8,128)(2,1)S(1)}, u32[]{:S(2)}, u32[]{:S(2)}) %collective-permute-start.18) | collective-permute-done | bytes 262176 | tf_op jit(solution)/shard_map/ppermute | solution.py:425
  38.8 0.5 collective-permute-start.20
  39.5 1.0 %attend.5.refs_2_ = f32[512,512]{1,0:T(8,128)S(1)} custom-call(s32[2]{0:T(128)S(1)} %pad_add_fusion.2.info, s32[2048]{0:T(1024)} %ids.7, s32[4,1,512]{2,1,0:T(1,128)} %bitcast.18, bf16[512,256]{1,0:T(8,128)(2,1)S(1)} %get-tuple-element.52.q_ref, bf16[256,512]{1,0:T(8,128)(2,1)S(1)} %collective-permute-done.17.refs_0_, ...), custom_call_target="tpu_custom_call" | custom-call | flops 1048576 | bytes 1024 | tf_op jit(solution)/shard_map/attend/pallas_call | solution.py:351
  40.7 2.8 %attend_last.1 = (bf16[256,256]{1,0:T(8,128)(2,1)S(1)}, bf16[256,256]{1,0:T(8,128)(2,1)S(1)}, bf16[256,256]{1,0:T(8,128)(2,1)S(1)}, bf16[256,256]{1,0:T(8,128)(2...) custom-call(s32[18]{0:T(128)S(1)} %stack.83.info, ...), custom_call_target="tpu_custom_call" | custom-call | flops 1048576 | bytes 1024 | tf_op jit(solution)/shard_map/attend_last/pallas_call | solution.py:351
  43.5 0.5 collective-permute-start.31
  44.0 1.5 %collective-permute-start.27 = (bf16[256,256]{1,0:T(8,128)(2,1)S(1)}, bf16[256,256]{1,0:T(8,128)(2,1)S(1)}, u32[]{:S(2)}, u32[]{:S(2)}) collective-permute-start(bf16[256,256]{1,0:T(8,128)(2,1)S(1)} %get-tuple-element.75), channel_id=1, source_target_pairs={{0,1},{2,0},{4,2},{6,4},{7,6},{5,7},{3,5},{1,3},{8,9},{10,8},{12,1... | collective-permute-start | bytes 393224 | tf_op jit(solution)/shard_map/ppermute | solution.py:33
  45.5 1.6 %collective-permute-start.24 = (bf16[256,256]{1,0:T(8,128)(2,1)S(1)}, bf16[256,256]{1,0:T(8,128)(2,1)S(1)}, u32[]{:S(2)}, u32[]{:S(2)}) collective-permute-start(bf16[256,256]{1,0:T(8,128)(2,1)S(1)} %get-tuple-element.71), channel_id=1, source_target_pairs={{0,1},{2,0},{4,2},{6,4},{7,6},{5,7},{3,5},{1,3},{8,9},{10,8},{12,1... | collective-permute-start | bytes 393224 | tf_op jit(solution)/shard_map/ppermute | solution.py:33
  47.1 0.4 collective-permute-start.21
  47.6 1.6 %collective-permute-done.31 = bf16[256,256]{1,0:T(8,128)(2,1)S(1)} collective-permute-done((bf16[256,256]{1,0:T(8,128)(2,1)S(1)}, bf16[256,256]{1,0:T(8,128)(2,1)S(1)}, u32[]{:S(2)}, u32[]{:S(2)}) %collective-permute-start.31) | collective-permute-done | bytes 131104 | tf_op jit(solution)/shard_map/ppermute | solution.py:33
  49.3 0.6 collective-permute-start.32
  49.8 0.5 collective-permute-done.27
  50.4 1.6 %collective-permute-start.28 = (bf16[256,256]{1,0:T(8,128)(2,1)S(1)}, bf16[256,256]{1,0:T(8,128)(2,1)S(1)}, u32[]{:S(2)}, u32[]{:S(2)}) collective-permute-start(bf16[256,256]{1,0:T(8,128)(2,1)S(1)} %add_convert_fusion.7), channel_id=1, source_target_pairs={{0,1},{2,0},{4,2},{6,4},{7,6},{5,7},{3,5},{1,3},{8,9},{10,8},{12,1... | collective-permute-start | bytes 393224 | tf_op jit(solution)/shard_map/ppermute | solution.py:33
  52.0 0.7 %collective-permute-done.24 = bf16[256,256]{1,0:T(8,128)(2,1)S(1)} collective-permute-done((bf16[256,256]{1,0:T(8,128)(2,1)S(1)}, bf16[256,256]{1,0:T(8,128)(2,1)S(1)}, u32[]{:S(2)}, u32[]{:S(2)}) %collective-permute-start.24) | collective-permute-done | bytes 131104 | tf_op jit(solution)/shard_map/ppermute | solution.py:33
  52.7 1.6 %collective-permute-start.25 = (bf16[256,256]{1,0:T(8,128)(2,1)S(1)}, bf16[256,256]{1,0:T(8,128)(2,1)S(1)}, u32[]{:S(2)}, u32[]{:S(2)}) collective-permute-start(bf16[256,256]{1,0:T(8,128)(2,1)S(1)} %add_convert_fusion.9), channel_id=1, source_target_pairs={{0,1},{2,0},{4,2},{6,4},{7,6},{5,7},{3,5},{1,3},{8,9},{10,8},{12,1... | collective-permute-start | bytes 393224 | tf_op jit(solution)/shard_map/ppermute | solution.py:33
  54.4 0.5 collective-permute-start.22
  55.0 1.6 %collective-permute-start.33 = (bf16[256,256]{1,0:T(8,128)(2,1)S(1)}, bf16[256,256]{1,0:T(8,128)(2,1)S(1)}, u32[]{:S(2)}, u32[]{:S(2)}) collective-permute-start(bf16[256,256]{1,0:T(8,128)(2,1)S(1)} %add_convert_fusion.3), channel_id=1, source_target_pairs={{0,2},{2,4},{4,6},{6,7},{7,5},{5,3},{3,1},{1,0},{8,10},{10,12},{12... | collective-permute-start | bytes 393224 | tf_op jit(solution)/shard_map/ppermute | solution.py:33
  56.8 1.6 %collective-permute-start.29 = (bf16[256,256]{1,0:T(8,128)(2,1)S(1)}, bf16[256,256]{1,0:T(8,128)(2,1)S(1)}, u32[]{:S(2)}, u32[]{:S(2)}) collective-permute-start(bf16[256,256]{1,0:T(8,128)(2,1)S(1)} %add_convert_fusion.6), channel_id=1, source_target_pairs={{0,1},{2,0},{4,2},{6,4},{7,6},{5,7},{3,5},{1,3},{8,9},{10,8},{12,1... | collective-permute-start | bytes 393224 | tf_op jit(solution)/shard_map/ppermute | solution.py:33
  58.4 0.9 %collective-permute-done.25 = bf16[256,256]{1,0:T(8,128)(2,1)S(1)} collective-permute-done((bf16[256,256]{1,0:T(8,128)(2,1)S(1)}, bf16[256,256]{1,0:T(8,128)(2,1)S(1)}, u32[]{:S(2)}, u32[]{:S(2)}) %collective-permute-start.25) | collective-permute-done | bytes 131104 | tf_op jit(solution)/shard_map/ppermute | solution.py:33
  59.3 1.6 %collective-permute-start.26 = (bf16[256,256]{1,0:T(8,128)(2,1)S(1)}, bf16[256,256]{1,0:T(8,128)(2,1)S(1)}, u32[]{:S(2)}, u32[]{:S(2)}) collective-permute-start(bf16[256,256]{1,0:T(8,128)(2,1)S(1)} %add_convert_fusion.8), channel_id=1, source_target_pairs={{0,1},{2,0},{4,2},{6,4},{7,6},{5,7},{3,5},{1,3},{8,9},{10,8},{12,1... | collective-permute-start | bytes 393224 | tf_op jit(solution)/shard_map/ppermute | solution.py:33
  60.9 0.5 collective-permute-start.23
  61.5 1.8 %collective-permute-start.34 = (bf16[256,256]{1,0:T(8,128)(2,1)S(1)}, bf16[256,256]{1,0:T(8,128)(2,1)S(1)}, u32[]{:S(2)}, u32[]{:S(2)}) collective-permute-start(bf16[256,256]{1,0:T(8,128)(2,1)S(1)} %add_convert_fusion.2), channel_id=1, source_target_pairs={{0,2},{2,4},{4,6},{6,7},{7,5},{5,3},{3,1},{1,0},{8,10},{10,12},{12... | collective-permute-start | bytes 393224 | tf_op jit(solution)/shard_map/ppermute | solution.py:33
  63.3 0.9 %collective-permute-start.30 = (bf16[256,256]{1,0:T(8,128)(2,1)S(1)}, bf16[256,256]{1,0:T(8,128)(2,1)S(1)}, u32[]{:S(2)}, u32[]{:S(2)}) collective-permute-start(bf16[256,256]{1,0:T(8,128)(2,1)S(1)} %add_convert_fusion.5), channel_id=1, source_target_pairs={{0,1},{2,0},{4,2},{6,4},{7,6},{5,7},{3,5},{1,3},{8,9},{10,8},{12,1... | collective-permute-start | bytes 393224 | tf_op jit(solution)/shard_map/ppermute | solution.py:33
  64.1 1.4 %collective-permute-done.26 = bf16[256,256]{1,0:T(8,128)(2,1)S(1)} collective-permute-done((bf16[256,256]{1,0:T(8,128)(2,1)S(1)}, bf16[256,256]{1,0:T(8,128)(2,1)S(1)}, u32[]{:S(2)}, u32[]{:S(2)}) %collective-permute-start.26) | collective-permute-done | bytes 131104 | tf_op jit(solution)/shard_map/ppermute | solution.py:33
  65.9 1.4 %collective-permute-done.34 = bf16[256,256]{1,0:T(8,128)(2,1)S(1)} collective-permute-done((bf16[256,256]{1,0:T(8,128)(2,1)S(1)}, bf16[256,256]{1,0:T(8,128)(2,1)S(1)}, u32[]{:S(2)}, u32[]{:S(2)}) %collective-permute-start.34) | collective-permute-done | bytes 131104 | tf_op jit(solution)/shard_map/ppermute | solution.py:33
  67.3 1.0 %collective-permute-done.30 = bf16[256,256]{1,0:T(8,128)(2,1)S(1)} collective-permute-done((bf16[256,256]{1,0:T(8,128)(2,1)S(1)}, bf16[256,256]{1,0:T(8,128)(2,1)S(1)}, u32[]{:S(2)}, u32[]{:S(2)}) %collective-permute-start.30) | collective-permute-done | bytes 131104 | tf_op jit(solution)/shard_map/ppermute | solution.py:33
  68.4 0.7 %pad_maximum_fusion = bf16[512,256]{1,0:T(8,128)(2,1)} fusion(bf16[256,256]{1,0:T(8,128)(2,1)S(1)} %get-tuple-element.87, bf16[256,256]{1,0:T(8,128)(2,1)S(1)} %get-tuple-element.88), kind=kLoop, calls=%fused_computation | loop fusion | flops 524288 | bytes 524288 | tf_op jit(solution)/shard_map/concatenate | solution.py:452
  (50 shorter events, 3.6 us)
Async XLA Ops:
  1.0 8.1 %collective-permute-start.3 = (bf16[256,256]{1,0:T(8,128)(2,1)S(1)}, bf16[256,256]{1,0:T(8,128)(2,1)S(1)}, u32[]{:S(2)}, u32[]{:S(2)}) collective-permute-start(bf16[256,256]{1,0:T(8,128)(2,1)S(1)} %get-tuple-element.85), channel_id=1, source_target_pairs={{0,1},{2,0},{4,2},{6,4},{7,6},{5,7},{3,5},{1,3},{8,9},{10,8},{12,1... | collective-permute-start | bytes 393224 | tf_op jit(solution)/shard_map/ppermute | solution.py:33
  4.0 7.1 %collective-permute-start = (bf16[256,256]{1,0:T(8,128)(2,1)S(1)}, bf16[256,256]{1,0:T(8,128)(2,1)S(1)}, u32[]{:S(2)}, u32[]{:S(2)}) collective-permute-start(bf16[256,256]{1,0:T(8,128)(2,1)S(1)} %get-tuple-element.86), channel_id=1, source_target_pairs={{0,2},{2,4},{4,6},{6,7},{7,5},{5,3},{3,1},{1,0},{8,10},{10,12},{12... | collective-permute-start | bytes 393224 | tf_op jit(solution)/shard_map/ppermute | solution.py:33
  4.1 7.1 %collective-permute-start.6 = (bf16[256,256]{1,0:T(8,128)(2,1)S(1)}, bf16[256,256]{1,0:T(8,128)(2,1)S(1)}, u32[]{:S(2)}, u32[]{:S(2)}) collective-permute-start(bf16[256,256]{1,0:T(8,128)(2,1)S(1)} %get-tuple-element.86), channel_id=1, source_target_pairs={{0,1},{2,0},{4,2},{6,4},{7,6},{5,7},{3,5},{1,3},{8,9},{10,8},{12,1... | collective-permute-start | bytes 393224 | tf_op jit(solution)/shard_map/ppermute | solution.py:33
  6.0 7.1 %collective-permute-start.8 = (bf16[256,256]{1,0:T(8,128)(2,1)S(1)}, bf16[256,256]{1,0:T(8,128)(2,1)S(1)}, u32[]{:S(2)}, u32[]{:S(2)}) collective-permute-start(bf16[256,256]{1,0:T(8,128)(2,1)S(1)} %get-tuple-element.85), channel_id=1, source_target_pairs={{0,2},{2,4},{4,6},{6,7},{7,5},{5,3},{3,1},{1,0},{8,10},{10,12},{12... | collective-permute-start | bytes 393224 | tf_op jit(solution)/shard_map/ppermute | solution.py:33
  9.1 6.4 %collective-permute-start.4 = (bf16[256,256]{1,0:T(8,128)(2,1)S(1)}, bf16[256,256]{1,0:T(8,128)(2,1)S(1)}, u32[]{:S(2)}, u32[]{:S(2)}) collective-permute-start(bf16[256,256]{1,0:T(8,128)(2,1)S(1)} %collective-permute-done.3.refs_1_), channel_id=1, source_target_pairs={{0,1},{2,0},{4,2},{6,4},{7,6},{5,7},{3,5},{1,3},{8,9},{10,8},{12,1... | collective-permute-start | bytes 393224 | tf_op jit(solution)/shard_map/ppermute | solution.py:33
  11.1 6.0 %collective-permute-start.1 = (bf16[256,256]{1,0:T(8,128)(2,1)S(1)}, bf16[256,256]{1,0:T(8,128)(2,1)S(1)}, u32[]{:S(2)}, u32[]{:S(2)}) collective-permute-start(bf16[256,256]{1,0:T(8,128)(2,1)S(1)} %collective-permute-done.refs_0_), channel_id=1, source_target_pairs={{0,2},{2,4},{4,6},{6,7},{7,5},{5,3},{3,1},{1,0},{8,10},{10,12},{12... | collective-permute-start | bytes 393224 | tf_op jit(solution)/shard_map/ppermute | solution.py:33
  11.2 7.1 %collective-permute-start.7 = (bf16[256,256]{1,0:T(8,128)(2,1)S(1)}, bf16[256,256]{1,0:T(8,128)(2,1)S(1)}, u32[]{:S(2)}, u32[]{:S(2)}) collective-permute-start(bf16[256,256]{1,0:T(8,128)(2,1)S(1)} %collective-permute-done.6.refs_2_), channel_id=1, source_target_pairs={{0,1},{2,0},{4,2},{6,4},{7,6},{5,7},{3,5},{1,3},{8,9},{10,8},{12,1... | collective-permute-start | bytes 393224 | tf_op jit(solution)/shard_map/ppermute | solution.py:33
  13.1 6.8 %collective-permute-start.9 = (bf16[256,256]{1,0:T(8,128)(2,1)S(1)}, bf16[256,256]{1,0:T(8,128)(2,1)S(1)}, u32[]{:S(2)}, u32[]{:S(2)}) collective-permute-start(bf16[256,256]{1,0:T(8,128)(2,1)S(1)} %collective-permute-done.8.refs_3_), channel_id=1, source_target_pairs={{0,2},{2,4},{4,6},{6,7},{7,5},{5,3},{3,1},{1,0},{8,10},{10,12},{12... | collective-permute-start | bytes 393224 | tf_op jit(solution)/shard_map/ppermute | solution.py:33
  15.5 5.7 %collective-permute-start.5 = (bf16[256,256]{1,0:T(8,128)(2,1)S(1)}, bf16[256,256]{1,0:T(8,128)(2,1)S(1)}, u32[]{:S(2)}, u32[]{:S(2)}) collective-permute-start(bf16[256,256]{1,0:T(8,128)(2,1)S(1)} %collective-permute-done.4.refs_1_), channel_id=1, source_target_pairs={{0,1},{2,0},{4,2},{6,4},{7,6},{5,7},{3,5},{1,3},{8,9},{10,8},{12,1... | collective-permute-start | bytes 393224 | tf_op jit(solution)/shard_map/ppermute | solution.py:33
  17.1 5.7 %collective-permute-start.2 = (bf16[256,256]{1,0:T(8,128)(2,1)S(1)}, bf16[256,256]{1,0:T(8,128)(2,1)S(1)}, u32[]{:S(2)}, u32[]{:S(2)}) collective-permute-start(bf16[256,256]{1,0:T(8,128)(2,1)S(1)} %collective-permute-done.1.refs_0_), channel_id=1, source_target_pairs={{0,2},{2,4},{4,6},{6,7},{7,5},{5,3},{3,1},{1,0},{8,10},{10,12},{12... | collective-permute-start | bytes 393224 | tf_op jit(solution)/shard_map/ppermute | solution.py:33
  18.3 5.2 %collective-permute-start.10 = (bf16[256,256]{1,0:T(8,128)(2,1)S(1)}, bf16[256,256]{1,0:T(8,128)(2,1)S(1)}, u32[]{:S(2)}, u32[]{:S(2)}) collective-permute-start(bf16[256,256]{1,0:T(8,128)(2,1)S(1)} %collective-permute-done.7.refs_2_), channel_id=1, source_target_pairs={{0,1},{2,0},{4,2},{6,4},{7,6},{5,7},{3,5},{1,3},{8,9},{10,8},{12,1... | collective-permute-start | bytes 393224 | tf_op jit(solution)/shard_map/ppermute | solution.py:33
  19.9 5.0 %collective-permute-start.11 = (bf16[256,256]{1,0:T(8,128)(2,1)S(1)}, bf16[256,256]{1,0:T(8,128)(2,1)S(1)}, u32[]{:S(2)}, u32[]{:S(2)}) collective-permute-start(bf16[256,256]{1,0:T(8,128)(2,1)S(1)} %collective-permute-done.9.refs_3_), channel_id=1, source_target_pairs={{0,2},{2,4},{4,6},{6,7},{7,5},{5,3},{3,1},{1,0},{8,10},{10,12},{12... | collective-permute-start | bytes 393224 | tf_op jit(solution)/shard_map/ppermute | solution.py:33
  21.2 5.7 %collective-permute-start.13 = (bf16[256,256]{1,0:T(8,128)(2,1)S(1)}, bf16[256,256]{1,0:T(8,128)(2,1)S(1)}, u32[]{:S(2)}, u32[]{:S(2)}) collective-permute-start(bf16[256,256]{1,0:T(8,128)(2,1)S(1)} %collective-permute-done.5.refs_1_), channel_id=1, source_target_pairs={{0,1},{2,0},{4,2},{6,4},{7,6},{5,7},{3,5},{1,3},{8,9},{10,8},{12,1... | collective-permute-start | bytes 393224 | tf_op jit(solution)/shard_map/ppermute | solution.py:33
  22.8 5.0 %collective-permute-start.12 = (bf16[256,256]{1,0:T(8,128)(2,1)S(1)}, bf16[256,256]{1,0:T(8,128)(2,1)S(1)}, u32[]{:S(2)}, u32[]{:S(2)}) collective-permute-start(bf16[256,256]{1,0:T(8,128)(2,1)S(1)} %collective-permute-done.2.refs_0_), channel_id=1, source_target_pairs={{0,2},{2,4},{4,6},{6,7},{7,5},{5,3},{3,1},{1,0},{8,10},{10,12},{12... | collective-permute-start | bytes 393224 | tf_op jit(solution)/shard_map/ppermute | solution.py:33
  29.1 6.9 %collective-permute-start.17 = (bf16[256,512]{1,0:T(8,128)(2,1)S(1)}, bf16[256,512]{1,0:T(8,128)(2,1)S(1)}, u32[]{:S(2)}, u32[]{:S(2)}) collective-permute-start(bf16[256,512]{1,0:T(8,128)(2,1)S(1)} %get-tuple-element.53.refs_0_), channel_id=1, source_target_pairs={{0,16},{8,24},{16,0},{24,8},{1,17},{9,25},{17,1},{25,9},{2,18},{10... | collective-permute-start | bytes 786440 | tf_op jit(solution)/shard_map/ppermute | solution.py:425
  30.6 8.2 %collective-permute-start.18 = (bf16[256,512]{1,0:T(8,128)(2,1)S(1)}, bf16[256,512]{1,0:T(8,128)(2,1)S(1)}, u32[]{:S(2)}, u32[]{:S(2)}) collective-permute-start(bf16[256,512]{1,0:T(8,128)(2,1)S(1)} %get-tuple-element.54.refs_1_), channel_id=1, source_target_pairs={{0,16},{8,24},{16,0},{24,8},{1,17},{9,25},{17,1},{25,9},{2,18},{10... | collective-permute-start | bytes 786440 | tf_op jit(solution)/shard_map/ppermute | solution.py:425
  31.1 3.0 %collective-permute-start.15 = (bf16[176,512]{1,0:T(8,128)(2,1)S(1)}, bf16[176,512]{1,0:T(8,128)(2,1)S(1)}, u32[]{:S(2)}, u32[]{:S(2)}) collective-permute-start(bf16[176,512]{1,0:T(8,128)(2,1)S(1)} %get-tuple-element.56), channel_id=1, source_target_pairs={{0,8},{8,0},{16,24},{24,16},{1,9},{9,1},{17,25},{25,17},{2,10},{10... | collective-permute-start | bytes 540680 | tf_op jit(solution)/shard_map/ppermute | solution.py:39
  31.1 3.0 %collective-permute-start.16 = (bf16[176,512]{1,0:T(8,128)(2,1)S(1)}, bf16[176,512]{1,0:T(8,128)(2,1)S(1)}, u32[]{:S(2)}, u32[]{:S(2)}) collective-permute-start(bf16[176,512]{1,0:T(8,128)(2,1)S(1)} %get-tuple-element.57), channel_id=1, source_target_pairs={{0,8},{8,0},{16,24},{24,16},{1,9},{9,1},{17,25},{25,17},{2,10},{10... | collective-permute-start | bytes 540680 | tf_op jit(solution)/shard_map/ppermute | solution.py:39
  31.7 2.5 %collective-permute-start.14 = (bf16[160,512]{1,0:T(8,128)(2,1)S(1)}, bf16[160,512]{1,0:T(8,128)(2,1)S(1)}, u32[]{:S(2)}, u32[]{:S(2)}) collective-permute-start(bf16[160,512]{1,0:T(8,128)(2,1)S(1)} %get-tuple-element.55), channel_id=1, source_target_pairs={{0,8},{8,0},{16,24},{24,16},{1,9},{9,1},{17,25},{25,17},{2,10},{10... | collective-permute-start | bytes 491528 | tf_op jit(solution)/shard_map/ppermute | solution.py:39
  38.8 1.7 %collective-permute-start.19 = (bf16[256,512]{1,0:T(8,128)(2,1)S(1)}, bf16[256,512]{1,0:T(8,128)(2,1)S(1)}, u32[]{:S(2)}, u32[]{:S(2)}) collective-permute-start(bf16[256,512]{1,0:T(8,128)(2,1)S(1)} %collective-permute-done.17.refs_0_), channel_id=1, source_target_pairs={{0,8},{8,0},{16,24},{24,16},{1,9},{9,1},{17,25},{25,17},{2,10},{10... | collective-permute-start | bytes 786440 | tf_op jit(solution)/shard_map/ppermute | solution.py:39
  38.8 1.9 %collective-permute-start.20 = (bf16[256,512]{1,0:T(8,128)(2,1)S(1)}, bf16[256,512]{1,0:T(8,128)(2,1)S(1)}, u32[]{:S(2)}, u32[]{:S(2)}) collective-permute-start(bf16[256,512]{1,0:T(8,128)(2,1)S(1)} %collective-permute-done.18.refs_1_), channel_id=1, source_target_pairs={{0,8},{8,0},{16,24},{24,16},{1,9},{9,1},{17,25},{25,17},{2,10},{10... | collective-permute-start | bytes 786440 | tf_op jit(solution)/shard_map/ppermute | solution.py:39
  43.5 5.8 %collective-permute-start.31 = (bf16[256,256]{1,0:T(8,128)(2,1)S(1)}, bf16[256,256]{1,0:T(8,128)(2,1)S(1)}, u32[]{:S(2)}, u32[]{:S(2)}) collective-permute-start(bf16[256,256]{1,0:T(8,128)(2,1)S(1)} %get-tuple-element.79), channel_id=1, source_target_pairs={{0,2},{2,4},{4,6},{6,7},{7,5},{5,3},{3,1},{1,0},{8,10},{10,12},{12... | collective-permute-start | bytes 393224 | tf_op jit(solution)/shard_map/ppermute | solution.py:33
  44.0 6.4 %collective-permute-start.27 = (bf16[256,256]{1,0:T(8,128)(2,1)S(1)}, bf16[256,256]{1,0:T(8,128)(2,1)S(1)}, u32[]{:S(2)}, u32[]{:S(2)}) collective-permute-start(bf16[256,256]{1,0:T(8,128)(2,1)S(1)} %get-tuple-element.75), channel_id=1, source_target_pairs={{0,1},{2,0},{4,2},{6,4},{7,6},{5,7},{3,5},{1,3},{8,9},{10,8},{12,1... | collective-permute-start | bytes 393224 | tf_op jit(solution)/shard_map/ppermute | solution.py:33
  45.5 7.2 %collective-permute-start.24 = (bf16[256,256]{1,0:T(8,128)(2,1)S(1)}, bf16[256,256]{1,0:T(8,128)(2,1)S(1)}, u32[]{:S(2)}, u32[]{:S(2)}) collective-permute-start(bf16[256,256]{1,0:T(8,128)(2,1)S(1)} %get-tuple-element.71), channel_id=1, source_target_pairs={{0,1},{2,0},{4,2},{6,4},{7,6},{5,7},{3,5},{1,3},{8,9},{10,8},{12,1... | collective-permute-start | bytes 393224 | tf_op jit(solution)/shard_map/ppermute | solution.py:33
  47.1 7.2 %collective-permute-start.21 = (bf16[256,256]{1,0:T(8,128)(2,1)S(1)}, bf16[256,256]{1,0:T(8,128)(2,1)S(1)}, u32[]{:S(2)}, u32[]{:S(2)}) collective-permute-start(bf16[256,256]{1,0:T(8,128)(2,1)S(1)} %get-tuple-element.68), channel_id=1, source_target_pairs={{0,2},{2,4},{4,6},{6,7},{7,5},{5,3},{3,1},{1,0},{8,10},{10,12},{12... | collective-permute-start | bytes 393224 | tf_op jit(solution)/shard_map/ppermute | solution.py:33
  49.3 5.7 %collective-permute-start.32 = (bf16[256,256]{1,0:T(8,128)(2,1)S(1)}, bf16[256,256]{1,0:T(8,128)(2,1)S(1)}, u32[]{:S(2)}, u32[]{:S(2)}) collective-permute-start(bf16[256,256]{1,0:T(8,128)(2,1)S(1)} %add_convert_fusion.4), channel_id=1, source_target_pairs={{0,2},{2,4},{4,6},{6,7},{7,5},{5,3},{3,1},{1,0},{8,10},{10,12},{12... | collective-permute-start | bytes 393224 | tf_op jit(solution)/shard_map/ppermute | solution.py:33
  50.4 6.3 %collective-permute-start.28 = (bf16[256,256]{1,0:T(8,128)(2,1)S(1)}, bf16[256,256]{1,0:T(8,128)(2,1)S(1)}, u32[]{:S(2)}, u32[]{:S(2)}) collective-permute-start(bf16[256,256]{1,0:T(8,128)(2,1)S(1)} %add_convert_fusion.7), channel_id=1, source_target_pairs={{0,1},{2,0},{4,2},{6,4},{7,6},{5,7},{3,5},{1,3},{8,9},{10,8},{12,1... | collective-permute-start | bytes 393224 | tf_op jit(solution)/shard_map/ppermute | solution.py:33
  52.7 6.5 %collective-permute-start.25 = (bf16[256,256]{1,0:T(8,128)(2,1)S(1)}, bf16[256,256]{1,0:T(8,128)(2,1)S(1)}, u32[]{:S(2)}, u32[]{:S(2)}) collective-permute-start(bf16[256,256]{1,0:T(8,128)(2,1)S(1)} %add_convert_fusion.9), channel_id=1, source_target_pairs={{0,1},{2,0},{4,2},{6,4},{7,6},{5,7},{3,5},{1,3},{8,9},{10,8},{12,1... | collective-permute-start | bytes 393224 | tf_op jit(solution)/shard_map/ppermute | solution.py:33
  54.4 6.5 %collective-permute-start.22 = (bf16[256,256]{1,0:T(8,128)(2,1)S(1)}, bf16[256,256]{1,0:T(8,128)(2,1)S(1)}, u32[]{:S(2)}, u32[]{:S(2)}) collective-permute-start(bf16[256,256]{1,0:T(8,128)(2,1)S(1)} %add_convert_fusion.11), channel_id=1, source_target_pairs={{0,2},{2,4},{4,6},{6,7},{7,5},{5,3},{3,1},{1,0},{8,10},{10,12},{12... | collective-permute-start | bytes 393224 | tf_op jit(solution)/shard_map/ppermute | solution.py:33
  55.0 6.5 %collective-permute-start.33 = (bf16[256,256]{1,0:T(8,128)(2,1)S(1)}, bf16[256,256]{1,0:T(8,128)(2,1)S(1)}, u32[]{:S(2)}, u32[]{:S(2)}) collective-permute-start(bf16[256,256]{1,0:T(8,128)(2,1)S(1)} %add_convert_fusion.3), channel_id=1, source_target_pairs={{0,2},{2,4},{4,6},{6,7},{7,5},{5,3},{3,1},{1,0},{8,10},{10,12},{12... | collective-permute-start | bytes 393224 | tf_op jit(solution)/shard_map/ppermute | solution.py:33
  56.8 6.5 %collective-permute-start.29 = (bf16[256,256]{1,0:T(8,128)(2,1)S(1)}, bf16[256,256]{1,0:T(8,128)(2,1)S(1)}, u32[]{:S(2)}, u32[]{:S(2)}) collective-permute-start(bf16[256,256]{1,0:T(8,128)(2,1)S(1)} %add_convert_fusion.6), channel_id=1, source_target_pairs={{0,1},{2,0},{4,2},{6,4},{7,6},{5,7},{3,5},{1,3},{8,9},{10,8},{12,1... | collective-permute-start | bytes 393224 | tf_op jit(solution)/shard_map/ppermute | solution.py:33
  59.3 6.3 %collective-permute-start.26 = (bf16[256,256]{1,0:T(8,128)(2,1)S(1)}, bf16[256,256]{1,0:T(8,128)(2,1)S(1)}, u32[]{:S(2)}, u32[]{:S(2)}) collective-permute-start(bf16[256,256]{1,0:T(8,128)(2,1)S(1)} %add_convert_fusion.8), channel_id=1, source_target_pairs={{0,1},{2,0},{4,2},{6,4},{7,6},{5,7},{3,5},{1,3},{8,9},{10,8},{12,1... | collective-permute-start | bytes 393224 | tf_op jit(solution)/shard_map/ppermute | solution.py:33
  60.9 5.0 %collective-permute-start.23 = (bf16[256,256]{1,0:T(8,128)(2,1)S(1)}, bf16[256,256]{1,0:T(8,128)(2,1)S(1)}, u32[]{:S(2)}, u32[]{:S(2)}) collective-permute-start(bf16[256,256]{1,0:T(8,128)(2,1)S(1)} %add_convert_fusion.10), channel_id=1, source_target_pairs={{0,2},{2,4},{4,6},{6,7},{7,5},{5,3},{3,1},{1,0},{8,10},{10,12},{12... | collective-permute-start | bytes 393224 | tf_op jit(solution)/shard_map/ppermute | solution.py:33
  61.5 5.8 %collective-permute-start.34 = (bf16[256,256]{1,0:T(8,128)(2,1)S(1)}, bf16[256,256]{1,0:T(8,128)(2,1)S(1)}, u32[]{:S(2)}, u32[]{:S(2)}) collective-permute-start(bf16[256,256]{1,0:T(8,128)(2,1)S(1)} %add_convert_fusion.2), channel_id=1, source_target_pairs={{0,2},{2,4},{4,6},{6,7},{7,5},{5,3},{3,1},{1,0},{8,10},{10,12},{12... | collective-permute-start | bytes 393224 | tf_op jit(solution)/shard_map/ppermute | solution.py:33
  63.3 5.0 %collective-permute-start.30 = (bf16[256,256]{1,0:T(8,128)(2,1)S(1)}, bf16[256,256]{1,0:T(8,128)(2,1)S(1)}, u32[]{:S(2)}, u32[]{:S(2)}) collective-permute-start(bf16[256,256]{1,0:T(8,128)(2,1)S(1)} %add_convert_fusion.5), channel_id=1, source_target_pairs={{0,1},{2,0},{4,2},{6,4},{7,6},{5,7},{3,5},{1,3},{8,9},{10,8},{12,1... | collective-permute-start | bytes 393224 | tf_op jit(solution)/shard_map/ppermute | solution.py:33
